TPU v7x, 32 devices: a whole 2x2x4 slice. The times are simulated.
32 devices in a mesh: batch: 8 (over z, core), mp: 4 (over y, x).
Axes of the slice: x: 2, y: 2, z: 4, core: 2. Of those that a mesh axis runs over, the one named last changes fastest.
Arguments:
- queries: bfloat16 [128, 4096], P('batch', 'mp'), may hold values from -384 to 384, as said below
- prompt_cache: bfloat16 [8, 4, 4096, 256], P('batch', 'mp'), may hold values from -48 to 48, as said below
- pool: bfloat16 [256, 4, 64, 256], P('batch', 'mp'), may hold values from -48 to 48, as said below
- block_table: int32 [128, 4], replicated, may hold values from 0 to 255, as said below
- parents: int32 [128], replicated, may hold values from 0 to 127, as said below
- lengths: int32 [8], P('batch'), may hold values from 2048 to 8192, as said below
Outputs:
- attended: float32 [128, 4096], P('batch', 'mp')
Inputs may be any that keep to these rules, and one draw needn't show every extreme that they name: `queries`: custom float draw of activations; entries stay within the range. `prompt_cache`: keys are of order one and values about eight times larger. `pool`: keys are of order one and values larger, as in prompt_cache. `block_table`: block b is held by batch index b // 32. A row's 4 entries are distinct. The rows of one request name at most 4 distinct blocks held by any one batch index, and exactly 4 held by some index. parents[i] // 16 == i // 16: a row continues a beam of its own request. `lengths`: some request has 8192 valid prompt tokens.
All inputs are finite; a program needn't handle non-finite values.
Results may differ from a plain program's by a relative error of at most 0.007.
Values may be sent and summed in bfloat16 or wider, within the bound.
No kernel may reach another device: no remote copies, remote signals or barrier semaphores. Data moves between devices by JAX's collectives and lax.ppermute only.
A program may use at most 64 MiB of HBM per device.

v0:
```python
import jax
import jax.numpy as jnp
from jax import lax
from jax.sharding import PartitionSpec as P

HD = 128
GROUP = 16
BEAMS = 16
SUF = 4


big_negative = -1e30


def swapped(value, axis, stride):
    mask = 2**stride
    pairs = [(source, source ^ mask) for source in range(lax.axis_size(axis))]
    return lax.ppermute(value, axis, pairs)


def partial_softmax(scores, keep, values):
    top = jnp.max(jnp.where(keep, scores, big_negative), axis=-1)
    weights = jnp.where(keep, jnp.exp(scores - top[..., None]), 0.0)
    total = jnp.sum(weights, axis=-1)
    summed = jnp.dot(weights.astype(jnp.bfloat16), values, preferred_element_type=jnp.float32)
    return (top, total, summed)


def combine(first, second):
    top = jnp.maximum(first[0], second[0])
    scale_a = jnp.exp(first[0] - top)
    scale_b = jnp.exp(second[0] - top)
    total = first[1] * scale_a + second[1] * scale_b
    summed = first[2] * scale_a[..., None] + second[2] * scale_b[..., None]
    return (top, total, summed)


def pick_slots(wanted, slot_ids, capacity):
    hit = jnp.any(wanted[:, :, None] == slot_ids[:, None, :], axis=1)
    rank = jnp.cumsum(hit.astype(jnp.int32), axis=1) - 1
    order = jnp.arange(capacity, dtype=jnp.int32)
    chosen = hit[:, None, :] & (rank[:, None, :] == order[None, :, None])
    positions = jnp.arange(slot_ids.shape[1], dtype=jnp.int32)
    local_index = jnp.sum(jnp.where(chosen, positions[None, None, :], 0), axis=2)
    global_ids = jnp.sum(jnp.where(chosen, slot_ids[:, None, :], 0), axis=2)
    present = jnp.any(chosen, axis=2)
    return (local_index, global_ids, present)


def on_device(queries, prompt_cache, pool, block_table, parents, lengths):
    n_batch = lax.axis_size("batch")
    myself = lax.axis_index("batch")
    parity = lax.axis_index("mp") % 2
    ndist = 2 ** (SUF + 1) - 2
    capacity = 2 * ((ndist // 2 + n_batch - 1) // n_batch)
    half = pool.shape[2]
    slots = pool.shape[0]
    scale = HD ** (-0.5)
    vec_rows = BEAMS * GROUP
    own = queries.reshape(BEAMS, GROUP // 2, HD)
    other = swapped(queries, "mp", 0).reshape(BEAMS, GROUP // 2, HD)
    lower = jnp.where(parity == 0, own, other)
    upper = jnp.where(parity == 0, other, own)
    vectors = jnp.concatenate([lower, upper], axis=1).reshape(vec_rows, HD)
    prompt_rows = prompt_cache[0, 0]
    token = jnp.arange(prompt_rows.shape[0], dtype=jnp.int32)
    position = token // half * (2 * half) + parity * half + token % half
    keep_prompt = (position < lengths[0])[None, :]
    prompt_scores = (
        jnp.einsum("qd,td->qt", vectors, prompt_rows[:, :HD], preferred_element_type=jnp.float32)
        * scale
    )
    prompt_part = partial_softmax(prompt_scores, keep_prompt, prompt_rows[:, HD:])
    referenced = block_table[parents]
    mine = lax.dynamic_slice_in_dim(referenced, myself * BEAMS, BEAMS, 0)
    by_dest = referenced.reshape(n_batch, BEAMS * SUF)
    held = jnp.broadcast_to(
        myself * slots + jnp.arange(slots, dtype=jnp.int32)[None, :], (n_batch, slots)
    )
    send_local, send_ids, send_present = pick_slots(by_dest, held, capacity)
    outgoing = pool[:, 0][send_local]
    incoming = lax.all_to_all(outgoing, "batch", split_axis=0, concat_axis=0, tiled=True)
    owner_slots = (
        jnp.arange(n_batch, dtype=jnp.int32)[:, None] * slots
        + jnp.arange(slots, dtype=jnp.int32)[None, :]
    )
    wanted = jnp.broadcast_to(mine.reshape(1, BEAMS * SUF), (n_batch, BEAMS * SUF))
    got_local, got_ids, got_present = pick_slots(wanted, owner_slots, capacity)
    member = jnp.any(mine[:, :, None] == got_ids.reshape(1, 1, -1), axis=1) & got_present.reshape(
        1, -1
    )
    flat = incoming.reshape(n_batch * capacity * half, 2 * HD)
    suffix_scores = (
        jnp.einsum("qd,td->qt", vectors, flat[:, :HD], preferred_element_type=jnp.float32) * scale
    )
    keep_suffix = jnp.broadcast_to(
        member[:, None, :, None], (BEAMS, GROUP, n_batch * capacity, half)
    )
    keep_suffix = keep_suffix.reshape(vec_rows, n_batch * capacity * half)
    suffix_part = partial_softmax(suffix_scores, keep_suffix, flat[:, HD:])
    top, total, summed = combine(prompt_part, suffix_part)
    top = top.reshape(BEAMS, GROUP)
    total = total.reshape(BEAMS, GROUP)
    summed = summed.reshape(BEAMS, GROUP, HD)
    split = GROUP // 2
    kept = (
        jnp.where(parity == 0, top[:, :split], top[:, split:]),
        jnp.where(parity == 0, total[:, :split], total[:, split:]),
        jnp.where(parity == 0, summed[:, :split], summed[:, split:]),
    )
    given = (
        jnp.where(parity == 0, top[:, split:], top[:, :split]),
        jnp.where(parity == 0, total[:, split:], total[:, :split]),
        jnp.where(parity == 0, summed[:, split:], summed[:, :split]),
    )
    received = swapped((given[0], given[1], given[2]), "mp", 0)
    final = combine(kept, received)
    return (final[2] / final[1][..., None]).reshape(BEAMS, split * HD)


def solution(mesh):
    return jax.shard_map(
        on_device,
        mesh=mesh,
        in_specs=(
            P("batch", "mp"),
            P("batch", "mp", None, None),
            P("batch", "mp", None, None),
            P(),
            P(),
            P("batch"),
        ),
        out_specs=P("batch", "mp"),
        check_vma=False,
    )
```

profile of v0, /device:TPU:0, one launch (start us, length us, event | category | flops | bytes accessed | tf_op | source)
XLA Modules:
  0.0 55.3 jit_solution(15592631242726684690)
XLA Ops:
  0.0 2.9 %collective-permute-start = (bf16[16,1024]{1,0:T(8,128)(2,1)}, bf16[16,1024]{1,0:T(8,128)(2,1)S(1)}, u32[]{:S(2)}, u32[]{:S(2)}) collective-permute-start(bf16[16,1024]{1,0:T(8,128)(2,1)} %param.6), channel_id=1, source_target_pairs={{0,1},{1,0},{2,3},{3,2},{4,5},{5,4},{6,7},{7,6},{8,9},{9,8},{10,11... | collective-permute-start | bytes 98312 | tf_op jit(solution)/shard_map/ppermute | solution.py:18
  2.9 0.8 %copy.11 = s32[128,4]{1,0:T(8,128)S(1)} copy(s32[128,4]{0,1:T(4,128)} %param.9) | data formatting | bytes 4096 | tf_op args[3]
  3.7 0.7 %compare_select_fusion.1 = s32[128]{0:T(128)S(1)} fusion(s32[128]{0:T(128)} %param.10), kind=kLoop, calls=%fused_computation.70 | loop fusion | flops 384 | bytes 1024 | tf_op jit(solution)/shard_map/select_n | solution.py:74
  4.4 0.6 %gather_fusion = s32[128,4]{1,0:T(8,128)S(1)} fusion(s32[128,4]{1,0:T(8,128)S(1)} %copy.11, s32[1024]{0:T(1024)S(1)} %pad_clamp_fusion.1), kind=kCustom, calls=%fused_computation | custom fusion | bytes 4608 | tf_op jit(solution)/shard_map/gather | solution.py:74
  5.1 0.3 compare_reduce_fusion
  5.4 0.2 reduce_window_sum.18
  6.0 1.6 %gather_fusion.1 = bf16[32,64,256]{2,1,0:T(8,128)(2,1)} fusion(bf16[32,64,256]{2,1,0:T(8,128)(2,1)S(1)} %bitcast.26, s32[1024]{0:T(1024)S(1)} %pad_clamp_fusion), kind=kCustom, calls=%fused_computation.1 | custom fusion | bytes 2097280 | tf_op jit(solution)/shard_map/gather | solution.py:81
  7.6 5.0 %all-to-all-start = ((bf16[8,4,64,256]{3,2,1,0:T(8,128)(2,1)}), bf16[8,4,64,256]{3,2,1,0:T(8,128)(2,1)S(1)}, u32[]{:S(2)}, u32[]{:S(2)}) async-start(bf16[8,4,64,256]{3,2,1,0:T(8,128)(2,1)} %bitcast.5), calls=%async_computation | async-start | bytes 2097152 | tf_op jit(solution)/shard_map/all_to_all | solution.py:82
  13.5 0.3 compare_reduce_fusion.1
  14.8 0.3 broadcast_in_dim.84
  15.2 3.2 %reshape.159 = pred[256,2048]{1,0:T(32,128)(4,1)} reshape(pred[16,16,32,64]{3,2,1,0:T(32,128)(4,1)S(1)} %broadcast_in_dim.84) | data formatting | bytes 1048576 | tf_op jit(solution)/shard_map/reshape | solution.py:99
  18.5 3.9 %select_reduce_fusion = (f32[256]{0:T(256)S(1)}, f32[256,4096]{1,0:T(8,128)}) fusion(pred[4096]{0:T(1024)(128)(4,1)S(1)} %fusion.29, bf16[256,128]{1,0:T(8,128)(2,1)S(1)} %bitcast.31, bf16[4096,256]{1,0:T(8,128)(2,1)} %bitcast.33), kind=kOutput, calls=%fused_computation.4 | convolution fusion | flops 271580928 | bytes 5313536 | tf_op jit(solution)/shard_map/qd,td->qt/dot_general | solution.py:70
  22.4 3.1 %fusion = f32[256]{0:T(256)S(1)} fusion(f32[256,4096]{1,0:T(8,128)} %get-tuple-element.15, f32[256]{0:T(256)S(1)} %get-tuple-element.14, pred[4096]{0:T(1024)(128)(4,1)S(1)} %fusion.29), kind=kLoop, calls=%fused_computation.5 | loop fusion | flops 3145472 | bytes 4200448 | tf_op jit(solution)/shard_map/reduce_sum | solution.py:24
  25.6 13.6 %all-to-all-done = bf16[8,4,64,256]{3,2,1,0:T(8,128)(2,1)S(1)} async-done(((bf16[8,4,64,256]{3,2,1,0:T(8,128)(2,1)}), bf16[8,4,64,256]{3,2,1,0:T(8,128)(2,1)S(1)}, u32[]{:S(2)}, u32[]{:S(2)}) %all-to-all-start) | async-done | bytes 1048608 | tf_op jit(solution)/shard_map/all_to_all | solution.py:82
  39.2 1.0 %copy-done.2 = bf16[8,4,64,256]{3,2,1,0:T(8,128)(2,1)} copy-done((bf16[8,4,64,256]{3,2,1,0:T(8,128)(2,1)}, bf16[8,4,64,256]{3,2,1,0:T(8,128)(2,1)S(1)}, u32[]{:S(2)}) %copy-start.2) | copy-done | bytes 1048600
  40.2 1.8 %select_reduce_fusion.1 = (f32[256]{0:T(256)S(1)}, f32[256,2048]{1,0:T(8,128)S(1)}) fusion(pred[256,2048]{1,0:T(32,128)(4,1)} %reshape.159, bf16[256,128]{1,0:T(8,128)(2,1)S(1)} %bitcast.32, bf16[2048,256]{1,0:T(8,128)(2,1)} %bitcast.27), kind=kOutput, calls=%fused_computation.10 | convolution fusion | flops 135790336 | bytes 3212288 | tf_op jit(solution)/shard_map/qd,td->qt/dot_general | solution.py:94
  42.0 3.4 %fusion.10 = f32[256,128]{1,0:T(8,128)S(1)} fusion(f32[256,4096]{1,0:T(8,128)} %get-tuple-element.15, f32[256]{0:T(256)S(1)} %get-tuple-element.14, pred[4096]{0:T(1024)(128)(4,1)S(1)} %fusion.29, bf16[4096,256]{1,0:T(8,128)(2,1)} %bitcast.34, f32[256]{0:T(256)S(1)} %get-tuple-element.13), kind=kOutput, calls=%fused_computation.18 | convolution fusion | flops 271613952 | bytes 5380096 | tf_op jit(solution)/shard_map/dot_general | solution.py:25
  45.4 0.6 %fusion.7 = f32[256]{0:T(256)S(1)} fusion(pred[256,2048]{1,0:T(32,128)(4,1)S(1)} %copy-done.1, f32[256,2048]{1,0:T(8,128)S(1)} %get-tuple-element.17, f32[256]{0:T(256)S(1)} %get-tuple-element.16), kind=kLoop, calls=%fused_computation.14 | loop fusion | flops 1572608 | bytes 2623488 | tf_op jit(solution)/shard_map/reduce_sum | solution.py:24
  46.2 0.5 collective-permute-start.3
  46.9 1.5 %collective-permute-start.1 = (f32[16,8]{1,0:T(8,128)S(1)}, f32[16,8]{1,0:T(8,128)S(1)}, u32[]{:S(2)}, u32[]{:S(2)}) collective-permute-start(f32[16,8]{1,0:T(8,128)S(1)} %slice_select_fusion.2), channel_id=1, source_target_pairs={{0,1},{1,0},{2,3},{3,2},{4,5},{5,4},{6,7},{7,6},{8,9},{9,8},{10,11... | collective-permute-start | bytes 1544 | tf_op jit(solution)/shard_map/ppermute | solution.py:18
  48.4 1.8 %fusion.9 = f32[256,128]{1,0:T(8,128)S(1)} fusion(f32[256,128]{1,0:T(8,128)S(1)} %fusion.10, pred[256,2048]{1,0:T(32,128)(4,1)} %reshape.159, f32[256,2048]{1,0:T(8,128)S(1)} %get-tuple-element.17, f32[256]{0:T(256)S(1)} %get-tuple-element.16, bf16[2048,256]{1,0:T(8,128)(2,1)} %bitcast.28, f32[256]{0:T(256)S(1)} %get-tuple-element.12), kind=kOutput, calls=%fused_computation.17 | convolution fusion | flops 135856128 | bytes 3409920 | tf_op jit(solution)/shard_map/dot_general | solution.py:25
  50.2 0.6 %collective-permute-start.2 = (f32[16,8,128]{2,1,0:T(8,128)S(1)}, f32[16,8,128]{2,1,0:T(8,128)S(1)}, u32[]{:S(2)}, u32[]{:S(2)}) collective-permute-start(f32[16,8,128]{2,1,0:T(8,128)S(1)} %slice_select_fusion), channel_id=1, source_target_pairs={{0,1},{1,0},{2,3},{3,2},{4,5},{5,4},{6,7},{7,6},{8,9},{9,8},{10,11... | collective-permute-start | bytes 196616 | tf_op jit(solution)/shard_map/ppermute | solution.py:18
  50.9 3.6 %collective-permute-done.2 = f32[16,8,128]{2,1,0:T(8,128)S(1)} collective-permute-done((f32[16,8,128]{2,1,0:T(8,128)S(1)}, f32[16,8,128]{2,1,0:T(8,128)S(1)}, u32[]{:S(2)}, u32[]{:S(2)}) %collective-permute-start.2) | collective-permute-done | bytes 65568 | tf_op jit(solution)/shard_map/ppermute | solution.py:18
  54.7 0.6 %copy.20 = f32[2,8,8,128]{3,1,2,0:T(8,128)} copy(f32[2,8,8,128]{3,2,1,0:T(8,128)S(1)} %bitcast.35) | data formatting | bytes 131072
  (52 shorter events, 2.4 us)
Async XLA Ops:
  0.0 6.0 %copy-start = (bf16[32,1,64,256]{3,2,1,0:T(8,128)(2,1)S(1)}, bf16[32,1,64,256]{3,2,1,0:T(8,128)(2,1)}, u32[]{:S(2)}) copy-start(bf16[32,1,64,256]{3,2,1,0:T(8,128)(2,1)} %param.8) | copy-start | bytes 3145732
  0.0 18.4 %collective-permute-start = (bf16[16,1024]{1,0:T(8,128)(2,1)}, bf16[16,1024]{1,0:T(8,128)(2,1)S(1)}, u32[]{:S(2)}, u32[]{:S(2)}) collective-permute-start(bf16[16,1024]{1,0:T(8,128)(2,1)} %param.6), channel_id=1, source_target_pairs={{0,1},{1,0},{2,3},{3,2},{4,5},{5,4},{6,7},{7,6},{8,9},{9,8},{10,11... | collective-permute-start | bytes 98312 | tf_op jit(solution)/shard_map/ppermute | solution.py:18
  7.6 10.8 %copy-start.3 = (bf16[16,1024]{1,0:T(8,128)(2,1)S(1)}, bf16[16,1024]{1,0:T(8,128)(2,1)}, u32[]{:S(2)}) copy-start(bf16[16,1024]{1,0:T(8,128)(2,1)} %param.6) | copy-start | bytes 98308
  7.6 31.6 %all-to-all-start = ((bf16[8,4,64,256]{3,2,1,0:T(8,128)(2,1)}), bf16[8,4,64,256]{3,2,1,0:T(8,128)(2,1)S(1)}, u32[]{:S(2)}, u32[]{:S(2)}) async-start(bf16[8,4,64,256]{3,2,1,0:T(8,128)(2,1)} %bitcast.5), calls=%async_computation | async-start | bytes 2097152 | tf_op jit(solution)/shard_map/all_to_all | solution.py:82
  39.2 1.0 %copy-start.2 = (bf16[8,4,64,256]{3,2,1,0:T(8,128)(2,1)}, bf16[8,4,64,256]{3,2,1,0:T(8,128)(2,1)S(1)}, u32[]{:S(2)}) copy-start(bf16[8,4,64,256]{3,2,1,0:T(8,128)(2,1)S(1)} %all-to-all-done) | copy-start | bytes 3145732
  42.0 3.4 %copy-start.1 = (pred[256,2048]{1,0:T(32,128)(4,1)S(1)}, pred[256,2048]{1,0:T(32,128)(4,1)}, u32[]{:S(2)}) copy-start(pred[256,2048]{1,0:T(32,128)(4,1)} %reshape.159) | copy-start | bytes 1572868
  46.2 4.6 %collective-permute-start.3 = (f32[16,8]{1,0:T(8,128)S(1)}, f32[16,8]{1,0:T(8,128)S(1)}, u32[]{:S(2)}, u32[]{:S(2)}) collective-permute-start(f32[16,8]{1,0:T(8,128)S(1)} %slice_select_fusion.1), channel_id=1, source_target_pairs={{0,1},{1,0},{2,3},{3,2},{4,5},{5,4},{6,7},{7,6},{8,9},{9,8},{10,11... | collective-permute-start | bytes 1544 | tf_op jit(solution)/shard_map/ppermute | solution.py:18
  46.9 3.9 %collective-permute-start.1 = (f32[16,8]{1,0:T(8,128)S(1)}, f32[16,8]{1,0:T(8,128)S(1)}, u32[]{:S(2)}, u32[]{:S(2)}) collective-permute-start(f32[16,8]{1,0:T(8,128)S(1)} %slice_select_fusion.2), channel_id=1, source_target_pairs={{0,1},{1,0},{2,3},{3,2},{4,5},{5,4},{6,7},{7,6},{8,9},{9,8},{10,11... | collective-permute-start | bytes 1544 | tf_op jit(solution)/shard_map/ppermute | solution.py:18
  50.2 4.3 %collective-permute-start.2 = (f32[16,8,128]{2,1,0:T(8,128)S(1)}, f32[16,8,128]{2,1,0:T(8,128)S(1)}, u32[]{:S(2)}, u32[]{:S(2)}) collective-permute-start(f32[16,8,128]{2,1,0:T(8,128)S(1)} %slice_select_fusion), channel_id=1, source_target_pairs={{0,1},{1,0},{2,3},{3,2},{4,5},{5,4},{6,7},{7,6},{8,9},{9,8},{10,11... | collective-permute-start | bytes 196616 | tf_op jit(solution)/shard_map/ppermute | solution.py:18
where the time goes:
time: 55.7 us; the launch traced here: 55.3 us
  waiting for transfers between devices  17.2 us (31%)
  matrix products  10.9 us (20%)
  starting transfers between devices  10.6 us (19%)
  local copies, waits for them, and re-layouts  9.32 us (17%)
  other arithmetic  6.44 us (12%)
  between operations  0.85 us (2%)
    all_to_all x1, waiting for transfers between devices, on_device(): lax.all_to_all(outgoing, 'batch', split_axis=0, concat_axis=0, tiled=True)  13.6 us
    ppermute x4, starting transfers between devices, swapped(): return lax.ppermute(value, axis, pairs)  5.57 us
    dot_general x2, matrix products, partial_softmax(): jnp.dot(weights.astype(jnp.bfloat16), values, preferred_element_type=jnp....  5.2 us
    all_to_all x1, starting transfers between devices, on_device(): lax.all_to_all(outgoing, 'batch', split_axis=0, concat_axis=0, tiled=True)  5.01 us
    dot_general x1, matrix products, on_device(): jnp.einsum('qd,td->qt', vectors, prompt_rows[:, :HD], preferred_element_t...  3.9 us
    reduce_sum x2, other arithmetic, partial_softmax(): total = jnp.sum(weights, axis=-1)  3.72 us
    ppermute x4, waiting for transfers between devices, swapped(): return lax.ppermute(value, axis, pairs)  3.65 us
    reshape x1, local copies, waits for them, and re-layouts, on_device(): keep_suffix = keep_suffix.reshape(vec_rows, n_batch * capacity * half)  3.22 us
  transfers between devices with their start and end apart: 5, of which 2 were waited for; matrix products, arithmetic and copies ran while one was open for 34% of the time, Pallas kernels for 0%

commit v1 on v0

v1 whole, which is shorter than its diff:
```python
import functools

import jax
import jax.numpy as jnp
from jax import lax
from jax.experimental import pallas as pl
from jax.experimental.pallas import tpu as pltpu
from jax.sharding import PartitionSpec as P

HD = 128
GROUP = 16
BEAMS = 16
SUF = 4
HEADS = GROUP // 2
VECS = HEADS * BEAMS
STAT_ROWS = 16
UNIT_ROWS = HD + STAT_ROWS
CHUNK = 512

big_negative = -1e30
to_exp2 = HD ** (-0.5) * 1.4426950408889634


def exchanged(value, z_mask, pair_mask, core_mask=0):
    n_mp = lax.axis_size("mp")
    n_batch = lax.axis_size("batch")
    pairs = []
    for b in range(n_batch):
        for m in range(n_mp):
            other = (b ^ (2 * z_mask + core_mask)) * n_mp + (m ^ pair_mask)
            pairs.append((b * n_mp + m, other))
    return lax.ppermute(value, ("batch", "mp"), pairs)


def stacked_heads(q):
    return jnp.concatenate([q[:, h * HD : (h + 1) * HD] for h in range(HEADS)], axis=0)


def scores_of(keys, vectors):
    return lax.dot_general(
        keys, vectors, (((1,), (1,)), ((), ())), preferred_element_type=jnp.float32
    )


def summed_of(values, weights):
    return lax.dot_general(
        values,
        weights.astype(jnp.bfloat16),
        (((0,), (0,)), ((), ())),
        preferred_element_type=jnp.float32,
    )


def merged(parts):
    top = functools.reduce(jnp.maximum, [p[0] for p in parts])
    total = 0.0
    summed = 0.0
    for part_top, part_total, part_summed in parts:
        factor = jnp.exp2((part_top - top) * to_exp2)
        total = total + part_total * factor
        summed = summed + part_summed * factor
    return top, total, summed


def softmax_part(scores, values):
    top = jnp.max(scores, axis=0, keepdims=True)
    weights = jnp.exp2((scores - top) * to_exp2)
    total = jnp.sum(weights, axis=0, keepdims=True)
    return top, total, summed_of(values, weights)


def three_pieces(x):
    first = x.astype(jnp.bfloat16).astype(jnp.float32)
    rest = x - first
    second = rest.astype(jnp.bfloat16).astype(jnp.float32)
    return [first, second, rest - second]


def store_unit(ref, top, total, summed):
    ref[:HD, :] = summed.astype(jnp.bfloat16)
    rows = three_pieces(top) + three_pieces(total)
    rows.append(jnp.zeros((STAT_ROWS - len(rows), VECS), jnp.float32))
    ref[HD:, :] = jnp.concatenate(rows, axis=0).astype(jnp.bfloat16)


def load_unit(ref):
    stats = ref[HD:, :].astype(jnp.float32)
    top = stats[0:1] + stats[1:2] + stats[2:3]
    total = stats[3:4] + stats[4:5] + stats[5:6]
    return top, total, ref[:HD, :].astype(jnp.float32)


def prompt_kernel(valid_ref, own_ref, pair_ref, prompt_ref, summed_ref, stats_ref):
    vectors = jnp.concatenate([stacked_heads(own_ref[...]), stacked_heads(pair_ref[...])], axis=0)
    valid = valid_ref[0]
    tokens = prompt_ref.shape[0]
    parts = []
    for start in range(0, tokens, CHUNK):
        scores = scores_of(prompt_ref[start : start + CHUNK, :HD], vectors)
        token = lax.broadcasted_iota(jnp.int32, scores.shape, 0)
        scores = jnp.where(token < valid - start, scores, big_negative)
        parts.append(softmax_part(scores, prompt_ref[start : start + CHUNK, HD:]))
        if len(parts) == 2:
            parts = [merged(parts)]
    top, total, summed = merged(parts)
    summed_ref[...] = summed
    stats_ref[...] = jnp.concatenate(
        [top, total, jnp.zeros((6, 2 * VECS), jnp.float32)], axis=0
    )


def gather_kernel(meta_ref, ids_ref, near_ref, far_ref, out_ref, sem):
    n_req, n_slots, half, _ = out_ref.shape
    capacity = n_slots // 2
    z, core = meta_ref[0], meta_ref[1]
    copies = []
    for d in range(n_req):
        request = (z ^ d) * 2 + core
        for k in range(n_slots):
            slot = jnp.maximum(ids_ref[request, k], 0)
            pool = near_ref if k < capacity else far_ref
            copy = pltpu.make_async_copy(pool.at[slot], out_ref.at[d, k], sem.at[d, k])
            copy.start()
            copies.append(copy)
    for copy in copies:
        copy.wait()


def request_part(d, meta_ref, ids_ref, refs_ref, blocks_ref, vectors):
    _, n_slots, half, width = blocks_ref.shape
    capacity = n_slots // 2
    z, core, slots = meta_ref[0], meta_ref[1], meta_ref[2]
    request = (z ^ d) * 2 + core
    wanted = refs_ref[request]
    blocks = blocks_ref[d].reshape(n_slots * half, width)
    scores = scores_of(blocks[:, :HD], vectors)
    pieces = []
    for k in range(n_slots):
        slot = ids_ref[request, k]
        holder = z * 2 + (core if k < capacity else 1 - core)
        block = jnp.where(slot < 0, -1, holder * slots + slot)
        member = jnp.max((wanted == block).astype(jnp.int32), axis=0, keepdims=True) > 0
        piece = scores[k * half : (k + 1) * half]
        pieces.append(jnp.where(member, piece, big_negative))
    scores = jnp.concatenate(pieces, axis=0)
    return softmax_part(scores, blocks[:, HD:])


def away_kernel(n_req, meta_ref, ids_ref, refs_ref, blocks_ref, *rest):
    queries, outs = rest[: 2 * (n_req - 1)], rest[2 * (n_req - 1) :]
    for d in range(1, n_req):
        own_ref, pair_ref = queries[2 * (d - 1) : 2 * d]
        vectors = jnp.concatenate(
            [stacked_heads(own_ref[...]), stacked_heads(pair_ref[...])], axis=0
        )
        top, total, summed = request_part(d, meta_ref, ids_ref, refs_ref, blocks_ref, vectors)
        for side in range(2):
            lanes = slice(side * VECS, (side + 1) * VECS)
            store_unit(
                outs[2 * (d - 1) + side], top[:, lanes], total[:, lanes], summed[:, lanes]
            )


def home_kernel(
    meta_ref, ids_ref, refs_ref, blocks_ref, own_ref, pair_ref, summed_ref, stats_ref,
    kept_ref, kept_stats_ref, given_ref,
):
    vectors = jnp.concatenate([stacked_heads(own_ref[...]), stacked_heads(pair_ref[...])], axis=0)
    suffix = request_part(0, meta_ref, ids_ref, refs_ref, blocks_ref, vectors)
    prompt = (stats_ref[0:1], stats_ref[1:2], summed_ref[...])
    top, total, summed = merged([prompt, suffix])
    kept_ref[...] = summed[:, :VECS]
    kept_stats_ref[...] = jnp.concatenate(
        [top[:, :VECS], total[:, :VECS], jnp.zeros((6, VECS), jnp.float32)], axis=0
    )
    store_unit(given_ref, top[:, VECS:], total[:, VECS:], summed[:, VECS:])


def final_kernel(kept_ref, kept_stats_ref, *rest):
    units, out_ref = rest[:-1], rest[-1]
    parts = [(kept_stats_ref[0:1], kept_stats_ref[1:2], kept_ref[...])]
    parts += [load_unit(unit) for unit in units]
    _, total, summed = merged(parts)
    attended = (summed / total).T
    for h in range(HEADS):
        out_ref[:, h * HD : (h + 1) * HD] = attended[h * BEAMS : (h + 1) * BEAMS]


def slots_of(block_table, n_batch, slots, capacity, z, core):
    entries = block_table.reshape(n_batch, 1, 1, BEAMS * SUF)
    holder = jnp.stack([z * 2 + core, z * 2 + 1 - core]).reshape(1, 2, 1, 1)
    slot = jnp.arange(slots, dtype=jnp.int32).reshape(1, 1, slots, 1)
    hit = jnp.any(entries == holder * slots + slot, axis=3)
    order = jnp.arange(slots, dtype=jnp.int32)
    before = (order[None, :] < order[:, None])[None, None]
    rank = jnp.sum((hit[:, :, None, :] & before).astype(jnp.int32), axis=3)
    index = jnp.arange(capacity, dtype=jnp.int32).reshape(1, 1, capacity, 1)
    chosen = hit[:, :, None, :] & (rank[:, :, None, :] == index)
    found = jnp.sum(jnp.where(chosen, order + 1, 0), axis=3) - 1
    return found.reshape(n_batch, 2 * capacity)


def on_device(queries, prompt_cache, pool, block_table, parents, lengths):
    n_batch = lax.axis_size("batch")
    myself = lax.axis_index("batch")
    parity = lax.axis_index("mp") % 2
    z, core = myself // 2, myself % 2
    n_req = n_batch // 2
    ndist = 2 ** (SUF + 1) - 2
    capacity = 2 * ((ndist // 2 + n_batch - 1) // n_batch)
    slots, _, half, width = pool.shape
    tokens = prompt_cache.shape[2]
    smem = pl.BlockSpec(memory_space=pltpu.SMEM)
    vmem = pl.BlockSpec(memory_space=pltpu.VMEM)
    anywhere = pl.BlockSpec(memory_space=pl.ANY)
    params = pltpu.CompilerParams(vmem_limit_bytes=40 * 2**20)
    unit = jax.ShapeDtypeStruct((UNIT_ROWS, VECS), jnp.bfloat16)

    other = exchanged(queries, 0, 1)
    sent = []
    for d in range(1, n_req):
        sent += [exchanged(queries, d, 0), exchanged(queries, d, 1)]
    near = pool.reshape(slots, half, width)
    far = exchanged(near, 0, 0, 1)

    meta = jnp.stack([z, core, jnp.int32(slots)]).astype(jnp.int32)
    ids = slots_of(block_table, n_batch, slots, capacity, z, core)
    wanted = block_table[parents].reshape(n_batch, BEAMS, SUF).transpose(0, 2, 1)
    wanted = jnp.tile(wanted, (1, 1, GROUP))

    length = lengths[0]
    valid = length // (2 * half) * half + jnp.clip(length % (2 * half) - parity * half, 0, half)
    summed, stats = pl.pallas_call(
        prompt_kernel,
        out_shape=(
            jax.ShapeDtypeStruct((HD, 2 * VECS), jnp.float32),
            jax.ShapeDtypeStruct((8, 2 * VECS), jnp.float32),
        ),
        in_specs=[smem, vmem, vmem, vmem],
        out_specs=(vmem, vmem),
        compiler_params=params,
        name="prompt_part",
    )(valid.reshape(1), queries, other, prompt_cache.reshape(tokens, width))

    blocks = pl.pallas_call(
        gather_kernel,
        out_shape=jax.ShapeDtypeStruct((n_req, 2 * capacity, half, width), jnp.bfloat16),
        in_specs=[smem, smem, anywhere, anywhere],
        out_specs=anywhere,
        scratch_shapes=[pltpu.SemaphoreType.DMA((n_req, 2 * capacity))],
        name="named_blocks",
    )(meta, ids, near, far)

    units = pl.pallas_call(
        functools.partial(away_kernel, n_req),
        out_shape=(unit,) * (2 * (n_req - 1)),
        in_specs=[smem, smem] + [vmem] * (2 + 2 * (n_req - 1)),
        out_specs=(vmem,) * (2 * (n_req - 1)),
        compiler_params=params,
        name="suffix_away",
    )(meta, ids, wanted, blocks, *sent)
    received = []
    for d in range(1, n_req):
        for side in range(2):
            received.append(exchanged(units[2 * (d - 1) + side], d, side))

    kept, kept_stats, given = pl.pallas_call(
        home_kernel,
        out_shape=(
            jax.ShapeDtypeStruct((HD, VECS), jnp.float32),
            jax.ShapeDtypeStruct((8, VECS), jnp.float32),
            unit,
        ),
        in_specs=[smem, smem] + [vmem] * 6,
        out_specs=(vmem,) * 3,
        compiler_params=params,
        name="suffix_home",
    )(meta, ids, wanted, blocks, queries, other, summed, stats)
    received.append(exchanged(given, 0, 1))

    return pl.pallas_call(
        final_kernel,
        out_shape=jax.ShapeDtypeStruct((BEAMS, HEADS * HD), jnp.float32),
        in_specs=[vmem] * (2 + len(received)),
        out_specs=vmem,
        compiler_params=params,
        name="combine",
    )(kept, kept_stats, *received)


def solution(mesh):
    return jax.shard_map(
        on_device,
        mesh=mesh,
        in_specs=(
            P("batch", "mp"),
            P("batch", "mp", None, None),
            P("batch", "mp", None, None),
            P(),
            P(),
            P("batch"),
        ),
        out_specs=P("batch", "mp"),
        check_vma=False,
    )
```

time: 55.7 us -> 81.2 us (1.46)
  Pallas kernels: 0 us -> 41.7 us
  starting transfers between devices: 10.6 us -> 24.9 us
  matrix products: 10.9 us -> 0 us
  waiting for transfers between devices: 17.2 us -> 6.68 us
  local copies, waits for them, and re-layouts: 9.32 us -> 4.34 us
  other arithmetic: 6.44 us -> 2.44 us
    pallas_call x0 -> x5, Pallas kernels: none -> 41.7 us  [the longest x1 34 us: on_device(): pl.pallas_call(gather_kernel, out_shape=jax.ShapeDtypeStruct((n_req, 2 *...]
    ppermute x4 -> x15, starting transfers between devices: 5.57 us -> 24.9 us  [exchanged(): return lax.ppermute(value, ('batch', 'mp'), pairs)]
    all_to_all x1 -> x0, waiting for transfers between devices: 13.6 us -> none  [on_device(): lax.all_to_all(outgoing, 'batch', split_axis=0, concat_axis=0, tiled=True)]
    dot_general x4 -> x0, matrix products: 10.9 us -> none  [the longest x2 5.2 us: partial_softmax(): jnp.dot(weights.astype(jnp.bfloat16), values, preferred_element_type=jnp....]
    all_to_all x1 -> x0, starting transfers between devices: 5.01 us -> none  [on_device(): lax.all_to_all(outgoing, 'batch', split_axis=0, concat_axis=0, tiled=True)]
    reduce_sum x4 -> x2, other arithmetic: 4.02 us -> 0.59 us  [the longest x1 0.37 us: slots_of(): rank = jnp.sum((hit[:, :, None, :] & before).astype(jnp.int32), axis=3)]
    reshape x2 -> x0, local copies, waits for them, and re-layouts: 3.3 us -> none  [the longest x1 3.22 us: on_device(): keep_suffix = keep_suffix.reshape(vec_rows, n_batch * capacity * half)]
    ppermute x4 -> x15, waiting for transfers between devices: 3.65 us -> 6.68 us  [exchanged(): return lax.ppermute(value, ('batch', 'mp'), pairs)]
  transfers between devices with their start and end apart: 5 -> 15, of which waited for: 2 -> 2; matrix products, arithmetic and copies ran while one was open for 34% -> 6% of each run, Pallas kernels for 0% -> 48%
where the time goes in v1:
time: 81.2 us; the launch traced here: 80.9 us
  Pallas kernels  41.7 us (51%)
  starting transfers between devices  24.9 us (31%)
  waiting for transfers between devices  6.68 us (8%)
  local copies, waits for them, and re-layouts  4.34 us (5%)
  other arithmetic  2.44 us (3%)
  between operations  0.89 us (1%)
    pallas_call x1, Pallas kernels, on_device(): pl.pallas_call(gather_kernel, out_shape=jax.ShapeDtypeStruct((n_req, 2 *...  34 us
    ppermute x15, starting transfers between devices, exchanged(): return lax.ppermute(value, ('batch', 'mp'), pairs)  24.9 us
    ppermute x15, waiting for transfers between devices, exchanged(): return lax.ppermute(value, ('batch', 'mp'), pairs)  6.68 us
    pallas_call x1, Pallas kernels, on_device(): pl.pallas_call(prompt_kernel, out_shape=(jax.ShapeDtypeStruct((HD, 2 * VE...  3.51 us
    unnamed x19, local copies, waits for them, and re-layouts  2.64 us
    pallas_call x1, Pallas kernels, on_device(): pl.pallas_call(functools.partial(away_kernel, n_req), out_shape=(unit,) *...  2.24 us
  transfers between devices with their start and end apart: 15, of which 2 were waited for; matrix products, arithmetic and copies ran while one was open for 6% of the time, Pallas kernels for 48%

profile of v1, /device:TPU:0, one launch (start us, length us, event | category | flops | bytes accessed | tf_op | source)
XLA Modules:
  0.0 80.9 jit_solution(9271016555727205923)
XLA Ops:
  0.0 3.0 %collective-permute-start.2 = (bf16[16,1024]{1,0:T(8,128)(2,1)}, bf16[16,1024]{1,0:T(8,128)(2,1)S(1)}, u32[]{:S(2)}, u32[]{:S(2)}) collective-permute-start(bf16[16,1024]{1,0:T(8,128)(2,1)} %own_ref.3), channel_id=1, source_target_pairs={{0,8},{1,9},{2,10},{3,11},{4,12},{5,13},{6,14},{7,15},{8,0},{9,1},... | collective-permute-start | bytes 98312 | tf_op jit(solution)/shard_map/ppermute | solution.py:32
  3.0 1.4 %collective-permute-start.3 = (bf16[16,1024]{1,0:T(8,128)(2,1)}, bf16[16,1024]{1,0:T(8,128)(2,1)S(1)}, u32[]{:S(2)}, u32[]{:S(2)}) collective-permute-start(bf16[16,1024]{1,0:T(8,128)(2,1)} %own_ref.3), channel_id=1, source_target_pairs={{0,9},{1,8},{2,11},{3,10},{4,13},{5,12},{6,15},{7,14},{8,1},{9,0},... | collective-permute-start | bytes 98312 | tf_op jit(solution)/shard_map/ppermute | solution.py:32
  4.4 2.6 %collective-permute-start.4 = (bf16[16,1024]{1,0:T(8,128)(2,1)}, bf16[16,1024]{1,0:T(8,128)(2,1)S(1)}, u32[]{:S(2)}, u32[]{:S(2)}) collective-permute-start(bf16[16,1024]{1,0:T(8,128)(2,1)} %own_ref.3), channel_id=1, source_target_pairs={{0,16},{1,17},{2,18},{3,19},{4,20},{5,21},{6,22},{7,23},{8,24},{9,... | collective-permute-start | bytes 98312 | tf_op jit(solution)/shard_map/ppermute | solution.py:32
  7.1 0.8 copy.18
  9.1 0.7 compare_select_fusion
  9.8 4.0 %collective-permute-start.6 = (bf16[16,1024]{1,0:T(8,128)(2,1)}, bf16[16,1024]{1,0:T(8,128)(2,1)S(1)}, u32[]{:S(2)}, u32[]{:S(2)}) collective-permute-start(bf16[16,1024]{1,0:T(8,128)(2,1)} %own_ref.3), channel_id=1, source_target_pairs={{0,24},{1,25},{2,26},{3,27},{4,28},{5,29},{6,30},{7,31},{8,16},{9,... | collective-permute-start | bytes 98312 | tf_op jit(solution)/shard_map/ppermute | solution.py:32
  13.8 1.2 %collective-permute-start.7 = (bf16[16,1024]{1,0:T(8,128)(2,1)}, bf16[16,1024]{1,0:T(8,128)(2,1)S(1)}, u32[]{:S(2)}, u32[]{:S(2)}) collective-permute-start(bf16[16,1024]{1,0:T(8,128)(2,1)} %own_ref.3), channel_id=1, source_target_pairs={{0,25},{1,24},{2,27},{3,26},{4,29},{5,28},{6,31},{7,30},{8,17},{9,... | collective-permute-start | bytes 98312 | tf_op jit(solution)/shard_map/ppermute | solution.py:32
  15.5 0.7 copy.24.ids_ref
  16.2 0.6 gather_fusion
  17.2 34.0 %named_blocks.1.blocks_ref = bf16[4,8,64,256]{3,2,1,0:T(8,128)(2,1)} custom-call(s32[3]{0:T(128)} %pad_add_fusion.meta_ref, s32[8,8]{1,0:T(8,128)} %copy.24.ids_ref, bf16[32,64,256]{2,1,0:T(8,128)(2,1)} %bitcast.20, bf16[32,64,256]{2,1,0:T(8,128)(2,1)} %copy-done.8), custom_call_target="tpu_custom_call" | custom-call | tf_op jit(solution)/shard_map/named_blocks/pallas_call | solution.py:245
  51.3 1.2 %copy-done = bf16[4,8,64,256]{3,2,1,0:T(8,128)(2,1)S(1)} copy-done((bf16[4,8,64,256]{3,2,1,0:T(8,128)(2,1)S(1)}, bf16[4,8,64,256]{3,2,1,0:T(8,128)(2,1)}, u32[]{:S(2)}) %copy-start) | copy-done | bytes 1048600
  52.5 2.2 %suffix_away.1 = (bf16[144,128]{1,0:T(8,128)(2,1)}, bf16[144,128]{1,0:T(8,128)(2,1)}, bf16[144,128]{1,0:T(8,128)(2,1)S(1)}, bf16[144,128]{1,0:T(8,128)(2,1)S(1)}...) custom-call(s32[3]{0:T(128)S(1)} %copy-done.5, s32[8,8]{1,0:T(8,128)S(1)} %copy-done.4, ...), custom_call_target="tpu_custom_call" | custom-call | tf_op jit(solution)/shard_map/suffix_away/pallas_call | solution.py:254
  54.7 0.6 copy-done.6
  55.3 2.0 %collective-permute-start.9 = (bf16[144,128]{1,0:T(8,128)(2,1)}, bf16[144,128]{1,0:T(8,128)(2,1)S(1)}, u32[]{:S(2)}, u32[]{:S(2)}) collective-permute-start(bf16[144,128]{1,0:T(8,128)(2,1)} %get-tuple-element.21), channel_id=1, source_target_pairs={{0,9},{1,8},{2,11},{3,10},{4,13},{5,12},{6,15},{7,14},{8,1},{9,0},... | collective-permute-start | bytes 110600 | tf_op jit(solution)/shard_map/ppermute | solution.py:32
  57.3 1.5 %collective-permute-start.1 = (bf16[16,1024]{1,0:T(8,128)(2,1)S(1)}, bf16[16,1024]{1,0:T(8,128)(2,1)S(1)}, u32[]{:S(2)}, u32[]{:S(2)}) collective-permute-start(bf16[16,1024]{1,0:T(8,128)(2,1)S(1)} %copy-done.3), channel_id=1, source_target_pairs={{0,1},{1,0},{2,3},{3,2},{4,5},{5,4},{6,7},{7,6},{8,9},{9,8},{10,11... | collective-permute-start | bytes 98312 | tf_op jit(solution)/shard_map/ppermute | solution.py:32
  59.5 1.7 %collective-permute-done.1.pair_ref = bf16[16,1024]{1,0:T(8,128)(2,1)S(1)} collective-permute-done((bf16[16,1024]{1,0:T(8,128)(2,1)S(1)}, bf16[16,1024]{1,0:T(8,128)(2,1)S(1)}, u32[]{:S(2)}, u32[]{:S(2)}) %collective-permute-start.1) | collective-permute-done | bytes 32800 | tf_op jit(solution)/shard_map/ppermute | solution.py:32
  61.2 3.5 %prompt_part.1 = (f32[128,256]{1,0:T(8,128)S(1)}, f32[8,256]{1,0:T(8,128)S(1)}) custom-call(s32[1]{0:T(128)} %bitcast.9.valid_ref, bf16[16,1024]{1,0:T(8,128)(2,1)S(1)} %copy-done.3, bf16[16,1024]{1,0:T(8,128)(2,1)S(1)} %collective-permute-done.1.pair_ref, bf16[4096,256]{1,0:T(8,128)(2,1)S(1)} %bitcast.18), custom_call_target="tpu_custom_call" | custom-call | tf_op jit(solution)/shard_map/prompt_part/pallas_call | solution.py:233
  64.8 2.4 %collective-permute-start.10 = (bf16[144,128]{1,0:T(8,128)(2,1)S(1)}, bf16[144,128]{1,0:T(8,128)(2,1)S(1)}, u32[]{:S(2)}, u32[]{:S(2)}) collective-permute-start(bf16[144,128]{1,0:T(8,128)(2,1)S(1)} %copy-done.7), channel_id=1, source_target_pairs={{0,16},{1,17},{2,18},{3,19},{4,20},{5,21},{6,22},{7,23},{8,24},{9,... | collective-permute-start | bytes 110600 | tf_op jit(solution)/shard_map/ppermute | solution.py:32
  67.2 1.5 %collective-permute-start.11 = (bf16[144,128]{1,0:T(8,128)(2,1)S(1)}, bf16[144,128]{1,0:T(8,128)(2,1)S(1)}, u32[]{:S(2)}, u32[]{:S(2)}) collective-permute-start(bf16[144,128]{1,0:T(8,128)(2,1)S(1)} %get-tuple-element.23), channel_id=1, source_target_pairs={{0,17},{1,16},{2,19},{3,18},{4,21},{5,20},{6,23},{7,22},{8,25},{9,... | collective-permute-start | bytes 110600 | tf_op jit(solution)/shard_map/ppermute | solution.py:32
  68.7 3.6 %collective-permute-start.12 = (bf16[144,128]{1,0:T(8,128)(2,1)S(1)}, bf16[144,128]{1,0:T(8,128)(2,1)S(1)}, u32[]{:S(2)}, u32[]{:S(2)}) collective-permute-start(bf16[144,128]{1,0:T(8,128)(2,1)S(1)} %get-tuple-element.24), channel_id=1, source_target_pairs={{0,24},{1,25},{2,26},{3,27},{4,28},{5,29},{6,30},{7,31},{8,16},{9,... | collective-permute-start | bytes 110600 | tf_op jit(solution)/shard_map/ppermute | solution.py:32
  72.3 1.1 %suffix_home.1 = (f32[128,128]{1,0:T(8,128)S(1)}, f32[8,128]{1,0:T(8,128)S(1)}, bf16[144,128]{1,0:T(8,128)(2,1)S(1)}) custom-call(s32[3]{0:T(128)S(1)} %copy-done.5, s32[8,8]{1,0:T(8,128)S(1)} %copy-done.4, s32[8,4,256]{2,1,0:T(4,128)S(1)} %tile.10.refs_ref, bf16[4,8,64,256]{3,2,1,0:T(8,128)(2,1)S(1)} %copy-done.1, bf16[16,1024]{1,0:T(8,128)(2,1)S(1)} %copy-done.3, ...), custom_call_target="tpu_custom_call" | custom-call | tf_op jit(solution)/shard_map/suffix_home/pallas_call | solution.py:267
  73.7 1.5 %collective-permute-start.14 = (bf16[144,128]{1,0:T(8,128)(2,1)S(1)}, bf16[144,128]{1,0:T(8,128)(2,1)S(1)}, u32[]{:S(2)}, u32[]{:S(2)}) collective-permute-start(bf16[144,128]{1,0:T(8,128)(2,1)S(1)} %get-tuple-element.26), channel_id=1, source_target_pairs={{0,1},{1,0},{2,3},{3,2},{4,5},{5,4},{6,7},{7,6},{8,9},{9,8},{10,11... | collective-permute-start | bytes 110600 | tf_op jit(solution)/shard_map/ppermute | solution.py:32
  75.2 4.9 %collective-permute-done.13.rest_5_ = bf16[144,128]{1,0:T(8,128)(2,1)S(1)} collective-permute-done((bf16[144,128]{1,0:T(8,128)(2,1)S(1)}, bf16[144,128]{1,0:T(8,128)(2,1)S(1)}, u32[]{:S(2)}, u32[]{:S(2)}) %collective-permute-start.13) | collective-permute-done | bytes 36896 | tf_op jit(solution)/shard_map/ppermute | solution.py:32
  80.2 0.8 combine.1
  (49 shorter events, 2.5 us)
Async XLA Ops:
  0.0 9.8 %collective-permute-start.2 = (bf16[16,1024]{1,0:T(8,128)(2,1)}, bf16[16,1024]{1,0:T(8,128)(2,1)S(1)}, u32[]{:S(2)}, u32[]{:S(2)}) collective-permute-start(bf16[16,1024]{1,0:T(8,128)(2,1)} %own_ref.3), channel_id=1, source_target_pairs={{0,8},{1,9},{2,10},{3,11},{4,12},{5,13},{6,14},{7,15},{8,0},{9,1},... | collective-permute-start | bytes 98312 | tf_op jit(solution)/shard_map/ppermute | solution.py:32
  3.0 48.2 %collective-permute-start.3 = (bf16[16,1024]{1,0:T(8,128)(2,1)}, bf16[16,1024]{1,0:T(8,128)(2,1)S(1)}, u32[]{:S(2)}, u32[]{:S(2)}) collective-permute-start(bf16[16,1024]{1,0:T(8,128)(2,1)} %own_ref.3), channel_id=1, source_target_pairs={{0,9},{1,8},{2,11},{3,10},{4,13},{5,12},{6,15},{7,14},{8,1},{9,0},... | collective-permute-start | bytes 98312 | tf_op jit(solution)/shard_map/ppermute | solution.py:32
  4.4 46.8 %collective-permute-start.4 = (bf16[16,1024]{1,0:T(8,128)(2,1)}, bf16[16,1024]{1,0:T(8,128)(2,1)S(1)}, u32[]{:S(2)}, u32[]{:S(2)}) collective-permute-start(bf16[16,1024]{1,0:T(8,128)(2,1)} %own_ref.3), channel_id=1, source_target_pairs={{0,16},{1,17},{2,18},{3,19},{4,20},{5,21},{6,22},{7,23},{8,24},{9,... | collective-permute-start | bytes 98312 | tf_op jit(solution)/shard_map/ppermute | solution.py:32
  7.0 44.2 %collective-permute-start.5 = (bf16[16,1024]{1,0:T(8,128)(2,1)}, bf16[16,1024]{1,0:T(8,128)(2,1)S(1)}, u32[]{:S(2)}, u32[]{:S(2)}) collective-permute-start(bf16[16,1024]{1,0:T(8,128)(2,1)} %own_ref.3), channel_id=1, source_target_pairs={{0,17},{1,16},{2,19},{3,18},{4,21},{5,20},{6,23},{7,22},{8,25},{9,... | collective-permute-start | bytes 98312 | tf_op jit(solution)/shard_map/ppermute | solution.py:32
  7.0 6.8 %collective-permute-start = (bf16[32,64,256]{2,1,0:T(8,128)(2,1)}, bf16[32,64,256]{2,1,0:T(8,128)(2,1)S(1)}, u32[]{:S(2)}, u32[]{:S(2)}) collective-permute-start(bf16[32,64,256]{2,1,0:T(8,128)(2,1)} %bitcast.19), channel_id=1, source_target_pairs={{0,4},{1,5},{2,6},{3,7},{4,0},{5,1},{6,2},{7,3},{8,12},{9,13},{10,... | collective-permute-start | bytes 3145736 | tf_op jit(solution)/shard_map/ppermute | solution.py:32
  9.8 41.4 %collective-permute-start.6 = (bf16[16,1024]{1,0:T(8,128)(2,1)}, bf16[16,1024]{1,0:T(8,128)(2,1)S(1)}, u32[]{:S(2)}, u32[]{:S(2)}) collective-permute-start(bf16[16,1024]{1,0:T(8,128)(2,1)} %own_ref.3), channel_id=1, source_target_pairs={{0,24},{1,25},{2,26},{3,27},{4,28},{5,29},{6,30},{7,31},{8,16},{9,... | collective-permute-start | bytes 98312 | tf_op jit(solution)/shard_map/ppermute | solution.py:32
  13.8 3.1 %copy-start.8 = (bf16[32,64,256]{2,1,0:T(8,128)(2,1)}, bf16[32,64,256]{2,1,0:T(8,128)(2,1)S(1)}, u32[]{:S(2)}) copy-start(bf16[32,64,256]{2,1,0:T(8,128)(2,1)S(1)} %collective-permute-done.far_ref) | copy-start | bytes 3145732
  13.8 37.5 %collective-permute-start.7 = (bf16[16,1024]{1,0:T(8,128)(2,1)}, bf16[16,1024]{1,0:T(8,128)(2,1)S(1)}, u32[]{:S(2)}, u32[]{:S(2)}) collective-permute-start(bf16[16,1024]{1,0:T(8,128)(2,1)} %own_ref.3), channel_id=1, source_target_pairs={{0,25},{1,24},{2,27},{3,26},{4,29},{5,28},{6,31},{7,30},{8,17},{9,... | collective-permute-start | bytes 98312 | tf_op jit(solution)/shard_map/ppermute | solution.py:32
  16.2 35.1 %copy-start.4 = (s32[8,8]{1,0:T(8,128)S(1)}, s32[8,8]{1,0:T(8,128)}, u32[]{:S(2)}) copy-start(s32[8,8]{1,0:T(8,128)} %copy.24.ids_ref) | copy-start | bytes 772
  16.2 35.1 %copy-start.5 = (s32[3]{0:T(128)S(1)}, s32[3]{0:T(128)}, u32[]{:S(2)}) copy-start(s32[3]{0:T(128)} %pad_add_fusion.meta_ref) | copy-start | bytes 40
  17.1 40.2 %copy-start.3 = (bf16[16,1024]{1,0:T(8,128)(2,1)S(1)}, bf16[16,1024]{1,0:T(8,128)(2,1)}, u32[]{:S(2)}) copy-start(bf16[16,1024]{1,0:T(8,128)(2,1)} %own_ref.3) | copy-start | bytes 98308
  17.1 44.1 %copy-start.2 = (bf16[1,1,4096,256]{3,2,1,0:T(8,128)(2,1)S(1)}, bf16[1,1,4096,256]{3,2,1,0:T(8,128)(2,1)}, u32[]{:S(2)}) copy-start(bf16[1,1,4096,256]{3,2,1,0:T(8,128)(2,1)} %param.7) | copy-start | bytes 6291460
  51.3 1.2 %copy-start = (bf16[4,8,64,256]{3,2,1,0:T(8,128)(2,1)S(1)}, bf16[4,8,64,256]{3,2,1,0:T(8,128)(2,1)}, u32[]{:S(2)}) copy-start(bf16[4,8,64,256]{3,2,1,0:T(8,128)(2,1)} %named_blocks.1.blocks_ref) | copy-start | bytes 3145732
  52.5 19.8 %copy-start.1 = (bf16[4,8,64,256]{3,2,1,0:T(8,128)(2,1)S(1)}, bf16[4,8,64,256]{3,2,1,0:T(8,128)(2,1)}, u32[]{:S(2)}) copy-start(bf16[4,8,64,256]{3,2,1,0:T(8,128)(2,1)} %named_blocks.1.blocks_ref) | copy-start | bytes 3145732
  54.7 0.6 copy-start.6
  55.3 9.4 %copy-start.7 = (bf16[144,128]{1,0:T(8,128)(2,1)S(1)}, bf16[144,128]{1,0:T(8,128)(2,1)}, u32[]{:S(2)}) copy-start(bf16[144,128]{1,0:T(8,128)(2,1)} %copy-done.6) | copy-start | bytes 110596
  55.3 18.1 %collective-permute-start.8 = (bf16[144,128]{1,0:T(8,128)(2,1)}, bf16[144,128]{1,0:T(8,128)(2,1)S(1)}, u32[]{:S(2)}, u32[]{:S(2)}) collective-permute-start(bf16[144,128]{1,0:T(8,128)(2,1)} %get-tuple-element.20), channel_id=1, source_target_pairs={{0,8},{1,9},{2,10},{3,11},{4,12},{5,13},{6,14},{7,15},{8,0},{9,1},... | collective-permute-start | bytes 110600 | tf_op jit(solution)/shard_map/ppermute | solution.py:32
  55.3 18.3 %collective-permute-start.9 = (bf16[144,128]{1,0:T(8,128)(2,1)}, bf16[144,128]{1,0:T(8,128)(2,1)S(1)}, u32[]{:S(2)}, u32[]{:S(2)}) collective-permute-start(bf16[144,128]{1,0:T(8,128)(2,1)} %get-tuple-element.21), channel_id=1, source_target_pairs={{0,9},{1,8},{2,11},{3,10},{4,13},{5,12},{6,15},{7,14},{8,1},{9,0},... | collective-permute-start | bytes 110600 | tf_op jit(solution)/shard_map/ppermute | solution.py:32
  57.3 3.9 %collective-permute-start.1 = (bf16[16,1024]{1,0:T(8,128)(2,1)S(1)}, bf16[16,1024]{1,0:T(8,128)(2,1)S(1)}, u32[]{:S(2)}, u32[]{:S(2)}) collective-permute-start(bf16[16,1024]{1,0:T(8,128)(2,1)S(1)} %copy-done.3), channel_id=1, source_target_pairs={{0,1},{1,0},{2,3},{3,2},{4,5},{5,4},{6,7},{7,6},{8,9},{9,8},{10,11... | collective-permute-start | bytes 98312 | tf_op jit(solution)/shard_map/ppermute | solution.py:32
  64.8 10.5 %collective-permute-start.10 = (bf16[144,128]{1,0:T(8,128)(2,1)S(1)}, bf16[144,128]{1,0:T(8,128)(2,1)S(1)}, u32[]{:S(2)}, u32[]{:S(2)}) collective-permute-start(bf16[144,128]{1,0:T(8,128)(2,1)S(1)} %copy-done.7), channel_id=1, source_target_pairs={{0,16},{1,17},{2,18},{3,19},{4,20},{5,21},{6,22},{7,23},{8,24},{9,... | collective-permute-start | bytes 110600 | tf_op jit(solution)/shard_map/ppermute | solution.py:32
  67.2 8.0 %collective-permute-start.11 = (bf16[144,128]{1,0:T(8,128)(2,1)S(1)}, bf16[144,128]{1,0:T(8,128)(2,1)S(1)}, u32[]{:S(2)}, u32[]{:S(2)}) collective-permute-start(bf16[144,128]{1,0:T(8,128)(2,1)S(1)} %get-tuple-element.23), channel_id=1, source_target_pairs={{0,17},{1,16},{2,19},{3,18},{4,21},{5,20},{6,23},{7,22},{8,25},{9,... | collective-permute-start | bytes 110600 | tf_op jit(solution)/shard_map/ppermute | solution.py:32
  68.7 6.5 %collective-permute-start.12 = (bf16[144,128]{1,0:T(8,128)(2,1)S(1)}, bf16[144,128]{1,0:T(8,128)(2,1)S(1)}, u32[]{:S(2)}, u32[]{:S(2)}) collective-permute-start(bf16[144,128]{1,0:T(8,128)(2,1)S(1)} %get-tuple-element.24), channel_id=1, source_target_pairs={{0,24},{1,25},{2,26},{3,27},{4,28},{5,29},{6,30},{7,31},{8,16},{9,... | collective-permute-start | bytes 110600 | tf_op jit(solution)/shard_map/ppermute | solution.py:32
  73.4 6.7 %collective-permute-start.13 = (bf16[144,128]{1,0:T(8,128)(2,1)S(1)}, bf16[144,128]{1,0:T(8,128)(2,1)S(1)}, u32[]{:S(2)}, u32[]{:S(2)}) collective-permute-start(bf16[144,128]{1,0:T(8,128)(2,1)S(1)} %get-tuple-element.25), channel_id=1, source_target_pairs={{0,25},{1,24},{2,27},{3,26},{4,29},{5,28},{6,31},{7,30},{8,17},{9,... | collective-permute-start | bytes 110600 | tf_op jit(solution)/shard_map/ppermute | solution.py:32
  73.7 6.5 %collective-permute-start.14 = (bf16[144,128]{1,0:T(8,128)(2,1)S(1)}, bf16[144,128]{1,0:T(8,128)(2,1)S(1)}, u32[]{:S(2)}, u32[]{:S(2)}) collective-permute-start(bf16[144,128]{1,0:T(8,128)(2,1)S(1)} %get-tuple-element.26), channel_id=1, source_target_pairs={{0,1},{1,0},{2,3},{3,2},{4,5},{5,4},{6,7},{7,6},{8,9},{9,8},{10,11... | collective-permute-start | bytes 110600 | tf_op jit(solution)/shard_map/ppermute | solution.py:32

commit v2 on v1

v2 whole, which is shorter than its diff:
```python
import functools

import jax
import jax.numpy as jnp
from jax import lax
from jax.experimental import pallas as pl
from jax.experimental.pallas import tpu as pltpu
from jax.sharding import PartitionSpec as P

HD = 128
GROUP = 16
BEAMS = 16
SUF = 4
HEADS = GROUP // 2
VECS = HEADS * BEAMS
STAT_ROWS = 16
UNIT_ROWS = HD + STAT_ROWS
CHUNK = 512

big_negative = -1e30
to_exp2 = HD ** (-0.5) * 1.4426950408889634


def swapped(value, axis):
    return lax.ppermute(value, axis, [(0, 1), (1, 0)])


def stacked_heads(q):
    return jnp.concatenate([q[:, h * HD : (h + 1) * HD] for h in range(HEADS)], axis=0)


def scores_of(keys, vectors):
    return lax.dot_general(
        keys, vectors, (((1,), (1,)), ((), ())), preferred_element_type=jnp.float32
    )


def summed_of(values, weights):
    return lax.dot_general(
        values,
        weights.astype(jnp.bfloat16),
        (((0,), (0,)), ((), ())),
        preferred_element_type=jnp.float32,
    )


def merged(parts):
    top = functools.reduce(jnp.maximum, [p[0] for p in parts])
    total = 0.0
    summed = 0.0
    for part_top, part_total, part_summed in parts:
        factor = jnp.exp2((part_top - top) * to_exp2)
        total = total + part_total * factor
        summed = summed + part_summed * factor
    return top, total, summed


def softmax_part(scores, values):
    top = jnp.max(scores, axis=0, keepdims=True)
    weights = jnp.exp2((scores - top) * to_exp2)
    total = jnp.sum(weights, axis=0, keepdims=True)
    return top, total, summed_of(values, weights)


def three_pieces(x):
    first = x.astype(jnp.bfloat16).astype(jnp.float32)
    rest = x - first
    second = rest.astype(jnp.bfloat16).astype(jnp.float32)
    return [first, second, rest - second]


def store_unit(ref, top, total, summed):
    ref[:HD, :] = summed.astype(jnp.bfloat16)
    rows = three_pieces(top) + three_pieces(total)
    rows.append(jnp.zeros((STAT_ROWS - len(rows), VECS), jnp.float32))
    ref[HD:, :] = jnp.concatenate(rows, axis=0).astype(jnp.bfloat16)


def load_unit(ref):
    stats = ref[HD:, :].astype(jnp.float32)
    top = stats[0:1] + stats[1:2] + stats[2:3]
    total = stats[3:4] + stats[4:5] + stats[5:6]
    return top, total, ref[:HD, :].astype(jnp.float32)


def prompt_kernel(valid_ref, own_ref, pair_ref, prompt_ref, summed_ref, stats_ref):
    vectors = jnp.concatenate([stacked_heads(own_ref[...]), stacked_heads(pair_ref[...])], axis=0)
    valid = valid_ref[0]
    tokens = prompt_ref.shape[0]
    parts = []
    for start in range(0, tokens, CHUNK):
        scores = scores_of(prompt_ref[start : start + CHUNK, :HD], vectors)
        token = lax.broadcasted_iota(jnp.int32, scores.shape, 0)
        scores = jnp.where(token < valid - start, scores, big_negative)
        parts.append(softmax_part(scores, prompt_ref[start : start + CHUNK, HD:]))
        if len(parts) == 2:
            parts = [merged(parts)]
    top, total, summed = merged(parts)
    summed_ref[...] = summed
    stats_ref[...] = jnp.concatenate(
        [top, total, jnp.zeros((6, 2 * VECS), jnp.float32)], axis=0
    )


def suffix_kernel(
    meta_ref, ids_ref, refs_ref, near_ref, far_ref, queries_ref, summed_ref, stats_ref, out_ref
):
    n_req = queries_ref.shape[0]
    n_slots = ids_ref.shape[1]
    capacity = n_slots // 2
    slots, half, _ = near_ref.shape
    z, core, parity = meta_ref[0], meta_ref[1], meta_ref[2]
    for d in range(n_req):
        target = z ^ d
        request = target * 2 + core
        vectors = jnp.concatenate(
            [
                stacked_heads(queries_ref[target, parity]),
                stacked_heads(queries_ref[target, 1 - parity]),
            ],
            axis=0,
        )
        wanted = refs_ref[request]
        blocks, biases = [], []
        for k in range(n_slots):
            slot = ids_ref[request, k]
            pool_ref = near_ref if k < capacity else far_ref
            blocks.append(pool_ref[jnp.maximum(slot, 0)])
            holder = z * 2 + (core if k < capacity else 1 - core)
            block = jnp.where(slot < 0, -1, holder * slots + slot)
            member = jnp.max((wanted == block).astype(jnp.int32), axis=0, keepdims=True) > 0
            biases.append(member)
        blocks = jnp.concatenate(blocks, axis=0)
        scores = scores_of(blocks[:, :HD], vectors)
        scores = jnp.concatenate(
            [
                jnp.where(member, scores[k * half : (k + 1) * half], big_negative)
                for k, member in enumerate(biases)
            ],
            axis=0,
        )
        part = softmax_part(scores, blocks[:, HD:])
        if d == 0:
            part = merged([part, (stats_ref[0:1], stats_ref[1:2], summed_ref[...])])
        top, total, summed = part
        for side in range(2):
            lanes = slice(side * VECS, (side + 1) * VECS)
            owner = parity if side == 0 else 1 - parity
            store_unit(
                out_ref.at[target, owner], top[:, lanes], total[:, lanes], summed[:, lanes]
            )


def final_kernel(units_ref, out_ref):
    n_req, n_pair = units_ref.shape[:2]
    parts = [load_unit(units_ref.at[r, p]) for r in range(n_req) for p in range(n_pair)]
    _, total, summed = merged(parts)
    attended = (summed / total).T
    for h in range(HEADS):
        out_ref[:, h * HD : (h + 1) * HD] = attended[h * BEAMS : (h + 1) * BEAMS]


def slots_of(block_table, n_batch, slots, capacity, z, core):
    entries = block_table.reshape(n_batch, 1, 1, BEAMS * SUF)
    holder = jnp.stack([z * 2 + core, z * 2 + 1 - core]).reshape(1, 2, 1, 1)
    slot = jnp.arange(slots, dtype=jnp.int32).reshape(1, 1, slots, 1)
    hit = jnp.any(entries == holder * slots + slot, axis=3)
    order = jnp.arange(slots, dtype=jnp.int32)
    before = (order[None, :] < order[:, None])[None, None]
    rank = jnp.sum((hit[:, :, None, :] & before).astype(jnp.int32), axis=3)
    index = jnp.arange(capacity, dtype=jnp.int32).reshape(1, 1, capacity, 1)
    chosen = hit[:, :, None, :] & (rank[:, :, None, :] == index)
    found = jnp.sum(jnp.where(chosen, order + 1, 0), axis=3) - 1
    return found.reshape(n_batch, 2 * capacity)


def on_device(queries, prompt_cache, pool, block_table, parents, lengths):
    n_req = lax.axis_size("z")
    n_batch = 2 * n_req
    z, core, parity = lax.axis_index("z"), lax.axis_index("core"), lax.axis_index("pair")
    ndist = 2 ** (SUF + 1) - 2
    capacity = 2 * ((ndist // 2 + n_batch - 1) // n_batch)
    slots, _, half, width = pool.shape
    tokens = prompt_cache.shape[2]
    smem = pl.BlockSpec(memory_space=pltpu.SMEM)
    vmem = pl.BlockSpec(memory_space=pltpu.VMEM)
    params = pltpu.CompilerParams(vmem_limit_bytes=40 * 2**20)

    gathered = lax.all_gather(queries, ("z", "pair"), axis=0)
    gathered = gathered.reshape(n_req, 2, BEAMS, HEADS * HD)
    other = swapped(queries, "pair")
    near = pool.reshape(slots, half, width)
    far = swapped(near, "core")

    meta = jnp.stack([z, core, parity]).astype(jnp.int32)
    ids = slots_of(block_table, n_batch, slots, capacity, z, core)
    wanted = block_table[parents].reshape(n_batch, BEAMS, SUF).transpose(0, 2, 1)
    wanted = jnp.tile(wanted, (1, 1, GROUP))

    length = lengths[0]
    valid = length // (2 * half) * half + jnp.clip(length % (2 * half) - parity * half, 0, half)
    summed, stats = pl.pallas_call(
        prompt_kernel,
        out_shape=(
            jax.ShapeDtypeStruct((HD, 2 * VECS), jnp.float32),
            jax.ShapeDtypeStruct((8, 2 * VECS), jnp.float32),
        ),
        in_specs=[smem, vmem, vmem, vmem],
        out_specs=(vmem, vmem),
        compiler_params=params,
        name="prompt_part",
    )(valid.reshape(1), queries, other, prompt_cache.reshape(tokens, width))

    units = pl.pallas_call(
        suffix_kernel,
        out_shape=jax.ShapeDtypeStruct((n_req, 2, UNIT_ROWS, VECS), jnp.bfloat16),
        in_specs=[smem, smem] + [vmem] * 6,
        out_specs=vmem,
        compiler_params=params,
        name="suffix_parts",
    )(meta, ids, wanted, near, far, gathered, summed, stats)
    units = units.reshape(2 * n_req, UNIT_ROWS, VECS)
    units = lax.all_to_all(units, ("z", "pair"), split_axis=0, concat_axis=0, tiled=True)

    return pl.pallas_call(
        final_kernel,
        out_shape=jax.ShapeDtypeStruct((BEAMS, HEADS * HD), jnp.float32),
        in_specs=[vmem],
        out_specs=vmem,
        compiler_params=params,
        name="combine",
    )(units.reshape(n_req, 2, UNIT_ROWS, VECS))


def solution(mesh):
    n_batch, n_mp = mesh.devices.shape
    split = jax.sharding.Mesh(
        mesh.devices.reshape(n_batch // 2, 2, n_mp // 2, 2), ("z", "core", "group", "pair")
    )
    batch, mp = ("z", "core"), ("group", "pair")
    return jax.shard_map(
        on_device,
        mesh=split,
        in_specs=(
            P(batch, mp),
            P(batch, mp, None, None),
            P(batch, mp, None, None),
            P(),
            P(),
            P(batch),
        ),
        out_specs=P(batch, mp),
        check_vma=False,
    )
```

time: 81.2 us -> 61.4 us (0.76)
  blocking collectives: 0 us -> 44.5 us
  Pallas kernels: 41.7 us -> 6.68 us
  starting transfers between devices: 24.9 us -> 2.94 us
  waiting for transfers between devices: 6.68 us -> 0.01 us
    pallas_call x3 -> x1, Pallas kernels: 37.4 us -> 2.38 us  [on_device(): pl.pallas_call(suffix_kernel, out_shape=jax.ShapeDtypeStruct((n_req, 2, U...]
    all_gather x0 -> x1, blocking collectives: none -> 31.5 us  [on_device(): gathered = lax.all_gather(queries, ('z', 'pair'), axis=0)]
    ppermute x15 -> x2, starting transfers between devices: 24.9 us -> 2.94 us  [swapped(): return lax.ppermute(value, axis, [(0, 1), (1, 0)])]
    all_to_all x0 -> x1, blocking collectives: none -> 13 us  [on_device(): lax.all_to_all(units, ('z', 'pair'), split_axis=0, concat_axis=0, tiled=T...]
    ppermute x15 -> x2, waiting for transfers between devices: 6.68 us -> 0.01 us  [swapped(): return lax.ppermute(value, axis, [(0, 1), (1, 0)])]
    unnamed x19 -> x7, local copies, waits for them, and re-layouts: 2.64 us -> 3.13 us
  transfers between devices with their start and end apart: 15 -> 2, of which waited for: 2 -> 0; matrix products, arithmetic and copies ran while one was open for 6% -> 6% of each run, Pallas kernels for 48% -> 6%
where the time goes in v2:
time: 61.4 us; the launch traced here: 61.1 us
  blocking collectives  44.5 us (72%)
  Pallas kernels  6.68 us (11%)
  local copies, waits for them, and re-layouts  4.24 us (7%)
  starting transfers between devices  2.94 us (5%)
  other arithmetic  1.93 us (3%)
  between operations  0.8 us (1%)
    all_gather x1, blocking collectives, on_device(): gathered = lax.all_gather(queries, ('z', 'pair'), axis=0)  31.5 us
    all_to_all x1, blocking collectives, on_device(): lax.all_to_all(units, ('z', 'pair'), split_axis=0, concat_axis=0, tiled=T...  13 us
    pallas_call x1, Pallas kernels, on_device(): pl.pallas_call(prompt_kernel, out_shape=(jax.ShapeDtypeStruct((HD, 2 * VE...  3.52 us
    unnamed x7, local copies, waits for them, and re-layouts  3.13 us
    ppermute x2, starting transfers between devices, swapped(): return lax.ppermute(value, axis, [(0, 1), (1, 0)])  2.94 us
    pallas_call x1, Pallas kernels, on_device(): pl.pallas_call(suffix_kernel, out_shape=jax.ShapeDtypeStruct((n_req, 2, U...  2.38 us
  transfers between devices with their start and end apart: 2, of which 0 were waited for; matrix products, arithmetic and copies ran while one was open for 6% of the time, Pallas kernels for 6%

profile of v2, /device:TPU:0, one launch (start us, length us, event | category | flops | bytes accessed | tf_op | source)
XLA Modules:
  0.0 61.1 jit_solution(733281929803573429)
XLA Ops:
  0.0 2.9 %collective-permute-start.1 = (bf16[16,1024]{1,0:T(8,128)(2,1)}, bf16[16,1024]{1,0:T(8,128)(2,1)S(1)}, u32[]{:S(2)}, u32[]{:S(2)}) collective-permute-start(bf16[16,1024]{1,0:T(8,128)(2,1)} %own_ref.1), channel_id=1, source_target_pairs={{0,1},{1,0},{2,3},{3,2},{4,5},{5,4},{6,7},{7,6},{8,9},{9,8},{10,11... | collective-permute-start | bytes 98312 | tf_op jit(solution)/shard_map/ppermute | solution.py:25
  2.9 0.0 collective-permute-start
  3.0 0.1 add_multiply_fusion
  3.0 0.1 iota_add_fusion
  3.1 0.8 %copy.14 = s32[128,4]{1,0:T(8,128)S(1)} copy(s32[128,4]{0,1:T(4,128)} %param.9) | data formatting | bytes 4096 | tf_op args[3]
  3.9 0.1 eq.30
  4.0 0.4 compare_reduce_fusion
  4.4 0.4 convert_reduce_fusion
  4.8 0.7 %compare_select_fusion = s32[128]{0:T(128)S(1)} fusion(s32[128]{0:T(128)} %param.10), kind=kLoop, calls=%fused_computation.8 | loop fusion | flops 384 | bytes 1024 | tf_op jit(solution)/shard_map/select_n | solution.py:197
  5.5 0.2 select_reduce_fusion
  5.7 31.5 %all-gather = bf16[128,1024]{1,0:T(8,128)(2,1)S(1)} all-gather(bf16[16,1024]{1,0:T(8,128)(2,1)} %own_ref.1), channel_id=2, replica_groups=mesh['z'=4,'core'=2,'group'=2,'pair'=2] {'z','pair'}, dimensions={0}, use_global_device_ids=true | all-gather | bytes 294912 | tf_op jit(solution)/shard_map/all_gather | solution.py:189
  37.3 0.1 pad_add_fusion.meta_ref
  38.0 0.6 %gather_fusion = s32[128,4]{1,0:T(8,128)S(1)} fusion(s32[128,4]{1,0:T(8,128)S(1)} %copy.14, s32[1024]{0:T(1024)S(1)} %pad_clamp_fusion), kind=kCustom, calls=%fused_computation | custom fusion | bytes 4608 | tf_op jit(solution)/shard_map/gather | solution.py:197
  38.7 0.1 copy.18
  38.8 0.1 copy.19.ids_ref
  38.9 0.2 tile.10.refs_ref
  39.0 0.0 collective-permute-done.1.pair_ref
  39.1 0.0 copy-start
  39.1 1.6 %copy-done = bf16[1,1,4096,256]{3,2,1,0:T(8,128)(2,1)S(1)} copy-done((bf16[1,1,4096,256]{3,2,1,0:T(8,128)(2,1)S(1)}, bf16[1,1,4096,256]{3,2,1,0:T(8,128)(2,1)}, u32[]{:S(2)}) %copy-start) | copy-done | bytes 2097176
  40.7 0.8 %copy-done.2 = bf16[16,1024]{1,0:T(8,128)(2,1)S(1)} copy-done((bf16[16,1024]{1,0:T(8,128)(2,1)S(1)}, bf16[16,1024]{1,0:T(8,128)(2,1)}, u32[]{:S(2)}) %copy-start.2) | copy-done | bytes 32792
  41.4 3.5 %prompt_part.1 = (f32[128,256]{1,0:T(8,128)S(1)}, f32[8,256]{1,0:T(8,128)S(1)}) custom-call(s32[1]{0:T(128)} %bitcast.11.valid_ref, bf16[16,1024]{1,0:T(8,128)(2,1)S(1)} %copy-done.2, bf16[16,1024]{1,0:T(8,128)(2,1)S(1)} %collective-permute-done.1.pair_ref, bf16[4096,256]{1,0:T(8,128)(2,1)S(1)} %bitcast.22), custom_call_target="tpu_custom_call" | custom-call | tf_op jit(solution)/shard_map/prompt_part/pallas_call | solution.py:202
  45.0 2.4 %suffix_parts.1 = bf16[4,2,144,128]{3,2,1,0:T(8,128)(2,1)S(1)} custom-call(s32[3]{0:T(128)S(1)} %pad_add_fusion.meta_ref, s32[8,8]{1,0:T(8,128)S(1)} %copy.19.ids_ref, s32[8,4,256]{2,1,0:T(4,128)S(1)} %tile.10.refs_ref, bf16[32,64,256]{2,1,0:T(8,128)(2,1)S(1)} %bitcast.27, bf16[32,64,256]{2,1,0:T(8,128)(2,1)S(1)} %collective-permute-done.far_ref, ...), custom_call_target="tpu_custom_call" | custom-call | tf_op jit(solution)/shard_map/suffix_parts/pallas_call | solution.py:214
  47.3 13.0 %all_to_all.5 = bf16[8,144,128]{2,1,0:T(8,128)(2,1)S(1)} all-to-all(bf16[8,144,128]{2,1,0:T(8,128)(2,1)S(1)} %bitcast.23), channel_id=1, replica_groups=mesh['z'=4,'core'=2,'group'=2,'pair'=2] {'z','pair'}, dimensions={0} | all-to-all | bytes 589824 | tf_op jit(solution)/shard_map/all_to_all | solution.py:223
  60.4 0.8 %combine.1 = f32[16,1024]{1,0:T(8,128)} custom-call(bf16[4,2,144,128]{3,2,1,0:T(8,128)(2,1)S(1)} %bitcast.24), custom_call_target="tpu_custom_call" | custom-call | tf_op jit(solution)/shard_map/combine/pallas_call | solution.py:225
  (11 shorter events, 0.1 us)
Async XLA Ops:
  0.0 44.9 %copy-start.1 = (bf16[32,1,64,256]{3,2,1,0:T(8,128)(2,1)S(1)}, bf16[32,1,64,256]{3,2,1,0:T(8,128)(2,1)}, u32[]{:S(2)}) copy-start(bf16[32,1,64,256]{3,2,1,0:T(8,128)(2,1)} %param.8) | copy-start | bytes 3145732
  0.0 39.0 %collective-permute-start.1 = (bf16[16,1024]{1,0:T(8,128)(2,1)}, bf16[16,1024]{1,0:T(8,128)(2,1)S(1)}, u32[]{:S(2)}, u32[]{:S(2)}) collective-permute-start(bf16[16,1024]{1,0:T(8,128)(2,1)} %own_ref.1), channel_id=1, source_target_pairs={{0,1},{1,0},{2,3},{3,2},{4,5},{5,4},{6,7},{7,6},{8,9},{9,8},{10,11... | collective-permute-start | bytes 98312 | tf_op jit(solution)/shard_map/ppermute | solution.py:25
  2.9 42.0 %collective-permute-start = (bf16[32,64,256]{2,1,0:T(8,128)(2,1)}, bf16[32,64,256]{2,1,0:T(8,128)(2,1)S(1)}, u32[]{:S(2)}, u32[]{:S(2)}) collective-permute-start(bf16[32,64,256]{2,1,0:T(8,128)(2,1)} %bitcast.26), channel_id=1, source_target_pairs={{0,4},{4,0},{1,5},{5,1},{2,6},{6,2},{3,7},{7,3},{8,12},{12,8},{9,1... | collective-permute-start | bytes 3145736 | tf_op jit(solution)/shard_map/ppermute | solution.py:25
  39.1 1.6 %copy-start = (bf16[1,1,4096,256]{3,2,1,0:T(8,128)(2,1)S(1)}, bf16[1,1,4096,256]{3,2,1,0:T(8,128)(2,1)}, u32[]{:S(2)}) copy-start(bf16[1,1,4096,256]{3,2,1,0:T(8,128)(2,1)} %param.7) | copy-start | bytes 6291460
  40.6 0.8 %copy-start.2 = (bf16[16,1024]{1,0:T(8,128)(2,1)S(1)}, bf16[16,1024]{1,0:T(8,128)(2,1)}, u32[]{:S(2)}) copy-start(bf16[16,1024]{1,0:T(8,128)(2,1)} %own_ref.1) | copy-start | bytes 98308

commit v3 on v2

--- a/solution.py
+++ b/solution.py
@@ -186,7 +186,8 @@
     vmem = pl.BlockSpec(memory_space=pltpu.VMEM)
     params = pltpu.CompilerParams(vmem_limit_bytes=40 * 2**20)
 
-    gathered = lax.all_gather(queries, ("z", "pair"), axis=0)
+    copies = jnp.broadcast_to(queries[None], (2 * n_req,) + queries.shape)
+    gathered = lax.all_to_all(copies, ("z", "pair"), split_axis=0, concat_axis=0, tiled=True)
     gathered = gathered.reshape(n_req, 2, BEAMS, HEADS * HD)
     other = swapped(queries, "pair")
     near = pool.reshape(slots, half, width)

time: 61.4 us -> 45.4 us (0.74)
  blocking collectives: 44.5 us -> 16.8 us
  starting transfers between devices: 2.94 us -> 8 us
  local copies, waits for them, and re-layouts: 4.24 us -> 8.19 us
  other arithmetic: 1.93 us -> 3.76 us
  Pallas kernels: 6.68 us -> 7.3 us
    all_gather x1 -> x0, blocking collectives: 31.5 us -> none  [on_device(): gathered = lax.all_gather(queries, ('z', 'pair'), axis=0)]
    all_to_all x0 -> x1, starting transfers between devices: none -> 5.05 us  [on_device(): lax.all_to_all(copies, ('z', 'pair'), split_axis=0, concat_axis=0, tiled=...]
    all_to_all x1, blocking collectives: 13 us -> 16.8 us  [on_device(): lax.all_to_all(units, ('z', 'pair'), split_axis=0, concat_axis=0, tiled=T...]
    another operation x2, local copies, waits for them, and re-layouts: 0.18 us -> 1.83 us  [on_device(): wanted = jnp.tile(wanted, (1, 1, GROUP))]
    broadcast_in_dim x0 -> x1, local copies, waits for them, and re-layouts: none -> 1.53 us  [on_device(): copies = jnp.broadcast_to(queries[None], (2 * n_req,) + queries.shape)]
    transpose x1, local copies, waits for them, and re-layouts: 0.11 us -> 0.95 us  [on_device(): block_table[parents].reshape(n_batch, BEAMS, SUF).transpose(0, 2, 1)]
    unnamed x7 -> x11, local copies, waits for them, and re-layouts: 3.13 us -> 2.34 us
    gather x1, local copies, waits for them, and re-layouts: 0.65 us -> 1.36 us  [on_device(): block_table[parents].reshape(n_batch, BEAMS, SUF).transpose(0, 2, 1)]
  transfers between devices with their start and end apart: 2 -> 3, of which waited for: 0 -> 0; matrix products, arithmetic and copies ran while one was open for 6% -> 23% of each run, Pallas kernels for 6% -> 8%
where the time goes in v3:
time: 45.4 us; the launch traced here: 44.8 us
  blocking collectives  16.8 us (37%)
  local copies, waits for them, and re-layouts  8.19 us (18%)
  starting transfers between devices  8 us (18%)
  Pallas kernels  7.3 us (16%)
  other arithmetic  3.76 us (8%)
  between operations  0.81 us (2%)
    all_to_all x1, blocking collectives, on_device(): lax.all_to_all(units, ('z', 'pair'), split_axis=0, concat_axis=0, tiled=T...  16.8 us
    all_to_all x1, starting transfers between devices, on_device(): lax.all_to_all(copies, ('z', 'pair'), split_axis=0, concat_axis=0, tiled=...  5.05 us
    pallas_call x1, Pallas kernels, on_device(): pl.pallas_call(prompt_kernel, out_shape=(jax.ShapeDtypeStruct((HD, 2 * VE...  3.51 us
    pallas_call x1, Pallas kernels, on_device(): pl.pallas_call(suffix_kernel, out_shape=jax.ShapeDtypeStruct((n_req, 2, U...  3.01 us
    ppermute x2, starting transfers between devices, swapped(): return lax.ppermute(value, axis, [(0, 1), (1, 0)])  2.94 us
    unnamed x11, local copies, waits for them, and re-layouts  2.34 us
    another operation x2, local copies, waits for them, and re-layouts, on_device(): wanted = jnp.tile(wanted, (1, 1, GROUP))  1.83 us
    broadcast_in_dim x1, local copies, waits for them, and re-layouts, on_device(): copies = jnp.broadcast_to(queries[None], (2 * n_req,) + queries.shape)  1.53 us
  transfers between devices with their start and end apart: 3, of which 0 were waited for; matrix products, arithmetic and copies ran while one was open for 23% of the time, Pallas kernels for 8%

profile of v3, /device:TPU:0, one launch (start us, length us, event | category | flops | bytes accessed | tf_op | source)
XLA Modules:
  0.0 44.8 jit_solution(9609870309194819981)
XLA Ops:
  0.0 2.9 %collective-permute-start.1 = (bf16[16,1024]{1,0:T(8,128)(2,1)}, bf16[16,1024]{1,0:T(8,128)(2,1)S(1)}, u32[]{:S(2)}, u32[]{:S(2)}) collective-permute-start(bf16[16,1024]{1,0:T(8,128)(2,1)} %own_ref.1), channel_id=1, source_target_pairs={{0,1},{1,0},{2,3},{3,2},{4,5},{5,4},{6,7},{7,6},{8,9},{9,8},{10,11... | collective-permute-start | bytes 98312 | tf_op jit(solution)/shard_map/ppermute | solution.py:25
  2.9 1.5 %broadcast_in_dim.26 = bf16[8,16,1024]{2,1,0:T(8,128)(2,1)} broadcast(bf16[16,1024]{1,0:T(8,128)(2,1)} %own_ref.1), dimensions={1,2} | broadcast | bytes 294912 | tf_op jit(solution)/shard_map/broadcast_in_dim | solution.py:189
  4.5 5.1 %all-to-all-start = ((bf16[8,16,1024]{2,1,0:T(8,128)(2,1)}), bf16[8,16,1024]{2,1,0:T(8,128)(2,1)S(1)}, u32[]{:S(2)}, u32[]{:S(2)}) async-start(bf16[8,16,1024]{2,1,0:T(8,128)(2,1)} %broadcast_in_dim.26), calls=%async_computation | async-start | bytes 524288 | tf_op jit(solution)/shard_map/all_to_all | solution.py:190
  9.6 0.7 %compare_select_fusion = s32[128]{0:T(128)S(1)} fusion(s32[128]{0:T(128)} %param.10), kind=kLoop, calls=%fused_computation.8 | loop fusion | flops 384 | bytes 1024 | tf_op jit(solution)/shard_map/select_n | solution.py:198
  10.2 0.6 %pad_clamp_fusion = s32[1024]{0:T(1024)} fusion(s32[128]{0:T(128)S(1)} %compare_select_fusion), kind=kLoop, calls=%fused_computation.7 | loop fusion | flops 1024 | bytes 4608 | tf_op jit(solution)/shard_map/gather | solution.py:198
  10.8 0.1 add_multiply_fusion
  10.9 0.8 %copy.14 = s32[128,4]{1,0:T(8,128)S(1)} copy(s32[128,4]{0,1:T(4,128)} %param.9) | data formatting | bytes 4096 | tf_op args[3]
  11.7 0.1 eq.30
  11.8 0.1 iota_add_fusion
  11.9 0.4 compare_reduce_fusion
  12.3 0.4 convert_reduce_fusion
  12.7 0.6 %iota_add_fusion.1 = s32[32]{0:T(128)} fusion(), kind=kLoop, calls=%fused_computation.13 | loop fusion | flops 32 | bytes 128 | tf_op jit(solution)/shard_map/add | solution.py:173
  13.3 0.9 %select_reduce_fusion = s32[8,2,4]{0,2,1:T(4,128)S(1)} fusion(s32[32]{0:T(128)} %iota_add_fusion.1, s32[8,2,32]{2,0,1:T(8,128)S(1)} %copy.16, pred[8,2,32]{2,0,1:T(8,128)(4,1)S(1)} %copy.15), kind=kLoop, calls=%fused_computation.3 | loop fusion | flops 8128 | bytes 2944 | tf_op jit(solution)/shard_map/reduce_sum | solution.py:173
  14.2 0.1 pad_add_fusion.meta_ref
  14.9 1.4 %gather_fusion = s32[128,4]{1,0:T(8,128)} fusion(s32[128,4]{1,0:T(8,128)S(1)} %copy.14, s32[1024]{0:T(1024)} %pad_clamp_fusion), kind=kCustom, calls=%fused_computation | custom fusion | bytes 4608 | tf_op jit(solution)/shard_map/gather | solution.py:198
  16.3 1.0 %copy.18 = s32[8,4,16]{2,1,0:T(4,128)S(1)} copy(s32[8,4,16]{1,2,0:T(8,128)} %bitcast.28) | data formatting | bytes 4096 | tf_op jit(solution)/shard_map/transpose | solution.py:198
  17.3 0.7 %tile.4 = s32[8,4,16,16]{3,2,1,0:T(8,128)} broadcast(s32[8,4,16]{2,1,0:T(4,128)S(1)} %copy.18), dimensions={0,1,3} | broadcast | bytes 34816 | tf_op jit(solution)/shard_map/tile | solution.py:199
  18.1 1.1 %tile.10.refs_ref = s32[8,4,256]{2,1,0:T(4,128)S(1)} reshape(s32[8,4,16,16]{3,2,1,0:T(8,128)} %tile.4) | data formatting | bytes 65536 | tf_op jit(solution)/shard_map/tile | solution.py:199
  19.2 3.5 %prompt_part.1 = (f32[128,256]{1,0:T(8,128)S(1)}, f32[8,256]{1,0:T(8,128)S(1)}) custom-call(s32[1]{0:T(128)} %bitcast.11.valid_ref, bf16[16,1024]{1,0:T(8,128)(2,1)S(1)} %copy-done.2, bf16[16,1024]{1,0:T(8,128)(2,1)S(1)} %collective-permute-done.1.pair_ref, bf16[4096,256]{1,0:T(8,128)(2,1)S(1)} %bitcast.22), custom_call_target="tpu_custom_call" | custom-call | tf_op jit(solution)/shard_map/prompt_part/pallas_call | solution.py:203
  22.7 0.6 %copy-done.3 = f32[128,256]{1,0:T(8,128)} copy-done((f32[128,256]{1,0:T(8,128)}, f32[128,256]{1,0:T(8,128)S(1)}, u32[]{:S(2)}) %copy-start.3) | copy-done | bytes 131096
  23.4 0.9 %copy-done.4 = f32[128,256]{1,0:T(8,128)S(1)} copy-done((f32[128,256]{1,0:T(8,128)S(1)}, f32[128,256]{1,0:T(8,128)}, u32[]{:S(2)}) %copy-start.4) | copy-done | bytes 131096
  24.3 3.0 %suffix_parts.1 = bf16[4,2,144,128]{3,2,1,0:T(8,128)(2,1)S(1)} custom-call(s32[3]{0:T(128)S(1)} %pad_add_fusion.meta_ref, s32[8,8]{1,0:T(8,128)S(1)} %copy.19.ids_ref, s32[8,4,256]{2,1,0:T(4,128)S(1)} %tile.10.refs_ref, bf16[32,64,256]{2,1,0:T(8,128)(2,1)S(1)} %bitcast.27, bf16[32,64,256]{2,1,0:T(8,128)(2,1)} %collective-permute-done.far_ref, ...), custom_call_target="tpu_custom_call" | custom-call | tf_op jit(solution)/shard_map/suffix_parts/pallas_call | solution.py:215
  27.3 16.8 %all_to_all.10 = bf16[8,144,128]{2,1,0:T(8,128)(2,1)S(1)} all-to-all(bf16[8,144,128]{2,1,0:T(8,128)(2,1)S(1)} %bitcast.23), channel_id=1, replica_groups=mesh['z'=4,'core'=2,'group'=2,'pair'=2] {'z','pair'}, dimensions={0} | all-to-all | bytes 589824 | tf_op jit(solution)/shard_map/all_to_all | solution.py:224
  44.1 0.8 %combine.1 = f32[16,1024]{1,0:T(8,128)} custom-call(bf16[4,2,144,128]{3,2,1,0:T(8,128)(2,1)S(1)} %bitcast.24), custom_call_target="tpu_custom_call" | custom-call | tf_op jit(solution)/shard_map/combine/pallas_call | solution.py:226
  (17 shorter events, 0.1 us)
Async XLA Ops:
  0.0 19.2 %copy-start.2 = (bf16[16,1024]{1,0:T(8,128)(2,1)S(1)}, bf16[16,1024]{1,0:T(8,128)(2,1)}, u32[]{:S(2)}) copy-start(bf16[16,1024]{1,0:T(8,128)(2,1)} %own_ref.1) | copy-start | bytes 98308
  0.0 19.2 %copy-start = (bf16[1,1,4096,256]{3,2,1,0:T(8,128)(2,1)S(1)}, bf16[1,1,4096,256]{3,2,1,0:T(8,128)(2,1)}, u32[]{:S(2)}) copy-start(bf16[1,1,4096,256]{3,2,1,0:T(8,128)(2,1)} %param.7) | copy-start | bytes 6291460
  0.0 19.1 %collective-permute-start.1 = (bf16[16,1024]{1,0:T(8,128)(2,1)}, bf16[16,1024]{1,0:T(8,128)(2,1)S(1)}, u32[]{:S(2)}, u32[]{:S(2)}) collective-permute-start(bf16[16,1024]{1,0:T(8,128)(2,1)} %own_ref.1), channel_id=1, source_target_pairs={{0,1},{1,0},{2,3},{3,2},{4,5},{5,4},{6,7},{7,6},{8,9},{9,8},{10,11... | collective-permute-start | bytes 98312 | tf_op jit(solution)/shard_map/ppermute | solution.py:25
  4.5 18.9 %copy-start.1 = (bf16[32,1,64,256]{3,2,1,0:T(8,128)(2,1)S(1)}, bf16[32,1,64,256]{3,2,1,0:T(8,128)(2,1)}, u32[]{:S(2)}) copy-start(bf16[32,1,64,256]{3,2,1,0:T(8,128)(2,1)} %param.8) | copy-start | bytes 3145732
  4.5 18.9 %all-to-all-start = ((bf16[8,16,1024]{2,1,0:T(8,128)(2,1)}), bf16[8,16,1024]{2,1,0:T(8,128)(2,1)S(1)}, u32[]{:S(2)}, u32[]{:S(2)}) async-start(bf16[8,16,1024]{2,1,0:T(8,128)(2,1)} %broadcast_in_dim.26), calls=%async_computation | async-start | bytes 524288 | tf_op jit(solution)/shard_map/all_to_all | solution.py:190
  9.5 13.8 %collective-permute-start = (bf16[32,64,256]{2,1,0:T(8,128)(2,1)}, bf16[32,64,256]{2,1,0:T(8,128)(2,1)}, u32[]{:S(2)}, u32[]{:S(2)}) collective-permute-start(bf16[32,64,256]{2,1,0:T(8,128)(2,1)} %bitcast.26), channel_id=1, source_target_pairs={{0,4},{4,0},{1,5},{5,1},{2,6},{6,2},{3,7},{7,3},{8,12},{12,8},{9,1... | collective-permute-start | bytes 3145736 | tf_op jit(solution)/shard_map/ppermute | solution.py:25
  22.7 0.7 %copy-start.3 = (f32[128,256]{1,0:T(8,128)}, f32[128,256]{1,0:T(8,128)S(1)}, u32[]{:S(2)}) copy-start(f32[128,256]{1,0:T(8,128)S(1)} %get-tuple-element.7.summed_ref) | copy-start | bytes 393220
  23.4 0.9 %copy-start.4 = (f32[128,256]{1,0:T(8,128)S(1)}, f32[128,256]{1,0:T(8,128)}, u32[]{:S(2)}) copy-start(f32[128,256]{1,0:T(8,128)} %copy-done.3) | copy-start | bytes 393220

commit v4 on v3

v4 whole, which is shorter than its diff:
```python
import functools

import jax
import jax.numpy as jnp
from jax import lax
from jax.experimental import pallas as pl
from jax.experimental.pallas import tpu as pltpu
from jax.sharding import PartitionSpec as P

HD = 128
GROUP = 16
BEAMS = 16
SUF = 4
HEADS = GROUP // 2
VECS = HEADS * BEAMS
STAT_ROWS = 16
UNIT_ROWS = HD + STAT_ROWS
CHUNK = 512

big_negative = -1e30
to_exp2 = HD ** (-0.5) * 1.4426950408889634


def swapped(value, axis):
    return lax.ppermute(value, axis, [(0, 1), (1, 0)])


def stacked_heads(q):
    return jnp.concatenate([q[:, h * HD : (h + 1) * HD] for h in range(HEADS)], axis=0)


def scores_of(keys, vectors):
    return lax.dot_general(
        keys, vectors, (((1,), (1,)), ((), ())), preferred_element_type=jnp.float32
    )


def summed_of(values, weights):
    return lax.dot_general(
        values,
        weights.astype(jnp.bfloat16),
        (((0,), (0,)), ((), ())),
        preferred_element_type=jnp.float32,
    )


def merged(parts):
    top = functools.reduce(jnp.maximum, [p[0] for p in parts])
    total = 0.0
    summed = 0.0
    for part_top, part_total, part_summed in parts:
        factor = jnp.exp2((part_top - top) * to_exp2)
        total = total + part_total * factor
        summed = summed + part_summed * factor
    return top, total, summed


def weighted(scores):
    top = jnp.max(scores, axis=0, keepdims=True)
    weights = jnp.exp2((scores - top) * to_exp2)
    return top, jnp.sum(weights, axis=0, keepdims=True), weights


def three_pieces(x):
    first = x.astype(jnp.bfloat16).astype(jnp.float32)
    rest = x - first
    second = rest.astype(jnp.bfloat16).astype(jnp.float32)
    return [first, second, rest - second]


def store_unit(ref, top, total, summed):
    ref[:HD, :] = summed.astype(jnp.bfloat16)
    rows = three_pieces(top) + three_pieces(total)
    rows.append(jnp.zeros((STAT_ROWS - len(rows), VECS), jnp.float32))
    ref[HD:, :] = jnp.concatenate(rows, axis=0).astype(jnp.bfloat16)


def load_unit(ref):
    stats = ref[HD:, :].astype(jnp.float32)
    top = stats[0:1] + stats[1:2] + stats[2:3]
    total = stats[3:4] + stats[4:5] + stats[5:6]
    return top, total, ref[:HD, :].astype(jnp.float32)


def count(left, right):
    return jnp.dot(
        left.astype(jnp.bfloat16), right.astype(jnp.bfloat16), preferred_element_type=jnp.float32
    )


def iota(shape, axis):
    return lax.broadcasted_iota(jnp.int32, shape, axis)


def prepare_kernel(
    capacity, length_ref, own_ref, pair_ref, prompt_ref, table_ref, parents_ref, near_ref, far_ref,
    summed_ref, stats_ref, keys_ref, values_ref, member_ref, rows_ref,
):
    n_req = keys_ref.shape[0]
    slots, half, _ = near_ref.shape
    rows = table_ref.shape[1]
    n_batch = rows // BEAMS
    z, core, parity = lax.axis_index("z"), lax.axis_index("core"), lax.axis_index("pair")

    slot = iota((2 * slots, rows), 0)
    mine = slot < slots
    block = jnp.where(mine, slot, slot - slots) + jnp.where(mine, 2 * z + core, 2 * z + 1 - core) * slots
    named = functools.reduce(
        jnp.logical_or, [table_ref[j : j + 1, :] == block for j in range(SUF)]
    ).astype(jnp.float32)
    group = (iota((rows, n_batch), 0) // BEAMS == iota((rows, n_batch), 1)).astype(jnp.float32)
    hit = jnp.where(count(named, group) > 0.0, 1.0, 0.0)
    left, right = iota((2 * slots, 2 * slots), 0), iota((2 * slots, 2 * slots), 1)
    before = (left // slots == right // slots) & (right < left)
    rank = count(before.astype(jnp.float32), hit)
    taken = (iota((rows, rows), 0) == parents_ref[...]).astype(jnp.float32)
    continued = count(named, taken)

    place = iota((2 * slots, n_batch), 0)
    found = []
    for k in range(2 * capacity):
        holder = k // capacity
        chosen = (hit > 0.0) & (rank == float(k % capacity)) & (place // slots == holder)
        found.append(jnp.sum(jnp.where(chosen, place + 1, 0), axis=0, keepdims=True))
    found = jnp.concatenate(found, axis=0)

    for d in range(n_req):
        request = (z ^ d) * 2 + core
        lane = iota((rows, 2 * VECS), 1)
        spread = iota((rows, 2 * VECS), 0) == request * BEAMS + lane % BEAMS
        rows_ref[: 2 * slots, :] = count(continued, spread.astype(jnp.float32))
        rows_ref[2 * slots :, :] = jnp.zeros((8, 2 * VECS), jnp.float32)
        mask = iota(found.shape, 1) == request
        picked = jnp.sum(jnp.where(mask, found, 0), axis=1, keepdims=True)
        values = []
        for k in range(2 * capacity):
            index = picked[k, 0]
            row = jnp.where(index > 0, index - 1, 2 * slots)
            member_ref[d, k : k + 1, :] = rows_ref[pl.ds(row, 1), :]
            pool_ref = near_ref if k < capacity else far_ref
            base = 0 if k < capacity else slots
            content = pool_ref[jnp.maximum(index - 1 - base, 0)]
            keys_ref[d, k * half : (k + 1) * half, :] = content[:, :HD]
            values.append(content[:, HD:])
        values_ref[d] = jnp.concatenate(values, axis=0).T

    vectors = jnp.concatenate([stacked_heads(own_ref[...]), stacked_heads(pair_ref[...])], axis=0)
    length = length_ref[0]
    whole = lax.div(length, 2 * half)
    valid = whole * half + jnp.clip(length - whole * (2 * half) - parity * half, 0, half)
    parts = []
    for start in range(0, prompt_ref.shape[0], CHUNK):
        scores = scores_of(prompt_ref[start : start + CHUNK, :HD], vectors)
        token = iota(scores.shape, 0)
        scores = jnp.where(token < valid - start, scores, big_negative)
        top, total, weights = weighted(scores)
        parts.append((top, total, summed_of(prompt_ref[start : start + CHUNK, HD:], weights)))
        if len(parts) == 2:
            parts = [merged(parts)]
    top, total, summed = merged(parts)
    summed_ref[...] = summed
    stats_ref[...] = jnp.concatenate(
        [top, total, jnp.zeros((6, 2 * VECS), jnp.float32)], axis=0
    )


def suffix_kernel(keys_ref, values_ref, member_ref, queries_ref, summed_ref, stats_ref, out_ref):
    n_req = queries_ref.shape[0]
    n_slots = member_ref.shape[1]
    half = keys_ref.shape[1] // n_slots
    z, parity = lax.axis_index("z"), lax.axis_index("pair")
    for d in range(n_req):
        target = z ^ d
        vectors = jnp.concatenate(
            [
                stacked_heads(queries_ref[target, parity]),
                stacked_heads(queries_ref[target, 1 - parity]),
            ],
            axis=0,
        )
        scores = scores_of(keys_ref[d], vectors)
        scores = jnp.concatenate(
            [
                jnp.where(
                    member_ref[d, k : k + 1, :] > 0.0,
                    scores[k * half : (k + 1) * half],
                    big_negative,
                )
                for k in range(n_slots)
            ],
            axis=0,
        )
        top, total, weights = weighted(scores)
        summed = jnp.dot(
            values_ref[d], weights.astype(jnp.bfloat16), preferred_element_type=jnp.float32
        )
        if d == 0:
            prompt = (stats_ref[0:1], stats_ref[1:2], summed_ref[...])
            top, total, summed = merged([(top, total, summed), prompt])
        for side in range(2):
            lanes = slice(side * VECS, (side + 1) * VECS)
            owner = parity if side == 0 else 1 - parity
            store_unit(
                out_ref.at[target, owner], top[:, lanes], total[:, lanes], summed[:, lanes]
            )


def final_kernel(units_ref, out_ref):
    n_req, n_pair = units_ref.shape[:2]
    parts = [load_unit(units_ref.at[r, p]) for r in range(n_req) for p in range(n_pair)]
    _, total, summed = merged(parts)
    attended = (summed / total).T
    for h in range(HEADS):
        out_ref[:, h * HD : (h + 1) * HD] = attended[h * BEAMS : (h + 1) * BEAMS]


def on_device(queries, prompt_cache, pool, block_table, parents, lengths):
    n_req = lax.axis_size("z")
    n_batch = 2 * n_req
    ndist = 2 ** (SUF + 1) - 2
    capacity = 2 * ((ndist // 2 + n_batch - 1) // n_batch)
    slots, _, half, width = pool.shape
    tokens = prompt_cache.shape[2]
    rows = block_table.shape[0]
    smem = pl.BlockSpec(memory_space=pltpu.SMEM)
    vmem = pl.BlockSpec(memory_space=pltpu.VMEM)
    params = pltpu.CompilerParams(vmem_limit_bytes=40 * 2**20)

    copies = jnp.broadcast_to(queries[None], (2 * n_req,) + queries.shape)
    gathered = lax.all_to_all(copies, ("z", "pair"), split_axis=0, concat_axis=0, tiled=True)
    gathered = gathered.reshape(n_req, 2, BEAMS, HEADS * HD)
    other = swapped(queries, "pair")
    near = pool.reshape(slots, half, width)
    far = swapped(near, "core")

    summed, stats, keys, values, member = pl.pallas_call(
        functools.partial(prepare_kernel, capacity),
        out_shape=(
            jax.ShapeDtypeStruct((HD, 2 * VECS), jnp.float32),
            jax.ShapeDtypeStruct((8, 2 * VECS), jnp.float32),
            jax.ShapeDtypeStruct((n_req, 2 * capacity * half, HD), jnp.bfloat16),
            jax.ShapeDtypeStruct((n_req, HD, 2 * capacity * half), jnp.bfloat16),
            jax.ShapeDtypeStruct((n_req, 2 * capacity, 2 * VECS), jnp.float32),
        ),
        in_specs=[smem] + [vmem] * 7,
        out_specs=(vmem,) * 5,
        scratch_shapes=[pltpu.VMEM((2 * slots + 8, 2 * VECS), jnp.float32)],
        compiler_params=params,
        name="prepare",
    )(
        lengths,
        queries,
        other,
        prompt_cache.reshape(tokens, width),
        block_table.T,
        parents.reshape(1, rows),
        near,
        far,
    )

    units = pl.pallas_call(
        suffix_kernel,
        out_shape=jax.ShapeDtypeStruct((n_req, 2, UNIT_ROWS, VECS), jnp.bfloat16),
        in_specs=[vmem] * 6,
        out_specs=vmem,
        compiler_params=params,
        name="suffix_parts",
    )(keys, values, member, gathered, summed, stats)
    units = units.reshape(2 * n_req, UNIT_ROWS, VECS)
    units = lax.all_to_all(units, ("z", "pair"), split_axis=0, concat_axis=0, tiled=True)

    return pl.pallas_call(
        final_kernel,
        out_shape=jax.ShapeDtypeStruct((BEAMS, HEADS * HD), jnp.float32),
        in_specs=[vmem],
        out_specs=vmem,
        compiler_params=params,
        name="combine",
    )(units.reshape(n_req, 2, UNIT_ROWS, VECS))


def solution(mesh):
    n_batch, n_mp = mesh.devices.shape
    split = jax.sharding.Mesh(
        mesh.devices.reshape(n_batch // 2, 2, n_mp // 2, 2), ("z", "core", "group", "pair")
    )
    batch, mp = ("z", "core"), ("group", "pair")
    return jax.shard_map(
        on_device,
        mesh=split,
        in_specs=(
            P(batch, mp),
            P(batch, mp, None, None),
            P(batch, mp, None, None),
            P(),
            P(),
            P(batch),
        ),
        out_specs=P(batch, mp),
        check_vma=False,
    )
```

time: 45.4 us -> 40.8 us (0.90)
  other arithmetic: 3.76 us -> 0 us
  waiting for transfers between devices: 0.01 us -> 2.15 us
  local copies, waits for them, and re-layouts: 8.19 us -> 6.39 us
  blocking collectives: 16.8 us -> 15.4 us
  starting transfers between devices: 8 us -> 9.28 us
  Pallas kernels: 7.3 us -> 6.42 us
    unnamed x11 -> x10, local copies, waits for them, and re-layouts: 2.34 us -> 4.91 us
    ppermute x2, waiting for transfers between devices: 0.01 us -> 2.15 us  [swapped(): return lax.ppermute(value, axis, [(0, 1), (1, 0)])]
    another operation x2 -> x0, local copies, waits for them, and re-layouts: 1.83 us -> none  [on_device(): wanted = jnp.tile(wanted, (1, 1, GROUP))]
    all_to_all x1, starting transfers between devices: 5.05 us -> 6.8 us  [on_device(): lax.all_to_all(copies, ('z', 'pair'), split_axis=0, concat_axis=0, tiled=...]
    all_to_all x1, blocking collectives: 16.8 us -> 15.4 us  [on_device(): lax.all_to_all(units, ('z', 'pair'), split_axis=0, concat_axis=0, tiled=T...]
    gather x1 -> x0, local copies, waits for them, and re-layouts: 1.36 us -> none  [on_device(): block_table[parents].reshape(n_batch, BEAMS, SUF).transpose(0, 2, 1)]
    reduce_sum x2 -> x0, other arithmetic: 1.26 us -> none  [the longest x1 0.88 us: slots_of(): found = jnp.sum(jnp.where(chosen, order + 1, 0), axis=3) - 1]
    pallas_call x1, Pallas kernels: 3.01 us -> 1.79 us  [on_device(): pl.pallas_call(suffix_kernel, out_shape=jax.ShapeDtypeStruct((n_req, 2, U...]
  transfers between devices with their start and end apart: 3 -> 3, of which waited for: 0 -> 1; matrix products, arithmetic and copies ran while one was open for 23% -> 4% of each run, Pallas kernels for 8% -> 10%
where the time goes in v4:
time: 40.8 us; the launch traced here: 40.3 us
  blocking collectives  15.4 us (38%)
  starting transfers between devices  9.28 us (23%)
  Pallas kernels  6.42 us (16%)
  local copies, waits for them, and re-layouts  6.39 us (16%)
  waiting for transfers between devices  2.15 us (5%)
  between operations  0.68 us (2%)
    all_to_all x1, blocking collectives, on_device(): lax.all_to_all(units, ('z', 'pair'), split_axis=0, concat_axis=0, tiled=T...  15.4 us
    all_to_all x1, starting transfers between devices, on_device(): lax.all_to_all(copies, ('z', 'pair'), split_axis=0, concat_axis=0, tiled=...  6.8 us
    unnamed x10, local copies, waits for them, and re-layouts  4.91 us
    pallas_call x1, Pallas kernels, on_device(): pl.pallas_call(functools.partial(prepare_kernel, capacity), out_shape=(ja...  3.85 us
    ppermute x2, starting transfers between devices, swapped(): return lax.ppermute(value, axis, [(0, 1), (1, 0)])  2.47 us
    ppermute x2, waiting for transfers between devices, swapped(): return lax.ppermute(value, axis, [(0, 1), (1, 0)])  2.15 us
    pallas_call x1, Pallas kernels, on_device(): pl.pallas_call(suffix_kernel, out_shape=jax.ShapeDtypeStruct((n_req, 2, U...  1.79 us
    broadcast_in_dim x1, local copies, waits for them, and re-layouts, on_device(): copies = jnp.broadcast_to(queries[None], (2 * n_req,) + queries.shape)  1.48 us
  transfers between devices with their start and end apart: 3, of which 1 were waited for; matrix products, arithmetic and copies ran while one was open for 4% of the time, Pallas kernels for 10%

profile of v4, /device:TPU:0, one launch (start us, length us, event | category | flops | bytes accessed | tf_op | source)
XLA Modules:
  0.0 40.3 jit_solution(7351653792457269417)
XLA Ops:
  0.0 0.5 %collective-permute-start.1 = (bf16[32,64,256]{2,1,0:T(8,128)(2,1)}, bf16[32,64,256]{2,1,0:T(8,128)(2,1)S(1)}, u32[]{:S(2)}, u32[]{:S(2)}) collective-permute-start(bf16[32,64,256]{2,1,0:T(8,128)(2,1)} %bitcast.11), channel_id=1, source_target_pairs={{0,4},{4,0},{1,5},{5,1},{2,6},{6,2},{3,7},{7,3},{8,12},{12,8},{9,1... | collective-permute-start | bytes 3145736 | tf_op jit(solution)/shard_map/ppermute | solution.py:25
  0.5 1.5 %broadcast_in_dim.2 = bf16[8,16,1024]{2,1,0:T(8,128)(2,1)} broadcast(bf16[16,1024]{1,0:T(8,128)(2,1)} %own_ref.1), dimensions={1,2} | broadcast | bytes 294912 | tf_op jit(solution)/shard_map/broadcast_in_dim | solution.py:229
  1.9 6.8 %all-to-all-start = ((bf16[8,16,1024]{2,1,0:T(8,128)(2,1)}), bf16[8,16,1024]{2,1,0:T(8,128)(2,1)S(1)}, u32[]{:S(2)}, u32[]{:S(2)}) async-start(bf16[8,16,1024]{2,1,0:T(8,128)(2,1)} %broadcast_in_dim.2), calls=%async_computation | async-start | bytes 524288 | tf_op jit(solution)/shard_map/all_to_all | solution.py:230
  8.7 2.0 %collective-permute-start = (bf16[16,1024]{1,0:T(8,128)(2,1)}, bf16[16,1024]{1,0:T(8,128)(2,1)S(1)}, u32[]{:S(2)}, u32[]{:S(2)}) collective-permute-start(bf16[16,1024]{1,0:T(8,128)(2,1)} %own_ref.1), channel_id=1, source_target_pairs={{0,1},{1,0},{2,3},{3,2},{4,5},{5,4},{6,7},{7,6},{8,9},{9,8},{10,11... | collective-permute-start | bytes 98312 | tf_op jit(solution)/shard_map/ppermute | solution.py:25
  11.4 2.1 %collective-permute-done.pair_ref = bf16[16,1024]{1,0:T(8,128)(2,1)S(1)} collective-permute-done((bf16[16,1024]{1,0:T(8,128)(2,1)}, bf16[16,1024]{1,0:T(8,128)(2,1)S(1)}, u32[]{:S(2)}, u32[]{:S(2)}) %collective-permute-start) | collective-permute-done | bytes 32800 | tf_op jit(solution)/shard_map/ppermute | solution.py:25
  13.6 0.0 collective-permute-done.1.far_ref
  13.6 0.0 copy-start
  13.6 1.6 %copy-done = bf16[1,1,4096,256]{3,2,1,0:T(8,128)(2,1)S(1)} copy-done((bf16[1,1,4096,256]{3,2,1,0:T(8,128)(2,1)S(1)}, bf16[1,1,4096,256]{3,2,1,0:T(8,128)(2,1)}, u32[]{:S(2)}) %copy-start) | copy-done | bytes 2097176
  15.2 0.0 copy-start.1
  15.2 1.2 %copy-done.1 = bf16[32,1,64,256]{3,2,1,0:T(8,128)(2,1)S(1)} copy-done((bf16[32,1,64,256]{3,2,1,0:T(8,128)(2,1)S(1)}, bf16[32,1,64,256]{3,2,1,0:T(8,128)(2,1)}, u32[]{:S(2)}) %copy-start.1) | copy-done | bytes 1048600
  16.4 0.0 copy-start.2
  16.4 0.8 %copy-done.2 = bf16[16,1024]{1,0:T(8,128)(2,1)S(1)} copy-done((bf16[16,1024]{1,0:T(8,128)(2,1)S(1)}, bf16[16,1024]{1,0:T(8,128)(2,1)}, u32[]{:S(2)}) %copy-start.2) | copy-done | bytes 32792
  17.1 0.0 copy-start.3
  17.1 0.7 %copy-done.3 = s32[128,4]{0,1:T(4,128)S(1)} copy-done((s32[128,4]{0,1:T(4,128)S(1)}, s32[128,4]{0,1:T(4,128)}, u32[]{:S(2)}) %copy-start.3) | copy-done | bytes 2072
  17.8 0.0 copy-start.4
  17.8 0.7 %copy-done.4 = s32[128]{0:T(128)S(1)} copy-done((s32[128]{0:T(128)S(1)}, s32[128]{0:T(128)}, u32[]{:S(2)}) %copy-start.4) | copy-done | bytes 536
  18.5 3.9 %prepare.1 = (f32[128,256]{1,0:T(8,128)S(1)}, f32[8,256]{1,0:T(8,128)S(1)}, bf16[4,512,128]{2,1,0:T(8,128)(2,1)S(1)}, bf16[4,128,512]{2,1,0:T(8,128)(2,1)S(1)}, f32[4,8,256]{2,1,0:T(8,128)S(1)}) custom-call(s32[1]{0:T(128)S(6)} %copy.7.length_ref, bf16[16,1024]{1,0:T(8,128)(2,1)S(1)} %copy-done.2, bf16[16,1024]{1,0:T(8,128)(2,1)S(1)} %collective-permute-done.pair_ref, ...), custom_call_target="tpu_custom_call" | custom-call | tf_op jit(solution)/shard_map/prepare/pallas_call | solution.py:236
  22.3 0.0 all-to-all-done
  22.3 1.8 %suffix_parts.1 = bf16[4,2,144,128]{3,2,1,0:T(8,128)(2,1)S(1)} custom-call(bf16[4,512,128]{2,1,0:T(8,128)(2,1)S(1)} %get-tuple-element.10.keys_ref, bf16[4,128,512]{2,1,0:T(8,128)(2,1)S(1)} %get-tuple-element.11.values_ref, f32[4,8,256]{2,1,0:T(8,128)S(1)} %get-tuple-element.12.member_ref, bf16[4,2,16,1024]{3,2,1,0:T(8,128)(2,1)S(1)} %bitcast.10, ...), custom_call_target="tpu_custom_call" | custom-call | tf_op jit(solution)/shard_map/suffix_parts/pallas_call | solution.py:261
  24.1 15.4 %all_to_all.10 = bf16[8,144,128]{2,1,0:T(8,128)(2,1)S(1)} all-to-all(bf16[8,144,128]{2,1,0:T(8,128)(2,1)S(1)} %bitcast.8), channel_id=1, replica_groups=mesh['z'=4,'core'=2,'group'=2,'pair'=2] {'z','pair'}, dimensions={0} | all-to-all | bytes 589824 | tf_op jit(solution)/shard_map/all_to_all | solution.py:270
  39.5 0.8 %combine.1 = f32[16,1024]{1,0:T(8,128)} custom-call(bf16[4,2,144,128]{3,2,1,0:T(8,128)(2,1)S(1)} %bitcast.9), custom_call_target="tpu_custom_call" | custom-call | tf_op jit(solution)/shard_map/combine/pallas_call | solution.py:272
Async XLA Ops:
  0.0 13.6 %collective-permute-start.1 = (bf16[32,64,256]{2,1,0:T(8,128)(2,1)}, bf16[32,64,256]{2,1,0:T(8,128)(2,1)S(1)}, u32[]{:S(2)}, u32[]{:S(2)}) collective-permute-start(bf16[32,64,256]{2,1,0:T(8,128)(2,1)} %bitcast.11), channel_id=1, source_target_pairs={{0,4},{4,0},{1,5},{5,1},{2,6},{6,2},{3,7},{7,3},{8,12},{12,8},{9,1... | collective-permute-start | bytes 3145736 | tf_op jit(solution)/shard_map/ppermute | solution.py:25
  1.9 20.4 %all-to-all-start = ((bf16[8,16,1024]{2,1,0:T(8,128)(2,1)}), bf16[8,16,1024]{2,1,0:T(8,128)(2,1)S(1)}, u32[]{:S(2)}, u32[]{:S(2)}) async-start(bf16[8,16,1024]{2,1,0:T(8,128)(2,1)} %broadcast_in_dim.2), calls=%async_computation | async-start | bytes 524288 | tf_op jit(solution)/shard_map/all_to_all | solution.py:230
  8.7 4.8 %collective-permute-start = (bf16[16,1024]{1,0:T(8,128)(2,1)}, bf16[16,1024]{1,0:T(8,128)(2,1)S(1)}, u32[]{:S(2)}, u32[]{:S(2)}) collective-permute-start(bf16[16,1024]{1,0:T(8,128)(2,1)} %own_ref.1), channel_id=1, source_target_pairs={{0,1},{1,0},{2,3},{3,2},{4,5},{5,4},{6,7},{7,6},{8,9},{9,8},{10,11... | collective-permute-start | bytes 98312 | tf_op jit(solution)/shard_map/ppermute | solution.py:25
  13.6 1.6 %copy-start = (bf16[1,1,4096,256]{3,2,1,0:T(8,128)(2,1)S(1)}, bf16[1,1,4096,256]{3,2,1,0:T(8,128)(2,1)}, u32[]{:S(2)}) copy-start(bf16[1,1,4096,256]{3,2,1,0:T(8,128)(2,1)} %param.7) | copy-start | bytes 6291460
  15.2 1.2 %copy-start.1 = (bf16[32,1,64,256]{3,2,1,0:T(8,128)(2,1)S(1)}, bf16[32,1,64,256]{3,2,1,0:T(8,128)(2,1)}, u32[]{:S(2)}) copy-start(bf16[32,1,64,256]{3,2,1,0:T(8,128)(2,1)} %param.8) | copy-start | bytes 3145732
  16.4 0.8 %copy-start.2 = (bf16[16,1024]{1,0:T(8,128)(2,1)S(1)}, bf16[16,1024]{1,0:T(8,128)(2,1)}, u32[]{:S(2)}) copy-start(bf16[16,1024]{1,0:T(8,128)(2,1)} %own_ref.1) | copy-start | bytes 98308
  17.1 0.7 %copy-start.3 = (s32[128,4]{0,1:T(4,128)S(1)}, s32[128,4]{0,1:T(4,128)}, u32[]{:S(2)}) copy-start(s32[128,4]{0,1:T(4,128)} %param.9) | copy-start | bytes 6148
  17.8 0.7 %copy-start.4 = (s32[128]{0:T(128)S(1)}, s32[128]{0:T(128)}, u32[]{:S(2)}) copy-start(s32[128]{0:T(128)} %param.10) | copy-start | bytes 1540

commit v5 on v4

--- a/solution.py
+++ b/solution.py
@@ -92,28 +92,78 @@
     return lax.broadcasted_iota(jnp.int32, shape, axis)
 
 
+def copies_kernel(queries_ref, out_ref, sems):
+    copies = [
+        pltpu.make_async_copy(queries_ref, out_ref.at[i], sems.at[i])
+        for i in range(out_ref.shape[0])
+    ]
+    for copy in copies:
+        copy.start()
+    for copy in copies:
+        copy.wait()
+
+
+def prompt_chunks(prompt_ref, held_ref, sems):
+    copies = []
+    for i in range(held_ref.shape[0] // CHUNK):
+        part = pl.ds(i * CHUNK, CHUNK)
+        copies.append(pltpu.make_async_copy(prompt_ref.at[part], held_ref.at[part], sems.at[i]))
+    return copies
+
+
+def prompt_part(length, half, held_ref, copies, vectors):
+    parity = lax.axis_index("pair")
+    whole = lax.div(length, 2 * half)
+    valid = whole * half + jnp.clip(length - whole * (2 * half) - parity * half, 0, half)
+    parts = []
+    for i, copy in enumerate(copies):
+        copy.wait()
+        part = slice(i * CHUNK, (i + 1) * CHUNK)
+        scores = scores_of(held_ref[part, :HD], vectors)
+        token = iota(scores.shape, 0)
+        scores = jnp.where(token < valid - i * CHUNK, scores, big_negative)
+        top, total, weights = weighted(scores)
+        parts.append((top, total, summed_of(held_ref[part, HD:], weights)))
+        if len(parts) == 2:
+            parts = [merged(parts)]
+    return merged(parts)
+
+
 def prepare_kernel(
-    capacity, length_ref, own_ref, pair_ref, prompt_ref, table_ref, parents_ref, near_ref, far_ref,
-    summed_ref, stats_ref, keys_ref, values_ref, member_ref, rows_ref,
+    capacity, length_ref, own_ref, prompt_ref, table_ref, parents_ref, near_ref, far_ref,
+    summed_ref, stats_ref, keys_ref, values_ref, member_ref,
+    rows_ref, own, held, table, parents, near, sems, prompt_sems,
 ):
     n_req = keys_ref.shape[0]
-    slots, half, _ = near_ref.shape
-    rows = table_ref.shape[1]
+    slots, half, _ = near.shape
+    rows = table.shape[1]
     n_batch = rows // BEAMS
-    z, core, parity = lax.axis_index("z"), lax.axis_index("core"), lax.axis_index("pair")
-
+    z, core = lax.axis_index("z"), lax.axis_index("core")
+
+    small = [
+        pltpu.make_async_copy(source, target, sems.at[i])
+        for i, (source, target) in enumerate(
+            [(table_ref, table), (parents_ref, parents), (near_ref, near), (own_ref, own)]
+        )
+    ]
+    chunks = prompt_chunks(prompt_ref, held, prompt_sems)
+    for copy in small + chunks:
+        copy.start()
+
+    small[0].wait()
     slot = iota((2 * slots, rows), 0)
     mine = slot < slots
     block = jnp.where(mine, slot, slot - slots) + jnp.where(mine, 2 * z + core, 2 * z + 1 - core) * slots
     named = functools.reduce(
-        jnp.logical_or, [table_ref[j : j + 1, :] == block for j in range(SUF)]
+        jnp.logical_or, [table[j : j + 1, :] == block for j in range(SUF)]
     ).astype(jnp.float32)
     group = (iota((rows, n_batch), 0) // BEAMS == iota((rows, n_batch), 1)).astype(jnp.float32)
     hit = jnp.where(count(named, group) > 0.0, 1.0, 0.0)
     left, right = iota((2 * slots, 2 * slots), 0), iota((2 * slots, 2 * slots), 1)
     before = (left // slots == right // slots) & (right < left)
     rank = count(before.astype(jnp.float32), hit)
-    taken = (iota((rows, rows), 0) == parents_ref[...]).astype(jnp.float32)
+    small[1].wait()
+    taken = (iota((rows, rows), 0) == parents[...]).astype(jnp.float32)
     continued = count(named, taken)
 
     place = iota((2 * slots, n_batch), 0)
@@ -124,6 +174,7 @@
         found.append(jnp.sum(jnp.where(chosen, place + 1, 0), axis=0, keepdims=True))
     found = jnp.concatenate(found, axis=0)
 
+    small[2].wait()
     for d in range(n_req):
         request = (z ^ d) * 2 + core
         lane = iota((rows, 2 * VECS), 1)
@@ -137,31 +188,26 @@
             index = picked[k, 0]
             row = jnp.where(index > 0, index - 1, 2 * slots)
             member_ref[d, k : k + 1, :] = rows_ref[pl.ds(row, 1), :]
-            pool_ref = near_ref if k < capacity else far_ref
+            pool_ref = near if k < capacity else far_ref
             base = 0 if k < capacity else slots
             content = pool_ref[jnp.maximum(index - 1 - base, 0)]
             keys_ref[d, k * half : (k + 1) * half, :] = content[:, :HD]
             values.append(content[:, HD:])
         values_ref[d] = jnp.concatenate(values, axis=0).T
 
-    vectors = jnp.concatenate([stacked_heads(own_ref[...]), stacked_heads(pair_ref[...])], axis=0)
-    length = length_ref[0]
-    whole = lax.div(length, 2 * half)
-    valid = whole * half + jnp.clip(length - whole * (2 * half) - parity * half, 0, half)
-    parts = []
-    for start in range(0, prompt_ref.shape[0], CHUNK):
-        scores = scores_of(prompt_ref[start : start + CHUNK, :HD], vectors)
-        token = iota(scores.shape, 0)
-        scores = jnp.where(token < valid - start, scores, big_negative)
-        top, total, weights = weighted(scores)
-        parts.append((top, total, summed_of(prompt_ref[start : start + CHUNK, HD:], weights)))
-        if len(parts) == 2:
-            parts = [merged(parts)]
-    top, total, summed = merged(parts)
+    small[3].wait()
+    top, total, summed = prompt_part(length_ref[0], half, held, chunks, stacked_heads(own[...]))
     summed_ref[...] = summed
-    stats_ref[...] = jnp.concatenate(
-        [top, total, jnp.zeros((6, 2 * VECS), jnp.float32)], axis=0
-    )
+    stats_ref[...] = jnp.concatenate([top, total, jnp.zeros((6, VECS), jnp.float32)], axis=0)
+
+
+def other_heads_kernel(half, length_ref, gathered_ref, prompt_ref, out_ref, held, prompt_sems):
+    chunks = prompt_chunks(prompt_ref, held, prompt_sems)
+    for copy in chunks:
+        copy.start()
+    z, parity = lax.axis_index("z"), lax.axis_index("pair")
+    vectors = stacked_heads(gathered_ref[z, 1 - parity])
+    store_unit(out_ref, *prompt_part(length_ref[0], half, held, chunks, vectors))
 
 
 def suffix_kernel(keys_ref, values_ref, member_ref, queries_ref, summed_ref, stats_ref, out_ref):
@@ -194,24 +240,27 @@
         summed = jnp.dot(
             values_ref[d], weights.astype(jnp.bfloat16), preferred_element_type=jnp.float32
         )
-        if d == 0:
-            prompt = (stats_ref[0:1], stats_ref[1:2], summed_ref[...])
-            top, total, summed = merged([(top, total, summed), prompt])
         for side in range(2):
             lanes = slice(side * VECS, (side + 1) * VECS)
             owner = parity if side == 0 else 1 - parity
-            store_unit(
-                out_ref.at[target, owner], top[:, lanes], total[:, lanes], summed[:, lanes]
-            )
-
-
-def final_kernel(units_ref, out_ref):
+            part = (top[:, lanes], total[:, lanes], summed[:, lanes])
+            if d == 0 and side == 0:
+                part = merged([part, (stats_ref[0:1], stats_ref[1:2], summed_ref[...])])
+            store_unit(out_ref.at[target, owner], *part)
+
+
+def final_kernel(units_ref, last_ref, out_ref):
     n_req, n_pair = units_ref.shape[:2]
     parts = [load_unit(units_ref.at[r, p]) for r in range(n_req) for p in range(n_pair)]
+    parts.append(load_unit(last_ref))
     _, total, summed = merged(parts)
     attended = (summed / total).T
     for h in range(HEADS):
         out_ref[:, h * HD : (h + 1) * HD] = attended[h * BEAMS : (h + 1) * BEAMS]
+
+
+def in_hbm(value):
+    return pltpu.with_memory_space_constraint(value, pltpu.HBM)
 
 
 def on_device(queries, prompt_cache, pool, block_table, parents, lengths):
@@ -226,35 +275,56 @@
     vmem = pl.BlockSpec(memory_space=pltpu.VMEM)
     params = pltpu.CompilerParams(vmem_limit_bytes=40 * 2**20)
 
-    copies = jnp.broadcast_to(queries[None], (2 * n_req,) + queries.shape)
+    hbm = pl.BlockSpec(memory_space=pltpu.HBM)
+    chunk_sems = pltpu.SemaphoreType.DMA((tokens // CHUNK,))
+    prompt = in_hbm(prompt_cache.reshape(tokens, width))
+    near = pool.reshape(slots, half, width)
+    far = swapped(near, "core")
+
+    copies = pl.pallas_call(
+        copies_kernel,
+        out_shape=jax.ShapeDtypeStruct((2 * n_req,) + queries.shape, jnp.bfloat16),
+        in_specs=[hbm],
+        out_specs=vmem,
+        scratch_shapes=[pltpu.SemaphoreType.DMA((2 * n_req,))],
+        name="query_copies",
+    )(in_hbm(queries))
     gathered = lax.all_to_all(copies, ("z", "pair"), split_axis=0, concat_axis=0, tiled=True)
     gathered = gathered.reshape(n_req, 2, BEAMS, HEADS * HD)
-    other = swapped(queries, "pair")
-    near = pool.reshape(slots, half, width)
-    far = swapped(near, "core")
 
     summed, stats, keys, values, member = pl.pallas_call(
         functools.partial(prepare_kernel, capacity),
         out_shape=(
-            jax.ShapeDtypeStruct((HD, 2 * VECS), jnp.float32),
-            jax.ShapeDtypeStruct((8, 2 * VECS), jnp.float32),
+            jax.ShapeDtypeStruct((HD, VECS), jnp.float32),
+            jax.ShapeDtypeStruct((8, VECS), jnp.float32),
             jax.ShapeDtypeStruct((n_req, 2 * capacity * half, HD), jnp.bfloat16),
             jax.ShapeDtypeStruct((n_req, HD, 2 * capacity * half), jnp.bfloat16),
             jax.ShapeDtypeStruct((n_req, 2 * capacity, 2 * VECS), jnp.float32),
         ),
-        in_specs=[smem] + [vmem] * 7,
+        in_specs=[smem] + [hbm] * 5 + [vmem],
         out_specs=(vmem,) * 5,
-        scratch_shapes=[pltpu.VMEM((2 * slots + 8, 2 * VECS), jnp.float32)],
+        scratch_shapes=[
+            pltpu.VMEM((2 * slots + 8, 2 * VECS), jnp.float32),
+            pltpu.VMEM(queries.shape, jnp.bfloat16),
+            pltpu.VMEM((tokens, width), jnp.bfloat16),
+            pltpu.VMEM((SUF, rows), jnp.int32),
+            pltpu.VMEM((1, rows), jnp.int32),
+            pltpu.VMEM((slots, half, width), jnp.bfloat16),
+            pltpu.SemaphoreType.DMA((4,)),
+            chunk_sems,
+        ],
         compiler_params=params,
+        cost_estimate=pl.CostEstimate(
+            flops=4 * tokens * VECS * HD, bytes_accessed=4 * tokens * width, transcendentals=0
+        ),
         name="prepare",
     )(
         lengths,
-        queries,
-        other,
-        prompt_cache.reshape(tokens, width),
-        block_table.T,
-        parents.reshape(1, rows),
-        near,
+        in_hbm(queries),
+        prompt,
+        in_hbm(block_table.T),
+        in_hbm(parents.reshape(1, rows)),
+        in_hbm(near),
         far,
     )
 
@@ -266,17 +336,32 @@
         compiler_params=params,
         name="suffix_parts",
     )(keys, values, member, gathered, summed, stats)
+    units, gathered = lax.optimization_barrier((units, gathered))
     units = units.reshape(2 * n_req, UNIT_ROWS, VECS)
     units = lax.all_to_all(units, ("z", "pair"), split_axis=0, concat_axis=0, tiled=True)
+
+    given = pl.pallas_call(
+        functools.partial(other_heads_kernel, half),
+        out_shape=jax.ShapeDtypeStruct((UNIT_ROWS, VECS), jnp.bfloat16),
+        in_specs=[smem, vmem, hbm],
+        out_specs=vmem,
+        scratch_shapes=[pltpu.VMEM((tokens, width), jnp.bfloat16), chunk_sems],
+        compiler_params=params,
+        cost_estimate=pl.CostEstimate(
+            flops=4 * tokens * VECS * HD, bytes_accessed=2 * tokens * width, transcendentals=0
+        ),
+        name="other_heads",
+    )(lengths, gathered, prompt)
+    last = swapped(given, "pair")
 
     return pl.pallas_call(
         final_kernel,
         out_shape=jax.ShapeDtypeStruct((BEAMS, HEADS * HD), jnp.float32),
-        in_specs=[vmem],
+        in_specs=[vmem, vmem],
         out_specs=vmem,
         compiler_params=params,
         name="combine",
-    )(units.reshape(n_req, 2, UNIT_ROWS, VECS))
+    )(units.reshape(n_req, 2, UNIT_ROWS, VECS), last)
 
 
 def solution(mesh):

time: 40.8 us -> 35.8 us (0.88)
  blocking collectives: 15.4 us -> 0 us
  Pallas kernels: 6.42 us -> 15.5 us
  local copies, waits for them, and re-layouts: 6.39 us -> 0 us
  waiting for transfers between devices: 2.15 us -> 6.24 us
  starting transfers between devices: 9.28 us -> 12.9 us
    all_to_all x1 -> x0, blocking collectives: 15.4 us -> none  [on_device(): lax.all_to_all(units, ('z', 'pair'), split_axis=0, concat_axis=0, tiled=T...]
    pallas_call x0 -> x2, Pallas kernels: none -> 6.4 us  [the longest x1 4.58 us: on_device(): pl.pallas_call(functools.partial(other_heads_kernel, half), out_shape=jax...]
    unnamed x10 -> x0, local copies, waits for them, and re-layouts: 4.91 us -> none
    all_to_all x0 -> x1, starting transfers between devices: none -> 3.59 us  [on_device(): lax.all_to_all(units, ('z', 'pair'), split_axis=0, concat_axis=0, tiled=T...]
    all_to_all x1, waiting for transfers between devices: 0.01 us -> 3.13 us  [on_device(): lax.all_to_all(copies, ('z', 'pair'), split_axis=0, concat_axis=0, tiled=...]
    pallas_call x1, Pallas kernels: 3.85 us -> 5.79 us  [on_device(): pl.pallas_call(functools.partial(prepare_kernel, capacity), out_shape=(ja...]
    broadcast_in_dim x1 -> x0, local copies, waits for them, and re-layouts: 1.48 us -> none  [on_device(): copies = jnp.broadcast_to(queries[None], (2 * n_req,) + queries.shape)]
    all_to_all x0 -> x1, waiting for transfers between devices: none -> 1.17 us  [on_device(): lax.all_to_all(units, ('z', 'pair'), split_axis=0, concat_axis=0, tiled=T...]
  transfers between devices with their start and end apart: 3 -> 4, of which waited for: 1 -> 3; matrix products, arithmetic and copies ran while one was open for 4% -> 0% of each run, Pallas kernels for 10% -> 35%
where the time goes in v5:
time: 35.8 us; the launch traced here: 35.3 us
  Pallas kernels  15.5 us (43%)
  starting transfers between devices  12.9 us (36%)
  waiting for transfers between devices  6.24 us (17%)
  between operations  0.69 us (2%)
    all_to_all x1, starting transfers between devices, on_device(): lax.all_to_all(copies, ('z', 'pair'), split_axis=0, concat_axis=0, tiled=...  6.82 us
    pallas_call x1, Pallas kernels, on_device(): pl.pallas_call(functools.partial(prepare_kernel, capacity), out_shape=(ja...  5.79 us
    pallas_call x1, Pallas kernels, on_device(): pl.pallas_call(functools.partial(other_heads_kernel, half), out_shape=jax...  4.58 us
    all_to_all x1, starting transfers between devices, on_device(): lax.all_to_all(units, ('z', 'pair'), split_axis=0, concat_axis=0, tiled=T...  3.59 us
    all_to_all x1, waiting for transfers between devices, on_device(): lax.all_to_all(copies, ('z', 'pair'), split_axis=0, concat_axis=0, tiled=...  3.13 us
    ppermute x2, starting transfers between devices, swapped(): return lax.ppermute(value, axis, [(0, 1), (1, 0)])  2.54 us
    pallas_call x1, Pallas kernels, on_device(): pl.pallas_call(suffix_kernel, out_shape=jax.ShapeDtypeStruct((n_req, 2, U...  2.48 us
    ppermute x2, waiting for transfers between devices, swapped(): return lax.ppermute(value, axis, [(0, 1), (1, 0)])  1.94 us
  transfers between devices with their start and end apart: 4, of which 3 were waited for; matrix products, arithmetic and copies ran while one was open for 0% of the time, Pallas kernels for 35%

profile of v5, /device:TPU:0, one launch (start us, length us, event | category | flops | bytes accessed | tf_op | source)
XLA Modules:
  0.0 35.3 jit_solution(5152033057088972413)
XLA Ops:
  0.0 0.5 %collective-permute-start = (bf16[32,64,256]{2,1,0:T(8,128)(2,1)}, bf16[32,64,256]{2,1,0:T(8,128)(2,1)S(1)}, u32[]{:S(2)}, u32[]{:S(2)}) collective-permute-start(bf16[32,64,256]{2,1,0:T(8,128)(2,1)} %bitcast.12), channel_id=1, source_target_pairs={{0,4},{4,0},{1,5},{5,1},{2,6},{6,2},{3,7},{7,3},{8,12},{12,8},{9,1... | collective-permute-start | bytes 3145736 | tf_op jit(solution)/shard_map/ppermute | solution.py:25
  0.5 1.8 %query_copies.1 = bf16[8,16,1024]{2,1,0:T(8,128)(2,1)} custom-call(bf16[16,1024]{1,0:T(8,128)(2,1)} %queries_ref.1), custom_call_target="tpu_custom_call" | custom-call | tf_op jit(solution)/shard_map/query_copies/pallas_call | solution.py:284
  2.3 6.8 %all-to-all-start = ((bf16[8,16,1024]{2,1,0:T(8,128)(2,1)}), bf16[8,16,1024]{2,1,0:T(8,128)(2,1)S(1)}, u32[]{:S(2)}, u32[]{:S(2)}) async-start(bf16[8,16,1024]{2,1,0:T(8,128)(2,1)} %query_copies.1), calls=%async_computation | async-start | bytes 524288 | tf_op jit(solution)/shard_map/all_to_all | solution.py:292
  9.7 0.0 collective-permute-done.far_ref
  9.8 5.8 %prepare.1 = (f32[128,128]{1,0:T(8,128)S(1)}, f32[8,128]{1,0:T(8,128)S(1)}, bf16[4,512,128]{2,1,0:T(8,128)(2,1)S(1)}, bf16[4,128,512]{2,1,0:T(8,128)(2,1)S(1)}, f32[4,8,256]{2,1,0:T(8,128)S(1)}) custom-call(s32[1]{0:T(128)S(6)} %copy.7.length_ref, bf16[16,1024]{1,0:T(8,128)(2,1)} %queries_ref.1, bf16[4096,256]{1,0:T(8,128)(2,1)} %bitcast.10, ...), custom_call_target="tpu_custom_call" | custom-call | flops 268435456 | bytes 4194304 | tf_op jit(solution)/shard_map/prepare/pallas_call | solution.py:295
  15.6 3.1 %all-to-all-done = bf16[8,16,1024]{2,1,0:T(8,128)(2,1)S(1)} async-done(((bf16[8,16,1024]{2,1,0:T(8,128)(2,1)}), bf16[8,16,1024]{2,1,0:T(8,128)(2,1)S(1)}, u32[]{:S(2)}, u32[]{:S(2)}) %all-to-all-start) | async-done | bytes 262176 | tf_op jit(solution)/shard_map/all_to_all | solution.py:292
  18.7 2.5 %suffix_parts.1 = bf16[4,2,144,128]{3,2,1,0:T(8,128)(2,1)} custom-call(bf16[4,512,128]{2,1,0:T(8,128)(2,1)S(1)} %get-tuple-element.12.keys_ref, bf16[4,128,512]{2,1,0:T(8,128)(2,1)S(1)} %get-tuple-element.13.values_ref, f32[4,8,256]{2,1,0:T(8,128)S(1)} %get-tuple-element.14.member_ref, bf16[4,2,16,1024]{3,2,1,0:T(8,128)(2,1)S(1)} %bitcast.7, ...), custom_call_target="tpu_custom_call" | custom-call | tf_op jit(solution)/shard_map/suffix_parts/pallas_call | solution.py:331
  21.2 3.6 %all-to-all-start.1 = ((bf16[8,144,128]{2,1,0:T(8,128)(2,1)}), bf16[8,144,128]{2,1,0:T(8,128)(2,1)S(1)}, u32[]{:S(2)}, u32[]{:S(2)}) async-start(bf16[8,144,128]{2,1,0:T(8,128)(2,1)} %bitcast.5), calls=%async_computation.1 | async-start | bytes 589824 | tf_op jit(solution)/shard_map/all_to_all | solution.py:341
  24.8 4.6 %other_heads.1 = bf16[144,128]{1,0:T(8,128)(2,1)S(1)} custom-call(s32[1]{0:T(128)S(6)} %copy.7.length_ref, bf16[4,2,16,1024]{3,2,1,0:T(8,128)(2,1)S(1)} %bitcast.8, bf16[4096,256]{1,0:T(8,128)(2,1)} %bitcast.11), custom_call_target="tpu_custom_call" | custom-call | flops 268435456 | bytes 2097152 | tf_op jit(solution)/shard_map/other_heads/pallas_call | solution.py:343
  29.3 2.1 %collective-permute-start.1 = (bf16[144,128]{1,0:T(8,128)(2,1)S(1)}, bf16[144,128]{1,0:T(8,128)(2,1)S(1)}, u32[]{:S(2)}, u32[]{:S(2)}) collective-permute-start(bf16[144,128]{1,0:T(8,128)(2,1)S(1)} %other_heads.1), channel_id=1, source_target_pairs={{0,1},{1,0},{2,3},{3,2},{4,5},{5,4},{6,7},{7,6},{8,9},{9,8},{10,11... | collective-permute-start | bytes 110600 | tf_op jit(solution)/shard_map/ppermute | solution.py:25
  31.4 1.9 %collective-permute-done.1.last_ref = bf16[144,128]{1,0:T(8,128)(2,1)S(1)} collective-permute-done((bf16[144,128]{1,0:T(8,128)(2,1)S(1)}, bf16[144,128]{1,0:T(8,128)(2,1)S(1)}, u32[]{:S(2)}, u32[]{:S(2)}) %collective-permute-start.1) | collective-permute-done | bytes 36896 | tf_op jit(solution)/shard_map/ppermute | solution.py:25
  33.4 1.2 %all-to-all-done.1 = bf16[8,144,128]{2,1,0:T(8,128)(2,1)S(1)} async-done(((bf16[8,144,128]{2,1,0:T(8,128)(2,1)}), bf16[8,144,128]{2,1,0:T(8,128)(2,1)S(1)}, u32[]{:S(2)}, u32[]{:S(2)}) %all-to-all-start.1) | async-done | bytes 294944 | tf_op jit(solution)/shard_map/all_to_all | solution.py:341
  34.5 0.8 %combine.1 = f32[16,1024]{1,0:T(8,128)} custom-call(bf16[4,2,144,128]{3,2,1,0:T(8,128)(2,1)S(1)} %bitcast.9, bf16[144,128]{1,0:T(8,128)(2,1)S(1)} %collective-permute-done.1.last_ref), custom_call_target="tpu_custom_call" | custom-call | tf_op jit(solution)/shard_map/combine/pallas_call | solution.py:357
Async XLA Ops:
  0.0 9.7 %collective-permute-start = (bf16[32,64,256]{2,1,0:T(8,128)(2,1)}, bf16[32,64,256]{2,1,0:T(8,128)(2,1)S(1)}, u32[]{:S(2)}, u32[]{:S(2)}) collective-permute-start(bf16[32,64,256]{2,1,0:T(8,128)(2,1)} %bitcast.12), channel_id=1, source_target_pairs={{0,4},{4,0},{1,5},{5,1},{2,6},{6,2},{3,7},{7,3},{8,12},{12,8},{9,1... | collective-permute-start | bytes 3145736 | tf_op jit(solution)/shard_map/ppermute | solution.py:25
  2.3 16.4 %all-to-all-start = ((bf16[8,16,1024]{2,1,0:T(8,128)(2,1)}), bf16[8,16,1024]{2,1,0:T(8,128)(2,1)S(1)}, u32[]{:S(2)}, u32[]{:S(2)}) async-start(bf16[8,16,1024]{2,1,0:T(8,128)(2,1)} %query_copies.1), calls=%async_computation | async-start | bytes 524288 | tf_op jit(solution)/shard_map/all_to_all | solution.py:292
  21.2 13.4 %all-to-all-start.1 = ((bf16[8,144,128]{2,1,0:T(8,128)(2,1)}), bf16[8,144,128]{2,1,0:T(8,128)(2,1)S(1)}, u32[]{:S(2)}, u32[]{:S(2)}) async-start(bf16[8,144,128]{2,1,0:T(8,128)(2,1)} %bitcast.5), calls=%async_computation.1 | async-start | bytes 589824 | tf_op jit(solution)/shard_map/all_to_all | solution.py:341
  29.3 4.0 %collective-permute-start.1 = (bf16[144,128]{1,0:T(8,128)(2,1)S(1)}, bf16[144,128]{1,0:T(8,128)(2,1)S(1)}, u32[]{:S(2)}, u32[]{:S(2)}) collective-permute-start(bf16[144,128]{1,0:T(8,128)(2,1)S(1)} %other_heads.1), channel_id=1, source_target_pairs={{0,1},{1,0},{2,3},{3,2},{4,5},{5,4},{6,7},{7,6},{8,9},{9,8},{10,11... | collective-permute-start | bytes 110600 | tf_op jit(solution)/shard_map/ppermute | solution.py:25

commit v6 on v5

--- a/solution.py
+++ b/solution.py
@@ -21,8 +21,8 @@
 to_exp2 = HD ** (-0.5) * 1.4426950408889634
 
 
-def swapped(value, axis):
-    return lax.ppermute(value, axis, [(0, 1), (1, 0)])
+def swapped(value, axis, mask=1):
+    return lax.ppermute(value, axis, [(i, i ^ mask) for i in range(lax.axis_size(axis))])
 
 
 def stacked_heads(q):
@@ -90,17 +90,6 @@
 
 def iota(shape, axis):
     return lax.broadcasted_iota(jnp.int32, shape, axis)
-
-
-def copies_kernel(queries_ref, out_ref, sems):
-    copies = [
-        pltpu.make_async_copy(queries_ref, out_ref.at[i], sems.at[i])
-        for i in range(out_ref.shape[0])
-    ]
-    for copy in copies:
-        copy.start()
-    for copy in copies:
-        copy.wait()
 
 
 def prompt_chunks(prompt_ref, held_ref, sems):
@@ -130,9 +119,8 @@
 
 
 def prepare_kernel(
-    capacity, length_ref, own_ref, prompt_ref, table_ref, parents_ref, near_ref, far_ref,
-    summed_ref, stats_ref, keys_ref, values_ref, member_ref,
-    rows_ref, own, held, table, parents, near, sems, prompt_sems,
+    capacity, table_ref, parents_ref, near_ref, far_ref, keys_ref, values_ref, member_ref,
+    rows_ref, table, parents, near, sems,
 ):
     n_req = keys_ref.shape[0]
     slots, half, _ = near.shape
@@ -143,11 +131,10 @@
     small = [
         pltpu.make_async_copy(source, target, sems.at[i])
         for i, (source, target) in enumerate(
-            [(table_ref, table), (parents_ref, parents), (near_ref, near), (own_ref, own)]
+            [(table_ref, table), (parents_ref, parents), (near_ref, near)]
         )
     ]
-    chunks = prompt_chunks(prompt_ref, held, prompt_sems)
-    for copy in small + chunks:
+    for copy in small:
         copy.start()
 
     small[0].wait()
@@ -195,34 +182,34 @@
             values.append(content[:, HD:])
         values_ref[d] = jnp.concatenate(values, axis=0).T
 
-    small[3].wait()
-    top, total, summed = prompt_part(length_ref[0], half, held, chunks, stacked_heads(own[...]))
-    summed_ref[...] = summed
-    stats_ref[...] = jnp.concatenate([top, total, jnp.zeros((6, VECS), jnp.float32)], axis=0)
-
-
-def other_heads_kernel(half, length_ref, gathered_ref, prompt_ref, out_ref, held, prompt_sems):
+
+def prompt_kernel(
+    half, length_ref, own_ref, pair_ref, prompt_ref, summed_ref, stats_ref, out_ref,
+    held, prompt_sems,
+):
     chunks = prompt_chunks(prompt_ref, held, prompt_sems)
     for copy in chunks:
         copy.start()
-    z, parity = lax.axis_index("z"), lax.axis_index("pair")
-    vectors = stacked_heads(gathered_ref[z, 1 - parity])
-    store_unit(out_ref, *prompt_part(length_ref[0], half, held, chunks, vectors))
-
-
-def suffix_kernel(keys_ref, values_ref, member_ref, queries_ref, summed_ref, stats_ref, out_ref):
-    n_req = queries_ref.shape[0]
+    vectors = jnp.concatenate([stacked_heads(own_ref[...]), stacked_heads(pair_ref[...])], axis=0)
+    top, total, summed = prompt_part(length_ref[0], half, held, chunks, vectors)
+    summed_ref[...] = summed[:, :VECS]
+    stats_ref[...] = jnp.concatenate(
+        [top[:, :VECS], total[:, :VECS], jnp.zeros((6, VECS), jnp.float32)], axis=0
+    )
+    store_unit(out_ref, top[:, VECS:], total[:, VECS:], summed[:, VECS:])
+
+
+def suffix_kernel(keys_ref, values_ref, member_ref, *rest):
+    queries, out_ref = rest[:-1], rest[-1]
+    n_req = keys_ref.shape[0]
     n_slots = member_ref.shape[1]
     half = keys_ref.shape[1] // n_slots
     z, parity = lax.axis_index("z"), lax.axis_index("pair")
     for d in range(n_req):
         target = z ^ d
+        own_ref, pair_ref = queries[2 * d : 2 * d + 2]
         vectors = jnp.concatenate(
-            [
-                stacked_heads(queries_ref[target, parity]),
-                stacked_heads(queries_ref[target, 1 - parity]),
-            ],
-            axis=0,
+            [stacked_heads(own_ref[...]), stacked_heads(pair_ref[...])], axis=0
         )
         scores = scores_of(keys_ref[d], vectors)
         scores = jnp.concatenate(
@@ -243,16 +230,15 @@
         for side in range(2):
             lanes = slice(side * VECS, (side + 1) * VECS)
             owner = parity if side == 0 else 1 - parity
-            part = (top[:, lanes], total[:, lanes], summed[:, lanes])
-            if d == 0 and side == 0:
-                part = merged([part, (stats_ref[0:1], stats_ref[1:2], summed_ref[...])])
-            store_unit(out_ref.at[target, owner], *part)
-
-
-def final_kernel(units_ref, last_ref, out_ref):
+            store_unit(
+                out_ref.at[target, owner], top[:, lanes], total[:, lanes], summed[:, lanes]
+            )
+
+
+def final_kernel(units_ref, last_ref, summed_ref, stats_ref, out_ref):
     n_req, n_pair = units_ref.shape[:2]
     parts = [load_unit(units_ref.at[r, p]) for r in range(n_req) for p in range(n_pair)]
-    parts.append(load_unit(last_ref))
+    parts += [load_unit(last_ref), (stats_ref[0:1], stats_ref[1:2], summed_ref[...])]
     _, total, summed = merged(parts)
     attended = (summed / total).T
     for h in range(HEADS):
@@ -276,92 +262,74 @@
     params = pltpu.CompilerParams(vmem_limit_bytes=40 * 2**20)
 
     hbm = pl.BlockSpec(memory_space=pltpu.HBM)
-    chunk_sems = pltpu.SemaphoreType.DMA((tokens // CHUNK,))
-    prompt = in_hbm(prompt_cache.reshape(tokens, width))
     near = pool.reshape(slots, half, width)
     far = swapped(near, "core")
-
-    copies = pl.pallas_call(
-        copies_kernel,
-        out_shape=jax.ShapeDtypeStruct((2 * n_req,) + queries.shape, jnp.bfloat16),
-        in_specs=[hbm],
-        out_specs=vmem,
-        scratch_shapes=[pltpu.SemaphoreType.DMA((2 * n_req,))],
-        name="query_copies",
-    )(in_hbm(queries))
-    gathered = lax.all_to_all(copies, ("z", "pair"), split_axis=0, concat_axis=0, tiled=True)
-    gathered = gathered.reshape(n_req, 2, BEAMS, HEADS * HD)
-
-    summed, stats, keys, values, member = pl.pallas_call(
+    sent = [queries, swapped(queries, "pair")]
+    arrived = [swapped(queries, "z", d) for d in range(1, n_req)]
+    for piece in arrived:
+        sent += [piece, swapped(piece, "pair")]
+
+    keys, values, member = pl.pallas_call(
         functools.partial(prepare_kernel, capacity),
         out_shape=(
-            jax.ShapeDtypeStruct((HD, VECS), jnp.float32),
-            jax.ShapeDtypeStruct((8, VECS), jnp.float32),
             jax.ShapeDtypeStruct((n_req, 2 * capacity * half, HD), jnp.bfloat16),
             jax.ShapeDtypeStruct((n_req, HD, 2 * capacity * half), jnp.bfloat16),
             jax.ShapeDtypeStruct((n_req, 2 * capacity, 2 * VECS), jnp.float32),
         ),
-        in_specs=[smem] + [hbm] * 5 + [vmem],
-        out_specs=(vmem,) * 5,
+        in_specs=[hbm] * 3 + [vmem],
+        out_specs=(vmem,) * 3,
         scratch_shapes=[
             pltpu.VMEM((2 * slots + 8, 2 * VECS), jnp.float32),
-            pltpu.VMEM(queries.shape, jnp.bfloat16),
-            pltpu.VMEM((tokens, width), jnp.bfloat16),
             pltpu.VMEM((SUF, rows), jnp.int32),
             pltpu.VMEM((1, rows), jnp.int32),
             pltpu.VMEM((slots, half, width), jnp.bfloat16),
-            pltpu.SemaphoreType.DMA((4,)),
-            chunk_sems,
+            pltpu.SemaphoreType.DMA((3,)),
+        ],
+        compiler_params=params,
+        name="prepare",
+    )(in_hbm(block_table.T), in_hbm(parents.reshape(1, rows)), in_hbm(near), far)
+
+    units = pl.pallas_call(
+        suffix_kernel,
+        out_shape=jax.ShapeDtypeStruct((n_req, 2, UNIT_ROWS, VECS), jnp.bfloat16),
+        in_specs=[vmem] * (3 + 2 * n_req),
+        out_specs=vmem,
+        compiler_params=params,
+        name="suffix_parts",
+    )(keys, values, member, *sent)
+    units, other = lax.optimization_barrier((units, sent[1]))
+    units = units.reshape(2 * n_req, UNIT_ROWS, VECS)
+    units = lax.all_to_all(units, ("z", "pair"), split_axis=0, concat_axis=0, tiled=True)
+
+    summed, stats, given = pl.pallas_call(
+        functools.partial(prompt_kernel, half),
+        out_shape=(
+            jax.ShapeDtypeStruct((HD, VECS), jnp.float32),
+            jax.ShapeDtypeStruct((8, VECS), jnp.float32),
+            jax.ShapeDtypeStruct((UNIT_ROWS, VECS), jnp.bfloat16),
+        ),
+        in_specs=[smem, vmem, vmem, hbm],
+        out_specs=(vmem,) * 3,
+        scratch_shapes=[
+            pltpu.VMEM((tokens, width), jnp.bfloat16),
+            pltpu.SemaphoreType.DMA((tokens // CHUNK,)),
         ],
         compiler_params=params,
         cost_estimate=pl.CostEstimate(
-            flops=4 * tokens * VECS * HD, bytes_accessed=4 * tokens * width, transcendentals=0
+            flops=8 * tokens * VECS * HD, bytes_accessed=2 * tokens * width, transcendentals=0
         ),
-        name="prepare",
-    )(
-        lengths,
-        in_hbm(queries),
-        prompt,
-        in_hbm(block_table.T),
-        in_hbm(parents.reshape(1, rows)),
-        in_hbm(near),
-        far,
-    )
-
-    units = pl.pallas_call(
-        suffix_kernel,
-        out_shape=jax.ShapeDtypeStruct((n_req, 2, UNIT_ROWS, VECS), jnp.bfloat16),
-        in_specs=[vmem] * 6,
-        out_specs=vmem,
-        compiler_params=params,
-        name="suffix_parts",
-    )(keys, values, member, gathered, summed, stats)
-    units, gathered = lax.optimization_barrier((units, gathered))
-    units = units.reshape(2 * n_req, UNIT_ROWS, VECS)
-    units = lax.all_to_all(units, ("z", "pair"), split_axis=0, concat_axis=0, tiled=True)
-
-    given = pl.pallas_call(
-        functools.partial(other_heads_kernel, half),
-        out_shape=jax.ShapeDtypeStruct((UNIT_ROWS, VECS), jnp.bfloat16),
-        in_specs=[smem, vmem, hbm],
-        out_specs=vmem,
-        scratch_shapes=[pltpu.VMEM((tokens, width), jnp.bfloat16), chunk_sems],
-        compiler_params=params,
-        cost_estimate=pl.CostEstimate(
-            flops=4 * tokens * VECS * HD, bytes_accessed=2 * tokens * width, transcendentals=0
-        ),
-        name="other_heads",
-    )(lengths, gathered, prompt)
+        name="prompt_part",
+    )(lengths, queries, other, in_hbm(prompt_cache.reshape(tokens, width)))
     last = swapped(given, "pair")
 
     return pl.pallas_call(
         final_kernel,
         out_shape=jax.ShapeDtypeStruct((BEAMS, HEADS * HD), jnp.float32),
-        in_specs=[vmem, vmem],
+        in_specs=[vmem] * 4,
         out_specs=vmem,
         compiler_params=params,
         name="combine",
-    )(units.reshape(n_req, 2, UNIT_ROWS, VECS), last)
+    )(units.reshape(n_req, 2, UNIT_ROWS, VECS), last, summed, stats)
 
 
 def solution(mesh):

time: 35.8 us -> 32.7 us (0.913)
  Pallas kernels: 15.5 us -> 10.5 us
  starting transfers between devices: 12.9 us -> 16.1 us
  waiting for transfers between devices: 6.24 us -> 5.17 us
    ppermute x2 -> x9, starting transfers between devices: 2.54 us -> 12.7 us  [swapped(): lax.ppermute(value, axis, [(i, i ^ mask) for i in range(lax.axis_size(axi...]
    all_to_all x1 -> x0, starting transfers between devices: 6.82 us -> none  [on_device(): lax.all_to_all(copies, ('z', 'pair'), split_axis=0, concat_axis=0, tiled=...]
    pallas_call x1, Pallas kernels: 5.79 us -> 1.65 us  [on_device(): pl.pallas_call(functools.partial(prepare_kernel, capacity), out_shape=(ja...]
    ppermute x2 -> x9, waiting for transfers between devices: 1.94 us -> 5.17 us  [swapped(): lax.ppermute(value, axis, [(i, i ^ mask) for i in range(lax.axis_size(axi...]
    all_to_all x1 -> x0, waiting for transfers between devices: 3.13 us -> none  [on_device(): lax.all_to_all(copies, ('z', 'pair'), split_axis=0, concat_axis=0, tiled=...]
    all_to_all x1, waiting for transfers between devices: 1.17 us -> 0.01 us  [on_device(): lax.all_to_all(units, ('z', 'pair'), split_axis=0, concat_axis=0, tiled=T...]
    pallas_call x2 -> x1, Pallas kernels: 6.4 us -> 5.56 us  [on_device(): pl.pallas_call(functools.partial(prompt_kernel, half), out_shape=(jax.Sha...]
  transfers between devices with their start and end apart: 4 -> 10, of which waited for: 3 -> 4; matrix products, arithmetic and copies ran while one was open for 0% -> 0% of each run, Pallas kernels for 35% -> 22%
where the time goes in v6:
time: 32.7 us; the launch traced here: 32.5 us
  starting transfers between devices  16.1 us (49%)
  Pallas kernels  10.5 us (32%)
  waiting for transfers between devices  5.17 us (16%)
  between operations  0.71 us (2%)
    ppermute x9, starting transfers between devices, swapped(): lax.ppermute(value, axis, [(i, i ^ mask) for i in range(lax.axis_size(axi...  12.7 us
    pallas_call x1, Pallas kernels, on_device(): pl.pallas_call(functools.partial(prompt_kernel, half), out_shape=(jax.Sha...  5.56 us
    ppermute x9, waiting for transfers between devices, swapped(): lax.ppermute(value, axis, [(i, i ^ mask) for i in range(lax.axis_size(axi...  5.17 us
    all_to_all x1, starting transfers between devices, on_device(): lax.all_to_all(units, ('z', 'pair'), split_axis=0, concat_axis=0, tiled=T...  3.42 us
    pallas_call x1, Pallas kernels, on_device(): pl.pallas_call(suffix_kernel, out_shape=jax.ShapeDtypeStruct((n_req, 2, U...  2.5 us
    pallas_call x1, Pallas kernels, on_device(): pl.pallas_call(functools.partial(prepare_kernel, capacity), out_shape=(ja...  1.65 us
    pallas_call x1, Pallas kernels, on_device(): pl.pallas_call(final_kernel, out_shape=jax.ShapeDtypeStruct((BEAMS, HEADS...  0.79 us
  transfers between devices with their start and end apart: 10, of which 4 were waited for; matrix products, arithmetic and copies ran while one was open for 0% of the time, Pallas kernels for 22%

profile of v6, /device:TPU:0, one launch (start us, length us, event | category | flops | bytes accessed | tf_op | source)
XLA Modules:
  0.0 32.5 jit_solution(7268635910411857521)
XLA Ops:
  0.0 0.5 %collective-permute-start = (bf16[32,64,256]{2,1,0:T(8,128)(2,1)}, bf16[32,64,256]{2,1,0:T(8,128)(2,1)S(1)}, u32[]{:S(2)}, u32[]{:S(2)}) collective-permute-start(bf16[32,64,256]{2,1,0:T(8,128)(2,1)} %bitcast.8), channel_id=1, source_target_pairs={{0,4},{4,0},{1,5},{5,1},{2,6},{6,2},{3,7},{7,3},{8,12},{12,8},{9,1... | collective-permute-start | bytes 3145736 | tf_op jit(solution)/shard_map/ppermute | solution.py:25
  0.5 2.6 %collective-permute-start.2 = (bf16[16,1024]{1,0:T(8,128)(2,1)}, bf16[16,1024]{1,0:T(8,128)(2,1)S(1)}, u32[]{:S(2)}, u32[]{:S(2)}) collective-permute-start(bf16[16,1024]{1,0:T(8,128)(2,1)} %own_ref.1), channel_id=1, source_target_pairs={{0,8},{8,0},{16,24},{24,16},{1,9},{9,1},{17,25},{25,17},{2,10},{10... | collective-permute-start | bytes 98312 | tf_op jit(solution)/shard_map/ppermute | solution.py:25
  3.1 2.6 %collective-permute-start.4 = (bf16[16,1024]{1,0:T(8,128)(2,1)}, bf16[16,1024]{1,0:T(8,128)(2,1)S(1)}, u32[]{:S(2)}, u32[]{:S(2)}) collective-permute-start(bf16[16,1024]{1,0:T(8,128)(2,1)} %own_ref.1), channel_id=1, source_target_pairs={{0,16},{8,24},{16,0},{24,8},{1,17},{9,25},{17,1},{25,9},{2,18},{10... | collective-permute-start | bytes 98312 | tf_op jit(solution)/shard_map/ppermute | solution.py:25
  5.7 0.0 collective-permute-start.6
  5.7 1.7 %collective-permute-start.1 = (bf16[16,1024]{1,0:T(8,128)(2,1)}, bf16[16,1024]{1,0:T(8,128)(2,1)S(1)}, u32[]{:S(2)}, u32[]{:S(2)}) collective-permute-start(bf16[16,1024]{1,0:T(8,128)(2,1)} %own_ref.1), channel_id=1, source_target_pairs={{0,1},{1,0},{2,3},{3,2},{4,5},{5,4},{6,7},{7,6},{8,9},{9,8},{10,11... | collective-permute-start | bytes 98312 | tf_op jit(solution)/shard_map/ppermute | solution.py:25
  7.4 0.0 collective-permute-done.2.rest_2_
  7.4 0.3 collective-permute-start.3
  7.7 1.0 %collective-permute-done.4.rest_4_ = bf16[16,1024]{1,0:T(8,128)(2,1)S(1)} collective-permute-done((bf16[16,1024]{1,0:T(8,128)(2,1)}, bf16[16,1024]{1,0:T(8,128)(2,1)S(1)}, u32[]{:S(2)}, u32[]{:S(2)}) %collective-permute-start.4) | collective-permute-done | bytes 32800 | tf_op jit(solution)/shard_map/ppermute | solution.py:25
  8.7 1.5 %collective-permute-start.5 = (bf16[16,1024]{1,0:T(8,128)(2,1)S(1)}, bf16[16,1024]{1,0:T(8,128)(2,1)S(1)}, u32[]{:S(2)}, u32[]{:S(2)}) collective-permute-start(bf16[16,1024]{1,0:T(8,128)(2,1)S(1)} %collective-permute-done.4.rest_4_), channel_id=1, source_target_pairs={{0,1},{1,0},{2,3},{3,2},{4,5},{5,4},{6,7},{7,6},{8,9},{9,8},{10,11... | collective-permute-start | bytes 98312 | tf_op jit(solution)/shard_map/ppermute | solution.py:25
  10.2 1.4 %collective-permute-done.6.rest_6_ = bf16[16,1024]{1,0:T(8,128)(2,1)S(1)} collective-permute-done((bf16[16,1024]{1,0:T(8,128)(2,1)}, bf16[16,1024]{1,0:T(8,128)(2,1)S(1)}, u32[]{:S(2)}, u32[]{:S(2)}) %collective-permute-start.6) | collective-permute-done | bytes 32800 | tf_op jit(solution)/shard_map/ppermute | solution.py:25
  11.6 1.5 %collective-permute-start.7 = (bf16[16,1024]{1,0:T(8,128)(2,1)S(1)}, bf16[16,1024]{1,0:T(8,128)(2,1)S(1)}, u32[]{:S(2)}, u32[]{:S(2)}) collective-permute-start(bf16[16,1024]{1,0:T(8,128)(2,1)S(1)} %collective-permute-done.6.rest_6_), channel_id=1, source_target_pairs={{0,1},{1,0},{2,3},{3,2},{4,5},{5,4},{6,7},{7,6},{8,9},{9,8},{10,11... | collective-permute-start | bytes 98312 | tf_op jit(solution)/shard_map/ppermute | solution.py:25
  13.1 0.0 collective-permute-done.far_ref
  13.1 1.7 %prepare.1 = (bf16[4,512,128]{2,1,0:T(8,128)(2,1)S(1)}, bf16[4,128,512]{2,1,0:T(8,128)(2,1)S(1)}, f32[4,8,256]{2,1,0:T(8,128)S(1)}) custom-call(s32[4,128]{1,0:T(4,128)} %bitcast.10, s32[1,128]{1,0:T(1,128)} %bitcast.11, bf16[32,64,256]{2,1,0:T(8,128)(2,1)} %bitcast.9, bf16[32,64,256]{2,1,0:T(8,128)(2,1)S(1)} %collective-permute-done.far_ref), custom_call_target="tpu_custom_call" | custom-call | tf_op jit(solution)/shard_map/prepare/pallas_call | solution.py:272
  14.8 0.0 collective-permute-done.1.rest_1_.pair_ref
  14.8 0.0 collective-permute-done.3.rest_3_
  14.8 0.0 collective-permute-done.5.rest_5_
  14.8 0.7 %collective-permute-done.7.rest_7_ = bf16[16,1024]{1,0:T(8,128)(2,1)S(1)} collective-permute-done((bf16[16,1024]{1,0:T(8,128)(2,1)S(1)}, bf16[16,1024]{1,0:T(8,128)(2,1)S(1)}, u32[]{:S(2)}, u32[]{:S(2)}) %collective-permute-start.7) | collective-permute-done | bytes 32800 | tf_op jit(solution)/shard_map/ppermute | solution.py:25
  15.5 2.5 %suffix_parts.1 = bf16[4,2,144,128]{3,2,1,0:T(8,128)(2,1)} custom-call(bf16[4,512,128]{2,1,0:T(8,128)(2,1)S(1)} %get-tuple-element.13.keys_ref, bf16[4,128,512]{2,1,0:T(8,128)(2,1)S(1)} %get-tuple-element.14.values_ref, f32[4,8,256]{2,1,0:T(8,128)S(1)} %get-tuple-element.15.member_ref, bf16[16,1024]{1,0:T(8,128)(2,1)S(1)} %copy-done, ...), custom_call_target="tpu_custom_call" | custom-call | tf_op jit(solution)/shard_map/suffix_parts/pallas_call | solution.py:292
  18.0 3.4 %all-to-all-start = ((bf16[8,144,128]{2,1,0:T(8,128)(2,1)}), bf16[8,144,128]{2,1,0:T(8,128)(2,1)S(1)}, u32[]{:S(2)}, u32[]{:S(2)}) async-start(bf16[8,144,128]{2,1,0:T(8,128)(2,1)} %bitcast.3), calls=%async_computation | async-start | bytes 589824 | tf_op jit(solution)/shard_map/all_to_all | solution.py:302
  22.1 5.6 %prompt_part.1 = (f32[128,128]{1,0:T(8,128)S(1)}, f32[8,128]{1,0:T(8,128)S(1)}, bf16[144,128]{1,0:T(8,128)(2,1)S(1)}) custom-call(s32[1]{0:T(128)S(6)} %copy.7.length_ref, bf16[16,1024]{1,0:T(8,128)(2,1)S(1)} %copy-done, bf16[16,1024]{1,0:T(8,128)(2,1)S(1)} %collective-permute-done.1.rest_1_.pair_ref, bf16[4096,256]{1,0:T(8,128)(2,1)} %bitcast.7), custom_call_target="tpu_custom_call" | custom-call | flops 536870912 | bytes 2097152 | tf_op jit(solution)/shard_map/prompt_part/pallas_call | solution.py:304
  27.7 2.0 %collective-permute-start.8 = (bf16[144,128]{1,0:T(8,128)(2,1)S(1)}, bf16[144,128]{1,0:T(8,128)(2,1)S(1)}, u32[]{:S(2)}, u32[]{:S(2)}) collective-permute-start(bf16[144,128]{1,0:T(8,128)(2,1)S(1)} %get-tuple-element.18), channel_id=1, source_target_pairs={{0,1},{1,0},{2,3},{3,2},{4,5},{5,4},{6,7},{7,6},{8,9},{9,8},{10,11... | collective-permute-start | bytes 110600 | tf_op jit(solution)/shard_map/ppermute | solution.py:25
  29.7 2.0 %collective-permute-done.8.last_ref = bf16[144,128]{1,0:T(8,128)(2,1)S(1)} collective-permute-done((bf16[144,128]{1,0:T(8,128)(2,1)S(1)}, bf16[144,128]{1,0:T(8,128)(2,1)S(1)}, u32[]{:S(2)}, u32[]{:S(2)}) %collective-permute-start.8) | collective-permute-done | bytes 36896 | tf_op jit(solution)/shard_map/ppermute | solution.py:25
  31.7 0.0 all-to-all-done
  31.7 0.8 %combine.1 = f32[16,1024]{1,0:T(8,128)} custom-call(bf16[4,2,144,128]{3,2,1,0:T(8,128)(2,1)S(1)} %bitcast.6, bf16[144,128]{1,0:T(8,128)(2,1)S(1)} %collective-permute-done.8.last_ref, f32[128,128]{1,0:T(8,128)S(1)} %get-tuple-element.19.summed_ref, f32[8,128]{1,0:T(8,128)S(1)} %get-tuple-element.20.stats_ref), custom_call_target="tpu_custom_call" | custom-call | tf_op jit(solution)/shard_map/combine/pallas_call | solution.py:325
  (2 shorter events, 0.0 us)
Async XLA Ops:
  0.0 15.5 %copy-start = (bf16[16,1024]{1,0:T(8,128)(2,1)S(1)}, bf16[16,1024]{1,0:T(8,128)(2,1)}, u32[]{:S(2)}) copy-start(bf16[16,1024]{1,0:T(8,128)(2,1)} %own_ref.1) | copy-start | bytes 98308
  0.0 13.1 %collective-permute-start = (bf16[32,64,256]{2,1,0:T(8,128)(2,1)}, bf16[32,64,256]{2,1,0:T(8,128)(2,1)S(1)}, u32[]{:S(2)}, u32[]{:S(2)}) collective-permute-start(bf16[32,64,256]{2,1,0:T(8,128)(2,1)} %bitcast.8), channel_id=1, source_target_pairs={{0,4},{4,0},{1,5},{5,1},{2,6},{6,2},{3,7},{7,3},{8,12},{12,8},{9,1... | collective-permute-start | bytes 3145736 | tf_op jit(solution)/shard_map/ppermute | solution.py:25
  0.5 6.9 %collective-permute-start.2 = (bf16[16,1024]{1,0:T(8,128)(2,1)}, bf16[16,1024]{1,0:T(8,128)(2,1)S(1)}, u32[]{:S(2)}, u32[]{:S(2)}) collective-permute-start(bf16[16,1024]{1,0:T(8,128)(2,1)} %own_ref.1), channel_id=1, source_target_pairs={{0,8},{8,0},{16,24},{24,16},{1,9},{9,1},{17,25},{25,17},{2,10},{10... | collective-permute-start | bytes 98312 | tf_op jit(solution)/shard_map/ppermute | solution.py:25
  3.1 5.6 %collective-permute-start.4 = (bf16[16,1024]{1,0:T(8,128)(2,1)}, bf16[16,1024]{1,0:T(8,128)(2,1)S(1)}, u32[]{:S(2)}, u32[]{:S(2)}) collective-permute-start(bf16[16,1024]{1,0:T(8,128)(2,1)} %own_ref.1), channel_id=1, source_target_pairs={{0,16},{8,24},{16,0},{24,8},{1,17},{9,25},{17,1},{25,9},{2,18},{10... | collective-permute-start | bytes 98312 | tf_op jit(solution)/shard_map/ppermute | solution.py:25
  5.7 5.9 %collective-permute-start.6 = (bf16[16,1024]{1,0:T(8,128)(2,1)}, bf16[16,1024]{1,0:T(8,128)(2,1)S(1)}, u32[]{:S(2)}, u32[]{:S(2)}) collective-permute-start(bf16[16,1024]{1,0:T(8,128)(2,1)} %own_ref.1), channel_id=1, source_target_pairs={{0,24},{8,16},{16,8},{24,0},{1,25},{9,17},{17,9},{25,1},{2,26},{10... | collective-permute-start | bytes 98312 | tf_op jit(solution)/shard_map/ppermute | solution.py:25
  5.7 9.1 %collective-permute-start.1 = (bf16[16,1024]{1,0:T(8,128)(2,1)}, bf16[16,1024]{1,0:T(8,128)(2,1)S(1)}, u32[]{:S(2)}, u32[]{:S(2)}) collective-permute-start(bf16[16,1024]{1,0:T(8,128)(2,1)} %own_ref.1), channel_id=1, source_target_pairs={{0,1},{1,0},{2,3},{3,2},{4,5},{5,4},{6,7},{7,6},{8,9},{9,8},{10,11... | collective-permute-start | bytes 98312 | tf_op jit(solution)/shard_map/ppermute | solution.py:25
  7.4 7.4 %collective-permute-start.3 = (bf16[16,1024]{1,0:T(8,128)(2,1)S(1)}, bf16[16,1024]{1,0:T(8,128)(2,1)S(1)}, u32[]{:S(2)}, u32[]{:S(2)}) collective-permute-start(bf16[16,1024]{1,0:T(8,128)(2,1)S(1)} %collective-permute-done.2.rest_2_), channel_id=1, source_target_pairs={{0,1},{1,0},{2,3},{3,2},{4,5},{5,4},{6,7},{7,6},{8,9},{9,8},{10,11... | collective-permute-start | bytes 98312 | tf_op jit(solution)/shard_map/ppermute | solution.py:25
  8.7 6.1 %collective-permute-start.5 = (bf16[16,1024]{1,0:T(8,128)(2,1)S(1)}, bf16[16,1024]{1,0:T(8,128)(2,1)S(1)}, u32[]{:S(2)}, u32[]{:S(2)}) collective-permute-start(bf16[16,1024]{1,0:T(8,128)(2,1)S(1)} %collective-permute-done.4.rest_4_), channel_id=1, source_target_pairs={{0,1},{1,0},{2,3},{3,2},{4,5},{5,4},{6,7},{7,6},{8,9},{9,8},{10,11... | collective-permute-start | bytes 98312 | tf_op jit(solution)/shard_map/ppermute | solution.py:25
  11.6 3.9 %collective-permute-start.7 = (bf16[16,1024]{1,0:T(8,128)(2,1)S(1)}, bf16[16,1024]{1,0:T(8,128)(2,1)S(1)}, u32[]{:S(2)}, u32[]{:S(2)}) collective-permute-start(bf16[16,1024]{1,0:T(8,128)(2,1)S(1)} %collective-permute-done.6.rest_6_), channel_id=1, source_target_pairs={{0,1},{1,0},{2,3},{3,2},{4,5},{5,4},{6,7},{7,6},{8,9},{9,8},{10,11... | collective-permute-start | bytes 98312 | tf_op jit(solution)/shard_map/ppermute | solution.py:25
  18.0 13.7 %all-to-all-start = ((bf16[8,144,128]{2,1,0:T(8,128)(2,1)}), bf16[8,144,128]{2,1,0:T(8,128)(2,1)S(1)}, u32[]{:S(2)}, u32[]{:S(2)}) async-start(bf16[8,144,128]{2,1,0:T(8,128)(2,1)} %bitcast.3), calls=%async_computation | async-start | bytes 589824 | tf_op jit(solution)/shard_map/all_to_all | solution.py:302
  27.7 4.0 %collective-permute-start.8 = (bf16[144,128]{1,0:T(8,128)(2,1)S(1)}, bf16[144,128]{1,0:T(8,128)(2,1)S(1)}, u32[]{:S(2)}, u32[]{:S(2)}) collective-permute-start(bf16[144,128]{1,0:T(8,128)(2,1)S(1)} %get-tuple-element.18), channel_id=1, source_target_pairs={{0,1},{1,0},{2,3},{3,2},{4,5},{5,4},{6,7},{7,6},{8,9},{9,8},{10,11... | collective-permute-start | bytes 110600 | tf_op jit(solution)/shard_map/ppermute | solution.py:25

commit v7 on v6

--- a/solution.py
+++ b/solution.py
@@ -75,6 +75,11 @@
     ref[HD:, :] = jnp.concatenate(rows, axis=0).astype(jnp.bfloat16)
 
 
+def empty_part():
+    zeros = jnp.zeros((1, VECS), jnp.float32)
+    return zeros + big_negative, zeros, jnp.zeros((HD, VECS), jnp.float32)
+
+
 def load_unit(ref):
     stats = ref[HD:, :].astype(jnp.float32)
     top = stats[0:1] + stats[1:2] + stats[2:3]
@@ -92,35 +97,23 @@
     return lax.broadcasted_iota(jnp.int32, shape, axis)
 
 
-def prompt_chunks(prompt_ref, held_ref, sems):
-    copies = []
-    for i in range(held_ref.shape[0] // CHUNK):
-        part = pl.ds(i * CHUNK, CHUNK)
-        copies.append(pltpu.make_async_copy(prompt_ref.at[part], held_ref.at[part], sems.at[i]))
-    return copies
-
-
-def prompt_part(length, half, held_ref, copies, vectors):
-    parity = lax.axis_index("pair")
-    whole = lax.div(length, 2 * half)
-    valid = whole * half + jnp.clip(length - whole * (2 * half) - parity * half, 0, half)
+def prompt_part(valid, prompt_ref, vectors):
     parts = []
-    for i, copy in enumerate(copies):
-        copy.wait()
-        part = slice(i * CHUNK, (i + 1) * CHUNK)
-        scores = scores_of(held_ref[part, :HD], vectors)
+    for start in range(0, prompt_ref.shape[0], CHUNK):
+        part = slice(start, start + CHUNK)
+        scores = scores_of(prompt_ref[part, :HD], vectors)
         token = iota(scores.shape, 0)
-        scores = jnp.where(token < valid - i * CHUNK, scores, big_negative)
+        scores = jnp.where(token < valid - start, scores, big_negative)
         top, total, weights = weighted(scores)
-        parts.append((top, total, summed_of(held_ref[part, HD:], weights)))
+        parts.append((top, total, summed_of(prompt_ref[part, HD:], weights)))
         if len(parts) == 2:
             parts = [merged(parts)]
     return merged(parts)
 
 
 def prepare_kernel(
-    capacity, table_ref, parents_ref, near_ref, far_ref, keys_ref, values_ref, member_ref,
-    rows_ref, table, parents, near, sems,
+    capacity, length_ref, table_ref, parents_ref, near_ref, prompt_ref, far_ref,
+    keys_ref, values_ref, member_ref, held_ref, valid_ref, rows_ref, table, parents, near, sems,
 ):
     n_req = keys_ref.shape[0]
     slots, half, _ = near.shape
@@ -131,11 +124,17 @@
     small = [
         pltpu.make_async_copy(source, target, sems.at[i])
         for i, (source, target) in enumerate(
-            [(table_ref, table), (parents_ref, parents), (near_ref, near)]
+            [(table_ref, table), (parents_ref, parents), (near_ref, near), (prompt_ref, held_ref)]
         )
     ]
     for copy in small:
         copy.start()
+
+    length = length_ref[0]
+    whole = lax.div(length, 2 * half)
+    parity = lax.axis_index("pair")
+    valid = whole * half + jnp.clip(length - whole * (2 * half) - parity * half, 0, half)
+    valid_ref[...] = jnp.full(valid_ref.shape, valid, jnp.int32)
 
     small[0].wait()
     slot = iota((2 * slots, rows), 0)
@@ -181,58 +180,70 @@
             keys_ref[d, k * half : (k + 1) * half, :] = content[:, :HD]
             values.append(content[:, HD:])
         values_ref[d] = jnp.concatenate(values, axis=0).T
-
-
-def prompt_kernel(
-    half, length_ref, own_ref, pair_ref, prompt_ref, summed_ref, stats_ref, out_ref,
-    held, prompt_sems,
-):
-    chunks = prompt_chunks(prompt_ref, held, prompt_sems)
-    for copy in chunks:
-        copy.start()
-    vectors = jnp.concatenate([stacked_heads(own_ref[...]), stacked_heads(pair_ref[...])], axis=0)
-    top, total, summed = prompt_part(length_ref[0], half, held, chunks, vectors)
-    summed_ref[...] = summed[:, :VECS]
-    stats_ref[...] = jnp.concatenate(
-        [top[:, :VECS], total[:, :VECS], jnp.zeros((6, VECS), jnp.float32)], axis=0
-    )
-    store_unit(out_ref, top[:, VECS:], total[:, VECS:], summed[:, VECS:])
-
-
-def suffix_kernel(keys_ref, values_ref, member_ref, *rest):
-    queries, out_ref = rest[:-1], rest[-1]
-    n_req = keys_ref.shape[0]
+    small[3].wait()
+
+
+def all_vectors(own_ref, pair_ref):
+    return jnp.concatenate([stacked_heads(own_ref[...]), stacked_heads(pair_ref[...])], axis=0)
+
+
+def suffix_parts(requests, queries, keys_ref, values_ref, member_ref):
     n_slots = member_ref.shape[1]
     half = keys_ref.shape[1] // n_slots
+    scores = [
+        scores_of(keys_ref[d], all_vectors(*queries[2 * i : 2 * i + 2]))
+        for i, d in enumerate(requests)
+    ]
+    softmaxes = []
+    for d, score in zip(requests, scores):
+        pieces = [
+            jnp.where(
+                member_ref[d, k : k + 1, :] > 0.0,
+                score[k * half : (k + 1) * half],
+                big_negative,
+            )
+            for k in range(n_slots)
+        ]
+        softmaxes.append(weighted(jnp.concatenate(pieces, axis=0)))
+    return [
+        (
+            top,
+            total,
+            jnp.dot(
+                values_ref[d], weights.astype(jnp.bfloat16), preferred_element_type=jnp.float32
+            ),
+        )
+        for d, (top, total, weights) in zip(requests, softmaxes)
+    ]
+
+
+def half_of(part, side):
+    lanes = slice(side * VECS, (side + 1) * VECS)
+    return [x[:, lanes] for x in part]
+
+
+def away_kernel(keys_ref, values_ref, member_ref, *rest):
+    queries, out_ref = rest[:-1], rest[-1]
+    requests = tuple(reversed(range(1, keys_ref.shape[0])))
     z, parity = lax.axis_index("z"), lax.axis_index("pair")
-    for d in range(n_req):
-        target = z ^ d
-        own_ref, pair_ref = queries[2 * d : 2 * d + 2]
-        vectors = jnp.concatenate(
-            [stacked_heads(own_ref[...]), stacked_heads(pair_ref[...])], axis=0
-        )
-        scores = scores_of(keys_ref[d], vectors)
-        scores = jnp.concatenate(
-            [
-                jnp.where(
-                    member_ref[d, k : k + 1, :] > 0.0,
-                    scores[k * half : (k + 1) * half],
-                    big_negative,
-                )
-                for k in range(n_slots)
-            ],
-            axis=0,
-        )
-        top, total, weights = weighted(scores)
-        summed = jnp.dot(
-            values_ref[d], weights.astype(jnp.bfloat16), preferred_element_type=jnp.float32
-        )
-        for side in range(2):
-            lanes = slice(side * VECS, (side + 1) * VECS)
-            owner = parity if side == 0 else 1 - parity
-            store_unit(
-                out_ref.at[target, owner], top[:, lanes], total[:, lanes], summed[:, lanes]
-            )
+    parts = suffix_parts(requests, queries, keys_ref, values_ref, member_ref)
+    for d, part in zip(requests, parts):
+        store_unit(out_ref.at[z ^ d, parity], *half_of(part, 0))
+        store_unit(out_ref.at[z ^ d, 1 - parity], *half_of(part, 1))
+    for side in range(2):
+        store_unit(out_ref.at[z, side], *empty_part())
+
+
+def home_kernel(
+    keys_ref, values_ref, member_ref, own_ref, pair_ref, prompt_ref, valid_ref,
+    summed_ref, stats_ref, out_ref,
+):
+    (suffix,) = suffix_parts((0,), (own_ref, pair_ref), keys_ref, values_ref, member_ref)
+    prompt = prompt_part(valid_ref[0:1, :], prompt_ref, all_vectors(own_ref, pair_ref))
+    part = merged([prompt, suffix])
+    top, total, summed_ref[...] = half_of(part, 0)
+    stats_ref[...] = jnp.concatenate([top, total, jnp.zeros((6, VECS), jnp.float32)], axis=0)
+    store_unit(out_ref, *half_of(part, 1))
 
 
 def final_kernel(units_ref, last_ref, summed_ref, stats_ref, out_ref):
@@ -257,69 +268,74 @@
     slots, _, half, width = pool.shape
     tokens = prompt_cache.shape[2]
     rows = block_table.shape[0]
-    smem = pl.BlockSpec(memory_space=pltpu.SMEM)
     vmem = pl.BlockSpec(memory_space=pltpu.VMEM)
     params = pltpu.CompilerParams(vmem_limit_bytes=40 * 2**20)
 
     hbm = pl.BlockSpec(memory_space=pltpu.HBM)
     near = pool.reshape(slots, half, width)
     far = swapped(near, "core")
-    sent = [queries, swapped(queries, "pair")]
-    arrived = [swapped(queries, "z", d) for d in range(1, n_req)]
+    arrived = [swapped(queries, "z", d) for d in reversed(range(1, n_req))]
+    sent = []
     for piece in arrived:
         sent += [piece, swapped(piece, "pair")]
-
-    keys, values, member = pl.pallas_call(
+    other = swapped(queries, "pair")
+
+    keys, values, member, prompt, valid = pl.pallas_call(
         functools.partial(prepare_kernel, capacity),
         out_shape=(
             jax.ShapeDtypeStruct((n_req, 2 * capacity * half, HD), jnp.bfloat16),
             jax.ShapeDtypeStruct((n_req, HD, 2 * capacity * half), jnp.bfloat16),
             jax.ShapeDtypeStruct((n_req, 2 * capacity, 2 * VECS), jnp.float32),
+            jax.ShapeDtypeStruct((tokens, width), jnp.bfloat16),
+            jax.ShapeDtypeStruct((8, 2 * VECS), jnp.int32),
         ),
-        in_specs=[hbm] * 3 + [vmem],
-        out_specs=(vmem,) * 3,
+        in_specs=[pl.BlockSpec(memory_space=pltpu.SMEM)] + [hbm] * 4 + [vmem],
+        out_specs=(vmem,) * 5,
         scratch_shapes=[
             pltpu.VMEM((2 * slots + 8, 2 * VECS), jnp.float32),
             pltpu.VMEM((SUF, rows), jnp.int32),
             pltpu.VMEM((1, rows), jnp.int32),
             pltpu.VMEM((slots, half, width), jnp.bfloat16),
-            pltpu.SemaphoreType.DMA((3,)),
+            pltpu.SemaphoreType.DMA((4,)),
         ],
         compiler_params=params,
         name="prepare",
-    )(in_hbm(block_table.T), in_hbm(parents.reshape(1, rows)), in_hbm(near), far)
+    )(
+        lengths,
+        in_hbm(block_table.T),
+        in_hbm(parents.reshape(1, rows)),
+        in_hbm(near),
+        in_hbm(prompt_cache.reshape(tokens, width)),
+        far,
+    )
 
     units = pl.pallas_call(
-        suffix_kernel,
+        away_kernel,
         out_shape=jax.ShapeDtypeStruct((n_req, 2, UNIT_ROWS, VECS), jnp.bfloat16),
-        in_specs=[vmem] * (3 + 2 * n_req),
+        in_specs=[vmem] * (3 + len(sent)),
         out_specs=vmem,
         compiler_params=params,
-        name="suffix_parts",
+        name="suffix_away",
     )(keys, values, member, *sent)
-    units, other = lax.optimization_barrier((units, sent[1]))
+    units, other = lax.optimization_barrier((units, other))
     units = units.reshape(2 * n_req, UNIT_ROWS, VECS)
     units = lax.all_to_all(units, ("z", "pair"), split_axis=0, concat_axis=0, tiled=True)
 
     summed, stats, given = pl.pallas_call(
-        functools.partial(prompt_kernel, half),
+        home_kernel,
         out_shape=(
             jax.ShapeDtypeStruct((HD, VECS), jnp.float32),
             jax.ShapeDtypeStruct((8, VECS), jnp.float32),
             jax.ShapeDtypeStruct((UNIT_ROWS, VECS), jnp.bfloat16),
         ),
-        in_specs=[smem, vmem, vmem, hbm],
+        in_specs=[vmem] * 7,
         out_specs=(vmem,) * 3,
-        scratch_shapes=[
-            pltpu.VMEM((tokens, width), jnp.bfloat16),
-            pltpu.SemaphoreType.DMA((tokens // CHUNK,)),
-        ],
         compiler_params=params,
         cost_estimate=pl.CostEstimate(
             flops=8 * tokens * VECS * HD, bytes_accessed=2 * tokens * width, transcendentals=0
         ),
-        name="prompt_part",
-    )(lengths, queries, other, in_hbm(prompt_cache.reshape(tokens, width)))
+        name="home_part",
+    )(keys, values, member, queries, other, prompt, valid)
     last = swapped(given, "pair")
 
     return pl.pallas_call(

time: 32.7 us -> 33.2 us (1.015)
  Pallas kernels: 10.5 us -> 7.61 us
  local copies, waits for them, and re-layouts: 0.01 us -> 2.83 us
  starting transfers between devices: 16.1 us -> 16.8 us
  waiting for transfers between devices: 5.17 us -> 4.8 us
    pallas_call x2, Pallas kernels: 8.05 us -> 4.84 us  [the longest x1 4.01 us: on_device(): pl.pallas_call(home_kernel, out_shape=(jax.ShapeDtypeStruct((HD, VECS), j...]
    unnamed x2 -> x8, local copies, waits for them, and re-layouts: 0.01 us -> 2.83 us
    all_to_all x1, starting transfers between devices: 3.42 us -> 3.99 us  [on_device(): lax.all_to_all(units, ('z', 'pair'), split_axis=0, concat_axis=0, tiled=T...]
    ppermute x9, waiting for transfers between devices: 5.17 us -> 4.8 us  [swapped(): lax.ppermute(value, axis, [(i, i ^ mask) for i in range(lax.axis_size(axi...]
  transfers between devices with their start and end apart: 10 -> 10, of which waited for: 4 -> 3; matrix products, arithmetic and copies ran while one was open for 0% -> 0% of each run, Pallas kernels for 22% -> 21%
where the time goes in v7:
time: 33.2 us; the launch traced here: 32.8 us
  starting transfers between devices  16.8 us (51%)
  Pallas kernels  7.61 us (23%)
  waiting for transfers between devices  4.8 us (14%)
  local copies, waits for them, and re-layouts  2.83 us (9%)
  between operations  0.73 us (2%)
    ppermute x9, starting transfers between devices, swapped(): lax.ppermute(value, axis, [(i, i ^ mask) for i in range(lax.axis_size(axi...  12.8 us
    ppermute x9, waiting for transfers between devices, swapped(): lax.ppermute(value, axis, [(i, i ^ mask) for i in range(lax.axis_size(axi...  4.8 us
    pallas_call x1, Pallas kernels, on_device(): pl.pallas_call(home_kernel, out_shape=(jax.ShapeDtypeStruct((HD, VECS), j...  4.01 us
    all_to_all x1, starting transfers between devices, on_device(): lax.all_to_all(units, ('z', 'pair'), split_axis=0, concat_axis=0, tiled=T...  3.99 us
    unnamed x8, local copies, waits for them, and re-layouts  2.83 us
    pallas_call x1, Pallas kernels, on_device(): pl.pallas_call(functools.partial(prepare_kernel, capacity), out_shape=(ja...  1.98 us
    pallas_call x1, Pallas kernels, on_device(): pl.pallas_call(away_kernel, out_shape=jax.ShapeDtypeStruct((n_req, 2, UNI...  0.83 us
    pallas_call x1, Pallas kernels, on_device(): pl.pallas_call(final_kernel, out_shape=jax.ShapeDtypeStruct((BEAMS, HEADS...  0.8 us
  transfers between devices with their start and end apart: 10, of which 3 were waited for; matrix products, arithmetic and copies ran while one was open for 0% of the time, Pallas kernels for 21%

profile of v7, /device:TPU:0, one launch (start us, length us, event | category | flops | bytes accessed | tf_op | source)
XLA Modules:
  0.0 32.8 jit_solution(14234983305190371325)
XLA Ops:
  0.0 0.5 %collective-permute-start = (bf16[32,64,256]{2,1,0:T(8,128)(2,1)}, bf16[32,64,256]{2,1,0:T(8,128)(2,1)S(1)}, u32[]{:S(2)}, u32[]{:S(2)}) collective-permute-start(bf16[32,64,256]{2,1,0:T(8,128)(2,1)} %bitcast.9), channel_id=1, source_target_pairs={{0,4},{4,0},{1,5},{5,1},{2,6},{6,2},{3,7},{7,3},{8,12},{12,8},{9,1... | collective-permute-start | bytes 3145736 | tf_op jit(solution)/shard_map/ppermute | solution.py:25
  0.5 4.6 %collective-permute-start.1 = (bf16[16,1024]{1,0:T(8,128)(2,1)}, bf16[16,1024]{1,0:T(8,128)(2,1)S(1)}, u32[]{:S(2)}, u32[]{:S(2)}) collective-permute-start(bf16[16,1024]{1,0:T(8,128)(2,1)} %own_ref.1), channel_id=1, source_target_pairs={{0,24},{8,16},{16,8},{24,0},{1,25},{9,17},{17,9},{25,1},{2,26},{10... | collective-permute-start | bytes 98312 | tf_op jit(solution)/shard_map/ppermute | solution.py:25
  5.1 0.0 collective-permute-start.3
  5.1 0.6 %collective-permute-start.5 = (bf16[16,1024]{1,0:T(8,128)(2,1)}, bf16[16,1024]{1,0:T(8,128)(2,1)S(1)}, u32[]{:S(2)}, u32[]{:S(2)}) collective-permute-start(bf16[16,1024]{1,0:T(8,128)(2,1)} %own_ref.1), channel_id=1, source_target_pairs={{0,8},{8,0},{16,24},{24,16},{1,9},{9,1},{17,25},{25,17},{2,10},{10... | collective-permute-start | bytes 98312 | tf_op jit(solution)/shard_map/ppermute | solution.py:25
  5.7 1.6 %collective-permute-done.1.rest_0_ = bf16[16,1024]{1,0:T(8,128)(2,1)S(1)} collective-permute-done((bf16[16,1024]{1,0:T(8,128)(2,1)}, bf16[16,1024]{1,0:T(8,128)(2,1)S(1)}, u32[]{:S(2)}, u32[]{:S(2)}) %collective-permute-start.1) | collective-permute-done | bytes 32800 | tf_op jit(solution)/shard_map/ppermute | solution.py:25
  7.3 1.5 %collective-permute-start.2 = (bf16[16,1024]{1,0:T(8,128)(2,1)S(1)}, bf16[16,1024]{1,0:T(8,128)(2,1)S(1)}, u32[]{:S(2)}, u32[]{:S(2)}) collective-permute-start(bf16[16,1024]{1,0:T(8,128)(2,1)S(1)} %collective-permute-done.1.rest_0_), channel_id=1, source_target_pairs={{0,1},{1,0},{2,3},{3,2},{4,5},{5,4},{6,7},{7,6},{8,9},{9,8},{10,11... | collective-permute-start | bytes 98312 | tf_op jit(solution)/shard_map/ppermute | solution.py:25
  8.9 1.2 %collective-permute-done.3.rest_2_ = bf16[16,1024]{1,0:T(8,128)(2,1)S(1)} collective-permute-done((bf16[16,1024]{1,0:T(8,128)(2,1)}, bf16[16,1024]{1,0:T(8,128)(2,1)S(1)}, u32[]{:S(2)}, u32[]{:S(2)}) %collective-permute-start.3) | collective-permute-done | bytes 32800 | tf_op jit(solution)/shard_map/ppermute | solution.py:25
  10.1 1.5 %collective-permute-start.4 = (bf16[16,1024]{1,0:T(8,128)(2,1)S(1)}, bf16[16,1024]{1,0:T(8,128)(2,1)S(1)}, u32[]{:S(2)}, u32[]{:S(2)}) collective-permute-start(bf16[16,1024]{1,0:T(8,128)(2,1)S(1)} %collective-permute-done.3.rest_2_), channel_id=1, source_target_pairs={{0,1},{1,0},{2,3},{3,2},{4,5},{5,4},{6,7},{7,6},{8,9},{9,8},{10,11... | collective-permute-start | bytes 98312 | tf_op jit(solution)/shard_map/ppermute | solution.py:25
  11.6 0.0 collective-permute-done.5.rest_4_
  11.6 0.5 %collective-permute-start.6 = (bf16[16,1024]{1,0:T(8,128)(2,1)S(1)}, bf16[16,1024]{1,0:T(8,128)(2,1)S(1)}, u32[]{:S(2)}, u32[]{:S(2)}) collective-permute-start(bf16[16,1024]{1,0:T(8,128)(2,1)S(1)} %collective-permute-done.5.rest_4_), channel_id=1, source_target_pairs={{0,1},{1,0},{2,3},{3,2},{4,5},{5,4},{6,7},{7,6},{8,9},{9,8},{10,11... | collective-permute-start | bytes 98312 | tf_op jit(solution)/shard_map/ppermute | solution.py:25
  12.1 1.5 %collective-permute-start.7 = (bf16[16,1024]{1,0:T(8,128)(2,1)}, bf16[16,1024]{1,0:T(8,128)(2,1)S(1)}, u32[]{:S(2)}, u32[]{:S(2)}) collective-permute-start(bf16[16,1024]{1,0:T(8,128)(2,1)} %own_ref.1), channel_id=1, source_target_pairs={{0,1},{1,0},{2,3},{3,2},{4,5},{5,4},{6,7},{7,6},{8,9},{9,8},{10,11... | collective-permute-start | bytes 98312 | tf_op jit(solution)/shard_map/ppermute | solution.py:25
  14.3 0.0 collective-permute-done.far_ref
  14.3 2.0 %prepare.1 = (bf16[4,512,128]{2,1,0:T(8,128)(2,1)S(1)}, bf16[4,128,512]{2,1,0:T(8,128)(2,1)S(1)}, f32[4,8,256]{2,1,0:T(8,128)S(1)}, bf16[4096,256]{1,0:T(8,128)(2,1)S(1)}, s32[8,256]{1,0:T(8,128)S(1)}) custom-call(s32[1]{0:T(128)S(6)} %copy.7.length_ref, s32[4,128]{1,0:T(4,128)} %bitcast.11, s32[1,128]{1,0:T(1,128)} %bitcast.12, ...), custom_call_target="tpu_custom_call" | custom-call | tf_op jit(solution)/shard_map/prepare/pallas_call | solution.py:283
  16.2 0.0 collective-permute-done.2.rest_1_
  16.3 0.8 %suffix_away.1 = bf16[4,2,144,128]{3,2,1,0:T(8,128)(2,1)S(1)} custom-call(bf16[4,512,128]{2,1,0:T(8,128)(2,1)S(1)} %get-tuple-element.15.keys_ref, bf16[4,128,512]{2,1,0:T(8,128)(2,1)S(1)} %get-tuple-element.16.values_ref, f32[4,8,256]{2,1,0:T(8,128)S(1)} %get-tuple-element.17.member_ref, bf16[16,1024]{1,0:T(8,128)(2,1)S(1)} %collective-permute-done.1.rest_0_, ...), custom_call_target="tpu_custom_call" | custom-call | tf_op jit(solution)/shard_map/suffix_away/pallas_call | solution.py:312
  17.1 0.7 %copy-done = bf16[4,2,144,128]{3,2,1,0:T(8,128)(2,1)} copy-done((bf16[4,2,144,128]{3,2,1,0:T(8,128)(2,1)}, bf16[4,2,144,128]{3,2,1,0:T(8,128)(2,1)S(1)}, u32[]{:S(2)}) %copy-start) | copy-done | bytes 294936
  17.8 0.6 %copy-done.2 = bf16[16,1024]{1,0:T(8,128)(2,1)} copy-done((bf16[16,1024]{1,0:T(8,128)(2,1)}, bf16[16,1024]{1,0:T(8,128)(2,1)S(1)}, u32[]{:S(2)}) %copy-start.2) | copy-done | bytes 32792
  18.5 4.0 %all-to-all-start = ((bf16[8,144,128]{2,1,0:T(8,128)(2,1)}), bf16[8,144,128]{2,1,0:T(8,128)(2,1)S(1)}, u32[]{:S(2)}, u32[]{:S(2)}) async-start(bf16[8,144,128]{2,1,0:T(8,128)(2,1)} %bitcast.7), calls=%async_computation | async-start | bytes 589824 | tf_op jit(solution)/shard_map/all_to_all | solution.py:322
  22.4 0.8 %copy-done.1 = bf16[16,1024]{1,0:T(8,128)(2,1)S(1)} copy-done((bf16[16,1024]{1,0:T(8,128)(2,1)S(1)}, bf16[16,1024]{1,0:T(8,128)(2,1)}, u32[]{:S(2)}) %copy-start.1) | copy-done | bytes 32792
  23.2 0.8 %copy-done.3 = bf16[16,1024]{1,0:T(8,128)(2,1)S(1)} copy-done((bf16[16,1024]{1,0:T(8,128)(2,1)S(1)}, bf16[16,1024]{1,0:T(8,128)(2,1)}, u32[]{:S(2)}) %copy-start.3) | copy-done | bytes 32792
  24.0 4.0 %home_part.1 = (f32[128,128]{1,0:T(8,128)S(1)}, f32[8,128]{1,0:T(8,128)S(1)}, bf16[144,128]{1,0:T(8,128)(2,1)S(1)}) custom-call(bf16[4,512,128]{2,1,0:T(8,128)(2,1)S(1)} %get-tuple-element.15.keys_ref, bf16[4,128,512]{2,1,0:T(8,128)(2,1)S(1)} %get-tuple-element.16.values_ref, f32[4,8,256]{2,1,0:T(8,128)S(1)} %get-tuple-element.17.member_ref, ...), custom_call_target="tpu_custom_call" | custom-call | flops 536870912 | bytes 2097152 | tf_op jit(solution)/shard_map/home_part/pallas_call | solution.py:324
  28.0 2.1 %collective-permute-start.8 = (bf16[144,128]{1,0:T(8,128)(2,1)S(1)}, bf16[144,128]{1,0:T(8,128)(2,1)S(1)}, u32[]{:S(2)}, u32[]{:S(2)}) collective-permute-start(bf16[144,128]{1,0:T(8,128)(2,1)S(1)} %get-tuple-element.22), channel_id=1, source_target_pairs={{0,1},{1,0},{2,3},{3,2},{4,5},{5,4},{6,7},{7,6},{8,9},{9,8},{10,11... | collective-permute-start | bytes 110600 | tf_op jit(solution)/shard_map/ppermute | solution.py:25
  30.1 1.9 %collective-permute-done.8.last_ref = bf16[144,128]{1,0:T(8,128)(2,1)S(1)} collective-permute-done((bf16[144,128]{1,0:T(8,128)(2,1)S(1)}, bf16[144,128]{1,0:T(8,128)(2,1)S(1)}, u32[]{:S(2)}, u32[]{:S(2)}) %collective-permute-start.8) | collective-permute-done | bytes 36896 | tf_op jit(solution)/shard_map/ppermute | solution.py:25
  32.0 0.8 %combine.1 = f32[16,1024]{1,0:T(8,128)} custom-call(bf16[4,2,144,128]{3,2,1,0:T(8,128)(2,1)S(1)} %bitcast.6, bf16[144,128]{1,0:T(8,128)(2,1)S(1)} %collective-permute-done.8.last_ref, f32[128,128]{1,0:T(8,128)S(1)} %get-tuple-element.23.summed_ref, f32[8,128]{1,0:T(8,128)S(1)} %get-tuple-element.24.stats_ref), custom_call_target="tpu_custom_call" | custom-call | tf_op jit(solution)/shard_map/combine/pallas_call | solution.py:341
  (8 shorter events, 0.0 us)
Async XLA Ops:
  0.0 14.3 %collective-permute-start = (bf16[32,64,256]{2,1,0:T(8,128)(2,1)}, bf16[32,64,256]{2,1,0:T(8,128)(2,1)S(1)}, u32[]{:S(2)}, u32[]{:S(2)}) collective-permute-start(bf16[32,64,256]{2,1,0:T(8,128)(2,1)} %bitcast.9), channel_id=1, source_target_pairs={{0,4},{4,0},{1,5},{5,1},{2,6},{6,2},{3,7},{7,3},{8,12},{12,8},{9,1... | collective-permute-start | bytes 3145736 | tf_op jit(solution)/shard_map/ppermute | solution.py:25
  0.5 6.9 %collective-permute-start.1 = (bf16[16,1024]{1,0:T(8,128)(2,1)}, bf16[16,1024]{1,0:T(8,128)(2,1)S(1)}, u32[]{:S(2)}, u32[]{:S(2)}) collective-permute-start(bf16[16,1024]{1,0:T(8,128)(2,1)} %own_ref.1), channel_id=1, source_target_pairs={{0,24},{8,16},{16,8},{24,0},{1,25},{9,17},{17,9},{25,1},{2,26},{10... | collective-permute-start | bytes 98312 | tf_op jit(solution)/shard_map/ppermute | solution.py:25
  5.1 5.0 %collective-permute-start.3 = (bf16[16,1024]{1,0:T(8,128)(2,1)}, bf16[16,1024]{1,0:T(8,128)(2,1)S(1)}, u32[]{:S(2)}, u32[]{:S(2)}) collective-permute-start(bf16[16,1024]{1,0:T(8,128)(2,1)} %own_ref.1), channel_id=1, source_target_pairs={{0,16},{8,24},{16,0},{24,8},{1,17},{9,25},{17,1},{25,9},{2,18},{10... | collective-permute-start | bytes 98312 | tf_op jit(solution)/shard_map/ppermute | solution.py:25
  5.1 6.5 %collective-permute-start.5 = (bf16[16,1024]{1,0:T(8,128)(2,1)}, bf16[16,1024]{1,0:T(8,128)(2,1)S(1)}, u32[]{:S(2)}, u32[]{:S(2)}) collective-permute-start(bf16[16,1024]{1,0:T(8,128)(2,1)} %own_ref.1), channel_id=1, source_target_pairs={{0,8},{8,0},{16,24},{24,16},{1,9},{9,1},{17,25},{25,17},{2,10},{10... | collective-permute-start | bytes 98312 | tf_op jit(solution)/shard_map/ppermute | solution.py:25
  7.3 8.9 %collective-permute-start.2 = (bf16[16,1024]{1,0:T(8,128)(2,1)S(1)}, bf16[16,1024]{1,0:T(8,128)(2,1)S(1)}, u32[]{:S(2)}, u32[]{:S(2)}) collective-permute-start(bf16[16,1024]{1,0:T(8,128)(2,1)S(1)} %collective-permute-done.1.rest_0_), channel_id=1, source_target_pairs={{0,1},{1,0},{2,3},{3,2},{4,5},{5,4},{6,7},{7,6},{8,9},{9,8},{10,11... | collective-permute-start | bytes 98312 | tf_op jit(solution)/shard_map/ppermute | solution.py:25
  10.1 6.2 %collective-permute-start.4 = (bf16[16,1024]{1,0:T(8,128)(2,1)S(1)}, bf16[16,1024]{1,0:T(8,128)(2,1)S(1)}, u32[]{:S(2)}, u32[]{:S(2)}) collective-permute-start(bf16[16,1024]{1,0:T(8,128)(2,1)S(1)} %collective-permute-done.3.rest_2_), channel_id=1, source_target_pairs={{0,1},{1,0},{2,3},{3,2},{4,5},{5,4},{6,7},{7,6},{8,9},{9,8},{10,11... | collective-permute-start | bytes 98312 | tf_op jit(solution)/shard_map/ppermute | solution.py:25
  11.6 4.7 %collective-permute-start.6 = (bf16[16,1024]{1,0:T(8,128)(2,1)S(1)}, bf16[16,1024]{1,0:T(8,128)(2,1)S(1)}, u32[]{:S(2)}, u32[]{:S(2)}) collective-permute-start(bf16[16,1024]{1,0:T(8,128)(2,1)S(1)} %collective-permute-done.5.rest_4_), channel_id=1, source_target_pairs={{0,1},{1,0},{2,3},{3,2},{4,5},{5,4},{6,7},{7,6},{8,9},{9,8},{10,11... | collective-permute-start | bytes 98312 | tf_op jit(solution)/shard_map/ppermute | solution.py:25
  12.1 5.7 %collective-permute-start.7 = (bf16[16,1024]{1,0:T(8,128)(2,1)}, bf16[16,1024]{1,0:T(8,128)(2,1)S(1)}, u32[]{:S(2)}, u32[]{:S(2)}) collective-permute-start(bf16[16,1024]{1,0:T(8,128)(2,1)} %own_ref.1), channel_id=1, source_target_pairs={{0,1},{1,0},{2,3},{3,2},{4,5},{5,4},{6,7},{7,6},{8,9},{9,8},{10,11... | collective-permute-start | bytes 98312 | tf_op jit(solution)/shard_map/ppermute | solution.py:25
  17.1 0.7 %copy-start = (bf16[4,2,144,128]{3,2,1,0:T(8,128)(2,1)}, bf16[4,2,144,128]{3,2,1,0:T(8,128)(2,1)S(1)}, u32[]{:S(2)}) copy-start(bf16[4,2,144,128]{3,2,1,0:T(8,128)(2,1)S(1)} %suffix_away.1) | copy-start | bytes 884740
  17.8 0.6 %copy-start.2 = (bf16[16,1024]{1,0:T(8,128)(2,1)}, bf16[16,1024]{1,0:T(8,128)(2,1)S(1)}, u32[]{:S(2)}) copy-start(bf16[16,1024]{1,0:T(8,128)(2,1)S(1)} %collective-permute-done.7.pair_ref) | copy-start | bytes 98308
  18.5 13.5 %all-to-all-start = ((bf16[8,144,128]{2,1,0:T(8,128)(2,1)}), bf16[8,144,128]{2,1,0:T(8,128)(2,1)S(1)}, u32[]{:S(2)}, u32[]{:S(2)}) async-start(bf16[8,144,128]{2,1,0:T(8,128)(2,1)} %bitcast.7), calls=%async_computation | async-start | bytes 589824 | tf_op jit(solution)/shard_map/all_to_all | solution.py:322
  22.4 0.8 %copy-start.1 = (bf16[16,1024]{1,0:T(8,128)(2,1)S(1)}, bf16[16,1024]{1,0:T(8,128)(2,1)}, u32[]{:S(2)}) copy-start(bf16[16,1024]{1,0:T(8,128)(2,1)} %own_ref.1) | copy-start | bytes 98308
  23.2 0.8 %copy-start.3 = (bf16[16,1024]{1,0:T(8,128)(2,1)S(1)}, bf16[16,1024]{1,0:T(8,128)(2,1)}, u32[]{:S(2)}) copy-start(bf16[16,1024]{1,0:T(8,128)(2,1)} %copy-done.2) | copy-start | bytes 98308
  28.0 4.0 %collective-permute-start.8 = (bf16[144,128]{1,0:T(8,128)(2,1)S(1)}, bf16[144,128]{1,0:T(8,128)(2,1)S(1)}, u32[]{:S(2)}, u32[]{:S(2)}) collective-permute-start(bf16[144,128]{1,0:T(8,128)(2,1)S(1)} %get-tuple-element.22), channel_id=1, source_target_pairs={{0,1},{1,0},{2,3},{3,2},{4,5},{5,4},{6,7},{7,6},{8,9},{9,8},{10,11... | collective-permute-start | bytes 110600 | tf_op jit(solution)/shard_map/ppermute | solution.py:25

commit v8 on v7

--- a/solution.py
+++ b/solution.py
@@ -97,7 +97,10 @@
     return lax.broadcasted_iota(jnp.int32, shape, axis)
 
 
-def prompt_part(valid, prompt_ref, vectors):
+def prompt_part(length, half, prompt_ref, vectors):
+    parity = lax.axis_index("pair")
+    whole = lax.div(length, 2 * half)
+    valid = whole * half + jnp.clip(length - whole * (2 * half) - parity * half, 0, half)
     parts = []
     for start in range(0, prompt_ref.shape[0], CHUNK):
         part = slice(start, start + CHUNK)
@@ -112,8 +115,8 @@
 
 
 def prepare_kernel(
-    capacity, length_ref, table_ref, parents_ref, near_ref, prompt_ref, far_ref,
-    keys_ref, values_ref, member_ref, held_ref, valid_ref, rows_ref, table, parents, near, sems,
+    capacity, table_ref, parents_ref, near_ref, prompt_ref, own_ref, far_ref,
+    keys_ref, values_ref, member_ref, held_ref, own, rows_ref, table, parents, near, sems,
 ):
     n_req = keys_ref.shape[0]
     slots, half, _ = near.shape
@@ -124,17 +127,17 @@
     small = [
         pltpu.make_async_copy(source, target, sems.at[i])
         for i, (source, target) in enumerate(
-            [(table_ref, table), (parents_ref, parents), (near_ref, near), (prompt_ref, held_ref)]
+            [
+                (table_ref, table),
+                (parents_ref, parents),
+                (near_ref, near),
+                (prompt_ref, held_ref),
+                (own_ref, own),
+            ]
         )
     ]
     for copy in small:
         copy.start()
-
-    length = length_ref[0]
-    whole = lax.div(length, 2 * half)
-    parity = lax.axis_index("pair")
-    valid = whole * half + jnp.clip(length - whole * (2 * half) - parity * half, 0, half)
-    valid_ref[...] = jnp.full(valid_ref.shape, valid, jnp.int32)
 
     small[0].wait()
     slot = iota((2 * slots, rows), 0)
@@ -181,6 +184,7 @@
             values.append(content[:, HD:])
         values_ref[d] = jnp.concatenate(values, axis=0).T
     small[3].wait()
+    small[4].wait()
 
 
 def all_vectors(own_ref, pair_ref):
@@ -223,7 +227,7 @@
 
 
 def away_kernel(keys_ref, values_ref, member_ref, *rest):
-    queries, out_ref = rest[:-1], rest[-1]
+    queries, out_ref = rest[:-2], rest[-1]
     requests = tuple(reversed(range(1, keys_ref.shape[0])))
     z, parity = lax.axis_index("z"), lax.axis_index("pair")
     parts = suffix_parts(requests, queries, keys_ref, values_ref, member_ref)
@@ -235,11 +239,11 @@
 
 
 def home_kernel(
-    keys_ref, values_ref, member_ref, own_ref, pair_ref, prompt_ref, valid_ref,
+    half, length_ref, keys_ref, values_ref, member_ref, own_ref, pair_ref, prompt_ref, after_ref,
     summed_ref, stats_ref, out_ref,
 ):
     (suffix,) = suffix_parts((0,), (own_ref, pair_ref), keys_ref, values_ref, member_ref)
-    prompt = prompt_part(valid_ref[0:1, :], prompt_ref, all_vectors(own_ref, pair_ref))
+    prompt = prompt_part(length_ref[0], half, prompt_ref, all_vectors(own_ref, pair_ref))
     part = merged([prompt, suffix])
     top, total, summed_ref[...] = half_of(part, 0)
     stats_ref[...] = jnp.concatenate([top, total, jnp.zeros((6, VECS), jnp.float32)], axis=0)
@@ -280,62 +284,62 @@
         sent += [piece, swapped(piece, "pair")]
     other = swapped(queries, "pair")
 
-    keys, values, member, prompt, valid = pl.pallas_call(
+    keys, values, member, prompt, own = pl.pallas_call(
         functools.partial(prepare_kernel, capacity),
         out_shape=(
             jax.ShapeDtypeStruct((n_req, 2 * capacity * half, HD), jnp.bfloat16),
             jax.ShapeDtypeStruct((n_req, HD, 2 * capacity * half), jnp.bfloat16),
             jax.ShapeDtypeStruct((n_req, 2 * capacity, 2 * VECS), jnp.float32),
             jax.ShapeDtypeStruct((tokens, width), jnp.bfloat16),
-            jax.ShapeDtypeStruct((8, 2 * VECS), jnp.int32),
+            jax.ShapeDtypeStruct(queries.shape, jnp.bfloat16),
         ),
-        in_specs=[pl.BlockSpec(memory_space=pltpu.SMEM)] + [hbm] * 4 + [vmem],
+        in_specs=[hbm] * 5 + [vmem],
         out_specs=(vmem,) * 5,
         scratch_shapes=[
             pltpu.VMEM((2 * slots + 8, 2 * VECS), jnp.float32),
             pltpu.VMEM((SUF, rows), jnp.int32),
             pltpu.VMEM((1, rows), jnp.int32),
             pltpu.VMEM((slots, half, width), jnp.bfloat16),
-            pltpu.SemaphoreType.DMA((4,)),
+            pltpu.SemaphoreType.DMA((5,)),
         ],
         compiler_params=params,
         name="prepare",
     )(
-        lengths,
         in_hbm(block_table.T),
         in_hbm(parents.reshape(1, rows)),
         in_hbm(near),
         in_hbm(prompt_cache.reshape(tokens, width)),
+        in_hbm(queries),
         far,
     )
 
     units = pl.pallas_call(
         away_kernel,
         out_shape=jax.ShapeDtypeStruct((n_req, 2, UNIT_ROWS, VECS), jnp.bfloat16),
-        in_specs=[vmem] * (3 + len(sent)),
+        in_specs=[vmem] * (4 + len(sent)),
         out_specs=vmem,
         compiler_params=params,
         name="suffix_away",
-    )(keys, values, member, *sent)
-    units, other = lax.optimization_barrier((units, other))
+    )(keys, values, member, *sent, other)
+    after = units
     units = units.reshape(2 * n_req, UNIT_ROWS, VECS)
     units = lax.all_to_all(units, ("z", "pair"), split_axis=0, concat_axis=0, tiled=True)
 
     summed, stats, given = pl.pallas_call(
-        home_kernel,
+        functools.partial(home_kernel, half),
         out_shape=(
             jax.ShapeDtypeStruct((HD, VECS), jnp.float32),
             jax.ShapeDtypeStruct((8, VECS), jnp.float32),
             jax.ShapeDtypeStruct((UNIT_ROWS, VECS), jnp.bfloat16),
         ),
-        in_specs=[vmem] * 7,
+        in_specs=[pl.BlockSpec(memory_space=pltpu.SMEM)] + [vmem] * 7,
         out_specs=(vmem,) * 3,
         compiler_params=params,
         cost_estimate=pl.CostEstimate(
             flops=8 * tokens * VECS * HD, bytes_accessed=2 * tokens * width, transcendentals=0
         ),
         name="home_part",
-    )(keys, values, member, queries, other, prompt, valid)
+    )(lengths, keys, values, member, own, other, prompt, after)
     last = swapped(given, "pair")
 
     return pl.pallas_call(

time: 33.2 us -> 33 us (level)
  Pallas kernels: 7.61 us -> 9.16 us
  local copies, waits for them, and re-layouts: 2.83 us -> 1.46 us
    unnamed x8 -> x4, local copies, waits for them, and re-layouts: 2.83 us -> 1.46 us
    pallas_call x1, Pallas kernels: 4.01 us -> 4.84 us  [on_device(): pl.pallas_call(functools.partial(home_kernel, half), out_shape=(jax.Shape...]
    pallas_call x1, Pallas kernels: 0.83 us -> 1.54 us  [on_device(): pl.pallas_call(away_kernel, out_shape=jax.ShapeDtypeStruct((n_req, 2, UNI...]
where the time goes in v8:
time: 33 us; the launch traced here: 32.7 us
  starting transfers between devices  16.9 us (51%)
  Pallas kernels  9.16 us (28%)
  waiting for transfers between devices  4.52 us (14%)
  local copies, waits for them, and re-layouts  1.46 us (4%)
  between operations  0.71 us (2%)
    ppermute x9, starting transfers between devices, swapped(): lax.ppermute(value, axis, [(i, i ^ mask) for i in range(lax.axis_size(axi...  12.9 us
    pallas_call x1, Pallas kernels, on_device(): pl.pallas_call(functools.partial(home_kernel, half), out_shape=(jax.Shape...  4.84 us
    ppermute x9, waiting for transfers between devices, swapped(): lax.ppermute(value, axis, [(i, i ^ mask) for i in range(lax.axis_size(axi...  4.51 us
    all_to_all x1, starting transfers between devices, on_device(): lax.all_to_all(units, ('z', 'pair'), split_axis=0, concat_axis=0, tiled=T...  3.98 us
    pallas_call x1, Pallas kernels, on_device(): pl.pallas_call(functools.partial(prepare_kernel, capacity), out_shape=(ja...  1.99 us
    pallas_call x1, Pallas kernels, on_device(): pl.pallas_call(away_kernel, out_shape=jax.ShapeDtypeStruct((n_req, 2, UNI...  1.54 us
    unnamed x4, local copies, waits for them, and re-layouts  1.46 us
    pallas_call x1, Pallas kernels, on_device(): pl.pallas_call(final_kernel, out_shape=jax.ShapeDtypeStruct((BEAMS, HEADS...  0.79 us
  transfers between devices with their start and end apart: 10, of which 3 were waited for; matrix products, arithmetic and copies ran while one was open for 0% of the time, Pallas kernels for 21%

profile of v8, /device:TPU:0, one launch (start us, length us, event | category | flops | bytes accessed | tf_op | source)
XLA Modules:
  0.0 32.7 jit_solution(11927038833333165990)
XLA Ops:
  0.0 0.5 %collective-permute-start = (bf16[32,64,256]{2,1,0:T(8,128)(2,1)}, bf16[32,64,256]{2,1,0:T(8,128)(2,1)S(1)}, u32[]{:S(2)}, u32[]{:S(2)}) collective-permute-start(bf16[32,64,256]{2,1,0:T(8,128)(2,1)} %bitcast.8), channel_id=1, source_target_pairs={{0,4},{4,0},{1,5},{5,1},{2,6},{6,2},{3,7},{7,3},{8,12},{12,8},{9,1... | collective-permute-start | bytes 3145736 | tf_op jit(solution)/shard_map/ppermute | solution.py:25
  0.5 4.6 %collective-permute-start.1 = (bf16[16,1024]{1,0:T(8,128)(2,1)}, bf16[16,1024]{1,0:T(8,128)(2,1)S(1)}, u32[]{:S(2)}, u32[]{:S(2)}) collective-permute-start(bf16[16,1024]{1,0:T(8,128)(2,1)} %own_ref.1), channel_id=1, source_target_pairs={{0,24},{8,16},{16,8},{24,0},{1,25},{9,17},{17,9},{25,1},{2,26},{10... | collective-permute-start | bytes 98312 | tf_op jit(solution)/shard_map/ppermute | solution.py:25
  5.1 0.0 collective-permute-start.3
  5.1 0.6 %collective-permute-start.5 = (bf16[16,1024]{1,0:T(8,128)(2,1)}, bf16[16,1024]{1,0:T(8,128)(2,1)S(1)}, u32[]{:S(2)}, u32[]{:S(2)}) collective-permute-start(bf16[16,1024]{1,0:T(8,128)(2,1)} %own_ref.1), channel_id=1, source_target_pairs={{0,8},{8,0},{16,24},{24,16},{1,9},{9,1},{17,25},{25,17},{2,10},{10... | collective-permute-start | bytes 98312 | tf_op jit(solution)/shard_map/ppermute | solution.py:25
  5.7 1.6 %collective-permute-start.7 = (bf16[16,1024]{1,0:T(8,128)(2,1)}, bf16[16,1024]{1,0:T(8,128)(2,1)S(1)}, u32[]{:S(2)}, u32[]{:S(2)}) collective-permute-start(bf16[16,1024]{1,0:T(8,128)(2,1)} %own_ref.1), channel_id=1, source_target_pairs={{0,1},{1,0},{2,3},{3,2},{4,5},{5,4},{6,7},{7,6},{8,9},{9,8},{10,11... | collective-permute-start | bytes 98312 | tf_op jit(solution)/shard_map/ppermute | solution.py:25
  7.3 1.5 %collective-permute-start.2 = (bf16[16,1024]{1,0:T(8,128)(2,1)S(1)}, bf16[16,1024]{1,0:T(8,128)(2,1)S(1)}, u32[]{:S(2)}, u32[]{:S(2)}) collective-permute-start(bf16[16,1024]{1,0:T(8,128)(2,1)S(1)} %collective-permute-done.1.rest_0_), channel_id=1, source_target_pairs={{0,1},{1,0},{2,3},{3,2},{4,5},{5,4},{6,7},{7,6},{8,9},{9,8},{10,11... | collective-permute-start | bytes 98312 | tf_op jit(solution)/shard_map/ppermute | solution.py:25
  8.9 1.2 %collective-permute-done.3.rest_2_ = bf16[16,1024]{1,0:T(8,128)(2,1)S(1)} collective-permute-done((bf16[16,1024]{1,0:T(8,128)(2,1)}, bf16[16,1024]{1,0:T(8,128)(2,1)S(1)}, u32[]{:S(2)}, u32[]{:S(2)}) %collective-permute-start.3) | collective-permute-done | bytes 32800 | tf_op jit(solution)/shard_map/ppermute | solution.py:25
  10.1 1.5 %collective-permute-start.4 = (bf16[16,1024]{1,0:T(8,128)(2,1)S(1)}, bf16[16,1024]{1,0:T(8,128)(2,1)S(1)}, u32[]{:S(2)}, u32[]{:S(2)}) collective-permute-start(bf16[16,1024]{1,0:T(8,128)(2,1)S(1)} %collective-permute-done.3.rest_2_), channel_id=1, source_target_pairs={{0,1},{1,0},{2,3},{3,2},{4,5},{5,4},{6,7},{7,6},{8,9},{9,8},{10,11... | collective-permute-start | bytes 98312 | tf_op jit(solution)/shard_map/ppermute | solution.py:25
  11.6 0.0 collective-permute-done.5.rest_4_
  11.6 0.5 %collective-permute-start.6 = (bf16[16,1024]{1,0:T(8,128)(2,1)S(1)}, bf16[16,1024]{1,0:T(8,128)(2,1)S(1)}, u32[]{:S(2)}, u32[]{:S(2)}) collective-permute-start(bf16[16,1024]{1,0:T(8,128)(2,1)S(1)} %collective-permute-done.5.rest_4_), channel_id=1, source_target_pairs={{0,1},{1,0},{2,3},{3,2},{4,5},{5,4},{6,7},{7,6},{8,9},{9,8},{10,11... | collective-permute-start | bytes 98312 | tf_op jit(solution)/shard_map/ppermute | solution.py:25
  12.1 2.0 %prepare.1 = (bf16[4,512,128]{2,1,0:T(8,128)(2,1)S(1)}, bf16[4,128,512]{2,1,0:T(8,128)(2,1)S(1)}, f32[4,8,256]{2,1,0:T(8,128)S(1)}, bf16[4096,256]{1,0:T(8,128)(2,1)S(1)}, bf16[16,1024]{1,0:T(8,128)(2,1)S(1)}) custom-call(s32[4,128]{1,0:T(4,128)} %bitcast.10, s32[1,128]{1,0:T(1,128)} %bitcast.11, bf16[32,64,256]{2,1,0:T(8,128)(2,1)} %bitcast.9, ...), custom_call_target="tpu_custom_call" | custom-call | tf_op jit(solution)/shard_map/prepare/pallas_call | solution.py:287
  14.1 0.0 collective-permute-done.7.rest_6_.pair_ref
  14.1 0.0 collective-permute-done.2.rest_1_
  14.1 1.3 %collective-permute-done.6.rest_5_ = bf16[16,1024]{1,0:T(8,128)(2,1)S(1)} collective-permute-done((bf16[16,1024]{1,0:T(8,128)(2,1)S(1)}, bf16[16,1024]{1,0:T(8,128)(2,1)S(1)}, u32[]{:S(2)}, u32[]{:S(2)}) %collective-permute-start.6) | collective-permute-done | bytes 32800 | tf_op jit(solution)/shard_map/ppermute | solution.py:25
  15.5 1.5 %suffix_away.1.after_ref = bf16[4,2,144,128]{3,2,1,0:T(8,128)(2,1)} custom-call(bf16[4,512,128]{2,1,0:T(8,128)(2,1)S(1)} %get-tuple-element.13.keys_ref, bf16[4,128,512]{2,1,0:T(8,128)(2,1)S(1)} %get-tuple-element.14.values_ref, f32[4,8,256]{2,1,0:T(8,128)S(1)} %get-tuple-element.15.member_ref, bf16[16,1024]{1,0:T(8,128)(2,1)S(1)} %collective-permute-done.1.rest_0_, ...), custom_call_target="tpu_custom_call" | custom-call | tf_op jit(solution)/shard_map/suffix_away/pallas_call | solution.py:316
  17.0 4.0 %all-to-all-start = ((bf16[8,144,128]{2,1,0:T(8,128)(2,1)}), bf16[8,144,128]{2,1,0:T(8,128)(2,1)S(1)}, u32[]{:S(2)}, u32[]{:S(2)}) async-start(bf16[8,144,128]{2,1,0:T(8,128)(2,1)} %bitcast.4), calls=%async_computation | async-start | bytes 589824 | tf_op jit(solution)/shard_map/all_to_all | solution.py:326
  21.7 4.8 %home_part.1 = (f32[128,128]{1,0:T(8,128)S(1)}, f32[8,128]{1,0:T(8,128)S(1)}, bf16[144,128]{1,0:T(8,128)(2,1)S(1)}) custom-call(s32[1]{0:T(128)S(6)} %copy.7.length_ref, bf16[4,512,128]{2,1,0:T(8,128)(2,1)S(1)} %get-tuple-element.13.keys_ref, bf16[4,128,512]{2,1,0:T(8,128)(2,1)S(1)} %get-tuple-element.14.values_ref, ...), custom_call_target="tpu_custom_call" | custom-call | flops 536870912 | bytes 2097152 | tf_op jit(solution)/shard_map/home_part/pallas_call | solution.py:328
  26.5 0.0 copy-start
  26.5 0.6 %copy-done = f32[128,128]{1,0:T(8,128)} copy-done((f32[128,128]{1,0:T(8,128)}, f32[128,128]{1,0:T(8,128)S(1)}, u32[]{:S(2)}) %copy-start) | copy-done | bytes 65560
  27.1 2.0 %collective-permute-start.8 = (bf16[144,128]{1,0:T(8,128)(2,1)S(1)}, bf16[144,128]{1,0:T(8,128)(2,1)S(1)}, u32[]{:S(2)}, u32[]{:S(2)}) collective-permute-start(bf16[144,128]{1,0:T(8,128)(2,1)S(1)} %get-tuple-element.18), channel_id=1, source_target_pairs={{0,1},{1,0},{2,3},{3,2},{4,5},{5,4},{6,7},{7,6},{8,9},{9,8},{10,11... | collective-permute-start | bytes 110600 | tf_op jit(solution)/shard_map/ppermute | solution.py:25
  29.2 1.9 %collective-permute-done.8.last_ref = bf16[144,128]{1,0:T(8,128)(2,1)S(1)} collective-permute-done((bf16[144,128]{1,0:T(8,128)(2,1)S(1)}, bf16[144,128]{1,0:T(8,128)(2,1)S(1)}, u32[]{:S(2)}, u32[]{:S(2)}) %collective-permute-start.8) | collective-permute-done | bytes 36896 | tf_op jit(solution)/shard_map/ppermute | solution.py:25
  31.1 0.0 all-to-all-done
  31.1 0.8 %copy-done.1 = f32[128,128]{1,0:T(8,128)S(1)} copy-done((f32[128,128]{1,0:T(8,128)S(1)}, f32[128,128]{1,0:T(8,128)}, u32[]{:S(2)}) %copy-start.1) | copy-done | bytes 65560
  31.9 0.8 %combine.1 = f32[16,1024]{1,0:T(8,128)} custom-call(bf16[4,2,144,128]{3,2,1,0:T(8,128)(2,1)S(1)} %bitcast.6, bf16[144,128]{1,0:T(8,128)(2,1)S(1)} %collective-permute-done.8.last_ref, f32[128,128]{1,0:T(8,128)S(1)} %copy-done.1, f32[8,128]{1,0:T(8,128)S(1)} %get-tuple-element.20.stats_ref), custom_call_target="tpu_custom_call" | custom-call | tf_op jit(solution)/shard_map/combine/pallas_call | solution.py:345
  (4 shorter events, 0.0 us)
Async XLA Ops:
  0.0 12.1 %collective-permute-start = (bf16[32,64,256]{2,1,0:T(8,128)(2,1)}, bf16[32,64,256]{2,1,0:T(8,128)(2,1)S(1)}, u32[]{:S(2)}, u32[]{:S(2)}) collective-permute-start(bf16[32,64,256]{2,1,0:T(8,128)(2,1)} %bitcast.8), channel_id=1, source_target_pairs={{0,4},{4,0},{1,5},{5,1},{2,6},{6,2},{3,7},{7,3},{8,12},{12,8},{9,1... | collective-permute-start | bytes 3145736 | tf_op jit(solution)/shard_map/ppermute | solution.py:25
  0.5 6.9 %collective-permute-start.1 = (bf16[16,1024]{1,0:T(8,128)(2,1)}, bf16[16,1024]{1,0:T(8,128)(2,1)S(1)}, u32[]{:S(2)}, u32[]{:S(2)}) collective-permute-start(bf16[16,1024]{1,0:T(8,128)(2,1)} %own_ref.1), channel_id=1, source_target_pairs={{0,24},{8,16},{16,8},{24,0},{1,25},{9,17},{17,9},{25,1},{2,26},{10... | collective-permute-start | bytes 98312 | tf_op jit(solution)/shard_map/ppermute | solution.py:25
  5.1 5.0 %collective-permute-start.3 = (bf16[16,1024]{1,0:T(8,128)(2,1)}, bf16[16,1024]{1,0:T(8,128)(2,1)S(1)}, u32[]{:S(2)}, u32[]{:S(2)}) collective-permute-start(bf16[16,1024]{1,0:T(8,128)(2,1)} %own_ref.1), channel_id=1, source_target_pairs={{0,16},{8,24},{16,0},{24,8},{1,17},{9,25},{17,1},{25,9},{2,18},{10... | collective-permute-start | bytes 98312 | tf_op jit(solution)/shard_map/ppermute | solution.py:25
  5.1 6.5 %collective-permute-start.5 = (bf16[16,1024]{1,0:T(8,128)(2,1)}, bf16[16,1024]{1,0:T(8,128)(2,1)S(1)}, u32[]{:S(2)}, u32[]{:S(2)}) collective-permute-start(bf16[16,1024]{1,0:T(8,128)(2,1)} %own_ref.1), channel_id=1, source_target_pairs={{0,8},{8,0},{16,24},{24,16},{1,9},{9,1},{17,25},{25,17},{2,10},{10... | collective-permute-start | bytes 98312 | tf_op jit(solution)/shard_map/ppermute | solution.py:25
  5.7 8.4 %collective-permute-start.7 = (bf16[16,1024]{1,0:T(8,128)(2,1)}, bf16[16,1024]{1,0:T(8,128)(2,1)S(1)}, u32[]{:S(2)}, u32[]{:S(2)}) collective-permute-start(bf16[16,1024]{1,0:T(8,128)(2,1)} %own_ref.1), channel_id=1, source_target_pairs={{0,1},{1,0},{2,3},{3,2},{4,5},{5,4},{6,7},{7,6},{8,9},{9,8},{10,11... | collective-permute-start | bytes 98312 | tf_op jit(solution)/shard_map/ppermute | solution.py:25
  7.3 6.8 %collective-permute-start.2 = (bf16[16,1024]{1,0:T(8,128)(2,1)S(1)}, bf16[16,1024]{1,0:T(8,128)(2,1)S(1)}, u32[]{:S(2)}, u32[]{:S(2)}) collective-permute-start(bf16[16,1024]{1,0:T(8,128)(2,1)S(1)} %collective-permute-done.1.rest_0_), channel_id=1, source_target_pairs={{0,1},{1,0},{2,3},{3,2},{4,5},{5,4},{6,7},{7,6},{8,9},{9,8},{10,11... | collective-permute-start | bytes 98312 | tf_op jit(solution)/shard_map/ppermute | solution.py:25
  10.1 4.1 %collective-permute-start.4 = (bf16[16,1024]{1,0:T(8,128)(2,1)S(1)}, bf16[16,1024]{1,0:T(8,128)(2,1)S(1)}, u32[]{:S(2)}, u32[]{:S(2)}) collective-permute-start(bf16[16,1024]{1,0:T(8,128)(2,1)S(1)} %collective-permute-done.3.rest_2_), channel_id=1, source_target_pairs={{0,1},{1,0},{2,3},{3,2},{4,5},{5,4},{6,7},{7,6},{8,9},{9,8},{10,11... | collective-permute-start | bytes 98312 | tf_op jit(solution)/shard_map/ppermute | solution.py:25
  11.6 3.9 %collective-permute-start.6 = (bf16[16,1024]{1,0:T(8,128)(2,1)S(1)}, bf16[16,1024]{1,0:T(8,128)(2,1)S(1)}, u32[]{:S(2)}, u32[]{:S(2)}) collective-permute-start(bf16[16,1024]{1,0:T(8,128)(2,1)S(1)} %collective-permute-done.5.rest_4_), channel_id=1, source_target_pairs={{0,1},{1,0},{2,3},{3,2},{4,5},{5,4},{6,7},{7,6},{8,9},{9,8},{10,11... | collective-permute-start | bytes 98312 | tf_op jit(solution)/shard_map/ppermute | solution.py:25
  17.0 14.1 %all-to-all-start = ((bf16[8,144,128]{2,1,0:T(8,128)(2,1)}), bf16[8,144,128]{2,1,0:T(8,128)(2,1)S(1)}, u32[]{:S(2)}, u32[]{:S(2)}) async-start(bf16[8,144,128]{2,1,0:T(8,128)(2,1)} %bitcast.4), calls=%async_computation | async-start | bytes 589824 | tf_op jit(solution)/shard_map/all_to_all | solution.py:326
  26.5 0.6 %copy-start = (f32[128,128]{1,0:T(8,128)}, f32[128,128]{1,0:T(8,128)S(1)}, u32[]{:S(2)}) copy-start(f32[128,128]{1,0:T(8,128)S(1)} %get-tuple-element.19.summed_ref) | copy-start | bytes 196612
  27.1 4.0 %collective-permute-start.8 = (bf16[144,128]{1,0:T(8,128)(2,1)S(1)}, bf16[144,128]{1,0:T(8,128)(2,1)S(1)}, u32[]{:S(2)}, u32[]{:S(2)}) collective-permute-start(bf16[144,128]{1,0:T(8,128)(2,1)S(1)} %get-tuple-element.18), channel_id=1, source_target_pairs={{0,1},{1,0},{2,3},{3,2},{4,5},{5,4},{6,7},{7,6},{8,9},{9,8},{10,11... | collective-permute-start | bytes 110600 | tf_op jit(solution)/shard_map/ppermute | solution.py:25
  31.1 0.8 %copy-start.1 = (f32[128,128]{1,0:T(8,128)S(1)}, f32[128,128]{1,0:T(8,128)}, u32[]{:S(2)}) copy-start(f32[128,128]{1,0:T(8,128)} %copy-done) | copy-start | bytes 196612

commit v9 on v8

--- a/solution.py
+++ b/solution.py
@@ -22,7 +22,8 @@
 
 
 def swapped(value, axis, mask=1):
-    return lax.ppermute(value, axis, [(i, i ^ mask) for i in range(lax.axis_size(axis))])
+    size = lax.axis_size(axis)
+    return lax.ppermute(value, axis, [(i, i ^ mask) for i in range(size)])
 
 
 def stacked_heads(q):
@@ -227,7 +228,8 @@
 
 
 def away_kernel(keys_ref, values_ref, member_ref, *rest):
-    queries, out_ref = rest[:-2], rest[-1]
+    queries, out_ref, after_ref = rest[:-3], rest[-2], rest[-1]
+    after_ref[...] = jnp.zeros(after_ref.shape, jnp.float32)
     requests = tuple(reversed(range(1, keys_ref.shape[0])))
     z, parity = lax.axis_index("z"), lax.axis_index("pair")
     parts = suffix_parts(requests, queries, keys_ref, values_ref, member_ref)
@@ -278,20 +280,19 @@
     hbm = pl.BlockSpec(memory_space=pltpu.HBM)
     near = pool.reshape(slots, half, width)
     far = swapped(near, "core")
-    arrived = [swapped(queries, "z", d) for d in reversed(range(1, n_req))]
     sent = []
-    for piece in arrived:
-        sent += [piece, swapped(piece, "pair")]
+    for d in reversed(range(1, n_req)):
+        sent += [swapped(queries, "z", d), swapped(queries, ("z", "pair"), 2 * d + 1)]
     other = swapped(queries, "pair")
 
     keys, values, member, prompt, own = pl.pallas_call(
         functools.partial(prepare_kernel, capacity),
         out_shape=(
-            jax.ShapeDtypeStruct((n_req, 2 * capacity * half, HD), jnp.bfloat16),
-            jax.ShapeDtypeStruct((n_req, HD, 2 * capacity * half), jnp.bfloat16),
-            jax.ShapeDtypeStruct((n_req, 2 * capacity, 2 * VECS), jnp.float32),
-            jax.ShapeDtypeStruct((tokens, width), jnp.bfloat16),
-            jax.ShapeDtypeStruct(queries.shape, jnp.bfloat16),
+            pltpu.VMEM((n_req, 2 * capacity * half, HD), jnp.bfloat16),
+            pltpu.VMEM((n_req, HD, 2 * capacity * half), jnp.bfloat16),
+            pltpu.VMEM((n_req, 2 * capacity, 2 * VECS), jnp.float32),
+            pltpu.VMEM((tokens, width), jnp.bfloat16),
+            pltpu.VMEM(queries.shape, jnp.bfloat16),
         ),
         in_specs=[hbm] * 5 + [vmem],
         out_specs=(vmem,) * 5,
@@ -313,24 +314,26 @@
         far,
     )
 
-    units = pl.pallas_call(
+    units, after = pl.pallas_call(
         away_kernel,
-        out_shape=jax.ShapeDtypeStruct((n_req, 2, UNIT_ROWS, VECS), jnp.bfloat16),
+        out_shape=(
+            pltpu.VMEM((n_req, 2, UNIT_ROWS, VECS), jnp.bfloat16),
+            pltpu.VMEM((8, VECS), jnp.float32),
+        ),
         in_specs=[vmem] * (4 + len(sent)),
-        out_specs=vmem,
+        out_specs=(vmem,) * 2,
         compiler_params=params,
         name="suffix_away",
     )(keys, values, member, *sent, other)
-    after = units
     units = units.reshape(2 * n_req, UNIT_ROWS, VECS)
     units = lax.all_to_all(units, ("z", "pair"), split_axis=0, concat_axis=0, tiled=True)
 
     summed, stats, given = pl.pallas_call(
         functools.partial(home_kernel, half),
         out_shape=(
-            jax.ShapeDtypeStruct((HD, VECS), jnp.float32),
-            jax.ShapeDtypeStruct((8, VECS), jnp.float32),
-            jax.ShapeDtypeStruct((UNIT_ROWS, VECS), jnp.bfloat16),
+            pltpu.VMEM((HD, VECS), jnp.float32),
+            pltpu.VMEM((8, VECS), jnp.float32),
+            pltpu.VMEM((UNIT_ROWS, VECS), jnp.bfloat16),
         ),
         in_specs=[pl.BlockSpec(memory_space=pltpu.SMEM)] + [vmem] * 7,
         out_specs=(vmem,) * 3,

time: 33 us -> 33.7 us (1.021)
  starting transfers between devices: 16.9 us -> 18.6 us
  Pallas kernels: 9.16 us -> 7.48 us
  local copies, waits for them, and re-layouts: 1.46 us -> 2.17 us
    pallas_call x3, Pallas kernels: 8.37 us -> 6.69 us  [the longest x1 3.88 us: on_device(): pl.pallas_call(functools.partial(home_kernel, half), out_shape=(pltpu.VME...]
    ppermute x9, starting transfers between devices: 12.9 us -> 14.4 us  [swapped(): return lax.ppermute(value, axis, [(i, i ^ mask) for i in range(size)])]
    unnamed x4 -> x6, local copies, waits for them, and re-layouts: 1.46 us -> 2.17 us
  transfers between devices with their start and end apart: 10 -> 10, of which waited for: 3 -> 3; matrix products, arithmetic and copies ran while one was open for 0% -> 0% of each run, Pallas kernels for 21% -> 18%
where the time goes in v9:
time: 33.7 us; the launch traced here: 33.4 us
  starting transfers between devices  18.6 us (55%)
  Pallas kernels  7.48 us (22%)
  waiting for transfers between devices  4.39 us (13%)
  local copies, waits for them, and re-layouts  2.17 us (6%)
  between operations  0.73 us (2%)
    ppermute x9, starting transfers between devices, swapped(): return lax.ppermute(value, axis, [(i, i ^ mask) for i in range(size)])  14.4 us
    ppermute x9, waiting for transfers between devices, swapped(): return lax.ppermute(value, axis, [(i, i ^ mask) for i in range(size)])  4.39 us
    all_to_all x1, starting transfers between devices, on_device(): lax.all_to_all(units, ('z', 'pair'), split_axis=0, concat_axis=0, tiled=T...  4.2 us
    pallas_call x1, Pallas kernels, on_device(): pl.pallas_call(functools.partial(home_kernel, half), out_shape=(pltpu.VME...  3.88 us
    unnamed x6, local copies, waits for them, and re-layouts  2.17 us
    pallas_call x1, Pallas kernels, on_device(): pl.pallas_call(functools.partial(prepare_kernel, capacity), out_shape=(pl...  1.99 us
    pallas_call x1, Pallas kernels, on_device(): pl.pallas_call(away_kernel, out_shape=(pltpu.VMEM((n_req, 2, UNIT_ROWS, V...  0.82 us
    pallas_call x1, Pallas kernels, on_device(): pl.pallas_call(final_kernel, out_shape=jax.ShapeDtypeStruct((BEAMS, HEADS...  0.79 us
  transfers between devices with their start and end apart: 10, of which 3 were waited for; matrix products, arithmetic and copies ran while one was open for 0% of the time, Pallas kernels for 18%

profile of v9, /device:TPU:0, one launch (start us, length us, event | category | flops | bytes accessed | tf_op | source)
XLA Modules:
  0.0 33.4 jit_solution(14330815941826098514)
XLA Ops:
  0.0 0.5 %collective-permute-start = (bf16[32,64,256]{2,1,0:T(8,128)(2,1)}, bf16[32,64,256]{2,1,0:T(8,128)(2,1)S(1)}, u32[]{:S(2)}, u32[]{:S(2)}) collective-permute-start(bf16[32,64,256]{2,1,0:T(8,128)(2,1)} %bitcast.9), channel_id=1, source_target_pairs={{0,4},{4,0},{1,5},{5,1},{2,6},{6,2},{3,7},{7,3},{8,12},{12,8},{9,1... | collective-permute-start | bytes 3145736 | tf_op jit(solution)/shard_map/ppermute | solution.py:26
  0.5 2.5 %collective-permute-start.7 = (bf16[16,1024]{1,0:T(8,128)(2,1)}, bf16[16,1024]{1,0:T(8,128)(2,1)S(1)}, u32[]{:S(2)}, u32[]{:S(2)}) collective-permute-start(bf16[16,1024]{1,0:T(8,128)(2,1)} %own_ref.1), channel_id=1, source_target_pairs={{0,1},{1,0},{2,3},{3,2},{4,5},{5,4},{6,7},{7,6},{8,9},{9,8},{10,11... | collective-permute-start | bytes 98312 | tf_op jit(solution)/shard_map/ppermute | solution.py:26
  2.9 3.6 %collective-permute-start.1 = (bf16[16,1024]{1,0:T(8,128)(2,1)}, bf16[16,1024]{1,0:T(8,128)(2,1)S(1)}, u32[]{:S(2)}, u32[]{:S(2)}) collective-permute-start(bf16[16,1024]{1,0:T(8,128)(2,1)} %own_ref.1), channel_id=1, source_target_pairs={{0,24},{8,16},{16,8},{24,0},{1,25},{9,17},{17,9},{25,1},{2,26},{10... | collective-permute-start | bytes 98312 | tf_op jit(solution)/shard_map/ppermute | solution.py:26
  6.5 0.0 collective-permute-start.2
  6.5 1.0 %collective-permute-start.3 = (bf16[16,1024]{1,0:T(8,128)(2,1)}, bf16[16,1024]{1,0:T(8,128)(2,1)S(1)}, u32[]{:S(2)}, u32[]{:S(2)}) collective-permute-start(bf16[16,1024]{1,0:T(8,128)(2,1)} %own_ref.1), channel_id=1, source_target_pairs={{0,16},{8,24},{16,0},{24,8},{1,17},{9,25},{17,1},{25,9},{2,18},{10... | collective-permute-start | bytes 98312 | tf_op jit(solution)/shard_map/ppermute | solution.py:26
  7.5 0.0 collective-permute-done.7.rest_6_.pair_ref
  7.5 3.1 %collective-permute-start.4 = (bf16[16,1024]{1,0:T(8,128)(2,1)}, bf16[16,1024]{1,0:T(8,128)(2,1)S(1)}, u32[]{:S(2)}, u32[]{:S(2)}) collective-permute-start(bf16[16,1024]{1,0:T(8,128)(2,1)} %own_ref.1), channel_id=1, source_target_pairs={{0,17},{1,16},{8,25},{9,24},{16,1},{17,0},{24,9},{25,8},{2,19},{3,... | collective-permute-start | bytes 98312 | tf_op jit(solution)/shard_map/ppermute | solution.py:26
  10.6 1.2 %collective-permute-start.5 = (bf16[16,1024]{1,0:T(8,128)(2,1)}, bf16[16,1024]{1,0:T(8,128)(2,1)S(1)}, u32[]{:S(2)}, u32[]{:S(2)}) collective-permute-start(bf16[16,1024]{1,0:T(8,128)(2,1)} %own_ref.1), channel_id=1, source_target_pairs={{0,8},{8,0},{16,24},{24,16},{1,9},{9,1},{17,25},{25,17},{2,10},{10... | collective-permute-start | bytes 98312 | tf_op jit(solution)/shard_map/ppermute | solution.py:26
  11.8 0.0 collective-permute-done.far_ref
  11.8 0.6 %collective-permute-start.6 = (bf16[16,1024]{1,0:T(8,128)(2,1)}, bf16[16,1024]{1,0:T(8,128)(2,1)S(1)}, u32[]{:S(2)}, u32[]{:S(2)}) collective-permute-start(bf16[16,1024]{1,0:T(8,128)(2,1)} %own_ref.1), channel_id=1, source_target_pairs={{0,9},{1,8},{8,1},{9,0},{16,25},{17,24},{24,17},{25,16},{2,11},{3,... | collective-permute-start | bytes 98312 | tf_op jit(solution)/shard_map/ppermute | solution.py:26
  12.4 2.0 %prepare.1 = (bf16[4,512,128]{2,1,0:T(8,128)(2,1)S(1)}, bf16[4,128,512]{2,1,0:T(8,128)(2,1)S(1)}, f32[4,8,256]{2,1,0:T(8,128)S(1)}, bf16[4096,256]{1,0:T(8,128)(2,1)S(1)}, bf16[16,1024]{1,0:T(8,128)(2,1)S(1)}) custom-call(s32[4,128]{1,0:T(4,128)} %bitcast.11, s32[1,128]{1,0:T(1,128)} %bitcast.12, bf16[32,64,256]{2,1,0:T(8,128)(2,1)} %bitcast.10, ...), custom_call_target="tpu_custom_call" | custom-call | tf_op jit(solution)/shard_map/prepare/pallas_call | solution.py:288
  14.4 0.0 collective-permute-done.2.rest_1_
  14.4 0.3 collective-permute-done.5.rest_4_
  14.7 2.1 %collective-permute-done.6.rest_5_ = bf16[16,1024]{1,0:T(8,128)(2,1)S(1)} collective-permute-done((bf16[16,1024]{1,0:T(8,128)(2,1)}, bf16[16,1024]{1,0:T(8,128)(2,1)S(1)}, u32[]{:S(2)}, u32[]{:S(2)}) %collective-permute-start.6) | collective-permute-done | bytes 32800 | tf_op jit(solution)/shard_map/ppermute | solution.py:26
  16.9 0.8 %suffix_away.1 = (bf16[4,2,144,128]{3,2,1,0:T(8,128)(2,1)S(1)}, f32[8,128]{1,0:T(8,128)S(1)}) custom-call(bf16[4,512,128]{2,1,0:T(8,128)(2,1)S(1)} %get-tuple-element.15.keys_ref, bf16[4,128,512]{2,1,0:T(8,128)(2,1)S(1)} %get-tuple-element.16.values_ref, f32[4,8,256]{2,1,0:T(8,128)S(1)} %get-tuple-element.17.member_ref, ...), custom_call_target="tpu_custom_call" | custom-call | tf_op jit(solution)/shard_map/suffix_away/pallas_call | solution.py:317
  17.7 0.7 %copy-done = bf16[4,2,144,128]{3,2,1,0:T(8,128)(2,1)} copy-done((bf16[4,2,144,128]{3,2,1,0:T(8,128)(2,1)}, bf16[4,2,144,128]{3,2,1,0:T(8,128)(2,1)S(1)}, u32[]{:S(2)}) %copy-start) | copy-done | bytes 294936
  18.4 4.2 %all-to-all-start = ((bf16[8,144,128]{2,1,0:T(8,128)(2,1)}), bf16[8,144,128]{2,1,0:T(8,128)(2,1)S(1)}, u32[]{:S(2)}, u32[]{:S(2)}) async-start(bf16[8,144,128]{2,1,0:T(8,128)(2,1)} %bitcast.7), calls=%async_computation | async-start | bytes 589824 | tf_op jit(solution)/shard_map/all_to_all | solution.py:329
  23.3 3.9 %home_part.1 = (f32[128,128]{1,0:T(8,128)S(1)}, f32[8,128]{1,0:T(8,128)S(1)}, bf16[144,128]{1,0:T(8,128)(2,1)S(1)}) custom-call(s32[1]{0:T(128)S(6)} %copy.7.length_ref, bf16[4,512,128]{2,1,0:T(8,128)(2,1)S(1)} %get-tuple-element.15.keys_ref, bf16[4,128,512]{2,1,0:T(8,128)(2,1)S(1)} %get-tuple-element.16.values_ref, ...), custom_call_target="tpu_custom_call" | custom-call | flops 536870912 | bytes 2097152 | tf_op jit(solution)/shard_map/home_part/pallas_call | solution.py:331
  27.2 0.0 copy-start.1
  27.2 0.6 %copy-done.1 = f32[128,128]{1,0:T(8,128)} copy-done((f32[128,128]{1,0:T(8,128)}, f32[128,128]{1,0:T(8,128)S(1)}, u32[]{:S(2)}) %copy-start.1) | copy-done | bytes 65560
  27.8 2.0 %collective-permute-start.8 = (bf16[144,128]{1,0:T(8,128)(2,1)S(1)}, bf16[144,128]{1,0:T(8,128)(2,1)S(1)}, u32[]{:S(2)}, u32[]{:S(2)}) collective-permute-start(bf16[144,128]{1,0:T(8,128)(2,1)S(1)} %get-tuple-element.22), channel_id=1, source_target_pairs={{0,1},{1,0},{2,3},{3,2},{4,5},{5,4},{6,7},{7,6},{8,9},{9,8},{10,11... | collective-permute-start | bytes 110600 | tf_op jit(solution)/shard_map/ppermute | solution.py:26
  29.8 1.9 %collective-permute-done.8.last_ref = bf16[144,128]{1,0:T(8,128)(2,1)S(1)} collective-permute-done((bf16[144,128]{1,0:T(8,128)(2,1)S(1)}, bf16[144,128]{1,0:T(8,128)(2,1)S(1)}, u32[]{:S(2)}, u32[]{:S(2)}) %collective-permute-start.8) | collective-permute-done | bytes 36896 | tf_op jit(solution)/shard_map/ppermute | solution.py:26
  31.8 0.8 %copy-done.2 = f32[128,128]{1,0:T(8,128)S(1)} copy-done((f32[128,128]{1,0:T(8,128)S(1)}, f32[128,128]{1,0:T(8,128)}, u32[]{:S(2)}) %copy-start.2) | copy-done | bytes 65560
  32.6 0.8 %combine.1 = f32[16,1024]{1,0:T(8,128)} custom-call(bf16[4,2,144,128]{3,2,1,0:T(8,128)(2,1)S(1)} %bitcast.6, bf16[144,128]{1,0:T(8,128)(2,1)S(1)} %collective-permute-done.8.last_ref, f32[128,128]{1,0:T(8,128)S(1)} %copy-done.2, f32[8,128]{1,0:T(8,128)S(1)} %get-tuple-element.24.stats_ref), custom_call_target="tpu_custom_call" | custom-call | tf_op jit(solution)/shard_map/combine/pallas_call | solution.py:348
  (6 shorter events, 0.0 us)
Async XLA Ops:
  0.0 11.8 %collective-permute-start = (bf16[32,64,256]{2,1,0:T(8,128)(2,1)}, bf16[32,64,256]{2,1,0:T(8,128)(2,1)S(1)}, u32[]{:S(2)}, u32[]{:S(2)}) collective-permute-start(bf16[32,64,256]{2,1,0:T(8,128)(2,1)} %bitcast.9), channel_id=1, source_target_pairs={{0,4},{4,0},{1,5},{5,1},{2,6},{6,2},{3,7},{7,3},{8,12},{12,8},{9,1... | collective-permute-start | bytes 3145736 | tf_op jit(solution)/shard_map/ppermute | solution.py:26
  0.5 7.1 %collective-permute-start.7 = (bf16[16,1024]{1,0:T(8,128)(2,1)}, bf16[16,1024]{1,0:T(8,128)(2,1)S(1)}, u32[]{:S(2)}, u32[]{:S(2)}) collective-permute-start(bf16[16,1024]{1,0:T(8,128)(2,1)} %own_ref.1), channel_id=1, source_target_pairs={{0,1},{1,0},{2,3},{3,2},{4,5},{5,4},{6,7},{7,6},{8,9},{9,8},{10,11... | collective-permute-start | bytes 98312 | tf_op jit(solution)/shard_map/ppermute | solution.py:26
  2.9 7.7 %collective-permute-start.1 = (bf16[16,1024]{1,0:T(8,128)(2,1)}, bf16[16,1024]{1,0:T(8,128)(2,1)S(1)}, u32[]{:S(2)}, u32[]{:S(2)}) collective-permute-start(bf16[16,1024]{1,0:T(8,128)(2,1)} %own_ref.1), channel_id=1, source_target_pairs={{0,24},{8,16},{16,8},{24,0},{1,25},{9,17},{17,9},{25,1},{2,26},{10... | collective-permute-start | bytes 98312 | tf_op jit(solution)/shard_map/ppermute | solution.py:26
  6.5 7.9 %collective-permute-start.2 = (bf16[16,1024]{1,0:T(8,128)(2,1)}, bf16[16,1024]{1,0:T(8,128)(2,1)S(1)}, u32[]{:S(2)}, u32[]{:S(2)}) collective-permute-start(bf16[16,1024]{1,0:T(8,128)(2,1)} %own_ref.1), channel_id=1, source_target_pairs={{0,25},{1,24},{8,17},{9,16},{16,9},{17,8},{24,1},{25,0},{2,27},{3,... | collective-permute-start | bytes 98312 | tf_op jit(solution)/shard_map/ppermute | solution.py:26
  6.5 7.9 %collective-permute-start.3 = (bf16[16,1024]{1,0:T(8,128)(2,1)}, bf16[16,1024]{1,0:T(8,128)(2,1)S(1)}, u32[]{:S(2)}, u32[]{:S(2)}) collective-permute-start(bf16[16,1024]{1,0:T(8,128)(2,1)} %own_ref.1), channel_id=1, source_target_pairs={{0,16},{8,24},{16,0},{24,8},{1,17},{9,25},{17,1},{25,9},{2,18},{10... | collective-permute-start | bytes 98312 | tf_op jit(solution)/shard_map/ppermute | solution.py:26
  7.5 6.9 %collective-permute-start.4 = (bf16[16,1024]{1,0:T(8,128)(2,1)}, bf16[16,1024]{1,0:T(8,128)(2,1)S(1)}, u32[]{:S(2)}, u32[]{:S(2)}) collective-permute-start(bf16[16,1024]{1,0:T(8,128)(2,1)} %own_ref.1), channel_id=1, source_target_pairs={{0,17},{1,16},{8,25},{9,24},{16,1},{17,0},{24,9},{25,8},{2,19},{3,... | collective-permute-start | bytes 98312 | tf_op jit(solution)/shard_map/ppermute | solution.py:26
  10.6 4.1 %collective-permute-start.5 = (bf16[16,1024]{1,0:T(8,128)(2,1)}, bf16[16,1024]{1,0:T(8,128)(2,1)S(1)}, u32[]{:S(2)}, u32[]{:S(2)}) collective-permute-start(bf16[16,1024]{1,0:T(8,128)(2,1)} %own_ref.1), channel_id=1, source_target_pairs={{0,8},{8,0},{16,24},{24,16},{1,9},{9,1},{17,25},{25,17},{2,10},{10... | collective-permute-start | bytes 98312 | tf_op jit(solution)/shard_map/ppermute | solution.py:26
  11.8 5.0 %collective-permute-start.6 = (bf16[16,1024]{1,0:T(8,128)(2,1)}, bf16[16,1024]{1,0:T(8,128)(2,1)S(1)}, u32[]{:S(2)}, u32[]{:S(2)}) collective-permute-start(bf16[16,1024]{1,0:T(8,128)(2,1)} %own_ref.1), channel_id=1, source_target_pairs={{0,9},{1,8},{8,1},{9,0},{16,25},{17,24},{24,17},{25,16},{2,11},{3,... | collective-permute-start | bytes 98312 | tf_op jit(solution)/shard_map/ppermute | solution.py:26
  17.7 0.7 %copy-start = (bf16[4,2,144,128]{3,2,1,0:T(8,128)(2,1)}, bf16[4,2,144,128]{3,2,1,0:T(8,128)(2,1)S(1)}, u32[]{:S(2)}) copy-start(bf16[4,2,144,128]{3,2,1,0:T(8,128)(2,1)S(1)} %get-tuple-element.18) | copy-start | bytes 884740
  18.4 13.3 %all-to-all-start = ((bf16[8,144,128]{2,1,0:T(8,128)(2,1)}), bf16[8,144,128]{2,1,0:T(8,128)(2,1)S(1)}, u32[]{:S(2)}, u32[]{:S(2)}) async-start(bf16[8,144,128]{2,1,0:T(8,128)(2,1)} %bitcast.7), calls=%async_computation | async-start | bytes 589824 | tf_op jit(solution)/shard_map/all_to_all | solution.py:329
  27.2 0.6 %copy-start.1 = (f32[128,128]{1,0:T(8,128)}, f32[128,128]{1,0:T(8,128)S(1)}, u32[]{:S(2)}) copy-start(f32[128,128]{1,0:T(8,128)S(1)} %get-tuple-element.23.summed_ref) | copy-start | bytes 196612
  27.8 4.0 %collective-permute-start.8 = (bf16[144,128]{1,0:T(8,128)(2,1)S(1)}, bf16[144,128]{1,0:T(8,128)(2,1)S(1)}, u32[]{:S(2)}, u32[]{:S(2)}) collective-permute-start(bf16[144,128]{1,0:T(8,128)(2,1)S(1)} %get-tuple-element.22), channel_id=1, source_target_pairs={{0,1},{1,0},{2,3},{3,2},{4,5},{5,4},{6,7},{7,6},{8,9},{9,8},{10,11... | collective-permute-start | bytes 110600 | tf_op jit(solution)/shard_map/ppermute | solution.py:26
  31.8 0.8 %copy-start.2 = (f32[128,128]{1,0:T(8,128)S(1)}, f32[128,128]{1,0:T(8,128)}, u32[]{:S(2)}) copy-start(f32[128,128]{1,0:T(8,128)} %copy-done.1) | copy-start | bytes 196612

commit v10 on v9

--- a/solution.py
+++ b/solution.py
@@ -16,6 +16,7 @@
 STAT_ROWS = 16
 UNIT_ROWS = HD + STAT_ROWS
 CHUNK = 512
+PASSED_ON = (2,)
 
 big_negative = -1e30
 to_exp2 = HD ** (-0.5) * 1.4426950408889634
@@ -24,6 +25,13 @@
 def swapped(value, axis, mask=1):
     size = lax.axis_size(axis)
     return lax.ppermute(value, axis, [(i, i ^ mask) for i in range(size)])
+
+
+def routes(n_req):
+    first = [(d, 0) for d in PASSED_ON if d < n_req]
+    last = [(d, 1) for d, _ in first]
+    direct = [(d, side) for d in range(n_req - 1, 0, -1) for side in (0, 1)]
+    return first + [route for route in direct if route not in first + last] + last
 
 
 def stacked_heads(q):
@@ -117,9 +125,9 @@
 
 def prepare_kernel(
     capacity, table_ref, parents_ref, near_ref, prompt_ref, own_ref, far_ref,
-    keys_ref, values_ref, member_ref, held_ref, own, rows_ref, table, parents, near, sems,
+    home_keys_ref, home_values_ref, keys_ref, values_ref, member_ref, held_ref, own, rows_ref, table, parents, near, sems,
 ):
-    n_req = keys_ref.shape[0]
+    n_req = keys_ref.shape[0] + 1
     slots, half, _ = near.shape
     rows = table.shape[1]
     n_batch = rows // BEAMS
@@ -181,9 +189,17 @@
             pool_ref = near if k < capacity else far_ref
             base = 0 if k < capacity else slots
             content = pool_ref[jnp.maximum(index - 1 - base, 0)]
-            keys_ref[d, k * half : (k + 1) * half, :] = content[:, :HD]
+            tokens = slice(k * half, (k + 1) * half)
+            if d == 0:
+                home_keys_ref[0, tokens, :] = content[:, :HD]
+            else:
+                keys_ref[d - 1, tokens, :] = content[:, :HD]
             values.append(content[:, HD:])
-        values_ref[d] = jnp.concatenate(values, axis=0).T
+        values = jnp.concatenate(values, axis=0).T
+        if d == 0:
+            home_values_ref[0] = values
+        else:
+            values_ref[d - 1] = values
     small[3].wait()
     small[4].wait()
 
@@ -192,20 +208,15 @@
     return jnp.concatenate([stacked_heads(own_ref[...]), stacked_heads(pair_ref[...])], axis=0)
 
 
-def suffix_parts(requests, queries, keys_ref, values_ref, member_ref):
-    n_slots = member_ref.shape[1]
+def suffix_parts(vectors, keys_ref, values_ref, members):
+    n_slots = members[0].shape[0]
     half = keys_ref.shape[1] // n_slots
-    scores = [
-        scores_of(keys_ref[d], all_vectors(*queries[2 * i : 2 * i + 2]))
-        for i, d in enumerate(requests)
-    ]
+    scores = [scores_of(keys_ref[i], each) for i, each in enumerate(vectors)]
     softmaxes = []
-    for d, score in zip(requests, scores):
+    for member, score in zip(members, scores):
         pieces = [
             jnp.where(
-                member_ref[d, k : k + 1, :] > 0.0,
-                score[k * half : (k + 1) * half],
-                big_negative,
+                member[k : k + 1, :] > 0.0, score[k * half : (k + 1) * half], big_negative
             )
             for k in range(n_slots)
         ]
@@ -215,10 +226,10 @@
             top,
             total,
             jnp.dot(
-                values_ref[d], weights.astype(jnp.bfloat16), preferred_element_type=jnp.float32
+                values_ref[i], weights.astype(jnp.bfloat16), preferred_element_type=jnp.float32
             ),
         )
-        for d, (top, total, weights) in zip(requests, softmaxes)
+        for i, (top, total, weights) in enumerate(softmaxes)
     ]
 
 
@@ -228,11 +239,15 @@
 
 
 def away_kernel(keys_ref, values_ref, member_ref, *rest):
-    queries, out_ref, after_ref = rest[:-3], rest[-2], rest[-1]
+    queries, out_ref, after_ref = rest[:-2], rest[-2], rest[-1]
     after_ref[...] = jnp.zeros(after_ref.shape, jnp.float32)
-    requests = tuple(reversed(range(1, keys_ref.shape[0])))
+    requests = range(1, keys_ref.shape[0] + 1)
     z, parity = lax.axis_index("z"), lax.axis_index("pair")
-    parts = suffix_parts(requests, queries, keys_ref, values_ref, member_ref)
+    order = routes(len(requests) + 1)
+    vectors = [
+        all_vectors(queries[order.index((d, 0))], queries[order.index((d, 1))]) for d in requests
+    ]
+    parts = suffix_parts(vectors, keys_ref, values_ref, [member_ref[d] for d in requests])
     for d, part in zip(requests, parts):
         store_unit(out_ref.at[z ^ d, parity], *half_of(part, 0))
         store_unit(out_ref.at[z ^ d, 1 - parity], *half_of(part, 1))
@@ -244,8 +259,9 @@
     half, length_ref, keys_ref, values_ref, member_ref, own_ref, pair_ref, prompt_ref, after_ref,
     summed_ref, stats_ref, out_ref,
 ):
-    (suffix,) = suffix_parts((0,), (own_ref, pair_ref), keys_ref, values_ref, member_ref)
-    prompt = prompt_part(length_ref[0], half, prompt_ref, all_vectors(own_ref, pair_ref))
+    vectors = all_vectors(own_ref, pair_ref)
+    (suffix,) = suffix_parts([vectors], keys_ref, values_ref, [member_ref[0]])
+    prompt = prompt_part(length_ref[0], half, prompt_ref, vectors)
     part = merged([prompt, suffix])
     top, total, summed_ref[...] = half_of(part, 0)
     stats_ref[...] = jnp.concatenate([top, total, jnp.zeros((6, VECS), jnp.float32)], axis=0)
@@ -280,22 +296,29 @@
     hbm = pl.BlockSpec(memory_space=pltpu.HBM)
     near = pool.reshape(slots, half, width)
     far = swapped(near, "core")
-    sent = []
-    for d in reversed(range(1, n_req)):
-        sent += [swapped(queries, "z", d), swapped(queries, ("z", "pair"), 2 * d + 1)]
+    sent = {}
+    for d, side in routes(n_req):
+        if side == 0:
+            sent[d, 0] = swapped(queries, "z", d)
+        elif d in PASSED_ON:
+            sent[d, 1] = swapped(sent[d, 0], "pair")
+        else:
+            sent[d, 1] = swapped(queries, ("z", "pair"), 2 * d + 1)
     other = swapped(queries, "pair")
 
-    keys, values, member, prompt, own = pl.pallas_call(
+    home_keys, home_values, keys, values, member, prompt, own = pl.pallas_call(
         functools.partial(prepare_kernel, capacity),
         out_shape=(
-            pltpu.VMEM((n_req, 2 * capacity * half, HD), jnp.bfloat16),
-            pltpu.VMEM((n_req, HD, 2 * capacity * half), jnp.bfloat16),
+            pltpu.VMEM((1, 2 * capacity * half, HD), jnp.bfloat16),
+            pltpu.VMEM((1, HD, 2 * capacity * half), jnp.bfloat16),
+            pltpu.VMEM((n_req - 1, 2 * capacity * half, HD), jnp.bfloat16),
+            pltpu.VMEM((n_req - 1, HD, 2 * capacity * half), jnp.bfloat16),
             pltpu.VMEM((n_req, 2 * capacity, 2 * VECS), jnp.float32),
             pltpu.VMEM((tokens, width), jnp.bfloat16),
             pltpu.VMEM(queries.shape, jnp.bfloat16),
         ),
         in_specs=[hbm] * 5 + [vmem],
-        out_specs=(vmem,) * 5,
+        out_specs=(vmem,) * 7,
         scratch_shapes=[
             pltpu.VMEM((2 * slots + 8, 2 * VECS), jnp.float32),
             pltpu.VMEM((SUF, rows), jnp.int32),
@@ -320,11 +343,11 @@
             pltpu.VMEM((n_req, 2, UNIT_ROWS, VECS), jnp.bfloat16),
             pltpu.VMEM((8, VECS), jnp.float32),
         ),
-        in_specs=[vmem] * (4 + len(sent)),
+        in_specs=[vmem] * (3 + len(sent)),
         out_specs=(vmem,) * 2,
         compiler_params=params,
         name="suffix_away",
-    )(keys, values, member, *sent, other)
+    )(keys, values, member, *sent.values())
     units = units.reshape(2 * n_req, UNIT_ROWS, VECS)
     units = lax.all_to_all(units, ("z", "pair"), split_axis=0, concat_axis=0, tiled=True)
 
@@ -342,7 +365,7 @@
             flops=8 * tokens * VECS * HD, bytes_accessed=2 * tokens * width, transcendentals=0
         ),
         name="home_part",
-    )(lengths, keys, values, member, own, other, prompt, after)
+    )(lengths, home_keys, home_values, member, own, other, prompt, after)
     last = swapped(given, "pair")
 
     return pl.pallas_call(

time: 33.7 us -> 33.6 us (level)
  local copies, waits for them, and re-layouts: 2.17 us -> 0.01 us
  starting transfers between devices: 18.6 us -> 20 us
  Pallas kernels: 7.48 us -> 8.2 us
    unnamed x6 -> x2, local copies, waits for them, and re-layouts: 2.17 us -> 0.01 us
    ppermute x9, starting transfers between devices: 14.4 us -> 16.1 us  [swapped(): return lax.ppermute(value, axis, [(i, i ^ mask) for i in range(size)])]
    pallas_call x1, Pallas kernels: 0.82 us -> 1.54 us  [on_device(): pl.pallas_call(away_kernel, out_shape=(pltpu.VMEM((n_req, 2, UNIT_ROWS, V...]
where the time goes in v10:
time: 33.6 us; the launch traced here: 33.4 us
  starting transfers between devices  20 us (60%)
  Pallas kernels  8.2 us (24%)
  waiting for transfers between devices  4.48 us (13%)
  between operations  0.71 us (2%)
    ppermute x9, starting transfers between devices, swapped(): return lax.ppermute(value, axis, [(i, i ^ mask) for i in range(size)])  16.1 us
    ppermute x9, waiting for transfers between devices, swapped(): return lax.ppermute(value, axis, [(i, i ^ mask) for i in range(size)])  4.48 us
    all_to_all x1, starting transfers between devices, on_device(): lax.all_to_all(units, ('z', 'pair'), split_axis=0, concat_axis=0, tiled=T...  3.91 us
    pallas_call x1, Pallas kernels, on_device(): pl.pallas_call(functools.partial(home_kernel, half), out_shape=(pltpu.VME...  3.88 us
    pallas_call x1, Pallas kernels, on_device(): pl.pallas_call(functools.partial(prepare_kernel, capacity), out_shape=(pl...  1.99 us
    pallas_call x1, Pallas kernels, on_device(): pl.pallas_call(away_kernel, out_shape=(pltpu.VMEM((n_req, 2, UNIT_ROWS, V...  1.54 us
    pallas_call x1, Pallas kernels, on_device(): pl.pallas_call(final_kernel, out_shape=jax.ShapeDtypeStruct((BEAMS, HEADS...  0.79 us
  transfers between devices with their start and end apart: 10, of which 3 were waited for; matrix products, arithmetic and copies ran while one was open for 0% of the time, Pallas kernels for 18%

profile of v10, /device:TPU:0, one launch (start us, length us, event | category | flops | bytes accessed | tf_op | source)
XLA Modules:
  0.0 33.4 jit_solution(13830604377748645030)
XLA Ops:
  0.0 0.5 %collective-permute-start = (bf16[32,64,256]{2,1,0:T(8,128)(2,1)}, bf16[32,64,256]{2,1,0:T(8,128)(2,1)S(1)}, u32[]{:S(2)}, u32[]{:S(2)}) collective-permute-start(bf16[32,64,256]{2,1,0:T(8,128)(2,1)} %bitcast.8), channel_id=1, source_target_pairs={{0,4},{4,0},{1,5},{5,1},{2,6},{6,2},{3,7},{7,3},{8,12},{12,8},{9,1... | collective-permute-start | bytes 3145736 | tf_op jit(solution)/shard_map/ppermute | solution.py:27
  0.5 3.6 %collective-permute-start.1 = (bf16[16,1024]{1,0:T(8,128)(2,1)}, bf16[16,1024]{1,0:T(8,128)(2,1)S(1)}, u32[]{:S(2)}, u32[]{:S(2)}) collective-permute-start(bf16[16,1024]{1,0:T(8,128)(2,1)} %own_ref.1), channel_id=1, source_target_pairs={{0,16},{8,24},{16,0},{24,8},{1,17},{9,25},{17,1},{25,9},{2,18},{10... | collective-permute-start | bytes 98312 | tf_op jit(solution)/shard_map/ppermute | solution.py:27
  4.0 1.3 %collective-permute-start.2 = (bf16[16,1024]{1,0:T(8,128)(2,1)}, bf16[16,1024]{1,0:T(8,128)(2,1)S(1)}, u32[]{:S(2)}, u32[]{:S(2)}) collective-permute-start(bf16[16,1024]{1,0:T(8,128)(2,1)} %own_ref.1), channel_id=1, source_target_pairs={{0,24},{8,16},{16,8},{24,0},{1,25},{9,17},{17,9},{25,1},{2,26},{10... | collective-permute-start | bytes 98312 | tf_op jit(solution)/shard_map/ppermute | solution.py:27
  5.4 3.4 %collective-permute-start.3 = (bf16[16,1024]{1,0:T(8,128)(2,1)}, bf16[16,1024]{1,0:T(8,128)(2,1)S(1)}, u32[]{:S(2)}, u32[]{:S(2)}) collective-permute-start(bf16[16,1024]{1,0:T(8,128)(2,1)} %own_ref.1), channel_id=1, source_target_pairs={{0,25},{1,24},{8,17},{9,16},{16,9},{17,8},{24,1},{25,0},{2,27},{3,... | collective-permute-start | bytes 98312 | tf_op jit(solution)/shard_map/ppermute | solution.py:27
  8.8 0.0 collective-permute-start.4
  8.8 0.0 collective-permute-done.1.rest_0_
  8.8 2.0 %collective-permute-start.5 = (bf16[16,1024]{1,0:T(8,128)(2,1)}, bf16[16,1024]{1,0:T(8,128)(2,1)S(1)}, u32[]{:S(2)}, u32[]{:S(2)}) collective-permute-start(bf16[16,1024]{1,0:T(8,128)(2,1)} %own_ref.1), channel_id=1, source_target_pairs={{0,9},{1,8},{8,1},{9,0},{16,25},{17,24},{24,17},{25,16},{2,11},{3,... | collective-permute-start | bytes 98312 | tf_op jit(solution)/shard_map/ppermute | solution.py:27
  10.8 0.0 collective-permute-done.far_ref
  10.8 1.5 %collective-permute-start.6 = (bf16[16,1024]{1,0:T(8,128)(2,1)S(1)}, bf16[16,1024]{1,0:T(8,128)(2,1)S(1)}, u32[]{:S(2)}, u32[]{:S(2)}) collective-permute-start(bf16[16,1024]{1,0:T(8,128)(2,1)S(1)} %collective-permute-done.1.rest_0_), channel_id=1, source_target_pairs={{0,1},{1,0},{2,3},{3,2},{4,5},{5,4},{6,7},{7,6},{8,9},{9,8},{10,11... | collective-permute-start | bytes 98312 | tf_op jit(solution)/shard_map/ppermute | solution.py:27
  12.3 2.0 %prepare.1 = (bf16[1,512,128]{2,1,0:T(8,128)(2,1)S(1)}, bf16[1,128,512]{2,1,0:T(8,128)(2,1)S(1)}, bf16[3,512,128]{2,1,0:T(8,128)(2,1)S(1)}, bf16[3,128,512]{2,1,...) custom-call(s32[4,128]{1,0:T(4,128)} %bitcast.10, ...), custom_call_target="tpu_custom_call" | custom-call | tf_op jit(solution)/shard_map/prepare/pallas_call | solution.py:309
  14.3 0.0 collective-permute-done.2.rest_1_
  14.3 0.0 collective-permute-done.3.rest_2_
  14.3 0.0 collective-permute-done.4.rest_3_
  14.3 0.0 collective-permute-done.5.rest_4_
  14.3 0.4 %collective-permute-done.6.rest_5_ = bf16[16,1024]{1,0:T(8,128)(2,1)S(1)} collective-permute-done((bf16[16,1024]{1,0:T(8,128)(2,1)S(1)}, bf16[16,1024]{1,0:T(8,128)(2,1)S(1)}, u32[]{:S(2)}, u32[]{:S(2)}) %collective-permute-start.6) | collective-permute-done | bytes 32800 | tf_op jit(solution)/shard_map/ppermute | solution.py:27
  14.7 1.5 %suffix_away.1 = (bf16[4,2,144,128]{3,2,1,0:T(8,128)(2,1)}, f32[8,128]{1,0:T(8,128)S(1)}) custom-call(bf16[3,512,128]{2,1,0:T(8,128)(2,1)S(1)} %get-tuple-element.17.keys_ref, bf16[3,128,512]{2,1,0:T(8,128)(2,1)S(1)} %get-tuple-element.18.values_ref, f32[4,8,256]{2,1,0:T(8,128)S(1)} %get-tuple-element.19.member_ref, ...), custom_call_target="tpu_custom_call" | custom-call | tf_op jit(solution)/shard_map/suffix_away/pallas_call | solution.py:340
  16.2 3.9 %all-to-all-start = ((bf16[8,144,128]{2,1,0:T(8,128)(2,1)}), bf16[8,144,128]{2,1,0:T(8,128)(2,1)S(1)}, u32[]{:S(2)}, u32[]{:S(2)}) async-start(bf16[8,144,128]{2,1,0:T(8,128)(2,1)} %bitcast.4), calls=%async_computation | async-start | bytes 589824 | tf_op jit(solution)/shard_map/all_to_all | solution.py:352
  20.2 2.0 %collective-permute-start.7 = (bf16[16,1024]{1,0:T(8,128)(2,1)S(1)}, bf16[16,1024]{1,0:T(8,128)(2,1)S(1)}, u32[]{:S(2)}, u32[]{:S(2)}) collective-permute-start(bf16[16,1024]{1,0:T(8,128)(2,1)S(1)} %copy-done), channel_id=1, source_target_pairs={{0,1},{1,0},{2,3},{3,2},{4,5},{5,4},{6,7},{7,6},{8,9},{9,8},{10,11... | collective-permute-start | bytes 98312 | tf_op jit(solution)/shard_map/ppermute | solution.py:27
  22.8 1.8 %collective-permute-done.7.pair_ref = bf16[16,1024]{1,0:T(8,128)(2,1)S(1)} collective-permute-done((bf16[16,1024]{1,0:T(8,128)(2,1)S(1)}, bf16[16,1024]{1,0:T(8,128)(2,1)S(1)}, u32[]{:S(2)}, u32[]{:S(2)}) %collective-permute-start.7) | collective-permute-done | bytes 32800 | tf_op jit(solution)/shard_map/ppermute | solution.py:27
  24.7 3.9 %home_part.1 = (f32[128,128]{1,0:T(8,128)S(1)}, f32[8,128]{1,0:T(8,128)S(1)}, bf16[144,128]{1,0:T(8,128)(2,1)S(1)}) custom-call(s32[1]{0:T(128)S(6)} %copy.7.length_ref, bf16[1,512,128]{2,1,0:T(8,128)(2,1)S(1)} %get-tuple-element.21.keys_ref, bf16[1,128,512]{2,1,0:T(8,128)(2,1)S(1)} %get-tuple-element.22.values_ref, ...), custom_call_target="tpu_custom_call" | custom-call | flops 536870912 | bytes 2097152 | tf_op jit(solution)/shard_map/home_part/pallas_call | solution.py:354
  28.6 1.8 %collective-permute-start.8 = (bf16[144,128]{1,0:T(8,128)(2,1)S(1)}, bf16[144,128]{1,0:T(8,128)(2,1)S(1)}, u32[]{:S(2)}, u32[]{:S(2)}) collective-permute-start(bf16[144,128]{1,0:T(8,128)(2,1)S(1)} %get-tuple-element.26), channel_id=1, source_target_pairs={{0,1},{1,0},{2,3},{3,2},{4,5},{5,4},{6,7},{7,6},{8,9},{9,8},{10,11... | collective-permute-start | bytes 110600 | tf_op jit(solution)/shard_map/ppermute | solution.py:27
  30.3 2.2 %collective-permute-done.8.last_ref = bf16[144,128]{1,0:T(8,128)(2,1)S(1)} collective-permute-done((bf16[144,128]{1,0:T(8,128)(2,1)S(1)}, bf16[144,128]{1,0:T(8,128)(2,1)S(1)}, u32[]{:S(2)}, u32[]{:S(2)}) %collective-permute-start.8) | collective-permute-done | bytes 36896 | tf_op jit(solution)/shard_map/ppermute | solution.py:27
  32.6 0.0 all-to-all-done
  32.6 0.8 %combine.1 = f32[16,1024]{1,0:T(8,128)} custom-call(bf16[4,2,144,128]{3,2,1,0:T(8,128)(2,1)S(1)} %bitcast.6, bf16[144,128]{1,0:T(8,128)(2,1)S(1)} %collective-permute-done.8.last_ref, f32[128,128]{1,0:T(8,128)S(1)} %get-tuple-element.27.summed_ref, f32[8,128]{1,0:T(8,128)S(1)} %get-tuple-element.28.stats_ref), custom_call_target="tpu_custom_call" | custom-call | tf_op jit(solution)/shard_map/combine/pallas_call | solution.py:371
  (2 shorter events, 0.0 us)
Async XLA Ops:
  0.0 10.8 %collective-permute-start = (bf16[32,64,256]{2,1,0:T(8,128)(2,1)}, bf16[32,64,256]{2,1,0:T(8,128)(2,1)S(1)}, u32[]{:S(2)}, u32[]{:S(2)}) collective-permute-start(bf16[32,64,256]{2,1,0:T(8,128)(2,1)} %bitcast.8), channel_id=1, source_target_pairs={{0,4},{4,0},{1,5},{5,1},{2,6},{6,2},{3,7},{7,3},{8,12},{12,8},{9,1... | collective-permute-start | bytes 3145736 | tf_op jit(solution)/shard_map/ppermute | solution.py:27
  0.5 8.3 %collective-permute-start.1 = (bf16[16,1024]{1,0:T(8,128)(2,1)}, bf16[16,1024]{1,0:T(8,128)(2,1)S(1)}, u32[]{:S(2)}, u32[]{:S(2)}) collective-permute-start(bf16[16,1024]{1,0:T(8,128)(2,1)} %own_ref.1), channel_id=1, source_target_pairs={{0,16},{8,24},{16,0},{24,8},{1,17},{9,25},{17,1},{25,9},{2,18},{10... | collective-permute-start | bytes 98312 | tf_op jit(solution)/shard_map/ppermute | solution.py:27
  4.0 10.3 %collective-permute-start.2 = (bf16[16,1024]{1,0:T(8,128)(2,1)}, bf16[16,1024]{1,0:T(8,128)(2,1)S(1)}, u32[]{:S(2)}, u32[]{:S(2)}) collective-permute-start(bf16[16,1024]{1,0:T(8,128)(2,1)} %own_ref.1), channel_id=1, source_target_pairs={{0,24},{8,16},{16,8},{24,0},{1,25},{9,17},{17,9},{25,1},{2,26},{10... | collective-permute-start | bytes 98312 | tf_op jit(solution)/shard_map/ppermute | solution.py:27
  5.4 8.9 %collective-permute-start.3 = (bf16[16,1024]{1,0:T(8,128)(2,1)}, bf16[16,1024]{1,0:T(8,128)(2,1)S(1)}, u32[]{:S(2)}, u32[]{:S(2)}) collective-permute-start(bf16[16,1024]{1,0:T(8,128)(2,1)} %own_ref.1), channel_id=1, source_target_pairs={{0,25},{1,24},{8,17},{9,16},{16,9},{17,8},{24,1},{25,0},{2,27},{3,... | collective-permute-start | bytes 98312 | tf_op jit(solution)/shard_map/ppermute | solution.py:27
  8.8 5.5 %collective-permute-start.4 = (bf16[16,1024]{1,0:T(8,128)(2,1)}, bf16[16,1024]{1,0:T(8,128)(2,1)S(1)}, u32[]{:S(2)}, u32[]{:S(2)}) collective-permute-start(bf16[16,1024]{1,0:T(8,128)(2,1)} %own_ref.1), channel_id=1, source_target_pairs={{0,8},{8,0},{16,24},{24,16},{1,9},{9,1},{17,25},{25,17},{2,10},{10... | collective-permute-start | bytes 98312 | tf_op jit(solution)/shard_map/ppermute | solution.py:27
  8.8 5.5 %collective-permute-start.5 = (bf16[16,1024]{1,0:T(8,128)(2,1)}, bf16[16,1024]{1,0:T(8,128)(2,1)S(1)}, u32[]{:S(2)}, u32[]{:S(2)}) collective-permute-start(bf16[16,1024]{1,0:T(8,128)(2,1)} %own_ref.1), channel_id=1, source_target_pairs={{0,9},{1,8},{8,1},{9,0},{16,25},{17,24},{24,17},{25,16},{2,11},{3,... | collective-permute-start | bytes 98312 | tf_op jit(solution)/shard_map/ppermute | solution.py:27
  10.8 3.9 %collective-permute-start.6 = (bf16[16,1024]{1,0:T(8,128)(2,1)S(1)}, bf16[16,1024]{1,0:T(8,128)(2,1)S(1)}, u32[]{:S(2)}, u32[]{:S(2)}) collective-permute-start(bf16[16,1024]{1,0:T(8,128)(2,1)S(1)} %collective-permute-done.1.rest_0_), channel_id=1, source_target_pairs={{0,1},{1,0},{2,3},{3,2},{4,5},{5,4},{6,7},{7,6},{8,9},{9,8},{10,11... | collective-permute-start | bytes 98312 | tf_op jit(solution)/shard_map/ppermute | solution.py:27
  12.3 7.9 %copy-start = (bf16[16,1024]{1,0:T(8,128)(2,1)S(1)}, bf16[16,1024]{1,0:T(8,128)(2,1)}, u32[]{:S(2)}) copy-start(bf16[16,1024]{1,0:T(8,128)(2,1)} %own_ref.1) | copy-start | bytes 98308
  16.2 16.3 %all-to-all-start = ((bf16[8,144,128]{2,1,0:T(8,128)(2,1)}), bf16[8,144,128]{2,1,0:T(8,128)(2,1)S(1)}, u32[]{:S(2)}, u32[]{:S(2)}) async-start(bf16[8,144,128]{2,1,0:T(8,128)(2,1)} %bitcast.4), calls=%async_computation | async-start | bytes 589824 | tf_op jit(solution)/shard_map/all_to_all | solution.py:352
  20.2 4.5 %collective-permute-start.7 = (bf16[16,1024]{1,0:T(8,128)(2,1)S(1)}, bf16[16,1024]{1,0:T(8,128)(2,1)S(1)}, u32[]{:S(2)}, u32[]{:S(2)}) collective-permute-start(bf16[16,1024]{1,0:T(8,128)(2,1)S(1)} %copy-done), channel_id=1, source_target_pairs={{0,1},{1,0},{2,3},{3,2},{4,5},{5,4},{6,7},{7,6},{8,9},{9,8},{10,11... | collective-permute-start | bytes 98312 | tf_op jit(solution)/shard_map/ppermute | solution.py:27
  28.6 4.0 %collective-permute-start.8 = (bf16[144,128]{1,0:T(8,128)(2,1)S(1)}, bf16[144,128]{1,0:T(8,128)(2,1)S(1)}, u32[]{:S(2)}, u32[]{:S(2)}) collective-permute-start(bf16[144,128]{1,0:T(8,128)(2,1)S(1)} %get-tuple-element.26), channel_id=1, source_target_pairs={{0,1},{1,0},{2,3},{3,2},{4,5},{5,4},{6,7},{7,6},{8,9},{9,8},{10,11... | collective-permute-start | bytes 110600 | tf_op jit(solution)/shard_map/ppermute | solution.py:27

commit v11 on v10

--- a/solution.py
+++ b/solution.py
@@ -16,7 +16,6 @@
 STAT_ROWS = 16
 UNIT_ROWS = HD + STAT_ROWS
 CHUNK = 512
-PASSED_ON = (2,)
 
 big_negative = -1e30
 to_exp2 = HD ** (-0.5) * 1.4426950408889634
@@ -27,11 +26,9 @@
     return lax.ppermute(value, axis, [(i, i ^ mask) for i in range(size)])
 
 
-def routes(n_req):
-    first = [(d, 0) for d in PASSED_ON if d < n_req]
-    last = [(d, 1) for d, _ in first]
-    direct = [(d, side) for d in range(n_req - 1, 0, -1) for side in (0, 1)]
-    return first + [route for route in direct if route not in first + last] + last
+def request_order(n_req):
+    masks = list(range(n_req - 1, 0, -1))
+    return [2, 3, 1] if masks == [3, 2, 1] else masks
 
 
 def stacked_heads(q):
@@ -82,11 +79,6 @@
     rows = three_pieces(top) + three_pieces(total)
     rows.append(jnp.zeros((STAT_ROWS - len(rows), VECS), jnp.float32))
     ref[HD:, :] = jnp.concatenate(rows, axis=0).astype(jnp.bfloat16)
-
-
-def empty_part():
-    zeros = jnp.zeros((1, VECS), jnp.float32)
-    return zeros + big_negative, zeros, jnp.zeros((HD, VECS), jnp.float32)
 
 
 def load_unit(ref):
@@ -208,10 +200,10 @@
     return jnp.concatenate([stacked_heads(own_ref[...]), stacked_heads(pair_ref[...])], axis=0)
 
 
-def suffix_parts(vectors, keys_ref, values_ref, members):
+def suffix_parts(vectors, keys_ref, values_ref, members, places):
     n_slots = members[0].shape[0]
     half = keys_ref.shape[1] // n_slots
-    scores = [scores_of(keys_ref[i], each) for i, each in enumerate(vectors)]
+    scores = [scores_of(keys_ref[i], each) for i, each in zip(places, vectors)]
     softmaxes = []
     for member, score in zip(members, scores):
         pieces = [
@@ -229,7 +221,7 @@
                 values_ref[i], weights.astype(jnp.bfloat16), preferred_element_type=jnp.float32
             ),
         )
-        for i, (top, total, weights) in enumerate(softmaxes)
+        for i, (top, total, weights) in zip(places, softmaxes)
     ]
 
 
@@ -239,20 +231,25 @@
 
 
 def away_kernel(keys_ref, values_ref, member_ref, *rest):
-    queries, out_ref, after_ref = rest[:-2], rest[-2], rest[-1]
+    queries, (_, out_ref, after_ref, units, sems) = rest[:-5], rest[-5:]
     after_ref[...] = jnp.zeros(after_ref.shape, jnp.float32)
-    requests = range(1, keys_ref.shape[0] + 1)
+    requests = request_order(keys_ref.shape[0] + 1)
     z, parity = lax.axis_index("z"), lax.axis_index("pair")
-    order = routes(len(requests) + 1)
-    vectors = [
-        all_vectors(queries[order.index((d, 0))], queries[order.index((d, 1))]) for d in requests
-    ]
-    parts = suffix_parts(vectors, keys_ref, values_ref, [member_ref[d] for d in requests])
-    for d, part in zip(requests, parts):
-        store_unit(out_ref.at[z ^ d, parity], *half_of(part, 0))
-        store_unit(out_ref.at[z ^ d, 1 - parity], *half_of(part, 1))
-    for side in range(2):
-        store_unit(out_ref.at[z, side], *empty_part())
+    vectors = [all_vectors(*queries[2 * i : 2 * i + 2]) for i in range(len(requests))]
+    members = [member_ref[d] for d in requests]
+    copies = []
+    parts = suffix_parts(vectors, keys_ref, values_ref, members, [d - 1 for d in requests])
+    for i, (d, part) in enumerate(zip(requests, parts)):
+        for side in range(2):
+            store_unit(units.at[i, side], *half_of(part, side))
+            owner = parity if side == 0 else 1 - parity
+            copy = pltpu.make_async_copy(
+                units.at[i, side], out_ref.at[z ^ d, owner], sems.at[i, side]
+            )
+            copy.start()
+            copies.append(copy)
+    for copy in copies:
+        copy.wait()
 
 
 def home_kernel(
@@ -260,7 +257,7 @@
     summed_ref, stats_ref, out_ref,
 ):
     vectors = all_vectors(own_ref, pair_ref)
-    (suffix,) = suffix_parts([vectors], keys_ref, values_ref, [member_ref[0]])
+    (suffix,) = suffix_parts([vectors], keys_ref, values_ref, [member_ref[0]], [0])
     prompt = prompt_part(length_ref[0], half, prompt_ref, vectors)
     part = merged([prompt, suffix])
     top, total, summed_ref[...] = half_of(part, 0)
@@ -270,7 +267,8 @@
 
 def final_kernel(units_ref, last_ref, summed_ref, stats_ref, out_ref):
     n_req, n_pair = units_ref.shape[:2]
-    parts = [load_unit(units_ref.at[r, p]) for r in range(n_req) for p in range(n_pair)]
+    z = lax.axis_index("z")
+    parts = [load_unit(units_ref.at[z ^ d, p]) for d in range(1, n_req) for p in range(n_pair)]
     parts += [load_unit(last_ref), (stats_ref[0:1], stats_ref[1:2], summed_ref[...])]
     _, total, summed = merged(parts)
     attended = (summed / total).T
@@ -296,14 +294,10 @@
     hbm = pl.BlockSpec(memory_space=pltpu.HBM)
     near = pool.reshape(slots, half, width)
     far = swapped(near, "core")
-    sent = {}
-    for d, side in routes(n_req):
-        if side == 0:
-            sent[d, 0] = swapped(queries, "z", d)
-        elif d in PASSED_ON:
-            sent[d, 1] = swapped(sent[d, 0], "pair")
-        else:
-            sent[d, 1] = swapped(queries, ("z", "pair"), 2 * d + 1)
+    sent = []
+    for d in request_order(n_req):
+        piece = swapped(queries, "z", d)
+        sent += [piece, swapped(piece, "pair")]
     other = swapped(queries, "pair")
 
     home_keys, home_values, keys, values, member, prompt, own = pl.pallas_call(
@@ -340,14 +334,18 @@
     units, after = pl.pallas_call(
         away_kernel,
         out_shape=(
-            pltpu.VMEM((n_req, 2, UNIT_ROWS, VECS), jnp.bfloat16),
+            pltpu.HBM((n_req, 2, UNIT_ROWS, VECS), jnp.bfloat16),
             pltpu.VMEM((8, VECS), jnp.float32),
         ),
-        in_specs=[vmem] * (3 + len(sent)),
-        out_specs=(vmem,) * 2,
+        in_specs=[vmem] * (4 + len(sent)),
+        out_specs=(hbm, vmem),
+        scratch_shapes=[
+            pltpu.VMEM((n_req - 1, 2, UNIT_ROWS, VECS), jnp.bfloat16),
+            pltpu.SemaphoreType.DMA((n_req - 1, 2)),
+        ],
         compiler_params=params,
         name="suffix_away",
-    )(keys, values, member, *sent.values())
+    )(keys, values, member, *sent, other)
     units = units.reshape(2 * n_req, UNIT_ROWS, VECS)
     units = lax.all_to_all(units, ("z", "pair"), split_axis=0, concat_axis=0, tiled=True)
 

time: 33.6 us -> 30.9 us (0.920)
  starting transfers between devices: 20 us -> 16.2 us
  waiting for transfers between devices: 4.48 us -> 5.6 us
    ppermute x9, starting transfers between devices: 16.1 us -> 12.1 us  [swapped(): return lax.ppermute(value, axis, [(i, i ^ mask) for i in range(size)])]
    ppermute x9, waiting for transfers between devices: 4.48 us -> 5.6 us  [swapped(): return lax.ppermute(value, axis, [(i, i ^ mask) for i in range(size)])]
  transfers between devices with their start and end apart: 10 -> 10, of which waited for: 3 -> 3; matrix products, arithmetic and copies ran while one was open for 0% -> 0% of each run, Pallas kernels for 18% -> 19%
where the time goes in v11:
time: 30.9 us; the launch traced here: 30.7 us
  starting transfers between devices  16.2 us (52%)
  Pallas kernels  8.16 us (26%)
  waiting for transfers between devices  5.6 us (18%)
  between operations  0.71 us (2%)
    ppermute x9, starting transfers between devices, swapped(): return lax.ppermute(value, axis, [(i, i ^ mask) for i in range(size)])  12.1 us
    ppermute x9, waiting for transfers between devices, swapped(): return lax.ppermute(value, axis, [(i, i ^ mask) for i in range(size)])  5.6 us
    all_to_all x1, starting transfers between devices, on_device(): lax.all_to_all(units, ('z', 'pair'), split_axis=0, concat_axis=0, tiled=T...  4.11 us
    pallas_call x1, Pallas kernels, on_device(): pl.pallas_call(functools.partial(home_kernel, half), out_shape=(pltpu.VME...  3.88 us
    pallas_call x1, Pallas kernels, on_device(): pl.pallas_call(functools.partial(prepare_kernel, capacity), out_shape=(pl...  1.99 us
    pallas_call x1, Pallas kernels, on_device(): pl.pallas_call(away_kernel, out_shape=(pltpu.HBM((n_req, 2, UNIT_ROWS, VE...  1.51 us
    pallas_call x1, Pallas kernels, on_device(): pl.pallas_call(final_kernel, out_shape=jax.ShapeDtypeStruct((BEAMS, HEADS...  0.78 us
  transfers between devices with their start and end apart: 10, of which 3 were waited for; matrix products, arithmetic and copies ran while one was open for 0% of the time, Pallas kernels for 19%

profile of v11, /device:TPU:0, one launch (start us, length us, event | category | flops | bytes accessed | tf_op | source)
XLA Modules:
  0.0 30.7 jit_solution(14109767808712007897)
XLA Ops:
  0.0 0.5 %collective-permute-start = (bf16[32,64,256]{2,1,0:T(8,128)(2,1)}, bf16[32,64,256]{2,1,0:T(8,128)(2,1)S(1)}, u32[]{:S(2)}, u32[]{:S(2)}) collective-permute-start(bf16[32,64,256]{2,1,0:T(8,128)(2,1)} %bitcast.8), channel_id=1, source_target_pairs={{0,4},{4,0},{1,5},{5,1},{2,6},{6,2},{3,7},{7,3},{8,12},{12,8},{9,1... | collective-permute-start | bytes 3145736 | tf_op jit(solution)/shard_map/ppermute | solution.py:26
  0.5 3.6 %collective-permute-start.1 = (bf16[16,1024]{1,0:T(8,128)(2,1)}, bf16[16,1024]{1,0:T(8,128)(2,1)S(1)}, u32[]{:S(2)}, u32[]{:S(2)}) collective-permute-start(bf16[16,1024]{1,0:T(8,128)(2,1)} %own_ref.1), channel_id=1, source_target_pairs={{0,16},{8,24},{16,0},{24,8},{1,17},{9,25},{17,1},{25,9},{2,18},{10... | collective-permute-start | bytes 98312 | tf_op jit(solution)/shard_map/ppermute | solution.py:26
  4.0 1.3 %collective-permute-start.3 = (bf16[16,1024]{1,0:T(8,128)(2,1)}, bf16[16,1024]{1,0:T(8,128)(2,1)S(1)}, u32[]{:S(2)}, u32[]{:S(2)}) collective-permute-start(bf16[16,1024]{1,0:T(8,128)(2,1)} %own_ref.1), channel_id=1, source_target_pairs={{0,24},{8,16},{16,8},{24,0},{1,25},{9,17},{17,9},{25,1},{2,26},{10... | collective-permute-start | bytes 98312 | tf_op jit(solution)/shard_map/ppermute | solution.py:26
  5.4 0.2 collective-permute-start.5
  5.6 1.5 %collective-permute-start.7 = (bf16[16,1024]{1,0:T(8,128)(2,1)}, bf16[16,1024]{1,0:T(8,128)(2,1)S(1)}, u32[]{:S(2)}, u32[]{:S(2)}) collective-permute-start(bf16[16,1024]{1,0:T(8,128)(2,1)} %own_ref.1), channel_id=1, source_target_pairs={{0,1},{1,0},{2,3},{3,2},{4,5},{5,4},{6,7},{7,6},{8,9},{9,8},{10,11... | collective-permute-start | bytes 98312 | tf_op jit(solution)/shard_map/ppermute | solution.py:26
  7.1 0.0 collective-permute-done.1.rest_0_
  7.1 0.9 %collective-permute-start.2 = (bf16[16,1024]{1,0:T(8,128)(2,1)S(1)}, bf16[16,1024]{1,0:T(8,128)(2,1)S(1)}, u32[]{:S(2)}, u32[]{:S(2)}) collective-permute-start(bf16[16,1024]{1,0:T(8,128)(2,1)S(1)} %collective-permute-done.1.rest_0_), channel_id=1, source_target_pairs={{0,1},{1,0},{2,3},{3,2},{4,5},{5,4},{6,7},{7,6},{8,9},{9,8},{10,11... | collective-permute-start | bytes 98312 | tf_op jit(solution)/shard_map/ppermute | solution.py:26
  8.0 2.0 %collective-permute-done.3.rest_2_ = bf16[16,1024]{1,0:T(8,128)(2,1)S(1)} collective-permute-done((bf16[16,1024]{1,0:T(8,128)(2,1)}, bf16[16,1024]{1,0:T(8,128)(2,1)S(1)}, u32[]{:S(2)}, u32[]{:S(2)}) %collective-permute-start.3) | collective-permute-done | bytes 32800 | tf_op jit(solution)/shard_map/ppermute | solution.py:26
  10.0 1.5 %collective-permute-start.4 = (bf16[16,1024]{1,0:T(8,128)(2,1)S(1)}, bf16[16,1024]{1,0:T(8,128)(2,1)S(1)}, u32[]{:S(2)}, u32[]{:S(2)}) collective-permute-start(bf16[16,1024]{1,0:T(8,128)(2,1)S(1)} %collective-permute-done.3.rest_2_), channel_id=1, source_target_pairs={{0,1},{1,0},{2,3},{3,2},{4,5},{5,4},{6,7},{7,6},{8,9},{9,8},{10,11... | collective-permute-start | bytes 98312 | tf_op jit(solution)/shard_map/ppermute | solution.py:26
  11.5 0.0 collective-permute-done.5.rest_4_
  11.5 0.5 %collective-permute-start.6 = (bf16[16,1024]{1,0:T(8,128)(2,1)S(1)}, bf16[16,1024]{1,0:T(8,128)(2,1)S(1)}, u32[]{:S(2)}, u32[]{:S(2)}) collective-permute-start(bf16[16,1024]{1,0:T(8,128)(2,1)S(1)} %collective-permute-done.5.rest_4_), channel_id=1, source_target_pairs={{0,1},{1,0},{2,3},{3,2},{4,5},{5,4},{6,7},{7,6},{8,9},{9,8},{10,11... | collective-permute-start | bytes 98312 | tf_op jit(solution)/shard_map/ppermute | solution.py:26
  12.1 0.0 collective-permute-done.far_ref
  12.1 2.0 %prepare.1 = (bf16[1,512,128]{2,1,0:T(8,128)(2,1)S(1)}, bf16[1,128,512]{2,1,0:T(8,128)(2,1)S(1)}, bf16[3,512,128]{2,1,0:T(8,128)(2,1)S(1)}, bf16[3,128,512]{2,1,...) custom-call(s32[4,128]{1,0:T(4,128)} %bitcast.11, ...), custom_call_target="tpu_custom_call" | custom-call | tf_op jit(solution)/shard_map/prepare/pallas_call | solution.py:303
  14.1 0.0 collective-permute-done.7.rest_6_.pair_ref
  14.1 0.0 collective-permute-done.2.rest_1_
  14.1 0.0 collective-permute-done.4.rest_3_
  14.1 1.3 %collective-permute-done.6.rest_5_ = bf16[16,1024]{1,0:T(8,128)(2,1)S(1)} collective-permute-done((bf16[16,1024]{1,0:T(8,128)(2,1)S(1)}, bf16[16,1024]{1,0:T(8,128)(2,1)S(1)}, u32[]{:S(2)}, u32[]{:S(2)}) %collective-permute-start.6) | collective-permute-done | bytes 32800 | tf_op jit(solution)/shard_map/ppermute | solution.py:26
  15.4 1.5 %suffix_away.1 = (bf16[4,2,144,128]{3,2,1,0:T(8,128)(2,1)}, f32[8,128]{1,0:T(8,128)S(1)}) custom-call(bf16[3,512,128]{2,1,0:T(8,128)(2,1)S(1)} %get-tuple-element.17.keys_ref, bf16[3,128,512]{2,1,0:T(8,128)(2,1)S(1)} %get-tuple-element.18.values_ref, f32[4,8,256]{2,1,0:T(8,128)S(1)} %get-tuple-element.19.member_ref, ...), custom_call_target="tpu_custom_call" | custom-call | tf_op jit(solution)/shard_map/suffix_away/pallas_call | solution.py:334
  16.9 4.1 %all-to-all-start = ((bf16[8,144,128]{2,1,0:T(8,128)(2,1)}), bf16[8,144,128]{2,1,0:T(8,128)(2,1)S(1)}, u32[]{:S(2)}, u32[]{:S(2)}) async-start(bf16[8,144,128]{2,1,0:T(8,128)(2,1)} %bitcast.10), calls=%async_computation | async-start | bytes 589824 | tf_op jit(solution)/shard_map/all_to_all | solution.py:350
  21.7 3.9 %home_part.1 = (f32[128,128]{1,0:T(8,128)S(1)}, f32[8,128]{1,0:T(8,128)S(1)}, bf16[144,128]{1,0:T(8,128)(2,1)S(1)}) custom-call(s32[1]{0:T(128)S(6)} %copy.7.length_ref, bf16[1,512,128]{2,1,0:T(8,128)(2,1)S(1)} %get-tuple-element.21.keys_ref, bf16[1,128,512]{2,1,0:T(8,128)(2,1)S(1)} %get-tuple-element.22.values_ref, ...), custom_call_target="tpu_custom_call" | custom-call | flops 536870912 | bytes 2097152 | tf_op jit(solution)/shard_map/home_part/pallas_call | solution.py:352
  25.6 2.1 %collective-permute-start.8 = (bf16[144,128]{1,0:T(8,128)(2,1)S(1)}, bf16[144,128]{1,0:T(8,128)(2,1)S(1)}, u32[]{:S(2)}, u32[]{:S(2)}) collective-permute-start(bf16[144,128]{1,0:T(8,128)(2,1)S(1)} %get-tuple-element.26), channel_id=1, source_target_pairs={{0,1},{1,0},{2,3},{3,2},{4,5},{5,4},{6,7},{7,6},{8,9},{9,8},{10,11... | collective-permute-start | bytes 110600 | tf_op jit(solution)/shard_map/ppermute | solution.py:26
  27.7 2.2 %collective-permute-done.8.last_ref = bf16[144,128]{1,0:T(8,128)(2,1)S(1)} collective-permute-done((bf16[144,128]{1,0:T(8,128)(2,1)S(1)}, bf16[144,128]{1,0:T(8,128)(2,1)S(1)}, u32[]{:S(2)}, u32[]{:S(2)}) %collective-permute-start.8) | collective-permute-done | bytes 36896 | tf_op jit(solution)/shard_map/ppermute | solution.py:26
  29.9 0.0 all-to-all-done
  29.9 0.8 %combine.1 = f32[16,1024]{1,0:T(8,128)} custom-call(bf16[4,2,144,128]{3,2,1,0:T(8,128)(2,1)S(1)} %bitcast.6, bf16[144,128]{1,0:T(8,128)(2,1)S(1)} %collective-permute-done.8.last_ref, f32[128,128]{1,0:T(8,128)S(1)} %get-tuple-element.27.summed_ref, f32[8,128]{1,0:T(8,128)S(1)} %get-tuple-element.28.stats_ref), custom_call_target="tpu_custom_call" | custom-call | tf_op jit(solution)/shard_map/combine/pallas_call | solution.py:369
Async XLA Ops:
  0.0 12.1 %collective-permute-start = (bf16[32,64,256]{2,1,0:T(8,128)(2,1)}, bf16[32,64,256]{2,1,0:T(8,128)(2,1)S(1)}, u32[]{:S(2)}, u32[]{:S(2)}) collective-permute-start(bf16[32,64,256]{2,1,0:T(8,128)(2,1)} %bitcast.8), channel_id=1, source_target_pairs={{0,4},{4,0},{1,5},{5,1},{2,6},{6,2},{3,7},{7,3},{8,12},{12,8},{9,1... | collective-permute-start | bytes 3145736 | tf_op jit(solution)/shard_map/ppermute | solution.py:26
  0.5 6.7 %collective-permute-start.1 = (bf16[16,1024]{1,0:T(8,128)(2,1)}, bf16[16,1024]{1,0:T(8,128)(2,1)S(1)}, u32[]{:S(2)}, u32[]{:S(2)}) collective-permute-start(bf16[16,1024]{1,0:T(8,128)(2,1)} %own_ref.1), channel_id=1, source_target_pairs={{0,16},{8,24},{16,0},{24,8},{1,17},{9,25},{17,1},{25,9},{2,18},{10... | collective-permute-start | bytes 98312 | tf_op jit(solution)/shard_map/ppermute | solution.py:26
  4.0 6.0 %collective-permute-start.3 = (bf16[16,1024]{1,0:T(8,128)(2,1)}, bf16[16,1024]{1,0:T(8,128)(2,1)S(1)}, u32[]{:S(2)}, u32[]{:S(2)}) collective-permute-start(bf16[16,1024]{1,0:T(8,128)(2,1)} %own_ref.1), channel_id=1, source_target_pairs={{0,24},{8,16},{16,8},{24,0},{1,25},{9,17},{17,9},{25,1},{2,26},{10... | collective-permute-start | bytes 98312 | tf_op jit(solution)/shard_map/ppermute | solution.py:26
  5.4 6.1 %collective-permute-start.5 = (bf16[16,1024]{1,0:T(8,128)(2,1)}, bf16[16,1024]{1,0:T(8,128)(2,1)S(1)}, u32[]{:S(2)}, u32[]{:S(2)}) collective-permute-start(bf16[16,1024]{1,0:T(8,128)(2,1)} %own_ref.1), channel_id=1, source_target_pairs={{0,8},{8,0},{16,24},{24,16},{1,9},{9,1},{17,25},{25,17},{2,10},{10... | collective-permute-start | bytes 98312 | tf_op jit(solution)/shard_map/ppermute | solution.py:26
  5.6 8.4 %collective-permute-start.7 = (bf16[16,1024]{1,0:T(8,128)(2,1)}, bf16[16,1024]{1,0:T(8,128)(2,1)S(1)}, u32[]{:S(2)}, u32[]{:S(2)}) collective-permute-start(bf16[16,1024]{1,0:T(8,128)(2,1)} %own_ref.1), channel_id=1, source_target_pairs={{0,1},{1,0},{2,3},{3,2},{4,5},{5,4},{6,7},{7,6},{8,9},{9,8},{10,11... | collective-permute-start | bytes 98312 | tf_op jit(solution)/shard_map/ppermute | solution.py:26
  7.1 7.0 %collective-permute-start.2 = (bf16[16,1024]{1,0:T(8,128)(2,1)S(1)}, bf16[16,1024]{1,0:T(8,128)(2,1)S(1)}, u32[]{:S(2)}, u32[]{:S(2)}) collective-permute-start(bf16[16,1024]{1,0:T(8,128)(2,1)S(1)} %collective-permute-done.1.rest_0_), channel_id=1, source_target_pairs={{0,1},{1,0},{2,3},{3,2},{4,5},{5,4},{6,7},{7,6},{8,9},{9,8},{10,11... | collective-permute-start | bytes 98312 | tf_op jit(solution)/shard_map/ppermute | solution.py:26
  10.0 4.1 %collective-permute-start.4 = (bf16[16,1024]{1,0:T(8,128)(2,1)S(1)}, bf16[16,1024]{1,0:T(8,128)(2,1)S(1)}, u32[]{:S(2)}, u32[]{:S(2)}) collective-permute-start(bf16[16,1024]{1,0:T(8,128)(2,1)S(1)} %collective-permute-done.3.rest_2_), channel_id=1, source_target_pairs={{0,1},{1,0},{2,3},{3,2},{4,5},{5,4},{6,7},{7,6},{8,9},{9,8},{10,11... | collective-permute-start | bytes 98312 | tf_op jit(solution)/shard_map/ppermute | solution.py:26
  11.5 3.9 %collective-permute-start.6 = (bf16[16,1024]{1,0:T(8,128)(2,1)S(1)}, bf16[16,1024]{1,0:T(8,128)(2,1)S(1)}, u32[]{:S(2)}, u32[]{:S(2)}) collective-permute-start(bf16[16,1024]{1,0:T(8,128)(2,1)S(1)} %collective-permute-done.5.rest_4_), channel_id=1, source_target_pairs={{0,1},{1,0},{2,3},{3,2},{4,5},{5,4},{6,7},{7,6},{8,9},{9,8},{10,11... | collective-permute-start | bytes 98312 | tf_op jit(solution)/shard_map/ppermute | solution.py:26
  16.9 13.0 %all-to-all-start = ((bf16[8,144,128]{2,1,0:T(8,128)(2,1)}), bf16[8,144,128]{2,1,0:T(8,128)(2,1)S(1)}, u32[]{:S(2)}, u32[]{:S(2)}) async-start(bf16[8,144,128]{2,1,0:T(8,128)(2,1)} %bitcast.10), calls=%async_computation | async-start | bytes 589824 | tf_op jit(solution)/shard_map/all_to_all | solution.py:350
  25.6 4.3 %collective-permute-start.8 = (bf16[144,128]{1,0:T(8,128)(2,1)S(1)}, bf16[144,128]{1,0:T(8,128)(2,1)S(1)}, u32[]{:S(2)}, u32[]{:S(2)}) collective-permute-start(bf16[144,128]{1,0:T(8,128)(2,1)S(1)} %get-tuple-element.26), channel_id=1, source_target_pairs={{0,1},{1,0},{2,3},{3,2},{4,5},{5,4},{6,7},{7,6},{8,9},{9,8},{10,11... | collective-permute-start | bytes 110600 | tf_op jit(solution)/shard_map/ppermute | solution.py:26

commit v12 on v11

--- a/solution.py
+++ b/solution.py
@@ -98,26 +98,28 @@
     return lax.broadcasted_iota(jnp.int32, shape, axis)
 
 
-def prompt_part(length, half, prompt_ref, vectors):
-    parity = lax.axis_index("pair")
-    whole = lax.div(length, 2 * half)
-    valid = whole * half + jnp.clip(length - whole * (2 * half) - parity * half, 0, half)
-    parts = []
-    for start in range(0, prompt_ref.shape[0], CHUNK):
-        part = slice(start, start + CHUNK)
-        scores = scores_of(prompt_ref[part, :HD], vectors)
-        token = iota(scores.shape, 0)
-        scores = jnp.where(token < valid - start, scores, big_negative)
-        top, total, weights = weighted(scores)
-        parts.append((top, total, summed_of(prompt_ref[part, HD:], weights)))
-        if len(parts) == 2:
-            parts = [merged(parts)]
-    return merged(parts)
+def prompt_part(valid, prompt_ref, vectors):
+    chunks = [slice(i, i + CHUNK) for i in range(0, prompt_ref.shape[0], CHUNK)]
+    scores = [scores_of(prompt_ref[chunk, :HD], vectors) for chunk in chunks]
+    place = iota(scores[0].shape, 0)
+    scores = [
+        jnp.where(place < valid - chunk.start, score, big_negative)
+        for chunk, score in zip(chunks, scores)
+    ]
+    tops = [jnp.max(score, axis=0, keepdims=True) for score in scores]
+    top = functools.reduce(jnp.maximum, tops)
+    total, summed = 0.0, 0.0
+    for chunk, score in zip(chunks, scores):
+        weights = jnp.exp2((score - top) * to_exp2)
+        total = total + jnp.sum(weights, axis=0, keepdims=True)
+        summed = summed + summed_of(prompt_ref[chunk, HD:], weights)
+    return top, total, summed
 
 
 def prepare_kernel(
-    capacity, table_ref, parents_ref, near_ref, prompt_ref, own_ref, far_ref,
-    home_keys_ref, home_values_ref, keys_ref, values_ref, member_ref, held_ref, own, rows_ref, table, parents, near, sems,
+    capacity, length_ref, table_ref, parents_ref, near_ref, prompt_ref, own_ref, far_ref,
+    home_keys_ref, home_values_ref, keys_ref, values_ref, member_ref, held_ref, own, valid_ref,
+    rows_ref, table, parents, near, sems,
 ):
     n_req = keys_ref.shape[0] + 1
     slots, half, _ = near.shape
@@ -139,6 +141,12 @@
     ]
     for copy in small:
         copy.start()
+
+    length = length_ref[0]
+    whole = lax.div(length, 2 * half)
+    parity = lax.axis_index("pair")
+    valid = whole * half + jnp.clip(length - whole * (2 * half) - parity * half, 0, half)
+    valid_ref[...] = jnp.full(valid_ref.shape, valid, jnp.int32)
 
     small[0].wait()
     slot = iota((2 * slots, rows), 0)
@@ -253,12 +261,12 @@
 
 
 def home_kernel(
-    half, length_ref, keys_ref, values_ref, member_ref, own_ref, pair_ref, prompt_ref, after_ref,
+    valid_ref, keys_ref, values_ref, member_ref, own_ref, pair_ref, prompt_ref, after_ref,
     summed_ref, stats_ref, out_ref,
 ):
     vectors = all_vectors(own_ref, pair_ref)
     (suffix,) = suffix_parts([vectors], keys_ref, values_ref, [member_ref[0]], [0])
-    prompt = prompt_part(length_ref[0], half, prompt_ref, vectors)
+    prompt = prompt_part(valid_ref[0:1, :], prompt_ref, vectors)
     part = merged([prompt, suffix])
     top, total, summed_ref[...] = half_of(part, 0)
     stats_ref[...] = jnp.concatenate([top, total, jnp.zeros((6, VECS), jnp.float32)], axis=0)
@@ -300,7 +308,7 @@
         sent += [piece, swapped(piece, "pair")]
     other = swapped(queries, "pair")
 
-    home_keys, home_values, keys, values, member, prompt, own = pl.pallas_call(
+    home_keys, home_values, keys, values, member, prompt, own, valid = pl.pallas_call(
         functools.partial(prepare_kernel, capacity),
         out_shape=(
             pltpu.VMEM((1, 2 * capacity * half, HD), jnp.bfloat16),
@@ -310,9 +318,10 @@
             pltpu.VMEM((n_req, 2 * capacity, 2 * VECS), jnp.float32),
             pltpu.VMEM((tokens, width), jnp.bfloat16),
             pltpu.VMEM(queries.shape, jnp.bfloat16),
+            pltpu.VMEM((8, 2 * VECS), jnp.int32),
         ),
-        in_specs=[hbm] * 5 + [vmem],
-        out_specs=(vmem,) * 7,
+        in_specs=[pl.BlockSpec(memory_space=pltpu.SMEM)] + [hbm] * 5 + [vmem],
+        out_specs=(vmem,) * 8,
         scratch_shapes=[
             pltpu.VMEM((2 * slots + 8, 2 * VECS), jnp.float32),
             pltpu.VMEM((SUF, rows), jnp.int32),
@@ -323,6 +332,7 @@
         compiler_params=params,
         name="prepare",
     )(
+        lengths,
         in_hbm(block_table.T),
         in_hbm(parents.reshape(1, rows)),
         in_hbm(near),
@@ -350,20 +360,20 @@
     units = lax.all_to_all(units, ("z", "pair"), split_axis=0, concat_axis=0, tiled=True)
 
     summed, stats, given = pl.pallas_call(
-        functools.partial(home_kernel, half),
+        home_kernel,
         out_shape=(
             pltpu.VMEM((HD, VECS), jnp.float32),
             pltpu.VMEM((8, VECS), jnp.float32),
             pltpu.VMEM((UNIT_ROWS, VECS), jnp.bfloat16),
         ),
-        in_specs=[pl.BlockSpec(memory_space=pltpu.SMEM)] + [vmem] * 7,
+        in_specs=[vmem] * 8,
         out_specs=(vmem,) * 3,
         compiler_params=params,
         cost_estimate=pl.CostEstimate(
             flops=8 * tokens * VECS * HD, bytes_accessed=2 * tokens * width, transcendentals=0
         ),
         name="home_part",
-    )(lengths, home_keys, home_values, member, own, other, prompt, after)
+    )(valid, home_keys, home_values, member, own, other, prompt, after)
     last = swapped(given, "pair")
 
     return pl.pallas_call(

time: 30.9 us -> 30.5 us (0.987)
  Pallas kernels: 8.16 us -> 6.76 us
  waiting for transfers between devices: 5.6 us -> 6.6 us
    pallas_call x1, Pallas kernels: 3.88 us -> 2.47 us  [on_device(): pl.pallas_call(home_kernel, out_shape=(pltpu.VMEM((HD, VECS), jnp.float32...]
    all_to_all x1, waiting for transfers between devices: 0.01 us -> 1.33 us  [on_device(): lax.all_to_all(units, ('z', 'pair'), split_axis=0, concat_axis=0, tiled=T...]
    ppermute x9, waiting for transfers between devices: 5.6 us -> 5.27 us  [swapped(): return lax.ppermute(value, axis, [(i, i ^ mask) for i in range(size)])]
  transfers between devices with their start and end apart: 10 -> 10, of which waited for: 3 -> 4; matrix products, arithmetic and copies ran while one was open for 0% -> 0% of each run, Pallas kernels for 19% -> 15%
where the time goes in v12:
time: 30.5 us; the launch traced here: 30.3 us
  starting transfers between devices  16.2 us (53%)
  Pallas kernels  6.76 us (22%)
  waiting for transfers between devices  6.6 us (22%)
  between operations  0.72 us (2%)
    ppermute x9, starting transfers between devices, swapped(): return lax.ppermute(value, axis, [(i, i ^ mask) for i in range(size)])  12.1 us
    ppermute x9, waiting for transfers between devices, swapped(): return lax.ppermute(value, axis, [(i, i ^ mask) for i in range(size)])  5.27 us
    all_to_all x1, starting transfers between devices, on_device(): lax.all_to_all(units, ('z', 'pair'), split_axis=0, concat_axis=0, tiled=T...  4.11 us
    pallas_call x1, Pallas kernels, on_device(): pl.pallas_call(home_kernel, out_shape=(pltpu.VMEM((HD, VECS), jnp.float32...  2.47 us
    pallas_call x1, Pallas kernels, on_device(): pl.pallas_call(functools.partial(prepare_kernel, capacity), out_shape=(pl...  1.99 us
    pallas_call x1, Pallas kernels, on_device(): pl.pallas_call(away_kernel, out_shape=(pltpu.HBM((n_req, 2, UNIT_ROWS, VE...  1.51 us
    all_to_all x1, waiting for transfers between devices, on_device(): lax.all_to_all(units, ('z', 'pair'), split_axis=0, concat_axis=0, tiled=T...  1.33 us
    pallas_call x1, Pallas kernels, on_device(): pl.pallas_call(final_kernel, out_shape=jax.ShapeDtypeStruct((BEAMS, HEADS...  0.78 us
  transfers between devices with their start and end apart: 10, of which 4 were waited for; matrix products, arithmetic and copies ran while one was open for 0% of the time, Pallas kernels for 15%

profile of v12, /device:TPU:0, one launch (start us, length us, event | category | flops | bytes accessed | tf_op | source)
XLA Modules:
  0.0 30.3 jit_solution(11988891896549596923)
XLA Ops:
  0.0 0.5 %collective-permute-start = (bf16[32,64,256]{2,1,0:T(8,128)(2,1)}, bf16[32,64,256]{2,1,0:T(8,128)(2,1)S(1)}, u32[]{:S(2)}, u32[]{:S(2)}) collective-permute-start(bf16[32,64,256]{2,1,0:T(8,128)(2,1)} %bitcast.8), channel_id=1, source_target_pairs={{0,4},{4,0},{1,5},{5,1},{2,6},{6,2},{3,7},{7,3},{8,12},{12,8},{9,1... | collective-permute-start | bytes 3145736 | tf_op jit(solution)/shard_map/ppermute | solution.py:26
  0.5 3.6 %collective-permute-start.1 = (bf16[16,1024]{1,0:T(8,128)(2,1)}, bf16[16,1024]{1,0:T(8,128)(2,1)S(1)}, u32[]{:S(2)}, u32[]{:S(2)}) collective-permute-start(bf16[16,1024]{1,0:T(8,128)(2,1)} %own_ref.1), channel_id=1, source_target_pairs={{0,16},{8,24},{16,0},{24,8},{1,17},{9,25},{17,1},{25,9},{2,18},{10... | collective-permute-start | bytes 98312 | tf_op jit(solution)/shard_map/ppermute | solution.py:26
  4.0 1.3 %collective-permute-start.3 = (bf16[16,1024]{1,0:T(8,128)(2,1)}, bf16[16,1024]{1,0:T(8,128)(2,1)S(1)}, u32[]{:S(2)}, u32[]{:S(2)}) collective-permute-start(bf16[16,1024]{1,0:T(8,128)(2,1)} %own_ref.1), channel_id=1, source_target_pairs={{0,24},{8,16},{16,8},{24,0},{1,25},{9,17},{17,9},{25,1},{2,26},{10... | collective-permute-start | bytes 98312 | tf_op jit(solution)/shard_map/ppermute | solution.py:26
  5.4 0.2 collective-permute-start.5
  5.6 1.5 %collective-permute-start.7 = (bf16[16,1024]{1,0:T(8,128)(2,1)}, bf16[16,1024]{1,0:T(8,128)(2,1)S(1)}, u32[]{:S(2)}, u32[]{:S(2)}) collective-permute-start(bf16[16,1024]{1,0:T(8,128)(2,1)} %own_ref.1), channel_id=1, source_target_pairs={{0,1},{1,0},{2,3},{3,2},{4,5},{5,4},{6,7},{7,6},{8,9},{9,8},{10,11... | collective-permute-start | bytes 98312 | tf_op jit(solution)/shard_map/ppermute | solution.py:26
  7.1 0.0 collective-permute-done.1.rest_0_
  7.1 0.9 %collective-permute-start.2 = (bf16[16,1024]{1,0:T(8,128)(2,1)S(1)}, bf16[16,1024]{1,0:T(8,128)(2,1)S(1)}, u32[]{:S(2)}, u32[]{:S(2)}) collective-permute-start(bf16[16,1024]{1,0:T(8,128)(2,1)S(1)} %collective-permute-done.1.rest_0_), channel_id=1, source_target_pairs={{0,1},{1,0},{2,3},{3,2},{4,5},{5,4},{6,7},{7,6},{8,9},{9,8},{10,11... | collective-permute-start | bytes 98312 | tf_op jit(solution)/shard_map/ppermute | solution.py:26
  8.0 2.0 %collective-permute-done.3.rest_2_ = bf16[16,1024]{1,0:T(8,128)(2,1)S(1)} collective-permute-done((bf16[16,1024]{1,0:T(8,128)(2,1)}, bf16[16,1024]{1,0:T(8,128)(2,1)S(1)}, u32[]{:S(2)}, u32[]{:S(2)}) %collective-permute-start.3) | collective-permute-done | bytes 32800 | tf_op jit(solution)/shard_map/ppermute | solution.py:26
  10.0 1.5 %collective-permute-start.4 = (bf16[16,1024]{1,0:T(8,128)(2,1)S(1)}, bf16[16,1024]{1,0:T(8,128)(2,1)S(1)}, u32[]{:S(2)}, u32[]{:S(2)}) collective-permute-start(bf16[16,1024]{1,0:T(8,128)(2,1)S(1)} %collective-permute-done.3.rest_2_), channel_id=1, source_target_pairs={{0,1},{1,0},{2,3},{3,2},{4,5},{5,4},{6,7},{7,6},{8,9},{9,8},{10,11... | collective-permute-start | bytes 98312 | tf_op jit(solution)/shard_map/ppermute | solution.py:26
  11.5 0.0 collective-permute-done.5.rest_4_
  11.5 0.5 %collective-permute-start.6 = (bf16[16,1024]{1,0:T(8,128)(2,1)S(1)}, bf16[16,1024]{1,0:T(8,128)(2,1)S(1)}, u32[]{:S(2)}, u32[]{:S(2)}) collective-permute-start(bf16[16,1024]{1,0:T(8,128)(2,1)S(1)} %collective-permute-done.5.rest_4_), channel_id=1, source_target_pairs={{0,1},{1,0},{2,3},{3,2},{4,5},{5,4},{6,7},{7,6},{8,9},{9,8},{10,11... | collective-permute-start | bytes 98312 | tf_op jit(solution)/shard_map/ppermute | solution.py:26
  12.7 0.0 collective-permute-done.far_ref
  12.7 2.0 %prepare.1 = (bf16[1,512,128]{2,1,0:T(8,128)(2,1)S(1)}, bf16[1,128,512]{2,1,0:T(8,128)(2,1)S(1)}, bf16[3,512,128]{2,1,0:T(8,128)(2,1)S(1)}, bf16[3,128,512]{2,1,...) custom-call(s32[1]{0:T(128)S(6)} %copy.7.length_ref, ...), custom_call_target="tpu_custom_call" | custom-call | tf_op jit(solution)/shard_map/prepare/pallas_call | solution.py:311
  14.7 0.0 collective-permute-done.7.rest_6_.pair_ref
  14.7 0.0 collective-permute-done.2.rest_1_
  14.7 0.0 collective-permute-done.4.rest_3_
  14.7 0.7 %collective-permute-done.6.rest_5_ = bf16[16,1024]{1,0:T(8,128)(2,1)S(1)} collective-permute-done((bf16[16,1024]{1,0:T(8,128)(2,1)S(1)}, bf16[16,1024]{1,0:T(8,128)(2,1)S(1)}, u32[]{:S(2)}, u32[]{:S(2)}) %collective-permute-start.6) | collective-permute-done | bytes 32800 | tf_op jit(solution)/shard_map/ppermute | solution.py:26
  15.4 1.5 %suffix_away.1 = (bf16[4,2,144,128]{3,2,1,0:T(8,128)(2,1)}, f32[8,128]{1,0:T(8,128)S(1)}) custom-call(bf16[3,512,128]{2,1,0:T(8,128)(2,1)S(1)} %get-tuple-element.18.keys_ref, bf16[3,128,512]{2,1,0:T(8,128)(2,1)S(1)} %get-tuple-element.19.values_ref, f32[4,8,256]{2,1,0:T(8,128)S(1)} %get-tuple-element.20.member_ref, ...), custom_call_target="tpu_custom_call" | custom-call | tf_op jit(solution)/shard_map/suffix_away/pallas_call | solution.py:344
  16.9 4.1 %all-to-all-start = ((bf16[8,144,128]{2,1,0:T(8,128)(2,1)}), bf16[8,144,128]{2,1,0:T(8,128)(2,1)S(1)}, u32[]{:S(2)}, u32[]{:S(2)}) async-start(bf16[8,144,128]{2,1,0:T(8,128)(2,1)} %bitcast.10), calls=%async_computation | async-start | bytes 589824 | tf_op jit(solution)/shard_map/all_to_all | solution.py:360
  21.0 2.5 %home_part.1 = (f32[128,128]{1,0:T(8,128)S(1)}, f32[8,128]{1,0:T(8,128)S(1)}, bf16[144,128]{1,0:T(8,128)(2,1)S(1)}) custom-call(s32[8,256]{1,0:T(8,128)S(1)} %get-tuple-element.22.valid_ref, bf16[1,512,128]{2,1,0:T(8,128)(2,1)S(1)} %get-tuple-element.23.keys_ref, bf16[1,128,512]{2,1,0:T(8,128)(2,1)S(1)} %get-tuple-element.24.values_ref, ...), custom_call_target="tpu_custom_call" | custom-call | flops 536870912 | bytes 2097152 | tf_op jit(solution)/shard_map/home_part/pallas_call | solution.py:362
  23.5 2.1 %collective-permute-start.8 = (bf16[144,128]{1,0:T(8,128)(2,1)S(1)}, bf16[144,128]{1,0:T(8,128)(2,1)S(1)}, u32[]{:S(2)}, u32[]{:S(2)}) collective-permute-start(bf16[144,128]{1,0:T(8,128)(2,1)S(1)} %get-tuple-element.28), channel_id=1, source_target_pairs={{0,1},{1,0},{2,3},{3,2},{4,5},{5,4},{6,7},{7,6},{8,9},{9,8},{10,11... | collective-permute-start | bytes 110600 | tf_op jit(solution)/shard_map/ppermute | solution.py:26
  25.6 2.5 %collective-permute-done.8.last_ref = bf16[144,128]{1,0:T(8,128)(2,1)S(1)} collective-permute-done((bf16[144,128]{1,0:T(8,128)(2,1)S(1)}, bf16[144,128]{1,0:T(8,128)(2,1)S(1)}, u32[]{:S(2)}, u32[]{:S(2)}) %collective-permute-start.8) | collective-permute-done | bytes 36896 | tf_op jit(solution)/shard_map/ppermute | solution.py:26
  28.2 1.3 %all-to-all-done = bf16[8,144,128]{2,1,0:T(8,128)(2,1)S(1)} async-done(((bf16[8,144,128]{2,1,0:T(8,128)(2,1)}), bf16[8,144,128]{2,1,0:T(8,128)(2,1)S(1)}, u32[]{:S(2)}, u32[]{:S(2)}) %all-to-all-start) | async-done | bytes 294944 | tf_op jit(solution)/shard_map/all_to_all | solution.py:360
  29.5 0.8 %combine.1 = f32[16,1024]{1,0:T(8,128)} custom-call(bf16[4,2,144,128]{3,2,1,0:T(8,128)(2,1)S(1)} %bitcast.6, bf16[144,128]{1,0:T(8,128)(2,1)S(1)} %collective-permute-done.8.last_ref, f32[128,128]{1,0:T(8,128)S(1)} %get-tuple-element.29.summed_ref, f32[8,128]{1,0:T(8,128)S(1)} %get-tuple-element.30.stats_ref), custom_call_target="tpu_custom_call" | custom-call | tf_op jit(solution)/shard_map/combine/pallas_call | solution.py:379
Async XLA Ops:
  0.0 12.7 %collective-permute-start = (bf16[32,64,256]{2,1,0:T(8,128)(2,1)}, bf16[32,64,256]{2,1,0:T(8,128)(2,1)S(1)}, u32[]{:S(2)}, u32[]{:S(2)}) collective-permute-start(bf16[32,64,256]{2,1,0:T(8,128)(2,1)} %bitcast.8), channel_id=1, source_target_pairs={{0,4},{4,0},{1,5},{5,1},{2,6},{6,2},{3,7},{7,3},{8,12},{12,8},{9,1... | collective-permute-start | bytes 3145736 | tf_op jit(solution)/shard_map/ppermute | solution.py:26
  0.5 6.7 %collective-permute-start.1 = (bf16[16,1024]{1,0:T(8,128)(2,1)}, bf16[16,1024]{1,0:T(8,128)(2,1)S(1)}, u32[]{:S(2)}, u32[]{:S(2)}) collective-permute-start(bf16[16,1024]{1,0:T(8,128)(2,1)} %own_ref.1), channel_id=1, source_target_pairs={{0,16},{8,24},{16,0},{24,8},{1,17},{9,25},{17,1},{25,9},{2,18},{10... | collective-permute-start | bytes 98312 | tf_op jit(solution)/shard_map/ppermute | solution.py:26
  4.0 6.0 %collective-permute-start.3 = (bf16[16,1024]{1,0:T(8,128)(2,1)}, bf16[16,1024]{1,0:T(8,128)(2,1)S(1)}, u32[]{:S(2)}, u32[]{:S(2)}) collective-permute-start(bf16[16,1024]{1,0:T(8,128)(2,1)} %own_ref.1), channel_id=1, source_target_pairs={{0,24},{8,16},{16,8},{24,0},{1,25},{9,17},{17,9},{25,1},{2,26},{10... | collective-permute-start | bytes 98312 | tf_op jit(solution)/shard_map/ppermute | solution.py:26
  5.4 6.1 %collective-permute-start.5 = (bf16[16,1024]{1,0:T(8,128)(2,1)}, bf16[16,1024]{1,0:T(8,128)(2,1)S(1)}, u32[]{:S(2)}, u32[]{:S(2)}) collective-permute-start(bf16[16,1024]{1,0:T(8,128)(2,1)} %own_ref.1), channel_id=1, source_target_pairs={{0,8},{8,0},{16,24},{24,16},{1,9},{9,1},{17,25},{25,17},{2,10},{10... | collective-permute-start | bytes 98312 | tf_op jit(solution)/shard_map/ppermute | solution.py:26
  5.6 9.1 %collective-permute-start.7 = (bf16[16,1024]{1,0:T(8,128)(2,1)}, bf16[16,1024]{1,0:T(8,128)(2,1)S(1)}, u32[]{:S(2)}, u32[]{:S(2)}) collective-permute-start(bf16[16,1024]{1,0:T(8,128)(2,1)} %own_ref.1), channel_id=1, source_target_pairs={{0,1},{1,0},{2,3},{3,2},{4,5},{5,4},{6,7},{7,6},{8,9},{9,8},{10,11... | collective-permute-start | bytes 98312 | tf_op jit(solution)/shard_map/ppermute | solution.py:26
  7.1 7.6 %collective-permute-start.2 = (bf16[16,1024]{1,0:T(8,128)(2,1)S(1)}, bf16[16,1024]{1,0:T(8,128)(2,1)S(1)}, u32[]{:S(2)}, u32[]{:S(2)}) collective-permute-start(bf16[16,1024]{1,0:T(8,128)(2,1)S(1)} %collective-permute-done.1.rest_0_), channel_id=1, source_target_pairs={{0,1},{1,0},{2,3},{3,2},{4,5},{5,4},{6,7},{7,6},{8,9},{9,8},{10,11... | collective-permute-start | bytes 98312 | tf_op jit(solution)/shard_map/ppermute | solution.py:26
  10.0 4.7 %collective-permute-start.4 = (bf16[16,1024]{1,0:T(8,128)(2,1)S(1)}, bf16[16,1024]{1,0:T(8,128)(2,1)S(1)}, u32[]{:S(2)}, u32[]{:S(2)}) collective-permute-start(bf16[16,1024]{1,0:T(8,128)(2,1)S(1)} %collective-permute-done.3.rest_2_), channel_id=1, source_target_pairs={{0,1},{1,0},{2,3},{3,2},{4,5},{5,4},{6,7},{7,6},{8,9},{9,8},{10,11... | collective-permute-start | bytes 98312 | tf_op jit(solution)/shard_map/ppermute | solution.py:26
  11.5 3.9 %collective-permute-start.6 = (bf16[16,1024]{1,0:T(8,128)(2,1)S(1)}, bf16[16,1024]{1,0:T(8,128)(2,1)S(1)}, u32[]{:S(2)}, u32[]{:S(2)}) collective-permute-start(bf16[16,1024]{1,0:T(8,128)(2,1)S(1)} %collective-permute-done.5.rest_4_), channel_id=1, source_target_pairs={{0,1},{1,0},{2,3},{3,2},{4,5},{5,4},{6,7},{7,6},{8,9},{9,8},{10,11... | collective-permute-start | bytes 98312 | tf_op jit(solution)/shard_map/ppermute | solution.py:26
  16.9 12.6 %all-to-all-start = ((bf16[8,144,128]{2,1,0:T(8,128)(2,1)}), bf16[8,144,128]{2,1,0:T(8,128)(2,1)S(1)}, u32[]{:S(2)}, u32[]{:S(2)}) async-start(bf16[8,144,128]{2,1,0:T(8,128)(2,1)} %bitcast.10), calls=%async_computation | async-start | bytes 589824 | tf_op jit(solution)/shard_map/all_to_all | solution.py:360
  23.5 4.6 %collective-permute-start.8 = (bf16[144,128]{1,0:T(8,128)(2,1)S(1)}, bf16[144,128]{1,0:T(8,128)(2,1)S(1)}, u32[]{:S(2)}, u32[]{:S(2)}) collective-permute-start(bf16[144,128]{1,0:T(8,128)(2,1)S(1)} %get-tuple-element.28), channel_id=1, source_target_pairs={{0,1},{1,0},{2,3},{3,2},{4,5},{5,4},{6,7},{7,6},{8,9},{9,8},{10,11... | collective-permute-start | bytes 110600 | tf_op jit(solution)/shard_map/ppermute | solution.py:26

commit v13 on v12

--- a/solution.py
+++ b/solution.py
@@ -21,14 +21,42 @@
 to_exp2 = HD ** (-0.5) * 1.4426950408889634
 
 
-def swapped(value, axis, mask=1):
-    size = lax.axis_size(axis)
-    return lax.ppermute(value, axis, [(i, i ^ mask) for i in range(size)])
-
-
-def request_order(n_req):
-    masks = list(range(n_req - 1, 0, -1))
-    return [2, 3, 1] if masks == [3, 2, 1] else masks
+def swapped(value, axis):
+    return lax.ppermute(value, axis, [(0, 1), (1, 0)])
+
+
+def shares(n_req):
+    both = n_req // 2
+    rest = [d for d in range(1, n_req) if d != both]
+    return both, (rest[: len(rest) // 2], rest[len(rest) // 2 :])
+
+
+def exchanged(value, message):
+    n_req = lax.axis_size("z")
+    both, own = shares(n_req)
+    pairs = []
+    for z in range(n_req):
+        for core in range(2):
+            for pair in range(2):
+                if message == 0:
+                    mask, side = both, core
+                else:
+                    mask, side = own[core][(message - 1) // 2], (message - 1) % 2
+                target = ((z ^ mask) * 2 + core) * 2 + (pair ^ side)
+                pairs.append(((z * 2 + core) * 2 + pair, target))
+    return lax.ppermute(value, ("z", "core", "pair"), pairs)
+
+
+def masks_here(n_req):
+    both, own = shares(n_req)
+    core = lax.axis_index("core")
+    return [both] + [jnp.where(core == 0, d0, d1) for d0, d1 in zip(*own)]
+
+
+def pack_kernel(own_ref, sibling_ref, out_ref):
+    core = lax.axis_index("core")
+    out_ref[core] = own_ref[...]
+    out_ref[1 - core] = sibling_ref[...]
 
 
 def stacked_heads(q):
@@ -121,7 +149,7 @@
     home_keys_ref, home_values_ref, keys_ref, values_ref, member_ref, held_ref, own, valid_ref,
     rows_ref, table, parents, near, sems,
 ):
-    n_req = keys_ref.shape[0] + 1
+    n_req = lax.axis_size("z")
     slots, half, _ = near.shape
     rows = table.shape[1]
     n_batch = rows // BEAMS
@@ -173,33 +201,36 @@
     found = jnp.concatenate(found, axis=0)
 
     small[2].wait()
-    for d in range(n_req):
-        request = (z ^ d) * 2 + core
-        lane = iota((rows, 2 * VECS), 1)
-        spread = iota((rows, 2 * VECS), 0) == request * BEAMS + lane % BEAMS
+    requests = [z * 2 + core]
+    for mask in masks_here(n_req):
+        requests += [(z ^ mask) * 2, (z ^ mask) * 2 + 1]
+    for i, request in enumerate(requests):
+        lane = iota((rows, VECS), 1)
+        spread = iota((rows, VECS), 0) == request * BEAMS + lane % BEAMS
         rows_ref[: 2 * slots, :] = count(continued, spread.astype(jnp.float32))
-        rows_ref[2 * slots :, :] = jnp.zeros((8, 2 * VECS), jnp.float32)
+        rows_ref[2 * slots :, :] = jnp.zeros((8, VECS), jnp.float32)
         mask = iota(found.shape, 1) == request
         picked = jnp.sum(jnp.where(mask, found, 0), axis=1, keepdims=True)
         values = []
         for k in range(2 * capacity):
             index = picked[k, 0]
             row = jnp.where(index > 0, index - 1, 2 * slots)
-            member_ref[d, k : k + 1, :] = rows_ref[pl.ds(row, 1), :]
+            member_ref[i, k : k + 1, :] = rows_ref[pl.ds(row, 1), :]
             pool_ref = near if k < capacity else far_ref
             base = 0 if k < capacity else slots
             content = pool_ref[jnp.maximum(index - 1 - base, 0)]
             tokens = slice(k * half, (k + 1) * half)
-            if d == 0:
+            if i == 0:
                 home_keys_ref[0, tokens, :] = content[:, :HD]
             else:
-                keys_ref[d - 1, tokens, :] = content[:, :HD]
+                keys_ref[i - 1, tokens, :] = content[:, :HD]
             values.append(content[:, HD:])
         values = jnp.concatenate(values, axis=0).T
-        if d == 0:
+        if i == 0:
             home_values_ref[0] = values
         else:
-            values_ref[d - 1] = values
+            values_ref[i - 1] = values
+
     small[3].wait()
     small[4].wait()
 
@@ -208,12 +239,13 @@
     return jnp.concatenate([stacked_heads(own_ref[...]), stacked_heads(pair_ref[...])], axis=0)
 
 
-def suffix_parts(vectors, keys_ref, values_ref, members, places):
+def suffix_parts(vectors, keys_ref, values_ref, members):
     n_slots = members[0].shape[0]
     half = keys_ref.shape[1] // n_slots
-    scores = [scores_of(keys_ref[i], each) for i, each in zip(places, vectors)]
+    scores = [scores_of(keys_ref[i], each) for i, each in enumerate(vectors)]
     softmaxes = []
     for member, score in zip(members, scores):
+        member = jnp.concatenate([member] * (score.shape[1] // VECS), axis=1)
         pieces = [
             jnp.where(
                 member[k : k + 1, :] > 0.0, score[k * half : (k + 1) * half], big_negative
@@ -229,7 +261,7 @@
                 values_ref[i], weights.astype(jnp.bfloat16), preferred_element_type=jnp.float32
             ),
         )
-        for i, (top, total, weights) in zip(places, softmaxes)
+        for i, (top, total, weights) in enumerate(softmaxes)
     ]
 
 
@@ -238,26 +270,23 @@
     return [x[:, lanes] for x in part]
 
 
-def away_kernel(keys_ref, values_ref, member_ref, *rest):
-    queries, (_, out_ref, after_ref, units, sems) = rest[:-5], rest[-5:]
+def away_kernel(n_messages, keys_ref, values_ref, member_ref, *rest):
+    messages, units, after_ref = rest[:n_messages], rest[-n_messages - 1 : -1], rest[-1]
     after_ref[...] = jnp.zeros(after_ref.shape, jnp.float32)
-    requests = request_order(keys_ref.shape[0] + 1)
-    z, parity = lax.axis_index("z"), lax.axis_index("pair")
-    vectors = [all_vectors(*queries[2 * i : 2 * i + 2]) for i in range(len(requests))]
-    members = [member_ref[d] for d in requests]
-    copies = []
-    parts = suffix_parts(vectors, keys_ref, values_ref, members, [d - 1 for d in requests])
-    for i, (d, part) in enumerate(zip(requests, parts)):
-        for side in range(2):
-            store_unit(units.at[i, side], *half_of(part, side))
-            owner = parity if side == 0 else 1 - parity
-            copy = pltpu.make_async_copy(
-                units.at[i, side], out_ref.at[z ^ d, owner], sems.at[i, side]
-            )
-            copy.start()
-            copies.append(copy)
-    for copy in copies:
-        copy.wait()
+    vectors = [stacked_heads(messages[0][core]) for core in range(2)]
+    for k in range(1, n_messages, 2):
+        for core in range(2):
+            halves = [stacked_heads(messages[k + side][core]) for side in range(2)]
+            vectors.append(jnp.concatenate(halves, axis=0))
+    members = [member_ref[1 + i] for i in range(len(vectors))]
+    parts = suffix_parts(vectors, keys_ref, values_ref, members)
+    for i, part in enumerate(parts):
+        core = i % 2
+        if i < 2:
+            store_unit(units[0].at[core], *part)
+        else:
+            for side in range(2):
+                store_unit(units[i // 2 * 2 - 1 + side].at[core], *half_of(part, side))
 
 
 def home_kernel(
@@ -265,7 +294,7 @@
     summed_ref, stats_ref, out_ref,
 ):
     vectors = all_vectors(own_ref, pair_ref)
-    (suffix,) = suffix_parts([vectors], keys_ref, values_ref, [member_ref[0]], [0])
+    (suffix,) = suffix_parts([vectors], keys_ref, values_ref, [member_ref[0]])
     prompt = prompt_part(valid_ref[0:1, :], prompt_ref, vectors)
     part = merged([prompt, suffix])
     top, total, summed_ref[...] = half_of(part, 0)
@@ -273,11 +302,18 @@
     store_unit(out_ref, *half_of(part, 1))
 
 
-def final_kernel(units_ref, last_ref, summed_ref, stats_ref, out_ref):
-    n_req, n_pair = units_ref.shape[:2]
-    z = lax.axis_index("z")
-    parts = [load_unit(units_ref.at[z ^ d, p]) for d in range(1, n_req) for p in range(n_pair)]
-    parts += [load_unit(last_ref), (stats_ref[0:1], stats_ref[1:2], summed_ref[...])]
+def sibling_kernel(*rest):
+    units, out_ref = rest[:-1], rest[-1]
+    core = lax.axis_index("core")
+    store_unit(out_ref, *merged([load_unit(unit.at[1 - core]) for unit in units]))
+
+
+def final_kernel(*rest):
+    units, (last_ref, shared_ref, summed_ref, stats_ref, out_ref) = rest[:-5], rest[-5:]
+    core = lax.axis_index("core")
+    parts = [load_unit(unit.at[core]) for unit in units]
+    parts += [load_unit(last_ref), load_unit(shared_ref)]
+    parts.append((stats_ref[0:1], stats_ref[1:2], summed_ref[...]))
     _, total, summed = merged(parts)
     attended = (summed / total).T
     for h in range(HEADS):
@@ -302,20 +338,25 @@
     hbm = pl.BlockSpec(memory_space=pltpu.HBM)
     near = pool.reshape(slots, half, width)
     far = swapped(near, "core")
-    sent = []
-    for d in request_order(n_req):
-        piece = swapped(queries, "z", d)
-        sent += [piece, swapped(piece, "pair")]
     other = swapped(queries, "pair")
+    both = pl.pallas_call(
+        pack_kernel,
+        out_shape=pltpu.VMEM((2,) + queries.shape, jnp.bfloat16),
+        in_specs=[vmem] * 2,
+        out_specs=vmem,
+        name="both_cores",
+    )(queries, swapped(queries, "core"))
+    n_messages = n_req - 1
+    messages = [exchanged(both, k) for k in range(n_messages)]
 
     home_keys, home_values, keys, values, member, prompt, own, valid = pl.pallas_call(
         functools.partial(prepare_kernel, capacity),
         out_shape=(
             pltpu.VMEM((1, 2 * capacity * half, HD), jnp.bfloat16),
             pltpu.VMEM((1, HD, 2 * capacity * half), jnp.bfloat16),
-            pltpu.VMEM((n_req - 1, 2 * capacity * half, HD), jnp.bfloat16),
-            pltpu.VMEM((n_req - 1, HD, 2 * capacity * half), jnp.bfloat16),
-            pltpu.VMEM((n_req, 2 * capacity, 2 * VECS), jnp.float32),
+            pltpu.VMEM((n_req, 2 * capacity * half, HD), jnp.bfloat16),
+            pltpu.VMEM((n_req, HD, 2 * capacity * half), jnp.bfloat16),
+            pltpu.VMEM((1 + n_req, 2 * capacity, VECS), jnp.float32),
             pltpu.VMEM((tokens, width), jnp.bfloat16),
             pltpu.VMEM(queries.shape, jnp.bfloat16),
             pltpu.VMEM((8, 2 * VECS), jnp.int32),
@@ -323,7 +364,7 @@
         in_specs=[pl.BlockSpec(memory_space=pltpu.SMEM)] + [hbm] * 5 + [vmem],
         out_specs=(vmem,) * 8,
         scratch_shapes=[
-            pltpu.VMEM((2 * slots + 8, 2 * VECS), jnp.float32),
+            pltpu.VMEM((2 * slots + 8, VECS), jnp.float32),
             pltpu.VMEM((SUF, rows), jnp.int32),
             pltpu.VMEM((1, rows), jnp.int32),
             pltpu.VMEM((slots, half, width), jnp.bfloat16),
@@ -341,23 +382,17 @@
         far,
     )
 
-    units, after = pl.pallas_call(
-        away_kernel,
-        out_shape=(
-            pltpu.HBM((n_req, 2, UNIT_ROWS, VECS), jnp.bfloat16),
-            pltpu.VMEM((8, VECS), jnp.float32),
-        ),
-        in_specs=[vmem] * (4 + len(sent)),
-        out_specs=(hbm, vmem),
-        scratch_shapes=[
-            pltpu.VMEM((n_req - 1, 2, UNIT_ROWS, VECS), jnp.bfloat16),
-            pltpu.SemaphoreType.DMA((n_req - 1, 2)),
-        ],
+    unit = pltpu.VMEM((UNIT_ROWS, VECS), jnp.bfloat16)
+    *units, after = pl.pallas_call(
+        functools.partial(away_kernel, n_messages),
+        out_shape=(pltpu.VMEM((2, UNIT_ROWS, VECS), jnp.bfloat16),) * n_messages
+        + (pltpu.VMEM((8, VECS), jnp.float32),),
+        in_specs=[vmem] * (4 + n_messages),
+        out_specs=(vmem,) * (n_messages + 1),
         compiler_params=params,
         name="suffix_away",
-    )(keys, values, member, *sent, other)
-    units = units.reshape(2 * n_req, UNIT_ROWS, VECS)
-    units = lax.all_to_all(units, ("z", "pair"), split_axis=0, concat_axis=0, tiled=True)
+    )(keys, values, member, *messages, other)
+    received = [exchanged(each, k) for k, each in enumerate(units)]
 
     summed, stats, given = pl.pallas_call(
         home_kernel,
@@ -376,14 +411,23 @@
     )(valid, home_keys, home_values, member, own, other, prompt, after)
     last = swapped(given, "pair")
 
+    share = pl.pallas_call(
+        sibling_kernel,
+        out_shape=unit,
+        in_specs=[vmem] * n_messages,
+        out_specs=vmem,
+        compiler_params=params,
+        name="sibling_share",
+    )(*received)
+
     return pl.pallas_call(
         final_kernel,
         out_shape=jax.ShapeDtypeStruct((BEAMS, HEADS * HD), jnp.float32),
-        in_specs=[vmem] * 4,
+        in_specs=[vmem] * (4 + n_messages),
         out_specs=vmem,
         compiler_params=params,
         name="combine",
-    )(units.reshape(n_req, 2, UNIT_ROWS, VECS), last, summed, stats)
+    )(*received, last, swapped(share, "core"), summed, stats)
 
 
 def solution(mesh):

time: 30.5 us -> 29.6 us (0.970)
  starting transfers between devices: 16.2 us -> 11.8 us
  waiting for transfers between devices: 6.6 us -> 9.35 us
  local copies, waits for them, and re-layouts: 0 us -> 0.61 us
    all_to_all x1 -> x0, starting transfers between devices: 4.11 us -> none  [on_device(): lax.all_to_all(units, ('z', 'pair'), split_axis=0, concat_axis=0, tiled=T...]
    ppermute x9 -> x11, waiting for transfers between devices: 5.27 us -> 9.35 us  [the longest x5 5.92 us: swapped(): return lax.ppermute(value, axis, [(0, 1), (1, 0)])]
    all_to_all x1 -> x0, waiting for transfers between devices: 1.33 us -> none  [on_device(): lax.all_to_all(units, ('z', 'pair'), split_axis=0, concat_axis=0, tiled=T...]
    unnamed x0 -> x2, local copies, waits for them, and re-layouts: none -> 0.61 us
    ppermute x9 -> x11, starting transfers between devices: 12.1 us -> 11.8 us  [the longest x6 9.52 us: exchanged(): return lax.ppermute(value, ('z', 'core', 'pair'), pairs)]
    pallas_call x1 -> x3, Pallas kernels: 1.51 us -> 1.7 us  [the longest x1 0.87 us: on_device(): pl.pallas_call(functools.partial(away_kernel, n_messages), out_shape=(plt...]
  transfers between devices with their start and end apart: 10 -> 11, of which waited for: 4 -> 6; matrix products, arithmetic and copies ran while one was open for 0% -> 0% of each run, Pallas kernels for 15% -> 18%
where the time goes in v13:
time: 29.6 us; the launch traced here: 29.4 us
  starting transfers between devices  11.8 us (40%)
  waiting for transfers between devices  9.35 us (32%)
  Pallas kernels  6.98 us (24%)
  between operations  0.72 us (2%)
  local copies, waits for them, and re-layouts  0.61 us (2%)
    ppermute x6, starting transfers between devices, exchanged(): return lax.ppermute(value, ('z', 'core', 'pair'), pairs)  9.52 us
    ppermute x5, waiting for transfers between devices, swapped(): return lax.ppermute(value, axis, [(0, 1), (1, 0)])  5.92 us
    ppermute x6, waiting for transfers between devices, exchanged(): return lax.ppermute(value, ('z', 'core', 'pair'), pairs)  3.43 us
    pallas_call x1, Pallas kernels, on_device(): pl.pallas_call(home_kernel, out_shape=(pltpu.VMEM((HD, VECS), jnp.float32...  2.51 us
    ppermute x5, starting transfers between devices, swapped(): return lax.ppermute(value, axis, [(0, 1), (1, 0)])  2.26 us
    pallas_call x1, Pallas kernels, on_device(): pl.pallas_call(functools.partial(prepare_kernel, capacity), out_shape=(pl...  2 us
    pallas_call x1, Pallas kernels, on_device(): pl.pallas_call(functools.partial(away_kernel, n_messages), out_shape=(plt...  0.87 us
    pallas_call x1, Pallas kernels, on_device(): pl.pallas_call(pack_kernel, out_shape=pltpu.VMEM((2,) + queries.shape, jn...  0.78 us
  transfers between devices with their start and end apart: 11, of which 6 were waited for; matrix products, arithmetic and copies ran while one was open for 0% of the time, Pallas kernels for 18%

profile of v13, /device:TPU:0, one launch (start us, length us, event | category | flops | bytes accessed | tf_op | source)
XLA Modules:
  0.0 29.4 jit_solution(11369388826400364017)
XLA Ops:
  0.0 0.5 %collective-permute-start = (bf16[32,64,256]{2,1,0:T(8,128)(2,1)}, bf16[32,64,256]{2,1,0:T(8,128)(2,1)S(1)}, u32[]{:S(2)}, u32[]{:S(2)}) collective-permute-start(bf16[32,64,256]{2,1,0:T(8,128)(2,1)} %bitcast.5), channel_id=1, source_target_pairs={{0,4},{4,0},{1,5},{5,1},{2,6},{6,2},{3,7},{7,3},{8,12},{12,8},{9,1... | collective-permute-start | bytes 3145736 | tf_op jit(solution)/shard_map/ppermute | solution.py:25
  0.5 0.1 collective-permute-start.1
  0.5 2.5 %collective-permute-done.1.sibling_ref = bf16[16,1024]{1,0:T(8,128)(2,1)S(1)} collective-permute-done((bf16[16,1024]{1,0:T(8,128)(2,1)}, bf16[16,1024]{1,0:T(8,128)(2,1)S(1)}, u32[]{:S(2)}, u32[]{:S(2)}) %collective-permute-start.1) | collective-permute-done | bytes 32800 | tf_op jit(solution)/shard_map/ppermute | solution.py:25
  3.0 0.6 %copy-done = bf16[16,1024]{1,0:T(8,128)(2,1)} copy-done((bf16[16,1024]{1,0:T(8,128)(2,1)}, bf16[16,1024]{1,0:T(8,128)(2,1)S(1)}, u32[]{:S(2)}) %copy-start) | copy-done | bytes 32792
  3.6 0.8 %both_cores.1 = bf16[2,16,1024]{2,1,0:T(8,128)(2,1)S(1)} custom-call(bf16[16,1024]{1,0:T(8,128)(2,1)} %own_ref.3, bf16[16,1024]{1,0:T(8,128)(2,1)} %copy-done), custom_call_target="tpu_custom_call" | custom-call | tf_op jit(solution)/shard_map/both_cores/pallas_call | solution.py:342
  4.4 4.0 %collective-permute-start.2 = (bf16[2,16,1024]{2,1,0:T(8,128)(2,1)S(1)}, bf16[2,16,1024]{2,1,0:T(8,128)(2,1)S(1)}, u32[]{:S(2)}, u32[]{:S(2)}) collective-permute-start(bf16[2,16,1024]{2,1,0:T(8,128)(2,1)S(1)} %both_cores.1), channel_id=1, source_target_pairs={{0,16},{1,17},{4,21},{5,20},{8,24},{9,25},{12,29},{13,28},{16,0},{... | collective-permute-start | bytes 196616 | tf_op jit(solution)/shard_map/ppermute | solution.py:47
  8.4 1.6 %collective-permute-start.3 = (bf16[2,16,1024]{2,1,0:T(8,128)(2,1)S(1)}, bf16[2,16,1024]{2,1,0:T(8,128)(2,1)S(1)}, u32[]{:S(2)}, u32[]{:S(2)}) collective-permute-start(bf16[2,16,1024]{2,1,0:T(8,128)(2,1)S(1)} %both_cores.1), channel_id=1, source_target_pairs={{0,8},{1,9},{4,28},{5,29},{8,0},{9,1},{12,20},{13,21},{16,24},{17,... | collective-permute-start | bytes 196616 | tf_op jit(solution)/shard_map/ppermute | solution.py:47
  10.0 1.4 %collective-permute-start.4 = (bf16[2,16,1024]{2,1,0:T(8,128)(2,1)S(1)}, bf16[2,16,1024]{2,1,0:T(8,128)(2,1)S(1)}, u32[]{:S(2)}, u32[]{:S(2)}) collective-permute-start(bf16[2,16,1024]{2,1,0:T(8,128)(2,1)S(1)} %both_cores.1), channel_id=1, source_target_pairs={{0,9},{1,8},{4,29},{5,28},{8,1},{9,0},{12,21},{13,20},{16,25},{17,... | collective-permute-start | bytes 196616 | tf_op jit(solution)/shard_map/ppermute | solution.py:47
  11.4 0.5 %collective-permute-start.5 = (bf16[16,1024]{1,0:T(8,128)(2,1)}, bf16[16,1024]{1,0:T(8,128)(2,1)S(1)}, u32[]{:S(2)}, u32[]{:S(2)}) collective-permute-start(bf16[16,1024]{1,0:T(8,128)(2,1)} %own_ref.3), channel_id=1, source_target_pairs={{0,1},{1,0},{2,3},{3,2},{4,5},{5,4},{6,7},{7,6},{8,9},{9,8},{10,11... | collective-permute-start | bytes 98312 | tf_op jit(solution)/shard_map/ppermute | solution.py:25
  12.6 0.0 collective-permute-done.far_ref
  12.6 2.0 %prepare.1 = (bf16[1,512,128]{2,1,0:T(8,128)(2,1)S(1)}, bf16[1,128,512]{2,1,0:T(8,128)(2,1)S(1)}, bf16[4,512,128]{2,1,0:T(8,128)(2,1)S(1)}, bf16[4,128,512]{2,1,...) custom-call(s32[1]{0:T(128)S(6)} %copy.7.length_ref, ...), custom_call_target="tpu_custom_call" | custom-call | tf_op jit(solution)/shard_map/prepare/pallas_call | solution.py:352
  14.6 2.2 %collective-permute-done.5.rest_3_.pair_ref = bf16[16,1024]{1,0:T(8,128)(2,1)S(1)} collective-permute-done((bf16[16,1024]{1,0:T(8,128)(2,1)}, bf16[16,1024]{1,0:T(8,128)(2,1)S(1)}, u32[]{:S(2)}, u32[]{:S(2)}) %collective-permute-start.5) | collective-permute-done | bytes 32800 | tf_op jit(solution)/shard_map/ppermute | solution.py:25
  16.8 0.9 %suffix_away.1 = (bf16[2,144,128]{2,1,0:T(8,128)(2,1)S(1)}, bf16[2,144,128]{2,1,0:T(8,128)(2,1)S(1)}, bf16[2,144,128]{2,1,0:T(8,128)(2,1)S(1)}, f32[8,128]{1,0:T(8,128)S(1)}) custom-call(bf16[4,512,128]{2,1,0:T(8,128)(2,1)S(1)} %get-tuple-element.20.keys_ref, bf16[4,128,512]{2,1,0:T(8,128)(2,1)S(1)} %get-tuple-element.21.values_ref, ...), custom_call_target="tpu_custom_call" | custom-call | tf_op jit(solution)/shard_map/suffix_away/pallas_call | solution.py:386
  17.7 0.1 collective-permute-start.6
  17.8 1.6 %collective-permute-start.7 = (bf16[2,144,128]{2,1,0:T(8,128)(2,1)S(1)}, bf16[2,144,128]{2,1,0:T(8,128)(2,1)S(1)}, u32[]{:S(2)}, u32[]{:S(2)}) collective-permute-start(bf16[2,144,128]{2,1,0:T(8,128)(2,1)S(1)} %get-tuple-element.24), channel_id=1, source_target_pairs={{0,8},{1,9},{4,28},{5,29},{8,0},{9,1},{12,20},{13,21},{16,24},{17,... | collective-permute-start | bytes 221192 | tf_op jit(solution)/shard_map/ppermute | solution.py:47
  19.4 0.9 %collective-permute-start.8 = (bf16[2,144,128]{2,1,0:T(8,128)(2,1)S(1)}, bf16[2,144,128]{2,1,0:T(8,128)(2,1)S(1)}, u32[]{:S(2)}, u32[]{:S(2)}) collective-permute-start(bf16[2,144,128]{2,1,0:T(8,128)(2,1)S(1)} %get-tuple-element.25), channel_id=1, source_target_pairs={{0,9},{1,8},{4,29},{5,28},{8,1},{9,0},{12,21},{13,20},{16,25},{17,... | collective-permute-start | bytes 221192 | tf_op jit(solution)/shard_map/ppermute | solution.py:47
  20.2 2.5 %home_part.1 = (f32[128,128]{1,0:T(8,128)S(1)}, f32[8,128]{1,0:T(8,128)S(1)}, bf16[144,128]{1,0:T(8,128)(2,1)S(1)}) custom-call(s32[8,256]{1,0:T(8,128)S(1)} %get-tuple-element.26.valid_ref, bf16[1,512,128]{2,1,0:T(8,128)(2,1)S(1)} %get-tuple-element.27.keys_ref, bf16[1,128,512]{2,1,0:T(8,128)(2,1)S(1)} %get-tuple-element.28.values_ref, ...), custom_call_target="tpu_custom_call" | custom-call | flops 536870912 | bytes 2097152 | tf_op jit(solution)/shard_map/home_part/pallas_call | solution.py:397
  22.8 1.1 %collective-permute-start.9 = (bf16[144,128]{1,0:T(8,128)(2,1)S(1)}, bf16[144,128]{1,0:T(8,128)(2,1)S(1)}, u32[]{:S(2)}, u32[]{:S(2)}) collective-permute-start(bf16[144,128]{1,0:T(8,128)(2,1)S(1)} %get-tuple-element.32), channel_id=1, source_target_pairs={{0,1},{1,0},{2,3},{3,2},{4,5},{5,4},{6,7},{7,6},{8,9},{9,8},{10,11... | collective-permute-start | bytes 110600 | tf_op jit(solution)/shard_map/ppermute | solution.py:25
  23.9 1.7 %collective-permute-done.6.rest_0_ = bf16[2,144,128]{2,1,0:T(8,128)(2,1)S(1)} collective-permute-done((bf16[2,144,128]{2,1,0:T(8,128)(2,1)S(1)}, bf16[2,144,128]{2,1,0:T(8,128)(2,1)S(1)}, u32[]{:S(2)}, u32[]{:S(2)}) %collective-permute-start.6) | collective-permute-done | bytes 73760 | tf_op jit(solution)/shard_map/ppermute | solution.py:47
  25.6 1.7 %collective-permute-done.8.rest_2_ = bf16[2,144,128]{2,1,0:T(8,128)(2,1)S(1)} collective-permute-done((bf16[2,144,128]{2,1,0:T(8,128)(2,1)S(1)}, bf16[2,144,128]{2,1,0:T(8,128)(2,1)S(1)}, u32[]{:S(2)}, u32[]{:S(2)}) %collective-permute-start.8) | collective-permute-done | bytes 73760 | tf_op jit(solution)/shard_map/ppermute | solution.py:47
  27.4 0.1 collective-permute-start.10
  27.5 0.2 collective-permute-done.9.rest_3_
  27.6 1.0 %collective-permute-done.10.rest_4_ = bf16[144,128]{1,0:T(8,128)(2,1)S(1)} collective-permute-done((bf16[144,128]{1,0:T(8,128)(2,1)S(1)}, bf16[144,128]{1,0:T(8,128)(2,1)S(1)}, u32[]{:S(2)}, u32[]{:S(2)}) %collective-permute-start.10) | collective-permute-done | bytes 36896 | tf_op jit(solution)/shard_map/ppermute | solution.py:25
  28.7 0.8 %combine.1 = f32[16,1024]{1,0:T(8,128)} custom-call(bf16[2,144,128]{2,1,0:T(8,128)(2,1)S(1)} %collective-permute-done.6.rest_0_, bf16[2,144,128]{2,1,0:T(8,128)(2,1)S(1)} %collective-permute-done.7.rest_1_, bf16[2,144,128]{2,1,0:T(8,128)(2,1)S(1)} %collective-permute-done.8.rest_2_, bf16[144,128]{1,0:T(8,128)(2,1)S(1)} %collective-permute-done.9.rest_3_, ...), custom_call_target="tpu_custom_call" | custom-call | tf_op jit(solution)/shard_map/combine/pallas_call | solution.py:423
  (6 shorter events, 0.1 us)
Async XLA Ops:
  0.0 12.6 %collective-permute-start = (bf16[32,64,256]{2,1,0:T(8,128)(2,1)}, bf16[32,64,256]{2,1,0:T(8,128)(2,1)S(1)}, u32[]{:S(2)}, u32[]{:S(2)}) collective-permute-start(bf16[32,64,256]{2,1,0:T(8,128)(2,1)} %bitcast.5), channel_id=1, source_target_pairs={{0,4},{4,0},{1,5},{5,1},{2,6},{6,2},{3,7},{7,3},{8,12},{12,8},{9,1... | collective-permute-start | bytes 3145736 | tf_op jit(solution)/shard_map/ppermute | solution.py:25
  0.5 2.5 %collective-permute-start.1 = (bf16[16,1024]{1,0:T(8,128)(2,1)}, bf16[16,1024]{1,0:T(8,128)(2,1)S(1)}, u32[]{:S(2)}, u32[]{:S(2)}) collective-permute-start(bf16[16,1024]{1,0:T(8,128)(2,1)} %own_ref.3), channel_id=1, source_target_pairs={{0,4},{4,0},{1,5},{5,1},{2,6},{6,2},{3,7},{7,3},{8,12},{12,8},{9,1... | collective-permute-start | bytes 98312 | tf_op jit(solution)/shard_map/ppermute | solution.py:25
  3.0 0.6 %copy-start = (bf16[16,1024]{1,0:T(8,128)(2,1)}, bf16[16,1024]{1,0:T(8,128)(2,1)S(1)}, u32[]{:S(2)}) copy-start(bf16[16,1024]{1,0:T(8,128)(2,1)S(1)} %collective-permute-done.1.sibling_ref) | copy-start | bytes 98308
  4.4 12.4 %collective-permute-start.2 = (bf16[2,16,1024]{2,1,0:T(8,128)(2,1)S(1)}, bf16[2,16,1024]{2,1,0:T(8,128)(2,1)S(1)}, u32[]{:S(2)}, u32[]{:S(2)}) collective-permute-start(bf16[2,16,1024]{2,1,0:T(8,128)(2,1)S(1)} %both_cores.1), channel_id=1, source_target_pairs={{0,16},{1,17},{4,21},{5,20},{8,24},{9,25},{12,29},{13,28},{16,0},{... | collective-permute-start | bytes 196616 | tf_op jit(solution)/shard_map/ppermute | solution.py:47
  8.4 8.4 %collective-permute-start.3 = (bf16[2,16,1024]{2,1,0:T(8,128)(2,1)S(1)}, bf16[2,16,1024]{2,1,0:T(8,128)(2,1)S(1)}, u32[]{:S(2)}, u32[]{:S(2)}) collective-permute-start(bf16[2,16,1024]{2,1,0:T(8,128)(2,1)S(1)} %both_cores.1), channel_id=1, source_target_pairs={{0,8},{1,9},{4,28},{5,29},{8,0},{9,1},{12,20},{13,21},{16,24},{17,... | collective-permute-start | bytes 196616 | tf_op jit(solution)/shard_map/ppermute | solution.py:47
  10.0 6.8 %collective-permute-start.4 = (bf16[2,16,1024]{2,1,0:T(8,128)(2,1)S(1)}, bf16[2,16,1024]{2,1,0:T(8,128)(2,1)S(1)}, u32[]{:S(2)}, u32[]{:S(2)}) collective-permute-start(bf16[2,16,1024]{2,1,0:T(8,128)(2,1)S(1)} %both_cores.1), channel_id=1, source_target_pairs={{0,9},{1,8},{4,29},{5,28},{8,1},{9,0},{12,21},{13,20},{16,25},{17,... | collective-permute-start | bytes 196616 | tf_op jit(solution)/shard_map/ppermute | solution.py:47
  11.4 5.4 %collective-permute-start.5 = (bf16[16,1024]{1,0:T(8,128)(2,1)}, bf16[16,1024]{1,0:T(8,128)(2,1)S(1)}, u32[]{:S(2)}, u32[]{:S(2)}) collective-permute-start(bf16[16,1024]{1,0:T(8,128)(2,1)} %own_ref.3), channel_id=1, source_target_pairs={{0,1},{1,0},{2,3},{3,2},{4,5},{5,4},{6,7},{7,6},{8,9},{9,8},{10,11... | collective-permute-start | bytes 98312 | tf_op jit(solution)/shard_map/ppermute | solution.py:25
  17.7 7.9 %collective-permute-start.6 = (bf16[2,144,128]{2,1,0:T(8,128)(2,1)S(1)}, bf16[2,144,128]{2,1,0:T(8,128)(2,1)S(1)}, u32[]{:S(2)}, u32[]{:S(2)}) collective-permute-start(bf16[2,144,128]{2,1,0:T(8,128)(2,1)S(1)} %get-tuple-element.23), channel_id=1, source_target_pairs={{0,16},{1,17},{4,21},{5,20},{8,24},{9,25},{12,29},{13,28},{16,0},{... | collective-permute-start | bytes 221192 | tf_op jit(solution)/shard_map/ppermute | solution.py:47
  17.8 7.8 %collective-permute-start.7 = (bf16[2,144,128]{2,1,0:T(8,128)(2,1)S(1)}, bf16[2,144,128]{2,1,0:T(8,128)(2,1)S(1)}, u32[]{:S(2)}, u32[]{:S(2)}) collective-permute-start(bf16[2,144,128]{2,1,0:T(8,128)(2,1)S(1)} %get-tuple-element.24), channel_id=1, source_target_pairs={{0,8},{1,9},{4,28},{5,29},{8,0},{9,1},{12,20},{13,21},{16,24},{17,... | collective-permute-start | bytes 221192 | tf_op jit(solution)/shard_map/ppermute | solution.py:47
  19.4 8.0 %collective-permute-start.8 = (bf16[2,144,128]{2,1,0:T(8,128)(2,1)S(1)}, bf16[2,144,128]{2,1,0:T(8,128)(2,1)S(1)}, u32[]{:S(2)}, u32[]{:S(2)}) collective-permute-start(bf16[2,144,128]{2,1,0:T(8,128)(2,1)S(1)} %get-tuple-element.25), channel_id=1, source_target_pairs={{0,9},{1,8},{4,29},{5,28},{8,1},{9,0},{12,21},{13,20},{16,25},{17,... | collective-permute-start | bytes 221192 | tf_op jit(solution)/shard_map/ppermute | solution.py:47
  22.8 4.9 %collective-permute-start.9 = (bf16[144,128]{1,0:T(8,128)(2,1)S(1)}, bf16[144,128]{1,0:T(8,128)(2,1)S(1)}, u32[]{:S(2)}, u32[]{:S(2)}) collective-permute-start(bf16[144,128]{1,0:T(8,128)(2,1)S(1)} %get-tuple-element.32), channel_id=1, source_target_pairs={{0,1},{1,0},{2,3},{3,2},{4,5},{5,4},{6,7},{7,6},{8,9},{9,8},{10,11... | collective-permute-start | bytes 110600 | tf_op jit(solution)/shard_map/ppermute | solution.py:25
  27.4 1.3 %collective-permute-start.10 = (bf16[144,128]{1,0:T(8,128)(2,1)S(1)}, bf16[144,128]{1,0:T(8,128)(2,1)S(1)}, u32[]{:S(2)}, u32[]{:S(2)}) collective-permute-start(bf16[144,128]{1,0:T(8,128)(2,1)S(1)} %sibling_share.1), channel_id=1, source_target_pairs={{0,4},{4,0},{1,5},{5,1},{2,6},{6,2},{3,7},{7,3},{8,12},{12,8},{9,1... | collective-permute-start | bytes 110600 | tf_op jit(solution)/shard_map/ppermute | solution.py:25

commit v14 on v13

--- a/solution.py
+++ b/solution.py
@@ -51,6 +51,19 @@
     both, own = shares(n_req)
     core = lax.axis_index("core")
     return [both] + [jnp.where(core == 0, d0, d1) for d0, d1 in zip(*own)]
+
+
+def stage_kernel(*refs):
+    half = (len(refs) - 1) // 2
+    sources, targets, sems = refs[:half], refs[half:-1], refs[-1]
+    copies = [
+        pltpu.make_async_copy(source, target, sems.at[i])
+        for i, (source, target) in enumerate(zip(sources, targets))
+    ]
+    for copy in copies:
+        copy.start()
+    for copy in copies:
+        copy.wait()
 
 
 def pack_kernel(own_ref, sibling_ref, out_ref):
@@ -145,9 +158,9 @@
 
 
 def prepare_kernel(
-    capacity, length_ref, table_ref, parents_ref, near_ref, prompt_ref, own_ref, far_ref,
-    home_keys_ref, home_values_ref, keys_ref, values_ref, member_ref, held_ref, own, valid_ref,
-    rows_ref, table, parents, near, sems,
+    capacity, length_ref, prompt_ref, table, parents, near, far_ref,
+    home_keys_ref, home_values_ref, keys_ref, values_ref, member_ref, held_ref, valid_ref,
+    rows_ref, sem,
 ):
     n_req = lax.axis_size("z")
     slots, half, _ = near.shape
@@ -155,20 +168,8 @@
     n_batch = rows // BEAMS
     z, core = lax.axis_index("z"), lax.axis_index("core")
 
-    small = [
-        pltpu.make_async_copy(source, target, sems.at[i])
-        for i, (source, target) in enumerate(
-            [
-                (table_ref, table),
-                (parents_ref, parents),
-                (near_ref, near),
-                (prompt_ref, held_ref),
-                (own_ref, own),
-            ]
-        )
-    ]
-    for copy in small:
-        copy.start()
+    copy = pltpu.make_async_copy(prompt_ref, held_ref, sem)
+    copy.start()
 
     length = length_ref[0]
     whole = lax.div(length, 2 * half)
@@ -176,7 +177,6 @@
     valid = whole * half + jnp.clip(length - whole * (2 * half) - parity * half, 0, half)
     valid_ref[...] = jnp.full(valid_ref.shape, valid, jnp.int32)
 
-    small[0].wait()
     slot = iota((2 * slots, rows), 0)
     mine = slot < slots
     block = jnp.where(mine, slot, slot - slots) + jnp.where(mine, 2 * z + core, 2 * z + 1 - core) * slots
@@ -188,7 +188,6 @@
     left, right = iota((2 * slots, 2 * slots), 0), iota((2 * slots, 2 * slots), 1)
     before = (left // slots == right // slots) & (right < left)
     rank = count(before.astype(jnp.float32), hit)
-    small[1].wait()
     taken = (iota((rows, rows), 0) == parents[...]).astype(jnp.float32)
     continued = count(named, taken)
 
@@ -200,7 +199,6 @@
         found.append(jnp.sum(jnp.where(chosen, place + 1, 0), axis=0, keepdims=True))
     found = jnp.concatenate(found, axis=0)
 
-    small[2].wait()
     requests = [z * 2 + core]
     for mask in masks_here(n_req):
         requests += [(z ^ mask) * 2, (z ^ mask) * 2 + 1]
@@ -231,8 +229,7 @@
         else:
             values_ref[i - 1] = values
 
-    small[3].wait()
-    small[4].wait()
+    copy.wait()
 
 
 def all_vectors(own_ref, pair_ref):
@@ -336,7 +333,17 @@
     params = pltpu.CompilerParams(vmem_limit_bytes=40 * 2**20)
 
     hbm = pl.BlockSpec(memory_space=pltpu.HBM)
-    near = pool.reshape(slots, half, width)
+    sibling = swapped(queries, "core")
+    staged = [queries, pool.reshape(slots, half, width), block_table.T, parents.reshape(1, rows)]
+    own, near, table, row_parents = pl.pallas_call(
+        stage_kernel,
+        out_shape=tuple(pltpu.VMEM(each.shape, each.dtype) for each in staged),
+        in_specs=[hbm] * len(staged),
+        out_specs=(vmem,) * len(staged),
+        scratch_shapes=[pltpu.SemaphoreType.DMA((len(staged),))],
+        compiler_params=params,
+        name="stage",
+    )(*[in_hbm(each) for each in staged])
     far = swapped(near, "core")
     other = swapped(queries, "pair")
     both = pl.pallas_call(
@@ -345,11 +352,11 @@
         in_specs=[vmem] * 2,
         out_specs=vmem,
         name="both_cores",
-    )(queries, swapped(queries, "core"))
+    )(own, sibling)
     n_messages = n_req - 1
     messages = [exchanged(both, k) for k in range(n_messages)]
 
-    home_keys, home_values, keys, values, member, prompt, own, valid = pl.pallas_call(
+    home_keys, home_values, keys, values, member, prompt, valid = pl.pallas_call(
         functools.partial(prepare_kernel, capacity),
         out_shape=(
             pltpu.VMEM((1, 2 * capacity * half, HD), jnp.bfloat16),
@@ -358,27 +365,22 @@
             pltpu.VMEM((n_req, HD, 2 * capacity * half), jnp.bfloat16),
             pltpu.VMEM((1 + n_req, 2 * capacity, VECS), jnp.float32),
             pltpu.VMEM((tokens, width), jnp.bfloat16),
-            pltpu.VMEM(queries.shape, jnp.bfloat16),
             pltpu.VMEM((8, 2 * VECS), jnp.int32),
         ),
-        in_specs=[pl.BlockSpec(memory_space=pltpu.SMEM)] + [hbm] * 5 + [vmem],
-        out_specs=(vmem,) * 8,
+        in_specs=[pl.BlockSpec(memory_space=pltpu.SMEM), hbm] + [vmem] * 4,
+        out_specs=(vmem,) * 7,
         scratch_shapes=[
             pltpu.VMEM((2 * slots + 8, VECS), jnp.float32),
-            pltpu.VMEM((SUF, rows), jnp.int32),
-            pltpu.VMEM((1, rows), jnp.int32),
-            pltpu.VMEM((slots, half, width), jnp.bfloat16),
-            pltpu.SemaphoreType.DMA((5,)),
+            pltpu.SemaphoreType.DMA,
         ],
         compiler_params=params,
         name="prepare",
     )(
         lengths,
-        in_hbm(block_table.T),
-        in_hbm(parents.reshape(1, rows)),
-        in_hbm(near),
         in_hbm(prompt_cache.reshape(tokens, width)),
-        in_hbm(queries),
+        table,
+        row_parents,
+        near,
         far,
     )
 
@@ -387,11 +389,11 @@
         functools.partial(away_kernel, n_messages),
         out_shape=(pltpu.VMEM((2, UNIT_ROWS, VECS), jnp.bfloat16),) * n_messages
         + (pltpu.VMEM((8, VECS), jnp.float32),),
-        in_specs=[vmem] * (4 + n_messages),
+        in_specs=[vmem] * (3 + n_messages),
         out_specs=(vmem,) * (n_messages + 1),
         compiler_params=params,
         name="suffix_away",
-    )(keys, values, member, *messages, other)
+    )(keys, values, member, *messages)
     received = [exchanged(each, k) for k, each in enumerate(units)]
 
     summed, stats, given = pl.pallas_call(

time: 29.6 us -> 30.9 us (1.044)
  the two profiles are of different devices: /device:TPU:0 before, /device:TPU:1 now
where the time goes in v14:
time: 30.9 us; the launch traced here: 30.7 us
  starting transfers between devices  16.4 us (53%)
  Pallas kernels  8.48 us (27%)
  waiting for transfers between devices  3.85 us (12%)
  local copies, waits for them, and re-layouts  1.22 us (4%)
  between operations  0.75 us (2%)
    ppermute x6, starting transfers between devices, exchanged(): return lax.ppermute(value, ('z', 'core', 'pair'), pairs)  13.6 us
    ppermute x5, waiting for transfers between devices, swapped(): return lax.ppermute(value, axis, [(0, 1), (1, 0)])  3.84 us
    ppermute x5, starting transfers between devices, swapped(): return lax.ppermute(value, axis, [(0, 1), (1, 0)])  2.78 us
    pallas_call x1, Pallas kernels, on_device(): pl.pallas_call(home_kernel, out_shape=(pltpu.VMEM((HD, VECS), jnp.float32...  2.52 us
    pallas_call x1, Pallas kernels, on_device(): pl.pallas_call(functools.partial(prepare_kernel, capacity), out_shape=(pl...  2.2 us
    pallas_call x1, Pallas kernels, on_device(): pl.pallas_call(stage_kernel, out_shape=tuple((pltpu.VMEM(each.shape, each...  1.28 us
    unnamed x6, local copies, waits for them, and re-layouts  1.22 us
    pallas_call x1, Pallas kernels, on_device(): pl.pallas_call(functools.partial(away_kernel, n_messages), out_shape=(plt...  0.87 us
  transfers between devices with their start and end apart: 11, of which 2 were waited for; matrix products, arithmetic and copies ran while one was open for 0% of the time, Pallas kernels for 21%

profile of v14, /device:TPU:1, one launch (start us, length us, event | category | flops | bytes accessed | tf_op | source)
XLA Modules:
  0.0 30.7 jit_solution(15962133944134102293)
XLA Ops:
  0.0 1.3 %stage.1 = (bf16[16,1024]{1,0:T(8,128)(2,1)S(1)}, bf16[32,64,256]{2,1,0:T(8,128)(2,1)S(1)}, s32[4,128]{1,0:T(4,128)S(1)}, s32[1,128]{1,0:T(1,128)S(1)}) custom-call(bf16[16,1024]{1,0:T(8,128)(2,1)} %refs_0_.1, bf16[32,64,256]{2,1,0:T(8,128)(2,1)} %bitcast.5, s32[4,128]{1,0:T(4,128)} %bitcast.6, s32[1,128]{1,0:T(1,128)} %bitcast.7), custom_call_target="tpu_custom_call" | custom-call | tf_op jit(solution)/shard_map/stage/pallas_call | solution.py:338
  1.3 0.0 copy-start
  1.3 0.6 %copy-done = bf16[16,1024]{1,0:T(8,128)(2,1)} copy-done((bf16[16,1024]{1,0:T(8,128)(2,1)}, bf16[16,1024]{1,0:T(8,128)(2,1)S(1)}, u32[]{:S(2)}) %copy-start) | copy-done | bytes 32792
  1.9 0.1 collective-permute-start
  2.0 0.5 %collective-permute-start.1 = (bf16[16,1024]{1,0:T(8,128)(2,1)}, bf16[16,1024]{1,0:T(8,128)(2,1)S(1)}, u32[]{:S(2)}, u32[]{:S(2)}) collective-permute-start(bf16[16,1024]{1,0:T(8,128)(2,1)} %refs_0_.1), channel_id=1, source_target_pairs={{0,4},{4,0},{1,5},{5,1},{2,6},{6,2},{3,7},{7,3},{8,12},{12,8},{9,1... | collective-permute-start | bytes 98312 | tf_op jit(solution)/shard_map/ppermute | solution.py:25
  2.4 2.1 %collective-permute-done.1.sibling_ref = bf16[16,1024]{1,0:T(8,128)(2,1)S(1)} collective-permute-done((bf16[16,1024]{1,0:T(8,128)(2,1)}, bf16[16,1024]{1,0:T(8,128)(2,1)S(1)}, u32[]{:S(2)}, u32[]{:S(2)}) %collective-permute-start.1) | collective-permute-done | bytes 32800 | tf_op jit(solution)/shard_map/ppermute | solution.py:25
  4.5 0.6 %copy-done.2 = bf16[16,1024]{1,0:T(8,128)(2,1)} copy-done((bf16[16,1024]{1,0:T(8,128)(2,1)}, bf16[16,1024]{1,0:T(8,128)(2,1)S(1)}, u32[]{:S(2)}) %copy-start.2) | copy-done | bytes 32792
  5.1 0.8 %both_cores.1 = bf16[2,16,1024]{2,1,0:T(8,128)(2,1)S(1)} custom-call(bf16[16,1024]{1,0:T(8,128)(2,1)} %copy-done, bf16[16,1024]{1,0:T(8,128)(2,1)} %copy-done.2), custom_call_target="tpu_custom_call" | custom-call | tf_op jit(solution)/shard_map/both_cores/pallas_call | solution.py:349
  5.9 4.6 %collective-permute-start.2 = (bf16[2,16,1024]{2,1,0:T(8,128)(2,1)S(1)}, bf16[2,16,1024]{2,1,0:T(8,128)(2,1)S(1)}, u32[]{:S(2)}, u32[]{:S(2)}) collective-permute-start(bf16[2,16,1024]{2,1,0:T(8,128)(2,1)S(1)} %both_cores.1), channel_id=1, source_target_pairs={{0,16},{1,17},{4,21},{5,20},{8,24},{9,25},{12,29},{13,28},{16,0},{... | collective-permute-start | bytes 196616 | tf_op jit(solution)/shard_map/ppermute | solution.py:47
  10.5 1.1 %collective-permute-start.3 = (bf16[2,16,1024]{2,1,0:T(8,128)(2,1)S(1)}, bf16[2,16,1024]{2,1,0:T(8,128)(2,1)S(1)}, u32[]{:S(2)}, u32[]{:S(2)}) collective-permute-start(bf16[2,16,1024]{2,1,0:T(8,128)(2,1)S(1)} %both_cores.1), channel_id=1, source_target_pairs={{0,8},{1,9},{4,28},{5,29},{8,0},{9,1},{12,20},{13,21},{16,24},{17,... | collective-permute-start | bytes 196616 | tf_op jit(solution)/shard_map/ppermute | solution.py:47
  11.6 2.2 %collective-permute-start.4 = (bf16[2,16,1024]{2,1,0:T(8,128)(2,1)S(1)}, bf16[2,16,1024]{2,1,0:T(8,128)(2,1)S(1)}, u32[]{:S(2)}, u32[]{:S(2)}) collective-permute-start(bf16[2,16,1024]{2,1,0:T(8,128)(2,1)S(1)} %both_cores.1), channel_id=1, source_target_pairs={{0,9},{1,8},{4,29},{5,28},{8,1},{9,0},{12,21},{13,20},{16,25},{17,... | collective-permute-start | bytes 196616 | tf_op jit(solution)/shard_map/ppermute | solution.py:47
  13.7 1.2 %collective-permute-start.8 = (bf16[16,1024]{1,0:T(8,128)(2,1)}, bf16[16,1024]{1,0:T(8,128)(2,1)S(1)}, u32[]{:S(2)}, u32[]{:S(2)}) collective-permute-start(bf16[16,1024]{1,0:T(8,128)(2,1)} %refs_0_.1), channel_id=1, source_target_pairs={{0,1},{1,0},{2,3},{3,2},{4,5},{5,4},{6,7},{7,6},{8,9},{9,8},{10,11... | collective-permute-start | bytes 98312 | tf_op jit(solution)/shard_map/ppermute | solution.py:25
  15.6 0.0 copy-start.1
  15.6 2.2 %prepare.1 = (bf16[1,512,128]{2,1,0:T(8,128)(2,1)S(1)}, bf16[1,128,512]{2,1,0:T(8,128)(2,1)S(1)}, bf16[4,512,128]{2,1,0:T(8,128)(2,1)S(1)}, bf16[4,128,512]{2,1,...) custom-call(s32[1]{0:T(128)S(6)} %copy.7.length_ref, ...), custom_call_target="tpu_custom_call" | custom-call | tf_op jit(solution)/shard_map/prepare/pallas_call | solution.py:359
  17.8 0.0 collective-permute-done.3.rest_1_
  17.9 0.9 %suffix_away.1 = (bf16[2,144,128]{2,1,0:T(8,128)(2,1)S(1)}, bf16[2,144,128]{2,1,0:T(8,128)(2,1)S(1)}, bf16[2,144,128]{2,1,0:T(8,128)(2,1)S(1)}, f32[8,128]{1,0:T(8,128)S(1)}) custom-call(bf16[4,512,128]{2,1,0:T(8,128)(2,1)S(1)} %get-tuple-element.26.keys_ref, bf16[4,128,512]{2,1,0:T(8,128)(2,1)S(1)} %get-tuple-element.27.values_ref, ...), custom_call_target="tpu_custom_call" | custom-call | tf_op jit(solution)/shard_map/suffix_away/pallas_call | solution.py:388
  18.7 2.2 %collective-permute-start.5 = (bf16[2,144,128]{2,1,0:T(8,128)(2,1)S(1)}, bf16[2,144,128]{2,1,0:T(8,128)(2,1)S(1)}, u32[]{:S(2)}, u32[]{:S(2)}) collective-permute-start(bf16[2,144,128]{2,1,0:T(8,128)(2,1)S(1)} %get-tuple-element.30), channel_id=1, source_target_pairs={{0,16},{1,17},{4,21},{5,20},{8,24},{9,25},{12,29},{13,28},{16,0},{... | collective-permute-start | bytes 221192 | tf_op jit(solution)/shard_map/ppermute | solution.py:47
  21.0 3.5 %collective-permute-start.7 = (bf16[2,144,128]{2,1,0:T(8,128)(2,1)S(1)}, bf16[2,144,128]{2,1,0:T(8,128)(2,1)S(1)}, u32[]{:S(2)}, u32[]{:S(2)}) collective-permute-start(bf16[2,144,128]{2,1,0:T(8,128)(2,1)S(1)} %get-tuple-element.32), channel_id=1, source_target_pairs={{0,9},{1,8},{4,29},{5,28},{8,1},{9,0},{12,21},{13,20},{16,25},{17,... | collective-permute-start | bytes 221192 | tf_op jit(solution)/shard_map/ppermute | solution.py:47
  24.5 2.5 %home_part.1 = (f32[128,128]{1,0:T(8,128)S(1)}, f32[8,128]{1,0:T(8,128)S(1)}, bf16[144,128]{1,0:T(8,128)(2,1)S(1)}) custom-call(s32[8,256]{1,0:T(8,128)S(1)} %get-tuple-element.33.valid_ref, bf16[1,512,128]{2,1,0:T(8,128)(2,1)S(1)} %get-tuple-element.34.keys_ref, bf16[1,128,512]{2,1,0:T(8,128)(2,1)S(1)} %get-tuple-element.35.values_ref, ...), custom_call_target="tpu_custom_call" | custom-call | flops 536870912 | bytes 2097152 | tf_op jit(solution)/shard_map/home_part/pallas_call | solution.py:399
  27.0 1.0 %collective-permute-start.9 = (bf16[144,128]{1,0:T(8,128)(2,1)S(1)}, bf16[144,128]{1,0:T(8,128)(2,1)S(1)}, u32[]{:S(2)}, u32[]{:S(2)}) collective-permute-start(bf16[144,128]{1,0:T(8,128)(2,1)S(1)} %get-tuple-element.38), channel_id=1, source_target_pairs={{0,1},{1,0},{2,3},{3,2},{4,5},{5,4},{6,7},{7,6},{8,9},{9,8},{10,11... | collective-permute-start | bytes 110600 | tf_op jit(solution)/shard_map/ppermute | solution.py:25
  28.0 0.1 sibling_share.1
  28.1 0.1 collective-permute-start.10
  28.2 1.7 %collective-permute-done.9.rest_3_ = bf16[144,128]{1,0:T(8,128)(2,1)S(1)} collective-permute-done((bf16[144,128]{1,0:T(8,128)(2,1)S(1)}, bf16[144,128]{1,0:T(8,128)(2,1)S(1)}, u32[]{:S(2)}, u32[]{:S(2)}) %collective-permute-start.9) | collective-permute-done | bytes 36896 | tf_op jit(solution)/shard_map/ppermute | solution.py:25
  29.9 0.8 %combine.1 = f32[16,1024]{1,0:T(8,128)} custom-call(bf16[2,144,128]{2,1,0:T(8,128)(2,1)S(1)} %collective-permute-done.5.rest_0_, bf16[2,144,128]{2,1,0:T(8,128)(2,1)S(1)} %collective-permute-done.6.rest_1_, bf16[2,144,128]{2,1,0:T(8,128)(2,1)S(1)} %collective-permute-done.7.rest_2_, bf16[144,128]{1,0:T(8,128)(2,1)S(1)} %collective-permute-done.9.rest_3_, ...), custom_call_target="tpu_custom_call" | custom-call | tf_op jit(solution)/shard_map/combine/pallas_call | solution.py:425
  (11 shorter events, 0.0 us)
Async XLA Ops:
  1.3 0.6 %copy-start = (bf16[16,1024]{1,0:T(8,128)(2,1)}, bf16[16,1024]{1,0:T(8,128)(2,1)S(1)}, u32[]{:S(2)}) copy-start(bf16[16,1024]{1,0:T(8,128)(2,1)S(1)} %get-tuple-element.29.own_ref) | copy-start | bytes 98308
  1.9 13.7 %collective-permute-start = (bf16[32,64,256]{2,1,0:T(8,128)(2,1)S(1)}, bf16[32,64,256]{2,1,0:T(8,128)(2,1)S(1)}, u32[]{:S(2)}, u32[]{:S(2)}) collective-permute-start(bf16[32,64,256]{2,1,0:T(8,128)(2,1)S(1)} %get-tuple-element.25.near), channel_id=1, source_target_pairs={{0,4},{4,0},{1,5},{5,1},{2,6},{6,2},{3,7},{7,3},{8,12},{12,8},{9,1... | collective-permute-start | bytes 3145736 | tf_op jit(solution)/shard_map/ppermute | solution.py:25
  2.0 2.5 %collective-permute-start.1 = (bf16[16,1024]{1,0:T(8,128)(2,1)}, bf16[16,1024]{1,0:T(8,128)(2,1)S(1)}, u32[]{:S(2)}, u32[]{:S(2)}) collective-permute-start(bf16[16,1024]{1,0:T(8,128)(2,1)} %refs_0_.1), channel_id=1, source_target_pairs={{0,4},{4,0},{1,5},{5,1},{2,6},{6,2},{3,7},{7,3},{8,12},{12,8},{9,1... | collective-permute-start | bytes 98312 | tf_op jit(solution)/shard_map/ppermute | solution.py:25
  4.5 0.6 %copy-start.2 = (bf16[16,1024]{1,0:T(8,128)(2,1)}, bf16[16,1024]{1,0:T(8,128)(2,1)S(1)}, u32[]{:S(2)}) copy-start(bf16[16,1024]{1,0:T(8,128)(2,1)S(1)} %collective-permute-done.1.sibling_ref) | copy-start | bytes 98308
  5.9 11.9 %collective-permute-start.2 = (bf16[2,16,1024]{2,1,0:T(8,128)(2,1)S(1)}, bf16[2,16,1024]{2,1,0:T(8,128)(2,1)S(1)}, u32[]{:S(2)}, u32[]{:S(2)}) collective-permute-start(bf16[2,16,1024]{2,1,0:T(8,128)(2,1)S(1)} %both_cores.1), channel_id=1, source_target_pairs={{0,16},{1,17},{4,21},{5,20},{8,24},{9,25},{12,29},{13,28},{16,0},{... | collective-permute-start | bytes 196616 | tf_op jit(solution)/shard_map/ppermute | solution.py:47
  10.5 7.3 %collective-permute-start.3 = (bf16[2,16,1024]{2,1,0:T(8,128)(2,1)S(1)}, bf16[2,16,1024]{2,1,0:T(8,128)(2,1)S(1)}, u32[]{:S(2)}, u32[]{:S(2)}) collective-permute-start(bf16[2,16,1024]{2,1,0:T(8,128)(2,1)S(1)} %both_cores.1), channel_id=1, source_target_pairs={{0,8},{1,9},{4,28},{5,29},{8,0},{9,1},{12,20},{13,21},{16,24},{17,... | collective-permute-start | bytes 196616 | tf_op jit(solution)/shard_map/ppermute | solution.py:47
  11.6 6.3 %collective-permute-start.4 = (bf16[2,16,1024]{2,1,0:T(8,128)(2,1)S(1)}, bf16[2,16,1024]{2,1,0:T(8,128)(2,1)S(1)}, u32[]{:S(2)}, u32[]{:S(2)}) collective-permute-start(bf16[2,16,1024]{2,1,0:T(8,128)(2,1)S(1)} %both_cores.1), channel_id=1, source_target_pairs={{0,9},{1,8},{4,29},{5,28},{8,1},{9,0},{12,21},{13,20},{16,25},{17,... | collective-permute-start | bytes 196616 | tf_op jit(solution)/shard_map/ppermute | solution.py:47
  13.7 10.8 %collective-permute-start.8 = (bf16[16,1024]{1,0:T(8,128)(2,1)}, bf16[16,1024]{1,0:T(8,128)(2,1)S(1)}, u32[]{:S(2)}, u32[]{:S(2)}) collective-permute-start(bf16[16,1024]{1,0:T(8,128)(2,1)} %refs_0_.1), channel_id=1, source_target_pairs={{0,1},{1,0},{2,3},{3,2},{4,5},{5,4},{6,7},{7,6},{8,9},{9,8},{10,11... | collective-permute-start | bytes 98312 | tf_op jit(solution)/shard_map/ppermute | solution.py:25
  15.6 8.9 %copy-start.1 = (bf16[16,1024]{1,0:T(8,128)(2,1)S(1)}, bf16[16,1024]{1,0:T(8,128)(2,1)}, u32[]{:S(2)}) copy-start(bf16[16,1024]{1,0:T(8,128)(2,1)} %copy-done) | copy-start | bytes 98308
  18.7 9.3 %collective-permute-start.5 = (bf16[2,144,128]{2,1,0:T(8,128)(2,1)S(1)}, bf16[2,144,128]{2,1,0:T(8,128)(2,1)S(1)}, u32[]{:S(2)}, u32[]{:S(2)}) collective-permute-start(bf16[2,144,128]{2,1,0:T(8,128)(2,1)S(1)} %get-tuple-element.30), channel_id=1, source_target_pairs={{0,16},{1,17},{4,21},{5,20},{8,24},{9,25},{12,29},{13,28},{16,0},{... | collective-permute-start | bytes 221192 | tf_op jit(solution)/shard_map/ppermute | solution.py:47
  21.0 7.0 %collective-permute-start.6 = (bf16[2,144,128]{2,1,0:T(8,128)(2,1)S(1)}, bf16[2,144,128]{2,1,0:T(8,128)(2,1)S(1)}, u32[]{:S(2)}, u32[]{:S(2)}) collective-permute-start(bf16[2,144,128]{2,1,0:T(8,128)(2,1)S(1)} %get-tuple-element.31), channel_id=1, source_target_pairs={{0,8},{1,9},{4,28},{5,29},{8,0},{9,1},{12,20},{13,21},{16,24},{17,... | collective-permute-start | bytes 221192 | tf_op jit(solution)/shard_map/ppermute | solution.py:47
  21.0 7.0 %collective-permute-start.7 = (bf16[2,144,128]{2,1,0:T(8,128)(2,1)S(1)}, bf16[2,144,128]{2,1,0:T(8,128)(2,1)S(1)}, u32[]{:S(2)}, u32[]{:S(2)}) collective-permute-start(bf16[2,144,128]{2,1,0:T(8,128)(2,1)S(1)} %get-tuple-element.32), channel_id=1, source_target_pairs={{0,9},{1,8},{4,29},{5,28},{8,1},{9,0},{12,21},{13,20},{16,25},{17,... | collective-permute-start | bytes 221192 | tf_op jit(solution)/shard_map/ppermute | solution.py:47
  27.0 2.9 %collective-permute-start.9 = (bf16[144,128]{1,0:T(8,128)(2,1)S(1)}, bf16[144,128]{1,0:T(8,128)(2,1)S(1)}, u32[]{:S(2)}, u32[]{:S(2)}) collective-permute-start(bf16[144,128]{1,0:T(8,128)(2,1)S(1)} %get-tuple-element.38), channel_id=1, source_target_pairs={{0,1},{1,0},{2,3},{3,2},{4,5},{5,4},{6,7},{7,6},{8,9},{9,8},{10,11... | collective-permute-start | bytes 110600 | tf_op jit(solution)/shard_map/ppermute | solution.py:25
  28.1 1.8 %collective-permute-start.10 = (bf16[144,128]{1,0:T(8,128)(2,1)S(1)}, bf16[144,128]{1,0:T(8,128)(2,1)S(1)}, u32[]{:S(2)}, u32[]{:S(2)}) collective-permute-start(bf16[144,128]{1,0:T(8,128)(2,1)S(1)} %sibling_share.1), channel_id=1, source_target_pairs={{0,4},{4,0},{1,5},{5,1},{2,6},{6,2},{3,7},{7,3},{8,12},{12,8},{9,1... | collective-permute-start | bytes 110600 | tf_op jit(solution)/shard_map/ppermute | solution.py:25

commit v15 on v13

--- a/solution.py
+++ b/solution.py
@@ -333,7 +333,8 @@
     tokens = prompt_cache.shape[2]
     rows = block_table.shape[0]
     vmem = pl.BlockSpec(memory_space=pltpu.VMEM)
-    params = pltpu.CompilerParams(vmem_limit_bytes=40 * 2**20)
+    params = pltpu.CompilerParams(vmem_limit_bytes=32 * 2**20)
+    early = pl.CostEstimate(flops=2 * 10**10, bytes_accessed=0, transcendentals=0)
 
     hbm = pl.BlockSpec(memory_space=pltpu.HBM)
     near = pool.reshape(slots, half, width)
@@ -344,6 +345,8 @@
         out_shape=pltpu.VMEM((2,) + queries.shape, jnp.bfloat16),
         in_specs=[vmem] * 2,
         out_specs=vmem,
+        compiler_params=params,
+        cost_estimate=early,
         name="both_cores",
     )(queries, swapped(queries, "core"))
     n_messages = n_req - 1
@@ -387,11 +390,11 @@
         functools.partial(away_kernel, n_messages),
         out_shape=(pltpu.VMEM((2, UNIT_ROWS, VECS), jnp.bfloat16),) * n_messages
         + (pltpu.VMEM((8, VECS), jnp.float32),),
-        in_specs=[vmem] * (4 + n_messages),
+        in_specs=[vmem] * (3 + n_messages),
         out_specs=(vmem,) * (n_messages + 1),
         compiler_params=params,
         name="suffix_away",
-    )(keys, values, member, *messages, other)
+    )(keys, values, member, *messages)
     received = [exchanged(each, k) for k, each in enumerate(units)]
 
     summed, stats, given = pl.pallas_call(

time: 29.6 us -> 27.2 us (0.919)
  waiting for transfers between devices: 9.35 us -> 6.74 us
  starting transfers between devices: 11.8 us -> 12.6 us
  local copies, waits for them, and re-layouts: 0.61 us -> 0 us
    ppermute x5, waiting for transfers between devices: 5.92 us -> 2.22 us  [swapped(): return lax.ppermute(value, axis, [(0, 1), (1, 0)])]
    ppermute x6, starting transfers between devices: 9.52 us -> 10.8 us  [exchanged(): return lax.ppermute(value, ('z', 'core', 'pair'), pairs)]
    ppermute x6, waiting for transfers between devices: 3.43 us -> 4.53 us  [exchanged(): return lax.ppermute(value, ('z', 'core', 'pair'), pairs)]
    unnamed x2 -> x0, local copies, waits for them, and re-layouts: 0.61 us -> none
    ppermute x5, starting transfers between devices: 2.26 us -> 1.78 us  [swapped(): return lax.ppermute(value, axis, [(0, 1), (1, 0)])]
  transfers between devices with their start and end apart: 11 -> 11, of which waited for: 6 -> 6; matrix products, arithmetic and copies ran while one was open for 0% -> 0% of each run, Pallas kernels for 18% -> 23%
where the time goes in v15:
time: 27.2 us; the launch traced here: 27 us
  starting transfers between devices  12.6 us (46%)
  Pallas kernels  6.95 us (26%)
  waiting for transfers between devices  6.74 us (25%)
  between operations  0.72 us (3%)
    ppermute x6, starting transfers between devices, exchanged(): return lax.ppermute(value, ('z', 'core', 'pair'), pairs)  10.8 us
    ppermute x6, waiting for transfers between devices, exchanged(): return lax.ppermute(value, ('z', 'core', 'pair'), pairs)  4.53 us
    pallas_call x1, Pallas kernels, on_device(): pl.pallas_call(home_kernel, out_shape=(pltpu.VMEM((HD, VECS), jnp.float32...  2.52 us
    ppermute x5, waiting for transfers between devices, swapped(): return lax.ppermute(value, axis, [(0, 1), (1, 0)])  2.22 us
    pallas_call x1, Pallas kernels, on_device(): pl.pallas_call(functools.partial(prepare_kernel, capacity), out_shape=(pl...  2 us
    ppermute x5, starting transfers between devices, swapped(): return lax.ppermute(value, axis, [(0, 1), (1, 0)])  1.78 us
    pallas_call x1, Pallas kernels, on_device(): pl.pallas_call(functools.partial(away_kernel, n_messages), out_shape=(plt...  0.86 us
    pallas_call x1, Pallas kernels, on_device(): pl.pallas_call(final_kernel, out_shape=jax.ShapeDtypeStruct((BEAMS, HEADS...  0.77 us
  transfers between devices with their start and end apart: 11, of which 6 were waited for; matrix products, arithmetic and copies ran while one was open for 0% of the time, Pallas kernels for 23%

profile of v15, /device:TPU:0, one launch (start us, length us, event | category | flops | bytes accessed | tf_op | source)
XLA Modules:
  0.0 27.0 jit_solution(4947378456677996226)
XLA Ops:
  0.0 0.5 %collective-permute-start.1 = (bf16[16,1024]{1,0:T(8,128)(2,1)}, bf16[16,1024]{1,0:T(8,128)(2,1)S(1)}, u32[]{:S(2)}, u32[]{:S(2)}) collective-permute-start(bf16[16,1024]{1,0:T(8,128)(2,1)} %own_ref.3), channel_id=1, source_target_pairs={{0,4},{4,0},{1,5},{5,1},{2,6},{6,2},{3,7},{7,3},{8,12},{12,8},{9,1... | collective-permute-start | bytes 98312 | tf_op jit(solution)/shard_map/ppermute | solution.py:25
  0.5 0.1 collective-permute-start
  0.5 1.0 %collective-permute-done.1.sibling_ref = bf16[16,1024]{1,0:T(8,128)(2,1)S(1)} collective-permute-done((bf16[16,1024]{1,0:T(8,128)(2,1)}, bf16[16,1024]{1,0:T(8,128)(2,1)S(1)}, u32[]{:S(2)}, u32[]{:S(2)}) %collective-permute-start.1) | collective-permute-done | bytes 32800 | tf_op jit(solution)/shard_map/ppermute | solution.py:25
  1.5 0.8 %both_cores.1 = bf16[2,16,1024]{2,1,0:T(8,128)(2,1)S(1)} custom-call(bf16[16,1024]{1,0:T(8,128)(2,1)} %own_ref.3, bf16[16,1024]{1,0:T(8,128)(2,1)S(1)} %collective-permute-done.1.sibling_ref), custom_call_target="tpu_custom_call" | custom-call | flops 20000000000 | tf_op jit(solution)/shard_map/both_cores/pallas_call | solution.py:343
  2.3 3.9 %collective-permute-start.2 = (bf16[2,16,1024]{2,1,0:T(8,128)(2,1)S(1)}, bf16[2,16,1024]{2,1,0:T(8,128)(2,1)S(1)}, u32[]{:S(2)}, u32[]{:S(2)}) collective-permute-start(bf16[2,16,1024]{2,1,0:T(8,128)(2,1)S(1)} %both_cores.1), channel_id=1, source_target_pairs={{0,16},{1,17},{4,21},{5,20},{8,24},{9,25},{12,29},{13,28},{16,0},{... | collective-permute-start | bytes 196616 | tf_op jit(solution)/shard_map/ppermute | solution.py:47
  6.2 1.6 %collective-permute-start.3 = (bf16[2,16,1024]{2,1,0:T(8,128)(2,1)S(1)}, bf16[2,16,1024]{2,1,0:T(8,128)(2,1)S(1)}, u32[]{:S(2)}, u32[]{:S(2)}) collective-permute-start(bf16[2,16,1024]{2,1,0:T(8,128)(2,1)S(1)} %both_cores.1), channel_id=1, source_target_pairs={{0,8},{1,9},{4,28},{5,29},{8,0},{9,1},{12,20},{13,21},{16,24},{17,... | collective-permute-start | bytes 196616 | tf_op jit(solution)/shard_map/ppermute | solution.py:47
  7.8 1.4 %collective-permute-start.4 = (bf16[2,16,1024]{2,1,0:T(8,128)(2,1)S(1)}, bf16[2,16,1024]{2,1,0:T(8,128)(2,1)S(1)}, u32[]{:S(2)}, u32[]{:S(2)}) collective-permute-start(bf16[2,16,1024]{2,1,0:T(8,128)(2,1)S(1)} %both_cores.1), channel_id=1, source_target_pairs={{0,9},{1,8},{4,29},{5,28},{8,1},{9,0},{12,21},{13,20},{16,25},{17,... | collective-permute-start | bytes 196616 | tf_op jit(solution)/shard_map/ppermute | solution.py:47
  9.2 0.5 %collective-permute-start.8 = (bf16[16,1024]{1,0:T(8,128)(2,1)}, bf16[16,1024]{1,0:T(8,128)(2,1)S(1)}, u32[]{:S(2)}, u32[]{:S(2)}) collective-permute-start(bf16[16,1024]{1,0:T(8,128)(2,1)} %own_ref.3), channel_id=1, source_target_pairs={{0,1},{1,0},{2,3},{3,2},{4,5},{5,4},{6,7},{7,6},{8,9},{9,8},{10,11... | collective-permute-start | bytes 98312 | tf_op jit(solution)/shard_map/ppermute | solution.py:25
  10.4 0.0 collective-permute-done.far_ref
  10.4 2.0 %prepare.1 = (bf16[1,512,128]{2,1,0:T(8,128)(2,1)S(1)}, bf16[1,128,512]{2,1,0:T(8,128)(2,1)S(1)}, bf16[4,512,128]{2,1,0:T(8,128)(2,1)S(1)}, bf16[4,128,512]{2,1,...) custom-call(s32[1]{0:T(128)S(6)} %copy.7.length_ref, ...), custom_call_target="tpu_custom_call" | custom-call | tf_op jit(solution)/shard_map/prepare/pallas_call | solution.py:355
  12.4 0.8 %collective-permute-done.4.rest_2_ = bf16[2,16,1024]{2,1,0:T(8,128)(2,1)S(1)} collective-permute-done((bf16[2,16,1024]{2,1,0:T(8,128)(2,1)S(1)}, bf16[2,16,1024]{2,1,0:T(8,128)(2,1)S(1)}, u32[]{:S(2)}, u32[]{:S(2)}) %collective-permute-start.4) | collective-permute-done | bytes 65568 | tf_op jit(solution)/shard_map/ppermute | solution.py:47
  13.2 0.9 %suffix_away.1 = (bf16[2,144,128]{2,1,0:T(8,128)(2,1)S(1)}, bf16[2,144,128]{2,1,0:T(8,128)(2,1)S(1)}, bf16[2,144,128]{2,1,0:T(8,128)(2,1)S(1)}, f32[8,128]{1,0:T(8,128)S(1)}) custom-call(bf16[4,512,128]{2,1,0:T(8,128)(2,1)S(1)} %get-tuple-element.20.keys_ref, bf16[4,128,512]{2,1,0:T(8,128)(2,1)S(1)} %get-tuple-element.21.values_ref, ...), custom_call_target="tpu_custom_call" | custom-call | tf_op jit(solution)/shard_map/suffix_away/pallas_call | solution.py:389
  14.1 0.3 %collective-permute-start.5 = (bf16[2,144,128]{2,1,0:T(8,128)(2,1)S(1)}, bf16[2,144,128]{2,1,0:T(8,128)(2,1)S(1)}, u32[]{:S(2)}, u32[]{:S(2)}) collective-permute-start(bf16[2,144,128]{2,1,0:T(8,128)(2,1)S(1)} %get-tuple-element.23), channel_id=1, source_target_pairs={{0,16},{1,17},{4,21},{5,20},{8,24},{9,25},{12,29},{13,28},{16,0},{... | collective-permute-start | bytes 221192 | tf_op jit(solution)/shard_map/ppermute | solution.py:47
  14.4 2.8 %collective-permute-start.6 = (bf16[2,144,128]{2,1,0:T(8,128)(2,1)S(1)}, bf16[2,144,128]{2,1,0:T(8,128)(2,1)S(1)}, u32[]{:S(2)}, u32[]{:S(2)}) collective-permute-start(bf16[2,144,128]{2,1,0:T(8,128)(2,1)S(1)} %get-tuple-element.24), channel_id=1, source_target_pairs={{0,8},{1,9},{4,28},{5,29},{8,0},{9,1},{12,20},{13,21},{16,24},{17,... | collective-permute-start | bytes 221192 | tf_op jit(solution)/shard_map/ppermute | solution.py:47
  17.2 0.9 %collective-permute-start.7 = (bf16[2,144,128]{2,1,0:T(8,128)(2,1)S(1)}, bf16[2,144,128]{2,1,0:T(8,128)(2,1)S(1)}, u32[]{:S(2)}, u32[]{:S(2)}) collective-permute-start(bf16[2,144,128]{2,1,0:T(8,128)(2,1)S(1)} %get-tuple-element.25), channel_id=1, source_target_pairs={{0,9},{1,8},{4,29},{5,28},{8,1},{9,0},{12,21},{13,20},{16,25},{17,... | collective-permute-start | bytes 221192 | tf_op jit(solution)/shard_map/ppermute | solution.py:47
  18.0 0.0 collective-permute-done.8.pair_ref
  18.0 2.5 %home_part.1 = (f32[128,128]{1,0:T(8,128)S(1)}, f32[8,128]{1,0:T(8,128)S(1)}, bf16[144,128]{1,0:T(8,128)(2,1)S(1)}) custom-call(s32[8,256]{1,0:T(8,128)S(1)} %get-tuple-element.26.valid_ref, bf16[1,512,128]{2,1,0:T(8,128)(2,1)S(1)} %get-tuple-element.27.keys_ref, bf16[1,128,512]{2,1,0:T(8,128)(2,1)S(1)} %get-tuple-element.28.values_ref, ...), custom_call_target="tpu_custom_call" | custom-call | flops 536870912 | bytes 2097152 | tf_op jit(solution)/shard_map/home_part/pallas_call | solution.py:400
  20.6 0.7 %collective-permute-start.9 = (bf16[144,128]{1,0:T(8,128)(2,1)S(1)}, bf16[144,128]{1,0:T(8,128)(2,1)S(1)}, u32[]{:S(2)}, u32[]{:S(2)}) collective-permute-start(bf16[144,128]{1,0:T(8,128)(2,1)S(1)} %get-tuple-element.32), channel_id=1, source_target_pairs={{0,1},{1,0},{2,3},{3,2},{4,5},{5,4},{6,7},{7,6},{8,9},{9,8},{10,11... | collective-permute-start | bytes 110600 | tf_op jit(solution)/shard_map/ppermute | solution.py:25
  21.2 0.5 %collective-permute-done.5.rest_0_ = bf16[2,144,128]{2,1,0:T(8,128)(2,1)S(1)} collective-permute-done((bf16[2,144,128]{2,1,0:T(8,128)(2,1)S(1)}, bf16[2,144,128]{2,1,0:T(8,128)(2,1)S(1)}, u32[]{:S(2)}, u32[]{:S(2)}) %collective-permute-start.5) | collective-permute-done | bytes 73760 | tf_op jit(solution)/shard_map/ppermute | solution.py:47
  21.7 3.2 %collective-permute-done.7.rest_2_ = bf16[2,144,128]{2,1,0:T(8,128)(2,1)S(1)} collective-permute-done((bf16[2,144,128]{2,1,0:T(8,128)(2,1)S(1)}, bf16[2,144,128]{2,1,0:T(8,128)(2,1)S(1)}, u32[]{:S(2)}, u32[]{:S(2)}) %collective-permute-start.7) | collective-permute-done | bytes 73760 | tf_op jit(solution)/shard_map/ppermute | solution.py:47
  25.0 0.1 collective-permute-start.10
  25.0 0.2 collective-permute-done.9.rest_3_
  25.2 1.0 %collective-permute-done.10.rest_4_ = bf16[144,128]{1,0:T(8,128)(2,1)S(1)} collective-permute-done((bf16[144,128]{1,0:T(8,128)(2,1)S(1)}, bf16[144,128]{1,0:T(8,128)(2,1)S(1)}, u32[]{:S(2)}, u32[]{:S(2)}) %collective-permute-start.10) | collective-permute-done | bytes 36896 | tf_op jit(solution)/shard_map/ppermute | solution.py:25
  26.2 0.8 %combine.1 = f32[16,1024]{1,0:T(8,128)} custom-call(bf16[2,144,128]{2,1,0:T(8,128)(2,1)S(1)} %collective-permute-done.5.rest_0_, bf16[2,144,128]{2,1,0:T(8,128)(2,1)S(1)} %collective-permute-done.6.rest_1_, bf16[2,144,128]{2,1,0:T(8,128)(2,1)S(1)} %collective-permute-done.7.rest_2_, bf16[144,128]{1,0:T(8,128)(2,1)S(1)} %collective-permute-done.9.rest_3_, ...), custom_call_target="tpu_custom_call" | custom-call | tf_op jit(solution)/shard_map/combine/pallas_call | solution.py:426
  (4 shorter events, 0.1 us)
Async XLA Ops:
  0.0 1.5 %collective-permute-start.1 = (bf16[16,1024]{1,0:T(8,128)(2,1)}, bf16[16,1024]{1,0:T(8,128)(2,1)S(1)}, u32[]{:S(2)}, u32[]{:S(2)}) collective-permute-start(bf16[16,1024]{1,0:T(8,128)(2,1)} %own_ref.3), channel_id=1, source_target_pairs={{0,4},{4,0},{1,5},{5,1},{2,6},{6,2},{3,7},{7,3},{8,12},{12,8},{9,1... | collective-permute-start | bytes 98312 | tf_op jit(solution)/shard_map/ppermute | solution.py:25
  0.5 9.9 %collective-permute-start = (bf16[32,64,256]{2,1,0:T(8,128)(2,1)}, bf16[32,64,256]{2,1,0:T(8,128)(2,1)S(1)}, u32[]{:S(2)}, u32[]{:S(2)}) collective-permute-start(bf16[32,64,256]{2,1,0:T(8,128)(2,1)} %bitcast.5), channel_id=1, source_target_pairs={{0,4},{4,0},{1,5},{5,1},{2,6},{6,2},{3,7},{7,3},{8,12},{12,8},{9,1... | collective-permute-start | bytes 3145736 | tf_op jit(solution)/shard_map/ppermute | solution.py:25
  2.3 10.1 %collective-permute-start.2 = (bf16[2,16,1024]{2,1,0:T(8,128)(2,1)S(1)}, bf16[2,16,1024]{2,1,0:T(8,128)(2,1)S(1)}, u32[]{:S(2)}, u32[]{:S(2)}) collective-permute-start(bf16[2,16,1024]{2,1,0:T(8,128)(2,1)S(1)} %both_cores.1), channel_id=1, source_target_pairs={{0,16},{1,17},{4,21},{5,20},{8,24},{9,25},{12,29},{13,28},{16,0},{... | collective-permute-start | bytes 196616 | tf_op jit(solution)/shard_map/ppermute | solution.py:47
  6.2 6.2 %collective-permute-start.3 = (bf16[2,16,1024]{2,1,0:T(8,128)(2,1)S(1)}, bf16[2,16,1024]{2,1,0:T(8,128)(2,1)S(1)}, u32[]{:S(2)}, u32[]{:S(2)}) collective-permute-start(bf16[2,16,1024]{2,1,0:T(8,128)(2,1)S(1)} %both_cores.1), channel_id=1, source_target_pairs={{0,8},{1,9},{4,28},{5,29},{8,0},{9,1},{12,20},{13,21},{16,24},{17,... | collective-permute-start | bytes 196616 | tf_op jit(solution)/shard_map/ppermute | solution.py:47
  7.8 5.4 %collective-permute-start.4 = (bf16[2,16,1024]{2,1,0:T(8,128)(2,1)S(1)}, bf16[2,16,1024]{2,1,0:T(8,128)(2,1)S(1)}, u32[]{:S(2)}, u32[]{:S(2)}) collective-permute-start(bf16[2,16,1024]{2,1,0:T(8,128)(2,1)S(1)} %both_cores.1), channel_id=1, source_target_pairs={{0,9},{1,8},{4,29},{5,28},{8,1},{9,0},{12,21},{13,20},{16,25},{17,... | collective-permute-start | bytes 196616 | tf_op jit(solution)/shard_map/ppermute | solution.py:47
  9.2 8.9 %collective-permute-start.8 = (bf16[16,1024]{1,0:T(8,128)(2,1)}, bf16[16,1024]{1,0:T(8,128)(2,1)S(1)}, u32[]{:S(2)}, u32[]{:S(2)}) collective-permute-start(bf16[16,1024]{1,0:T(8,128)(2,1)} %own_ref.3), channel_id=1, source_target_pairs={{0,1},{1,0},{2,3},{3,2},{4,5},{5,4},{6,7},{7,6},{8,9},{9,8},{10,11... | collective-permute-start | bytes 98312 | tf_op jit(solution)/shard_map/ppermute | solution.py:25
  14.1 7.6 %collective-permute-start.5 = (bf16[2,144,128]{2,1,0:T(8,128)(2,1)S(1)}, bf16[2,144,128]{2,1,0:T(8,128)(2,1)S(1)}, u32[]{:S(2)}, u32[]{:S(2)}) collective-permute-start(bf16[2,144,128]{2,1,0:T(8,128)(2,1)S(1)} %get-tuple-element.23), channel_id=1, source_target_pairs={{0,16},{1,17},{4,21},{5,20},{8,24},{9,25},{12,29},{13,28},{16,0},{... | collective-permute-start | bytes 221192 | tf_op jit(solution)/shard_map/ppermute | solution.py:47
  14.4 7.3 %collective-permute-start.6 = (bf16[2,144,128]{2,1,0:T(8,128)(2,1)S(1)}, bf16[2,144,128]{2,1,0:T(8,128)(2,1)S(1)}, u32[]{:S(2)}, u32[]{:S(2)}) collective-permute-start(bf16[2,144,128]{2,1,0:T(8,128)(2,1)S(1)} %get-tuple-element.24), channel_id=1, source_target_pairs={{0,8},{1,9},{4,28},{5,29},{8,0},{9,1},{12,20},{13,21},{16,24},{17,... | collective-permute-start | bytes 221192 | tf_op jit(solution)/shard_map/ppermute | solution.py:47
  17.2 7.7 %collective-permute-start.7 = (bf16[2,144,128]{2,1,0:T(8,128)(2,1)S(1)}, bf16[2,144,128]{2,1,0:T(8,128)(2,1)S(1)}, u32[]{:S(2)}, u32[]{:S(2)}) collective-permute-start(bf16[2,144,128]{2,1,0:T(8,128)(2,1)S(1)} %get-tuple-element.25), channel_id=1, source_target_pairs={{0,9},{1,8},{4,29},{5,28},{8,1},{9,0},{12,21},{13,20},{16,25},{17,... | collective-permute-start | bytes 221192 | tf_op jit(solution)/shard_map/ppermute | solution.py:47
  20.6 4.7 %collective-permute-start.9 = (bf16[144,128]{1,0:T(8,128)(2,1)S(1)}, bf16[144,128]{1,0:T(8,128)(2,1)S(1)}, u32[]{:S(2)}, u32[]{:S(2)}) collective-permute-start(bf16[144,128]{1,0:T(8,128)(2,1)S(1)} %get-tuple-element.32), channel_id=1, source_target_pairs={{0,1},{1,0},{2,3},{3,2},{4,5},{5,4},{6,7},{7,6},{8,9},{9,8},{10,11... | collective-permute-start | bytes 110600 | tf_op jit(solution)/shard_map/ppermute | solution.py:25
  25.0 1.3 %collective-permute-start.10 = (bf16[144,128]{1,0:T(8,128)(2,1)S(1)}, bf16[144,128]{1,0:T(8,128)(2,1)S(1)}, u32[]{:S(2)}, u32[]{:S(2)}) collective-permute-start(bf16[144,128]{1,0:T(8,128)(2,1)S(1)} %sibling_share.1), channel_id=1, source_target_pairs={{0,4},{4,0},{1,5},{5,1},{2,6},{6,2},{3,7},{7,3},{8,12},{12,8},{9,1... | collective-permute-start | bytes 110600 | tf_op jit(solution)/shard_map/ppermute | solution.py:25

commit v16 on v14

--- a/solution.py
+++ b/solution.py
@@ -14,7 +14,6 @@
 HEADS = GROUP // 2
 VECS = HEADS * BEAMS
 STAT_ROWS = 16
-UNIT_ROWS = HD + STAT_ROWS
 CHUNK = 512
 
 big_negative = -1e30
@@ -54,11 +53,9 @@
 
 
 def stage_kernel(*refs):
-    half = (len(refs) - 1) // 2
-    sources, targets, sems = refs[:half], refs[half:-1], refs[-1]
+    n = (len(refs) - 1) // 2
     copies = [
-        pltpu.make_async_copy(source, target, sems.at[i])
-        for i, (source, target) in enumerate(zip(sources, targets))
+        pltpu.make_async_copy(refs[i], refs[n + i], refs[-1].at[i]) for i in range(n)
     ]
     for copy in copies:
         copy.start()
@@ -115,18 +112,24 @@
     return [first, second, rest - second]
 
 
-def store_unit(ref, top, total, summed):
-    ref[:HD, :] = summed.astype(jnp.bfloat16)
-    rows = three_pieces(top) + three_pieces(total)
+def store_units(ref, parts):
+    rows = []
+    for i, (top, total, summed) in enumerate(parts):
+        ref[i * HD : (i + 1) * HD, :] = summed.astype(jnp.bfloat16)
+        rows += three_pieces(top) + three_pieces(total)
     rows.append(jnp.zeros((STAT_ROWS - len(rows), VECS), jnp.float32))
-    ref[HD:, :] = jnp.concatenate(rows, axis=0).astype(jnp.bfloat16)
-
-
-def load_unit(ref):
-    stats = ref[HD:, :].astype(jnp.float32)
-    top = stats[0:1] + stats[1:2] + stats[2:3]
-    total = stats[3:4] + stats[4:5] + stats[5:6]
-    return top, total, ref[:HD, :].astype(jnp.float32)
+    ref[len(parts) * HD :, :] = jnp.concatenate(rows, axis=0).astype(jnp.bfloat16)
+
+
+def load_unit(ref, i=0):
+    sums = ref.shape[0] - STAT_ROWS
+    stats = ref[sums:, :].astype(jnp.float32)
+    if isinstance(i, int):
+        rows = [stats[6 * i + k : 6 * i + k + 1] for k in range(6)]
+    else:
+        rows = [jnp.where(i == 0, stats[k : k + 1], stats[6 + k : 7 + k]) for k in range(6)]
+    part = ref[pl.ds(pl.multiple_of(i * HD, HD), HD), :]
+    return rows[0] + rows[1] + rows[2], rows[3] + rows[4] + rows[5], part.astype(jnp.float32)
 
 
 def count(left, right):
@@ -139,7 +142,10 @@
     return lax.broadcasted_iota(jnp.int32, shape, axis)
 
 
-def prompt_part(valid, prompt_ref, vectors):
+def prompt_part(length, half, prompt_ref, vectors):
+    parity = lax.axis_index("pair")
+    whole = lax.div(length, 2 * half)
+    valid = whole * half + jnp.clip(length - whole * (2 * half) - parity * half, 0, half)
     chunks = [slice(i, i + CHUNK) for i in range(0, prompt_ref.shape[0], CHUNK)]
     scores = [scores_of(prompt_ref[chunk, :HD], vectors) for chunk in chunks]
     place = iota(scores[0].shape, 0)
@@ -158,9 +164,9 @@
 
 
 def prepare_kernel(
-    capacity, length_ref, prompt_ref, table, parents, near, far_ref,
-    home_keys_ref, home_values_ref, keys_ref, values_ref, member_ref, held_ref, valid_ref,
-    rows_ref, sem,
+    capacity, near_ref, prompt_ref, table, parents, far_ref,
+    home_keys_ref, home_values_ref, keys_ref, values_ref, member_ref, held_ref,
+    rows_ref, near, sems,
 ):
     n_req = lax.axis_size("z")
     slots, half, _ = near.shape
@@ -168,14 +174,12 @@
     n_batch = rows // BEAMS
     z, core = lax.axis_index("z"), lax.axis_index("core")
 
-    copy = pltpu.make_async_copy(prompt_ref, held_ref, sem)
-    copy.start()
-
-    length = length_ref[0]
-    whole = lax.div(length, 2 * half)
-    parity = lax.axis_index("pair")
-    valid = whole * half + jnp.clip(length - whole * (2 * half) - parity * half, 0, half)
-    valid_ref[...] = jnp.full(valid_ref.shape, valid, jnp.int32)
+    copies = [
+        pltpu.make_async_copy(near_ref, near, sems.at[0]),
+        pltpu.make_async_copy(prompt_ref, held_ref, sems.at[1]),
+    ]
+    for copy in copies:
+        copy.start()
 
     slot = iota((2 * slots, rows), 0)
     mine = slot < slots
@@ -199,6 +203,7 @@
         found.append(jnp.sum(jnp.where(chosen, place + 1, 0), axis=0, keepdims=True))
     found = jnp.concatenate(found, axis=0)
 
+    copies[0].wait()
     requests = [z * 2 + core]
     for mask in masks_here(n_req):
         requests += [(z ^ mask) * 2, (z ^ mask) * 2 + 1]
@@ -229,17 +234,17 @@
         else:
             values_ref[i - 1] = values
 
-    copy.wait()
+    copies[1].wait()
 
 
 def all_vectors(own_ref, pair_ref):
     return jnp.concatenate([stacked_heads(own_ref[...]), stacked_heads(pair_ref[...])], axis=0)
 
 
-def suffix_parts(vectors, keys_ref, values_ref, members):
+def suffix_parts(vectors, keys_ref, values_ref, members, place=0):
     n_slots = members[0].shape[0]
     half = keys_ref.shape[1] // n_slots
-    scores = [scores_of(keys_ref[i], each) for i, each in enumerate(vectors)]
+    scores = [scores_of(keys_ref[place + i], each) for i, each in enumerate(vectors)]
     softmaxes = []
     for member, score in zip(members, scores):
         member = jnp.concatenate([member] * (score.shape[1] // VECS), axis=1)
@@ -255,7 +260,7 @@
             top,
             total,
             jnp.dot(
-                values_ref[i], weights.astype(jnp.bfloat16), preferred_element_type=jnp.float32
+                values_ref[place + i], weights.astype(jnp.bfloat16), preferred_element_type=jnp.float32
             ),
         )
         for i, (top, total, weights) in enumerate(softmaxes)
@@ -267,48 +272,37 @@
     return [x[:, lanes] for x in part]
 
 
-def away_kernel(n_messages, keys_ref, values_ref, member_ref, *rest):
-    messages, units, after_ref = rest[:n_messages], rest[-n_messages - 1 : -1], rest[-1]
+def away_kernel(place, keys_ref, values_ref, member_ref, message_ref, out_ref, after_ref):
     after_ref[...] = jnp.zeros(after_ref.shape, jnp.float32)
-    vectors = [stacked_heads(messages[0][core]) for core in range(2)]
-    for k in range(1, n_messages, 2):
-        for core in range(2):
-            halves = [stacked_heads(messages[k + side][core]) for side in range(2)]
-            vectors.append(jnp.concatenate(halves, axis=0))
-    members = [member_ref[1 + i] for i in range(len(vectors))]
-    parts = suffix_parts(vectors, keys_ref, values_ref, members)
-    for i, part in enumerate(parts):
-        core = i % 2
-        if i < 2:
-            store_unit(units[0].at[core], *part)
-        else:
-            for side in range(2):
-                store_unit(units[i // 2 * 2 - 1 + side].at[core], *half_of(part, side))
+    vectors = [stacked_heads(message_ref[core]) for core in range(2)]
+    members = [member_ref[1 + place + core] for core in range(2)]
+    store_units(out_ref, suffix_parts(vectors, keys_ref, values_ref, members, place))
 
 
 def home_kernel(
-    valid_ref, keys_ref, values_ref, member_ref, own_ref, pair_ref, prompt_ref, after_ref,
+    length_ref, keys_ref, values_ref, member_ref, own_ref, pair_ref, prompt_ref, after_ref,
     summed_ref, stats_ref, out_ref,
 ):
     vectors = all_vectors(own_ref, pair_ref)
+    half = keys_ref.shape[1] // member_ref.shape[1]
     (suffix,) = suffix_parts([vectors], keys_ref, values_ref, [member_ref[0]])
-    prompt = prompt_part(valid_ref[0:1, :], prompt_ref, vectors)
+    prompt = prompt_part(length_ref[0], half, prompt_ref, vectors)
     part = merged([prompt, suffix])
     top, total, summed_ref[...] = half_of(part, 0)
     stats_ref[...] = jnp.concatenate([top, total, jnp.zeros((6, VECS), jnp.float32)], axis=0)
-    store_unit(out_ref, *half_of(part, 1))
+    store_units(out_ref, [half_of(part, 1)])
 
 
 def sibling_kernel(*rest):
     units, out_ref = rest[:-1], rest[-1]
     core = lax.axis_index("core")
-    store_unit(out_ref, *merged([load_unit(unit.at[1 - core]) for unit in units]))
+    store_units(out_ref, [merged([load_unit(unit, 1 - core) for unit in units])])
 
 
 def final_kernel(*rest):
     units, (last_ref, shared_ref, summed_ref, stats_ref, out_ref) = rest[:-5], rest[-5:]
     core = lax.axis_index("core")
-    parts = [load_unit(unit.at[core]) for unit in units]
+    parts = [load_unit(unit, core) for unit in units]
     parts += [load_unit(last_ref), load_unit(shared_ref)]
     parts.append((stats_ref[0:1], stats_ref[1:2], summed_ref[...]))
     _, total, summed = merged(parts)
@@ -330,12 +324,15 @@
     tokens = prompt_cache.shape[2]
     rows = block_table.shape[0]
     vmem = pl.BlockSpec(memory_space=pltpu.VMEM)
-    params = pltpu.CompilerParams(vmem_limit_bytes=40 * 2**20)
+    params = pltpu.CompilerParams(vmem_limit_bytes=32 * 2**20)
+    early = pl.CostEstimate(flops=2 * 10**10, bytes_accessed=0, transcendentals=0)
 
     hbm = pl.BlockSpec(memory_space=pltpu.HBM)
-    sibling = swapped(queries, "core")
-    staged = [queries, pool.reshape(slots, half, width), block_table.T, parents.reshape(1, rows)]
-    own, near, table, row_parents = pl.pallas_call(
+    near = pool.reshape(slots, half, width)
+    far = swapped(near, "core")
+    other = swapped(queries, "pair")
+    staged = [queries, block_table.T, parents.reshape(1, rows)]
+    own, table, row_parents = pl.pallas_call(
         stage_kernel,
         out_shape=tuple(pltpu.VMEM(each.shape, each.dtype) for each in staged),
         in_specs=[hbm] * len(staged),
@@ -344,19 +341,19 @@
         compiler_params=params,
         name="stage",
     )(*[in_hbm(each) for each in staged])
-    far = swapped(near, "core")
-    other = swapped(queries, "pair")
     both = pl.pallas_call(
         pack_kernel,
         out_shape=pltpu.VMEM((2,) + queries.shape, jnp.bfloat16),
         in_specs=[vmem] * 2,
         out_specs=vmem,
+        compiler_params=params,
+        cost_estimate=early,
         name="both_cores",
-    )(own, sibling)
+    )(own, swapped(queries, "core"))
     n_messages = n_req - 1
     messages = [exchanged(both, k) for k in range(n_messages)]
 
-    home_keys, home_values, keys, values, member, prompt, valid = pl.pallas_call(
+    home_keys, home_values, keys, values, member, prompt = pl.pallas_call(
         functools.partial(prepare_kernel, capacity),
         out_shape=(
             pltpu.VMEM((1, 2 * capacity * half, HD), jnp.bfloat16),
@@ -365,57 +362,59 @@
             pltpu.VMEM((n_req, HD, 2 * capacity * half), jnp.bfloat16),
             pltpu.VMEM((1 + n_req, 2 * capacity, VECS), jnp.float32),
             pltpu.VMEM((tokens, width), jnp.bfloat16),
-            pltpu.VMEM((8, 2 * VECS), jnp.int32),
         ),
-        in_specs=[pl.BlockSpec(memory_space=pltpu.SMEM), hbm] + [vmem] * 4,
-        out_specs=(vmem,) * 7,
+        in_specs=[hbm] * 2 + [vmem] * 3,
+        out_specs=(vmem,) * 6,
         scratch_shapes=[
             pltpu.VMEM((2 * slots + 8, VECS), jnp.float32),
-            pltpu.SemaphoreType.DMA,
+            pltpu.VMEM((slots, half, width), jnp.bfloat16),
+            pltpu.SemaphoreType.DMA((2,)),
         ],
         compiler_params=params,
         name="prepare",
     )(
-        lengths,
+        in_hbm(near),
         in_hbm(prompt_cache.reshape(tokens, width)),
         table,
         row_parents,
-        near,
         far,
     )
 
-    unit = pltpu.VMEM((UNIT_ROWS, VECS), jnp.bfloat16)
-    *units, after = pl.pallas_call(
-        functools.partial(away_kernel, n_messages),
-        out_shape=(pltpu.VMEM((2, UNIT_ROWS, VECS), jnp.bfloat16),) * n_messages
-        + (pltpu.VMEM((8, VECS), jnp.float32),),
-        in_specs=[vmem] * (3 + n_messages),
-        out_specs=(vmem,) * (n_messages + 1),
-        compiler_params=params,
-        name="suffix_away",
-    )(keys, values, member, *messages)
-    received = [exchanged(each, k) for k, each in enumerate(units)]
+    received = []
+    for k, message in reversed(list(enumerate(messages))):
+        units, after = pl.pallas_call(
+            functools.partial(away_kernel, 2 * ((k + 1) // 2)),
+            out_shape=(
+                pltpu.VMEM((2 * HD + STAT_ROWS, VECS), jnp.bfloat16),
+                pltpu.VMEM((8, VECS), jnp.float32),
+            ),
+            in_specs=[vmem] * 4,
+            out_specs=(vmem,) * 2,
+            compiler_params=params,
+            name="suffix_away",
+        )(keys, values, member, message)
+        received.append(exchanged(units, k))
 
     summed, stats, given = pl.pallas_call(
         home_kernel,
         out_shape=(
             pltpu.VMEM((HD, VECS), jnp.float32),
             pltpu.VMEM((8, VECS), jnp.float32),
-            pltpu.VMEM((UNIT_ROWS, VECS), jnp.bfloat16),
+            pltpu.VMEM((HD + STAT_ROWS, VECS), jnp.bfloat16),
         ),
-        in_specs=[vmem] * 8,
+        in_specs=[pl.BlockSpec(memory_space=pltpu.SMEM)] + [vmem] * 7,
         out_specs=(vmem,) * 3,
         compiler_params=params,
         cost_estimate=pl.CostEstimate(
             flops=8 * tokens * VECS * HD, bytes_accessed=2 * tokens * width, transcendentals=0
         ),
         name="home_part",
-    )(valid, home_keys, home_values, member, own, other, prompt, after)
+    )(lengths, home_keys, home_values, member, own, other, prompt, after)
     last = swapped(given, "pair")
 
     share = pl.pallas_call(
         sibling_kernel,
-        out_shape=unit,
+        out_shape=pltpu.VMEM((HD + STAT_ROWS, VECS), jnp.bfloat16),
         in_specs=[vmem] * n_messages,
         out_specs=vmem,
         compiler_params=params,

time: 30.9 us -> 26.2 us (0.85)
  the two profiles are of different devices: /device:TPU:1 before, /device:TPU:0 now
where the time goes in v16:
time: 26.2 us; the launch traced here: 26 us
  starting transfers between devices  14 us (53%)
  Pallas kernels  8.44 us (32%)
  waiting for transfers between devices  2.84 us (11%)
  between operations  0.72 us (3%)
    ppermute x6, starting transfers between devices, exchanged(): return lax.ppermute(value, ('z', 'core', 'pair'), pairs)  11.3 us
    ppermute x5, starting transfers between devices, swapped(): return lax.ppermute(value, axis, [(0, 1), (1, 0)])  2.64 us
    pallas_call x3, Pallas kernels, on_device(): pl.pallas_call(functools.partial(away_kernel, 2 * ((k + 1) // 2)), out_sh...  2.44 us
    pallas_call x1, Pallas kernels, on_device(): pl.pallas_call(home_kernel, out_shape=(pltpu.VMEM((HD, VECS), jnp.float32...  2.44 us
    pallas_call x1, Pallas kernels, on_device(): pl.pallas_call(functools.partial(prepare_kernel, capacity), out_shape=(pl...  1.95 us
    ppermute x5, waiting for transfers between devices, swapped(): return lax.ppermute(value, axis, [(0, 1), (1, 0)])  1.62 us
    ppermute x6, waiting for transfers between devices, exchanged(): return lax.ppermute(value, ('z', 'core', 'pair'), pairs)  1.23 us
    pallas_call x1, Pallas kernels, on_device(): pl.pallas_call(stage_kernel, out_shape=tuple((pltpu.VMEM(each.shape, each...  0.79 us
  transfers between devices with their start and end apart: 11, of which 3 were waited for; matrix products, arithmetic and copies ran while one was open for 0% of the time, Pallas kernels for 30%

profile of v16, /device:TPU:0, one launch (start us, length us, event | category | flops | bytes accessed | tf_op | source)
XLA Modules:
  0.0 26.0 jit_solution(8200292517946703884)
XLA Ops:
  0.0 0.5 %collective-permute-start.1 = (bf16[16,1024]{1,0:T(8,128)(2,1)}, bf16[16,1024]{1,0:T(8,128)(2,1)S(1)}, u32[]{:S(2)}, u32[]{:S(2)}) collective-permute-start(bf16[16,1024]{1,0:T(8,128)(2,1)} %refs_0_.1), channel_id=1, source_target_pairs={{0,4},{4,0},{1,5},{5,1},{2,6},{6,2},{3,7},{7,3},{8,12},{12,8},{9,1... | collective-permute-start | bytes 98312 | tf_op jit(solution)/shard_map/ppermute | solution.py:24
  0.5 0.1 collective-permute-start
  0.5 0.8 %stage.1 = (bf16[16,1024]{1,0:T(8,128)(2,1)S(1)}, s32[4,128]{1,0:T(4,128)S(1)}, s32[1,128]{1,0:T(1,128)S(1)}) custom-call(bf16[16,1024]{1,0:T(8,128)(2,1)} %refs_0_.1, s32[4,128]{1,0:T(4,128)} %bitcast.7, s32[1,128]{1,0:T(1,128)} %bitcast.8), custom_call_target="tpu_custom_call" | custom-call | tf_op jit(solution)/shard_map/stage/pallas_call | solution.py:335
  1.3 0.2 collective-permute-done.1.sibling_ref
  1.5 4.0 %collective-permute-start.6 = (bf16[2,16,1024]{2,1,0:T(8,128)(2,1)S(1)}, bf16[2,16,1024]{2,1,0:T(8,128)(2,1)S(1)}, u32[]{:S(2)}, u32[]{:S(2)}) collective-permute-start(bf16[2,16,1024]{2,1,0:T(8,128)(2,1)S(1)} %both_cores.1), channel_id=1, source_target_pairs={{0,16},{1,17},{4,21},{5,20},{8,24},{9,25},{12,29},{13,28},{16,0},{... | collective-permute-start | bytes 196616 | tf_op jit(solution)/shard_map/ppermute | solution.py:46
  5.5 1.6 %collective-permute-start.4 = (bf16[2,16,1024]{2,1,0:T(8,128)(2,1)S(1)}, bf16[2,16,1024]{2,1,0:T(8,128)(2,1)S(1)}, u32[]{:S(2)}, u32[]{:S(2)}) collective-permute-start(bf16[2,16,1024]{2,1,0:T(8,128)(2,1)S(1)} %both_cores.1), channel_id=1, source_target_pairs={{0,8},{1,9},{4,28},{5,29},{8,0},{9,1},{12,20},{13,21},{16,24},{17,... | collective-permute-start | bytes 196616 | tf_op jit(solution)/shard_map/ppermute | solution.py:46
  7.1 1.4 %collective-permute-start.2 = (bf16[2,16,1024]{2,1,0:T(8,128)(2,1)S(1)}, bf16[2,16,1024]{2,1,0:T(8,128)(2,1)S(1)}, u32[]{:S(2)}, u32[]{:S(2)}) collective-permute-start(bf16[2,16,1024]{2,1,0:T(8,128)(2,1)S(1)} %both_cores.1), channel_id=1, source_target_pairs={{0,9},{1,8},{4,29},{5,28},{8,1},{9,0},{12,21},{13,20},{16,25},{17,... | collective-permute-start | bytes 196616 | tf_op jit(solution)/shard_map/ppermute | solution.py:46
  8.5 0.5 %collective-permute-start.8 = (bf16[16,1024]{1,0:T(8,128)(2,1)S(1)}, bf16[16,1024]{1,0:T(8,128)(2,1)S(1)}, u32[]{:S(2)}, u32[]{:S(2)}) collective-permute-start(bf16[16,1024]{1,0:T(8,128)(2,1)S(1)} %copy-done), channel_id=1, source_target_pairs={{0,1},{1,0},{2,3},{3,2},{4,5},{5,4},{6,7},{7,6},{8,9},{9,8},{10,11... | collective-permute-start | bytes 98312 | tf_op jit(solution)/shard_map/ppermute | solution.py:24
  9.0 0.0 collective-permute-done.far_ref
  9.0 2.0 %prepare.1 = (bf16[1,512,128]{2,1,0:T(8,128)(2,1)S(1)}, bf16[1,128,512]{2,1,0:T(8,128)(2,1)S(1)}, bf16[4,512,128]{2,1,0:T(8,128)(2,1)S(1)}, bf16[4,128,512]{2,1,...) custom-call(bf16[32,64,256]{2,1,0:T(8,128)(2,1)} %bitcast.6, bf16[4096,256]{1,0:T(8,128)(2,1)} %bitcast.4, ...), custom_call_target="tpu_custom_call" | custom-call | tf_op jit(solution)/shard_map/prepare/pallas_call | solution.py:356
  11.0 0.0 collective-permute-done.6.message_ref
  11.0 0.5 %suffix_away.5 = (bf16[272,128]{1,0:T(8,128)(2,1)S(1)}, f32[8,128]{1,0:T(8,128)S(1)}) custom-call(bf16[4,512,128]{2,1,0:T(8,128)(2,1)S(1)} %get-tuple-element.23.keys_ref, bf16[4,128,512]{2,1,0:T(8,128)(2,1)S(1)} %get-tuple-element.24.values_ref, f32[5,8,128]{2,1,0:T(8,128)S(1)} %get-tuple-element.25.member_ref, ...), custom_call_target="tpu_custom_call" | custom-call | tf_op jit(solution)/shard_map/suffix_away/pallas_call | solution.py:385
  11.5 0.4 %collective-permute-start.7 = (bf16[272,128]{1,0:T(8,128)(2,1)S(1)}, bf16[272,128]{1,0:T(8,128)(2,1)S(1)}, u32[]{:S(2)}, u32[]{:S(2)}) collective-permute-start(bf16[272,128]{1,0:T(8,128)(2,1)S(1)} %get-tuple-element.29), channel_id=1, source_target_pairs={{0,16},{1,17},{4,21},{5,20},{8,24},{9,25},{12,29},{13,28},{16,0},{... | collective-permute-start | bytes 208904 | tf_op jit(solution)/shard_map/ppermute | solution.py:46
  12.0 0.0 collective-permute-done.4.message_ref
  12.0 1.0 %suffix_away.4 = (bf16[272,128]{1,0:T(8,128)(2,1)S(1)}, f32[8,128]{1,0:T(8,128)}) custom-call(bf16[4,512,128]{2,1,0:T(8,128)(2,1)S(1)} %get-tuple-element.23.keys_ref, bf16[4,128,512]{2,1,0:T(8,128)(2,1)S(1)} %get-tuple-element.24.values_ref, f32[5,8,128]{2,1,0:T(8,128)S(1)} %get-tuple-element.25.member_ref, ...), custom_call_target="tpu_custom_call" | custom-call | tf_op jit(solution)/shard_map/suffix_away/pallas_call | solution.py:385
  12.9 3.9 %collective-permute-start.5 = (bf16[272,128]{1,0:T(8,128)(2,1)S(1)}, bf16[272,128]{1,0:T(8,128)(2,1)S(1)}, u32[]{:S(2)}, u32[]{:S(2)}) collective-permute-start(bf16[272,128]{1,0:T(8,128)(2,1)S(1)} %get-tuple-element.28), channel_id=1, source_target_pairs={{0,8},{1,9},{4,28},{5,29},{8,0},{9,1},{12,20},{13,21},{16,24},{17,... | collective-permute-start | bytes 208904 | tf_op jit(solution)/shard_map/ppermute | solution.py:46
  16.9 0.0 collective-permute-done.2.message_ref
  16.9 1.0 %suffix_away.3 = (bf16[272,128]{1,0:T(8,128)(2,1)S(1)}, f32[8,128]{1,0:T(8,128)}) custom-call(bf16[4,512,128]{2,1,0:T(8,128)(2,1)S(1)} %get-tuple-element.23.keys_ref, bf16[4,128,512]{2,1,0:T(8,128)(2,1)S(1)} %get-tuple-element.24.values_ref, f32[5,8,128]{2,1,0:T(8,128)S(1)} %get-tuple-element.25.member_ref, ...), custom_call_target="tpu_custom_call" | custom-call | tf_op jit(solution)/shard_map/suffix_away/pallas_call | solution.py:385
  18.5 2.4 %home_part.1 = (f32[128,128]{1,0:T(8,128)S(1)}, f32[8,128]{1,0:T(8,128)S(1)}, bf16[144,128]{1,0:T(8,128)(2,1)S(1)}) custom-call(s32[1]{0:T(128)S(6)} %copy.7.length_ref, bf16[1,512,128]{2,1,0:T(8,128)(2,1)S(1)} %get-tuple-element.30.keys_ref, bf16[1,128,512]{2,1,0:T(8,128)(2,1)S(1)} %get-tuple-element.31.values_ref, ...), custom_call_target="tpu_custom_call" | custom-call | flops 536870912 | bytes 2097152 | tf_op jit(solution)/shard_map/home_part/pallas_call | solution.py:398
  21.0 1.5 %collective-permute-start.9 = (bf16[144,128]{1,0:T(8,128)(2,1)S(1)}, bf16[144,128]{1,0:T(8,128)(2,1)S(1)}, u32[]{:S(2)}, u32[]{:S(2)}) collective-permute-start(bf16[144,128]{1,0:T(8,128)(2,1)S(1)} %get-tuple-element.34), channel_id=1, source_target_pairs={{0,1},{1,0},{2,3},{3,2},{4,5},{5,4},{6,7},{7,6},{8,9},{9,8},{10,11... | collective-permute-start | bytes 110600 | tf_op jit(solution)/shard_map/ppermute | solution.py:24
  22.5 1.2 %collective-permute-done.3.rest_0_ = bf16[272,128]{1,0:T(8,128)(2,1)S(1)} collective-permute-done((bf16[272,128]{1,0:T(8,128)(2,1)S(1)}, bf16[272,128]{1,0:T(8,128)(2,1)S(1)}, u32[]{:S(2)}, u32[]{:S(2)}) %collective-permute-start.3) | collective-permute-done | bytes 69664 | tf_op jit(solution)/shard_map/ppermute | solution.py:46
  23.8 0.1 collective-permute-start.10
  23.8 1.4 %collective-permute-done.9.rest_3_ = bf16[144,128]{1,0:T(8,128)(2,1)S(1)} collective-permute-done((bf16[144,128]{1,0:T(8,128)(2,1)S(1)}, bf16[144,128]{1,0:T(8,128)(2,1)S(1)}, u32[]{:S(2)}, u32[]{:S(2)}) %collective-permute-start.9) | collective-permute-done | bytes 36896 | tf_op jit(solution)/shard_map/ppermute | solution.py:24
  25.2 0.8 %combine.1 = f32[16,1024]{1,0:T(8,128)} custom-call(bf16[272,128]{1,0:T(8,128)(2,1)S(1)} %collective-permute-done.3.rest_0_, bf16[272,128]{1,0:T(8,128)(2,1)S(1)} %collective-permute-done.5.rest_1_, bf16[272,128]{1,0:T(8,128)(2,1)S(1)} %collective-permute-done.7.rest_2_, bf16[144,128]{1,0:T(8,128)(2,1)S(1)} %collective-permute-done.9.rest_3_, ...), custom_call_target="tpu_custom_call" | custom-call | tf_op jit(solution)/shard_map/combine/pallas_call | solution.py:424
  (9 shorter events, 0.1 us)
Async XLA Ops:
  0.0 1.5 %collective-permute-start.1 = (bf16[16,1024]{1,0:T(8,128)(2,1)}, bf16[16,1024]{1,0:T(8,128)(2,1)S(1)}, u32[]{:S(2)}, u32[]{:S(2)}) collective-permute-start(bf16[16,1024]{1,0:T(8,128)(2,1)} %refs_0_.1), channel_id=1, source_target_pairs={{0,4},{4,0},{1,5},{5,1},{2,6},{6,2},{3,7},{7,3},{8,12},{12,8},{9,1... | collective-permute-start | bytes 98312 | tf_op jit(solution)/shard_map/ppermute | solution.py:24
  0.5 8.6 %collective-permute-start = (bf16[32,64,256]{2,1,0:T(8,128)(2,1)}, bf16[32,64,256]{2,1,0:T(8,128)(2,1)S(1)}, u32[]{:S(2)}, u32[]{:S(2)}) collective-permute-start(bf16[32,64,256]{2,1,0:T(8,128)(2,1)} %bitcast.5), channel_id=1, source_target_pairs={{0,4},{4,0},{1,5},{5,1},{2,6},{6,2},{3,7},{7,3},{8,12},{12,8},{9,1... | collective-permute-start | bytes 3145736 | tf_op jit(solution)/shard_map/ppermute | solution.py:24
  1.5 7.0 %copy-start = (bf16[16,1024]{1,0:T(8,128)(2,1)S(1)}, bf16[16,1024]{1,0:T(8,128)(2,1)}, u32[]{:S(2)}) copy-start(bf16[16,1024]{1,0:T(8,128)(2,1)} %refs_0_.1) | copy-start | bytes 98308
  1.5 9.5 %collective-permute-start.6 = (bf16[2,16,1024]{2,1,0:T(8,128)(2,1)S(1)}, bf16[2,16,1024]{2,1,0:T(8,128)(2,1)S(1)}, u32[]{:S(2)}, u32[]{:S(2)}) collective-permute-start(bf16[2,16,1024]{2,1,0:T(8,128)(2,1)S(1)} %both_cores.1), channel_id=1, source_target_pairs={{0,16},{1,17},{4,21},{5,20},{8,24},{9,25},{12,29},{13,28},{16,0},{... | collective-permute-start | bytes 196616 | tf_op jit(solution)/shard_map/ppermute | solution.py:46
  5.5 6.4 %collective-permute-start.4 = (bf16[2,16,1024]{2,1,0:T(8,128)(2,1)S(1)}, bf16[2,16,1024]{2,1,0:T(8,128)(2,1)S(1)}, u32[]{:S(2)}, u32[]{:S(2)}) collective-permute-start(bf16[2,16,1024]{2,1,0:T(8,128)(2,1)S(1)} %both_cores.1), channel_id=1, source_target_pairs={{0,8},{1,9},{4,28},{5,29},{8,0},{9,1},{12,20},{13,21},{16,24},{17,... | collective-permute-start | bytes 196616 | tf_op jit(solution)/shard_map/ppermute | solution.py:46
  7.1 9.8 %collective-permute-start.2 = (bf16[2,16,1024]{2,1,0:T(8,128)(2,1)S(1)}, bf16[2,16,1024]{2,1,0:T(8,128)(2,1)S(1)}, u32[]{:S(2)}, u32[]{:S(2)}) collective-permute-start(bf16[2,16,1024]{2,1,0:T(8,128)(2,1)S(1)} %both_cores.1), channel_id=1, source_target_pairs={{0,9},{1,8},{4,29},{5,28},{8,1},{9,0},{12,21},{13,20},{16,25},{17,... | collective-permute-start | bytes 196616 | tf_op jit(solution)/shard_map/ppermute | solution.py:46
  8.5 10.0 %collective-permute-start.8 = (bf16[16,1024]{1,0:T(8,128)(2,1)S(1)}, bf16[16,1024]{1,0:T(8,128)(2,1)S(1)}, u32[]{:S(2)}, u32[]{:S(2)}) collective-permute-start(bf16[16,1024]{1,0:T(8,128)(2,1)S(1)} %copy-done), channel_id=1, source_target_pairs={{0,1},{1,0},{2,3},{3,2},{4,5},{5,4},{6,7},{7,6},{8,9},{9,8},{10,11... | collective-permute-start | bytes 98312 | tf_op jit(solution)/shard_map/ppermute | solution.py:24
  11.5 11.0 %collective-permute-start.7 = (bf16[272,128]{1,0:T(8,128)(2,1)S(1)}, bf16[272,128]{1,0:T(8,128)(2,1)S(1)}, u32[]{:S(2)}, u32[]{:S(2)}) collective-permute-start(bf16[272,128]{1,0:T(8,128)(2,1)S(1)} %get-tuple-element.29), channel_id=1, source_target_pairs={{0,16},{1,17},{4,21},{5,20},{8,24},{9,25},{12,29},{13,28},{16,0},{... | collective-permute-start | bytes 208904 | tf_op jit(solution)/shard_map/ppermute | solution.py:46
  12.9 9.6 %collective-permute-start.5 = (bf16[272,128]{1,0:T(8,128)(2,1)S(1)}, bf16[272,128]{1,0:T(8,128)(2,1)S(1)}, u32[]{:S(2)}, u32[]{:S(2)}) collective-permute-start(bf16[272,128]{1,0:T(8,128)(2,1)S(1)} %get-tuple-element.28), channel_id=1, source_target_pairs={{0,8},{1,9},{4,28},{5,29},{8,0},{9,1},{12,20},{13,21},{16,24},{17,... | collective-permute-start | bytes 208904 | tf_op jit(solution)/shard_map/ppermute | solution.py:46
  17.8 5.9 %collective-permute-start.3 = (bf16[272,128]{1,0:T(8,128)(2,1)S(1)}, bf16[272,128]{1,0:T(8,128)(2,1)S(1)}, u32[]{:S(2)}, u32[]{:S(2)}) collective-permute-start(bf16[272,128]{1,0:T(8,128)(2,1)S(1)} %get-tuple-element.27), channel_id=1, source_target_pairs={{0,9},{1,8},{4,29},{5,28},{8,1},{9,0},{12,21},{13,20},{16,25},{17,... | collective-permute-start | bytes 208904 | tf_op jit(solution)/shard_map/ppermute | solution.py:46
  21.0 4.3 %collective-permute-start.9 = (bf16[144,128]{1,0:T(8,128)(2,1)S(1)}, bf16[144,128]{1,0:T(8,128)(2,1)S(1)}, u32[]{:S(2)}, u32[]{:S(2)}) collective-permute-start(bf16[144,128]{1,0:T(8,128)(2,1)S(1)} %get-tuple-element.34), channel_id=1, source_target_pairs={{0,1},{1,0},{2,3},{3,2},{4,5},{5,4},{6,7},{7,6},{8,9},{9,8},{10,11... | collective-permute-start | bytes 110600 | tf_op jit(solution)/shard_map/ppermute | solution.py:24
  23.8 1.5 %collective-permute-start.10 = (bf16[144,128]{1,0:T(8,128)(2,1)S(1)}, bf16[144,128]{1,0:T(8,128)(2,1)S(1)}, u32[]{:S(2)}, u32[]{:S(2)}) collective-permute-start(bf16[144,128]{1,0:T(8,128)(2,1)S(1)} %sibling_share.1), channel_id=1, source_target_pairs={{0,4},{4,0},{1,5},{5,1},{2,6},{6,2},{3,7},{7,3},{8,12},{12,8},{9,1... | collective-permute-start | bytes 110600 | tf_op jit(solution)/shard_map/ppermute | solution.py:24

commit v17 on v16

--- a/solution.py
+++ b/solution.py
@@ -164,9 +164,8 @@
 
 
 def prepare_kernel(
-    capacity, near_ref, prompt_ref, table, parents, far_ref,
-    home_keys_ref, home_values_ref, keys_ref, values_ref, member_ref, held_ref,
-    rows_ref, near, sems,
+    capacity, near_ref, table, parents, far_ref,
+    home_keys_ref, home_values_ref, keys_ref, values_ref, member_ref, rows_ref, near, sem,
 ):
     n_req = lax.axis_size("z")
     slots, half, _ = near.shape
@@ -174,12 +173,8 @@
     n_batch = rows // BEAMS
     z, core = lax.axis_index("z"), lax.axis_index("core")
 
-    copies = [
-        pltpu.make_async_copy(near_ref, near, sems.at[0]),
-        pltpu.make_async_copy(prompt_ref, held_ref, sems.at[1]),
-    ]
-    for copy in copies:
-        copy.start()
+    copy = pltpu.make_async_copy(near_ref, near, sem)
+    copy.start()
 
     slot = iota((2 * slots, rows), 0)
     mine = slot < slots
@@ -203,7 +198,7 @@
         found.append(jnp.sum(jnp.where(chosen, place + 1, 0), axis=0, keepdims=True))
     found = jnp.concatenate(found, axis=0)
 
-    copies[0].wait()
+    copy.wait()
     requests = [z * 2 + core]
     for mask in masks_here(n_req):
         requests += [(z ^ mask) * 2, (z ^ mask) * 2 + 1]
@@ -234,8 +229,6 @@
         else:
             values_ref[i - 1] = values
 
-    copies[1].wait()
-
 
 def all_vectors(own_ref, pair_ref):
     return jnp.concatenate([stacked_heads(own_ref[...]), stacked_heads(pair_ref[...])], axis=0)
@@ -272,8 +265,9 @@
     return [x[:, lanes] for x in part]
 
 
-def away_kernel(place, keys_ref, values_ref, member_ref, message_ref, out_ref, after_ref):
-    after_ref[...] = jnp.zeros(after_ref.shape, jnp.float32)
+def away_kernel(place, keys_ref, values_ref, member_ref, message_ref, out_ref, *after_ref):
+    for ref in after_ref:
+        ref[...] = jnp.zeros(ref.shape, jnp.float32)
     vectors = [stacked_heads(message_ref[core]) for core in range(2)]
     members = [member_ref[1 + place + core] for core in range(2)]
     store_units(out_ref, suffix_parts(vectors, keys_ref, values_ref, members, place))
@@ -325,6 +319,7 @@
     rows = block_table.shape[0]
     vmem = pl.BlockSpec(memory_space=pltpu.VMEM)
     params = pltpu.CompilerParams(vmem_limit_bytes=32 * 2**20)
+    some = pl.CostEstimate(flops=2 * 10**8, bytes_accessed=2**21, transcendentals=0)
     early = pl.CostEstimate(flops=2 * 10**10, bytes_accessed=0, transcendentals=0)
 
     hbm = pl.BlockSpec(memory_space=pltpu.HBM)
@@ -351,9 +346,10 @@
         name="both_cores",
     )(own, swapped(queries, "core"))
     n_messages = n_req - 1
-    messages = [exchanged(both, k) for k in range(n_messages)]
-
-    home_keys, home_values, keys, values, member, prompt = pl.pallas_call(
+    order = [1, 0] + list(range(n_messages - 1, 1, -1)) if n_messages > 1 else [0]
+    messages = {k: exchanged(both, k) for k in order}
+
+    home_keys, home_values, keys, values, member = pl.pallas_call(
         functools.partial(prepare_kernel, capacity),
         out_shape=(
             pltpu.VMEM((1, 2 * capacity * half, HD), jnp.bfloat16),
@@ -361,39 +357,40 @@
             pltpu.VMEM((n_req, 2 * capacity * half, HD), jnp.bfloat16),
             pltpu.VMEM((n_req, HD, 2 * capacity * half), jnp.bfloat16),
             pltpu.VMEM((1 + n_req, 2 * capacity, VECS), jnp.float32),
-            pltpu.VMEM((tokens, width), jnp.bfloat16),
         ),
-        in_specs=[hbm] * 2 + [vmem] * 3,
-        out_specs=(vmem,) * 6,
+        in_specs=[hbm] + [vmem] * 3,
+        out_specs=(vmem,) * 5,
         scratch_shapes=[
             pltpu.VMEM((2 * slots + 8, VECS), jnp.float32),
             pltpu.VMEM((slots, half, width), jnp.bfloat16),
-            pltpu.SemaphoreType.DMA((2,)),
+            pltpu.SemaphoreType.DMA,
         ],
         compiler_params=params,
+        cost_estimate=some,
         name="prepare",
     )(
         in_hbm(near),
-        in_hbm(prompt_cache.reshape(tokens, width)),
         table,
         row_parents,
         far,
     )
 
-    received = []
-    for k, message in reversed(list(enumerate(messages))):
-        units, after = pl.pallas_call(
+    received, after = [], []
+    for k in order:
+        out = [pltpu.VMEM((2 * HD + STAT_ROWS, VECS), jnp.bfloat16)]
+        if k == 0:
+            out.append(pltpu.VMEM((8, VECS), jnp.float32))
+        units, *token = pl.pallas_call(
             functools.partial(away_kernel, 2 * ((k + 1) // 2)),
-            out_shape=(
-                pltpu.VMEM((2 * HD + STAT_ROWS, VECS), jnp.bfloat16),
-                pltpu.VMEM((8, VECS), jnp.float32),
-            ),
+            out_shape=out,
             in_specs=[vmem] * 4,
-            out_specs=(vmem,) * 2,
+            out_specs=[vmem] * len(out),
             compiler_params=params,
+            cost_estimate=some,
             name="suffix_away",
-        )(keys, values, member, message)
+        )(keys, values, member, messages[k])
         received.append(exchanged(units, k))
+        after += token
 
     summed, stats, given = pl.pallas_call(
         home_kernel,
@@ -409,7 +406,7 @@
             flops=8 * tokens * VECS * HD, bytes_accessed=2 * tokens * width, transcendentals=0
         ),
         name="home_part",
-    )(lengths, home_keys, home_values, member, own, other, prompt, after)
+    )(lengths, home_keys, home_values, member, own, other, prompt_cache.reshape(tokens, width), *after)
     last = swapped(given, "pair")
 
     share = pl.pallas_call(

time: 26.2 us -> 25.2 us (0.962)
  Pallas kernels: 8.44 us -> 7.24 us
  starting transfers between devices: 14 us -> 14.8 us
  waiting for transfers between devices: 2.84 us -> 2.1 us
    ppermute x6, waiting for transfers between devices: 1.23 us -> 0.02 us  [exchanged(): return lax.ppermute(value, ('z', 'core', 'pair'), pairs)]
    pallas_call x3, Pallas kernels: 2.44 us -> 1.52 us  [on_device(): pl.pallas_call(functools.partial(away_kernel, 2 * ((k + 1) // 2)), out_sh...]
    ppermute x5, starting transfers between devices: 2.64 us -> 3.15 us  [swapped(): return lax.ppermute(value, axis, [(0, 1), (1, 0)])]
    ppermute x5, waiting for transfers between devices: 1.62 us -> 2.09 us  [swapped(): return lax.ppermute(value, axis, [(0, 1), (1, 0)])]
    ppermute x6, starting transfers between devices: 11.3 us -> 11.7 us  [exchanged(): return lax.ppermute(value, ('z', 'core', 'pair'), pairs)]
    pallas_call x1, Pallas kernels: 1.95 us -> 1.67 us  [on_device(): pl.pallas_call(functools.partial(prepare_kernel, capacity), out_shape=(pl...]
  transfers between devices with their start and end apart: 11 -> 11, of which waited for: 3 -> 2; matrix products, arithmetic and copies ran while one was open for 0% -> 0% of each run, Pallas kernels for 30% -> 26%
where the time goes in v17:
time: 25.2 us; the launch traced here: 25 us
  starting transfers between devices  14.8 us (59%)
  Pallas kernels  7.24 us (29%)
  waiting for transfers between devices  2.1 us (8%)
  between operations  0.75 us (3%)
    ppermute x6, starting transfers between devices, exchanged(): return lax.ppermute(value, ('z', 'core', 'pair'), pairs)  11.7 us
    ppermute x5, starting transfers between devices, swapped(): return lax.ppermute(value, axis, [(0, 1), (1, 0)])  3.15 us
    pallas_call x1, Pallas kernels, on_device(): pl.pallas_call(home_kernel, out_shape=(pltpu.VMEM((HD, VECS), jnp.float32...  2.44 us
    ppermute x5, waiting for transfers between devices, swapped(): return lax.ppermute(value, axis, [(0, 1), (1, 0)])  2.09 us
    pallas_call x1, Pallas kernels, on_device(): pl.pallas_call(functools.partial(prepare_kernel, capacity), out_shape=(pl...  1.67 us
    pallas_call x3, Pallas kernels, on_device(): pl.pallas_call(functools.partial(away_kernel, 2 * ((k + 1) // 2)), out_sh...  1.52 us
    pallas_call x1, Pallas kernels, on_device(): pl.pallas_call(stage_kernel, out_shape=tuple((pltpu.VMEM(each.shape, each...  0.79 us
    pallas_call x1, Pallas kernels, on_device(): pl.pallas_call(final_kernel, out_shape=jax.ShapeDtypeStruct((BEAMS, HEADS...  0.77 us
  transfers between devices with their start and end apart: 11, of which 2 were waited for; matrix products, arithmetic and copies ran while one was open for 0% of the time, Pallas kernels for 26%

profile of v17, /device:TPU:0, one launch (start us, length us, event | category | flops | bytes accessed | tf_op | source)
XLA Modules:
  0.0 25.0 jit_solution(1251438607108647833)
XLA Ops:
  0.0 0.5 %collective-permute-start.1 = (bf16[16,1024]{1,0:T(8,128)(2,1)}, bf16[16,1024]{1,0:T(8,128)(2,1)S(1)}, u32[]{:S(2)}, u32[]{:S(2)}) collective-permute-start(bf16[16,1024]{1,0:T(8,128)(2,1)} %refs_0_.1), channel_id=1, source_target_pairs={{0,4},{4,0},{1,5},{5,1},{2,6},{6,2},{3,7},{7,3},{8,12},{12,8},{9,1... | collective-permute-start | bytes 98312 | tf_op jit(solution)/shard_map/ppermute | solution.py:24
  0.5 0.1 collective-permute-start
  0.5 0.8 %stage.1 = (bf16[16,1024]{1,0:T(8,128)(2,1)S(1)}, s32[4,128]{1,0:T(4,128)S(1)}, s32[1,128]{1,0:T(1,128)S(1)}) custom-call(bf16[16,1024]{1,0:T(8,128)(2,1)} %refs_0_.1, s32[4,128]{1,0:T(4,128)} %bitcast.7, s32[1,128]{1,0:T(1,128)} %bitcast.8), custom_call_target="tpu_custom_call" | custom-call | tf_op jit(solution)/shard_map/stage/pallas_call | solution.py:330
  1.3 0.2 collective-permute-done.1.sibling_ref
  1.5 4.0 %collective-permute-start.4 = (bf16[2,16,1024]{2,1,0:T(8,128)(2,1)S(1)}, bf16[2,16,1024]{2,1,0:T(8,128)(2,1)S(1)}, u32[]{:S(2)}, u32[]{:S(2)}) collective-permute-start(bf16[2,16,1024]{2,1,0:T(8,128)(2,1)S(1)} %both_cores.1), channel_id=1, source_target_pairs={{0,16},{1,17},{4,21},{5,20},{8,24},{9,25},{12,29},{13,28},{16,0},{... | collective-permute-start | bytes 196616 | tf_op jit(solution)/shard_map/ppermute | solution.py:46
  5.5 2.5 %collective-permute-start.6 = (bf16[2,16,1024]{2,1,0:T(8,128)(2,1)S(1)}, bf16[2,16,1024]{2,1,0:T(8,128)(2,1)S(1)}, u32[]{:S(2)}, u32[]{:S(2)}) collective-permute-start(bf16[2,16,1024]{2,1,0:T(8,128)(2,1)S(1)} %both_cores.1), channel_id=1, source_target_pairs={{0,9},{1,8},{4,29},{5,28},{8,1},{9,0},{12,21},{13,20},{16,25},{17,... | collective-permute-start | bytes 196616 | tf_op jit(solution)/shard_map/ppermute | solution.py:46
  8.0 0.4 %collective-permute-start.2 = (bf16[2,16,1024]{2,1,0:T(8,128)(2,1)S(1)}, bf16[2,16,1024]{2,1,0:T(8,128)(2,1)S(1)}, u32[]{:S(2)}, u32[]{:S(2)}) collective-permute-start(bf16[2,16,1024]{2,1,0:T(8,128)(2,1)S(1)} %both_cores.1), channel_id=1, source_target_pairs={{0,8},{1,9},{4,28},{5,29},{8,0},{9,1},{12,20},{13,21},{16,24},{17,... | collective-permute-start | bytes 196616 | tf_op jit(solution)/shard_map/ppermute | solution.py:46
  8.5 0.5 %collective-permute-start.8 = (bf16[16,1024]{1,0:T(8,128)(2,1)S(1)}, bf16[16,1024]{1,0:T(8,128)(2,1)S(1)}, u32[]{:S(2)}, u32[]{:S(2)}) collective-permute-start(bf16[16,1024]{1,0:T(8,128)(2,1)S(1)} %copy-done.1), channel_id=1, source_target_pairs={{0,1},{1,0},{2,3},{3,2},{4,5},{5,4},{6,7},{7,6},{8,9},{9,8},{10,11... | collective-permute-start | bytes 98312 | tf_op jit(solution)/shard_map/ppermute | solution.py:24
  9.0 1.7 %prepare.1 = (bf16[1,512,128]{2,1,0:T(8,128)(2,1)S(1)}, bf16[1,128,512]{2,1,0:T(8,128)(2,1)S(1)}, bf16[4,512,128]{2,1,0:T(8,128)(2,1)S(1)}, bf16[4,128,512]{2,1,0:T(8,128)(2,1)S(1)}, f32[5,8,128]{2,1,0:T(8,128)S(1)}) custom-call(bf16[32,64,256]{2,1,0:T(8,128)(2,1)} %bitcast.6, s32[4,128]{1,0:T(4,128)S(1)} %get-tuple-element.18.table, ...), custom_call_target="tpu_custom_call" | custom-call | flops 200000000 | bytes 2097152 | tf_op jit(solution)/shard_map/prepare/pallas_call | solution.py:352
  10.7 0.0 copy-start
  10.7 0.0 collective-permute-done.4.message_ref
  10.7 0.5 %suffix_away.4 = (bf16[272,128]{1,0:T(8,128)(2,1)S(1)}, f32[8,128]{1,0:T(8,128)S(1)}) custom-call(bf16[4,512,128]{2,1,0:T(8,128)(2,1)S(1)} %get-tuple-element.20.keys_ref, bf16[4,128,512]{2,1,0:T(8,128)(2,1)S(1)} %get-tuple-element.21.values_ref, f32[5,8,128]{2,1,0:T(8,128)S(1)} %get-tuple-element.22.member_ref, ...), custom_call_target="tpu_custom_call" | custom-call | flops 200000000 | bytes 2097152 | tf_op jit(solution)/shard_map/suffix_away/pallas_call | solution.py:383
  11.2 0.7 %collective-permute-start.5 = (bf16[272,128]{1,0:T(8,128)(2,1)S(1)}, bf16[272,128]{1,0:T(8,128)(2,1)S(1)}, u32[]{:S(2)}, u32[]{:S(2)}) collective-permute-start(bf16[272,128]{1,0:T(8,128)(2,1)S(1)} %get-tuple-element.24), channel_id=1, source_target_pairs={{0,16},{1,17},{4,21},{5,20},{8,24},{9,25},{12,29},{13,28},{16,0},{... | collective-permute-start | bytes 208904 | tf_op jit(solution)/shard_map/ppermute | solution.py:46
  12.0 0.0 collective-permute-done.6.message_ref
  12.0 0.5 %suffix_away.5 = bf16[272,128]{1,0:T(8,128)(2,1)S(1)} custom-call(bf16[4,512,128]{2,1,0:T(8,128)(2,1)S(1)} %get-tuple-element.20.keys_ref, bf16[4,128,512]{2,1,0:T(8,128)(2,1)S(1)} %get-tuple-element.21.values_ref, f32[5,8,128]{2,1,0:T(8,128)S(1)} %get-tuple-element.22.member_ref, bf16[2,16,1024]{2,1,0:T(8,128)(2,1)S(1)} %collective-permute-done.6.message_ref), custom_call_target="tpu_custom_call" | custom-call | flops 200000000 | bytes 2097152 | tf_op jit(solution)/shard_map/suffix_away/pallas_call | solution.py:383
  12.5 3.9 %collective-permute-start.7 = (bf16[272,128]{1,0:T(8,128)(2,1)S(1)}, bf16[272,128]{1,0:T(8,128)(2,1)S(1)}, u32[]{:S(2)}, u32[]{:S(2)}) collective-permute-start(bf16[272,128]{1,0:T(8,128)(2,1)S(1)} %suffix_away.5), channel_id=1, source_target_pairs={{0,9},{1,8},{4,29},{5,28},{8,1},{9,0},{12,21},{13,20},{16,25},{17,... | collective-permute-start | bytes 208904 | tf_op jit(solution)/shard_map/ppermute | solution.py:46
  16.4 0.5 %suffix_away.3 = bf16[272,128]{1,0:T(8,128)(2,1)S(1)} custom-call(bf16[4,512,128]{2,1,0:T(8,128)(2,1)S(1)} %get-tuple-element.20.keys_ref, bf16[4,128,512]{2,1,0:T(8,128)(2,1)S(1)} %get-tuple-element.21.values_ref, f32[5,8,128]{2,1,0:T(8,128)S(1)} %get-tuple-element.22.member_ref, bf16[2,16,1024]{2,1,0:T(8,128)(2,1)S(1)} %collective-permute-done.2.message_ref), custom_call_target="tpu_custom_call" | custom-call | flops 200000000 | bytes 2097152 | tf_op jit(solution)/shard_map/suffix_away/pallas_call | solution.py:383
  16.9 0.1 collective-permute-start.3
  17.7 2.4 %home_part.1 = (f32[128,128]{1,0:T(8,128)S(1)}, f32[8,128]{1,0:T(8,128)S(1)}, bf16[144,128]{1,0:T(8,128)(2,1)S(1)}) custom-call(s32[1]{0:T(128)S(6)} %copy.7.length_ref, bf16[1,512,128]{2,1,0:T(8,128)(2,1)S(1)} %get-tuple-element.25.keys_ref, bf16[1,128,512]{2,1,0:T(8,128)(2,1)S(1)} %get-tuple-element.26.values_ref, ...), custom_call_target="tpu_custom_call" | custom-call | flops 536870912 | bytes 2097152 | tf_op jit(solution)/shard_map/home_part/pallas_call | solution.py:395
  20.1 1.5 %collective-permute-start.9 = (bf16[144,128]{1,0:T(8,128)(2,1)S(1)}, bf16[144,128]{1,0:T(8,128)(2,1)S(1)}, u32[]{:S(2)}, u32[]{:S(2)}) collective-permute-start(bf16[144,128]{1,0:T(8,128)(2,1)S(1)} %get-tuple-element.28), channel_id=1, source_target_pairs={{0,1},{1,0},{2,3},{3,2},{4,5},{5,4},{6,7},{7,6},{8,9},{9,8},{10,11... | collective-permute-start | bytes 110600 | tf_op jit(solution)/shard_map/ppermute | solution.py:24
  21.7 0.1 sibling_share.1
  21.7 0.6 %collective-permute-start.10 = (bf16[144,128]{1,0:T(8,128)(2,1)S(1)}, bf16[144,128]{1,0:T(8,128)(2,1)S(1)}, u32[]{:S(2)}, u32[]{:S(2)}) collective-permute-start(bf16[144,128]{1,0:T(8,128)(2,1)S(1)} %sibling_share.1), channel_id=1, source_target_pairs={{0,4},{4,0},{1,5},{5,1},{2,6},{6,2},{3,7},{7,3},{8,12},{12,8},{9,1... | collective-permute-start | bytes 110600 | tf_op jit(solution)/shard_map/ppermute | solution.py:24
  22.3 1.9 %collective-permute-done.9.rest_3_ = bf16[144,128]{1,0:T(8,128)(2,1)S(1)} collective-permute-done((bf16[144,128]{1,0:T(8,128)(2,1)S(1)}, bf16[144,128]{1,0:T(8,128)(2,1)S(1)}, u32[]{:S(2)}, u32[]{:S(2)}) %collective-permute-start.9) | collective-permute-done | bytes 36896 | tf_op jit(solution)/shard_map/ppermute | solution.py:24
  24.2 0.8 %combine.1 = f32[16,1024]{1,0:T(8,128)} custom-call(bf16[272,128]{1,0:T(8,128)(2,1)S(1)} %collective-permute-done.3.rest_0_, bf16[272,128]{1,0:T(8,128)(2,1)S(1)} %collective-permute-done.5.rest_1_, bf16[272,128]{1,0:T(8,128)(2,1)S(1)} %collective-permute-done.7.rest_2_, bf16[144,128]{1,0:T(8,128)(2,1)S(1)} %collective-permute-done.9.rest_3_, ...), custom_call_target="tpu_custom_call" | custom-call | tf_op jit(solution)/shard_map/combine/pallas_call | solution.py:421
  (11 shorter events, 0.0 us)
Async XLA Ops:
  0.0 1.5 %collective-permute-start.1 = (bf16[16,1024]{1,0:T(8,128)(2,1)}, bf16[16,1024]{1,0:T(8,128)(2,1)S(1)}, u32[]{:S(2)}, u32[]{:S(2)}) collective-permute-start(bf16[16,1024]{1,0:T(8,128)(2,1)} %refs_0_.1), channel_id=1, source_target_pairs={{0,4},{4,0},{1,5},{5,1},{2,6},{6,2},{3,7},{7,3},{8,12},{12,8},{9,1... | collective-permute-start | bytes 98312 | tf_op jit(solution)/shard_map/ppermute | solution.py:24
  0.5 8.6 %collective-permute-start = (bf16[32,64,256]{2,1,0:T(8,128)(2,1)}, bf16[32,64,256]{2,1,0:T(8,128)(2,1)S(1)}, u32[]{:S(2)}, u32[]{:S(2)}) collective-permute-start(bf16[32,64,256]{2,1,0:T(8,128)(2,1)} %bitcast.5), channel_id=1, source_target_pairs={{0,4},{4,0},{1,5},{5,1},{2,6},{6,2},{3,7},{7,3},{8,12},{12,8},{9,1... | collective-permute-start | bytes 3145736 | tf_op jit(solution)/shard_map/ppermute | solution.py:24
  1.5 7.0 %copy-start.1 = (bf16[16,1024]{1,0:T(8,128)(2,1)S(1)}, bf16[16,1024]{1,0:T(8,128)(2,1)}, u32[]{:S(2)}) copy-start(bf16[16,1024]{1,0:T(8,128)(2,1)} %refs_0_.1) | copy-start | bytes 98308
  1.5 9.2 %collective-permute-start.4 = (bf16[2,16,1024]{2,1,0:T(8,128)(2,1)S(1)}, bf16[2,16,1024]{2,1,0:T(8,128)(2,1)S(1)}, u32[]{:S(2)}, u32[]{:S(2)}) collective-permute-start(bf16[2,16,1024]{2,1,0:T(8,128)(2,1)S(1)} %both_cores.1), channel_id=1, source_target_pairs={{0,16},{1,17},{4,21},{5,20},{8,24},{9,25},{12,29},{13,28},{16,0},{... | collective-permute-start | bytes 196616 | tf_op jit(solution)/shard_map/ppermute | solution.py:46
  5.5 6.4 %collective-permute-start.6 = (bf16[2,16,1024]{2,1,0:T(8,128)(2,1)S(1)}, bf16[2,16,1024]{2,1,0:T(8,128)(2,1)S(1)}, u32[]{:S(2)}, u32[]{:S(2)}) collective-permute-start(bf16[2,16,1024]{2,1,0:T(8,128)(2,1)S(1)} %both_cores.1), channel_id=1, source_target_pairs={{0,9},{1,8},{4,29},{5,28},{8,1},{9,0},{12,21},{13,20},{16,25},{17,... | collective-permute-start | bytes 196616 | tf_op jit(solution)/shard_map/ppermute | solution.py:46
  8.0 8.4 %collective-permute-start.2 = (bf16[2,16,1024]{2,1,0:T(8,128)(2,1)S(1)}, bf16[2,16,1024]{2,1,0:T(8,128)(2,1)S(1)}, u32[]{:S(2)}, u32[]{:S(2)}) collective-permute-start(bf16[2,16,1024]{2,1,0:T(8,128)(2,1)S(1)} %both_cores.1), channel_id=1, source_target_pairs={{0,8},{1,9},{4,28},{5,29},{8,0},{9,1},{12,20},{13,21},{16,24},{17,... | collective-permute-start | bytes 196616 | tf_op jit(solution)/shard_map/ppermute | solution.py:46
  8.5 9.2 %collective-permute-start.8 = (bf16[16,1024]{1,0:T(8,128)(2,1)S(1)}, bf16[16,1024]{1,0:T(8,128)(2,1)S(1)}, u32[]{:S(2)}, u32[]{:S(2)}) collective-permute-start(bf16[16,1024]{1,0:T(8,128)(2,1)S(1)} %copy-done.1), channel_id=1, source_target_pairs={{0,1},{1,0},{2,3},{3,2},{4,5},{5,4},{6,7},{7,6},{8,9},{9,8},{10,11... | collective-permute-start | bytes 98312 | tf_op jit(solution)/shard_map/ppermute | solution.py:24
  10.7 7.0 %copy-start = (bf16[1,1,4096,256]{3,2,1,0:T(8,128)(2,1)S(1)}, bf16[1,1,4096,256]{3,2,1,0:T(8,128)(2,1)}, u32[]{:S(2)}) copy-start(bf16[1,1,4096,256]{3,2,1,0:T(8,128)(2,1)} %param.7) | copy-start | bytes 6291460
  11.2 10.4 %collective-permute-start.5 = (bf16[272,128]{1,0:T(8,128)(2,1)S(1)}, bf16[272,128]{1,0:T(8,128)(2,1)S(1)}, u32[]{:S(2)}, u32[]{:S(2)}) collective-permute-start(bf16[272,128]{1,0:T(8,128)(2,1)S(1)} %get-tuple-element.24), channel_id=1, source_target_pairs={{0,16},{1,17},{4,21},{5,20},{8,24},{9,25},{12,29},{13,28},{16,0},{... | collective-permute-start | bytes 208904 | tf_op jit(solution)/shard_map/ppermute | solution.py:46
  12.5 9.2 %collective-permute-start.7 = (bf16[272,128]{1,0:T(8,128)(2,1)S(1)}, bf16[272,128]{1,0:T(8,128)(2,1)S(1)}, u32[]{:S(2)}, u32[]{:S(2)}) collective-permute-start(bf16[272,128]{1,0:T(8,128)(2,1)S(1)} %suffix_away.5), channel_id=1, source_target_pairs={{0,9},{1,8},{4,29},{5,28},{8,1},{9,0},{12,21},{13,20},{16,25},{17,... | collective-permute-start | bytes 208904 | tf_op jit(solution)/shard_map/ppermute | solution.py:46
  16.9 4.8 %collective-permute-start.3 = (bf16[272,128]{1,0:T(8,128)(2,1)S(1)}, bf16[272,128]{1,0:T(8,128)(2,1)S(1)}, u32[]{:S(2)}, u32[]{:S(2)}) collective-permute-start(bf16[272,128]{1,0:T(8,128)(2,1)S(1)} %suffix_away.3), channel_id=1, source_target_pairs={{0,8},{1,9},{4,28},{5,29},{8,0},{9,1},{12,20},{13,21},{16,24},{17,... | collective-permute-start | bytes 208904 | tf_op jit(solution)/shard_map/ppermute | solution.py:46
  20.1 4.0 %collective-permute-start.9 = (bf16[144,128]{1,0:T(8,128)(2,1)S(1)}, bf16[144,128]{1,0:T(8,128)(2,1)S(1)}, u32[]{:S(2)}, u32[]{:S(2)}) collective-permute-start(bf16[144,128]{1,0:T(8,128)(2,1)S(1)} %get-tuple-element.28), channel_id=1, source_target_pairs={{0,1},{1,0},{2,3},{3,2},{4,5},{5,4},{6,7},{7,6},{8,9},{9,8},{10,11... | collective-permute-start | bytes 110600 | tf_op jit(solution)/shard_map/ppermute | solution.py:24
  21.7 2.4 %collective-permute-start.10 = (bf16[144,128]{1,0:T(8,128)(2,1)S(1)}, bf16[144,128]{1,0:T(8,128)(2,1)S(1)}, u32[]{:S(2)}, u32[]{:S(2)}) collective-permute-start(bf16[144,128]{1,0:T(8,128)(2,1)S(1)} %sibling_share.1), channel_id=1, source_target_pairs={{0,4},{4,0},{1,5},{5,1},{2,6},{6,2},{3,7},{7,3},{8,12},{12,8},{9,1... | collective-permute-start | bytes 110600 | tf_op jit(solution)/shard_map/ppermute | solution.py:24

commit v18 on v17

--- a/solution.py
+++ b/solution.py
@@ -378,7 +378,7 @@
     received, after = [], []
     for k in order:
         out = [pltpu.VMEM((2 * HD + STAT_ROWS, VECS), jnp.bfloat16)]
-        if k == 0:
+        if k == order[0]:
             out.append(pltpu.VMEM((8, VECS), jnp.float32))
         units, *token = pl.pallas_call(
             functools.partial(away_kernel, 2 * ((k + 1) // 2)),

time: 25.2 us -> 25 us (level)
  starting transfers between devices: 14.8 us -> 12.9 us
  waiting for transfers between devices: 2.1 us -> 3.83 us
    ppermute x6, waiting for transfers between devices: 0.02 us -> 2.4 us  [exchanged(): return lax.ppermute(value, ('z', 'core', 'pair'), pairs)]
    ppermute x6, starting transfers between devices: 11.7 us -> 10.7 us  [exchanged(): return lax.ppermute(value, ('z', 'core', 'pair'), pairs)]
    ppermute x5, starting transfers between devices: 3.15 us -> 2.23 us  [swapped(): return lax.ppermute(value, axis, [(0, 1), (1, 0)])]
    ppermute x5, waiting for transfers between devices: 2.09 us -> 1.42 us  [swapped(): return lax.ppermute(value, axis, [(0, 1), (1, 0)])]
  transfers between devices with their start and end apart: 11 -> 11, of which waited for: 2 -> 4; matrix products, arithmetic and copies ran while one was open for 0% -> 0% of each run, Pallas kernels for 26% -> 26%
where the time goes in v18:
time: 25 us; the launch traced here: 24.8 us
  starting transfers between devices  12.9 us (52%)
  Pallas kernels  7.23 us (29%)
  waiting for transfers between devices  3.83 us (15%)
  between operations  0.75 us (3%)
    ppermute x6, starting transfers between devices, exchanged(): return lax.ppermute(value, ('z', 'core', 'pair'), pairs)  10.7 us
    pallas_call x1, Pallas kernels, on_device(): pl.pallas_call(home_kernel, out_shape=(pltpu.VMEM((HD, VECS), jnp.float32...  2.44 us
    ppermute x6, waiting for transfers between devices, exchanged(): return lax.ppermute(value, ('z', 'core', 'pair'), pairs)  2.4 us
    ppermute x5, starting transfers between devices, swapped(): return lax.ppermute(value, axis, [(0, 1), (1, 0)])  2.23 us
    pallas_call x1, Pallas kernels, on_device(): pl.pallas_call(functools.partial(prepare_kernel, capacity), out_shape=(pl...  1.67 us
    pallas_call x3, Pallas kernels, on_device(): pl.pallas_call(functools.partial(away_kernel, 2 * ((k + 1) // 2)), out_sh...  1.52 us
    ppermute x5, waiting for transfers between devices, swapped(): return lax.ppermute(value, axis, [(0, 1), (1, 0)])  1.42 us
    pallas_call x1, Pallas kernels, on_device(): pl.pallas_call(stage_kernel, out_shape=tuple((pltpu.VMEM(each.shape, each...  0.79 us
  transfers between devices with their start and end apart: 11, of which 4 were waited for; matrix products, arithmetic and copies ran while one was open for 0% of the time, Pallas kernels for 26%

profile of v18, /device:TPU:0, one launch (start us, length us, event | category | flops | bytes accessed | tf_op | source)
XLA Modules:
  0.0 24.8 jit_solution(10656959370969269628)
XLA Ops:
  0.0 0.5 %collective-permute-start.1 = (bf16[16,1024]{1,0:T(8,128)(2,1)}, bf16[16,1024]{1,0:T(8,128)(2,1)S(1)}, u32[]{:S(2)}, u32[]{:S(2)}) collective-permute-start(bf16[16,1024]{1,0:T(8,128)(2,1)} %refs_0_.1), channel_id=1, source_target_pairs={{0,4},{4,0},{1,5},{5,1},{2,6},{6,2},{3,7},{7,3},{8,12},{12,8},{9,1... | collective-permute-start | bytes 98312 | tf_op jit(solution)/shard_map/ppermute | solution.py:24
  0.5 0.1 collective-permute-start
  0.5 0.8 %stage.1 = (bf16[16,1024]{1,0:T(8,128)(2,1)S(1)}, s32[4,128]{1,0:T(4,128)S(1)}, s32[1,128]{1,0:T(1,128)S(1)}) custom-call(bf16[16,1024]{1,0:T(8,128)(2,1)} %refs_0_.1, s32[4,128]{1,0:T(4,128)} %bitcast.7, s32[1,128]{1,0:T(1,128)} %bitcast.8), custom_call_target="tpu_custom_call" | custom-call | tf_op jit(solution)/shard_map/stage/pallas_call | solution.py:330
  1.3 0.2 collective-permute-done.1.sibling_ref
  1.5 3.0 %collective-permute-start.2 = (bf16[2,16,1024]{2,1,0:T(8,128)(2,1)S(1)}, bf16[2,16,1024]{2,1,0:T(8,128)(2,1)S(1)}, u32[]{:S(2)}, u32[]{:S(2)}) collective-permute-start(bf16[2,16,1024]{2,1,0:T(8,128)(2,1)S(1)} %both_cores.1), channel_id=1, source_target_pairs={{0,8},{1,9},{4,28},{5,29},{8,0},{9,1},{12,20},{13,21},{16,24},{17,... | collective-permute-start | bytes 196616 | tf_op jit(solution)/shard_map/ppermute | solution.py:46
  4.5 1.4 %collective-permute-start.6 = (bf16[2,16,1024]{2,1,0:T(8,128)(2,1)S(1)}, bf16[2,16,1024]{2,1,0:T(8,128)(2,1)S(1)}, u32[]{:S(2)}, u32[]{:S(2)}) collective-permute-start(bf16[2,16,1024]{2,1,0:T(8,128)(2,1)S(1)} %both_cores.1), channel_id=1, source_target_pairs={{0,9},{1,8},{4,29},{5,28},{8,1},{9,0},{12,21},{13,20},{16,25},{17,... | collective-permute-start | bytes 196616 | tf_op jit(solution)/shard_map/ppermute | solution.py:46
  5.9 2.6 %collective-permute-start.4 = (bf16[2,16,1024]{2,1,0:T(8,128)(2,1)S(1)}, bf16[2,16,1024]{2,1,0:T(8,128)(2,1)S(1)}, u32[]{:S(2)}, u32[]{:S(2)}) collective-permute-start(bf16[2,16,1024]{2,1,0:T(8,128)(2,1)S(1)} %both_cores.1), channel_id=1, source_target_pairs={{0,16},{1,17},{4,21},{5,20},{8,24},{9,25},{12,29},{13,28},{16,0},{... | collective-permute-start | bytes 196616 | tf_op jit(solution)/shard_map/ppermute | solution.py:46
  8.5 0.5 %collective-permute-start.8 = (bf16[16,1024]{1,0:T(8,128)(2,1)S(1)}, bf16[16,1024]{1,0:T(8,128)(2,1)S(1)}, u32[]{:S(2)}, u32[]{:S(2)}) collective-permute-start(bf16[16,1024]{1,0:T(8,128)(2,1)S(1)} %copy-done.1), channel_id=1, source_target_pairs={{0,1},{1,0},{2,3},{3,2},{4,5},{5,4},{6,7},{7,6},{8,9},{9,8},{10,11... | collective-permute-start | bytes 98312 | tf_op jit(solution)/shard_map/ppermute | solution.py:24
  9.0 1.7 %prepare.1 = (bf16[1,512,128]{2,1,0:T(8,128)(2,1)S(1)}, bf16[1,128,512]{2,1,0:T(8,128)(2,1)S(1)}, bf16[4,512,128]{2,1,0:T(8,128)(2,1)S(1)}, bf16[4,128,512]{2,1,0:T(8,128)(2,1)S(1)}, f32[5,8,128]{2,1,0:T(8,128)S(1)}) custom-call(bf16[32,64,256]{2,1,0:T(8,128)(2,1)} %bitcast.6, s32[4,128]{1,0:T(4,128)S(1)} %get-tuple-element.18.table, ...), custom_call_target="tpu_custom_call" | custom-call | flops 200000000 | bytes 2097152 | tf_op jit(solution)/shard_map/prepare/pallas_call | solution.py:352
  10.7 0.0 copy-start
  10.7 0.5 %suffix_away.3 = (bf16[272,128]{1,0:T(8,128)(2,1)S(1)}, f32[8,128]{1,0:T(8,128)S(1)}) custom-call(bf16[4,512,128]{2,1,0:T(8,128)(2,1)S(1)} %get-tuple-element.20.keys_ref, bf16[4,128,512]{2,1,0:T(8,128)(2,1)S(1)} %get-tuple-element.21.values_ref, f32[5,8,128]{2,1,0:T(8,128)S(1)} %get-tuple-element.22.member_ref, ...), custom_call_target="tpu_custom_call" | custom-call | flops 200000000 | bytes 2097152 | tf_op jit(solution)/shard_map/suffix_away/pallas_call | solution.py:383
  11.2 1.6 %collective-permute-start.3 = (bf16[272,128]{1,0:T(8,128)(2,1)S(1)}, bf16[272,128]{1,0:T(8,128)(2,1)S(1)}, u32[]{:S(2)}, u32[]{:S(2)}) collective-permute-start(bf16[272,128]{1,0:T(8,128)(2,1)S(1)} %get-tuple-element.24), channel_id=1, source_target_pairs={{0,8},{1,9},{4,28},{5,29},{8,0},{9,1},{12,20},{13,21},{16,24},{17,... | collective-permute-start | bytes 208904 | tf_op jit(solution)/shard_map/ppermute | solution.py:46
  12.9 0.5 %suffix_away.5 = bf16[272,128]{1,0:T(8,128)(2,1)S(1)} custom-call(bf16[4,512,128]{2,1,0:T(8,128)(2,1)S(1)} %get-tuple-element.20.keys_ref, bf16[4,128,512]{2,1,0:T(8,128)(2,1)S(1)} %get-tuple-element.21.values_ref, f32[5,8,128]{2,1,0:T(8,128)S(1)} %get-tuple-element.22.member_ref, bf16[2,16,1024]{2,1,0:T(8,128)(2,1)S(1)} %collective-permute-done.6.message_ref), custom_call_target="tpu_custom_call" | custom-call | flops 200000000 | bytes 2097152 | tf_op jit(solution)/shard_map/suffix_away/pallas_call | solution.py:383
  13.4 1.4 %collective-permute-start.7 = (bf16[272,128]{1,0:T(8,128)(2,1)S(1)}, bf16[272,128]{1,0:T(8,128)(2,1)S(1)}, u32[]{:S(2)}, u32[]{:S(2)}) collective-permute-start(bf16[272,128]{1,0:T(8,128)(2,1)S(1)} %suffix_away.5), channel_id=1, source_target_pairs={{0,9},{1,8},{4,29},{5,28},{8,1},{9,0},{12,21},{13,20},{16,25},{17,... | collective-permute-start | bytes 208904 | tf_op jit(solution)/shard_map/ppermute | solution.py:46
  14.8 0.0 collective-permute-done.4.message_ref
  14.8 0.5 %suffix_away.4 = bf16[272,128]{1,0:T(8,128)(2,1)S(1)} custom-call(bf16[4,512,128]{2,1,0:T(8,128)(2,1)S(1)} %get-tuple-element.20.keys_ref, bf16[4,128,512]{2,1,0:T(8,128)(2,1)S(1)} %get-tuple-element.21.values_ref, f32[5,8,128]{2,1,0:T(8,128)S(1)} %get-tuple-element.22.member_ref, bf16[2,16,1024]{2,1,0:T(8,128)(2,1)S(1)} %collective-permute-done.4.message_ref), custom_call_target="tpu_custom_call" | custom-call | flops 200000000 | bytes 2097152 | tf_op jit(solution)/shard_map/suffix_away/pallas_call | solution.py:383
  15.4 0.7 %collective-permute-start.5 = (bf16[272,128]{1,0:T(8,128)(2,1)S(1)}, bf16[272,128]{1,0:T(8,128)(2,1)S(1)}, u32[]{:S(2)}, u32[]{:S(2)}) collective-permute-start(bf16[272,128]{1,0:T(8,128)(2,1)S(1)} %suffix_away.4), channel_id=1, source_target_pairs={{0,16},{1,17},{4,21},{5,20},{8,24},{9,25},{12,29},{13,28},{16,0},{... | collective-permute-start | bytes 208904 | tf_op jit(solution)/shard_map/ppermute | solution.py:46
  16.7 2.4 %home_part.1 = (f32[128,128]{1,0:T(8,128)S(1)}, f32[8,128]{1,0:T(8,128)S(1)}, bf16[144,128]{1,0:T(8,128)(2,1)S(1)}) custom-call(s32[1]{0:T(128)S(6)} %copy.7.length_ref, bf16[1,512,128]{2,1,0:T(8,128)(2,1)S(1)} %get-tuple-element.25.keys_ref, bf16[1,128,512]{2,1,0:T(8,128)(2,1)S(1)} %get-tuple-element.26.values_ref, ...), custom_call_target="tpu_custom_call" | custom-call | flops 536870912 | bytes 2097152 | tf_op jit(solution)/shard_map/home_part/pallas_call | solution.py:395
  19.1 1.1 %collective-permute-start.9 = (bf16[144,128]{1,0:T(8,128)(2,1)S(1)}, bf16[144,128]{1,0:T(8,128)(2,1)S(1)}, u32[]{:S(2)}, u32[]{:S(2)}) collective-permute-start(bf16[144,128]{1,0:T(8,128)(2,1)S(1)} %get-tuple-element.28), channel_id=1, source_target_pairs={{0,1},{1,0},{2,3},{3,2},{4,5},{5,4},{6,7},{7,6},{8,9},{9,8},{10,11... | collective-permute-start | bytes 110600 | tf_op jit(solution)/shard_map/ppermute | solution.py:24
  20.3 2.4 %collective-permute-done.5.rest_1_ = bf16[272,128]{1,0:T(8,128)(2,1)S(1)} collective-permute-done((bf16[272,128]{1,0:T(8,128)(2,1)S(1)}, bf16[272,128]{1,0:T(8,128)(2,1)S(1)}, u32[]{:S(2)}, u32[]{:S(2)}) %collective-permute-start.5) | collective-permute-done | bytes 69664 | tf_op jit(solution)/shard_map/ppermute | solution.py:46
  22.7 0.1 collective-permute-start.10
  22.8 0.4 %collective-permute-done.9.rest_3_ = bf16[144,128]{1,0:T(8,128)(2,1)S(1)} collective-permute-done((bf16[144,128]{1,0:T(8,128)(2,1)S(1)}, bf16[144,128]{1,0:T(8,128)(2,1)S(1)}, u32[]{:S(2)}, u32[]{:S(2)}) %collective-permute-start.9) | collective-permute-done | bytes 36896 | tf_op jit(solution)/shard_map/ppermute | solution.py:24
  23.2 0.8 %collective-permute-done.10.rest_4_ = bf16[144,128]{1,0:T(8,128)(2,1)S(1)} collective-permute-done((bf16[144,128]{1,0:T(8,128)(2,1)S(1)}, bf16[144,128]{1,0:T(8,128)(2,1)S(1)}, u32[]{:S(2)}, u32[]{:S(2)}) %collective-permute-start.10) | collective-permute-done | bytes 36896 | tf_op jit(solution)/shard_map/ppermute | solution.py:24
  24.0 0.8 %combine.1 = f32[16,1024]{1,0:T(8,128)} custom-call(bf16[272,128]{1,0:T(8,128)(2,1)S(1)} %collective-permute-done.3.rest_0_, bf16[272,128]{1,0:T(8,128)(2,1)S(1)} %collective-permute-done.5.rest_1_, bf16[272,128]{1,0:T(8,128)(2,1)S(1)} %collective-permute-done.7.rest_2_, bf16[144,128]{1,0:T(8,128)(2,1)S(1)} %collective-permute-done.9.rest_3_, ...), custom_call_target="tpu_custom_call" | custom-call | tf_op jit(solution)/shard_map/combine/pallas_call | solution.py:421
  (11 shorter events, 0.1 us)
Async XLA Ops:
  0.0 1.5 %collective-permute-start.1 = (bf16[16,1024]{1,0:T(8,128)(2,1)}, bf16[16,1024]{1,0:T(8,128)(2,1)S(1)}, u32[]{:S(2)}, u32[]{:S(2)}) collective-permute-start(bf16[16,1024]{1,0:T(8,128)(2,1)} %refs_0_.1), channel_id=1, source_target_pairs={{0,4},{4,0},{1,5},{5,1},{2,6},{6,2},{3,7},{7,3},{8,12},{12,8},{9,1... | collective-permute-start | bytes 98312 | tf_op jit(solution)/shard_map/ppermute | solution.py:24
  0.5 8.6 %collective-permute-start = (bf16[32,64,256]{2,1,0:T(8,128)(2,1)}, bf16[32,64,256]{2,1,0:T(8,128)(2,1)S(1)}, u32[]{:S(2)}, u32[]{:S(2)}) collective-permute-start(bf16[32,64,256]{2,1,0:T(8,128)(2,1)} %bitcast.5), channel_id=1, source_target_pairs={{0,4},{4,0},{1,5},{5,1},{2,6},{6,2},{3,7},{7,3},{8,12},{12,8},{9,1... | collective-permute-start | bytes 3145736 | tf_op jit(solution)/shard_map/ppermute | solution.py:24
  1.5 7.0 %copy-start.1 = (bf16[16,1024]{1,0:T(8,128)(2,1)S(1)}, bf16[16,1024]{1,0:T(8,128)(2,1)}, u32[]{:S(2)}) copy-start(bf16[16,1024]{1,0:T(8,128)(2,1)} %refs_0_.1) | copy-start | bytes 98308
  1.5 9.2 %collective-permute-start.2 = (bf16[2,16,1024]{2,1,0:T(8,128)(2,1)S(1)}, bf16[2,16,1024]{2,1,0:T(8,128)(2,1)S(1)}, u32[]{:S(2)}, u32[]{:S(2)}) collective-permute-start(bf16[2,16,1024]{2,1,0:T(8,128)(2,1)S(1)} %both_cores.1), channel_id=1, source_target_pairs={{0,8},{1,9},{4,28},{5,29},{8,0},{9,1},{12,20},{13,21},{16,24},{17,... | collective-permute-start | bytes 196616 | tf_op jit(solution)/shard_map/ppermute | solution.py:46
  4.5 8.4 %collective-permute-start.6 = (bf16[2,16,1024]{2,1,0:T(8,128)(2,1)S(1)}, bf16[2,16,1024]{2,1,0:T(8,128)(2,1)S(1)}, u32[]{:S(2)}, u32[]{:S(2)}) collective-permute-start(bf16[2,16,1024]{2,1,0:T(8,128)(2,1)S(1)} %both_cores.1), channel_id=1, source_target_pairs={{0,9},{1,8},{4,29},{5,28},{8,1},{9,0},{12,21},{13,20},{16,25},{17,... | collective-permute-start | bytes 196616 | tf_op jit(solution)/shard_map/ppermute | solution.py:46
  5.9 8.9 %collective-permute-start.4 = (bf16[2,16,1024]{2,1,0:T(8,128)(2,1)S(1)}, bf16[2,16,1024]{2,1,0:T(8,128)(2,1)S(1)}, u32[]{:S(2)}, u32[]{:S(2)}) collective-permute-start(bf16[2,16,1024]{2,1,0:T(8,128)(2,1)S(1)} %both_cores.1), channel_id=1, source_target_pairs={{0,16},{1,17},{4,21},{5,20},{8,24},{9,25},{12,29},{13,28},{16,0},{... | collective-permute-start | bytes 196616 | tf_op jit(solution)/shard_map/ppermute | solution.py:46
  8.5 8.2 %collective-permute-start.8 = (bf16[16,1024]{1,0:T(8,128)(2,1)S(1)}, bf16[16,1024]{1,0:T(8,128)(2,1)S(1)}, u32[]{:S(2)}, u32[]{:S(2)}) collective-permute-start(bf16[16,1024]{1,0:T(8,128)(2,1)S(1)} %copy-done.1), channel_id=1, source_target_pairs={{0,1},{1,0},{2,3},{3,2},{4,5},{5,4},{6,7},{7,6},{8,9},{9,8},{10,11... | collective-permute-start | bytes 98312 | tf_op jit(solution)/shard_map/ppermute | solution.py:24
  10.7 6.0 %copy-start = (bf16[1,1,4096,256]{3,2,1,0:T(8,128)(2,1)S(1)}, bf16[1,1,4096,256]{3,2,1,0:T(8,128)(2,1)}, u32[]{:S(2)}) copy-start(bf16[1,1,4096,256]{3,2,1,0:T(8,128)(2,1)} %param.7) | copy-start | bytes 6291460
  11.2 9.0 %collective-permute-start.3 = (bf16[272,128]{1,0:T(8,128)(2,1)S(1)}, bf16[272,128]{1,0:T(8,128)(2,1)S(1)}, u32[]{:S(2)}, u32[]{:S(2)}) collective-permute-start(bf16[272,128]{1,0:T(8,128)(2,1)S(1)} %get-tuple-element.24), channel_id=1, source_target_pairs={{0,8},{1,9},{4,28},{5,29},{8,0},{9,1},{12,20},{13,21},{16,24},{17,... | collective-permute-start | bytes 208904 | tf_op jit(solution)/shard_map/ppermute | solution.py:46
  13.4 6.9 %collective-permute-start.7 = (bf16[272,128]{1,0:T(8,128)(2,1)S(1)}, bf16[272,128]{1,0:T(8,128)(2,1)S(1)}, u32[]{:S(2)}, u32[]{:S(2)}) collective-permute-start(bf16[272,128]{1,0:T(8,128)(2,1)S(1)} %suffix_away.5), channel_id=1, source_target_pairs={{0,9},{1,8},{4,29},{5,28},{8,1},{9,0},{12,21},{13,20},{16,25},{17,... | collective-permute-start | bytes 208904 | tf_op jit(solution)/shard_map/ppermute | solution.py:46
  15.4 7.3 %collective-permute-start.5 = (bf16[272,128]{1,0:T(8,128)(2,1)S(1)}, bf16[272,128]{1,0:T(8,128)(2,1)S(1)}, u32[]{:S(2)}, u32[]{:S(2)}) collective-permute-start(bf16[272,128]{1,0:T(8,128)(2,1)S(1)} %suffix_away.4), channel_id=1, source_target_pairs={{0,16},{1,17},{4,21},{5,20},{8,24},{9,25},{12,29},{13,28},{16,0},{... | collective-permute-start | bytes 208904 | tf_op jit(solution)/shard_map/ppermute | solution.py:46
  19.1 4.1 %collective-permute-start.9 = (bf16[144,128]{1,0:T(8,128)(2,1)S(1)}, bf16[144,128]{1,0:T(8,128)(2,1)S(1)}, u32[]{:S(2)}, u32[]{:S(2)}) collective-permute-start(bf16[144,128]{1,0:T(8,128)(2,1)S(1)} %get-tuple-element.28), channel_id=1, source_target_pairs={{0,1},{1,0},{2,3},{3,2},{4,5},{5,4},{6,7},{7,6},{8,9},{9,8},{10,11... | collective-permute-start | bytes 110600 | tf_op jit(solution)/shard_map/ppermute | solution.py:24
  22.7 1.3 %collective-permute-start.10 = (bf16[144,128]{1,0:T(8,128)(2,1)S(1)}, bf16[144,128]{1,0:T(8,128)(2,1)S(1)}, u32[]{:S(2)}, u32[]{:S(2)}) collective-permute-start(bf16[144,128]{1,0:T(8,128)(2,1)S(1)} %sibling_share.1), channel_id=1, source_target_pairs={{0,4},{4,0},{1,5},{5,1},{2,6},{6,2},{3,7},{7,3},{8,12},{12,8},{9,1... | collective-permute-start | bytes 110600 | tf_op jit(solution)/shard_map/ppermute | solution.py:24

commit v19 on v18

--- a/solution.py
+++ b/solution.py
@@ -15,6 +15,7 @@
 VECS = HEADS * BEAMS
 STAT_ROWS = 16
 CHUNK = 512
+SURELY_VALID = 1024
 
 big_negative = -1e30
 to_exp2 = HD ** (-0.5) * 1.4426950408889634
@@ -150,7 +151,9 @@
     scores = [scores_of(prompt_ref[chunk, :HD], vectors) for chunk in chunks]
     place = iota(scores[0].shape, 0)
     scores = [
-        jnp.where(place < valid - chunk.start, score, big_negative)
+        score
+        if chunk.stop <= SURELY_VALID
+        else jnp.where(place < valid - chunk.start, score, big_negative)
         for chunk, score in zip(chunks, scores)
     ]
     tops = [jnp.max(score, axis=0, keepdims=True) for score in scores]
@@ -164,17 +167,14 @@
 
 
 def prepare_kernel(
-    capacity, near_ref, table, parents, far_ref,
-    home_keys_ref, home_values_ref, keys_ref, values_ref, member_ref, rows_ref, near, sem,
+    capacity, near, table, parents, far_ref,
+    home_keys_ref, home_values_ref, keys_ref, values_ref, member_ref, rows_ref,
 ):
     n_req = lax.axis_size("z")
     slots, half, _ = near.shape
     rows = table.shape[1]
     n_batch = rows // BEAMS
     z, core = lax.axis_index("z"), lax.axis_index("core")
-
-    copy = pltpu.make_async_copy(near_ref, near, sem)
-    copy.start()
 
     slot = iota((2 * slots, rows), 0)
     mine = slot < slots
@@ -198,7 +198,6 @@
         found.append(jnp.sum(jnp.where(chosen, place + 1, 0), axis=0, keepdims=True))
     found = jnp.concatenate(found, axis=0)
 
-    copy.wait()
     requests = [z * 2 + core]
     for mask in masks_here(n_req):
         requests += [(z ^ mask) * 2, (z ^ mask) * 2 + 1]
@@ -358,18 +357,14 @@
             pltpu.VMEM((n_req, HD, 2 * capacity * half), jnp.bfloat16),
             pltpu.VMEM((1 + n_req, 2 * capacity, VECS), jnp.float32),
         ),
-        in_specs=[hbm] + [vmem] * 3,
+        in_specs=[vmem] * 4,
         out_specs=(vmem,) * 5,
-        scratch_shapes=[
-            pltpu.VMEM((2 * slots + 8, VECS), jnp.float32),
-            pltpu.VMEM((slots, half, width), jnp.bfloat16),
-            pltpu.SemaphoreType.DMA,
-        ],
+        scratch_shapes=[pltpu.VMEM((2 * slots + 8, VECS), jnp.float32)],
         compiler_params=params,
         cost_estimate=some,
         name="prepare",
     )(
-        in_hbm(near),
+        near,
         table,
         row_parents,
         far,

time: 25 us -> 24.8 us (level)
  starting transfers between devices: 12.9 us -> 13.8 us
  Pallas kernels: 7.23 us -> 6.4 us
    ppermute x6, starting transfers between devices: 10.7 us -> 11.6 us  [exchanged(): return lax.ppermute(value, ('z', 'core', 'pair'), pairs)]
    pallas_call x1, Pallas kernels: 1.67 us -> 0.77 us  [on_device(): pl.pallas_call(functools.partial(prepare_kernel, capacity), out_shape=(pl...]
  transfers between devices with their start and end apart: 11 -> 11, of which waited for: 4 -> 4; matrix products, arithmetic and copies ran while one was open for 0% -> 0% of each run, Pallas kernels for 26% -> 23%
where the time goes in v19:
time: 24.8 us; the launch traced here: 24.6 us
  starting transfers between devices  13.8 us (56%)
  Pallas kernels  6.4 us (26%)
  waiting for transfers between devices  3.62 us (15%)
  between operations  0.75 us (3%)
    ppermute x6, starting transfers between devices, exchanged(): return lax.ppermute(value, ('z', 'core', 'pair'), pairs)  11.6 us
    pallas_call x1, Pallas kernels, on_device(): pl.pallas_call(home_kernel, out_shape=(pltpu.VMEM((HD, VECS), jnp.float32...  2.51 us
    ppermute x5, starting transfers between devices, swapped(): return lax.ppermute(value, axis, [(0, 1), (1, 0)])  2.23 us
    ppermute x6, waiting for transfers between devices, exchanged(): return lax.ppermute(value, ('z', 'core', 'pair'), pairs)  2.2 us
    pallas_call x3, Pallas kernels, on_device(): pl.pallas_call(functools.partial(away_kernel, 2 * ((k + 1) // 2)), out_sh...  1.51 us
    ppermute x5, waiting for transfers between devices, swapped(): return lax.ppermute(value, axis, [(0, 1), (1, 0)])  1.42 us
    pallas_call x1, Pallas kernels, on_device(): pl.pallas_call(stage_kernel, out_shape=tuple((pltpu.VMEM(each.shape, each...  0.79 us
    pallas_call x1, Pallas kernels, on_device(): pl.pallas_call(functools.partial(prepare_kernel, capacity), out_shape=(pl...  0.77 us
  transfers between devices with their start and end apart: 11, of which 4 were waited for; matrix products, arithmetic and copies ran while one was open for 0% of the time, Pallas kernels for 23%

profile of v19, /device:TPU:0, one launch (start us, length us, event | category | flops | bytes accessed | tf_op | source)
XLA Modules:
  0.0 24.6 jit_solution(9201706693904215439)
XLA Ops:
  0.0 0.5 %collective-permute-start.1 = (bf16[16,1024]{1,0:T(8,128)(2,1)}, bf16[16,1024]{1,0:T(8,128)(2,1)S(1)}, u32[]{:S(2)}, u32[]{:S(2)}) collective-permute-start(bf16[16,1024]{1,0:T(8,128)(2,1)} %refs_0_.1), channel_id=1, source_target_pairs={{0,4},{4,0},{1,5},{5,1},{2,6},{6,2},{3,7},{7,3},{8,12},{12,8},{9,1... | collective-permute-start | bytes 98312 | tf_op jit(solution)/shard_map/ppermute | solution.py:25
  0.5 0.1 collective-permute-start
  0.5 0.8 %stage.1 = (bf16[16,1024]{1,0:T(8,128)(2,1)S(1)}, s32[4,128]{1,0:T(4,128)S(1)}, s32[1,128]{1,0:T(1,128)S(1)}) custom-call(bf16[16,1024]{1,0:T(8,128)(2,1)} %refs_0_.1, s32[4,128]{1,0:T(4,128)} %bitcast.7, s32[1,128]{1,0:T(1,128)} %bitcast.8), custom_call_target="tpu_custom_call" | custom-call | tf_op jit(solution)/shard_map/stage/pallas_call | solution.py:329
  1.3 0.2 collective-permute-done.1.sibling_ref
  1.5 3.0 %collective-permute-start.2 = (bf16[2,16,1024]{2,1,0:T(8,128)(2,1)S(1)}, bf16[2,16,1024]{2,1,0:T(8,128)(2,1)S(1)}, u32[]{:S(2)}, u32[]{:S(2)}) collective-permute-start(bf16[2,16,1024]{2,1,0:T(8,128)(2,1)S(1)} %both_cores.1), channel_id=1, source_target_pairs={{0,8},{1,9},{4,28},{5,29},{8,0},{9,1},{12,20},{13,21},{16,24},{17,... | collective-permute-start | bytes 196616 | tf_op jit(solution)/shard_map/ppermute | solution.py:47
  4.5 1.4 %collective-permute-start.6 = (bf16[2,16,1024]{2,1,0:T(8,128)(2,1)S(1)}, bf16[2,16,1024]{2,1,0:T(8,128)(2,1)S(1)}, u32[]{:S(2)}, u32[]{:S(2)}) collective-permute-start(bf16[2,16,1024]{2,1,0:T(8,128)(2,1)S(1)} %both_cores.1), channel_id=1, source_target_pairs={{0,9},{1,8},{4,29},{5,28},{8,1},{9,0},{12,21},{13,20},{16,25},{17,... | collective-permute-start | bytes 196616 | tf_op jit(solution)/shard_map/ppermute | solution.py:47
  5.9 2.6 %collective-permute-start.4 = (bf16[2,16,1024]{2,1,0:T(8,128)(2,1)S(1)}, bf16[2,16,1024]{2,1,0:T(8,128)(2,1)S(1)}, u32[]{:S(2)}, u32[]{:S(2)}) collective-permute-start(bf16[2,16,1024]{2,1,0:T(8,128)(2,1)S(1)} %both_cores.1), channel_id=1, source_target_pairs={{0,16},{1,17},{4,21},{5,20},{8,24},{9,25},{12,29},{13,28},{16,0},{... | collective-permute-start | bytes 196616 | tf_op jit(solution)/shard_map/ppermute | solution.py:47
  8.5 0.5 %collective-permute-start.8 = (bf16[16,1024]{1,0:T(8,128)(2,1)S(1)}, bf16[16,1024]{1,0:T(8,128)(2,1)S(1)}, u32[]{:S(2)}, u32[]{:S(2)}) collective-permute-start(bf16[16,1024]{1,0:T(8,128)(2,1)S(1)} %copy-done.2), channel_id=1, source_target_pairs={{0,1},{1,0},{2,3},{3,2},{4,5},{5,4},{6,7},{7,6},{8,9},{9,8},{10,11... | collective-permute-start | bytes 98312 | tf_op jit(solution)/shard_map/ppermute | solution.py:25
  9.0 0.0 collective-permute-done.far_ref
  9.0 0.8 %prepare.1 = (bf16[1,512,128]{2,1,0:T(8,128)(2,1)S(1)}, bf16[1,128,512]{2,1,0:T(8,128)(2,1)S(1)}, bf16[4,512,128]{2,1,0:T(8,128)(2,1)S(1)}, bf16[4,128,512]{2,1,0:T(8,128)(2,1)S(1)}, f32[5,8,128]{2,1,0:T(8,128)S(1)}) custom-call(bf16[32,64,256]{2,1,0:T(8,128)(2,1)S(1)} %bitcast.6, s32[4,128]{1,0:T(4,128)S(1)} %get-tuple-element.18.table, ...), custom_call_target="tpu_custom_call" | custom-call | flops 200000000 | bytes 2097152 | tf_op jit(solution)/shard_map/prepare/pallas_call | solution.py:351
  9.8 0.0 copy-start
  9.8 0.5 %suffix_away.3 = (bf16[272,128]{1,0:T(8,128)(2,1)S(1)}, f32[8,128]{1,0:T(8,128)S(1)}) custom-call(bf16[4,512,128]{2,1,0:T(8,128)(2,1)S(1)} %get-tuple-element.20.keys_ref, bf16[4,128,512]{2,1,0:T(8,128)(2,1)S(1)} %get-tuple-element.21.values_ref, f32[5,8,128]{2,1,0:T(8,128)S(1)} %get-tuple-element.22.member_ref, ...), custom_call_target="tpu_custom_call" | custom-call | flops 200000000 | bytes 2097152 | tf_op jit(solution)/shard_map/suffix_away/pallas_call | solution.py:378
  10.4 1.6 %collective-permute-start.3 = (bf16[272,128]{1,0:T(8,128)(2,1)S(1)}, bf16[272,128]{1,0:T(8,128)(2,1)S(1)}, u32[]{:S(2)}, u32[]{:S(2)}) collective-permute-start(bf16[272,128]{1,0:T(8,128)(2,1)S(1)} %get-tuple-element.24), channel_id=1, source_target_pairs={{0,8},{1,9},{4,28},{5,29},{8,0},{9,1},{12,20},{13,21},{16,24},{17,... | collective-permute-start | bytes 208904 | tf_op jit(solution)/shard_map/ppermute | solution.py:47
  12.0 0.5 %suffix_away.5 = bf16[272,128]{1,0:T(8,128)(2,1)S(1)} custom-call(bf16[4,512,128]{2,1,0:T(8,128)(2,1)S(1)} %get-tuple-element.20.keys_ref, bf16[4,128,512]{2,1,0:T(8,128)(2,1)S(1)} %get-tuple-element.21.values_ref, f32[5,8,128]{2,1,0:T(8,128)S(1)} %get-tuple-element.22.member_ref, bf16[2,16,1024]{2,1,0:T(8,128)(2,1)S(1)} %collective-permute-done.6.message_ref), custom_call_target="tpu_custom_call" | custom-call | flops 200000000 | bytes 2097152 | tf_op jit(solution)/shard_map/suffix_away/pallas_call | solution.py:378
  12.5 1.4 %collective-permute-start.7 = (bf16[272,128]{1,0:T(8,128)(2,1)S(1)}, bf16[272,128]{1,0:T(8,128)(2,1)S(1)}, u32[]{:S(2)}, u32[]{:S(2)}) collective-permute-start(bf16[272,128]{1,0:T(8,128)(2,1)S(1)} %suffix_away.5), channel_id=1, source_target_pairs={{0,9},{1,8},{4,29},{5,28},{8,1},{9,0},{12,21},{13,20},{16,25},{17,... | collective-permute-start | bytes 208904 | tf_op jit(solution)/shard_map/ppermute | solution.py:47
  14.0 0.5 %suffix_away.4 = bf16[272,128]{1,0:T(8,128)(2,1)S(1)} custom-call(bf16[4,512,128]{2,1,0:T(8,128)(2,1)S(1)} %get-tuple-element.20.keys_ref, bf16[4,128,512]{2,1,0:T(8,128)(2,1)S(1)} %get-tuple-element.21.values_ref, f32[5,8,128]{2,1,0:T(8,128)S(1)} %get-tuple-element.22.member_ref, bf16[2,16,1024]{2,1,0:T(8,128)(2,1)S(1)} %collective-permute-done.4.message_ref), custom_call_target="tpu_custom_call" | custom-call | flops 200000000 | bytes 2097152 | tf_op jit(solution)/shard_map/suffix_away/pallas_call | solution.py:378
  14.5 1.6 %collective-permute-start.5 = (bf16[272,128]{1,0:T(8,128)(2,1)S(1)}, bf16[272,128]{1,0:T(8,128)(2,1)S(1)}, u32[]{:S(2)}, u32[]{:S(2)}) collective-permute-start(bf16[272,128]{1,0:T(8,128)(2,1)S(1)} %suffix_away.4), channel_id=1, source_target_pairs={{0,16},{1,17},{4,21},{5,20},{8,24},{9,25},{12,29},{13,28},{16,0},{... | collective-permute-start | bytes 208904 | tf_op jit(solution)/shard_map/ppermute | solution.py:47
  16.7 2.5 %home_part.1 = (f32[128,128]{1,0:T(8,128)S(1)}, f32[8,128]{1,0:T(8,128)S(1)}, bf16[144,128]{1,0:T(8,128)(2,1)S(1)}) custom-call(s32[1]{0:T(128)S(6)} %copy.7.length_ref, bf16[1,512,128]{2,1,0:T(8,128)(2,1)S(1)} %get-tuple-element.25.keys_ref, bf16[1,128,512]{2,1,0:T(8,128)(2,1)S(1)} %get-tuple-element.26.values_ref, ...), custom_call_target="tpu_custom_call" | custom-call | flops 536870912 | bytes 2097152 | tf_op jit(solution)/shard_map/home_part/pallas_call | solution.py:390
  19.2 1.1 %collective-permute-start.9 = (bf16[144,128]{1,0:T(8,128)(2,1)S(1)}, bf16[144,128]{1,0:T(8,128)(2,1)S(1)}, u32[]{:S(2)}, u32[]{:S(2)}) collective-permute-start(bf16[144,128]{1,0:T(8,128)(2,1)S(1)} %get-tuple-element.28), channel_id=1, source_target_pairs={{0,1},{1,0},{2,3},{3,2},{4,5},{5,4},{6,7},{7,6},{8,9},{9,8},{10,11... | collective-permute-start | bytes 110600 | tf_op jit(solution)/shard_map/ppermute | solution.py:25
  20.3 2.2 %collective-permute-done.5.rest_1_ = bf16[272,128]{1,0:T(8,128)(2,1)S(1)} collective-permute-done((bf16[272,128]{1,0:T(8,128)(2,1)S(1)}, bf16[272,128]{1,0:T(8,128)(2,1)S(1)}, u32[]{:S(2)}, u32[]{:S(2)}) %collective-permute-start.5) | collective-permute-done | bytes 69664 | tf_op jit(solution)/shard_map/ppermute | solution.py:47
  22.6 0.1 collective-permute-start.10
  22.7 0.7 %collective-permute-done.9.rest_3_ = bf16[144,128]{1,0:T(8,128)(2,1)S(1)} collective-permute-done((bf16[144,128]{1,0:T(8,128)(2,1)S(1)}, bf16[144,128]{1,0:T(8,128)(2,1)S(1)}, u32[]{:S(2)}, u32[]{:S(2)}) %collective-permute-start.9) | collective-permute-done | bytes 36896 | tf_op jit(solution)/shard_map/ppermute | solution.py:25
  23.4 0.5 %collective-permute-done.10.rest_4_ = bf16[144,128]{1,0:T(8,128)(2,1)S(1)} collective-permute-done((bf16[144,128]{1,0:T(8,128)(2,1)S(1)}, bf16[144,128]{1,0:T(8,128)(2,1)S(1)}, u32[]{:S(2)}, u32[]{:S(2)}) %collective-permute-start.10) | collective-permute-done | bytes 36896 | tf_op jit(solution)/shard_map/ppermute | solution.py:25
  23.9 0.8 %combine.1 = f32[16,1024]{1,0:T(8,128)} custom-call(bf16[272,128]{1,0:T(8,128)(2,1)S(1)} %collective-permute-done.3.rest_0_, bf16[272,128]{1,0:T(8,128)(2,1)S(1)} %collective-permute-done.5.rest_1_, bf16[272,128]{1,0:T(8,128)(2,1)S(1)} %collective-permute-done.7.rest_2_, bf16[144,128]{1,0:T(8,128)(2,1)S(1)} %collective-permute-done.9.rest_3_, ...), custom_call_target="tpu_custom_call" | custom-call | tf_op jit(solution)/shard_map/combine/pallas_call | solution.py:416
  (13 shorter events, 0.1 us)
Async XLA Ops:
  0.0 1.5 %collective-permute-start.1 = (bf16[16,1024]{1,0:T(8,128)(2,1)}, bf16[16,1024]{1,0:T(8,128)(2,1)S(1)}, u32[]{:S(2)}, u32[]{:S(2)}) collective-permute-start(bf16[16,1024]{1,0:T(8,128)(2,1)} %refs_0_.1), channel_id=1, source_target_pairs={{0,4},{4,0},{1,5},{5,1},{2,6},{6,2},{3,7},{7,3},{8,12},{12,8},{9,1... | collective-permute-start | bytes 98312 | tf_op jit(solution)/shard_map/ppermute | solution.py:25
  0.5 8.6 %collective-permute-start = (bf16[32,64,256]{2,1,0:T(8,128)(2,1)}, bf16[32,64,256]{2,1,0:T(8,128)(2,1)S(1)}, u32[]{:S(2)}, u32[]{:S(2)}) collective-permute-start(bf16[32,64,256]{2,1,0:T(8,128)(2,1)} %bitcast.5), channel_id=1, source_target_pairs={{0,4},{4,0},{1,5},{5,1},{2,6},{6,2},{3,7},{7,3},{8,12},{12,8},{9,1... | collective-permute-start | bytes 3145736 | tf_op jit(solution)/shard_map/ppermute | solution.py:25
  1.5 7.0 %copy-start.2 = (bf16[16,1024]{1,0:T(8,128)(2,1)S(1)}, bf16[16,1024]{1,0:T(8,128)(2,1)}, u32[]{:S(2)}) copy-start(bf16[16,1024]{1,0:T(8,128)(2,1)} %refs_0_.1) | copy-start | bytes 98308
  1.5 7.5 %copy-start.1 = (bf16[32,1,64,256]{3,2,1,0:T(8,128)(2,1)S(1)}, bf16[32,1,64,256]{3,2,1,0:T(8,128)(2,1)}, u32[]{:S(2)}) copy-start(bf16[32,1,64,256]{3,2,1,0:T(8,128)(2,1)} %param.8) | copy-start | bytes 3145732
  1.5 8.3 %collective-permute-start.2 = (bf16[2,16,1024]{2,1,0:T(8,128)(2,1)S(1)}, bf16[2,16,1024]{2,1,0:T(8,128)(2,1)S(1)}, u32[]{:S(2)}, u32[]{:S(2)}) collective-permute-start(bf16[2,16,1024]{2,1,0:T(8,128)(2,1)S(1)} %both_cores.1), channel_id=1, source_target_pairs={{0,8},{1,9},{4,28},{5,29},{8,0},{9,1},{12,20},{13,21},{16,24},{17,... | collective-permute-start | bytes 196616 | tf_op jit(solution)/shard_map/ppermute | solution.py:47
  4.5 7.5 %collective-permute-start.6 = (bf16[2,16,1024]{2,1,0:T(8,128)(2,1)S(1)}, bf16[2,16,1024]{2,1,0:T(8,128)(2,1)S(1)}, u32[]{:S(2)}, u32[]{:S(2)}) collective-permute-start(bf16[2,16,1024]{2,1,0:T(8,128)(2,1)S(1)} %both_cores.1), channel_id=1, source_target_pairs={{0,9},{1,8},{4,29},{5,28},{8,1},{9,0},{12,21},{13,20},{16,25},{17,... | collective-permute-start | bytes 196616 | tf_op jit(solution)/shard_map/ppermute | solution.py:47
  5.9 8.0 %collective-permute-start.4 = (bf16[2,16,1024]{2,1,0:T(8,128)(2,1)S(1)}, bf16[2,16,1024]{2,1,0:T(8,128)(2,1)S(1)}, u32[]{:S(2)}, u32[]{:S(2)}) collective-permute-start(bf16[2,16,1024]{2,1,0:T(8,128)(2,1)S(1)} %both_cores.1), channel_id=1, source_target_pairs={{0,16},{1,17},{4,21},{5,20},{8,24},{9,25},{12,29},{13,28},{16,0},{... | collective-permute-start | bytes 196616 | tf_op jit(solution)/shard_map/ppermute | solution.py:47
  8.5 8.2 %collective-permute-start.8 = (bf16[16,1024]{1,0:T(8,128)(2,1)S(1)}, bf16[16,1024]{1,0:T(8,128)(2,1)S(1)}, u32[]{:S(2)}, u32[]{:S(2)}) collective-permute-start(bf16[16,1024]{1,0:T(8,128)(2,1)S(1)} %copy-done.2), channel_id=1, source_target_pairs={{0,1},{1,0},{2,3},{3,2},{4,5},{5,4},{6,7},{7,6},{8,9},{9,8},{10,11... | collective-permute-start | bytes 98312 | tf_op jit(solution)/shard_map/ppermute | solution.py:25
  9.8 6.9 %copy-start = (bf16[1,1,4096,256]{3,2,1,0:T(8,128)(2,1)S(1)}, bf16[1,1,4096,256]{3,2,1,0:T(8,128)(2,1)}, u32[]{:S(2)}) copy-start(bf16[1,1,4096,256]{3,2,1,0:T(8,128)(2,1)} %param.7) | copy-start | bytes 6291460
  10.4 10.0 %collective-permute-start.3 = (bf16[272,128]{1,0:T(8,128)(2,1)S(1)}, bf16[272,128]{1,0:T(8,128)(2,1)S(1)}, u32[]{:S(2)}, u32[]{:S(2)}) collective-permute-start(bf16[272,128]{1,0:T(8,128)(2,1)S(1)} %get-tuple-element.24), channel_id=1, source_target_pairs={{0,8},{1,9},{4,28},{5,29},{8,0},{9,1},{12,20},{13,21},{16,24},{17,... | collective-permute-start | bytes 208904 | tf_op jit(solution)/shard_map/ppermute | solution.py:47
  12.5 7.8 %collective-permute-start.7 = (bf16[272,128]{1,0:T(8,128)(2,1)S(1)}, bf16[272,128]{1,0:T(8,128)(2,1)S(1)}, u32[]{:S(2)}, u32[]{:S(2)}) collective-permute-start(bf16[272,128]{1,0:T(8,128)(2,1)S(1)} %suffix_away.5), channel_id=1, source_target_pairs={{0,9},{1,8},{4,29},{5,28},{8,1},{9,0},{12,21},{13,20},{16,25},{17,... | collective-permute-start | bytes 208904 | tf_op jit(solution)/shard_map/ppermute | solution.py:47
  14.5 8.1 %collective-permute-start.5 = (bf16[272,128]{1,0:T(8,128)(2,1)S(1)}, bf16[272,128]{1,0:T(8,128)(2,1)S(1)}, u32[]{:S(2)}, u32[]{:S(2)}) collective-permute-start(bf16[272,128]{1,0:T(8,128)(2,1)S(1)} %suffix_away.4), channel_id=1, source_target_pairs={{0,16},{1,17},{4,21},{5,20},{8,24},{9,25},{12,29},{13,28},{16,0},{... | collective-permute-start | bytes 208904 | tf_op jit(solution)/shard_map/ppermute | solution.py:47
  19.2 4.2 %collective-permute-start.9 = (bf16[144,128]{1,0:T(8,128)(2,1)S(1)}, bf16[144,128]{1,0:T(8,128)(2,1)S(1)}, u32[]{:S(2)}, u32[]{:S(2)}) collective-permute-start(bf16[144,128]{1,0:T(8,128)(2,1)S(1)} %get-tuple-element.28), channel_id=1, source_target_pairs={{0,1},{1,0},{2,3},{3,2},{4,5},{5,4},{6,7},{7,6},{8,9},{9,8},{10,11... | collective-permute-start | bytes 110600 | tf_op jit(solution)/shard_map/ppermute | solution.py:25
  22.6 1.3 %collective-permute-start.10 = (bf16[144,128]{1,0:T(8,128)(2,1)S(1)}, bf16[144,128]{1,0:T(8,128)(2,1)S(1)}, u32[]{:S(2)}, u32[]{:S(2)}) collective-permute-start(bf16[144,128]{1,0:T(8,128)(2,1)S(1)} %sibling_share.1), channel_id=1, source_target_pairs={{0,4},{4,0},{1,5},{5,1},{2,6},{6,2},{3,7},{7,3},{8,12},{12,8},{9,1... | collective-permute-start | bytes 110600 | tf_op jit(solution)/shard_map/ppermute | solution.py:25

commit v20 on v19

--- a/solution.py
+++ b/solution.py
@@ -26,7 +26,7 @@
 
 
 def shares(n_req):
-    both = n_req // 2
+    both = n_req - 1
     rest = [d for d in range(1, n_req) if d != both]
     return both, (rest[: len(rest) // 2], rest[len(rest) // 2 :])
 

time: 24.8 us -> 24.8 us (level)
    ppermute x6, starting transfers between devices: 11.6 us -> 12.2 us  [exchanged(): return lax.ppermute(value, ('z', 'core', 'pair'), pairs)]
    ppermute x5, starting transfers between devices: 2.23 us -> 1.74 us  [swapped(): return lax.ppermute(value, axis, [(0, 1), (1, 0)])]
    ppermute x6, waiting for transfers between devices: 2.2 us -> 1.78 us  [exchanged(): return lax.ppermute(value, ('z', 'core', 'pair'), pairs)]
    ppermute x5, waiting for transfers between devices: 1.42 us -> 1.72 us  [swapped(): return lax.ppermute(value, axis, [(0, 1), (1, 0)])]
  transfers between devices with their start and end apart: 11 -> 11, of which waited for: 4 -> 3; matrix products, arithmetic and copies ran while one was open for 0% -> 0% of each run, Pallas kernels for 23% -> 23%
where the time goes in v20:
time: 24.8 us; the launch traced here: 24.6 us
  starting transfers between devices  13.9 us (56%)
  Pallas kernels  6.41 us (26%)
  waiting for transfers between devices  3.51 us (14%)
  between operations  0.76 us (3%)
    ppermute x6, starting transfers between devices, exchanged(): return lax.ppermute(value, ('z', 'core', 'pair'), pairs)  12.2 us
    pallas_call x1, Pallas kernels, on_device(): pl.pallas_call(home_kernel, out_shape=(pltpu.VMEM((HD, VECS), jnp.float32...  2.51 us
    ppermute x6, waiting for transfers between devices, exchanged(): return lax.ppermute(value, ('z', 'core', 'pair'), pairs)  1.78 us
    ppermute x5, starting transfers between devices, swapped(): return lax.ppermute(value, axis, [(0, 1), (1, 0)])  1.74 us
    ppermute x5, waiting for transfers between devices, swapped(): return lax.ppermute(value, axis, [(0, 1), (1, 0)])  1.72 us
    pallas_call x3, Pallas kernels, on_device(): pl.pallas_call(functools.partial(away_kernel, 2 * ((k + 1) // 2)), out_sh...  1.51 us
    pallas_call x1, Pallas kernels, on_device(): pl.pallas_call(stage_kernel, out_shape=tuple((pltpu.VMEM(each.shape, each...  0.79 us
    pallas_call x1, Pallas kernels, on_device(): pl.pallas_call(functools.partial(prepare_kernel, capacity), out_shape=(pl...  0.77 us
  transfers between devices with their start and end apart: 11, of which 3 were waited for; matrix products, arithmetic and copies ran while one was open for 0% of the time, Pallas kernels for 23%

profile of v20, /device:TPU:0, one launch (start us, length us, event | category | flops | bytes accessed | tf_op | source)
XLA Modules:
  0.0 24.6 jit_solution(8020588712716101419)
XLA Ops:
  0.0 0.5 %collective-permute-start.1 = (bf16[16,1024]{1,0:T(8,128)(2,1)}, bf16[16,1024]{1,0:T(8,128)(2,1)S(1)}, u32[]{:S(2)}, u32[]{:S(2)}) collective-permute-start(bf16[16,1024]{1,0:T(8,128)(2,1)} %refs_0_.1), channel_id=1, source_target_pairs={{0,4},{4,0},{1,5},{5,1},{2,6},{6,2},{3,7},{7,3},{8,12},{12,8},{9,1... | collective-permute-start | bytes 98312 | tf_op jit(solution)/shard_map/ppermute | solution.py:25
  0.5 0.1 collective-permute-start
  0.5 0.8 %stage.1 = (bf16[16,1024]{1,0:T(8,128)(2,1)S(1)}, s32[4,128]{1,0:T(4,128)S(1)}, s32[1,128]{1,0:T(1,128)S(1)}) custom-call(bf16[16,1024]{1,0:T(8,128)(2,1)} %refs_0_.1, s32[4,128]{1,0:T(4,128)} %bitcast.7, s32[1,128]{1,0:T(1,128)} %bitcast.8), custom_call_target="tpu_custom_call" | custom-call | tf_op jit(solution)/shard_map/stage/pallas_call | solution.py:329
  1.3 0.2 collective-permute-done.1.sibling_ref
  1.5 3.0 %collective-permute-start.2 = (bf16[2,16,1024]{2,1,0:T(8,128)(2,1)S(1)}, bf16[2,16,1024]{2,1,0:T(8,128)(2,1)S(1)}, u32[]{:S(2)}, u32[]{:S(2)}) collective-permute-start(bf16[2,16,1024]{2,1,0:T(8,128)(2,1)S(1)} %both_cores.1), channel_id=1, source_target_pairs={{0,8},{1,9},{4,20},{5,21},{8,0},{9,1},{12,28},{13,29},{16,24},{17,... | collective-permute-start | bytes 196616 | tf_op jit(solution)/shard_map/ppermute | solution.py:47
  4.5 1.4 %collective-permute-start.6 = (bf16[2,16,1024]{2,1,0:T(8,128)(2,1)S(1)}, bf16[2,16,1024]{2,1,0:T(8,128)(2,1)S(1)}, u32[]{:S(2)}, u32[]{:S(2)}) collective-permute-start(bf16[2,16,1024]{2,1,0:T(8,128)(2,1)S(1)} %both_cores.1), channel_id=1, source_target_pairs={{0,9},{1,8},{4,21},{5,20},{8,1},{9,0},{12,29},{13,28},{16,25},{17,... | collective-permute-start | bytes 196616 | tf_op jit(solution)/shard_map/ppermute | solution.py:47
  5.9 3.6 %collective-permute-start.4 = (bf16[2,16,1024]{2,1,0:T(8,128)(2,1)S(1)}, bf16[2,16,1024]{2,1,0:T(8,128)(2,1)S(1)}, u32[]{:S(2)}, u32[]{:S(2)}) collective-permute-start(bf16[2,16,1024]{2,1,0:T(8,128)(2,1)S(1)} %both_cores.1), channel_id=1, source_target_pairs={{0,24},{1,25},{4,29},{5,28},{8,16},{9,17},{12,21},{13,20},{16,8},{... | collective-permute-start | bytes 196616 | tf_op jit(solution)/shard_map/ppermute | solution.py:47
  9.5 0.5 %collective-permute-start.8 = (bf16[16,1024]{1,0:T(8,128)(2,1)S(1)}, bf16[16,1024]{1,0:T(8,128)(2,1)S(1)}, u32[]{:S(2)}, u32[]{:S(2)}) collective-permute-start(bf16[16,1024]{1,0:T(8,128)(2,1)S(1)} %copy-done.2), channel_id=1, source_target_pairs={{0,1},{1,0},{2,3},{3,2},{4,5},{5,4},{6,7},{7,6},{8,9},{9,8},{10,11... | collective-permute-start | bytes 98312 | tf_op jit(solution)/shard_map/ppermute | solution.py:25
  10.1 0.8 %prepare.1 = (bf16[1,512,128]{2,1,0:T(8,128)(2,1)S(1)}, bf16[1,128,512]{2,1,0:T(8,128)(2,1)S(1)}, bf16[4,512,128]{2,1,0:T(8,128)(2,1)S(1)}, bf16[4,128,512]{2,1,0:T(8,128)(2,1)S(1)}, f32[5,8,128]{2,1,0:T(8,128)S(1)}) custom-call(bf16[32,64,256]{2,1,0:T(8,128)(2,1)S(1)} %bitcast.6, s32[4,128]{1,0:T(4,128)S(1)} %get-tuple-element.18.table, ...), custom_call_target="tpu_custom_call" | custom-call | flops 200000000 | bytes 2097152 | tf_op jit(solution)/shard_map/prepare/pallas_call | solution.py:351
  10.8 0.0 copy-start
  10.8 0.0 collective-permute-done.2.message_ref
  10.9 0.5 %suffix_away.3 = (bf16[272,128]{1,0:T(8,128)(2,1)S(1)}, f32[8,128]{1,0:T(8,128)S(1)}) custom-call(bf16[4,512,128]{2,1,0:T(8,128)(2,1)S(1)} %get-tuple-element.20.keys_ref, bf16[4,128,512]{2,1,0:T(8,128)(2,1)S(1)} %get-tuple-element.21.values_ref, f32[5,8,128]{2,1,0:T(8,128)S(1)} %get-tuple-element.22.member_ref, ...), custom_call_target="tpu_custom_call" | custom-call | flops 200000000 | bytes 2097152 | tf_op jit(solution)/shard_map/suffix_away/pallas_call | solution.py:378
  11.4 0.1 collective-permute-start.3
  11.4 0.0 collective-permute-done.6.message_ref
  11.5 0.5 %suffix_away.5 = bf16[272,128]{1,0:T(8,128)(2,1)S(1)} custom-call(bf16[4,512,128]{2,1,0:T(8,128)(2,1)S(1)} %get-tuple-element.20.keys_ref, bf16[4,128,512]{2,1,0:T(8,128)(2,1)S(1)} %get-tuple-element.21.values_ref, f32[5,8,128]{2,1,0:T(8,128)S(1)} %get-tuple-element.22.member_ref, bf16[2,16,1024]{2,1,0:T(8,128)(2,1)S(1)} %collective-permute-done.6.message_ref), custom_call_target="tpu_custom_call" | custom-call | flops 200000000 | bytes 2097152 | tf_op jit(solution)/shard_map/suffix_away/pallas_call | solution.py:378
  12.0 3.0 %collective-permute-start.7 = (bf16[272,128]{1,0:T(8,128)(2,1)S(1)}, bf16[272,128]{1,0:T(8,128)(2,1)S(1)}, u32[]{:S(2)}, u32[]{:S(2)}) collective-permute-start(bf16[272,128]{1,0:T(8,128)(2,1)S(1)} %suffix_away.5), channel_id=1, source_target_pairs={{0,9},{1,8},{4,21},{5,20},{8,1},{9,0},{12,29},{13,28},{16,25},{17,... | collective-permute-start | bytes 208904 | tf_op jit(solution)/shard_map/ppermute | solution.py:47
  15.0 0.5 %suffix_away.4 = bf16[272,128]{1,0:T(8,128)(2,1)S(1)} custom-call(bf16[4,512,128]{2,1,0:T(8,128)(2,1)S(1)} %get-tuple-element.20.keys_ref, bf16[4,128,512]{2,1,0:T(8,128)(2,1)S(1)} %get-tuple-element.21.values_ref, f32[5,8,128]{2,1,0:T(8,128)S(1)} %get-tuple-element.22.member_ref, bf16[2,16,1024]{2,1,0:T(8,128)(2,1)S(1)} %collective-permute-done.4.message_ref), custom_call_target="tpu_custom_call" | custom-call | flops 200000000 | bytes 2097152 | tf_op jit(solution)/shard_map/suffix_away/pallas_call | solution.py:378
  15.5 1.1 %collective-permute-start.5 = (bf16[272,128]{1,0:T(8,128)(2,1)S(1)}, bf16[272,128]{1,0:T(8,128)(2,1)S(1)}, u32[]{:S(2)}, u32[]{:S(2)}) collective-permute-start(bf16[272,128]{1,0:T(8,128)(2,1)S(1)} %suffix_away.4), channel_id=1, source_target_pairs={{0,24},{1,25},{4,29},{5,28},{8,16},{9,17},{12,21},{13,20},{16,8},{... | collective-permute-start | bytes 208904 | tf_op jit(solution)/shard_map/ppermute | solution.py:47
  17.3 2.5 %home_part.1 = (f32[128,128]{1,0:T(8,128)S(1)}, f32[8,128]{1,0:T(8,128)S(1)}, bf16[144,128]{1,0:T(8,128)(2,1)S(1)}) custom-call(s32[1]{0:T(128)S(6)} %copy.7.length_ref, bf16[1,512,128]{2,1,0:T(8,128)(2,1)S(1)} %get-tuple-element.25.keys_ref, bf16[1,128,512]{2,1,0:T(8,128)(2,1)S(1)} %get-tuple-element.26.values_ref, ...), custom_call_target="tpu_custom_call" | custom-call | flops 536870912 | bytes 2097152 | tf_op jit(solution)/shard_map/home_part/pallas_call | solution.py:390
  19.8 0.6 %collective-permute-start.9 = (bf16[144,128]{1,0:T(8,128)(2,1)S(1)}, bf16[144,128]{1,0:T(8,128)(2,1)S(1)}, u32[]{:S(2)}, u32[]{:S(2)}) collective-permute-start(bf16[144,128]{1,0:T(8,128)(2,1)S(1)} %get-tuple-element.28), channel_id=1, source_target_pairs={{0,1},{1,0},{2,3},{3,2},{4,5},{5,4},{6,7},{7,6},{8,9},{9,8},{10,11... | collective-permute-start | bytes 110600 | tf_op jit(solution)/shard_map/ppermute | solution.py:25
  20.4 1.8 %collective-permute-done.5.rest_1_ = bf16[272,128]{1,0:T(8,128)(2,1)S(1)} collective-permute-done((bf16[272,128]{1,0:T(8,128)(2,1)S(1)}, bf16[272,128]{1,0:T(8,128)(2,1)S(1)}, u32[]{:S(2)}, u32[]{:S(2)}) %collective-permute-start.5) | collective-permute-done | bytes 69664 | tf_op jit(solution)/shard_map/ppermute | solution.py:47
  22.2 0.1 collective-permute-start.10
  22.3 1.5 %collective-permute-done.9.rest_3_ = bf16[144,128]{1,0:T(8,128)(2,1)S(1)} collective-permute-done((bf16[144,128]{1,0:T(8,128)(2,1)S(1)}, bf16[144,128]{1,0:T(8,128)(2,1)S(1)}, u32[]{:S(2)}, u32[]{:S(2)}) %collective-permute-start.9) | collective-permute-done | bytes 36896 | tf_op jit(solution)/shard_map/ppermute | solution.py:25
  23.8 0.8 %combine.1 = f32[16,1024]{1,0:T(8,128)} custom-call(bf16[272,128]{1,0:T(8,128)(2,1)S(1)} %collective-permute-done.3.rest_0_, bf16[272,128]{1,0:T(8,128)(2,1)S(1)} %collective-permute-done.5.rest_1_, bf16[272,128]{1,0:T(8,128)(2,1)S(1)} %collective-permute-done.7.rest_2_, bf16[144,128]{1,0:T(8,128)(2,1)S(1)} %collective-permute-done.9.rest_3_, ...), custom_call_target="tpu_custom_call" | custom-call | tf_op jit(solution)/shard_map/combine/pallas_call | solution.py:416
  (13 shorter events, 0.1 us)
Async XLA Ops:
  0.0 1.5 %collective-permute-start.1 = (bf16[16,1024]{1,0:T(8,128)(2,1)}, bf16[16,1024]{1,0:T(8,128)(2,1)S(1)}, u32[]{:S(2)}, u32[]{:S(2)}) collective-permute-start(bf16[16,1024]{1,0:T(8,128)(2,1)} %refs_0_.1), channel_id=1, source_target_pairs={{0,4},{4,0},{1,5},{5,1},{2,6},{6,2},{3,7},{7,3},{8,12},{12,8},{9,1... | collective-permute-start | bytes 98312 | tf_op jit(solution)/shard_map/ppermute | solution.py:25
  0.5 9.6 %collective-permute-start = (bf16[32,64,256]{2,1,0:T(8,128)(2,1)}, bf16[32,64,256]{2,1,0:T(8,128)(2,1)S(1)}, u32[]{:S(2)}, u32[]{:S(2)}) collective-permute-start(bf16[32,64,256]{2,1,0:T(8,128)(2,1)} %bitcast.5), channel_id=1, source_target_pairs={{0,4},{4,0},{1,5},{5,1},{2,6},{6,2},{3,7},{7,3},{8,12},{12,8},{9,1... | collective-permute-start | bytes 3145736 | tf_op jit(solution)/shard_map/ppermute | solution.py:25
  1.5 8.0 %copy-start.2 = (bf16[16,1024]{1,0:T(8,128)(2,1)S(1)}, bf16[16,1024]{1,0:T(8,128)(2,1)}, u32[]{:S(2)}) copy-start(bf16[16,1024]{1,0:T(8,128)(2,1)} %refs_0_.1) | copy-start | bytes 98308
  1.5 8.5 %copy-start.1 = (bf16[32,1,64,256]{3,2,1,0:T(8,128)(2,1)S(1)}, bf16[32,1,64,256]{3,2,1,0:T(8,128)(2,1)}, u32[]{:S(2)}) copy-start(bf16[32,1,64,256]{3,2,1,0:T(8,128)(2,1)} %param.8) | copy-start | bytes 3145732
  1.5 9.3 %collective-permute-start.2 = (bf16[2,16,1024]{2,1,0:T(8,128)(2,1)S(1)}, bf16[2,16,1024]{2,1,0:T(8,128)(2,1)S(1)}, u32[]{:S(2)}, u32[]{:S(2)}) collective-permute-start(bf16[2,16,1024]{2,1,0:T(8,128)(2,1)S(1)} %both_cores.1), channel_id=1, source_target_pairs={{0,8},{1,9},{4,20},{5,21},{8,0},{9,1},{12,28},{13,29},{16,24},{17,... | collective-permute-start | bytes 196616 | tf_op jit(solution)/shard_map/ppermute | solution.py:47
  4.5 6.9 %collective-permute-start.6 = (bf16[2,16,1024]{2,1,0:T(8,128)(2,1)S(1)}, bf16[2,16,1024]{2,1,0:T(8,128)(2,1)S(1)}, u32[]{:S(2)}, u32[]{:S(2)}) collective-permute-start(bf16[2,16,1024]{2,1,0:T(8,128)(2,1)S(1)} %both_cores.1), channel_id=1, source_target_pairs={{0,9},{1,8},{4,21},{5,20},{8,1},{9,0},{12,29},{13,28},{16,25},{17,... | collective-permute-start | bytes 196616 | tf_op jit(solution)/shard_map/ppermute | solution.py:47
  5.9 9.1 %collective-permute-start.4 = (bf16[2,16,1024]{2,1,0:T(8,128)(2,1)S(1)}, bf16[2,16,1024]{2,1,0:T(8,128)(2,1)S(1)}, u32[]{:S(2)}, u32[]{:S(2)}) collective-permute-start(bf16[2,16,1024]{2,1,0:T(8,128)(2,1)S(1)} %both_cores.1), channel_id=1, source_target_pairs={{0,24},{1,25},{4,29},{5,28},{8,16},{9,17},{12,21},{13,20},{16,8},{... | collective-permute-start | bytes 196616 | tf_op jit(solution)/shard_map/ppermute | solution.py:47
  9.5 7.7 %collective-permute-start.8 = (bf16[16,1024]{1,0:T(8,128)(2,1)S(1)}, bf16[16,1024]{1,0:T(8,128)(2,1)S(1)}, u32[]{:S(2)}, u32[]{:S(2)}) collective-permute-start(bf16[16,1024]{1,0:T(8,128)(2,1)S(1)} %copy-done.2), channel_id=1, source_target_pairs={{0,1},{1,0},{2,3},{3,2},{4,5},{5,4},{6,7},{7,6},{8,9},{9,8},{10,11... | collective-permute-start | bytes 98312 | tf_op jit(solution)/shard_map/ppermute | solution.py:25
  10.8 6.4 %copy-start = (bf16[1,1,4096,256]{3,2,1,0:T(8,128)(2,1)S(1)}, bf16[1,1,4096,256]{3,2,1,0:T(8,128)(2,1)}, u32[]{:S(2)}) copy-start(bf16[1,1,4096,256]{3,2,1,0:T(8,128)(2,1)} %param.7) | copy-start | bytes 6291460
  11.4 9.0 %collective-permute-start.3 = (bf16[272,128]{1,0:T(8,128)(2,1)S(1)}, bf16[272,128]{1,0:T(8,128)(2,1)S(1)}, u32[]{:S(2)}, u32[]{:S(2)}) collective-permute-start(bf16[272,128]{1,0:T(8,128)(2,1)S(1)} %get-tuple-element.24), channel_id=1, source_target_pairs={{0,8},{1,9},{4,20},{5,21},{8,0},{9,1},{12,28},{13,29},{16,24},{17,... | collective-permute-start | bytes 208904 | tf_op jit(solution)/shard_map/ppermute | solution.py:47
  12.0 8.4 %collective-permute-start.7 = (bf16[272,128]{1,0:T(8,128)(2,1)S(1)}, bf16[272,128]{1,0:T(8,128)(2,1)S(1)}, u32[]{:S(2)}, u32[]{:S(2)}) collective-permute-start(bf16[272,128]{1,0:T(8,128)(2,1)S(1)} %suffix_away.5), channel_id=1, source_target_pairs={{0,9},{1,8},{4,21},{5,20},{8,1},{9,0},{12,29},{13,28},{16,25},{17,... | collective-permute-start | bytes 208904 | tf_op jit(solution)/shard_map/ppermute | solution.py:47
  15.5 6.7 %collective-permute-start.5 = (bf16[272,128]{1,0:T(8,128)(2,1)S(1)}, bf16[272,128]{1,0:T(8,128)(2,1)S(1)}, u32[]{:S(2)}, u32[]{:S(2)}) collective-permute-start(bf16[272,128]{1,0:T(8,128)(2,1)S(1)} %suffix_away.4), channel_id=1, source_target_pairs={{0,24},{1,25},{4,29},{5,28},{8,16},{9,17},{12,21},{13,20},{16,8},{... | collective-permute-start | bytes 208904 | tf_op jit(solution)/shard_map/ppermute | solution.py:47
  19.8 4.0 %collective-permute-start.9 = (bf16[144,128]{1,0:T(8,128)(2,1)S(1)}, bf16[144,128]{1,0:T(8,128)(2,1)S(1)}, u32[]{:S(2)}, u32[]{:S(2)}) collective-permute-start(bf16[144,128]{1,0:T(8,128)(2,1)S(1)} %get-tuple-element.28), channel_id=1, source_target_pairs={{0,1},{1,0},{2,3},{3,2},{4,5},{5,4},{6,7},{7,6},{8,9},{9,8},{10,11... | collective-permute-start | bytes 110600 | tf_op jit(solution)/shard_map/ppermute | solution.py:25
  22.2 1.6 %collective-permute-start.10 = (bf16[144,128]{1,0:T(8,128)(2,1)S(1)}, bf16[144,128]{1,0:T(8,128)(2,1)S(1)}, u32[]{:S(2)}, u32[]{:S(2)}) collective-permute-start(bf16[144,128]{1,0:T(8,128)(2,1)S(1)} %sibling_share.1), channel_id=1, source_target_pairs={{0,4},{4,0},{1,5},{5,1},{2,6},{6,2},{3,7},{7,3},{8,12},{12,8},{9,1... | collective-permute-start | bytes 110600 | tf_op jit(solution)/shard_map/ppermute | solution.py:25

commit v21 on v19

--- a/solution.py
+++ b/solution.py
@@ -148,22 +148,25 @@
     whole = lax.div(length, 2 * half)
     valid = whole * half + jnp.clip(length - whole * (2 * half) - parity * half, 0, half)
     chunks = [slice(i, i + CHUNK) for i in range(0, prompt_ref.shape[0], CHUNK)]
-    scores = [scores_of(prompt_ref[chunk, :HD], vectors) for chunk in chunks]
-    place = iota(scores[0].shape, 0)
+    scores = [scores_of(vectors, prompt_ref[chunk, :HD]) for chunk in chunks]
+    place = iota(scores[0].shape, 1)
     scores = [
         score
         if chunk.stop <= SURELY_VALID
         else jnp.where(place < valid - chunk.start, score, big_negative)
         for chunk, score in zip(chunks, scores)
     ]
-    tops = [jnp.max(score, axis=0, keepdims=True) for score in scores]
-    top = functools.reduce(jnp.maximum, tops)
-    total, summed = 0.0, 0.0
+    top = jnp.max(functools.reduce(jnp.maximum, scores), axis=1, keepdims=True)
+    totals, summed = 0.0, 0.0
     for chunk, score in zip(chunks, scores):
         weights = jnp.exp2((score - top) * to_exp2)
-        total = total + jnp.sum(weights, axis=0, keepdims=True)
-        summed = summed + summed_of(prompt_ref[chunk, HD:], weights)
-    return top, total, summed
+        totals = totals + weights
+        summed = summed + jnp.dot(
+            weights.astype(jnp.bfloat16), prompt_ref[chunk, HD:], preferred_element_type=jnp.float32
+        )
+    total = jnp.sum(totals, axis=1, keepdims=True)
+    stats = jnp.where(iota(summed.shape, 1) == 0, top, total).T
+    return stats[0:1], stats[1:2], summed.T
 
 
 def prepare_kernel(

time: 24.8 us -> 24.8 us (level)
  no operation moved by 1% of the time
where the time goes in v21:
time: 24.8 us; the launch traced here: 24.6 us
  starting transfers between devices  13.8 us (56%)
  Pallas kernels  6.4 us (26%)
  waiting for transfers between devices  3.63 us (15%)
  between operations  0.75 us (3%)
    ppermute x6, starting transfers between devices, exchanged(): return lax.ppermute(value, ('z', 'core', 'pair'), pairs)  11.6 us
    pallas_call x1, Pallas kernels, on_device(): pl.pallas_call(home_kernel, out_shape=(pltpu.VMEM((HD, VECS), jnp.float32...  2.51 us
    ppermute x5, starting transfers between devices, swapped(): return lax.ppermute(value, axis, [(0, 1), (1, 0)])  2.23 us
    ppermute x6, waiting for transfers between devices, exchanged(): return lax.ppermute(value, ('z', 'core', 'pair'), pairs)  2.21 us
    pallas_call x3, Pallas kernels, on_device(): pl.pallas_call(functools.partial(away_kernel, 2 * ((k + 1) // 2)), out_sh...  1.51 us
    ppermute x5, waiting for transfers between devices, swapped(): return lax.ppermute(value, axis, [(0, 1), (1, 0)])  1.42 us
    pallas_call x1, Pallas kernels, on_device(): pl.pallas_call(stage_kernel, out_shape=tuple((pltpu.VMEM(each.shape, each...  0.79 us
    pallas_call x1, Pallas kernels, on_device(): pl.pallas_call(functools.partial(prepare_kernel, capacity), out_shape=(pl...  0.77 us
  transfers between devices with their start and end apart: 11, of which 4 were waited for; matrix products, arithmetic and copies ran while one was open for 0% of the time, Pallas kernels for 23%

profile of v21, /device:TPU:0, one launch (start us, length us, event | category | flops | bytes accessed | tf_op | source)
XLA Modules:
  0.0 24.6 jit_solution(3599334048578650839)
XLA Ops:
  0.0 0.5 %collective-permute-start.1 = (bf16[16,1024]{1,0:T(8,128)(2,1)}, bf16[16,1024]{1,0:T(8,128)(2,1)S(1)}, u32[]{:S(2)}, u32[]{:S(2)}) collective-permute-start(bf16[16,1024]{1,0:T(8,128)(2,1)} %refs_0_.1), channel_id=1, source_target_pairs={{0,4},{4,0},{1,5},{5,1},{2,6},{6,2},{3,7},{7,3},{8,12},{12,8},{9,1... | collective-permute-start | bytes 98312 | tf_op jit(solution)/shard_map/ppermute | solution.py:25
  0.5 0.1 collective-permute-start
  0.5 0.8 %stage.1 = (bf16[16,1024]{1,0:T(8,128)(2,1)S(1)}, s32[4,128]{1,0:T(4,128)S(1)}, s32[1,128]{1,0:T(1,128)S(1)}) custom-call(bf16[16,1024]{1,0:T(8,128)(2,1)} %refs_0_.1, s32[4,128]{1,0:T(4,128)} %bitcast.7, s32[1,128]{1,0:T(1,128)} %bitcast.8), custom_call_target="tpu_custom_call" | custom-call | tf_op jit(solution)/shard_map/stage/pallas_call | solution.py:332
  1.3 0.2 collective-permute-done.1.sibling_ref
  1.5 3.0 %collective-permute-start.2 = (bf16[2,16,1024]{2,1,0:T(8,128)(2,1)S(1)}, bf16[2,16,1024]{2,1,0:T(8,128)(2,1)S(1)}, u32[]{:S(2)}, u32[]{:S(2)}) collective-permute-start(bf16[2,16,1024]{2,1,0:T(8,128)(2,1)S(1)} %both_cores.1), channel_id=1, source_target_pairs={{0,8},{1,9},{4,28},{5,29},{8,0},{9,1},{12,20},{13,21},{16,24},{17,... | collective-permute-start | bytes 196616 | tf_op jit(solution)/shard_map/ppermute | solution.py:47
  4.5 1.4 %collective-permute-start.6 = (bf16[2,16,1024]{2,1,0:T(8,128)(2,1)S(1)}, bf16[2,16,1024]{2,1,0:T(8,128)(2,1)S(1)}, u32[]{:S(2)}, u32[]{:S(2)}) collective-permute-start(bf16[2,16,1024]{2,1,0:T(8,128)(2,1)S(1)} %both_cores.1), channel_id=1, source_target_pairs={{0,9},{1,8},{4,29},{5,28},{8,1},{9,0},{12,21},{13,20},{16,25},{17,... | collective-permute-start | bytes 196616 | tf_op jit(solution)/shard_map/ppermute | solution.py:47
  5.9 2.6 %collective-permute-start.4 = (bf16[2,16,1024]{2,1,0:T(8,128)(2,1)S(1)}, bf16[2,16,1024]{2,1,0:T(8,128)(2,1)S(1)}, u32[]{:S(2)}, u32[]{:S(2)}) collective-permute-start(bf16[2,16,1024]{2,1,0:T(8,128)(2,1)S(1)} %both_cores.1), channel_id=1, source_target_pairs={{0,16},{1,17},{4,21},{5,20},{8,24},{9,25},{12,29},{13,28},{16,0},{... | collective-permute-start | bytes 196616 | tf_op jit(solution)/shard_map/ppermute | solution.py:47
  8.5 0.5 %collective-permute-start.8 = (bf16[16,1024]{1,0:T(8,128)(2,1)S(1)}, bf16[16,1024]{1,0:T(8,128)(2,1)S(1)}, u32[]{:S(2)}, u32[]{:S(2)}) collective-permute-start(bf16[16,1024]{1,0:T(8,128)(2,1)S(1)} %copy-done.2), channel_id=1, source_target_pairs={{0,1},{1,0},{2,3},{3,2},{4,5},{5,4},{6,7},{7,6},{8,9},{9,8},{10,11... | collective-permute-start | bytes 98312 | tf_op jit(solution)/shard_map/ppermute | solution.py:25
  9.0 0.8 %prepare.1 = (bf16[1,512,128]{2,1,0:T(8,128)(2,1)S(1)}, bf16[1,128,512]{2,1,0:T(8,128)(2,1)S(1)}, bf16[4,512,128]{2,1,0:T(8,128)(2,1)S(1)}, bf16[4,128,512]{2,1,0:T(8,128)(2,1)S(1)}, f32[5,8,128]{2,1,0:T(8,128)S(1)}) custom-call(bf16[32,64,256]{2,1,0:T(8,128)(2,1)S(1)} %bitcast.6, s32[4,128]{1,0:T(4,128)S(1)} %get-tuple-element.18.table, ...), custom_call_target="tpu_custom_call" | custom-call | flops 200000000 | bytes 2097152 | tf_op jit(solution)/shard_map/prepare/pallas_call | solution.py:354
  9.8 0.0 copy-start
  9.8 0.0 collective-permute-done.2.message_ref
  9.8 0.5 %suffix_away.3 = (bf16[272,128]{1,0:T(8,128)(2,1)S(1)}, f32[8,128]{1,0:T(8,128)S(1)}) custom-call(bf16[4,512,128]{2,1,0:T(8,128)(2,1)S(1)} %get-tuple-element.20.keys_ref, bf16[4,128,512]{2,1,0:T(8,128)(2,1)S(1)} %get-tuple-element.21.values_ref, f32[5,8,128]{2,1,0:T(8,128)S(1)} %get-tuple-element.22.member_ref, ...), custom_call_target="tpu_custom_call" | custom-call | flops 200000000 | bytes 2097152 | tf_op jit(solution)/shard_map/suffix_away/pallas_call | solution.py:381
  10.4 1.6 %collective-permute-start.3 = (bf16[272,128]{1,0:T(8,128)(2,1)S(1)}, bf16[272,128]{1,0:T(8,128)(2,1)S(1)}, u32[]{:S(2)}, u32[]{:S(2)}) collective-permute-start(bf16[272,128]{1,0:T(8,128)(2,1)S(1)} %get-tuple-element.24), channel_id=1, source_target_pairs={{0,8},{1,9},{4,28},{5,29},{8,0},{9,1},{12,20},{13,21},{16,24},{17,... | collective-permute-start | bytes 208904 | tf_op jit(solution)/shard_map/ppermute | solution.py:47
  12.0 0.5 %suffix_away.5 = bf16[272,128]{1,0:T(8,128)(2,1)S(1)} custom-call(bf16[4,512,128]{2,1,0:T(8,128)(2,1)S(1)} %get-tuple-element.20.keys_ref, bf16[4,128,512]{2,1,0:T(8,128)(2,1)S(1)} %get-tuple-element.21.values_ref, f32[5,8,128]{2,1,0:T(8,128)S(1)} %get-tuple-element.22.member_ref, bf16[2,16,1024]{2,1,0:T(8,128)(2,1)S(1)} %collective-permute-done.6.message_ref), custom_call_target="tpu_custom_call" | custom-call | flops 200000000 | bytes 2097152 | tf_op jit(solution)/shard_map/suffix_away/pallas_call | solution.py:381
  12.5 1.4 %collective-permute-start.7 = (bf16[272,128]{1,0:T(8,128)(2,1)S(1)}, bf16[272,128]{1,0:T(8,128)(2,1)S(1)}, u32[]{:S(2)}, u32[]{:S(2)}) collective-permute-start(bf16[272,128]{1,0:T(8,128)(2,1)S(1)} %suffix_away.5), channel_id=1, source_target_pairs={{0,9},{1,8},{4,29},{5,28},{8,1},{9,0},{12,21},{13,20},{16,25},{17,... | collective-permute-start | bytes 208904 | tf_op jit(solution)/shard_map/ppermute | solution.py:47
  14.0 0.5 %suffix_away.4 = bf16[272,128]{1,0:T(8,128)(2,1)S(1)} custom-call(bf16[4,512,128]{2,1,0:T(8,128)(2,1)S(1)} %get-tuple-element.20.keys_ref, bf16[4,128,512]{2,1,0:T(8,128)(2,1)S(1)} %get-tuple-element.21.values_ref, f32[5,8,128]{2,1,0:T(8,128)S(1)} %get-tuple-element.22.member_ref, bf16[2,16,1024]{2,1,0:T(8,128)(2,1)S(1)} %collective-permute-done.4.message_ref), custom_call_target="tpu_custom_call" | custom-call | flops 200000000 | bytes 2097152 | tf_op jit(solution)/shard_map/suffix_away/pallas_call | solution.py:381
  14.5 1.6 %collective-permute-start.5 = (bf16[272,128]{1,0:T(8,128)(2,1)S(1)}, bf16[272,128]{1,0:T(8,128)(2,1)S(1)}, u32[]{:S(2)}, u32[]{:S(2)}) collective-permute-start(bf16[272,128]{1,0:T(8,128)(2,1)S(1)} %suffix_away.4), channel_id=1, source_target_pairs={{0,16},{1,17},{4,21},{5,20},{8,24},{9,25},{12,29},{13,28},{16,0},{... | collective-permute-start | bytes 208904 | tf_op jit(solution)/shard_map/ppermute | solution.py:47
  16.7 2.5 %home_part.1 = (f32[128,128]{1,0:T(8,128)S(1)}, f32[8,128]{1,0:T(8,128)S(1)}, bf16[144,128]{1,0:T(8,128)(2,1)S(1)}) custom-call(s32[1]{0:T(128)S(6)} %copy.7.length_ref, bf16[1,512,128]{2,1,0:T(8,128)(2,1)S(1)} %get-tuple-element.25.keys_ref, bf16[1,128,512]{2,1,0:T(8,128)(2,1)S(1)} %get-tuple-element.26.values_ref, ...), custom_call_target="tpu_custom_call" | custom-call | flops 536870912 | bytes 2097152 | tf_op jit(solution)/shard_map/home_part/pallas_call | solution.py:393
  19.2 1.1 %collective-permute-start.9 = (bf16[144,128]{1,0:T(8,128)(2,1)S(1)}, bf16[144,128]{1,0:T(8,128)(2,1)S(1)}, u32[]{:S(2)}, u32[]{:S(2)}) collective-permute-start(bf16[144,128]{1,0:T(8,128)(2,1)S(1)} %get-tuple-element.28), channel_id=1, source_target_pairs={{0,1},{1,0},{2,3},{3,2},{4,5},{5,4},{6,7},{7,6},{8,9},{9,8},{10,11... | collective-permute-start | bytes 110600 | tf_op jit(solution)/shard_map/ppermute | solution.py:25
  20.3 2.2 %collective-permute-done.5.rest_1_ = bf16[272,128]{1,0:T(8,128)(2,1)S(1)} collective-permute-done((bf16[272,128]{1,0:T(8,128)(2,1)S(1)}, bf16[272,128]{1,0:T(8,128)(2,1)S(1)}, u32[]{:S(2)}, u32[]{:S(2)}) %collective-permute-start.5) | collective-permute-done | bytes 69664 | tf_op jit(solution)/shard_map/ppermute | solution.py:47
  22.6 0.1 collective-permute-start.10
  22.7 0.7 %collective-permute-done.9.rest_3_ = bf16[144,128]{1,0:T(8,128)(2,1)S(1)} collective-permute-done((bf16[144,128]{1,0:T(8,128)(2,1)S(1)}, bf16[144,128]{1,0:T(8,128)(2,1)S(1)}, u32[]{:S(2)}, u32[]{:S(2)}) %collective-permute-start.9) | collective-permute-done | bytes 36896 | tf_op jit(solution)/shard_map/ppermute | solution.py:25
  23.4 0.5 %collective-permute-done.10.rest_4_ = bf16[144,128]{1,0:T(8,128)(2,1)S(1)} collective-permute-done((bf16[144,128]{1,0:T(8,128)(2,1)S(1)}, bf16[144,128]{1,0:T(8,128)(2,1)S(1)}, u32[]{:S(2)}, u32[]{:S(2)}) %collective-permute-start.10) | collective-permute-done | bytes 36896 | tf_op jit(solution)/shard_map/ppermute | solution.py:25
  23.9 0.8 %combine.1 = f32[16,1024]{1,0:T(8,128)} custom-call(bf16[272,128]{1,0:T(8,128)(2,1)S(1)} %collective-permute-done.3.rest_0_, bf16[272,128]{1,0:T(8,128)(2,1)S(1)} %collective-permute-done.5.rest_1_, bf16[272,128]{1,0:T(8,128)(2,1)S(1)} %collective-permute-done.7.rest_2_, bf16[144,128]{1,0:T(8,128)(2,1)S(1)} %collective-permute-done.9.rest_3_, ...), custom_call_target="tpu_custom_call" | custom-call | tf_op jit(solution)/shard_map/combine/pallas_call | solution.py:419
  (13 shorter events, 0.1 us)
Async XLA Ops:
  0.0 1.5 %collective-permute-start.1 = (bf16[16,1024]{1,0:T(8,128)(2,1)}, bf16[16,1024]{1,0:T(8,128)(2,1)S(1)}, u32[]{:S(2)}, u32[]{:S(2)}) collective-permute-start(bf16[16,1024]{1,0:T(8,128)(2,1)} %refs_0_.1), channel_id=1, source_target_pairs={{0,4},{4,0},{1,5},{5,1},{2,6},{6,2},{3,7},{7,3},{8,12},{12,8},{9,1... | collective-permute-start | bytes 98312 | tf_op jit(solution)/shard_map/ppermute | solution.py:25
  0.5 8.6 %collective-permute-start = (bf16[32,64,256]{2,1,0:T(8,128)(2,1)}, bf16[32,64,256]{2,1,0:T(8,128)(2,1)S(1)}, u32[]{:S(2)}, u32[]{:S(2)}) collective-permute-start(bf16[32,64,256]{2,1,0:T(8,128)(2,1)} %bitcast.5), channel_id=1, source_target_pairs={{0,4},{4,0},{1,5},{5,1},{2,6},{6,2},{3,7},{7,3},{8,12},{12,8},{9,1... | collective-permute-start | bytes 3145736 | tf_op jit(solution)/shard_map/ppermute | solution.py:25
  1.5 7.0 %copy-start.2 = (bf16[16,1024]{1,0:T(8,128)(2,1)S(1)}, bf16[16,1024]{1,0:T(8,128)(2,1)}, u32[]{:S(2)}) copy-start(bf16[16,1024]{1,0:T(8,128)(2,1)} %refs_0_.1) | copy-start | bytes 98308
  1.5 7.5 %copy-start.1 = (bf16[32,1,64,256]{3,2,1,0:T(8,128)(2,1)S(1)}, bf16[32,1,64,256]{3,2,1,0:T(8,128)(2,1)}, u32[]{:S(2)}) copy-start(bf16[32,1,64,256]{3,2,1,0:T(8,128)(2,1)} %param.8) | copy-start | bytes 3145732
  1.5 8.3 %collective-permute-start.2 = (bf16[2,16,1024]{2,1,0:T(8,128)(2,1)S(1)}, bf16[2,16,1024]{2,1,0:T(8,128)(2,1)S(1)}, u32[]{:S(2)}, u32[]{:S(2)}) collective-permute-start(bf16[2,16,1024]{2,1,0:T(8,128)(2,1)S(1)} %both_cores.1), channel_id=1, source_target_pairs={{0,8},{1,9},{4,28},{5,29},{8,0},{9,1},{12,20},{13,21},{16,24},{17,... | collective-permute-start | bytes 196616 | tf_op jit(solution)/shard_map/ppermute | solution.py:47
  4.5 7.5 %collective-permute-start.6 = (bf16[2,16,1024]{2,1,0:T(8,128)(2,1)S(1)}, bf16[2,16,1024]{2,1,0:T(8,128)(2,1)S(1)}, u32[]{:S(2)}, u32[]{:S(2)}) collective-permute-start(bf16[2,16,1024]{2,1,0:T(8,128)(2,1)S(1)} %both_cores.1), channel_id=1, source_target_pairs={{0,9},{1,8},{4,29},{5,28},{8,1},{9,0},{12,21},{13,20},{16,25},{17,... | collective-permute-start | bytes 196616 | tf_op jit(solution)/shard_map/ppermute | solution.py:47
  5.9 8.1 %collective-permute-start.4 = (bf16[2,16,1024]{2,1,0:T(8,128)(2,1)S(1)}, bf16[2,16,1024]{2,1,0:T(8,128)(2,1)S(1)}, u32[]{:S(2)}, u32[]{:S(2)}) collective-permute-start(bf16[2,16,1024]{2,1,0:T(8,128)(2,1)S(1)} %both_cores.1), channel_id=1, source_target_pairs={{0,16},{1,17},{4,21},{5,20},{8,24},{9,25},{12,29},{13,28},{16,0},{... | collective-permute-start | bytes 196616 | tf_op jit(solution)/shard_map/ppermute | solution.py:47
  8.5 8.2 %collective-permute-start.8 = (bf16[16,1024]{1,0:T(8,128)(2,1)S(1)}, bf16[16,1024]{1,0:T(8,128)(2,1)S(1)}, u32[]{:S(2)}, u32[]{:S(2)}) collective-permute-start(bf16[16,1024]{1,0:T(8,128)(2,1)S(1)} %copy-done.2), channel_id=1, source_target_pairs={{0,1},{1,0},{2,3},{3,2},{4,5},{5,4},{6,7},{7,6},{8,9},{9,8},{10,11... | collective-permute-start | bytes 98312 | tf_op jit(solution)/shard_map/ppermute | solution.py:25
  9.8 6.9 %copy-start = (bf16[1,1,4096,256]{3,2,1,0:T(8,128)(2,1)S(1)}, bf16[1,1,4096,256]{3,2,1,0:T(8,128)(2,1)}, u32[]{:S(2)}) copy-start(bf16[1,1,4096,256]{3,2,1,0:T(8,128)(2,1)} %param.7) | copy-start | bytes 6291460
  10.4 10.0 %collective-permute-start.3 = (bf16[272,128]{1,0:T(8,128)(2,1)S(1)}, bf16[272,128]{1,0:T(8,128)(2,1)S(1)}, u32[]{:S(2)}, u32[]{:S(2)}) collective-permute-start(bf16[272,128]{1,0:T(8,128)(2,1)S(1)} %get-tuple-element.24), channel_id=1, source_target_pairs={{0,8},{1,9},{4,28},{5,29},{8,0},{9,1},{12,20},{13,21},{16,24},{17,... | collective-permute-start | bytes 208904 | tf_op jit(solution)/shard_map/ppermute | solution.py:47
  12.5 7.8 %collective-permute-start.7 = (bf16[272,128]{1,0:T(8,128)(2,1)S(1)}, bf16[272,128]{1,0:T(8,128)(2,1)S(1)}, u32[]{:S(2)}, u32[]{:S(2)}) collective-permute-start(bf16[272,128]{1,0:T(8,128)(2,1)S(1)} %suffix_away.5), channel_id=1, source_target_pairs={{0,9},{1,8},{4,29},{5,28},{8,1},{9,0},{12,21},{13,20},{16,25},{17,... | collective-permute-start | bytes 208904 | tf_op jit(solution)/shard_map/ppermute | solution.py:47
  14.5 8.1 %collective-permute-start.5 = (bf16[272,128]{1,0:T(8,128)(2,1)S(1)}, bf16[272,128]{1,0:T(8,128)(2,1)S(1)}, u32[]{:S(2)}, u32[]{:S(2)}) collective-permute-start(bf16[272,128]{1,0:T(8,128)(2,1)S(1)} %suffix_away.4), channel_id=1, source_target_pairs={{0,16},{1,17},{4,21},{5,20},{8,24},{9,25},{12,29},{13,28},{16,0},{... | collective-permute-start | bytes 208904 | tf_op jit(solution)/shard_map/ppermute | solution.py:47
  19.2 4.2 %collective-permute-start.9 = (bf16[144,128]{1,0:T(8,128)(2,1)S(1)}, bf16[144,128]{1,0:T(8,128)(2,1)S(1)}, u32[]{:S(2)}, u32[]{:S(2)}) collective-permute-start(bf16[144,128]{1,0:T(8,128)(2,1)S(1)} %get-tuple-element.28), channel_id=1, source_target_pairs={{0,1},{1,0},{2,3},{3,2},{4,5},{5,4},{6,7},{7,6},{8,9},{9,8},{10,11... | collective-permute-start | bytes 110600 | tf_op jit(solution)/shard_map/ppermute | solution.py:25
  22.6 1.3 %collective-permute-start.10 = (bf16[144,128]{1,0:T(8,128)(2,1)S(1)}, bf16[144,128]{1,0:T(8,128)(2,1)S(1)}, u32[]{:S(2)}, u32[]{:S(2)}) collective-permute-start(bf16[144,128]{1,0:T(8,128)(2,1)S(1)} %sibling_share.1), channel_id=1, source_target_pairs={{0,4},{4,0},{1,5},{5,1},{2,6},{6,2},{3,7},{7,3},{8,12},{12,8},{9,1... | collective-permute-start | bytes 110600 | tf_op jit(solution)/shard_map/ppermute | solution.py:25

commit v22 on v21

--- a/solution.py
+++ b/solution.py
@@ -348,7 +348,7 @@
         name="both_cores",
     )(own, swapped(queries, "core"))
     n_messages = n_req - 1
-    order = [1, 0] + list(range(n_messages - 1, 1, -1)) if n_messages > 1 else [0]
+    order = list(range(1, n_messages)) + [0]
     messages = {k: exchanged(both, k) for k in order}
 
     home_keys, home_values, keys, values, member = pl.pallas_call(

time: 24.8 us -> 25.9 us (1.044)
  waiting for transfers between devices: 3.63 us -> 4.37 us
  starting transfers between devices: 13.8 us -> 14.2 us
    ppermute x5, waiting for transfers between devices: 1.42 us -> 3.15 us  [swapped(): return lax.ppermute(value, axis, [(0, 1), (1, 0)])]
    ppermute x6, waiting for transfers between devices: 2.21 us -> 1.23 us  [exchanged(): return lax.ppermute(value, ('z', 'core', 'pair'), pairs)]
    ppermute x6, starting transfers between devices: 11.6 us -> 12.3 us  [exchanged(): return lax.ppermute(value, ('z', 'core', 'pair'), pairs)]
    ppermute x5, starting transfers between devices: 2.23 us -> 1.93 us  [swapped(): return lax.ppermute(value, axis, [(0, 1), (1, 0)])]
  transfers between devices with their start and end apart: 11 -> 11, of which waited for: 4 -> 4; matrix products, arithmetic and copies ran while one was open for 0% -> 0% of each run, Pallas kernels for 23% -> 22%
where the time goes in v22:
time: 25.9 us; the launch traced here: 25.7 us
  starting transfers between devices  14.2 us (55%)
  Pallas kernels  6.39 us (25%)
  waiting for transfers between devices  4.37 us (17%)
  between operations  0.75 us (3%)
    ppermute x6, starting transfers between devices, exchanged(): return lax.ppermute(value, ('z', 'core', 'pair'), pairs)  12.3 us
    ppermute x5, waiting for transfers between devices, swapped(): return lax.ppermute(value, axis, [(0, 1), (1, 0)])  3.15 us
    pallas_call x1, Pallas kernels, on_device(): pl.pallas_call(home_kernel, out_shape=(pltpu.VMEM((HD, VECS), jnp.float32...  2.5 us
    ppermute x5, starting transfers between devices, swapped(): return lax.ppermute(value, axis, [(0, 1), (1, 0)])  1.93 us
    pallas_call x3, Pallas kernels, on_device(): pl.pallas_call(functools.partial(away_kernel, 2 * ((k + 1) // 2)), out_sh...  1.51 us
    ppermute x6, waiting for transfers between devices, exchanged(): return lax.ppermute(value, ('z', 'core', 'pair'), pairs)  1.23 us
    pallas_call x1, Pallas kernels, on_device(): pl.pallas_call(stage_kernel, out_shape=tuple((pltpu.VMEM(each.shape, each...  0.79 us
    pallas_call x1, Pallas kernels, on_device(): pl.pallas_call(functools.partial(prepare_kernel, capacity), out_shape=(pl...  0.77 us
  transfers between devices with their start and end apart: 11, of which 4 were waited for; matrix products, arithmetic and copies ran while one was open for 0% of the time, Pallas kernels for 22%

profile of v22, /device:TPU:0, one launch (start us, length us, event | category | flops | bytes accessed | tf_op | source)
XLA Modules:
  0.0 25.7 jit_solution(12495093450446666414)
XLA Ops:
  0.0 0.5 %collective-permute-start.1 = (bf16[16,1024]{1,0:T(8,128)(2,1)}, bf16[16,1024]{1,0:T(8,128)(2,1)S(1)}, u32[]{:S(2)}, u32[]{:S(2)}) collective-permute-start(bf16[16,1024]{1,0:T(8,128)(2,1)} %refs_0_.1), channel_id=1, source_target_pairs={{0,4},{4,0},{1,5},{5,1},{2,6},{6,2},{3,7},{7,3},{8,12},{12,8},{9,1... | collective-permute-start | bytes 98312 | tf_op jit(solution)/shard_map/ppermute | solution.py:25
  0.5 0.1 collective-permute-start
  0.5 0.8 %stage.1 = (bf16[16,1024]{1,0:T(8,128)(2,1)S(1)}, s32[4,128]{1,0:T(4,128)S(1)}, s32[1,128]{1,0:T(1,128)S(1)}) custom-call(bf16[16,1024]{1,0:T(8,128)(2,1)} %refs_0_.1, s32[4,128]{1,0:T(4,128)} %bitcast.7, s32[1,128]{1,0:T(1,128)} %bitcast.8), custom_call_target="tpu_custom_call" | custom-call | tf_op jit(solution)/shard_map/stage/pallas_call | solution.py:332
  1.3 0.2 collective-permute-done.1.sibling_ref
  1.5 3.0 %collective-permute-start.2 = (bf16[2,16,1024]{2,1,0:T(8,128)(2,1)S(1)}, bf16[2,16,1024]{2,1,0:T(8,128)(2,1)S(1)}, u32[]{:S(2)}, u32[]{:S(2)}) collective-permute-start(bf16[2,16,1024]{2,1,0:T(8,128)(2,1)S(1)} %both_cores.1), channel_id=1, source_target_pairs={{0,8},{1,9},{4,28},{5,29},{8,0},{9,1},{12,20},{13,21},{16,24},{17,... | collective-permute-start | bytes 196616 | tf_op jit(solution)/shard_map/ppermute | solution.py:47
  4.5 2.6 %collective-permute-start.6 = (bf16[2,16,1024]{2,1,0:T(8,128)(2,1)S(1)}, bf16[2,16,1024]{2,1,0:T(8,128)(2,1)S(1)}, u32[]{:S(2)}, u32[]{:S(2)}) collective-permute-start(bf16[2,16,1024]{2,1,0:T(8,128)(2,1)S(1)} %both_cores.1), channel_id=1, source_target_pairs={{0,16},{1,17},{4,21},{5,20},{8,24},{9,25},{12,29},{13,28},{16,0},{... | collective-permute-start | bytes 196616 | tf_op jit(solution)/shard_map/ppermute | solution.py:47
  7.1 1.4 %collective-permute-start.4 = (bf16[2,16,1024]{2,1,0:T(8,128)(2,1)S(1)}, bf16[2,16,1024]{2,1,0:T(8,128)(2,1)S(1)}, u32[]{:S(2)}, u32[]{:S(2)}) collective-permute-start(bf16[2,16,1024]{2,1,0:T(8,128)(2,1)S(1)} %both_cores.1), channel_id=1, source_target_pairs={{0,9},{1,8},{4,29},{5,28},{8,1},{9,0},{12,21},{13,20},{16,25},{17,... | collective-permute-start | bytes 196616 | tf_op jit(solution)/shard_map/ppermute | solution.py:47
  8.5 0.5 %collective-permute-start.8 = (bf16[16,1024]{1,0:T(8,128)(2,1)S(1)}, bf16[16,1024]{1,0:T(8,128)(2,1)S(1)}, u32[]{:S(2)}, u32[]{:S(2)}) collective-permute-start(bf16[16,1024]{1,0:T(8,128)(2,1)S(1)} %copy-done.2), channel_id=1, source_target_pairs={{0,1},{1,0},{2,3},{3,2},{4,5},{5,4},{6,7},{7,6},{8,9},{9,8},{10,11... | collective-permute-start | bytes 98312 | tf_op jit(solution)/shard_map/ppermute | solution.py:25
  9.0 0.0 collective-permute-done.far_ref
  9.0 0.8 %prepare.1 = (bf16[1,512,128]{2,1,0:T(8,128)(2,1)S(1)}, bf16[1,128,512]{2,1,0:T(8,128)(2,1)S(1)}, bf16[4,512,128]{2,1,0:T(8,128)(2,1)S(1)}, bf16[4,128,512]{2,1,0:T(8,128)(2,1)S(1)}, f32[5,8,128]{2,1,0:T(8,128)S(1)}) custom-call(bf16[32,64,256]{2,1,0:T(8,128)(2,1)S(1)} %bitcast.6, s32[4,128]{1,0:T(4,128)S(1)} %get-tuple-element.18.table, ...), custom_call_target="tpu_custom_call" | custom-call | flops 200000000 | bytes 2097152 | tf_op jit(solution)/shard_map/prepare/pallas_call | solution.py:354
  9.8 0.0 copy-start
  9.8 0.5 %suffix_away.3 = (bf16[272,128]{1,0:T(8,128)(2,1)S(1)}, f32[8,128]{1,0:T(8,128)S(1)}) custom-call(bf16[4,512,128]{2,1,0:T(8,128)(2,1)S(1)} %get-tuple-element.20.keys_ref, bf16[4,128,512]{2,1,0:T(8,128)(2,1)S(1)} %get-tuple-element.21.values_ref, f32[5,8,128]{2,1,0:T(8,128)S(1)} %get-tuple-element.22.member_ref, ...), custom_call_target="tpu_custom_call" | custom-call | flops 200000000 | bytes 2097152 | tf_op jit(solution)/shard_map/suffix_away/pallas_call | solution.py:381
  10.4 1.6 %collective-permute-start.3 = (bf16[272,128]{1,0:T(8,128)(2,1)S(1)}, bf16[272,128]{1,0:T(8,128)(2,1)S(1)}, u32[]{:S(2)}, u32[]{:S(2)}) collective-permute-start(bf16[272,128]{1,0:T(8,128)(2,1)S(1)} %get-tuple-element.24), channel_id=1, source_target_pairs={{0,8},{1,9},{4,28},{5,29},{8,0},{9,1},{12,20},{13,21},{16,24},{17,... | collective-permute-start | bytes 208904 | tf_op jit(solution)/shard_map/ppermute | solution.py:47
  12.0 0.5 %suffix_away.5 = bf16[272,128]{1,0:T(8,128)(2,1)S(1)} custom-call(bf16[4,512,128]{2,1,0:T(8,128)(2,1)S(1)} %get-tuple-element.20.keys_ref, bf16[4,128,512]{2,1,0:T(8,128)(2,1)S(1)} %get-tuple-element.21.values_ref, f32[5,8,128]{2,1,0:T(8,128)S(1)} %get-tuple-element.22.member_ref, bf16[2,16,1024]{2,1,0:T(8,128)(2,1)S(1)} %collective-permute-done.6.message_ref), custom_call_target="tpu_custom_call" | custom-call | flops 200000000 | bytes 2097152 | tf_op jit(solution)/shard_map/suffix_away/pallas_call | solution.py:381
  12.5 0.5 %collective-permute-start.7 = (bf16[272,128]{1,0:T(8,128)(2,1)S(1)}, bf16[272,128]{1,0:T(8,128)(2,1)S(1)}, u32[]{:S(2)}, u32[]{:S(2)}) collective-permute-start(bf16[272,128]{1,0:T(8,128)(2,1)S(1)} %suffix_away.5), channel_id=1, source_target_pairs={{0,16},{1,17},{4,21},{5,20},{8,24},{9,25},{12,29},{13,28},{16,0},{... | collective-permute-start | bytes 208904 | tf_op jit(solution)/shard_map/ppermute | solution.py:47
  13.0 1.1 %collective-permute-done.4.message_ref = bf16[2,16,1024]{2,1,0:T(8,128)(2,1)S(1)} collective-permute-done((bf16[2,16,1024]{2,1,0:T(8,128)(2,1)S(1)}, bf16[2,16,1024]{2,1,0:T(8,128)(2,1)S(1)}, u32[]{:S(2)}, u32[]{:S(2)}) %collective-permute-start.4) | collective-permute-done | bytes 65568 | tf_op jit(solution)/shard_map/ppermute | solution.py:47
  14.0 0.5 %suffix_away.4 = bf16[272,128]{1,0:T(8,128)(2,1)S(1)} custom-call(bf16[4,512,128]{2,1,0:T(8,128)(2,1)S(1)} %get-tuple-element.20.keys_ref, bf16[4,128,512]{2,1,0:T(8,128)(2,1)S(1)} %get-tuple-element.21.values_ref, f32[5,8,128]{2,1,0:T(8,128)S(1)} %get-tuple-element.22.member_ref, bf16[2,16,1024]{2,1,0:T(8,128)(2,1)S(1)} %collective-permute-done.4.message_ref), custom_call_target="tpu_custom_call" | custom-call | flops 200000000 | bytes 2097152 | tf_op jit(solution)/shard_map/suffix_away/pallas_call | solution.py:381
  14.6 3.2 %collective-permute-start.5 = (bf16[272,128]{1,0:T(8,128)(2,1)S(1)}, bf16[272,128]{1,0:T(8,128)(2,1)S(1)}, u32[]{:S(2)}, u32[]{:S(2)}) collective-permute-start(bf16[272,128]{1,0:T(8,128)(2,1)S(1)} %suffix_away.4), channel_id=1, source_target_pairs={{0,9},{1,8},{4,29},{5,28},{8,1},{9,0},{12,21},{13,20},{16,25},{17,... | collective-permute-start | bytes 208904 | tf_op jit(solution)/shard_map/ppermute | solution.py:47
  18.4 2.5 %home_part.1 = (f32[128,128]{1,0:T(8,128)S(1)}, f32[8,128]{1,0:T(8,128)S(1)}, bf16[144,128]{1,0:T(8,128)(2,1)S(1)}) custom-call(s32[1]{0:T(128)S(6)} %copy.7.length_ref, bf16[1,512,128]{2,1,0:T(8,128)(2,1)S(1)} %get-tuple-element.25.keys_ref, bf16[1,128,512]{2,1,0:T(8,128)(2,1)S(1)} %get-tuple-element.26.values_ref, ...), custom_call_target="tpu_custom_call" | custom-call | flops 536870912 | bytes 2097152 | tf_op jit(solution)/shard_map/home_part/pallas_call | solution.py:393
  20.9 0.8 %collective-permute-start.9 = (bf16[144,128]{1,0:T(8,128)(2,1)S(1)}, bf16[144,128]{1,0:T(8,128)(2,1)S(1)}, u32[]{:S(2)}, u32[]{:S(2)}) collective-permute-start(bf16[144,128]{1,0:T(8,128)(2,1)S(1)} %get-tuple-element.28), channel_id=1, source_target_pairs={{0,1},{1,0},{2,3},{3,2},{4,5},{5,4},{6,7},{7,6},{8,9},{9,8},{10,11... | collective-permute-start | bytes 110600 | tf_op jit(solution)/shard_map/ppermute | solution.py:25
  21.8 0.2 collective-permute-done.5.rest_1_
  22.0 0.1 collective-permute-start.10
  22.1 2.9 %collective-permute-done.9.rest_3_ = bf16[144,128]{1,0:T(8,128)(2,1)S(1)} collective-permute-done((bf16[144,128]{1,0:T(8,128)(2,1)S(1)}, bf16[144,128]{1,0:T(8,128)(2,1)S(1)}, u32[]{:S(2)}, u32[]{:S(2)}) %collective-permute-start.9) | collective-permute-done | bytes 36896 | tf_op jit(solution)/shard_map/ppermute | solution.py:25
  25.0 0.8 %combine.1 = f32[16,1024]{1,0:T(8,128)} custom-call(bf16[272,128]{1,0:T(8,128)(2,1)S(1)} %collective-permute-done.3.rest_0_, bf16[272,128]{1,0:T(8,128)(2,1)S(1)} %collective-permute-done.5.rest_1_, bf16[272,128]{1,0:T(8,128)(2,1)S(1)} %collective-permute-done.7.rest_2_, bf16[144,128]{1,0:T(8,128)(2,1)S(1)} %collective-permute-done.9.rest_3_, ...), custom_call_target="tpu_custom_call" | custom-call | tf_op jit(solution)/shard_map/combine/pallas_call | solution.py:419
  (13 shorter events, 0.1 us)
Async XLA Ops:
  0.0 1.5 %collective-permute-start.1 = (bf16[16,1024]{1,0:T(8,128)(2,1)}, bf16[16,1024]{1,0:T(8,128)(2,1)S(1)}, u32[]{:S(2)}, u32[]{:S(2)}) collective-permute-start(bf16[16,1024]{1,0:T(8,128)(2,1)} %refs_0_.1), channel_id=1, source_target_pairs={{0,4},{4,0},{1,5},{5,1},{2,6},{6,2},{3,7},{7,3},{8,12},{12,8},{9,1... | collective-permute-start | bytes 98312 | tf_op jit(solution)/shard_map/ppermute | solution.py:25
  0.5 8.6 %collective-permute-start = (bf16[32,64,256]{2,1,0:T(8,128)(2,1)}, bf16[32,64,256]{2,1,0:T(8,128)(2,1)S(1)}, u32[]{:S(2)}, u32[]{:S(2)}) collective-permute-start(bf16[32,64,256]{2,1,0:T(8,128)(2,1)} %bitcast.5), channel_id=1, source_target_pairs={{0,4},{4,0},{1,5},{5,1},{2,6},{6,2},{3,7},{7,3},{8,12},{12,8},{9,1... | collective-permute-start | bytes 3145736 | tf_op jit(solution)/shard_map/ppermute | solution.py:25
  1.5 7.0 %copy-start.2 = (bf16[16,1024]{1,0:T(8,128)(2,1)S(1)}, bf16[16,1024]{1,0:T(8,128)(2,1)}, u32[]{:S(2)}) copy-start(bf16[16,1024]{1,0:T(8,128)(2,1)} %refs_0_.1) | copy-start | bytes 98308
  1.5 7.5 %copy-start.1 = (bf16[32,1,64,256]{3,2,1,0:T(8,128)(2,1)S(1)}, bf16[32,1,64,256]{3,2,1,0:T(8,128)(2,1)}, u32[]{:S(2)}) copy-start(bf16[32,1,64,256]{3,2,1,0:T(8,128)(2,1)} %param.8) | copy-start | bytes 3145732
  1.5 8.3 %collective-permute-start.2 = (bf16[2,16,1024]{2,1,0:T(8,128)(2,1)S(1)}, bf16[2,16,1024]{2,1,0:T(8,128)(2,1)S(1)}, u32[]{:S(2)}, u32[]{:S(2)}) collective-permute-start(bf16[2,16,1024]{2,1,0:T(8,128)(2,1)S(1)} %both_cores.1), channel_id=1, source_target_pairs={{0,8},{1,9},{4,28},{5,29},{8,0},{9,1},{12,20},{13,21},{16,24},{17,... | collective-permute-start | bytes 196616 | tf_op jit(solution)/shard_map/ppermute | solution.py:47
  4.5 7.5 %collective-permute-start.6 = (bf16[2,16,1024]{2,1,0:T(8,128)(2,1)S(1)}, bf16[2,16,1024]{2,1,0:T(8,128)(2,1)S(1)}, u32[]{:S(2)}, u32[]{:S(2)}) collective-permute-start(bf16[2,16,1024]{2,1,0:T(8,128)(2,1)S(1)} %both_cores.1), channel_id=1, source_target_pairs={{0,16},{1,17},{4,21},{5,20},{8,24},{9,25},{12,29},{13,28},{16,0},{... | collective-permute-start | bytes 196616 | tf_op jit(solution)/shard_map/ppermute | solution.py:47
  7.1 6.9 %collective-permute-start.4 = (bf16[2,16,1024]{2,1,0:T(8,128)(2,1)S(1)}, bf16[2,16,1024]{2,1,0:T(8,128)(2,1)S(1)}, u32[]{:S(2)}, u32[]{:S(2)}) collective-permute-start(bf16[2,16,1024]{2,1,0:T(8,128)(2,1)S(1)} %both_cores.1), channel_id=1, source_target_pairs={{0,9},{1,8},{4,29},{5,28},{8,1},{9,0},{12,21},{13,20},{16,25},{17,... | collective-permute-start | bytes 196616 | tf_op jit(solution)/shard_map/ppermute | solution.py:47
  8.5 9.9 %collective-permute-start.8 = (bf16[16,1024]{1,0:T(8,128)(2,1)S(1)}, bf16[16,1024]{1,0:T(8,128)(2,1)S(1)}, u32[]{:S(2)}, u32[]{:S(2)}) collective-permute-start(bf16[16,1024]{1,0:T(8,128)(2,1)S(1)} %copy-done.2), channel_id=1, source_target_pairs={{0,1},{1,0},{2,3},{3,2},{4,5},{5,4},{6,7},{7,6},{8,9},{9,8},{10,11... | collective-permute-start | bytes 98312 | tf_op jit(solution)/shard_map/ppermute | solution.py:25
  9.8 8.6 %copy-start = (bf16[1,1,4096,256]{3,2,1,0:T(8,128)(2,1)S(1)}, bf16[1,1,4096,256]{3,2,1,0:T(8,128)(2,1)}, u32[]{:S(2)}) copy-start(bf16[1,1,4096,256]{3,2,1,0:T(8,128)(2,1)} %param.7) | copy-start | bytes 6291460
  10.4 11.4 %collective-permute-start.3 = (bf16[272,128]{1,0:T(8,128)(2,1)S(1)}, bf16[272,128]{1,0:T(8,128)(2,1)S(1)}, u32[]{:S(2)}, u32[]{:S(2)}) collective-permute-start(bf16[272,128]{1,0:T(8,128)(2,1)S(1)} %get-tuple-element.24), channel_id=1, source_target_pairs={{0,8},{1,9},{4,28},{5,29},{8,0},{9,1},{12,20},{13,21},{16,24},{17,... | collective-permute-start | bytes 208904 | tf_op jit(solution)/shard_map/ppermute | solution.py:47
  12.5 9.3 %collective-permute-start.7 = (bf16[272,128]{1,0:T(8,128)(2,1)S(1)}, bf16[272,128]{1,0:T(8,128)(2,1)S(1)}, u32[]{:S(2)}, u32[]{:S(2)}) collective-permute-start(bf16[272,128]{1,0:T(8,128)(2,1)S(1)} %suffix_away.5), channel_id=1, source_target_pairs={{0,16},{1,17},{4,21},{5,20},{8,24},{9,25},{12,29},{13,28},{16,0},{... | collective-permute-start | bytes 208904 | tf_op jit(solution)/shard_map/ppermute | solution.py:47
  14.6 7.4 %collective-permute-start.5 = (bf16[272,128]{1,0:T(8,128)(2,1)S(1)}, bf16[272,128]{1,0:T(8,128)(2,1)S(1)}, u32[]{:S(2)}, u32[]{:S(2)}) collective-permute-start(bf16[272,128]{1,0:T(8,128)(2,1)S(1)} %suffix_away.4), channel_id=1, source_target_pairs={{0,9},{1,8},{4,29},{5,28},{8,1},{9,0},{12,21},{13,20},{16,25},{17,... | collective-permute-start | bytes 208904 | tf_op jit(solution)/shard_map/ppermute | solution.py:47
  20.9 4.0 %collective-permute-start.9 = (bf16[144,128]{1,0:T(8,128)(2,1)S(1)}, bf16[144,128]{1,0:T(8,128)(2,1)S(1)}, u32[]{:S(2)}, u32[]{:S(2)}) collective-permute-start(bf16[144,128]{1,0:T(8,128)(2,1)S(1)} %get-tuple-element.28), channel_id=1, source_target_pairs={{0,1},{1,0},{2,3},{3,2},{4,5},{5,4},{6,7},{7,6},{8,9},{9,8},{10,11... | collective-permute-start | bytes 110600 | tf_op jit(solution)/shard_map/ppermute | solution.py:25
  22.0 3.0 %collective-permute-start.10 = (bf16[144,128]{1,0:T(8,128)(2,1)S(1)}, bf16[144,128]{1,0:T(8,128)(2,1)S(1)}, u32[]{:S(2)}, u32[]{:S(2)}) collective-permute-start(bf16[144,128]{1,0:T(8,128)(2,1)S(1)} %sibling_share.1), channel_id=1, source_target_pairs={{0,4},{4,0},{1,5},{5,1},{2,6},{6,2},{3,7},{7,3},{8,12},{12,8},{9,1... | collective-permute-start | bytes 110600 | tf_op jit(solution)/shard_map/ppermute | solution.py:25

commit v23 on v21

--- a/solution.py
+++ b/solution.py
@@ -232,17 +232,12 @@
             values_ref[i - 1] = values
 
 
-def all_vectors(own_ref, pair_ref):
-    return jnp.concatenate([stacked_heads(own_ref[...]), stacked_heads(pair_ref[...])], axis=0)
-
-
 def suffix_parts(vectors, keys_ref, values_ref, members, place=0):
     n_slots = members[0].shape[0]
     half = keys_ref.shape[1] // n_slots
     scores = [scores_of(keys_ref[place + i], each) for i, each in enumerate(vectors)]
     softmaxes = []
     for member, score in zip(members, scores):
-        member = jnp.concatenate([member] * (score.shape[1] // VECS), axis=1)
         pieces = [
             jnp.where(
                 member[k : k + 1, :] > 0.0, score[k * half : (k + 1) * half], big_negative
@@ -262,11 +257,6 @@
     ]
 
 
-def half_of(part, side):
-    lanes = slice(side * VECS, (side + 1) * VECS)
-    return [x[:, lanes] for x in part]
-
-
 def away_kernel(place, keys_ref, values_ref, member_ref, message_ref, out_ref, *after_ref):
     for ref in after_ref:
         ref[...] = jnp.zeros(ref.shape, jnp.float32)
@@ -275,22 +265,26 @@
     store_units(out_ref, suffix_parts(vectors, keys_ref, values_ref, members, place))
 
 
-def home_kernel(
-    length_ref, keys_ref, values_ref, member_ref, own_ref, pair_ref, prompt_ref, after_ref,
-    summed_ref, stats_ref, out_ref,
-):
-    vectors = all_vectors(own_ref, pair_ref)
+def home_part(length_ref, keys_ref, values_ref, member_ref, queries_ref, prompt_ref):
+    vectors = stacked_heads(queries_ref[...])
     half = keys_ref.shape[1] // member_ref.shape[1]
     (suffix,) = suffix_parts([vectors], keys_ref, values_ref, [member_ref[0]])
-    prompt = prompt_part(length_ref[0], half, prompt_ref, vectors)
-    part = merged([prompt, suffix])
-    top, total, summed_ref[...] = half_of(part, 0)
+    return merged([prompt_part(length_ref[0], half, prompt_ref, vectors), suffix])
+
+
+def pair_heads_kernel(*refs):
+    *inputs, _, out_ref = refs
+    store_units(out_ref, [home_part(*inputs)])
+
+
+def own_heads_kernel(*refs):
+    *inputs, _, summed_ref, stats_ref = refs
+    top, total, summed_ref[...] = home_part(*inputs)
     stats_ref[...] = jnp.concatenate([top, total, jnp.zeros((6, VECS), jnp.float32)], axis=0)
-    store_units(out_ref, [half_of(part, 1)])
 
 
 def sibling_kernel(*rest):
-    units, out_ref = rest[:-1], rest[-1]
+    units, out_ref = rest[:-2], rest[-1]
     core = lax.axis_index("core")
     store_units(out_ref, [merged([load_unit(unit, 1 - core) for unit in units])])
 
@@ -390,31 +384,39 @@
         received.append(exchanged(units, k))
         after += token
 
-    summed, stats, given = pl.pallas_call(
-        home_kernel,
-        out_shape=(
-            pltpu.VMEM((HD, VECS), jnp.float32),
-            pltpu.VMEM((8, VECS), jnp.float32),
-            pltpu.VMEM((HD + STAT_ROWS, VECS), jnp.bfloat16),
-        ),
-        in_specs=[pl.BlockSpec(memory_space=pltpu.SMEM)] + [vmem] * 7,
-        out_specs=(vmem,) * 3,
-        compiler_params=params,
-        cost_estimate=pl.CostEstimate(
-            flops=8 * tokens * VECS * HD, bytes_accessed=2 * tokens * width, transcendentals=0
-        ),
-        name="home_part",
-    )(lengths, home_keys, home_values, member, own, other, prompt_cache.reshape(tokens, width), *after)
+    home = pl.CostEstimate(
+        flops=5 * tokens * VECS * HD, bytes_accessed=2 * tokens * width, transcendentals=0
+    )
+    home_specs = [pl.BlockSpec(memory_space=pltpu.SMEM)] + [vmem] * 6
+    prompt = prompt_cache.reshape(tokens, width)
+    given = pl.pallas_call(
+        pair_heads_kernel,
+        out_shape=pltpu.VMEM((HD + STAT_ROWS, VECS), jnp.bfloat16),
+        in_specs=home_specs,
+        out_specs=vmem,
+        compiler_params=params,
+        cost_estimate=home,
+        name="home_pair_heads",
+    )(lengths, home_keys, home_values, member, other, prompt, *after)
     last = swapped(given, "pair")
+    summed, stats = pl.pallas_call(
+        own_heads_kernel,
+        out_shape=(pltpu.VMEM((HD, VECS), jnp.float32), pltpu.VMEM((8, VECS), jnp.float32)),
+        in_specs=home_specs,
+        out_specs=(vmem,) * 2,
+        compiler_params=params,
+        cost_estimate=home,
+        name="home_own_heads",
+    )(lengths, home_keys, home_values, member, own, prompt, *after)
 
     share = pl.pallas_call(
         sibling_kernel,
         out_shape=pltpu.VMEM((HD + STAT_ROWS, VECS), jnp.bfloat16),
-        in_specs=[vmem] * n_messages,
+        in_specs=[vmem] * (n_messages + 1),
         out_specs=vmem,
         compiler_params=params,
         name="sibling_share",
-    )(*received)
+    )(*received, stats)
 
     return pl.pallas_call(
         final_kernel,

time: 24.8 us -> 24.8 us (level)
  waiting for transfers between devices: 3.63 us -> 2.99 us
  Pallas kernels: 6.4 us -> 7.03 us
    ppermute x6, waiting for transfers between devices: 2.21 us -> 1.57 us  [exchanged(): return lax.ppermute(value, ('z', 'core', 'pair'), pairs)]
    pallas_call x1 -> x2, Pallas kernels: 2.51 us -> 3.12 us  [the longest x1 1.57 us: on_device(): pl.pallas_call(pair_heads_kernel, out_shape=pltpu.VMEM((HD + STAT_ROWS, V...]
  transfers between devices with their start and end apart: 11 -> 11, of which waited for: 4 -> 4; matrix products, arithmetic and copies ran while one was open for 0% -> 0% of each run, Pallas kernels for 23% -> 25%
where the time goes in v23:
time: 24.8 us; the launch traced here: 24.6 us
  starting transfers between devices  13.8 us (56%)
  Pallas kernels  7.03 us (28%)
  waiting for transfers between devices  2.99 us (12%)
  between operations  0.77 us (3%)
    ppermute x6, starting transfers between devices, exchanged(): return lax.ppermute(value, ('z', 'core', 'pair'), pairs)  11.6 us
    ppermute x5, starting transfers between devices, swapped(): return lax.ppermute(value, axis, [(0, 1), (1, 0)])  2.23 us
    ppermute x6, waiting for transfers between devices, exchanged(): return lax.ppermute(value, ('z', 'core', 'pair'), pairs)  1.57 us
    pallas_call x1, Pallas kernels, on_device(): pl.pallas_call(pair_heads_kernel, out_shape=pltpu.VMEM((HD + STAT_ROWS, V...  1.57 us
    pallas_call x1, Pallas kernels, on_device(): pl.pallas_call(own_heads_kernel, out_shape=(pltpu.VMEM((HD, VECS), jnp.fl...  1.55 us
    pallas_call x3, Pallas kernels, on_device(): pl.pallas_call(functools.partial(away_kernel, 2 * ((k + 1) // 2)), out_sh...  1.53 us
    ppermute x5, waiting for transfers between devices, swapped(): return lax.ppermute(value, axis, [(0, 1), (1, 0)])  1.42 us
    pallas_call x1, Pallas kernels, on_device(): pl.pallas_call(stage_kernel, out_shape=tuple((pltpu.VMEM(each.shape, each...  0.79 us
  transfers between devices with their start and end apart: 11, of which 4 were waited for; matrix products, arithmetic and copies ran while one was open for 0% of the time, Pallas kernels for 25%

profile of v23, /device:TPU:0, one launch (start us, length us, event | category | flops | bytes accessed | tf_op | source)
XLA Modules:
  0.0 24.6 jit_solution(14682992905254666183)
XLA Ops:
  0.0 0.5 %collective-permute-start.1 = (bf16[16,1024]{1,0:T(8,128)(2,1)}, bf16[16,1024]{1,0:T(8,128)(2,1)S(1)}, u32[]{:S(2)}, u32[]{:S(2)}) collective-permute-start(bf16[16,1024]{1,0:T(8,128)(2,1)} %refs_0_.3), channel_id=1, source_target_pairs={{0,4},{4,0},{1,5},{5,1},{2,6},{6,2},{3,7},{7,3},{8,12},{12,8},{9,1... | collective-permute-start | bytes 98312 | tf_op jit(solution)/shard_map/ppermute | solution.py:25
  0.5 0.1 collective-permute-start
  0.5 0.8 %stage.1 = (bf16[16,1024]{1,0:T(8,128)(2,1)S(1)}, s32[4,128]{1,0:T(4,128)S(1)}, s32[1,128]{1,0:T(1,128)S(1)}) custom-call(bf16[16,1024]{1,0:T(8,128)(2,1)} %refs_0_.3, s32[4,128]{1,0:T(4,128)} %bitcast.8, s32[1,128]{1,0:T(1,128)} %bitcast.9), custom_call_target="tpu_custom_call" | custom-call | tf_op jit(solution)/shard_map/stage/pallas_call | solution.py:326
  1.3 0.2 collective-permute-done.1.sibling_ref
  1.5 3.0 %collective-permute-start.2 = (bf16[2,16,1024]{2,1,0:T(8,128)(2,1)S(1)}, bf16[2,16,1024]{2,1,0:T(8,128)(2,1)S(1)}, u32[]{:S(2)}, u32[]{:S(2)}) collective-permute-start(bf16[2,16,1024]{2,1,0:T(8,128)(2,1)S(1)} %both_cores.1), channel_id=1, source_target_pairs={{0,8},{1,9},{4,28},{5,29},{8,0},{9,1},{12,20},{13,21},{16,24},{17,... | collective-permute-start | bytes 196616 | tf_op jit(solution)/shard_map/ppermute | solution.py:47
  4.5 1.4 %collective-permute-start.6 = (bf16[2,16,1024]{2,1,0:T(8,128)(2,1)S(1)}, bf16[2,16,1024]{2,1,0:T(8,128)(2,1)S(1)}, u32[]{:S(2)}, u32[]{:S(2)}) collective-permute-start(bf16[2,16,1024]{2,1,0:T(8,128)(2,1)S(1)} %both_cores.1), channel_id=1, source_target_pairs={{0,9},{1,8},{4,29},{5,28},{8,1},{9,0},{12,21},{13,20},{16,25},{17,... | collective-permute-start | bytes 196616 | tf_op jit(solution)/shard_map/ppermute | solution.py:47
  5.9 2.6 %collective-permute-start.4 = (bf16[2,16,1024]{2,1,0:T(8,128)(2,1)S(1)}, bf16[2,16,1024]{2,1,0:T(8,128)(2,1)S(1)}, u32[]{:S(2)}, u32[]{:S(2)}) collective-permute-start(bf16[2,16,1024]{2,1,0:T(8,128)(2,1)S(1)} %both_cores.1), channel_id=1, source_target_pairs={{0,16},{1,17},{4,21},{5,20},{8,24},{9,25},{12,29},{13,28},{16,0},{... | collective-permute-start | bytes 196616 | tf_op jit(solution)/shard_map/ppermute | solution.py:47
  8.5 0.5 %collective-permute-start.8 = (bf16[16,1024]{1,0:T(8,128)(2,1)S(1)}, bf16[16,1024]{1,0:T(8,128)(2,1)S(1)}, u32[]{:S(2)}, u32[]{:S(2)}) collective-permute-start(bf16[16,1024]{1,0:T(8,128)(2,1)S(1)} %copy-done.2), channel_id=1, source_target_pairs={{0,1},{1,0},{2,3},{3,2},{4,5},{5,4},{6,7},{7,6},{8,9},{9,8},{10,11... | collective-permute-start | bytes 98312 | tf_op jit(solution)/shard_map/ppermute | solution.py:25
  9.0 0.8 %prepare.1 = (bf16[1,512,128]{2,1,0:T(8,128)(2,1)S(1)}, bf16[1,128,512]{2,1,0:T(8,128)(2,1)S(1)}, bf16[4,512,128]{2,1,0:T(8,128)(2,1)S(1)}, bf16[4,128,512]{2,1,0:T(8,128)(2,1)S(1)}, f32[5,8,128]{2,1,0:T(8,128)S(1)}) custom-call(bf16[32,64,256]{2,1,0:T(8,128)(2,1)S(1)} %bitcast.7, s32[4,128]{1,0:T(4,128)S(1)} %get-tuple-element.17.table, ...), custom_call_target="tpu_custom_call" | custom-call | flops 200000000 | bytes 2097152 | tf_op jit(solution)/shard_map/prepare/pallas_call | solution.py:348
  9.8 0.0 copy-start
  9.8 0.5 %suffix_away.3 = (bf16[272,128]{1,0:T(8,128)(2,1)S(1)}, f32[8,128]{1,0:T(8,128)S(1)}) custom-call(bf16[4,512,128]{2,1,0:T(8,128)(2,1)S(1)} %get-tuple-element.19.keys_ref, bf16[4,128,512]{2,1,0:T(8,128)(2,1)S(1)} %get-tuple-element.20.values_ref, f32[5,8,128]{2,1,0:T(8,128)S(1)} %get-tuple-element.21.member_ref.refs_3_, ...), custom_call_target="tpu_custom_call" | custom-call | flops 200000000 | bytes 2097152 | tf_op jit(solution)/shard_map/suffix_away/pallas_call | solution.py:375
  10.4 1.6 %collective-permute-start.3 = (bf16[272,128]{1,0:T(8,128)(2,1)S(1)}, bf16[272,128]{1,0:T(8,128)(2,1)S(1)}, u32[]{:S(2)}, u32[]{:S(2)}) collective-permute-start(bf16[272,128]{1,0:T(8,128)(2,1)S(1)} %get-tuple-element.23), channel_id=1, source_target_pairs={{0,8},{1,9},{4,28},{5,29},{8,0},{9,1},{12,20},{13,21},{16,24},{17,... | collective-permute-start | bytes 208904 | tf_op jit(solution)/shard_map/ppermute | solution.py:47
  12.0 0.5 %suffix_away.5 = bf16[272,128]{1,0:T(8,128)(2,1)S(1)} custom-call(bf16[4,512,128]{2,1,0:T(8,128)(2,1)S(1)} %get-tuple-element.19.keys_ref, bf16[4,128,512]{2,1,0:T(8,128)(2,1)S(1)} %get-tuple-element.20.values_ref, f32[5,8,128]{2,1,0:T(8,128)S(1)} %get-tuple-element.21.member_ref.refs_3_, bf16[2,16,1024]{2,1,0:T(8,128)(2,1)S(1)} %collective-permute-done.6.message_ref), custom_call_target="tpu_custom_call" | custom-call | flops 200000000 | bytes 2097152 | tf_op jit(solution)/shard_map/suffix_away/pallas_call | solution.py:375
  12.5 1.4 %collective-permute-start.7 = (bf16[272,128]{1,0:T(8,128)(2,1)S(1)}, bf16[272,128]{1,0:T(8,128)(2,1)S(1)}, u32[]{:S(2)}, u32[]{:S(2)}) collective-permute-start(bf16[272,128]{1,0:T(8,128)(2,1)S(1)} %suffix_away.5), channel_id=1, source_target_pairs={{0,9},{1,8},{4,29},{5,28},{8,1},{9,0},{12,21},{13,20},{16,25},{17,... | collective-permute-start | bytes 208904 | tf_op jit(solution)/shard_map/ppermute | solution.py:47
  14.0 0.5 %suffix_away.4 = bf16[272,128]{1,0:T(8,128)(2,1)S(1)} custom-call(bf16[4,512,128]{2,1,0:T(8,128)(2,1)S(1)} %get-tuple-element.19.keys_ref, bf16[4,128,512]{2,1,0:T(8,128)(2,1)S(1)} %get-tuple-element.20.values_ref, f32[5,8,128]{2,1,0:T(8,128)S(1)} %get-tuple-element.21.member_ref.refs_3_, bf16[2,16,1024]{2,1,0:T(8,128)(2,1)S(1)} %collective-permute-done.4.message_ref), custom_call_target="tpu_custom_call" | custom-call | flops 200000000 | bytes 2097152 | tf_op jit(solution)/shard_map/suffix_away/pallas_call | solution.py:375
  14.5 1.6 %collective-permute-start.5 = (bf16[272,128]{1,0:T(8,128)(2,1)S(1)}, bf16[272,128]{1,0:T(8,128)(2,1)S(1)}, u32[]{:S(2)}, u32[]{:S(2)}) collective-permute-start(bf16[272,128]{1,0:T(8,128)(2,1)S(1)} %suffix_away.4), channel_id=1, source_target_pairs={{0,16},{1,17},{4,21},{5,20},{8,24},{9,25},{12,29},{13,28},{16,0},{... | collective-permute-start | bytes 208904 | tf_op jit(solution)/shard_map/ppermute | solution.py:47
  16.7 1.6 %home_pair_heads.1 = bf16[144,128]{1,0:T(8,128)(2,1)S(1)} custom-call(s32[1]{0:T(128)S(6)} %copy.7.refs_0_, bf16[1,512,128]{2,1,0:T(8,128)(2,1)S(1)} %get-tuple-element.24.refs_1_, bf16[1,128,512]{2,1,0:T(8,128)(2,1)S(1)} %get-tuple-element.25.refs_2_, f32[5,8,128]{2,1,0:T(8,128)S(1)} %get-tuple-element.21.member_ref.refs_3_, ...), custom_call_target="tpu_custom_call" | custom-call | flops 335544320 | bytes 2097152 | tf_op jit(solution)/shard_map/home_pair_heads/pallas_call | solution.py:392
  18.3 1.1 %collective-permute-start.9 = (bf16[144,128]{1,0:T(8,128)(2,1)S(1)}, bf16[144,128]{1,0:T(8,128)(2,1)S(1)}, u32[]{:S(2)}, u32[]{:S(2)}) collective-permute-start(bf16[144,128]{1,0:T(8,128)(2,1)S(1)} %home_pair_heads.1), channel_id=1, source_target_pairs={{0,1},{1,0},{2,3},{3,2},{4,5},{5,4},{6,7},{7,6},{8,9},{9,8},{10,11... | collective-permute-start | bytes 110600 | tf_op jit(solution)/shard_map/ppermute | solution.py:25
  19.4 1.6 %home_own_heads.1 = (f32[128,128]{1,0:T(8,128)S(1)}, f32[8,128]{1,0:T(8,128)S(1)}) custom-call(s32[1]{0:T(128)S(6)} %copy.7.refs_0_, bf16[1,512,128]{2,1,0:T(8,128)(2,1)S(1)} %get-tuple-element.24.refs_1_, bf16[1,128,512]{2,1,0:T(8,128)(2,1)S(1)} %get-tuple-element.25.refs_2_, f32[5,8,128]{2,1,0:T(8,128)S(1)} %get-tuple-element.21.member_ref.refs_3_, ...), custom_call_target="tpu_custom_call" | custom-call | flops 335544320 | bytes 2097152 | tf_op jit(solution)/shard_map/home_own_heads/pallas_call | solution.py:402
  21.0 1.6 %collective-permute-done.5.rest_1_ = bf16[272,128]{1,0:T(8,128)(2,1)S(1)} collective-permute-done((bf16[272,128]{1,0:T(8,128)(2,1)S(1)}, bf16[272,128]{1,0:T(8,128)(2,1)S(1)}, u32[]{:S(2)}, u32[]{:S(2)}) %collective-permute-start.5) | collective-permute-done | bytes 69664 | tf_op jit(solution)/shard_map/ppermute | solution.py:47
  22.6 0.1 collective-permute-start.10
  22.7 0.3 %collective-permute-done.9.rest_3_ = bf16[144,128]{1,0:T(8,128)(2,1)S(1)} collective-permute-done((bf16[144,128]{1,0:T(8,128)(2,1)S(1)}, bf16[144,128]{1,0:T(8,128)(2,1)S(1)}, u32[]{:S(2)}, u32[]{:S(2)}) %collective-permute-start.9) | collective-permute-done | bytes 36896 | tf_op jit(solution)/shard_map/ppermute | solution.py:25
  22.9 0.9 %collective-permute-done.10.rest_4_ = bf16[144,128]{1,0:T(8,128)(2,1)S(1)} collective-permute-done((bf16[144,128]{1,0:T(8,128)(2,1)S(1)}, bf16[144,128]{1,0:T(8,128)(2,1)S(1)}, u32[]{:S(2)}, u32[]{:S(2)}) %collective-permute-start.10) | collective-permute-done | bytes 36896 | tf_op jit(solution)/shard_map/ppermute | solution.py:25
  23.9 0.8 %combine.1 = f32[16,1024]{1,0:T(8,128)} custom-call(bf16[272,128]{1,0:T(8,128)(2,1)S(1)} %collective-permute-done.3.rest_0_, bf16[272,128]{1,0:T(8,128)(2,1)S(1)} %collective-permute-done.5.rest_1_, bf16[272,128]{1,0:T(8,128)(2,1)S(1)} %collective-permute-done.7.rest_2_, bf16[144,128]{1,0:T(8,128)(2,1)S(1)} %collective-permute-done.9.rest_3_, ...), custom_call_target="tpu_custom_call" | custom-call | tf_op jit(solution)/shard_map/combine/pallas_call | solution.py:421
  (14 shorter events, 0.1 us)
Async XLA Ops:
  0.0 1.5 %collective-permute-start.1 = (bf16[16,1024]{1,0:T(8,128)(2,1)}, bf16[16,1024]{1,0:T(8,128)(2,1)S(1)}, u32[]{:S(2)}, u32[]{:S(2)}) collective-permute-start(bf16[16,1024]{1,0:T(8,128)(2,1)} %refs_0_.3), channel_id=1, source_target_pairs={{0,4},{4,0},{1,5},{5,1},{2,6},{6,2},{3,7},{7,3},{8,12},{12,8},{9,1... | collective-permute-start | bytes 98312 | tf_op jit(solution)/shard_map/ppermute | solution.py:25
  0.5 8.6 %collective-permute-start = (bf16[32,64,256]{2,1,0:T(8,128)(2,1)}, bf16[32,64,256]{2,1,0:T(8,128)(2,1)S(1)}, u32[]{:S(2)}, u32[]{:S(2)}) collective-permute-start(bf16[32,64,256]{2,1,0:T(8,128)(2,1)} %bitcast.6), channel_id=1, source_target_pairs={{0,4},{4,0},{1,5},{5,1},{2,6},{6,2},{3,7},{7,3},{8,12},{12,8},{9,1... | collective-permute-start | bytes 3145736 | tf_op jit(solution)/shard_map/ppermute | solution.py:25
  1.5 7.0 %copy-start.2 = (bf16[16,1024]{1,0:T(8,128)(2,1)S(1)}, bf16[16,1024]{1,0:T(8,128)(2,1)}, u32[]{:S(2)}) copy-start(bf16[16,1024]{1,0:T(8,128)(2,1)} %refs_0_.3) | copy-start | bytes 98308
  1.5 7.5 %copy-start.1 = (bf16[32,1,64,256]{3,2,1,0:T(8,128)(2,1)S(1)}, bf16[32,1,64,256]{3,2,1,0:T(8,128)(2,1)}, u32[]{:S(2)}) copy-start(bf16[32,1,64,256]{3,2,1,0:T(8,128)(2,1)} %param.8) | copy-start | bytes 3145732
  1.5 8.3 %collective-permute-start.2 = (bf16[2,16,1024]{2,1,0:T(8,128)(2,1)S(1)}, bf16[2,16,1024]{2,1,0:T(8,128)(2,1)S(1)}, u32[]{:S(2)}, u32[]{:S(2)}) collective-permute-start(bf16[2,16,1024]{2,1,0:T(8,128)(2,1)S(1)} %both_cores.1), channel_id=1, source_target_pairs={{0,8},{1,9},{4,28},{5,29},{8,0},{9,1},{12,20},{13,21},{16,24},{17,... | collective-permute-start | bytes 196616 | tf_op jit(solution)/shard_map/ppermute | solution.py:47
  4.5 7.5 %collective-permute-start.6 = (bf16[2,16,1024]{2,1,0:T(8,128)(2,1)S(1)}, bf16[2,16,1024]{2,1,0:T(8,128)(2,1)S(1)}, u32[]{:S(2)}, u32[]{:S(2)}) collective-permute-start(bf16[2,16,1024]{2,1,0:T(8,128)(2,1)S(1)} %both_cores.1), channel_id=1, source_target_pairs={{0,9},{1,8},{4,29},{5,28},{8,1},{9,0},{12,21},{13,20},{16,25},{17,... | collective-permute-start | bytes 196616 | tf_op jit(solution)/shard_map/ppermute | solution.py:47
  5.9 8.1 %collective-permute-start.4 = (bf16[2,16,1024]{2,1,0:T(8,128)(2,1)S(1)}, bf16[2,16,1024]{2,1,0:T(8,128)(2,1)S(1)}, u32[]{:S(2)}, u32[]{:S(2)}) collective-permute-start(bf16[2,16,1024]{2,1,0:T(8,128)(2,1)S(1)} %both_cores.1), channel_id=1, source_target_pairs={{0,16},{1,17},{4,21},{5,20},{8,24},{9,25},{12,29},{13,28},{16,0},{... | collective-permute-start | bytes 196616 | tf_op jit(solution)/shard_map/ppermute | solution.py:47
  8.5 8.2 %collective-permute-start.8 = (bf16[16,1024]{1,0:T(8,128)(2,1)S(1)}, bf16[16,1024]{1,0:T(8,128)(2,1)S(1)}, u32[]{:S(2)}, u32[]{:S(2)}) collective-permute-start(bf16[16,1024]{1,0:T(8,128)(2,1)S(1)} %copy-done.2), channel_id=1, source_target_pairs={{0,1},{1,0},{2,3},{3,2},{4,5},{5,4},{6,7},{7,6},{8,9},{9,8},{10,11... | collective-permute-start | bytes 98312 | tf_op jit(solution)/shard_map/ppermute | solution.py:25
  9.8 6.9 %copy-start = (bf16[1,1,4096,256]{3,2,1,0:T(8,128)(2,1)S(1)}, bf16[1,1,4096,256]{3,2,1,0:T(8,128)(2,1)}, u32[]{:S(2)}) copy-start(bf16[1,1,4096,256]{3,2,1,0:T(8,128)(2,1)} %param.7) | copy-start | bytes 6291460
  10.4 10.6 %collective-permute-start.3 = (bf16[272,128]{1,0:T(8,128)(2,1)S(1)}, bf16[272,128]{1,0:T(8,128)(2,1)S(1)}, u32[]{:S(2)}, u32[]{:S(2)}) collective-permute-start(bf16[272,128]{1,0:T(8,128)(2,1)S(1)} %get-tuple-element.23), channel_id=1, source_target_pairs={{0,8},{1,9},{4,28},{5,29},{8,0},{9,1},{12,20},{13,21},{16,24},{17,... | collective-permute-start | bytes 208904 | tf_op jit(solution)/shard_map/ppermute | solution.py:47
  12.5 8.5 %collective-permute-start.7 = (bf16[272,128]{1,0:T(8,128)(2,1)S(1)}, bf16[272,128]{1,0:T(8,128)(2,1)S(1)}, u32[]{:S(2)}, u32[]{:S(2)}) collective-permute-start(bf16[272,128]{1,0:T(8,128)(2,1)S(1)} %suffix_away.5), channel_id=1, source_target_pairs={{0,9},{1,8},{4,29},{5,28},{8,1},{9,0},{12,21},{13,20},{16,25},{17,... | collective-permute-start | bytes 208904 | tf_op jit(solution)/shard_map/ppermute | solution.py:47
  14.5 8.1 %collective-permute-start.5 = (bf16[272,128]{1,0:T(8,128)(2,1)S(1)}, bf16[272,128]{1,0:T(8,128)(2,1)S(1)}, u32[]{:S(2)}, u32[]{:S(2)}) collective-permute-start(bf16[272,128]{1,0:T(8,128)(2,1)S(1)} %suffix_away.4), channel_id=1, source_target_pairs={{0,16},{1,17},{4,21},{5,20},{8,24},{9,25},{12,29},{13,28},{16,0},{... | collective-permute-start | bytes 208904 | tf_op jit(solution)/shard_map/ppermute | solution.py:47
  18.3 4.6 %collective-permute-start.9 = (bf16[144,128]{1,0:T(8,128)(2,1)S(1)}, bf16[144,128]{1,0:T(8,128)(2,1)S(1)}, u32[]{:S(2)}, u32[]{:S(2)}) collective-permute-start(bf16[144,128]{1,0:T(8,128)(2,1)S(1)} %home_pair_heads.1), channel_id=1, source_target_pairs={{0,1},{1,0},{2,3},{3,2},{4,5},{5,4},{6,7},{7,6},{8,9},{9,8},{10,11... | collective-permute-start | bytes 110600 | tf_op jit(solution)/shard_map/ppermute | solution.py:25
  22.6 1.3 %collective-permute-start.10 = (bf16[144,128]{1,0:T(8,128)(2,1)S(1)}, bf16[144,128]{1,0:T(8,128)(2,1)S(1)}, u32[]{:S(2)}, u32[]{:S(2)}) collective-permute-start(bf16[144,128]{1,0:T(8,128)(2,1)S(1)} %sibling_share.1), channel_id=1, source_target_pairs={{0,4},{4,0},{1,5},{5,1},{2,6},{6,2},{3,7},{7,3},{8,12},{12,8},{9,1... | collective-permute-start | bytes 110600 | tf_op jit(solution)/shard_map/ppermute | solution.py:25

commit v24 on v23

--- a/solution.py
+++ b/solution.py
@@ -15,6 +15,7 @@
 VECS = HEADS * BEAMS
 STAT_ROWS = 16
 CHUNK = 512
+FIRST_MASKS = (2, 3, 1)
 SURELY_VALID = 1024
 
 big_negative = -1e30
@@ -25,32 +26,18 @@
     return lax.ppermute(value, axis, [(0, 1), (1, 0)])
 
 
-def shares(n_req):
-    both = n_req // 2
-    rest = [d for d in range(1, n_req) if d != both]
-    return both, (rest[: len(rest) // 2], rest[len(rest) // 2 :])
-
-
-def exchanged(value, message):
-    n_req = lax.axis_size("z")
-    both, own = shares(n_req)
+def exchanged(value, mask):
     pairs = []
-    for z in range(n_req):
+    for z in range(lax.axis_size("z")):
         for core in range(2):
             for pair in range(2):
-                if message == 0:
-                    mask, side = both, core
-                else:
-                    mask, side = own[core][(message - 1) // 2], (message - 1) % 2
-                target = ((z ^ mask) * 2 + core) * 2 + (pair ^ side)
+                target = ((z ^ mask) * 2 + core) * 2 + (pair ^ core)
                 pairs.append(((z * 2 + core) * 2 + pair, target))
     return lax.ppermute(value, ("z", "core", "pair"), pairs)
 
 
-def masks_here(n_req):
-    both, own = shares(n_req)
-    core = lax.axis_index("core")
-    return [both] + [jnp.where(core == 0, d0, d1) for d0, d1 in zip(*own)]
+def mask_order(n_req):
+    return FIRST_MASKS if n_req == 4 else tuple(range(n_req - 1, 0, -1))
 
 
 def stage_kernel(*refs):
@@ -202,7 +189,7 @@
     found = jnp.concatenate(found, axis=0)
 
     requests = [z * 2 + core]
-    for mask in masks_here(n_req):
+    for mask in range(1, n_req):
         requests += [(z ^ mask) * 2, (z ^ mask) * 2 + 1]
     for i, request in enumerate(requests):
         lane = iota((rows, VECS), 1)
@@ -341,18 +328,18 @@
         cost_estimate=early,
         name="both_cores",
     )(own, swapped(queries, "core"))
-    n_messages = n_req - 1
-    order = [1, 0] + list(range(n_messages - 1, 1, -1)) if n_messages > 1 else [0]
-    messages = {k: exchanged(both, k) for k in order}
+    first, *others = mask_order(n_req)
+    order = [first] + others[::-1]
+    messages = {mask: exchanged(both, mask) for mask in order}
 
     home_keys, home_values, keys, values, member = pl.pallas_call(
         functools.partial(prepare_kernel, capacity),
         out_shape=(
             pltpu.VMEM((1, 2 * capacity * half, HD), jnp.bfloat16),
             pltpu.VMEM((1, HD, 2 * capacity * half), jnp.bfloat16),
-            pltpu.VMEM((n_req, 2 * capacity * half, HD), jnp.bfloat16),
-            pltpu.VMEM((n_req, HD, 2 * capacity * half), jnp.bfloat16),
-            pltpu.VMEM((1 + n_req, 2 * capacity, VECS), jnp.float32),
+            pltpu.VMEM((2 * n_req - 2, 2 * capacity * half, HD), jnp.bfloat16),
+            pltpu.VMEM((2 * n_req - 2, HD, 2 * capacity * half), jnp.bfloat16),
+            pltpu.VMEM((2 * n_req - 1, 2 * capacity, VECS), jnp.float32),
         ),
         in_specs=[vmem] * 4,
         out_specs=(vmem,) * 5,
@@ -368,20 +355,20 @@
     )
 
     received, after = [], []
-    for k in order:
+    for mask in order:
         out = [pltpu.VMEM((2 * HD + STAT_ROWS, VECS), jnp.bfloat16)]
-        if k == order[0]:
+        if mask == first:
             out.append(pltpu.VMEM((8, VECS), jnp.float32))
         units, *token = pl.pallas_call(
-            functools.partial(away_kernel, 2 * ((k + 1) // 2)),
+            functools.partial(away_kernel, 2 * mask - 2),
             out_shape=out,
             in_specs=[vmem] * 4,
             out_specs=[vmem] * len(out),
             compiler_params=params,
             cost_estimate=some,
             name="suffix_away",
-        )(keys, values, member, messages[k])
-        received.append(exchanged(units, k))
+        )(keys, values, member, messages[mask])
+        received.append(exchanged(units, mask))
         after += token
 
     home = pl.CostEstimate(
@@ -412,7 +399,7 @@
     share = pl.pallas_call(
         sibling_kernel,
         out_shape=pltpu.VMEM((HD + STAT_ROWS, VECS), jnp.bfloat16),
-        in_specs=[vmem] * (n_messages + 1),
+        in_specs=[vmem] * n_req,
         out_specs=vmem,
         compiler_params=params,
         name="sibling_share",
@@ -421,7 +408,7 @@
     return pl.pallas_call(
         final_kernel,
         out_shape=jax.ShapeDtypeStruct((BEAMS, HEADS * HD), jnp.float32),
-        in_specs=[vmem] * (4 + n_messages),
+        in_specs=[vmem] * (3 + n_req),
         out_specs=vmem,
         compiler_params=params,
         name="combine",

time: 24.8 us -> 24.8 us (level)
  waiting for transfers between devices: 2.99 us -> 1.14 us
  starting transfers between devices: 13.8 us -> 15.5 us
    ppermute x6, waiting for transfers between devices: 1.57 us -> 0.02 us  [exchanged(): return lax.ppermute(value, ('z', 'core', 'pair'), pairs)]
    ppermute x5, starting transfers between devices: 2.23 us -> 3.47 us  [swapped(): return lax.ppermute(value, axis, [(0, 1), (1, 0)])]
    ppermute x6, starting transfers between devices: 11.6 us -> 12 us  [exchanged(): return lax.ppermute(value, ('z', 'core', 'pair'), pairs)]
    ppermute x5, waiting for transfers between devices: 1.42 us -> 1.12 us  [swapped(): return lax.ppermute(value, axis, [(0, 1), (1, 0)])]
  transfers between devices with their start and end apart: 11 -> 11, of which waited for: 4 -> 2; matrix products, arithmetic and copies ran while one was open for 0% -> 0% of each run, Pallas kernels for 25% -> 26%
where the time goes in v24:
time: 24.8 us; the launch traced here: 24.6 us
  starting transfers between devices  15.5 us (62%)
  Pallas kernels  7.21 us (29%)
  waiting for transfers between devices  1.14 us (5%)
  between operations  0.77 us (3%)
    ppermute x6, starting transfers between devices, exchanged(): return lax.ppermute(value, ('z', 'core', 'pair'), pairs)  12 us
    ppermute x5, starting transfers between devices, swapped(): return lax.ppermute(value, axis, [(0, 1), (1, 0)])  3.47 us
    pallas_call x1, Pallas kernels, on_device(): pl.pallas_call(pair_heads_kernel, out_shape=pltpu.VMEM((HD + STAT_ROWS, V...  1.57 us
    pallas_call x1, Pallas kernels, on_device(): pl.pallas_call(own_heads_kernel, out_shape=(pltpu.VMEM((HD, VECS), jnp.fl...  1.55 us
    pallas_call x3, Pallas kernels, on_device(): pl.pallas_call(functools.partial(away_kernel, 2 * mask - 2), out_shape=ou...  1.53 us
    ppermute x5, waiting for transfers between devices, swapped(): return lax.ppermute(value, axis, [(0, 1), (1, 0)])  1.12 us
    pallas_call x1, Pallas kernels, on_device(): pl.pallas_call(functools.partial(prepare_kernel, capacity), out_shape=(pl...  0.94 us
    pallas_call x1, Pallas kernels, on_device(): pl.pallas_call(stage_kernel, out_shape=tuple((pltpu.VMEM(each.shape, each...  0.79 us
  transfers between devices with their start and end apart: 11, of which 2 were waited for; matrix products, arithmetic and copies ran while one was open for 0% of the time, Pallas kernels for 26%

profile of v24, /device:TPU:0, one launch (start us, length us, event | category | flops | bytes accessed | tf_op | source)
XLA Modules:
  0.0 24.6 jit_solution(8727273824050708416)
XLA Ops:
  0.0 0.5 %collective-permute-start.1 = (bf16[16,1024]{1,0:T(8,128)(2,1)}, bf16[16,1024]{1,0:T(8,128)(2,1)S(1)}, u32[]{:S(2)}, u32[]{:S(2)}) collective-permute-start(bf16[16,1024]{1,0:T(8,128)(2,1)} %refs_0_.3), channel_id=1, source_target_pairs={{0,4},{4,0},{1,5},{5,1},{2,6},{6,2},{3,7},{7,3},{8,12},{12,8},{9,1... | collective-permute-start | bytes 98312 | tf_op jit(solution)/shard_map/ppermute | solution.py:26
  0.5 0.1 collective-permute-start
  0.5 0.8 %stage.1 = (bf16[16,1024]{1,0:T(8,128)(2,1)S(1)}, s32[4,128]{1,0:T(4,128)S(1)}, s32[1,128]{1,0:T(1,128)S(1)}) custom-call(bf16[16,1024]{1,0:T(8,128)(2,1)} %refs_0_.3, s32[4,128]{1,0:T(4,128)} %bitcast.8, s32[1,128]{1,0:T(1,128)} %bitcast.9), custom_call_target="tpu_custom_call" | custom-call | tf_op jit(solution)/shard_map/stage/pallas_call | solution.py:313
  1.3 0.2 collective-permute-done.1.sibling_ref
  1.5 4.0 %collective-permute-start.2 = (bf16[2,16,1024]{2,1,0:T(8,128)(2,1)S(1)}, bf16[2,16,1024]{2,1,0:T(8,128)(2,1)S(1)}, u32[]{:S(2)}, u32[]{:S(2)}) collective-permute-start(bf16[2,16,1024]{2,1,0:T(8,128)(2,1)S(1)} %both_cores.1), channel_id=1, source_target_pairs={{0,16},{1,17},{4,21},{5,20},{8,24},{9,25},{12,29},{13,28},{16,0},{... | collective-permute-start | bytes 196616 | tf_op jit(solution)/shard_map/ppermute | solution.py:36
  5.5 1.3 %collective-permute-start.6 = (bf16[2,16,1024]{2,1,0:T(8,128)(2,1)S(1)}, bf16[2,16,1024]{2,1,0:T(8,128)(2,1)S(1)}, u32[]{:S(2)}, u32[]{:S(2)}) collective-permute-start(bf16[2,16,1024]{2,1,0:T(8,128)(2,1)S(1)} %both_cores.1), channel_id=1, source_target_pairs={{0,24},{1,25},{4,29},{5,28},{8,16},{9,17},{12,21},{13,20},{16,8},{... | collective-permute-start | bytes 196616 | tf_op jit(solution)/shard_map/ppermute | solution.py:36
  6.9 0.2 collective-permute-start.4
  7.1 1.5 %collective-permute-start.8 = (bf16[16,1024]{1,0:T(8,128)(2,1)S(1)}, bf16[16,1024]{1,0:T(8,128)(2,1)S(1)}, u32[]{:S(2)}, u32[]{:S(2)}) collective-permute-start(bf16[16,1024]{1,0:T(8,128)(2,1)S(1)} %copy-done.2), channel_id=1, source_target_pairs={{0,1},{1,0},{2,3},{3,2},{4,5},{5,4},{6,7},{7,6},{8,9},{9,8},{10,11... | collective-permute-start | bytes 98312 | tf_op jit(solution)/shard_map/ppermute | solution.py:26
  8.6 0.0 collective-permute-done.far_ref
  8.6 0.9 %prepare.1 = (bf16[1,512,128]{2,1,0:T(8,128)(2,1)S(1)}, bf16[1,128,512]{2,1,0:T(8,128)(2,1)S(1)}, bf16[6,512,128]{2,1,0:T(8,128)(2,1)S(1)}, bf16[6,128,512]{2,1,0:T(8,128)(2,1)S(1)}, f32[7,8,128]{2,1,0:T(8,128)S(1)}) custom-call(bf16[32,64,256]{2,1,0:T(8,128)(2,1)S(1)} %bitcast.7, s32[4,128]{1,0:T(4,128)S(1)} %get-tuple-element.17.table, ...), custom_call_target="tpu_custom_call" | custom-call | flops 200000000 | bytes 2097152 | tf_op jit(solution)/shard_map/prepare/pallas_call | solution.py:335
  9.6 0.5 %suffix_away.3 = (bf16[272,128]{1,0:T(8,128)(2,1)S(1)}, f32[8,128]{1,0:T(8,128)S(1)}) custom-call(bf16[6,512,128]{2,1,0:T(8,128)(2,1)S(1)} %get-tuple-element.19.keys_ref, bf16[6,128,512]{2,1,0:T(8,128)(2,1)S(1)} %get-tuple-element.20.values_ref, f32[7,8,128]{2,1,0:T(8,128)S(1)} %get-tuple-element.21.member_ref.refs_3_, ...), custom_call_target="tpu_custom_call" | custom-call | flops 200000000 | bytes 2097152 | tf_op jit(solution)/shard_map/suffix_away/pallas_call | solution.py:362
  10.1 0.0 copy-start
  10.1 2.9 %collective-permute-start.3 = (bf16[272,128]{1,0:T(8,128)(2,1)S(1)}, bf16[272,128]{1,0:T(8,128)(2,1)S(1)}, u32[]{:S(2)}, u32[]{:S(2)}) collective-permute-start(bf16[272,128]{1,0:T(8,128)(2,1)S(1)} %get-tuple-element.23), channel_id=1, source_target_pairs={{0,16},{1,17},{4,21},{5,20},{8,24},{9,25},{12,29},{13,28},{16,0},{... | collective-permute-start | bytes 208904 | tf_op jit(solution)/shard_map/ppermute | solution.py:36
  13.0 0.5 %suffix_away.5 = bf16[272,128]{1,0:T(8,128)(2,1)S(1)} custom-call(bf16[6,512,128]{2,1,0:T(8,128)(2,1)S(1)} %get-tuple-element.19.keys_ref, bf16[6,128,512]{2,1,0:T(8,128)(2,1)S(1)} %get-tuple-element.20.values_ref, f32[7,8,128]{2,1,0:T(8,128)S(1)} %get-tuple-element.21.member_ref.refs_3_, bf16[2,16,1024]{2,1,0:T(8,128)(2,1)S(1)} %collective-permute-done.6.message_ref), custom_call_target="tpu_custom_call" | custom-call | flops 200000000 | bytes 2097152 | tf_op jit(solution)/shard_map/suffix_away/pallas_call | solution.py:362
  13.5 2.9 %collective-permute-start.7 = (bf16[272,128]{1,0:T(8,128)(2,1)S(1)}, bf16[272,128]{1,0:T(8,128)(2,1)S(1)}, u32[]{:S(2)}, u32[]{:S(2)}) collective-permute-start(bf16[272,128]{1,0:T(8,128)(2,1)S(1)} %suffix_away.5), channel_id=1, source_target_pairs={{0,24},{1,25},{4,29},{5,28},{8,16},{9,17},{12,21},{13,20},{16,8},{... | collective-permute-start | bytes 208904 | tf_op jit(solution)/shard_map/ppermute | solution.py:36
  16.4 0.5 %suffix_away.4 = bf16[272,128]{1,0:T(8,128)(2,1)S(1)} custom-call(bf16[6,512,128]{2,1,0:T(8,128)(2,1)S(1)} %get-tuple-element.19.keys_ref, bf16[6,128,512]{2,1,0:T(8,128)(2,1)S(1)} %get-tuple-element.20.values_ref, f32[7,8,128]{2,1,0:T(8,128)S(1)} %get-tuple-element.21.member_ref.refs_3_, bf16[2,16,1024]{2,1,0:T(8,128)(2,1)S(1)} %collective-permute-done.4.message_ref), custom_call_target="tpu_custom_call" | custom-call | flops 200000000 | bytes 2097152 | tf_op jit(solution)/shard_map/suffix_away/pallas_call | solution.py:362
  16.9 0.6 %collective-permute-start.5 = (bf16[272,128]{1,0:T(8,128)(2,1)S(1)}, bf16[272,128]{1,0:T(8,128)(2,1)S(1)}, u32[]{:S(2)}, u32[]{:S(2)}) collective-permute-start(bf16[272,128]{1,0:T(8,128)(2,1)S(1)} %suffix_away.4), channel_id=1, source_target_pairs={{0,8},{1,9},{4,13},{5,12},{8,0},{9,1},{12,5},{13,4},{16,24},{17,25... | collective-permute-start | bytes 208904 | tf_op jit(solution)/shard_map/ppermute | solution.py:36
  18.2 1.6 %home_pair_heads.1 = bf16[144,128]{1,0:T(8,128)(2,1)S(1)} custom-call(s32[1]{0:T(128)S(6)} %copy.7.refs_0_, bf16[1,512,128]{2,1,0:T(8,128)(2,1)S(1)} %get-tuple-element.24.refs_1_, bf16[1,128,512]{2,1,0:T(8,128)(2,1)S(1)} %get-tuple-element.25.refs_2_, f32[7,8,128]{2,1,0:T(8,128)S(1)} %get-tuple-element.21.member_ref.refs_3_, ...), custom_call_target="tpu_custom_call" | custom-call | flops 335544320 | bytes 2097152 | tf_op jit(solution)/shard_map/home_pair_heads/pallas_call | solution.py:379
  19.8 0.8 %collective-permute-start.9 = (bf16[144,128]{1,0:T(8,128)(2,1)S(1)}, bf16[144,128]{1,0:T(8,128)(2,1)S(1)}, u32[]{:S(2)}, u32[]{:S(2)}) collective-permute-start(bf16[144,128]{1,0:T(8,128)(2,1)S(1)} %home_pair_heads.1), channel_id=1, source_target_pairs={{0,1},{1,0},{2,3},{3,2},{4,5},{5,4},{6,7},{7,6},{8,9},{9,8},{10,11... | collective-permute-start | bytes 110600 | tf_op jit(solution)/shard_map/ppermute | solution.py:26
  20.6 1.6 %home_own_heads.1 = (f32[128,128]{1,0:T(8,128)S(1)}, f32[8,128]{1,0:T(8,128)S(1)}) custom-call(s32[1]{0:T(128)S(6)} %copy.7.refs_0_, bf16[1,512,128]{2,1,0:T(8,128)(2,1)S(1)} %get-tuple-element.24.refs_1_, bf16[1,128,512]{2,1,0:T(8,128)(2,1)S(1)} %get-tuple-element.25.refs_2_, f32[7,8,128]{2,1,0:T(8,128)S(1)} %get-tuple-element.21.member_ref.refs_3_, ...), custom_call_target="tpu_custom_call" | custom-call | flops 335544320 | bytes 2097152 | tf_op jit(solution)/shard_map/home_own_heads/pallas_call | solution.py:389
  22.2 0.1 sibling_share.1
  22.2 0.7 %collective-permute-start.10 = (bf16[144,128]{1,0:T(8,128)(2,1)S(1)}, bf16[144,128]{1,0:T(8,128)(2,1)S(1)}, u32[]{:S(2)}, u32[]{:S(2)}) collective-permute-start(bf16[144,128]{1,0:T(8,128)(2,1)S(1)} %sibling_share.1), channel_id=1, source_target_pairs={{0,4},{4,0},{1,5},{5,1},{2,6},{6,2},{3,7},{7,3},{8,12},{12,8},{9,1... | collective-permute-start | bytes 110600 | tf_op jit(solution)/shard_map/ppermute | solution.py:26
  22.9 0.9 %collective-permute-done.9.rest_3_ = bf16[144,128]{1,0:T(8,128)(2,1)S(1)} collective-permute-done((bf16[144,128]{1,0:T(8,128)(2,1)S(1)}, bf16[144,128]{1,0:T(8,128)(2,1)S(1)}, u32[]{:S(2)}, u32[]{:S(2)}) %collective-permute-start.9) | collective-permute-done | bytes 36896 | tf_op jit(solution)/shard_map/ppermute | solution.py:26
  23.8 0.8 %combine.1 = f32[16,1024]{1,0:T(8,128)} custom-call(bf16[272,128]{1,0:T(8,128)(2,1)S(1)} %collective-permute-done.3.rest_0_, bf16[272,128]{1,0:T(8,128)(2,1)S(1)} %collective-permute-done.5.rest_1_, bf16[272,128]{1,0:T(8,128)(2,1)S(1)} %collective-permute-done.7.rest_2_, bf16[144,128]{1,0:T(8,128)(2,1)S(1)} %collective-permute-done.9.rest_3_, ...), custom_call_target="tpu_custom_call" | custom-call | tf_op jit(solution)/shard_map/combine/pallas_call | solution.py:408
  (14 shorter events, 0.0 us)
Async XLA Ops:
  0.0 1.5 %collective-permute-start.1 = (bf16[16,1024]{1,0:T(8,128)(2,1)}, bf16[16,1024]{1,0:T(8,128)(2,1)S(1)}, u32[]{:S(2)}, u32[]{:S(2)}) collective-permute-start(bf16[16,1024]{1,0:T(8,128)(2,1)} %refs_0_.3), channel_id=1, source_target_pairs={{0,4},{4,0},{1,5},{5,1},{2,6},{6,2},{3,7},{7,3},{8,12},{12,8},{9,1... | collective-permute-start | bytes 98312 | tf_op jit(solution)/shard_map/ppermute | solution.py:26
  0.5 8.2 %collective-permute-start = (bf16[32,64,256]{2,1,0:T(8,128)(2,1)}, bf16[32,64,256]{2,1,0:T(8,128)(2,1)S(1)}, u32[]{:S(2)}, u32[]{:S(2)}) collective-permute-start(bf16[32,64,256]{2,1,0:T(8,128)(2,1)} %bitcast.6), channel_id=1, source_target_pairs={{0,4},{4,0},{1,5},{5,1},{2,6},{6,2},{3,7},{7,3},{8,12},{12,8},{9,1... | collective-permute-start | bytes 3145736 | tf_op jit(solution)/shard_map/ppermute | solution.py:26
  1.5 5.6 %copy-start.2 = (bf16[16,1024]{1,0:T(8,128)(2,1)S(1)}, bf16[16,1024]{1,0:T(8,128)(2,1)}, u32[]{:S(2)}) copy-start(bf16[16,1024]{1,0:T(8,128)(2,1)} %refs_0_.3) | copy-start | bytes 98308
  1.5 7.1 %copy-start.1 = (bf16[32,1,64,256]{3,2,1,0:T(8,128)(2,1)S(1)}, bf16[32,1,64,256]{3,2,1,0:T(8,128)(2,1)}, u32[]{:S(2)}) copy-start(bf16[32,1,64,256]{3,2,1,0:T(8,128)(2,1)} %param.8) | copy-start | bytes 3145732
  1.5 8.0 %collective-permute-start.2 = (bf16[2,16,1024]{2,1,0:T(8,128)(2,1)S(1)}, bf16[2,16,1024]{2,1,0:T(8,128)(2,1)S(1)}, u32[]{:S(2)}, u32[]{:S(2)}) collective-permute-start(bf16[2,16,1024]{2,1,0:T(8,128)(2,1)S(1)} %both_cores.1), channel_id=1, source_target_pairs={{0,16},{1,17},{4,21},{5,20},{8,24},{9,25},{12,29},{13,28},{16,0},{... | collective-permute-start | bytes 196616 | tf_op jit(solution)/shard_map/ppermute | solution.py:36
  5.5 7.4 %collective-permute-start.6 = (bf16[2,16,1024]{2,1,0:T(8,128)(2,1)S(1)}, bf16[2,16,1024]{2,1,0:T(8,128)(2,1)S(1)}, u32[]{:S(2)}, u32[]{:S(2)}) collective-permute-start(bf16[2,16,1024]{2,1,0:T(8,128)(2,1)S(1)} %both_cores.1), channel_id=1, source_target_pairs={{0,24},{1,25},{4,29},{5,28},{8,16},{9,17},{12,21},{13,20},{16,8},{... | collective-permute-start | bytes 196616 | tf_op jit(solution)/shard_map/ppermute | solution.py:36
  6.9 9.5 %collective-permute-start.4 = (bf16[2,16,1024]{2,1,0:T(8,128)(2,1)S(1)}, bf16[2,16,1024]{2,1,0:T(8,128)(2,1)S(1)}, u32[]{:S(2)}, u32[]{:S(2)}) collective-permute-start(bf16[2,16,1024]{2,1,0:T(8,128)(2,1)S(1)} %both_cores.1), channel_id=1, source_target_pairs={{0,8},{1,9},{4,13},{5,12},{8,0},{9,1},{12,5},{13,4},{16,24},{17,25... | collective-permute-start | bytes 196616 | tf_op jit(solution)/shard_map/ppermute | solution.py:36
  7.1 11.1 %collective-permute-start.8 = (bf16[16,1024]{1,0:T(8,128)(2,1)S(1)}, bf16[16,1024]{1,0:T(8,128)(2,1)S(1)}, u32[]{:S(2)}, u32[]{:S(2)}) collective-permute-start(bf16[16,1024]{1,0:T(8,128)(2,1)S(1)} %copy-done.2), channel_id=1, source_target_pairs={{0,1},{1,0},{2,3},{3,2},{4,5},{5,4},{6,7},{7,6},{8,9},{9,8},{10,11... | collective-permute-start | bytes 98312 | tf_op jit(solution)/shard_map/ppermute | solution.py:26
  10.1 8.1 %copy-start = (bf16[1,1,4096,256]{3,2,1,0:T(8,128)(2,1)S(1)}, bf16[1,1,4096,256]{3,2,1,0:T(8,128)(2,1)}, u32[]{:S(2)}) copy-start(bf16[1,1,4096,256]{3,2,1,0:T(8,128)(2,1)} %param.7) | copy-start | bytes 6291460
  10.1 12.0 %collective-permute-start.3 = (bf16[272,128]{1,0:T(8,128)(2,1)S(1)}, bf16[272,128]{1,0:T(8,128)(2,1)S(1)}, u32[]{:S(2)}, u32[]{:S(2)}) collective-permute-start(bf16[272,128]{1,0:T(8,128)(2,1)S(1)} %get-tuple-element.23), channel_id=1, source_target_pairs={{0,16},{1,17},{4,21},{5,20},{8,24},{9,25},{12,29},{13,28},{16,0},{... | collective-permute-start | bytes 208904 | tf_op jit(solution)/shard_map/ppermute | solution.py:36
  13.5 8.7 %collective-permute-start.7 = (bf16[272,128]{1,0:T(8,128)(2,1)S(1)}, bf16[272,128]{1,0:T(8,128)(2,1)S(1)}, u32[]{:S(2)}, u32[]{:S(2)}) collective-permute-start(bf16[272,128]{1,0:T(8,128)(2,1)S(1)} %suffix_away.5), channel_id=1, source_target_pairs={{0,24},{1,25},{4,29},{5,28},{8,16},{9,17},{12,21},{13,20},{16,8},{... | collective-permute-start | bytes 208904 | tf_op jit(solution)/shard_map/ppermute | solution.py:36
  16.9 5.2 %collective-permute-start.5 = (bf16[272,128]{1,0:T(8,128)(2,1)S(1)}, bf16[272,128]{1,0:T(8,128)(2,1)S(1)}, u32[]{:S(2)}, u32[]{:S(2)}) collective-permute-start(bf16[272,128]{1,0:T(8,128)(2,1)S(1)} %suffix_away.4), channel_id=1, source_target_pairs={{0,8},{1,9},{4,13},{5,12},{8,0},{9,1},{12,5},{13,4},{16,24},{17,25... | collective-permute-start | bytes 208904 | tf_op jit(solution)/shard_map/ppermute | solution.py:36
  19.8 4.0 %collective-permute-start.9 = (bf16[144,128]{1,0:T(8,128)(2,1)S(1)}, bf16[144,128]{1,0:T(8,128)(2,1)S(1)}, u32[]{:S(2)}, u32[]{:S(2)}) collective-permute-start(bf16[144,128]{1,0:T(8,128)(2,1)S(1)} %home_pair_heads.1), channel_id=1, source_target_pairs={{0,1},{1,0},{2,3},{3,2},{4,5},{5,4},{6,7},{7,6},{8,9},{9,8},{10,11... | collective-permute-start | bytes 110600 | tf_op jit(solution)/shard_map/ppermute | solution.py:26
  22.2 1.6 %collective-permute-start.10 = (bf16[144,128]{1,0:T(8,128)(2,1)S(1)}, bf16[144,128]{1,0:T(8,128)(2,1)S(1)}, u32[]{:S(2)}, u32[]{:S(2)}) collective-permute-start(bf16[144,128]{1,0:T(8,128)(2,1)S(1)} %sibling_share.1), channel_id=1, source_target_pairs={{0,4},{4,0},{1,5},{5,1},{2,6},{6,2},{3,7},{7,3},{8,12},{12,8},{9,1... | collective-permute-start | bytes 110600 | tf_op jit(solution)/shard_map/ppermute | solution.py:26

commit v25 on v24

--- a/solution.py
+++ b/solution.py
@@ -244,8 +244,8 @@
     ]
 
 
-def away_kernel(place, keys_ref, values_ref, member_ref, message_ref, out_ref, *after_ref):
-    for ref in after_ref:
+def away_kernel(place, keys_ref, values_ref, member_ref, message_ref, after_ref, out_ref, *next_ref):
+    for ref in next_ref:
         ref[...] = jnp.zeros(ref.shape, jnp.float32)
     vectors = [stacked_heads(message_ref[core]) for core in range(2)]
     members = [member_ref[1 + place + core] for core in range(2)]
@@ -260,7 +260,7 @@
 
 
 def pair_heads_kernel(*refs):
-    *inputs, _, out_ref = refs
+    *inputs, out_ref = refs
     store_units(out_ref, [home_part(*inputs)])
 
 
@@ -302,6 +302,7 @@
     rows = block_table.shape[0]
     vmem = pl.BlockSpec(memory_space=pltpu.VMEM)
     params = pltpu.CompilerParams(vmem_limit_bytes=32 * 2**20)
+    little = pl.CostEstimate(flops=10**6, bytes_accessed=0, transcendentals=0)
     some = pl.CostEstimate(flops=2 * 10**8, bytes_accessed=2**21, transcendentals=0)
     early = pl.CostEstimate(flops=2 * 10**10, bytes_accessed=0, transcendentals=0)
 
@@ -329,7 +330,7 @@
         name="both_cores",
     )(own, swapped(queries, "core"))
     first, *others = mask_order(n_req)
-    order = [first] + others[::-1]
+    order = others[::-1] + [first]
     messages = {mask: exchanged(both, mask) for mask in order}
 
     home_keys, home_values, keys, values, member = pl.pallas_call(
@@ -354,6 +355,20 @@
         far,
     )
 
+    home = pl.CostEstimate(
+        flops=5 * tokens * VECS * HD, bytes_accessed=2 * tokens * width, transcendentals=0
+    )
+    home_specs = [pl.BlockSpec(memory_space=pltpu.SMEM)] + [vmem] * 5
+    prompt = prompt_cache.reshape(tokens, width)
+    given = pl.pallas_call(
+        pair_heads_kernel,
+        out_shape=pltpu.VMEM((HD + STAT_ROWS, VECS), jnp.bfloat16),
+        in_specs=home_specs,
+        out_specs=vmem,
+        compiler_params=params,
+        cost_estimate=little,
+        name="home_pair_heads",
+    )(lengths, home_keys, home_values, member, other, prompt)
     received, after = [], []
     for mask in order:
         out = [pltpu.VMEM((2 * HD + STAT_ROWS, VECS), jnp.bfloat16)]
@@ -362,34 +377,20 @@
         units, *token = pl.pallas_call(
             functools.partial(away_kernel, 2 * mask - 2),
             out_shape=out,
-            in_specs=[vmem] * 4,
+            in_specs=[vmem] * 5,
             out_specs=[vmem] * len(out),
             compiler_params=params,
             cost_estimate=some,
             name="suffix_away",
-        )(keys, values, member, messages[mask])
+        )(keys, values, member, messages[mask], given)
         received.append(exchanged(units, mask))
         after += token
 
-    home = pl.CostEstimate(
-        flops=5 * tokens * VECS * HD, bytes_accessed=2 * tokens * width, transcendentals=0
-    )
-    home_specs = [pl.BlockSpec(memory_space=pltpu.SMEM)] + [vmem] * 6
-    prompt = prompt_cache.reshape(tokens, width)
-    given = pl.pallas_call(
-        pair_heads_kernel,
-        out_shape=pltpu.VMEM((HD + STAT_ROWS, VECS), jnp.bfloat16),
-        in_specs=home_specs,
-        out_specs=vmem,
-        compiler_params=params,
-        cost_estimate=home,
-        name="home_pair_heads",
-    )(lengths, home_keys, home_values, member, other, prompt, *after)
     last = swapped(given, "pair")
     summed, stats = pl.pallas_call(
         own_heads_kernel,
         out_shape=(pltpu.VMEM((HD, VECS), jnp.float32), pltpu.VMEM((8, VECS), jnp.float32)),
-        in_specs=home_specs,
+        in_specs=home_specs + [vmem],
         out_specs=(vmem,) * 2,
         compiler_params=params,
         cost_estimate=home,

time: 24.8 us -> 26.2 us (1.056)
  waiting for transfers between devices: 1.14 us -> 4.57 us
  starting transfers between devices: 15.5 us -> 13.5 us
    ppermute x6, waiting for transfers between devices: 0.02 us -> 2.91 us  [exchanged(): return lax.ppermute(value, ('z', 'core', 'pair'), pairs)]
    ppermute x6, starting transfers between devices: 12 us -> 9.51 us  [exchanged(): return lax.ppermute(value, ('z', 'core', 'pair'), pairs)]
    ppermute x5, waiting for transfers between devices: 1.12 us -> 1.66 us  [swapped(): return lax.ppermute(value, axis, [(0, 1), (1, 0)])]
    ppermute x5, starting transfers between devices: 3.47 us -> 3.95 us  [swapped(): return lax.ppermute(value, axis, [(0, 1), (1, 0)])]
  transfers between devices with their start and end apart: 11 -> 11, of which waited for: 2 -> 5; matrix products, arithmetic and copies ran while one was open for 0% -> 0% of each run, Pallas kernels for 26% -> 25%
where the time goes in v25:
time: 26.2 us; the launch traced here: 26 us
  starting transfers between devices  13.5 us (52%)
  Pallas kernels  7.19 us (27%)
  waiting for transfers between devices  4.57 us (17%)
  between operations  0.76 us (3%)
    ppermute x6, starting transfers between devices, exchanged(): return lax.ppermute(value, ('z', 'core', 'pair'), pairs)  9.51 us
    ppermute x5, starting transfers between devices, swapped(): return lax.ppermute(value, axis, [(0, 1), (1, 0)])  3.95 us
    ppermute x6, waiting for transfers between devices, exchanged(): return lax.ppermute(value, ('z', 'core', 'pair'), pairs)  2.91 us
    ppermute x5, waiting for transfers between devices, swapped(): return lax.ppermute(value, axis, [(0, 1), (1, 0)])  1.66 us
    pallas_call x1, Pallas kernels, on_device(): pl.pallas_call(pair_heads_kernel, out_shape=pltpu.VMEM((HD + STAT_ROWS, V...  1.57 us
    pallas_call x1, Pallas kernels, on_device(): pl.pallas_call(own_heads_kernel, out_shape=(pltpu.VMEM((HD, VECS), jnp.fl...  1.56 us
    pallas_call x3, Pallas kernels, on_device(): pl.pallas_call(functools.partial(away_kernel, 2 * mask - 2), out_shape=ou...  1.51 us
    pallas_call x1, Pallas kernels, on_device(): pl.pallas_call(functools.partial(prepare_kernel, capacity), out_shape=(pl...  0.94 us
  transfers between devices with their start and end apart: 11, of which 5 were waited for; matrix products, arithmetic and copies ran while one was open for 0% of the time, Pallas kernels for 25%

profile of v25, /device:TPU:0, one launch (start us, length us, event | category | flops | bytes accessed | tf_op | source)
XLA Modules:
  0.0 26.0 jit_solution(6481692367485610818)
XLA Ops:
  0.0 0.5 %collective-permute-start.1 = (bf16[16,1024]{1,0:T(8,128)(2,1)}, bf16[16,1024]{1,0:T(8,128)(2,1)S(1)}, u32[]{:S(2)}, u32[]{:S(2)}) collective-permute-start(bf16[16,1024]{1,0:T(8,128)(2,1)} %refs_0_.3), channel_id=1, source_target_pairs={{0,4},{4,0},{1,5},{5,1},{2,6},{6,2},{3,7},{7,3},{8,12},{12,8},{9,1... | collective-permute-start | bytes 98312 | tf_op jit(solution)/shard_map/ppermute | solution.py:26
  0.5 0.1 collective-permute-start
  0.5 0.8 %stage.1 = (bf16[16,1024]{1,0:T(8,128)(2,1)S(1)}, s32[4,128]{1,0:T(4,128)S(1)}, s32[1,128]{1,0:T(1,128)S(1)}) custom-call(bf16[16,1024]{1,0:T(8,128)(2,1)} %refs_0_.3, s32[4,128]{1,0:T(4,128)} %bitcast.8, s32[1,128]{1,0:T(1,128)} %bitcast.9), custom_call_target="tpu_custom_call" | custom-call | tf_op jit(solution)/shard_map/stage/pallas_call | solution.py:314
  1.3 0.2 collective-permute-done.1.sibling_ref
  1.6 4.0 %collective-permute-start.7 = (bf16[2,16,1024]{2,1,0:T(8,128)(2,1)S(1)}, bf16[2,16,1024]{2,1,0:T(8,128)(2,1)S(1)}, u32[]{:S(2)}, u32[]{:S(2)}) collective-permute-start(bf16[2,16,1024]{2,1,0:T(8,128)(2,1)S(1)} %both_cores.1), channel_id=1, source_target_pairs={{0,16},{1,17},{4,21},{5,20},{8,24},{9,25},{12,29},{13,28},{16,0},{... | collective-permute-start | bytes 196616 | tf_op jit(solution)/shard_map/ppermute | solution.py:36
  5.6 1.3 %collective-permute-start.5 = (bf16[2,16,1024]{2,1,0:T(8,128)(2,1)S(1)}, bf16[2,16,1024]{2,1,0:T(8,128)(2,1)S(1)}, u32[]{:S(2)}, u32[]{:S(2)}) collective-permute-start(bf16[2,16,1024]{2,1,0:T(8,128)(2,1)S(1)} %both_cores.1), channel_id=1, source_target_pairs={{0,24},{1,25},{4,29},{5,28},{8,16},{9,17},{12,21},{13,20},{16,8},{... | collective-permute-start | bytes 196616 | tf_op jit(solution)/shard_map/ppermute | solution.py:36
  6.9 1.5 %collective-permute-start.3 = (bf16[16,1024]{1,0:T(8,128)(2,1)S(1)}, bf16[16,1024]{1,0:T(8,128)(2,1)S(1)}, u32[]{:S(2)}, u32[]{:S(2)}) collective-permute-start(bf16[16,1024]{1,0:T(8,128)(2,1)S(1)} %copy-done.2), channel_id=1, source_target_pairs={{0,1},{1,0},{2,3},{3,2},{4,5},{5,4},{6,7},{7,6},{8,9},{9,8},{10,11... | collective-permute-start | bytes 98312 | tf_op jit(solution)/shard_map/ppermute | solution.py:26
  8.4 0.2 collective-permute-start.2
  9.3 0.9 %prepare.1 = (bf16[1,512,128]{2,1,0:T(8,128)(2,1)S(1)}, bf16[1,128,512]{2,1,0:T(8,128)(2,1)S(1)}, bf16[6,512,128]{2,1,0:T(8,128)(2,1)S(1)}, bf16[6,128,512]{2,1,0:T(8,128)(2,1)S(1)}, f32[7,8,128]{2,1,0:T(8,128)S(1)}) custom-call(bf16[32,64,256]{2,1,0:T(8,128)(2,1)S(1)} %bitcast.7, s32[4,128]{1,0:T(4,128)S(1)} %get-tuple-element.17.table, ...), custom_call_target="tpu_custom_call" | custom-call | flops 200000000 | bytes 2097152 | tf_op jit(solution)/shard_map/prepare/pallas_call | solution.py:336
  10.2 0.6 %collective-permute-done.3.refs_4_ = bf16[16,1024]{1,0:T(8,128)(2,1)S(1)} collective-permute-done((bf16[16,1024]{1,0:T(8,128)(2,1)S(1)}, bf16[16,1024]{1,0:T(8,128)(2,1)S(1)}, u32[]{:S(2)}, u32[]{:S(2)}) %collective-permute-start.3) | collective-permute-done | bytes 32800 | tf_op jit(solution)/shard_map/ppermute | solution.py:26
  10.8 1.6 %home_pair_heads.1.after_ref = bf16[144,128]{1,0:T(8,128)(2,1)S(1)} custom-call(s32[1]{0:T(128)S(6)} %copy.7.refs_0_, bf16[1,512,128]{2,1,0:T(8,128)(2,1)S(1)} %get-tuple-element.23.refs_1_, bf16[1,128,512]{2,1,0:T(8,128)(2,1)S(1)} %get-tuple-element.24.refs_2_, f32[7,8,128]{2,1,0:T(8,128)S(1)} %get-tuple-element.21.refs_3_.member_ref, ...), custom_call_target="tpu_custom_call" | custom-call | flops 1000000 | tf_op jit(solution)/shard_map/home_pair_heads/pallas_call | solution.py:363
  12.4 0.5 %suffix_away.5 = (bf16[272,128]{1,0:T(8,128)(2,1)S(1)}, f32[8,128]{1,0:T(8,128)S(1)}) custom-call(bf16[6,512,128]{2,1,0:T(8,128)(2,1)S(1)} %get-tuple-element.19.keys_ref, bf16[6,128,512]{2,1,0:T(8,128)(2,1)S(1)} %get-tuple-element.20.values_ref, f32[7,8,128]{2,1,0:T(8,128)S(1)} %get-tuple-element.21.refs_3_.member_ref, ...), custom_call_target="tpu_custom_call" | custom-call | flops 200000000 | bytes 2097152 | tf_op jit(solution)/shard_map/suffix_away/pallas_call | solution.py:377
  12.9 2.3 %collective-permute-start.8 = (bf16[272,128]{1,0:T(8,128)(2,1)S(1)}, bf16[272,128]{1,0:T(8,128)(2,1)S(1)}, u32[]{:S(2)}, u32[]{:S(2)}) collective-permute-start(bf16[272,128]{1,0:T(8,128)(2,1)S(1)} %get-tuple-element.25), channel_id=1, source_target_pairs={{0,16},{1,17},{4,21},{5,20},{8,24},{9,25},{12,29},{13,28},{16,0},{... | collective-permute-start | bytes 208904 | tf_op jit(solution)/shard_map/ppermute | solution.py:36
  15.2 0.5 %suffix_away.4 = bf16[272,128]{1,0:T(8,128)(2,1)S(1)} custom-call(bf16[6,512,128]{2,1,0:T(8,128)(2,1)S(1)} %get-tuple-element.19.keys_ref, bf16[6,128,512]{2,1,0:T(8,128)(2,1)S(1)} %get-tuple-element.20.values_ref, f32[7,8,128]{2,1,0:T(8,128)S(1)} %get-tuple-element.21.refs_3_.member_ref, bf16[2,16,1024]{2,1,0:T(8,128)(2,1)S(1)} %collective-permute-done.5.message_ref, ...), custom_call_target="tpu_custom_call" | custom-call | flops 200000000 | bytes 2097152 | tf_op jit(solution)/shard_map/suffix_away/pallas_call | solution.py:377
  15.8 1.4 %collective-permute-start.6 = (bf16[272,128]{1,0:T(8,128)(2,1)S(1)}, bf16[272,128]{1,0:T(8,128)(2,1)S(1)}, u32[]{:S(2)}, u32[]{:S(2)}) collective-permute-start(bf16[272,128]{1,0:T(8,128)(2,1)S(1)} %suffix_away.4), channel_id=1, source_target_pairs={{0,24},{1,25},{4,29},{5,28},{8,16},{9,17},{12,21},{13,20},{16,8},{... | collective-permute-start | bytes 208904 | tf_op jit(solution)/shard_map/ppermute | solution.py:36
  17.2 0.5 %suffix_away.3 = bf16[272,128]{1,0:T(8,128)(2,1)S(1)} custom-call(bf16[6,512,128]{2,1,0:T(8,128)(2,1)S(1)} %get-tuple-element.19.keys_ref, bf16[6,128,512]{2,1,0:T(8,128)(2,1)S(1)} %get-tuple-element.20.values_ref, f32[7,8,128]{2,1,0:T(8,128)S(1)} %get-tuple-element.21.refs_3_.member_ref, bf16[2,16,1024]{2,1,0:T(8,128)(2,1)S(1)} %collective-permute-done.2.message_ref, ...), custom_call_target="tpu_custom_call" | custom-call | flops 200000000 | bytes 2097152 | tf_op jit(solution)/shard_map/suffix_away/pallas_call | solution.py:377
  17.7 0.2 collective-permute-start.4
  17.9 1.4 %collective-permute-start.9 = (bf16[144,128]{1,0:T(8,128)(2,1)S(1)}, bf16[144,128]{1,0:T(8,128)(2,1)S(1)}, u32[]{:S(2)}, u32[]{:S(2)}) collective-permute-start(bf16[144,128]{1,0:T(8,128)(2,1)S(1)} %home_pair_heads.1.after_ref), channel_id=1, source_target_pairs={{0,1},{1,0},{2,3},{3,2},{4,5},{5,4},{6,7},{7,6},{8,9},{9,8},{10,11... | collective-permute-start | bytes 110600 | tf_op jit(solution)/shard_map/ppermute | solution.py:26
  19.3 1.6 %home_own_heads.1 = (f32[128,128]{1,0:T(8,128)S(1)}, f32[8,128]{1,0:T(8,128)S(1)}) custom-call(s32[1]{0:T(128)S(6)} %copy.7.refs_0_, bf16[1,512,128]{2,1,0:T(8,128)(2,1)S(1)} %get-tuple-element.23.refs_1_, bf16[1,128,512]{2,1,0:T(8,128)(2,1)S(1)} %get-tuple-element.24.refs_2_, f32[7,8,128]{2,1,0:T(8,128)S(1)} %get-tuple-element.21.refs_3_.member_ref, ...), custom_call_target="tpu_custom_call" | custom-call | flops 335544320 | bytes 2097152 | tf_op jit(solution)/shard_map/home_own_heads/pallas_call | solution.py:390
  20.9 1.5 %collective-permute-done.6.rest_1_ = bf16[272,128]{1,0:T(8,128)(2,1)S(1)} collective-permute-done((bf16[272,128]{1,0:T(8,128)(2,1)S(1)}, bf16[272,128]{1,0:T(8,128)(2,1)S(1)}, u32[]{:S(2)}, u32[]{:S(2)}) %collective-permute-start.6) | collective-permute-done | bytes 69664 | tf_op jit(solution)/shard_map/ppermute | solution.py:36
  22.4 1.4 %collective-permute-done.4.rest_0_ = bf16[272,128]{1,0:T(8,128)(2,1)S(1)} collective-permute-done((bf16[272,128]{1,0:T(8,128)(2,1)S(1)}, bf16[272,128]{1,0:T(8,128)(2,1)S(1)}, u32[]{:S(2)}, u32[]{:S(2)}) %collective-permute-start.4) | collective-permute-done | bytes 69664 | tf_op jit(solution)/shard_map/ppermute | solution.py:36
  23.8 0.5 %collective-permute-start.10 = (bf16[144,128]{1,0:T(8,128)(2,1)S(1)}, bf16[144,128]{1,0:T(8,128)(2,1)S(1)}, u32[]{:S(2)}, u32[]{:S(2)}) collective-permute-start(bf16[144,128]{1,0:T(8,128)(2,1)S(1)} %sibling_share.1), channel_id=1, source_target_pairs={{0,4},{4,0},{1,5},{5,1},{2,6},{6,2},{3,7},{7,3},{8,12},{12,8},{9,1... | collective-permute-start | bytes 110600 | tf_op jit(solution)/shard_map/ppermute | solution.py:26
  24.4 0.9 %collective-permute-done.10.rest_4_ = bf16[144,128]{1,0:T(8,128)(2,1)S(1)} collective-permute-done((bf16[144,128]{1,0:T(8,128)(2,1)S(1)}, bf16[144,128]{1,0:T(8,128)(2,1)S(1)}, u32[]{:S(2)}, u32[]{:S(2)}) %collective-permute-start.10) | collective-permute-done | bytes 36896 | tf_op jit(solution)/shard_map/ppermute | solution.py:26
  25.2 0.8 %combine.1 = f32[16,1024]{1,0:T(8,128)} custom-call(bf16[272,128]{1,0:T(8,128)(2,1)S(1)} %collective-permute-done.4.rest_0_, bf16[272,128]{1,0:T(8,128)(2,1)S(1)} %collective-permute-done.6.rest_1_, bf16[272,128]{1,0:T(8,128)(2,1)S(1)} %collective-permute-done.8.rest_2_, bf16[144,128]{1,0:T(8,128)(2,1)S(1)} %collective-permute-done.9.rest_3_, ...), custom_call_target="tpu_custom_call" | custom-call | tf_op jit(solution)/shard_map/combine/pallas_call | solution.py:409
  (14 shorter events, 0.1 us)
Async XLA Ops:
  0.0 1.5 %collective-permute-start.1 = (bf16[16,1024]{1,0:T(8,128)(2,1)}, bf16[16,1024]{1,0:T(8,128)(2,1)S(1)}, u32[]{:S(2)}, u32[]{:S(2)}) collective-permute-start(bf16[16,1024]{1,0:T(8,128)(2,1)} %refs_0_.3), channel_id=1, source_target_pairs={{0,4},{4,0},{1,5},{5,1},{2,6},{6,2},{3,7},{7,3},{8,12},{12,8},{9,1... | collective-permute-start | bytes 98312 | tf_op jit(solution)/shard_map/ppermute | solution.py:26
  0.5 8.8 %collective-permute-start = (bf16[32,64,256]{2,1,0:T(8,128)(2,1)}, bf16[32,64,256]{2,1,0:T(8,128)(2,1)S(1)}, u32[]{:S(2)}, u32[]{:S(2)}) collective-permute-start(bf16[32,64,256]{2,1,0:T(8,128)(2,1)} %bitcast.6), channel_id=1, source_target_pairs={{0,4},{4,0},{1,5},{5,1},{2,6},{6,2},{3,7},{7,3},{8,12},{12,8},{9,1... | collective-permute-start | bytes 3145736 | tf_op jit(solution)/shard_map/ppermute | solution.py:26
  1.5 5.4 %copy-start.2 = (bf16[16,1024]{1,0:T(8,128)(2,1)S(1)}, bf16[16,1024]{1,0:T(8,128)(2,1)}, u32[]{:S(2)}) copy-start(bf16[16,1024]{1,0:T(8,128)(2,1)} %refs_0_.3) | copy-start | bytes 98308
  1.5 7.8 %copy-start.1 = (bf16[32,1,64,256]{3,2,1,0:T(8,128)(2,1)S(1)}, bf16[32,1,64,256]{3,2,1,0:T(8,128)(2,1)}, u32[]{:S(2)}) copy-start(bf16[32,1,64,256]{3,2,1,0:T(8,128)(2,1)} %param.8) | copy-start | bytes 3145732
  1.5 9.3 %copy-start = (bf16[1,1,4096,256]{3,2,1,0:T(8,128)(2,1)S(1)}, bf16[1,1,4096,256]{3,2,1,0:T(8,128)(2,1)}, u32[]{:S(2)}) copy-start(bf16[1,1,4096,256]{3,2,1,0:T(8,128)(2,1)} %param.7) | copy-start | bytes 6291460
  1.6 10.8 %collective-permute-start.7 = (bf16[2,16,1024]{2,1,0:T(8,128)(2,1)S(1)}, bf16[2,16,1024]{2,1,0:T(8,128)(2,1)S(1)}, u32[]{:S(2)}, u32[]{:S(2)}) collective-permute-start(bf16[2,16,1024]{2,1,0:T(8,128)(2,1)S(1)} %both_cores.1), channel_id=1, source_target_pairs={{0,16},{1,17},{4,21},{5,20},{8,24},{9,25},{12,29},{13,28},{16,0},{... | collective-permute-start | bytes 196616 | tf_op jit(solution)/shard_map/ppermute | solution.py:36
  5.6 9.7 %collective-permute-start.5 = (bf16[2,16,1024]{2,1,0:T(8,128)(2,1)S(1)}, bf16[2,16,1024]{2,1,0:T(8,128)(2,1)S(1)}, u32[]{:S(2)}, u32[]{:S(2)}) collective-permute-start(bf16[2,16,1024]{2,1,0:T(8,128)(2,1)S(1)} %both_cores.1), channel_id=1, source_target_pairs={{0,24},{1,25},{4,29},{5,28},{8,16},{9,17},{12,21},{13,20},{16,8},{... | collective-permute-start | bytes 196616 | tf_op jit(solution)/shard_map/ppermute | solution.py:36
  6.9 3.9 %collective-permute-start.3 = (bf16[16,1024]{1,0:T(8,128)(2,1)S(1)}, bf16[16,1024]{1,0:T(8,128)(2,1)S(1)}, u32[]{:S(2)}, u32[]{:S(2)}) collective-permute-start(bf16[16,1024]{1,0:T(8,128)(2,1)S(1)} %copy-done.2), channel_id=1, source_target_pairs={{0,1},{1,0},{2,3},{3,2},{4,5},{5,4},{6,7},{7,6},{8,9},{9,8},{10,11... | collective-permute-start | bytes 98312 | tf_op jit(solution)/shard_map/ppermute | solution.py:26
  8.4 8.8 %collective-permute-start.2 = (bf16[2,16,1024]{2,1,0:T(8,128)(2,1)S(1)}, bf16[2,16,1024]{2,1,0:T(8,128)(2,1)S(1)}, u32[]{:S(2)}, u32[]{:S(2)}) collective-permute-start(bf16[2,16,1024]{2,1,0:T(8,128)(2,1)S(1)} %both_cores.1), channel_id=1, source_target_pairs={{0,8},{1,9},{4,13},{5,12},{8,0},{9,1},{12,5},{13,4},{16,24},{17,25... | collective-permute-start | bytes 196616 | tf_op jit(solution)/shard_map/ppermute | solution.py:36
  12.9 8.0 %collective-permute-start.8 = (bf16[272,128]{1,0:T(8,128)(2,1)S(1)}, bf16[272,128]{1,0:T(8,128)(2,1)S(1)}, u32[]{:S(2)}, u32[]{:S(2)}) collective-permute-start(bf16[272,128]{1,0:T(8,128)(2,1)S(1)} %get-tuple-element.25), channel_id=1, source_target_pairs={{0,16},{1,17},{4,21},{5,20},{8,24},{9,25},{12,29},{13,28},{16,0},{... | collective-permute-start | bytes 208904 | tf_op jit(solution)/shard_map/ppermute | solution.py:36
  15.8 6.7 %collective-permute-start.6 = (bf16[272,128]{1,0:T(8,128)(2,1)S(1)}, bf16[272,128]{1,0:T(8,128)(2,1)S(1)}, u32[]{:S(2)}, u32[]{:S(2)}) collective-permute-start(bf16[272,128]{1,0:T(8,128)(2,1)S(1)} %suffix_away.4), channel_id=1, source_target_pairs={{0,24},{1,25},{4,29},{5,28},{8,16},{9,17},{12,21},{13,20},{16,8},{... | collective-permute-start | bytes 208904 | tf_op jit(solution)/shard_map/ppermute | solution.py:36
  17.7 6.1 %collective-permute-start.4 = (bf16[272,128]{1,0:T(8,128)(2,1)S(1)}, bf16[272,128]{1,0:T(8,128)(2,1)S(1)}, u32[]{:S(2)}, u32[]{:S(2)}) collective-permute-start(bf16[272,128]{1,0:T(8,128)(2,1)S(1)} %suffix_away.3), channel_id=1, source_target_pairs={{0,8},{1,9},{4,13},{5,12},{8,0},{9,1},{12,5},{13,4},{16,24},{17,25... | collective-permute-start | bytes 208904 | tf_op jit(solution)/shard_map/ppermute | solution.py:36
  17.9 6.5 %collective-permute-start.9 = (bf16[144,128]{1,0:T(8,128)(2,1)S(1)}, bf16[144,128]{1,0:T(8,128)(2,1)S(1)}, u32[]{:S(2)}, u32[]{:S(2)}) collective-permute-start(bf16[144,128]{1,0:T(8,128)(2,1)S(1)} %home_pair_heads.1.after_ref), channel_id=1, source_target_pairs={{0,1},{1,0},{2,3},{3,2},{4,5},{5,4},{6,7},{7,6},{8,9},{9,8},{10,11... | collective-permute-start | bytes 110600 | tf_op jit(solution)/shard_map/ppermute | solution.py:26
  23.8 1.4 %collective-permute-start.10 = (bf16[144,128]{1,0:T(8,128)(2,1)S(1)}, bf16[144,128]{1,0:T(8,128)(2,1)S(1)}, u32[]{:S(2)}, u32[]{:S(2)}) collective-permute-start(bf16[144,128]{1,0:T(8,128)(2,1)S(1)} %sibling_share.1), channel_id=1, source_target_pairs={{0,4},{4,0},{1,5},{5,1},{2,6},{6,2},{3,7},{7,3},{8,12},{12,8},{9,1... | collective-permute-start | bytes 110600 | tf_op jit(solution)/shard_map/ppermute | solution.py:26

commit v26 on v24

--- a/solution.py
+++ b/solution.py
@@ -271,7 +271,7 @@
 
 
 def sibling_kernel(*rest):
-    units, out_ref = rest[:-2], rest[-1]
+    units, out_ref = rest[:-1], rest[-1]
     core = lax.axis_index("core")
     store_units(out_ref, [merged([load_unit(unit, 1 - core) for unit in units])])
 
@@ -372,7 +372,7 @@
         after += token
 
     home = pl.CostEstimate(
-        flops=5 * tokens * VECS * HD, bytes_accessed=2 * tokens * width, transcendentals=0
+        flops=12 * tokens * VECS * HD, bytes_accessed=2 * tokens * width, transcendentals=0
     )
     home_specs = [pl.BlockSpec(memory_space=pltpu.SMEM)] + [vmem] * 6
     prompt = prompt_cache.reshape(tokens, width)
@@ -399,11 +399,11 @@
     share = pl.pallas_call(
         sibling_kernel,
         out_shape=pltpu.VMEM((HD + STAT_ROWS, VECS), jnp.bfloat16),
-        in_specs=[vmem] * n_req,
+        in_specs=[vmem] * (n_req - 1),
         out_specs=vmem,
         compiler_params=params,
         name="sibling_share",
-    )(*received, stats)
+    )(*received)
 
     return pl.pallas_call(
         final_kernel,

time: 24.8 us -> 25.1 us (1.012)
  waiting for transfers between devices: 1.14 us -> 2.52 us
  starting transfers between devices: 15.5 us -> 14.5 us
    ppermute x6, waiting for transfers between devices: 0.02 us -> 2.3 us  [exchanged(): return lax.ppermute(value, ('z', 'core', 'pair'), pairs)]
    ppermute x5, waiting for transfers between devices: 1.12 us -> 0.23 us  [swapped(): return lax.ppermute(value, axis, [(0, 1), (1, 0)])]
    ppermute x6, starting transfers between devices: 12 us -> 11.3 us  [exchanged(): return lax.ppermute(value, ('z', 'core', 'pair'), pairs)]
    ppermute x5, starting transfers between devices: 3.47 us -> 3.17 us  [swapped(): return lax.ppermute(value, axis, [(0, 1), (1, 0)])]
  transfers between devices with their start and end apart: 11 -> 11, of which waited for: 2 -> 3; matrix products, arithmetic and copies ran while one was open for 0% -> 0% of each run, Pallas kernels for 26% -> 26%
where the time goes in v26:
time: 25.1 us; the launch traced here: 24.9 us
  starting transfers between devices  14.5 us (58%)
  Pallas kernels  7.14 us (28%)
  waiting for transfers between devices  2.52 us (10%)
  between operations  0.76 us (3%)
    ppermute x6, starting transfers between devices, exchanged(): return lax.ppermute(value, ('z', 'core', 'pair'), pairs)  11.3 us
    ppermute x5, starting transfers between devices, swapped(): return lax.ppermute(value, axis, [(0, 1), (1, 0)])  3.17 us
    ppermute x6, waiting for transfers between devices, exchanged(): return lax.ppermute(value, ('z', 'core', 'pair'), pairs)  2.3 us
    pallas_call x1, Pallas kernels, on_device(): pl.pallas_call(pair_heads_kernel, out_shape=pltpu.VMEM((HD + STAT_ROWS, V...  1.54 us
    pallas_call x1, Pallas kernels, on_device(): pl.pallas_call(own_heads_kernel, out_shape=(pltpu.VMEM((HD, VECS), jnp.fl...  1.52 us
    pallas_call x3, Pallas kernels, on_device(): pl.pallas_call(functools.partial(away_kernel, 2 * mask - 2), out_shape=ou...  1.52 us
    pallas_call x1, Pallas kernels, on_device(): pl.pallas_call(functools.partial(prepare_kernel, capacity), out_shape=(pl...  0.94 us
    pallas_call x1, Pallas kernels, on_device(): pl.pallas_call(stage_kernel, out_shape=tuple((pltpu.VMEM(each.shape, each...  0.79 us
  transfers between devices with their start and end apart: 11, of which 3 were waited for; matrix products, arithmetic and copies ran while one was open for 0% of the time, Pallas kernels for 26%

profile of v26, /device:TPU:0, one launch (start us, length us, event | category | flops | bytes accessed | tf_op | source)
XLA Modules:
  0.0 24.9 jit_solution(8574248668140569140)
XLA Ops:
  0.0 0.5 %collective-permute-start.1 = (bf16[16,1024]{1,0:T(8,128)(2,1)}, bf16[16,1024]{1,0:T(8,128)(2,1)S(1)}, u32[]{:S(2)}, u32[]{:S(2)}) collective-permute-start(bf16[16,1024]{1,0:T(8,128)(2,1)} %refs_0_.3), channel_id=1, source_target_pairs={{0,4},{4,0},{1,5},{5,1},{2,6},{6,2},{3,7},{7,3},{8,12},{12,8},{9,1... | collective-permute-start | bytes 98312 | tf_op jit(solution)/shard_map/ppermute | solution.py:26
  0.5 0.1 collective-permute-start
  0.5 0.8 %stage.1 = (bf16[16,1024]{1,0:T(8,128)(2,1)S(1)}, s32[4,128]{1,0:T(4,128)S(1)}, s32[1,128]{1,0:T(1,128)S(1)}) custom-call(bf16[16,1024]{1,0:T(8,128)(2,1)} %refs_0_.3, s32[4,128]{1,0:T(4,128)} %bitcast.8, s32[1,128]{1,0:T(1,128)} %bitcast.9), custom_call_target="tpu_custom_call" | custom-call | tf_op jit(solution)/shard_map/stage/pallas_call | solution.py:313
  1.3 0.2 collective-permute-done.1.sibling_ref
  1.5 4.0 %collective-permute-start.2 = (bf16[2,16,1024]{2,1,0:T(8,128)(2,1)S(1)}, bf16[2,16,1024]{2,1,0:T(8,128)(2,1)S(1)}, u32[]{:S(2)}, u32[]{:S(2)}) collective-permute-start(bf16[2,16,1024]{2,1,0:T(8,128)(2,1)S(1)} %both_cores.1), channel_id=1, source_target_pairs={{0,16},{1,17},{4,21},{5,20},{8,24},{9,25},{12,29},{13,28},{16,0},{... | collective-permute-start | bytes 196616 | tf_op jit(solution)/shard_map/ppermute | solution.py:36
  5.5 1.3 %collective-permute-start.6 = (bf16[2,16,1024]{2,1,0:T(8,128)(2,1)S(1)}, bf16[2,16,1024]{2,1,0:T(8,128)(2,1)S(1)}, u32[]{:S(2)}, u32[]{:S(2)}) collective-permute-start(bf16[2,16,1024]{2,1,0:T(8,128)(2,1)S(1)} %both_cores.1), channel_id=1, source_target_pairs={{0,24},{1,25},{4,29},{5,28},{8,16},{9,17},{12,21},{13,20},{16,8},{... | collective-permute-start | bytes 196616 | tf_op jit(solution)/shard_map/ppermute | solution.py:36
  6.9 0.2 collective-permute-start.4
  7.1 1.5 %collective-permute-start.8 = (bf16[16,1024]{1,0:T(8,128)(2,1)S(1)}, bf16[16,1024]{1,0:T(8,128)(2,1)S(1)}, u32[]{:S(2)}, u32[]{:S(2)}) collective-permute-start(bf16[16,1024]{1,0:T(8,128)(2,1)S(1)} %copy-done.2), channel_id=1, source_target_pairs={{0,1},{1,0},{2,3},{3,2},{4,5},{5,4},{6,7},{7,6},{8,9},{9,8},{10,11... | collective-permute-start | bytes 98312 | tf_op jit(solution)/shard_map/ppermute | solution.py:26
  9.3 0.0 collective-permute-done.far_ref
  9.3 0.9 %prepare.1 = (bf16[1,512,128]{2,1,0:T(8,128)(2,1)S(1)}, bf16[1,128,512]{2,1,0:T(8,128)(2,1)S(1)}, bf16[6,512,128]{2,1,0:T(8,128)(2,1)S(1)}, bf16[6,128,512]{2,1,0:T(8,128)(2,1)S(1)}, f32[7,8,128]{2,1,0:T(8,128)S(1)}) custom-call(bf16[32,64,256]{2,1,0:T(8,128)(2,1)S(1)} %bitcast.5, s32[4,128]{1,0:T(4,128)S(1)} %get-tuple-element.17.table, ...), custom_call_target="tpu_custom_call" | custom-call | flops 200000000 | bytes 2097152 | tf_op jit(solution)/shard_map/prepare/pallas_call | solution.py:335
  10.2 0.5 %suffix_away.3 = (bf16[272,128]{1,0:T(8,128)(2,1)S(1)}, f32[8,128]{1,0:T(8,128)S(1)}) custom-call(bf16[6,512,128]{2,1,0:T(8,128)(2,1)S(1)} %get-tuple-element.19.keys_ref, bf16[6,128,512]{2,1,0:T(8,128)(2,1)S(1)} %get-tuple-element.20.values_ref, f32[7,8,128]{2,1,0:T(8,128)S(1)} %get-tuple-element.21.member_ref.refs_3_, ...), custom_call_target="tpu_custom_call" | custom-call | flops 200000000 | bytes 2097152 | tf_op jit(solution)/shard_map/suffix_away/pallas_call | solution.py:362
  10.8 0.0 copy-start.1
  10.8 2.9 %collective-permute-start.3 = (bf16[272,128]{1,0:T(8,128)(2,1)S(1)}, bf16[272,128]{1,0:T(8,128)(2,1)S(1)}, u32[]{:S(2)}, u32[]{:S(2)}) collective-permute-start(bf16[272,128]{1,0:T(8,128)(2,1)S(1)} %get-tuple-element.23), channel_id=1, source_target_pairs={{0,16},{1,17},{4,21},{5,20},{8,24},{9,25},{12,29},{13,28},{16,0},{... | collective-permute-start | bytes 208904 | tf_op jit(solution)/shard_map/ppermute | solution.py:36
  13.6 0.5 %suffix_away.5 = bf16[272,128]{1,0:T(8,128)(2,1)S(1)} custom-call(bf16[6,512,128]{2,1,0:T(8,128)(2,1)S(1)} %get-tuple-element.19.keys_ref, bf16[6,128,512]{2,1,0:T(8,128)(2,1)S(1)} %get-tuple-element.20.values_ref, f32[7,8,128]{2,1,0:T(8,128)S(1)} %get-tuple-element.21.member_ref.refs_3_, bf16[2,16,1024]{2,1,0:T(8,128)(2,1)S(1)} %collective-permute-done.6.message_ref), custom_call_target="tpu_custom_call" | custom-call | flops 200000000 | bytes 2097152 | tf_op jit(solution)/shard_map/suffix_away/pallas_call | solution.py:362
  14.2 2.2 %collective-permute-start.7 = (bf16[272,128]{1,0:T(8,128)(2,1)S(1)}, bf16[272,128]{1,0:T(8,128)(2,1)S(1)}, u32[]{:S(2)}, u32[]{:S(2)}) collective-permute-start(bf16[272,128]{1,0:T(8,128)(2,1)S(1)} %suffix_away.5), channel_id=1, source_target_pairs={{0,24},{1,25},{4,29},{5,28},{8,16},{9,17},{12,21},{13,20},{16,8},{... | collective-permute-start | bytes 208904 | tf_op jit(solution)/shard_map/ppermute | solution.py:36
  16.4 0.5 %suffix_away.4 = bf16[272,128]{1,0:T(8,128)(2,1)S(1)} custom-call(bf16[6,512,128]{2,1,0:T(8,128)(2,1)S(1)} %get-tuple-element.19.keys_ref, bf16[6,128,512]{2,1,0:T(8,128)(2,1)S(1)} %get-tuple-element.20.values_ref, f32[7,8,128]{2,1,0:T(8,128)S(1)} %get-tuple-element.21.member_ref.refs_3_, bf16[2,16,1024]{2,1,0:T(8,128)(2,1)S(1)} %collective-permute-done.4.message_ref), custom_call_target="tpu_custom_call" | custom-call | flops 200000000 | bytes 2097152 | tf_op jit(solution)/shard_map/suffix_away/pallas_call | solution.py:362
  16.9 0.6 %collective-permute-start.5 = (bf16[272,128]{1,0:T(8,128)(2,1)S(1)}, bf16[272,128]{1,0:T(8,128)(2,1)S(1)}, u32[]{:S(2)}, u32[]{:S(2)}) collective-permute-start(bf16[272,128]{1,0:T(8,128)(2,1)S(1)} %suffix_away.4), channel_id=1, source_target_pairs={{0,8},{1,9},{4,13},{5,12},{8,0},{9,1},{12,5},{13,4},{16,24},{17,25... | collective-permute-start | bytes 208904 | tf_op jit(solution)/shard_map/ppermute | solution.py:36
  17.5 1.5 %home_pair_heads.1 = bf16[144,128]{1,0:T(8,128)(2,1)S(1)} custom-call(s32[1]{0:T(128)S(6)} %copy.7.refs_0_, bf16[1,512,128]{2,1,0:T(8,128)(2,1)S(1)} %get-tuple-element.24.refs_1_, bf16[1,128,512]{2,1,0:T(8,128)(2,1)S(1)} %get-tuple-element.25.refs_2_, f32[7,8,128]{2,1,0:T(8,128)S(1)} %get-tuple-element.21.member_ref.refs_3_, ...), custom_call_target="tpu_custom_call" | custom-call | flops 805306368 | bytes 2097152 | tf_op jit(solution)/shard_map/home_pair_heads/pallas_call | solution.py:379
  19.1 0.8 %collective-permute-start.9 = (bf16[144,128]{1,0:T(8,128)(2,1)S(1)}, bf16[144,128]{1,0:T(8,128)(2,1)S(1)}, u32[]{:S(2)}, u32[]{:S(2)}) collective-permute-start(bf16[144,128]{1,0:T(8,128)(2,1)S(1)} %home_pair_heads.1), channel_id=1, source_target_pairs={{0,1},{1,0},{2,3},{3,2},{4,5},{5,4},{6,7},{7,6},{8,9},{9,8},{10,11... | collective-permute-start | bytes 110600 | tf_op jit(solution)/shard_map/ppermute | solution.py:26
  19.9 0.9 %collective-permute-done.7.rest_2_ = bf16[272,128]{1,0:T(8,128)(2,1)S(1)} collective-permute-done((bf16[272,128]{1,0:T(8,128)(2,1)S(1)}, bf16[272,128]{1,0:T(8,128)(2,1)S(1)}, u32[]{:S(2)}, u32[]{:S(2)}) %collective-permute-start.7) | collective-permute-done | bytes 69664 | tf_op jit(solution)/shard_map/ppermute | solution.py:36
  20.8 1.4 %collective-permute-done.5.rest_1_ = bf16[272,128]{1,0:T(8,128)(2,1)S(1)} collective-permute-done((bf16[272,128]{1,0:T(8,128)(2,1)S(1)}, bf16[272,128]{1,0:T(8,128)(2,1)S(1)}, u32[]{:S(2)}, u32[]{:S(2)}) %collective-permute-start.5) | collective-permute-done | bytes 69664 | tf_op jit(solution)/shard_map/ppermute | solution.py:36
  22.2 0.4 %collective-permute-start.10 = (bf16[144,128]{1,0:T(8,128)(2,1)S(1)}, bf16[144,128]{1,0:T(8,128)(2,1)S(1)}, u32[]{:S(2)}, u32[]{:S(2)}) collective-permute-start(bf16[144,128]{1,0:T(8,128)(2,1)S(1)} %sibling_share.1), channel_id=1, source_target_pairs={{0,4},{4,0},{1,5},{5,1},{2,6},{6,2},{3,7},{7,3},{8,12},{12,8},{9,1... | collective-permute-start | bytes 110600 | tf_op jit(solution)/shard_map/ppermute | solution.py:26
  22.6 1.5 %home_own_heads.1 = (f32[128,128]{1,0:T(8,128)S(1)}, f32[8,128]{1,0:T(8,128)S(1)}) custom-call(s32[1]{0:T(128)S(6)} %copy.7.refs_0_, bf16[1,512,128]{2,1,0:T(8,128)(2,1)S(1)} %get-tuple-element.24.refs_1_, bf16[1,128,512]{2,1,0:T(8,128)(2,1)S(1)} %get-tuple-element.25.refs_2_, f32[7,8,128]{2,1,0:T(8,128)S(1)} %get-tuple-element.21.member_ref.refs_3_, ...), custom_call_target="tpu_custom_call" | custom-call | flops 805306368 | bytes 2097152 | tf_op jit(solution)/shard_map/home_own_heads/pallas_call | solution.py:389
  24.2 0.8 %combine.1 = f32[16,1024]{1,0:T(8,128)} custom-call(bf16[272,128]{1,0:T(8,128)(2,1)S(1)} %collective-permute-done.3.rest_0_, bf16[272,128]{1,0:T(8,128)(2,1)S(1)} %collective-permute-done.5.rest_1_, bf16[272,128]{1,0:T(8,128)(2,1)S(1)} %collective-permute-done.7.rest_2_, bf16[144,128]{1,0:T(8,128)(2,1)S(1)} %collective-permute-done.9.rest_3_, ...), custom_call_target="tpu_custom_call" | custom-call | tf_op jit(solution)/shard_map/combine/pallas_call | solution.py:408
  (14 shorter events, 0.1 us)
Async XLA Ops:
  0.0 1.5 %collective-permute-start.1 = (bf16[16,1024]{1,0:T(8,128)(2,1)}, bf16[16,1024]{1,0:T(8,128)(2,1)S(1)}, u32[]{:S(2)}, u32[]{:S(2)}) collective-permute-start(bf16[16,1024]{1,0:T(8,128)(2,1)} %refs_0_.3), channel_id=1, source_target_pairs={{0,4},{4,0},{1,5},{5,1},{2,6},{6,2},{3,7},{7,3},{8,12},{12,8},{9,1... | collective-permute-start | bytes 98312 | tf_op jit(solution)/shard_map/ppermute | solution.py:26
  0.5 8.8 %collective-permute-start = (bf16[32,64,256]{2,1,0:T(8,128)(2,1)}, bf16[32,64,256]{2,1,0:T(8,128)(2,1)S(1)}, u32[]{:S(2)}, u32[]{:S(2)}) collective-permute-start(bf16[32,64,256]{2,1,0:T(8,128)(2,1)} %bitcast.4), channel_id=1, source_target_pairs={{0,4},{4,0},{1,5},{5,1},{2,6},{6,2},{3,7},{7,3},{8,12},{12,8},{9,1... | collective-permute-start | bytes 3145736 | tf_op jit(solution)/shard_map/ppermute | solution.py:26
  1.5 5.6 %copy-start.2 = (bf16[16,1024]{1,0:T(8,128)(2,1)S(1)}, bf16[16,1024]{1,0:T(8,128)(2,1)}, u32[]{:S(2)}) copy-start(bf16[16,1024]{1,0:T(8,128)(2,1)} %refs_0_.3) | copy-start | bytes 98308
  1.5 7.8 %copy-start = (bf16[32,1,64,256]{3,2,1,0:T(8,128)(2,1)S(1)}, bf16[32,1,64,256]{3,2,1,0:T(8,128)(2,1)}, u32[]{:S(2)}) copy-start(bf16[32,1,64,256]{3,2,1,0:T(8,128)(2,1)} %param.8) | copy-start | bytes 3145732
  1.5 8.7 %collective-permute-start.2 = (bf16[2,16,1024]{2,1,0:T(8,128)(2,1)S(1)}, bf16[2,16,1024]{2,1,0:T(8,128)(2,1)S(1)}, u32[]{:S(2)}, u32[]{:S(2)}) collective-permute-start(bf16[2,16,1024]{2,1,0:T(8,128)(2,1)S(1)} %both_cores.1), channel_id=1, source_target_pairs={{0,16},{1,17},{4,21},{5,20},{8,24},{9,25},{12,29},{13,28},{16,0},{... | collective-permute-start | bytes 196616 | tf_op jit(solution)/shard_map/ppermute | solution.py:36
  5.5 8.1 %collective-permute-start.6 = (bf16[2,16,1024]{2,1,0:T(8,128)(2,1)S(1)}, bf16[2,16,1024]{2,1,0:T(8,128)(2,1)S(1)}, u32[]{:S(2)}, u32[]{:S(2)}) collective-permute-start(bf16[2,16,1024]{2,1,0:T(8,128)(2,1)S(1)} %both_cores.1), channel_id=1, source_target_pairs={{0,24},{1,25},{4,29},{5,28},{8,16},{9,17},{12,21},{13,20},{16,8},{... | collective-permute-start | bytes 196616 | tf_op jit(solution)/shard_map/ppermute | solution.py:36
  6.9 9.5 %collective-permute-start.4 = (bf16[2,16,1024]{2,1,0:T(8,128)(2,1)S(1)}, bf16[2,16,1024]{2,1,0:T(8,128)(2,1)S(1)}, u32[]{:S(2)}, u32[]{:S(2)}) collective-permute-start(bf16[2,16,1024]{2,1,0:T(8,128)(2,1)S(1)} %both_cores.1), channel_id=1, source_target_pairs={{0,8},{1,9},{4,13},{5,12},{8,0},{9,1},{12,5},{13,4},{16,24},{17,25... | collective-permute-start | bytes 196616 | tf_op jit(solution)/shard_map/ppermute | solution.py:36
  7.1 10.4 %collective-permute-start.8 = (bf16[16,1024]{1,0:T(8,128)(2,1)S(1)}, bf16[16,1024]{1,0:T(8,128)(2,1)S(1)}, u32[]{:S(2)}, u32[]{:S(2)}) collective-permute-start(bf16[16,1024]{1,0:T(8,128)(2,1)S(1)} %copy-done.2), channel_id=1, source_target_pairs={{0,1},{1,0},{2,3},{3,2},{4,5},{5,4},{6,7},{7,6},{8,9},{9,8},{10,11... | collective-permute-start | bytes 98312 | tf_op jit(solution)/shard_map/ppermute | solution.py:26
  10.8 6.8 %copy-start.1 = (bf16[1,1,4096,256]{3,2,1,0:T(8,128)(2,1)S(1)}, bf16[1,1,4096,256]{3,2,1,0:T(8,128)(2,1)}, u32[]{:S(2)}) copy-start(bf16[1,1,4096,256]{3,2,1,0:T(8,128)(2,1)} %param.7) | copy-start | bytes 6291460
  10.8 9.1 %collective-permute-start.3 = (bf16[272,128]{1,0:T(8,128)(2,1)S(1)}, bf16[272,128]{1,0:T(8,128)(2,1)S(1)}, u32[]{:S(2)}, u32[]{:S(2)}) collective-permute-start(bf16[272,128]{1,0:T(8,128)(2,1)S(1)} %get-tuple-element.23), channel_id=1, source_target_pairs={{0,16},{1,17},{4,21},{5,20},{8,24},{9,25},{12,29},{13,28},{16,0},{... | collective-permute-start | bytes 208904 | tf_op jit(solution)/shard_map/ppermute | solution.py:36
  14.2 6.6 %collective-permute-start.7 = (bf16[272,128]{1,0:T(8,128)(2,1)S(1)}, bf16[272,128]{1,0:T(8,128)(2,1)S(1)}, u32[]{:S(2)}, u32[]{:S(2)}) collective-permute-start(bf16[272,128]{1,0:T(8,128)(2,1)S(1)} %suffix_away.5), channel_id=1, source_target_pairs={{0,24},{1,25},{4,29},{5,28},{8,16},{9,17},{12,21},{13,20},{16,8},{... | collective-permute-start | bytes 208904 | tf_op jit(solution)/shard_map/ppermute | solution.py:36
  16.9 5.3 %collective-permute-start.5 = (bf16[272,128]{1,0:T(8,128)(2,1)S(1)}, bf16[272,128]{1,0:T(8,128)(2,1)S(1)}, u32[]{:S(2)}, u32[]{:S(2)}) collective-permute-start(bf16[272,128]{1,0:T(8,128)(2,1)S(1)} %suffix_away.4), channel_id=1, source_target_pairs={{0,8},{1,9},{4,13},{5,12},{8,0},{9,1},{12,5},{13,4},{16,24},{17,25... | collective-permute-start | bytes 208904 | tf_op jit(solution)/shard_map/ppermute | solution.py:36
  19.1 5.0 %collective-permute-start.9 = (bf16[144,128]{1,0:T(8,128)(2,1)S(1)}, bf16[144,128]{1,0:T(8,128)(2,1)S(1)}, u32[]{:S(2)}, u32[]{:S(2)}) collective-permute-start(bf16[144,128]{1,0:T(8,128)(2,1)S(1)} %home_pair_heads.1), channel_id=1, source_target_pairs={{0,1},{1,0},{2,3},{3,2},{4,5},{5,4},{6,7},{7,6},{8,9},{9,8},{10,11... | collective-permute-start | bytes 110600 | tf_op jit(solution)/shard_map/ppermute | solution.py:26
  22.2 1.9 %collective-permute-start.10 = (bf16[144,128]{1,0:T(8,128)(2,1)S(1)}, bf16[144,128]{1,0:T(8,128)(2,1)S(1)}, u32[]{:S(2)}, u32[]{:S(2)}) collective-permute-start(bf16[144,128]{1,0:T(8,128)(2,1)S(1)} %sibling_share.1), channel_id=1, source_target_pairs={{0,4},{4,0},{1,5},{5,1},{2,6},{6,2},{3,7},{7,3},{8,12},{12,8},{9,1... | collective-permute-start | bytes 110600 | tf_op jit(solution)/shard_map/ppermute | solution.py:26

commit v27 on v24

--- a/solution.py
+++ b/solution.py
@@ -372,7 +372,7 @@
         after += token
 
     home = pl.CostEstimate(
-        flops=5 * tokens * VECS * HD, bytes_accessed=2 * tokens * width, transcendentals=0
+        flops=8 * tokens * VECS * HD, bytes_accessed=2 * tokens * width, transcendentals=0
     )
     home_specs = [pl.BlockSpec(memory_space=pltpu.SMEM)] + [vmem] * 6
     prompt = prompt_cache.reshape(tokens, width)

time: 24.8 us -> 24.5 us (0.988)
  starting transfers between devices: 15.5 us -> 14.5 us
  waiting for transfers between devices: 1.14 us -> 1.84 us
    ppermute x6, waiting for transfers between devices: 0.02 us -> 0.69 us  [exchanged(): return lax.ppermute(value, ('z', 'core', 'pair'), pairs)]
    ppermute x6, starting transfers between devices: 12 us -> 11.3 us  [exchanged(): return lax.ppermute(value, ('z', 'core', 'pair'), pairs)]
    ppermute x5, starting transfers between devices: 3.47 us -> 3.14 us  [swapped(): return lax.ppermute(value, axis, [(0, 1), (1, 0)])]
  transfers between devices with their start and end apart: 11 -> 11, of which waited for: 2 -> 4; matrix products, arithmetic and copies ran while one was open for 0% -> 0% of each run, Pallas kernels for 26% -> 26%
where the time goes in v27:
time: 24.5 us; the launch traced here: 24.3 us
  starting transfers between devices  14.5 us (59%)
  Pallas kernels  7.21 us (29%)
  waiting for transfers between devices  1.84 us (8%)
  between operations  0.76 us (3%)
    ppermute x6, starting transfers between devices, exchanged(): return lax.ppermute(value, ('z', 'core', 'pair'), pairs)  11.3 us
    ppermute x5, starting transfers between devices, swapped(): return lax.ppermute(value, axis, [(0, 1), (1, 0)])  3.14 us
    pallas_call x1, Pallas kernels, on_device(): pl.pallas_call(pair_heads_kernel, out_shape=pltpu.VMEM((HD + STAT_ROWS, V...  1.57 us
    pallas_call x1, Pallas kernels, on_device(): pl.pallas_call(own_heads_kernel, out_shape=(pltpu.VMEM((HD, VECS), jnp.fl...  1.56 us
    pallas_call x3, Pallas kernels, on_device(): pl.pallas_call(functools.partial(away_kernel, 2 * mask - 2), out_shape=ou...  1.53 us
    ppermute x5, waiting for transfers between devices, swapped(): return lax.ppermute(value, axis, [(0, 1), (1, 0)])  1.15 us
    pallas_call x1, Pallas kernels, on_device(): pl.pallas_call(functools.partial(prepare_kernel, capacity), out_shape=(pl...  0.94 us
    pallas_call x1, Pallas kernels, on_device(): pl.pallas_call(stage_kernel, out_shape=tuple((pltpu.VMEM(each.shape, each...  0.79 us
  transfers between devices with their start and end apart: 11, of which 4 were waited for; matrix products, arithmetic and copies ran while one was open for 0% of the time, Pallas kernels for 26%

profile of v27, /device:TPU:0, one launch (start us, length us, event | category | flops | bytes accessed | tf_op | source)
XLA Modules:
  0.0 24.3 jit_solution(8311529798699385607)
XLA Ops:
  0.0 0.5 %collective-permute-start.1 = (bf16[16,1024]{1,0:T(8,128)(2,1)}, bf16[16,1024]{1,0:T(8,128)(2,1)S(1)}, u32[]{:S(2)}, u32[]{:S(2)}) collective-permute-start(bf16[16,1024]{1,0:T(8,128)(2,1)} %refs_0_.3), channel_id=1, source_target_pairs={{0,4},{4,0},{1,5},{5,1},{2,6},{6,2},{3,7},{7,3},{8,12},{12,8},{9,1... | collective-permute-start | bytes 98312 | tf_op jit(solution)/shard_map/ppermute | solution.py:26
  0.5 0.1 collective-permute-start
  0.5 0.8 %stage.1 = (bf16[16,1024]{1,0:T(8,128)(2,1)S(1)}, s32[4,128]{1,0:T(4,128)S(1)}, s32[1,128]{1,0:T(1,128)S(1)}) custom-call(bf16[16,1024]{1,0:T(8,128)(2,1)} %refs_0_.3, s32[4,128]{1,0:T(4,128)} %bitcast.8, s32[1,128]{1,0:T(1,128)} %bitcast.9), custom_call_target="tpu_custom_call" | custom-call | tf_op jit(solution)/shard_map/stage/pallas_call | solution.py:313
  1.3 0.2 collective-permute-done.1.sibling_ref
  1.5 4.0 %collective-permute-start.2 = (bf16[2,16,1024]{2,1,0:T(8,128)(2,1)S(1)}, bf16[2,16,1024]{2,1,0:T(8,128)(2,1)S(1)}, u32[]{:S(2)}, u32[]{:S(2)}) collective-permute-start(bf16[2,16,1024]{2,1,0:T(8,128)(2,1)S(1)} %both_cores.1), channel_id=1, source_target_pairs={{0,16},{1,17},{4,21},{5,20},{8,24},{9,25},{12,29},{13,28},{16,0},{... | collective-permute-start | bytes 196616 | tf_op jit(solution)/shard_map/ppermute | solution.py:36
  5.5 1.3 %collective-permute-start.6 = (bf16[2,16,1024]{2,1,0:T(8,128)(2,1)S(1)}, bf16[2,16,1024]{2,1,0:T(8,128)(2,1)S(1)}, u32[]{:S(2)}, u32[]{:S(2)}) collective-permute-start(bf16[2,16,1024]{2,1,0:T(8,128)(2,1)S(1)} %both_cores.1), channel_id=1, source_target_pairs={{0,24},{1,25},{4,29},{5,28},{8,16},{9,17},{12,21},{13,20},{16,8},{... | collective-permute-start | bytes 196616 | tf_op jit(solution)/shard_map/ppermute | solution.py:36
  6.9 0.2 collective-permute-start.4
  7.1 1.5 %collective-permute-start.8 = (bf16[16,1024]{1,0:T(8,128)(2,1)S(1)}, bf16[16,1024]{1,0:T(8,128)(2,1)S(1)}, u32[]{:S(2)}, u32[]{:S(2)}) collective-permute-start(bf16[16,1024]{1,0:T(8,128)(2,1)S(1)} %copy-done.2), channel_id=1, source_target_pairs={{0,1},{1,0},{2,3},{3,2},{4,5},{5,4},{6,7},{7,6},{8,9},{9,8},{10,11... | collective-permute-start | bytes 98312 | tf_op jit(solution)/shard_map/ppermute | solution.py:26
  9.3 0.9 %prepare.1 = (bf16[1,512,128]{2,1,0:T(8,128)(2,1)S(1)}, bf16[1,128,512]{2,1,0:T(8,128)(2,1)S(1)}, bf16[6,512,128]{2,1,0:T(8,128)(2,1)S(1)}, bf16[6,128,512]{2,1,0:T(8,128)(2,1)S(1)}, f32[7,8,128]{2,1,0:T(8,128)S(1)}) custom-call(bf16[32,64,256]{2,1,0:T(8,128)(2,1)S(1)} %bitcast.7, s32[4,128]{1,0:T(4,128)S(1)} %get-tuple-element.17.table, ...), custom_call_target="tpu_custom_call" | custom-call | flops 200000000 | bytes 2097152 | tf_op jit(solution)/shard_map/prepare/pallas_call | solution.py:335
  10.2 0.5 %suffix_away.3 = (bf16[272,128]{1,0:T(8,128)(2,1)S(1)}, f32[8,128]{1,0:T(8,128)S(1)}) custom-call(bf16[6,512,128]{2,1,0:T(8,128)(2,1)S(1)} %get-tuple-element.19.keys_ref, bf16[6,128,512]{2,1,0:T(8,128)(2,1)S(1)} %get-tuple-element.20.values_ref, f32[7,8,128]{2,1,0:T(8,128)S(1)} %get-tuple-element.21.member_ref.refs_3_, ...), custom_call_target="tpu_custom_call" | custom-call | flops 200000000 | bytes 2097152 | tf_op jit(solution)/shard_map/suffix_away/pallas_call | solution.py:362
  10.8 0.0 copy-start
  10.8 2.9 %collective-permute-start.3 = (bf16[272,128]{1,0:T(8,128)(2,1)S(1)}, bf16[272,128]{1,0:T(8,128)(2,1)S(1)}, u32[]{:S(2)}, u32[]{:S(2)}) collective-permute-start(bf16[272,128]{1,0:T(8,128)(2,1)S(1)} %get-tuple-element.23), channel_id=1, source_target_pairs={{0,16},{1,17},{4,21},{5,20},{8,24},{9,25},{12,29},{13,28},{16,0},{... | collective-permute-start | bytes 208904 | tf_op jit(solution)/shard_map/ppermute | solution.py:36
  13.7 0.5 %suffix_away.5 = bf16[272,128]{1,0:T(8,128)(2,1)S(1)} custom-call(bf16[6,512,128]{2,1,0:T(8,128)(2,1)S(1)} %get-tuple-element.19.keys_ref, bf16[6,128,512]{2,1,0:T(8,128)(2,1)S(1)} %get-tuple-element.20.values_ref, f32[7,8,128]{2,1,0:T(8,128)S(1)} %get-tuple-element.21.member_ref.refs_3_, bf16[2,16,1024]{2,1,0:T(8,128)(2,1)S(1)} %collective-permute-done.6.message_ref), custom_call_target="tpu_custom_call" | custom-call | flops 200000000 | bytes 2097152 | tf_op jit(solution)/shard_map/suffix_away/pallas_call | solution.py:362
  14.2 2.2 %collective-permute-start.7 = (bf16[272,128]{1,0:T(8,128)(2,1)S(1)}, bf16[272,128]{1,0:T(8,128)(2,1)S(1)}, u32[]{:S(2)}, u32[]{:S(2)}) collective-permute-start(bf16[272,128]{1,0:T(8,128)(2,1)S(1)} %suffix_away.5), channel_id=1, source_target_pairs={{0,24},{1,25},{4,29},{5,28},{8,16},{9,17},{12,21},{13,20},{16,8},{... | collective-permute-start | bytes 208904 | tf_op jit(solution)/shard_map/ppermute | solution.py:36
  16.4 0.5 %suffix_away.4 = bf16[272,128]{1,0:T(8,128)(2,1)S(1)} custom-call(bf16[6,512,128]{2,1,0:T(8,128)(2,1)S(1)} %get-tuple-element.19.keys_ref, bf16[6,128,512]{2,1,0:T(8,128)(2,1)S(1)} %get-tuple-element.20.values_ref, f32[7,8,128]{2,1,0:T(8,128)S(1)} %get-tuple-element.21.member_ref.refs_3_, bf16[2,16,1024]{2,1,0:T(8,128)(2,1)S(1)} %collective-permute-done.4.message_ref), custom_call_target="tpu_custom_call" | custom-call | flops 200000000 | bytes 2097152 | tf_op jit(solution)/shard_map/suffix_away/pallas_call | solution.py:362
  16.9 0.6 %collective-permute-start.5 = (bf16[272,128]{1,0:T(8,128)(2,1)S(1)}, bf16[272,128]{1,0:T(8,128)(2,1)S(1)}, u32[]{:S(2)}, u32[]{:S(2)}) collective-permute-start(bf16[272,128]{1,0:T(8,128)(2,1)S(1)} %suffix_away.4), channel_id=1, source_target_pairs={{0,8},{1,9},{4,13},{5,12},{8,0},{9,1},{12,5},{13,4},{16,24},{17,25... | collective-permute-start | bytes 208904 | tf_op jit(solution)/shard_map/ppermute | solution.py:36
  17.6 1.6 %home_pair_heads.1 = bf16[144,128]{1,0:T(8,128)(2,1)S(1)} custom-call(s32[1]{0:T(128)S(6)} %copy.7.refs_0_, bf16[1,512,128]{2,1,0:T(8,128)(2,1)S(1)} %get-tuple-element.24.refs_1_, bf16[1,128,512]{2,1,0:T(8,128)(2,1)S(1)} %get-tuple-element.25.refs_2_, f32[7,8,128]{2,1,0:T(8,128)S(1)} %get-tuple-element.21.member_ref.refs_3_, ...), custom_call_target="tpu_custom_call" | custom-call | flops 536870912 | bytes 2097152 | tf_op jit(solution)/shard_map/home_pair_heads/pallas_call | solution.py:379
  19.1 0.8 %collective-permute-start.9 = (bf16[144,128]{1,0:T(8,128)(2,1)S(1)}, bf16[144,128]{1,0:T(8,128)(2,1)S(1)}, u32[]{:S(2)}, u32[]{:S(2)}) collective-permute-start(bf16[144,128]{1,0:T(8,128)(2,1)S(1)} %home_pair_heads.1), channel_id=1, source_target_pairs={{0,1},{1,0},{2,3},{3,2},{4,5},{5,4},{6,7},{7,6},{8,9},{9,8},{10,11... | collective-permute-start | bytes 110600 | tf_op jit(solution)/shard_map/ppermute | solution.py:26
  19.9 1.6 %home_own_heads.1 = (f32[128,128]{1,0:T(8,128)S(1)}, f32[8,128]{1,0:T(8,128)S(1)}) custom-call(s32[1]{0:T(128)S(6)} %copy.7.refs_0_, bf16[1,512,128]{2,1,0:T(8,128)(2,1)S(1)} %get-tuple-element.24.refs_1_, bf16[1,128,512]{2,1,0:T(8,128)(2,1)S(1)} %get-tuple-element.25.refs_2_, f32[7,8,128]{2,1,0:T(8,128)S(1)} %get-tuple-element.21.member_ref.refs_3_, ...), custom_call_target="tpu_custom_call" | custom-call | flops 536870912 | bytes 2097152 | tf_op jit(solution)/shard_map/home_own_heads/pallas_call | solution.py:389
  21.5 0.7 %collective-permute-done.5.rest_1_ = bf16[272,128]{1,0:T(8,128)(2,1)S(1)} collective-permute-done((bf16[272,128]{1,0:T(8,128)(2,1)S(1)}, bf16[272,128]{1,0:T(8,128)(2,1)S(1)}, u32[]{:S(2)}, u32[]{:S(2)}) %collective-permute-start.5) | collective-permute-done | bytes 69664 | tf_op jit(solution)/shard_map/ppermute | solution.py:36
  22.2 0.4 %collective-permute-start.10 = (bf16[144,128]{1,0:T(8,128)(2,1)S(1)}, bf16[144,128]{1,0:T(8,128)(2,1)S(1)}, u32[]{:S(2)}, u32[]{:S(2)}) collective-permute-start(bf16[144,128]{1,0:T(8,128)(2,1)S(1)} %sibling_share.1), channel_id=1, source_target_pairs={{0,4},{4,0},{1,5},{5,1},{2,6},{6,2},{3,7},{7,3},{8,12},{12,8},{9,1... | collective-permute-start | bytes 110600 | tf_op jit(solution)/shard_map/ppermute | solution.py:26
  22.6 0.6 %collective-permute-done.9.rest_3_ = bf16[144,128]{1,0:T(8,128)(2,1)S(1)} collective-permute-done((bf16[144,128]{1,0:T(8,128)(2,1)S(1)}, bf16[144,128]{1,0:T(8,128)(2,1)S(1)}, u32[]{:S(2)}, u32[]{:S(2)}) %collective-permute-start.9) | collective-permute-done | bytes 36896 | tf_op jit(solution)/shard_map/ppermute | solution.py:26
  23.2 0.4 %collective-permute-done.10.rest_4_ = bf16[144,128]{1,0:T(8,128)(2,1)S(1)} collective-permute-done((bf16[144,128]{1,0:T(8,128)(2,1)S(1)}, bf16[144,128]{1,0:T(8,128)(2,1)S(1)}, u32[]{:S(2)}, u32[]{:S(2)}) %collective-permute-start.10) | collective-permute-done | bytes 36896 | tf_op jit(solution)/shard_map/ppermute | solution.py:26
  23.5 0.8 %combine.1 = f32[16,1024]{1,0:T(8,128)} custom-call(bf16[272,128]{1,0:T(8,128)(2,1)S(1)} %collective-permute-done.3.rest_0_, bf16[272,128]{1,0:T(8,128)(2,1)S(1)} %collective-permute-done.5.rest_1_, bf16[272,128]{1,0:T(8,128)(2,1)S(1)} %collective-permute-done.7.rest_2_, bf16[144,128]{1,0:T(8,128)(2,1)S(1)} %collective-permute-done.9.rest_3_, ...), custom_call_target="tpu_custom_call" | custom-call | tf_op jit(solution)/shard_map/combine/pallas_call | solution.py:408
  (14 shorter events, 0.1 us)
Async XLA Ops:
  0.0 1.5 %collective-permute-start.1 = (bf16[16,1024]{1,0:T(8,128)(2,1)}, bf16[16,1024]{1,0:T(8,128)(2,1)S(1)}, u32[]{:S(2)}, u32[]{:S(2)}) collective-permute-start(bf16[16,1024]{1,0:T(8,128)(2,1)} %refs_0_.3), channel_id=1, source_target_pairs={{0,4},{4,0},{1,5},{5,1},{2,6},{6,2},{3,7},{7,3},{8,12},{12,8},{9,1... | collective-permute-start | bytes 98312 | tf_op jit(solution)/shard_map/ppermute | solution.py:26
  0.5 8.8 %collective-permute-start = (bf16[32,64,256]{2,1,0:T(8,128)(2,1)}, bf16[32,64,256]{2,1,0:T(8,128)(2,1)S(1)}, u32[]{:S(2)}, u32[]{:S(2)}) collective-permute-start(bf16[32,64,256]{2,1,0:T(8,128)(2,1)} %bitcast.6), channel_id=1, source_target_pairs={{0,4},{4,0},{1,5},{5,1},{2,6},{6,2},{3,7},{7,3},{8,12},{12,8},{9,1... | collective-permute-start | bytes 3145736 | tf_op jit(solution)/shard_map/ppermute | solution.py:26
  1.5 5.6 %copy-start.2 = (bf16[16,1024]{1,0:T(8,128)(2,1)S(1)}, bf16[16,1024]{1,0:T(8,128)(2,1)}, u32[]{:S(2)}) copy-start(bf16[16,1024]{1,0:T(8,128)(2,1)} %refs_0_.3) | copy-start | bytes 98308
  1.5 7.8 %copy-start.1 = (bf16[32,1,64,256]{3,2,1,0:T(8,128)(2,1)S(1)}, bf16[32,1,64,256]{3,2,1,0:T(8,128)(2,1)}, u32[]{:S(2)}) copy-start(bf16[32,1,64,256]{3,2,1,0:T(8,128)(2,1)} %param.8) | copy-start | bytes 3145732
  1.5 8.7 %collective-permute-start.2 = (bf16[2,16,1024]{2,1,0:T(8,128)(2,1)S(1)}, bf16[2,16,1024]{2,1,0:T(8,128)(2,1)S(1)}, u32[]{:S(2)}, u32[]{:S(2)}) collective-permute-start(bf16[2,16,1024]{2,1,0:T(8,128)(2,1)S(1)} %both_cores.1), channel_id=1, source_target_pairs={{0,16},{1,17},{4,21},{5,20},{8,24},{9,25},{12,29},{13,28},{16,0},{... | collective-permute-start | bytes 196616 | tf_op jit(solution)/shard_map/ppermute | solution.py:36
  5.5 8.1 %collective-permute-start.6 = (bf16[2,16,1024]{2,1,0:T(8,128)(2,1)S(1)}, bf16[2,16,1024]{2,1,0:T(8,128)(2,1)S(1)}, u32[]{:S(2)}, u32[]{:S(2)}) collective-permute-start(bf16[2,16,1024]{2,1,0:T(8,128)(2,1)S(1)} %both_cores.1), channel_id=1, source_target_pairs={{0,24},{1,25},{4,29},{5,28},{8,16},{9,17},{12,21},{13,20},{16,8},{... | collective-permute-start | bytes 196616 | tf_op jit(solution)/shard_map/ppermute | solution.py:36
  6.9 9.5 %collective-permute-start.4 = (bf16[2,16,1024]{2,1,0:T(8,128)(2,1)S(1)}, bf16[2,16,1024]{2,1,0:T(8,128)(2,1)S(1)}, u32[]{:S(2)}, u32[]{:S(2)}) collective-permute-start(bf16[2,16,1024]{2,1,0:T(8,128)(2,1)S(1)} %both_cores.1), channel_id=1, source_target_pairs={{0,8},{1,9},{4,13},{5,12},{8,0},{9,1},{12,5},{13,4},{16,24},{17,25... | collective-permute-start | bytes 196616 | tf_op jit(solution)/shard_map/ppermute | solution.py:36
  7.1 10.4 %collective-permute-start.8 = (bf16[16,1024]{1,0:T(8,128)(2,1)S(1)}, bf16[16,1024]{1,0:T(8,128)(2,1)S(1)}, u32[]{:S(2)}, u32[]{:S(2)}) collective-permute-start(bf16[16,1024]{1,0:T(8,128)(2,1)S(1)} %copy-done.2), channel_id=1, source_target_pairs={{0,1},{1,0},{2,3},{3,2},{4,5},{5,4},{6,7},{7,6},{8,9},{9,8},{10,11... | collective-permute-start | bytes 98312 | tf_op jit(solution)/shard_map/ppermute | solution.py:26
  10.8 6.8 %copy-start = (bf16[1,1,4096,256]{3,2,1,0:T(8,128)(2,1)S(1)}, bf16[1,1,4096,256]{3,2,1,0:T(8,128)(2,1)}, u32[]{:S(2)}) copy-start(bf16[1,1,4096,256]{3,2,1,0:T(8,128)(2,1)} %param.7) | copy-start | bytes 6291460
  10.8 10.7 %collective-permute-start.3 = (bf16[272,128]{1,0:T(8,128)(2,1)S(1)}, bf16[272,128]{1,0:T(8,128)(2,1)S(1)}, u32[]{:S(2)}, u32[]{:S(2)}) collective-permute-start(bf16[272,128]{1,0:T(8,128)(2,1)S(1)} %get-tuple-element.23), channel_id=1, source_target_pairs={{0,16},{1,17},{4,21},{5,20},{8,24},{9,25},{12,29},{13,28},{16,0},{... | collective-permute-start | bytes 208904 | tf_op jit(solution)/shard_map/ppermute | solution.py:36
  14.2 7.3 %collective-permute-start.7 = (bf16[272,128]{1,0:T(8,128)(2,1)S(1)}, bf16[272,128]{1,0:T(8,128)(2,1)S(1)}, u32[]{:S(2)}, u32[]{:S(2)}) collective-permute-start(bf16[272,128]{1,0:T(8,128)(2,1)S(1)} %suffix_away.5), channel_id=1, source_target_pairs={{0,24},{1,25},{4,29},{5,28},{8,16},{9,17},{12,21},{13,20},{16,8},{... | collective-permute-start | bytes 208904 | tf_op jit(solution)/shard_map/ppermute | solution.py:36
  16.9 5.3 %collective-permute-start.5 = (bf16[272,128]{1,0:T(8,128)(2,1)S(1)}, bf16[272,128]{1,0:T(8,128)(2,1)S(1)}, u32[]{:S(2)}, u32[]{:S(2)}) collective-permute-start(bf16[272,128]{1,0:T(8,128)(2,1)S(1)} %suffix_away.4), channel_id=1, source_target_pairs={{0,8},{1,9},{4,13},{5,12},{8,0},{9,1},{12,5},{13,4},{16,24},{17,25... | collective-permute-start | bytes 208904 | tf_op jit(solution)/shard_map/ppermute | solution.py:36
  19.1 4.0 %collective-permute-start.9 = (bf16[144,128]{1,0:T(8,128)(2,1)S(1)}, bf16[144,128]{1,0:T(8,128)(2,1)S(1)}, u32[]{:S(2)}, u32[]{:S(2)}) collective-permute-start(bf16[144,128]{1,0:T(8,128)(2,1)S(1)} %home_pair_heads.1), channel_id=1, source_target_pairs={{0,1},{1,0},{2,3},{3,2},{4,5},{5,4},{6,7},{7,6},{8,9},{9,8},{10,11... | collective-permute-start | bytes 110600 | tf_op jit(solution)/shard_map/ppermute | solution.py:26
  22.2 1.3 %collective-permute-start.10 = (bf16[144,128]{1,0:T(8,128)(2,1)S(1)}, bf16[144,128]{1,0:T(8,128)(2,1)S(1)}, u32[]{:S(2)}, u32[]{:S(2)}) collective-permute-start(bf16[144,128]{1,0:T(8,128)(2,1)S(1)} %sibling_share.1), channel_id=1, source_target_pairs={{0,4},{4,0},{1,5},{5,1},{2,6},{6,2},{3,7},{7,3},{8,12},{12,8},{9,1... | collective-permute-start | bytes 110600 | tf_op jit(solution)/shard_map/ppermute | solution.py:26

commit v28 on v27

--- a/solution.py
+++ b/solution.py
@@ -15,7 +15,7 @@
 VECS = HEADS * BEAMS
 STAT_ROWS = 16
 CHUNK = 512
-FIRST_MASKS = (2, 3, 1)
+FIRST_MASKS = (3, 1, 2)
 SURELY_VALID = 1024
 
 big_negative = -1e30

time: 24.5 us -> 25.3 us (1.033)
  starting transfers between devices: 14.5 us -> 15.1 us
    ppermute x5, starting transfers between devices: 3.14 us -> 4.92 us  [swapped(): return lax.ppermute(value, axis, [(0, 1), (1, 0)])]
    ppermute x6, starting transfers between devices: 11.3 us -> 10.2 us  [exchanged(): return lax.ppermute(value, ('z', 'core', 'pair'), pairs)]
  transfers between devices with their start and end apart: 11 -> 11, of which waited for: 4 -> 3; matrix products, arithmetic and copies ran while one was open for 0% -> 0% of each run, Pallas kernels for 26% -> 26%
where the time goes in v28:
time: 25.3 us; the launch traced here: 25.1 us
  starting transfers between devices  15.1 us (60%)
  Pallas kernels  7.2 us (28%)
  waiting for transfers between devices  1.99 us (8%)
  between operations  0.78 us (3%)
    ppermute x6, starting transfers between devices, exchanged(): return lax.ppermute(value, ('z', 'core', 'pair'), pairs)  10.2 us
    ppermute x5, starting transfers between devices, swapped(): return lax.ppermute(value, axis, [(0, 1), (1, 0)])  4.92 us
    pallas_call x1, Pallas kernels, on_device(): pl.pallas_call(pair_heads_kernel, out_shape=pltpu.VMEM((HD + STAT_ROWS, V...  1.57 us
    pallas_call x1, Pallas kernels, on_device(): pl.pallas_call(own_heads_kernel, out_shape=(pltpu.VMEM((HD, VECS), jnp.fl...  1.55 us
    pallas_call x3, Pallas kernels, on_device(): pl.pallas_call(functools.partial(away_kernel, 2 * mask - 2), out_shape=ou...  1.53 us
    ppermute x5, waiting for transfers between devices, swapped(): return lax.ppermute(value, axis, [(0, 1), (1, 0)])  1.09 us
    pallas_call x1, Pallas kernels, on_device(): pl.pallas_call(functools.partial(prepare_kernel, capacity), out_shape=(pl...  0.94 us
    ppermute x6, waiting for transfers between devices, exchanged(): return lax.ppermute(value, ('z', 'core', 'pair'), pairs)  0.91 us
  transfers between devices with their start and end apart: 11, of which 3 were waited for; matrix products, arithmetic and copies ran while one was open for 0% of the time, Pallas kernels for 26%

profile of v28, /device:TPU:0, one launch (start us, length us, event | category | flops | bytes accessed | tf_op | source)
XLA Modules:
  0.0 25.1 jit_solution(6417514105711825105)
XLA Ops:
  0.0 0.5 %collective-permute-start.1 = (bf16[16,1024]{1,0:T(8,128)(2,1)}, bf16[16,1024]{1,0:T(8,128)(2,1)S(1)}, u32[]{:S(2)}, u32[]{:S(2)}) collective-permute-start(bf16[16,1024]{1,0:T(8,128)(2,1)} %refs_0_.3), channel_id=1, source_target_pairs={{0,4},{4,0},{1,5},{5,1},{2,6},{6,2},{3,7},{7,3},{8,12},{12,8},{9,1... | collective-permute-start | bytes 98312 | tf_op jit(solution)/shard_map/ppermute | solution.py:26
  0.5 0.1 collective-permute-start
  0.5 0.8 %stage.1 = (bf16[16,1024]{1,0:T(8,128)(2,1)S(1)}, s32[4,128]{1,0:T(4,128)S(1)}, s32[1,128]{1,0:T(1,128)S(1)}) custom-call(bf16[16,1024]{1,0:T(8,128)(2,1)} %refs_0_.3, s32[4,128]{1,0:T(4,128)} %bitcast.8, s32[1,128]{1,0:T(1,128)} %bitcast.9), custom_call_target="tpu_custom_call" | custom-call | tf_op jit(solution)/shard_map/stage/pallas_call | solution.py:313
  1.3 0.2 collective-permute-done.1.sibling_ref
  1.5 5.0 %collective-permute-start.2 = (bf16[2,16,1024]{2,1,0:T(8,128)(2,1)S(1)}, bf16[2,16,1024]{2,1,0:T(8,128)(2,1)S(1)}, u32[]{:S(2)}, u32[]{:S(2)}) collective-permute-start(bf16[2,16,1024]{2,1,0:T(8,128)(2,1)S(1)} %both_cores.1), channel_id=1, source_target_pairs={{0,24},{1,25},{4,29},{5,28},{8,16},{9,17},{12,21},{13,20},{16,8},{... | collective-permute-start | bytes 196616 | tf_op jit(solution)/shard_map/ppermute | solution.py:36
  6.6 0.0 collective-permute-start.6
  6.6 0.6 %collective-permute-start.4 = (bf16[2,16,1024]{2,1,0:T(8,128)(2,1)S(1)}, bf16[2,16,1024]{2,1,0:T(8,128)(2,1)S(1)}, u32[]{:S(2)}, u32[]{:S(2)}) collective-permute-start(bf16[2,16,1024]{2,1,0:T(8,128)(2,1)S(1)} %both_cores.1), channel_id=1, source_target_pairs={{0,16},{1,17},{4,21},{5,20},{8,24},{9,25},{12,29},{13,28},{16,0},{... | collective-permute-start | bytes 196616 | tf_op jit(solution)/shard_map/ppermute | solution.py:36
  7.2 1.6 %collective-permute-start.8 = (bf16[16,1024]{1,0:T(8,128)(2,1)S(1)}, bf16[16,1024]{1,0:T(8,128)(2,1)S(1)}, u32[]{:S(2)}, u32[]{:S(2)}) collective-permute-start(bf16[16,1024]{1,0:T(8,128)(2,1)S(1)} %copy-done.2), channel_id=1, source_target_pairs={{0,1},{1,0},{2,3},{3,2},{4,5},{5,4},{6,7},{7,6},{8,9},{9,8},{10,11... | collective-permute-start | bytes 98312 | tf_op jit(solution)/shard_map/ppermute | solution.py:26
  9.5 0.9 %prepare.1 = (bf16[1,512,128]{2,1,0:T(8,128)(2,1)S(1)}, bf16[1,128,512]{2,1,0:T(8,128)(2,1)S(1)}, bf16[6,512,128]{2,1,0:T(8,128)(2,1)S(1)}, bf16[6,128,512]{2,1,0:T(8,128)(2,1)S(1)}, f32[7,8,128]{2,1,0:T(8,128)S(1)}) custom-call(bf16[32,64,256]{2,1,0:T(8,128)(2,1)S(1)} %bitcast.7, s32[4,128]{1,0:T(4,128)S(1)} %get-tuple-element.17.table, ...), custom_call_target="tpu_custom_call" | custom-call | flops 200000000 | bytes 2097152 | tf_op jit(solution)/shard_map/prepare/pallas_call | solution.py:335
  10.5 0.5 %suffix_away.3 = (bf16[272,128]{1,0:T(8,128)(2,1)S(1)}, f32[8,128]{1,0:T(8,128)S(1)}) custom-call(bf16[6,512,128]{2,1,0:T(8,128)(2,1)S(1)} %get-tuple-element.19.keys_ref, bf16[6,128,512]{2,1,0:T(8,128)(2,1)S(1)} %get-tuple-element.20.values_ref, f32[7,8,128]{2,1,0:T(8,128)S(1)} %get-tuple-element.21.member_ref.refs_3_, ...), custom_call_target="tpu_custom_call" | custom-call | flops 200000000 | bytes 2097152 | tf_op jit(solution)/shard_map/suffix_away/pallas_call | solution.py:362
  11.0 0.0 copy-start
  11.0 3.7 %collective-permute-start.3 = (bf16[272,128]{1,0:T(8,128)(2,1)S(1)}, bf16[272,128]{1,0:T(8,128)(2,1)S(1)}, u32[]{:S(2)}, u32[]{:S(2)}) collective-permute-start(bf16[272,128]{1,0:T(8,128)(2,1)S(1)} %get-tuple-element.23), channel_id=1, source_target_pairs={{0,24},{1,25},{4,29},{5,28},{8,16},{9,17},{12,21},{13,20},{16,8},{... | collective-permute-start | bytes 208904 | tf_op jit(solution)/shard_map/ppermute | solution.py:36
  14.7 0.0 collective-permute-done.6.message_ref
  14.7 0.5 %suffix_away.5 = bf16[272,128]{1,0:T(8,128)(2,1)S(1)} custom-call(bf16[6,512,128]{2,1,0:T(8,128)(2,1)S(1)} %get-tuple-element.19.keys_ref, bf16[6,128,512]{2,1,0:T(8,128)(2,1)S(1)} %get-tuple-element.20.values_ref, f32[7,8,128]{2,1,0:T(8,128)S(1)} %get-tuple-element.21.member_ref.refs_3_, bf16[2,16,1024]{2,1,0:T(8,128)(2,1)S(1)} %collective-permute-done.6.message_ref), custom_call_target="tpu_custom_call" | custom-call | flops 200000000 | bytes 2097152 | tf_op jit(solution)/shard_map/suffix_away/pallas_call | solution.py:362
  15.2 0.1 collective-permute-start.7
  15.3 0.5 %suffix_away.4 = bf16[272,128]{1,0:T(8,128)(2,1)S(1)} custom-call(bf16[6,512,128]{2,1,0:T(8,128)(2,1)S(1)} %get-tuple-element.19.keys_ref, bf16[6,128,512]{2,1,0:T(8,128)(2,1)S(1)} %get-tuple-element.20.values_ref, f32[7,8,128]{2,1,0:T(8,128)S(1)} %get-tuple-element.21.member_ref.refs_3_, bf16[2,16,1024]{2,1,0:T(8,128)(2,1)S(1)} %collective-permute-done.4.message_ref), custom_call_target="tpu_custom_call" | custom-call | flops 200000000 | bytes 2097152 | tf_op jit(solution)/shard_map/suffix_away/pallas_call | solution.py:362
  15.8 0.8 %collective-permute-start.5 = (bf16[272,128]{1,0:T(8,128)(2,1)S(1)}, bf16[272,128]{1,0:T(8,128)(2,1)S(1)}, u32[]{:S(2)}, u32[]{:S(2)}) collective-permute-start(bf16[272,128]{1,0:T(8,128)(2,1)S(1)} %suffix_away.4), channel_id=1, source_target_pairs={{0,16},{1,17},{4,21},{5,20},{8,24},{9,25},{12,29},{13,28},{16,0},{... | collective-permute-start | bytes 208904 | tf_op jit(solution)/shard_map/ppermute | solution.py:36
  16.6 1.6 %home_pair_heads.1 = bf16[144,128]{1,0:T(8,128)(2,1)S(1)} custom-call(s32[1]{0:T(128)S(6)} %copy.7.refs_0_, bf16[1,512,128]{2,1,0:T(8,128)(2,1)S(1)} %get-tuple-element.24.refs_1_, bf16[1,128,512]{2,1,0:T(8,128)(2,1)S(1)} %get-tuple-element.25.refs_2_, f32[7,8,128]{2,1,0:T(8,128)S(1)} %get-tuple-element.21.member_ref.refs_3_, ...), custom_call_target="tpu_custom_call" | custom-call | flops 536870912 | bytes 2097152 | tf_op jit(solution)/shard_map/home_pair_heads/pallas_call | solution.py:379
  18.2 0.7 %collective-permute-start.9 = (bf16[144,128]{1,0:T(8,128)(2,1)S(1)}, bf16[144,128]{1,0:T(8,128)(2,1)S(1)}, u32[]{:S(2)}, u32[]{:S(2)}) collective-permute-start(bf16[144,128]{1,0:T(8,128)(2,1)S(1)} %home_pair_heads.1), channel_id=1, source_target_pairs={{0,1},{1,0},{2,3},{3,2},{4,5},{5,4},{6,7},{7,6},{8,9},{9,8},{10,11... | collective-permute-start | bytes 110600 | tf_op jit(solution)/shard_map/ppermute | solution.py:26
  18.9 1.6 %home_own_heads.1 = (f32[128,128]{1,0:T(8,128)S(1)}, f32[8,128]{1,0:T(8,128)S(1)}) custom-call(s32[1]{0:T(128)S(6)} %copy.7.refs_0_, bf16[1,512,128]{2,1,0:T(8,128)(2,1)S(1)} %get-tuple-element.24.refs_1_, bf16[1,128,512]{2,1,0:T(8,128)(2,1)S(1)} %get-tuple-element.25.refs_2_, f32[7,8,128]{2,1,0:T(8,128)S(1)} %get-tuple-element.21.member_ref.refs_3_, ...), custom_call_target="tpu_custom_call" | custom-call | flops 536870912 | bytes 2097152 | tf_op jit(solution)/shard_map/home_own_heads/pallas_call | solution.py:389
  20.5 0.9 %collective-permute-done.5.rest_1_ = bf16[272,128]{1,0:T(8,128)(2,1)S(1)} collective-permute-done((bf16[272,128]{1,0:T(8,128)(2,1)S(1)}, bf16[272,128]{1,0:T(8,128)(2,1)S(1)}, u32[]{:S(2)}, u32[]{:S(2)}) %collective-permute-start.5) | collective-permute-done | bytes 69664 | tf_op jit(solution)/shard_map/ppermute | solution.py:36
  21.4 2.1 %collective-permute-start.10 = (bf16[144,128]{1,0:T(8,128)(2,1)S(1)}, bf16[144,128]{1,0:T(8,128)(2,1)S(1)}, u32[]{:S(2)}, u32[]{:S(2)}) collective-permute-start(bf16[144,128]{1,0:T(8,128)(2,1)S(1)} %sibling_share.1), channel_id=1, source_target_pairs={{0,4},{4,0},{1,5},{5,1},{2,6},{6,2},{3,7},{7,3},{8,12},{12,8},{9,1... | collective-permute-start | bytes 110600 | tf_op jit(solution)/shard_map/ppermute | solution.py:26
  23.5 0.9 %collective-permute-done.10.rest_4_ = bf16[144,128]{1,0:T(8,128)(2,1)S(1)} collective-permute-done((bf16[144,128]{1,0:T(8,128)(2,1)S(1)}, bf16[144,128]{1,0:T(8,128)(2,1)S(1)}, u32[]{:S(2)}, u32[]{:S(2)}) %collective-permute-start.10) | collective-permute-done | bytes 36896 | tf_op jit(solution)/shard_map/ppermute | solution.py:26
  24.4 0.8 %combine.1 = f32[16,1024]{1,0:T(8,128)} custom-call(bf16[272,128]{1,0:T(8,128)(2,1)S(1)} %collective-permute-done.3.rest_0_, bf16[272,128]{1,0:T(8,128)(2,1)S(1)} %collective-permute-done.5.rest_1_, bf16[272,128]{1,0:T(8,128)(2,1)S(1)} %collective-permute-done.7.rest_2_, bf16[144,128]{1,0:T(8,128)(2,1)S(1)} %collective-permute-done.9.rest_3_, ...), custom_call_target="tpu_custom_call" | custom-call | tf_op jit(solution)/shard_map/combine/pallas_call | solution.py:408
  (14 shorter events, 0.1 us)
Async XLA Ops:
  0.0 1.5 %collective-permute-start.1 = (bf16[16,1024]{1,0:T(8,128)(2,1)}, bf16[16,1024]{1,0:T(8,128)(2,1)S(1)}, u32[]{:S(2)}, u32[]{:S(2)}) collective-permute-start(bf16[16,1024]{1,0:T(8,128)(2,1)} %refs_0_.3), channel_id=1, source_target_pairs={{0,4},{4,0},{1,5},{5,1},{2,6},{6,2},{3,7},{7,3},{8,12},{12,8},{9,1... | collective-permute-start | bytes 98312 | tf_op jit(solution)/shard_map/ppermute | solution.py:26
  0.5 9.0 %collective-permute-start = (bf16[32,64,256]{2,1,0:T(8,128)(2,1)}, bf16[32,64,256]{2,1,0:T(8,128)(2,1)S(1)}, u32[]{:S(2)}, u32[]{:S(2)}) collective-permute-start(bf16[32,64,256]{2,1,0:T(8,128)(2,1)} %bitcast.6), channel_id=1, source_target_pairs={{0,4},{4,0},{1,5},{5,1},{2,6},{6,2},{3,7},{7,3},{8,12},{12,8},{9,1... | collective-permute-start | bytes 3145736 | tf_op jit(solution)/shard_map/ppermute | solution.py:26
  1.5 5.7 %copy-start.2 = (bf16[16,1024]{1,0:T(8,128)(2,1)S(1)}, bf16[16,1024]{1,0:T(8,128)(2,1)}, u32[]{:S(2)}) copy-start(bf16[16,1024]{1,0:T(8,128)(2,1)} %refs_0_.3) | copy-start | bytes 98308
  1.5 8.0 %copy-start.1 = (bf16[32,1,64,256]{3,2,1,0:T(8,128)(2,1)S(1)}, bf16[32,1,64,256]{3,2,1,0:T(8,128)(2,1)}, u32[]{:S(2)}) copy-start(bf16[32,1,64,256]{3,2,1,0:T(8,128)(2,1)} %param.8) | copy-start | bytes 3145732
  1.5 8.9 %collective-permute-start.2 = (bf16[2,16,1024]{2,1,0:T(8,128)(2,1)S(1)}, bf16[2,16,1024]{2,1,0:T(8,128)(2,1)S(1)}, u32[]{:S(2)}, u32[]{:S(2)}) collective-permute-start(bf16[2,16,1024]{2,1,0:T(8,128)(2,1)S(1)} %both_cores.1), channel_id=1, source_target_pairs={{0,24},{1,25},{4,29},{5,28},{8,16},{9,17},{12,21},{13,20},{16,8},{... | collective-permute-start | bytes 196616 | tf_op jit(solution)/shard_map/ppermute | solution.py:36
  6.6 8.1 %collective-permute-start.6 = (bf16[2,16,1024]{2,1,0:T(8,128)(2,1)S(1)}, bf16[2,16,1024]{2,1,0:T(8,128)(2,1)S(1)}, u32[]{:S(2)}, u32[]{:S(2)}) collective-permute-start(bf16[2,16,1024]{2,1,0:T(8,128)(2,1)S(1)} %both_cores.1), channel_id=1, source_target_pairs={{0,8},{1,9},{4,13},{5,12},{8,0},{9,1},{12,5},{13,4},{16,24},{17,25... | collective-permute-start | bytes 196616 | tf_op jit(solution)/shard_map/ppermute | solution.py:36
  6.6 8.7 %collective-permute-start.4 = (bf16[2,16,1024]{2,1,0:T(8,128)(2,1)S(1)}, bf16[2,16,1024]{2,1,0:T(8,128)(2,1)S(1)}, u32[]{:S(2)}, u32[]{:S(2)}) collective-permute-start(bf16[2,16,1024]{2,1,0:T(8,128)(2,1)S(1)} %both_cores.1), channel_id=1, source_target_pairs={{0,16},{1,17},{4,21},{5,20},{8,24},{9,25},{12,29},{13,28},{16,0},{... | collective-permute-start | bytes 196616 | tf_op jit(solution)/shard_map/ppermute | solution.py:36
  7.2 9.4 %collective-permute-start.8 = (bf16[16,1024]{1,0:T(8,128)(2,1)S(1)}, bf16[16,1024]{1,0:T(8,128)(2,1)S(1)}, u32[]{:S(2)}, u32[]{:S(2)}) collective-permute-start(bf16[16,1024]{1,0:T(8,128)(2,1)S(1)} %copy-done.2), channel_id=1, source_target_pairs={{0,1},{1,0},{2,3},{3,2},{4,5},{5,4},{6,7},{7,6},{8,9},{9,8},{10,11... | collective-permute-start | bytes 98312 | tf_op jit(solution)/shard_map/ppermute | solution.py:26
  11.0 5.6 %copy-start = (bf16[1,1,4096,256]{3,2,1,0:T(8,128)(2,1)S(1)}, bf16[1,1,4096,256]{3,2,1,0:T(8,128)(2,1)}, u32[]{:S(2)}) copy-start(bf16[1,1,4096,256]{3,2,1,0:T(8,128)(2,1)} %param.7) | copy-start | bytes 6291460
  11.0 9.5 %collective-permute-start.3 = (bf16[272,128]{1,0:T(8,128)(2,1)S(1)}, bf16[272,128]{1,0:T(8,128)(2,1)S(1)}, u32[]{:S(2)}, u32[]{:S(2)}) collective-permute-start(bf16[272,128]{1,0:T(8,128)(2,1)S(1)} %get-tuple-element.23), channel_id=1, source_target_pairs={{0,24},{1,25},{4,29},{5,28},{8,16},{9,17},{12,21},{13,20},{16,8},{... | collective-permute-start | bytes 208904 | tf_op jit(solution)/shard_map/ppermute | solution.py:36
  15.2 5.3 %collective-permute-start.7 = (bf16[272,128]{1,0:T(8,128)(2,1)S(1)}, bf16[272,128]{1,0:T(8,128)(2,1)S(1)}, u32[]{:S(2)}, u32[]{:S(2)}) collective-permute-start(bf16[272,128]{1,0:T(8,128)(2,1)S(1)} %suffix_away.5), channel_id=1, source_target_pairs={{0,8},{1,9},{4,13},{5,12},{8,0},{9,1},{12,5},{13,4},{16,24},{17,25... | collective-permute-start | bytes 208904 | tf_op jit(solution)/shard_map/ppermute | solution.py:36
  15.8 5.6 %collective-permute-start.5 = (bf16[272,128]{1,0:T(8,128)(2,1)S(1)}, bf16[272,128]{1,0:T(8,128)(2,1)S(1)}, u32[]{:S(2)}, u32[]{:S(2)}) collective-permute-start(bf16[272,128]{1,0:T(8,128)(2,1)S(1)} %suffix_away.4), channel_id=1, source_target_pairs={{0,16},{1,17},{4,21},{5,20},{8,24},{9,25},{12,29},{13,28},{16,0},{... | collective-permute-start | bytes 208904 | tf_op jit(solution)/shard_map/ppermute | solution.py:36
  18.2 5.3 %collective-permute-start.9 = (bf16[144,128]{1,0:T(8,128)(2,1)S(1)}, bf16[144,128]{1,0:T(8,128)(2,1)S(1)}, u32[]{:S(2)}, u32[]{:S(2)}) collective-permute-start(bf16[144,128]{1,0:T(8,128)(2,1)S(1)} %home_pair_heads.1), channel_id=1, source_target_pairs={{0,1},{1,0},{2,3},{3,2},{4,5},{5,4},{6,7},{7,6},{8,9},{9,8},{10,11... | collective-permute-start | bytes 110600 | tf_op jit(solution)/shard_map/ppermute | solution.py:26
  21.4 3.0 %collective-permute-start.10 = (bf16[144,128]{1,0:T(8,128)(2,1)S(1)}, bf16[144,128]{1,0:T(8,128)(2,1)S(1)}, u32[]{:S(2)}, u32[]{:S(2)}) collective-permute-start(bf16[144,128]{1,0:T(8,128)(2,1)S(1)} %sibling_share.1), channel_id=1, source_target_pairs={{0,4},{4,0},{1,5},{5,1},{2,6},{6,2},{3,7},{7,3},{8,12},{12,8},{9,1... | collective-permute-start | bytes 110600 | tf_op jit(solution)/shard_map/ppermute | solution.py:26

commit v29 on v28

--- a/solution.py
+++ b/solution.py
@@ -15,7 +15,7 @@
 VECS = HEADS * BEAMS
 STAT_ROWS = 16
 CHUNK = 512
-FIRST_MASKS = (3, 1, 2)
+FIRST_MASKS = (2, 1, 3)
 SURELY_VALID = 1024
 
 big_negative = -1e30

time: 25.3 us -> 25.3 us (level)
  waiting for transfers between devices: 1.99 us -> 3.8 us
  starting transfers between devices: 15.1 us -> 13.3 us
    ppermute x5, starting transfers between devices: 4.92 us -> 3.12 us  [swapped(): return lax.ppermute(value, axis, [(0, 1), (1, 0)])]
    ppermute x6, waiting for transfers between devices: 0.91 us -> 2.48 us  [exchanged(): return lax.ppermute(value, ('z', 'core', 'pair'), pairs)]
where the time goes in v29:
time: 25.3 us; the launch traced here: 25.1 us
  starting transfers between devices  13.3 us (53%)
  Pallas kernels  7.21 us (28%)
  waiting for transfers between devices  3.8 us (15%)
  between operations  0.76 us (3%)
    ppermute x6, starting transfers between devices, exchanged(): return lax.ppermute(value, ('z', 'core', 'pair'), pairs)  10.2 us
    ppermute x5, starting transfers between devices, swapped(): return lax.ppermute(value, axis, [(0, 1), (1, 0)])  3.12 us
    ppermute x6, waiting for transfers between devices, exchanged(): return lax.ppermute(value, ('z', 'core', 'pair'), pairs)  2.48 us
    pallas_call x1, Pallas kernels, on_device(): pl.pallas_call(pair_heads_kernel, out_shape=pltpu.VMEM((HD + STAT_ROWS, V...  1.57 us
    pallas_call x1, Pallas kernels, on_device(): pl.pallas_call(own_heads_kernel, out_shape=(pltpu.VMEM((HD, VECS), jnp.fl...  1.56 us
    pallas_call x3, Pallas kernels, on_device(): pl.pallas_call(functools.partial(away_kernel, 2 * mask - 2), out_shape=ou...  1.53 us
    ppermute x5, waiting for transfers between devices, swapped(): return lax.ppermute(value, axis, [(0, 1), (1, 0)])  1.32 us
    pallas_call x1, Pallas kernels, on_device(): pl.pallas_call(functools.partial(prepare_kernel, capacity), out_shape=(pl...  0.94 us
  transfers between devices with their start and end apart: 11, of which 3 were waited for; matrix products, arithmetic and copies ran while one was open for 0% of the time, Pallas kernels for 26%

profile of v29, /device:TPU:0, one launch (start us, length us, event | category | flops | bytes accessed | tf_op | source)
XLA Modules:
  0.0 25.1 jit_solution(15409567717533718248)
XLA Ops:
  0.0 0.5 %collective-permute-start.1 = (bf16[16,1024]{1,0:T(8,128)(2,1)}, bf16[16,1024]{1,0:T(8,128)(2,1)S(1)}, u32[]{:S(2)}, u32[]{:S(2)}) collective-permute-start(bf16[16,1024]{1,0:T(8,128)(2,1)} %refs_0_.3), channel_id=1, source_target_pairs={{0,4},{4,0},{1,5},{5,1},{2,6},{6,2},{3,7},{7,3},{8,12},{12,8},{9,1... | collective-permute-start | bytes 98312 | tf_op jit(solution)/shard_map/ppermute | solution.py:26
  0.5 0.1 collective-permute-start
  0.5 0.8 %stage.1 = (bf16[16,1024]{1,0:T(8,128)(2,1)S(1)}, s32[4,128]{1,0:T(4,128)S(1)}, s32[1,128]{1,0:T(1,128)S(1)}) custom-call(bf16[16,1024]{1,0:T(8,128)(2,1)} %refs_0_.3, s32[4,128]{1,0:T(4,128)} %bitcast.8, s32[1,128]{1,0:T(1,128)} %bitcast.9), custom_call_target="tpu_custom_call" | custom-call | tf_op jit(solution)/shard_map/stage/pallas_call | solution.py:313
  1.3 0.2 collective-permute-done.1.sibling_ref
  1.5 4.0 %collective-permute-start.2 = (bf16[2,16,1024]{2,1,0:T(8,128)(2,1)S(1)}, bf16[2,16,1024]{2,1,0:T(8,128)(2,1)S(1)}, u32[]{:S(2)}, u32[]{:S(2)}) collective-permute-start(bf16[2,16,1024]{2,1,0:T(8,128)(2,1)S(1)} %both_cores.1), channel_id=1, source_target_pairs={{0,16},{1,17},{4,21},{5,20},{8,24},{9,25},{12,29},{13,28},{16,0},{... | collective-permute-start | bytes 196616 | tf_op jit(solution)/shard_map/ppermute | solution.py:36
  5.5 1.6 %collective-permute-start.6 = (bf16[2,16,1024]{2,1,0:T(8,128)(2,1)S(1)}, bf16[2,16,1024]{2,1,0:T(8,128)(2,1)S(1)}, u32[]{:S(2)}, u32[]{:S(2)}) collective-permute-start(bf16[2,16,1024]{2,1,0:T(8,128)(2,1)S(1)} %both_cores.1), channel_id=1, source_target_pairs={{0,8},{1,9},{4,13},{5,12},{8,0},{9,1},{12,5},{13,4},{16,24},{17,25... | collective-permute-start | bytes 196616 | tf_op jit(solution)/shard_map/ppermute | solution.py:36
  7.1 1.7 %collective-permute-start.8 = (bf16[16,1024]{1,0:T(8,128)(2,1)S(1)}, bf16[16,1024]{1,0:T(8,128)(2,1)S(1)}, u32[]{:S(2)}, u32[]{:S(2)}) collective-permute-start(bf16[16,1024]{1,0:T(8,128)(2,1)S(1)} %copy-done.2), channel_id=1, source_target_pairs={{0,1},{1,0},{2,3},{3,2},{4,5},{5,4},{6,7},{7,6},{8,9},{9,8},{10,11... | collective-permute-start | bytes 98312 | tf_op jit(solution)/shard_map/ppermute | solution.py:26
  9.5 0.0 collective-permute-done.far_ref
  9.5 0.9 %prepare.1 = (bf16[1,512,128]{2,1,0:T(8,128)(2,1)S(1)}, bf16[1,128,512]{2,1,0:T(8,128)(2,1)S(1)}, bf16[6,512,128]{2,1,0:T(8,128)(2,1)S(1)}, bf16[6,128,512]{2,1,0:T(8,128)(2,1)S(1)}, f32[7,8,128]{2,1,0:T(8,128)S(1)}) custom-call(bf16[32,64,256]{2,1,0:T(8,128)(2,1)S(1)} %bitcast.7, s32[4,128]{1,0:T(4,128)S(1)} %get-tuple-element.17.table, ...), custom_call_target="tpu_custom_call" | custom-call | flops 200000000 | bytes 2097152 | tf_op jit(solution)/shard_map/prepare/pallas_call | solution.py:335
  10.5 0.5 %suffix_away.3 = (bf16[272,128]{1,0:T(8,128)(2,1)S(1)}, f32[8,128]{1,0:T(8,128)S(1)}) custom-call(bf16[6,512,128]{2,1,0:T(8,128)(2,1)S(1)} %get-tuple-element.19.keys_ref, bf16[6,128,512]{2,1,0:T(8,128)(2,1)S(1)} %get-tuple-element.20.values_ref, f32[7,8,128]{2,1,0:T(8,128)S(1)} %get-tuple-element.21.member_ref.refs_3_, ...), custom_call_target="tpu_custom_call" | custom-call | flops 200000000 | bytes 2097152 | tf_op jit(solution)/shard_map/suffix_away/pallas_call | solution.py:362
  11.0 0.0 copy-start
  11.0 1.8 %collective-permute-start.3 = (bf16[272,128]{1,0:T(8,128)(2,1)S(1)}, bf16[272,128]{1,0:T(8,128)(2,1)S(1)}, u32[]{:S(2)}, u32[]{:S(2)}) collective-permute-start(bf16[272,128]{1,0:T(8,128)(2,1)S(1)} %get-tuple-element.23), channel_id=1, source_target_pairs={{0,16},{1,17},{4,21},{5,20},{8,24},{9,25},{12,29},{13,28},{16,0},{... | collective-permute-start | bytes 208904 | tf_op jit(solution)/shard_map/ppermute | solution.py:36
  12.7 0.0 collective-permute-done.6.message_ref
  12.8 0.5 %suffix_away.5 = bf16[272,128]{1,0:T(8,128)(2,1)S(1)} custom-call(bf16[6,512,128]{2,1,0:T(8,128)(2,1)S(1)} %get-tuple-element.19.keys_ref, bf16[6,128,512]{2,1,0:T(8,128)(2,1)S(1)} %get-tuple-element.20.values_ref, f32[7,8,128]{2,1,0:T(8,128)S(1)} %get-tuple-element.21.member_ref.refs_3_, bf16[2,16,1024]{2,1,0:T(8,128)(2,1)S(1)} %collective-permute-done.6.message_ref), custom_call_target="tpu_custom_call" | custom-call | flops 200000000 | bytes 2097152 | tf_op jit(solution)/shard_map/suffix_away/pallas_call | solution.py:362
  13.3 2.5 %collective-permute-start.7 = (bf16[272,128]{1,0:T(8,128)(2,1)S(1)}, bf16[272,128]{1,0:T(8,128)(2,1)S(1)}, u32[]{:S(2)}, u32[]{:S(2)}) collective-permute-start(bf16[272,128]{1,0:T(8,128)(2,1)S(1)} %suffix_away.5), channel_id=1, source_target_pairs={{0,8},{1,9},{4,13},{5,12},{8,0},{9,1},{12,5},{13,4},{16,24},{17,25... | collective-permute-start | bytes 208904 | tf_op jit(solution)/shard_map/ppermute | solution.py:36
  15.8 0.5 %suffix_away.4 = bf16[272,128]{1,0:T(8,128)(2,1)S(1)} custom-call(bf16[6,512,128]{2,1,0:T(8,128)(2,1)S(1)} %get-tuple-element.19.keys_ref, bf16[6,128,512]{2,1,0:T(8,128)(2,1)S(1)} %get-tuple-element.20.values_ref, f32[7,8,128]{2,1,0:T(8,128)S(1)} %get-tuple-element.21.member_ref.refs_3_, bf16[2,16,1024]{2,1,0:T(8,128)(2,1)S(1)} %collective-permute-done.4.message_ref), custom_call_target="tpu_custom_call" | custom-call | flops 200000000 | bytes 2097152 | tf_op jit(solution)/shard_map/suffix_away/pallas_call | solution.py:362
  16.3 0.3 %collective-permute-start.5 = (bf16[272,128]{1,0:T(8,128)(2,1)S(1)}, bf16[272,128]{1,0:T(8,128)(2,1)S(1)}, u32[]{:S(2)}, u32[]{:S(2)}) collective-permute-start(bf16[272,128]{1,0:T(8,128)(2,1)S(1)} %suffix_away.4), channel_id=1, source_target_pairs={{0,24},{1,25},{4,29},{5,28},{8,16},{9,17},{12,21},{13,20},{16,8},{... | collective-permute-start | bytes 208904 | tf_op jit(solution)/shard_map/ppermute | solution.py:36
  16.6 1.6 %home_pair_heads.1 = bf16[144,128]{1,0:T(8,128)(2,1)S(1)} custom-call(s32[1]{0:T(128)S(6)} %copy.7.refs_0_, bf16[1,512,128]{2,1,0:T(8,128)(2,1)S(1)} %get-tuple-element.24.refs_1_, bf16[1,128,512]{2,1,0:T(8,128)(2,1)S(1)} %get-tuple-element.25.refs_2_, f32[7,8,128]{2,1,0:T(8,128)S(1)} %get-tuple-element.21.member_ref.refs_3_, ...), custom_call_target="tpu_custom_call" | custom-call | flops 536870912 | bytes 2097152 | tf_op jit(solution)/shard_map/home_pair_heads/pallas_call | solution.py:379
  18.2 0.7 %collective-permute-start.9 = (bf16[144,128]{1,0:T(8,128)(2,1)S(1)}, bf16[144,128]{1,0:T(8,128)(2,1)S(1)}, u32[]{:S(2)}, u32[]{:S(2)}) collective-permute-start(bf16[144,128]{1,0:T(8,128)(2,1)S(1)} %home_pair_heads.1), channel_id=1, source_target_pairs={{0,1},{1,0},{2,3},{3,2},{4,5},{5,4},{6,7},{7,6},{8,9},{9,8},{10,11... | collective-permute-start | bytes 110600 | tf_op jit(solution)/shard_map/ppermute | solution.py:26
  18.9 1.6 %home_own_heads.1 = (f32[128,128]{1,0:T(8,128)S(1)}, f32[8,128]{1,0:T(8,128)S(1)}) custom-call(s32[1]{0:T(128)S(6)} %copy.7.refs_0_, bf16[1,512,128]{2,1,0:T(8,128)(2,1)S(1)} %get-tuple-element.24.refs_1_, bf16[1,128,512]{2,1,0:T(8,128)(2,1)S(1)} %get-tuple-element.25.refs_2_, f32[7,8,128]{2,1,0:T(8,128)S(1)} %get-tuple-element.21.member_ref.refs_3_, ...), custom_call_target="tpu_custom_call" | custom-call | flops 536870912 | bytes 2097152 | tf_op jit(solution)/shard_map/home_own_heads/pallas_call | solution.py:389
  20.5 2.5 %collective-permute-done.5.rest_1_ = bf16[272,128]{1,0:T(8,128)(2,1)S(1)} collective-permute-done((bf16[272,128]{1,0:T(8,128)(2,1)S(1)}, bf16[272,128]{1,0:T(8,128)(2,1)S(1)}, u32[]{:S(2)}, u32[]{:S(2)}) %collective-permute-start.5) | collective-permute-done | bytes 69664 | tf_op jit(solution)/shard_map/ppermute | solution.py:36
  23.0 0.2 collective-permute-start.10
  23.2 1.1 %collective-permute-done.10.rest_4_ = bf16[144,128]{1,0:T(8,128)(2,1)S(1)} collective-permute-done((bf16[144,128]{1,0:T(8,128)(2,1)S(1)}, bf16[144,128]{1,0:T(8,128)(2,1)S(1)}, u32[]{:S(2)}, u32[]{:S(2)}) %collective-permute-start.10) | collective-permute-done | bytes 36896 | tf_op jit(solution)/shard_map/ppermute | solution.py:26
  24.3 0.8 %combine.1 = f32[16,1024]{1,0:T(8,128)} custom-call(bf16[272,128]{1,0:T(8,128)(2,1)S(1)} %collective-permute-done.3.rest_0_, bf16[272,128]{1,0:T(8,128)(2,1)S(1)} %collective-permute-done.5.rest_1_, bf16[272,128]{1,0:T(8,128)(2,1)S(1)} %collective-permute-done.7.rest_2_, bf16[144,128]{1,0:T(8,128)(2,1)S(1)} %collective-permute-done.9.rest_3_, ...), custom_call_target="tpu_custom_call" | custom-call | tf_op jit(solution)/shard_map/combine/pallas_call | solution.py:408
  (14 shorter events, 0.1 us)
Async XLA Ops:
  0.0 1.5 %collective-permute-start.1 = (bf16[16,1024]{1,0:T(8,128)(2,1)}, bf16[16,1024]{1,0:T(8,128)(2,1)S(1)}, u32[]{:S(2)}, u32[]{:S(2)}) collective-permute-start(bf16[16,1024]{1,0:T(8,128)(2,1)} %refs_0_.3), channel_id=1, source_target_pairs={{0,4},{4,0},{1,5},{5,1},{2,6},{6,2},{3,7},{7,3},{8,12},{12,8},{9,1... | collective-permute-start | bytes 98312 | tf_op jit(solution)/shard_map/ppermute | solution.py:26
  0.5 9.0 %collective-permute-start = (bf16[32,64,256]{2,1,0:T(8,128)(2,1)}, bf16[32,64,256]{2,1,0:T(8,128)(2,1)S(1)}, u32[]{:S(2)}, u32[]{:S(2)}) collective-permute-start(bf16[32,64,256]{2,1,0:T(8,128)(2,1)} %bitcast.6), channel_id=1, source_target_pairs={{0,4},{4,0},{1,5},{5,1},{2,6},{6,2},{3,7},{7,3},{8,12},{12,8},{9,1... | collective-permute-start | bytes 3145736 | tf_op jit(solution)/shard_map/ppermute | solution.py:26
  1.5 5.6 %copy-start.2 = (bf16[16,1024]{1,0:T(8,128)(2,1)S(1)}, bf16[16,1024]{1,0:T(8,128)(2,1)}, u32[]{:S(2)}) copy-start(bf16[16,1024]{1,0:T(8,128)(2,1)} %refs_0_.3) | copy-start | bytes 98308
  1.5 8.0 %copy-start.1 = (bf16[32,1,64,256]{3,2,1,0:T(8,128)(2,1)S(1)}, bf16[32,1,64,256]{3,2,1,0:T(8,128)(2,1)}, u32[]{:S(2)}) copy-start(bf16[32,1,64,256]{3,2,1,0:T(8,128)(2,1)} %param.8) | copy-start | bytes 3145732
  1.5 8.9 %collective-permute-start.2 = (bf16[2,16,1024]{2,1,0:T(8,128)(2,1)S(1)}, bf16[2,16,1024]{2,1,0:T(8,128)(2,1)S(1)}, u32[]{:S(2)}, u32[]{:S(2)}) collective-permute-start(bf16[2,16,1024]{2,1,0:T(8,128)(2,1)S(1)} %both_cores.1), channel_id=1, source_target_pairs={{0,16},{1,17},{4,21},{5,20},{8,24},{9,25},{12,29},{13,28},{16,0},{... | collective-permute-start | bytes 196616 | tf_op jit(solution)/shard_map/ppermute | solution.py:36
  5.5 7.2 %collective-permute-start.6 = (bf16[2,16,1024]{2,1,0:T(8,128)(2,1)S(1)}, bf16[2,16,1024]{2,1,0:T(8,128)(2,1)S(1)}, u32[]{:S(2)}, u32[]{:S(2)}) collective-permute-start(bf16[2,16,1024]{2,1,0:T(8,128)(2,1)S(1)} %both_cores.1), channel_id=1, source_target_pairs={{0,8},{1,9},{4,13},{5,12},{8,0},{9,1},{12,5},{13,4},{16,24},{17,25... | collective-permute-start | bytes 196616 | tf_op jit(solution)/shard_map/ppermute | solution.py:36
  7.1 8.7 %collective-permute-start.4 = (bf16[2,16,1024]{2,1,0:T(8,128)(2,1)S(1)}, bf16[2,16,1024]{2,1,0:T(8,128)(2,1)S(1)}, u32[]{:S(2)}, u32[]{:S(2)}) collective-permute-start(bf16[2,16,1024]{2,1,0:T(8,128)(2,1)S(1)} %both_cores.1), channel_id=1, source_target_pairs={{0,24},{1,25},{4,29},{5,28},{8,16},{9,17},{12,21},{13,20},{16,8},{... | collective-permute-start | bytes 196616 | tf_op jit(solution)/shard_map/ppermute | solution.py:36
  7.1 9.5 %collective-permute-start.8 = (bf16[16,1024]{1,0:T(8,128)(2,1)S(1)}, bf16[16,1024]{1,0:T(8,128)(2,1)S(1)}, u32[]{:S(2)}, u32[]{:S(2)}) collective-permute-start(bf16[16,1024]{1,0:T(8,128)(2,1)S(1)} %copy-done.2), channel_id=1, source_target_pairs={{0,1},{1,0},{2,3},{3,2},{4,5},{5,4},{6,7},{7,6},{8,9},{9,8},{10,11... | collective-permute-start | bytes 98312 | tf_op jit(solution)/shard_map/ppermute | solution.py:26
  11.0 5.6 %copy-start = (bf16[1,1,4096,256]{3,2,1,0:T(8,128)(2,1)S(1)}, bf16[1,1,4096,256]{3,2,1,0:T(8,128)(2,1)}, u32[]{:S(2)}) copy-start(bf16[1,1,4096,256]{3,2,1,0:T(8,128)(2,1)} %param.7) | copy-start | bytes 6291460
  11.0 9.5 %collective-permute-start.3 = (bf16[272,128]{1,0:T(8,128)(2,1)S(1)}, bf16[272,128]{1,0:T(8,128)(2,1)S(1)}, u32[]{:S(2)}, u32[]{:S(2)}) collective-permute-start(bf16[272,128]{1,0:T(8,128)(2,1)S(1)} %get-tuple-element.23), channel_id=1, source_target_pairs={{0,16},{1,17},{4,21},{5,20},{8,24},{9,25},{12,29},{13,28},{16,0},{... | collective-permute-start | bytes 208904 | tf_op jit(solution)/shard_map/ppermute | solution.py:36
  13.3 7.2 %collective-permute-start.7 = (bf16[272,128]{1,0:T(8,128)(2,1)S(1)}, bf16[272,128]{1,0:T(8,128)(2,1)S(1)}, u32[]{:S(2)}, u32[]{:S(2)}) collective-permute-start(bf16[272,128]{1,0:T(8,128)(2,1)S(1)} %suffix_away.5), channel_id=1, source_target_pairs={{0,8},{1,9},{4,13},{5,12},{8,0},{9,1},{12,5},{13,4},{16,24},{17,25... | collective-permute-start | bytes 208904 | tf_op jit(solution)/shard_map/ppermute | solution.py:36
  16.3 6.6 %collective-permute-start.5 = (bf16[272,128]{1,0:T(8,128)(2,1)S(1)}, bf16[272,128]{1,0:T(8,128)(2,1)S(1)}, u32[]{:S(2)}, u32[]{:S(2)}) collective-permute-start(bf16[272,128]{1,0:T(8,128)(2,1)S(1)} %suffix_away.4), channel_id=1, source_target_pairs={{0,24},{1,25},{4,29},{5,28},{8,16},{9,17},{12,21},{13,20},{16,8},{... | collective-permute-start | bytes 208904 | tf_op jit(solution)/shard_map/ppermute | solution.py:36
  18.2 5.0 %collective-permute-start.9 = (bf16[144,128]{1,0:T(8,128)(2,1)S(1)}, bf16[144,128]{1,0:T(8,128)(2,1)S(1)}, u32[]{:S(2)}, u32[]{:S(2)}) collective-permute-start(bf16[144,128]{1,0:T(8,128)(2,1)S(1)} %home_pair_heads.1), channel_id=1, source_target_pairs={{0,1},{1,0},{2,3},{3,2},{4,5},{5,4},{6,7},{7,6},{8,9},{9,8},{10,11... | collective-permute-start | bytes 110600 | tf_op jit(solution)/shard_map/ppermute | solution.py:26
  23.0 1.3 %collective-permute-start.10 = (bf16[144,128]{1,0:T(8,128)(2,1)S(1)}, bf16[144,128]{1,0:T(8,128)(2,1)S(1)}, u32[]{:S(2)}, u32[]{:S(2)}) collective-permute-start(bf16[144,128]{1,0:T(8,128)(2,1)S(1)} %sibling_share.1), channel_id=1, source_target_pairs={{0,4},{4,0},{1,5},{5,1},{2,6},{6,2},{3,7},{7,3},{8,12},{12,8},{9,1... | collective-permute-start | bytes 110600 | tf_op jit(solution)/shard_map/ppermute | solution.py:26

commit v30 on v29

--- a/solution.py
+++ b/solution.py
@@ -15,7 +15,7 @@
 VECS = HEADS * BEAMS
 STAT_ROWS = 16
 CHUNK = 512
-FIRST_MASKS = (2, 1, 3)
+FIRST_MASKS = (3, 2, 1)
 SURELY_VALID = 1024
 
 big_negative = -1e30

time: 25.3 us -> 24.6 us (0.972)
  waiting for transfers between devices: 3.8 us -> 1.67 us
  starting transfers between devices: 13.3 us -> 14.7 us
    ppermute x6, waiting for transfers between devices: 2.48 us -> 0.58 us  [exchanged(): return lax.ppermute(value, ('z', 'core', 'pair'), pairs)]
    ppermute x5, starting transfers between devices: 3.12 us -> 3.88 us  [swapped(): return lax.ppermute(value, axis, [(0, 1), (1, 0)])]
    ppermute x6, starting transfers between devices: 10.2 us -> 10.8 us  [exchanged(): return lax.ppermute(value, ('z', 'core', 'pair'), pairs)]
  transfers between devices with their start and end apart: 11 -> 11, of which waited for: 3 -> 5; matrix products, arithmetic and copies ran while one was open for 0% -> 0% of each run, Pallas kernels for 26% -> 26%
where the time goes in v30:
time: 24.6 us; the launch traced here: 24.4 us
  starting transfers between devices  14.7 us (60%)
  Pallas kernels  7.21 us (29%)
  waiting for transfers between devices  1.67 us (7%)
  between operations  0.77 us (3%)
    ppermute x6, starting transfers between devices, exchanged(): return lax.ppermute(value, ('z', 'core', 'pair'), pairs)  10.8 us
    ppermute x5, starting transfers between devices, swapped(): return lax.ppermute(value, axis, [(0, 1), (1, 0)])  3.88 us
    pallas_call x1, Pallas kernels, on_device(): pl.pallas_call(pair_heads_kernel, out_shape=pltpu.VMEM((HD + STAT_ROWS, V...  1.57 us
    pallas_call x1, Pallas kernels, on_device(): pl.pallas_call(own_heads_kernel, out_shape=(pltpu.VMEM((HD, VECS), jnp.fl...  1.56 us
    pallas_call x3, Pallas kernels, on_device(): pl.pallas_call(functools.partial(away_kernel, 2 * mask - 2), out_shape=ou...  1.53 us
    ppermute x5, waiting for transfers between devices, swapped(): return lax.ppermute(value, axis, [(0, 1), (1, 0)])  1.09 us
    pallas_call x1, Pallas kernels, on_device(): pl.pallas_call(functools.partial(prepare_kernel, capacity), out_shape=(pl...  0.94 us
    pallas_call x1, Pallas kernels, on_device(): pl.pallas_call(stage_kernel, out_shape=tuple((pltpu.VMEM(each.shape, each...  0.79 us
  transfers between devices with their start and end apart: 11, of which 5 were waited for; matrix products, arithmetic and copies ran while one was open for 0% of the time, Pallas kernels for 26%

profile of v30, /device:TPU:0, one launch (start us, length us, event | category | flops | bytes accessed | tf_op | source)
XLA Modules:
  0.0 24.4 jit_solution(15821455557685863266)
XLA Ops:
  0.0 0.5 %collective-permute-start.1 = (bf16[16,1024]{1,0:T(8,128)(2,1)}, bf16[16,1024]{1,0:T(8,128)(2,1)S(1)}, u32[]{:S(2)}, u32[]{:S(2)}) collective-permute-start(bf16[16,1024]{1,0:T(8,128)(2,1)} %refs_0_.3), channel_id=1, source_target_pairs={{0,4},{4,0},{1,5},{5,1},{2,6},{6,2},{3,7},{7,3},{8,12},{12,8},{9,1... | collective-permute-start | bytes 98312 | tf_op jit(solution)/shard_map/ppermute | solution.py:26
  0.5 0.1 collective-permute-start
  0.5 0.8 %stage.1 = (bf16[16,1024]{1,0:T(8,128)(2,1)S(1)}, s32[4,128]{1,0:T(4,128)S(1)}, s32[1,128]{1,0:T(1,128)S(1)}) custom-call(bf16[16,1024]{1,0:T(8,128)(2,1)} %refs_0_.3, s32[4,128]{1,0:T(4,128)} %bitcast.8, s32[1,128]{1,0:T(1,128)} %bitcast.9), custom_call_target="tpu_custom_call" | custom-call | tf_op jit(solution)/shard_map/stage/pallas_call | solution.py:313
  1.3 0.2 collective-permute-done.1.sibling_ref
  1.5 5.0 %collective-permute-start.2 = (bf16[2,16,1024]{2,1,0:T(8,128)(2,1)S(1)}, bf16[2,16,1024]{2,1,0:T(8,128)(2,1)S(1)}, u32[]{:S(2)}, u32[]{:S(2)}) collective-permute-start(bf16[2,16,1024]{2,1,0:T(8,128)(2,1)S(1)} %both_cores.1), channel_id=1, source_target_pairs={{0,24},{1,25},{4,29},{5,28},{8,16},{9,17},{12,21},{13,20},{16,8},{... | collective-permute-start | bytes 196616 | tf_op jit(solution)/shard_map/ppermute | solution.py:36
  6.6 0.6 %collective-permute-start.4 = (bf16[2,16,1024]{2,1,0:T(8,128)(2,1)S(1)}, bf16[2,16,1024]{2,1,0:T(8,128)(2,1)S(1)}, u32[]{:S(2)}, u32[]{:S(2)}) collective-permute-start(bf16[2,16,1024]{2,1,0:T(8,128)(2,1)S(1)} %both_cores.1), channel_id=1, source_target_pairs={{0,8},{1,9},{4,13},{5,12},{8,0},{9,1},{12,5},{13,4},{16,24},{17,25... | collective-permute-start | bytes 196616 | tf_op jit(solution)/shard_map/ppermute | solution.py:36
  7.2 1.6 %collective-permute-start.8 = (bf16[16,1024]{1,0:T(8,128)(2,1)S(1)}, bf16[16,1024]{1,0:T(8,128)(2,1)S(1)}, u32[]{:S(2)}, u32[]{:S(2)}) collective-permute-start(bf16[16,1024]{1,0:T(8,128)(2,1)S(1)} %copy-done.2), channel_id=1, source_target_pairs={{0,1},{1,0},{2,3},{3,2},{4,5},{5,4},{6,7},{7,6},{8,9},{9,8},{10,11... | collective-permute-start | bytes 98312 | tf_op jit(solution)/shard_map/ppermute | solution.py:26
  9.5 0.9 %prepare.1 = (bf16[1,512,128]{2,1,0:T(8,128)(2,1)S(1)}, bf16[1,128,512]{2,1,0:T(8,128)(2,1)S(1)}, bf16[6,512,128]{2,1,0:T(8,128)(2,1)S(1)}, bf16[6,128,512]{2,1,0:T(8,128)(2,1)S(1)}, f32[7,8,128]{2,1,0:T(8,128)S(1)}) custom-call(bf16[32,64,256]{2,1,0:T(8,128)(2,1)S(1)} %bitcast.7, s32[4,128]{1,0:T(4,128)S(1)} %get-tuple-element.17.table, ...), custom_call_target="tpu_custom_call" | custom-call | flops 200000000 | bytes 2097152 | tf_op jit(solution)/shard_map/prepare/pallas_call | solution.py:335
  10.5 0.5 %suffix_away.3 = (bf16[272,128]{1,0:T(8,128)(2,1)S(1)}, f32[8,128]{1,0:T(8,128)S(1)}) custom-call(bf16[6,512,128]{2,1,0:T(8,128)(2,1)S(1)} %get-tuple-element.19.keys_ref, bf16[6,128,512]{2,1,0:T(8,128)(2,1)S(1)} %get-tuple-element.20.values_ref, f32[7,8,128]{2,1,0:T(8,128)S(1)} %get-tuple-element.21.member_ref.refs_3_, ...), custom_call_target="tpu_custom_call" | custom-call | flops 200000000 | bytes 2097152 | tf_op jit(solution)/shard_map/suffix_away/pallas_call | solution.py:362
  11.0 0.0 copy-start
  11.0 3.7 %collective-permute-start.3 = (bf16[272,128]{1,0:T(8,128)(2,1)S(1)}, bf16[272,128]{1,0:T(8,128)(2,1)S(1)}, u32[]{:S(2)}, u32[]{:S(2)}) collective-permute-start(bf16[272,128]{1,0:T(8,128)(2,1)S(1)} %get-tuple-element.23), channel_id=1, source_target_pairs={{0,24},{1,25},{4,29},{5,28},{8,16},{9,17},{12,21},{13,20},{16,8},{... | collective-permute-start | bytes 208904 | tf_op jit(solution)/shard_map/ppermute | solution.py:36
  14.7 0.5 %suffix_away.5 = bf16[272,128]{1,0:T(8,128)(2,1)S(1)} custom-call(bf16[6,512,128]{2,1,0:T(8,128)(2,1)S(1)} %get-tuple-element.19.keys_ref, bf16[6,128,512]{2,1,0:T(8,128)(2,1)S(1)} %get-tuple-element.20.values_ref, f32[7,8,128]{2,1,0:T(8,128)S(1)} %get-tuple-element.21.member_ref.refs_3_, bf16[2,16,1024]{2,1,0:T(8,128)(2,1)S(1)} %collective-permute-done.6.message_ref), custom_call_target="tpu_custom_call" | custom-call | flops 200000000 | bytes 2097152 | tf_op jit(solution)/shard_map/suffix_away/pallas_call | solution.py:362
  15.2 0.1 collective-permute-start.7
  15.3 0.5 %suffix_away.4 = bf16[272,128]{1,0:T(8,128)(2,1)S(1)} custom-call(bf16[6,512,128]{2,1,0:T(8,128)(2,1)S(1)} %get-tuple-element.19.keys_ref, bf16[6,128,512]{2,1,0:T(8,128)(2,1)S(1)} %get-tuple-element.20.values_ref, f32[7,8,128]{2,1,0:T(8,128)S(1)} %get-tuple-element.21.member_ref.refs_3_, bf16[2,16,1024]{2,1,0:T(8,128)(2,1)S(1)} %collective-permute-done.4.message_ref), custom_call_target="tpu_custom_call" | custom-call | flops 200000000 | bytes 2097152 | tf_op jit(solution)/shard_map/suffix_away/pallas_call | solution.py:362
  15.8 1.4 %collective-permute-start.5 = (bf16[272,128]{1,0:T(8,128)(2,1)S(1)}, bf16[272,128]{1,0:T(8,128)(2,1)S(1)}, u32[]{:S(2)}, u32[]{:S(2)}) collective-permute-start(bf16[272,128]{1,0:T(8,128)(2,1)S(1)} %suffix_away.4), channel_id=1, source_target_pairs={{0,8},{1,9},{4,13},{5,12},{8,0},{9,1},{12,5},{13,4},{16,24},{17,25... | collective-permute-start | bytes 208904 | tf_op jit(solution)/shard_map/ppermute | solution.py:36
  17.2 1.6 %home_pair_heads.1 = bf16[144,128]{1,0:T(8,128)(2,1)S(1)} custom-call(s32[1]{0:T(128)S(6)} %copy.7.refs_0_, bf16[1,512,128]{2,1,0:T(8,128)(2,1)S(1)} %get-tuple-element.24.refs_1_, bf16[1,128,512]{2,1,0:T(8,128)(2,1)S(1)} %get-tuple-element.25.refs_2_, f32[7,8,128]{2,1,0:T(8,128)S(1)} %get-tuple-element.21.member_ref.refs_3_, ...), custom_call_target="tpu_custom_call" | custom-call | flops 536870912 | bytes 2097152 | tf_op jit(solution)/shard_map/home_pair_heads/pallas_call | solution.py:379
  18.8 1.3 %collective-permute-start.9 = (bf16[144,128]{1,0:T(8,128)(2,1)S(1)}, bf16[144,128]{1,0:T(8,128)(2,1)S(1)}, u32[]{:S(2)}, u32[]{:S(2)}) collective-permute-start(bf16[144,128]{1,0:T(8,128)(2,1)S(1)} %home_pair_heads.1), channel_id=1, source_target_pairs={{0,1},{1,0},{2,3},{3,2},{4,5},{5,4},{6,7},{7,6},{8,9},{9,8},{10,11... | collective-permute-start | bytes 110600 | tf_op jit(solution)/shard_map/ppermute | solution.py:26
  20.1 1.6 %home_own_heads.1 = (f32[128,128]{1,0:T(8,128)S(1)}, f32[8,128]{1,0:T(8,128)S(1)}) custom-call(s32[1]{0:T(128)S(6)} %copy.7.refs_0_, bf16[1,512,128]{2,1,0:T(8,128)(2,1)S(1)} %get-tuple-element.24.refs_1_, bf16[1,128,512]{2,1,0:T(8,128)(2,1)S(1)} %get-tuple-element.25.refs_2_, f32[7,8,128]{2,1,0:T(8,128)S(1)} %get-tuple-element.21.member_ref.refs_3_, ...), custom_call_target="tpu_custom_call" | custom-call | flops 536870912 | bytes 2097152 | tf_op jit(solution)/shard_map/home_own_heads/pallas_call | solution.py:389
  21.7 0.1 collective-permute-done.7.rest_2_
  21.8 0.4 %collective-permute-done.5.rest_1_ = bf16[272,128]{1,0:T(8,128)(2,1)S(1)} collective-permute-done((bf16[272,128]{1,0:T(8,128)(2,1)S(1)}, bf16[272,128]{1,0:T(8,128)(2,1)S(1)}, u32[]{:S(2)}, u32[]{:S(2)}) %collective-permute-start.5) | collective-permute-done | bytes 69664 | tf_op jit(solution)/shard_map/ppermute | solution.py:36
  22.3 0.4 %collective-permute-start.10 = (bf16[144,128]{1,0:T(8,128)(2,1)S(1)}, bf16[144,128]{1,0:T(8,128)(2,1)S(1)}, u32[]{:S(2)}, u32[]{:S(2)}) collective-permute-start(bf16[144,128]{1,0:T(8,128)(2,1)S(1)} %sibling_share.1), channel_id=1, source_target_pairs={{0,4},{4,0},{1,5},{5,1},{2,6},{6,2},{3,7},{7,3},{8,12},{12,8},{9,1... | collective-permute-start | bytes 110600 | tf_op jit(solution)/shard_map/ppermute | solution.py:26
  22.7 0.6 %collective-permute-done.9.rest_3_ = bf16[144,128]{1,0:T(8,128)(2,1)S(1)} collective-permute-done((bf16[144,128]{1,0:T(8,128)(2,1)S(1)}, bf16[144,128]{1,0:T(8,128)(2,1)S(1)}, u32[]{:S(2)}, u32[]{:S(2)}) %collective-permute-start.9) | collective-permute-done | bytes 36896 | tf_op jit(solution)/shard_map/ppermute | solution.py:26
  23.3 0.3 %collective-permute-done.10.rest_4_ = bf16[144,128]{1,0:T(8,128)(2,1)S(1)} collective-permute-done((bf16[144,128]{1,0:T(8,128)(2,1)S(1)}, bf16[144,128]{1,0:T(8,128)(2,1)S(1)}, u32[]{:S(2)}, u32[]{:S(2)}) %collective-permute-start.10) | collective-permute-done | bytes 36896 | tf_op jit(solution)/shard_map/ppermute | solution.py:26
  23.6 0.8 %combine.1 = f32[16,1024]{1,0:T(8,128)} custom-call(bf16[272,128]{1,0:T(8,128)(2,1)S(1)} %collective-permute-done.3.rest_0_, bf16[272,128]{1,0:T(8,128)(2,1)S(1)} %collective-permute-done.5.rest_1_, bf16[272,128]{1,0:T(8,128)(2,1)S(1)} %collective-permute-done.7.rest_2_, bf16[144,128]{1,0:T(8,128)(2,1)S(1)} %collective-permute-done.9.rest_3_, ...), custom_call_target="tpu_custom_call" | custom-call | tf_op jit(solution)/shard_map/combine/pallas_call | solution.py:408
  (14 shorter events, 0.1 us)
Async XLA Ops:
  0.0 1.5 %collective-permute-start.1 = (bf16[16,1024]{1,0:T(8,128)(2,1)}, bf16[16,1024]{1,0:T(8,128)(2,1)S(1)}, u32[]{:S(2)}, u32[]{:S(2)}) collective-permute-start(bf16[16,1024]{1,0:T(8,128)(2,1)} %refs_0_.3), channel_id=1, source_target_pairs={{0,4},{4,0},{1,5},{5,1},{2,6},{6,2},{3,7},{7,3},{8,12},{12,8},{9,1... | collective-permute-start | bytes 98312 | tf_op jit(solution)/shard_map/ppermute | solution.py:26
  0.5 9.0 %collective-permute-start = (bf16[32,64,256]{2,1,0:T(8,128)(2,1)}, bf16[32,64,256]{2,1,0:T(8,128)(2,1)S(1)}, u32[]{:S(2)}, u32[]{:S(2)}) collective-permute-start(bf16[32,64,256]{2,1,0:T(8,128)(2,1)} %bitcast.6), channel_id=1, source_target_pairs={{0,4},{4,0},{1,5},{5,1},{2,6},{6,2},{3,7},{7,3},{8,12},{12,8},{9,1... | collective-permute-start | bytes 3145736 | tf_op jit(solution)/shard_map/ppermute | solution.py:26
  1.5 5.7 %copy-start.2 = (bf16[16,1024]{1,0:T(8,128)(2,1)S(1)}, bf16[16,1024]{1,0:T(8,128)(2,1)}, u32[]{:S(2)}) copy-start(bf16[16,1024]{1,0:T(8,128)(2,1)} %refs_0_.3) | copy-start | bytes 98308
  1.5 8.0 %copy-start.1 = (bf16[32,1,64,256]{3,2,1,0:T(8,128)(2,1)S(1)}, bf16[32,1,64,256]{3,2,1,0:T(8,128)(2,1)}, u32[]{:S(2)}) copy-start(bf16[32,1,64,256]{3,2,1,0:T(8,128)(2,1)} %param.8) | copy-start | bytes 3145732
  1.5 8.9 %collective-permute-start.2 = (bf16[2,16,1024]{2,1,0:T(8,128)(2,1)S(1)}, bf16[2,16,1024]{2,1,0:T(8,128)(2,1)S(1)}, u32[]{:S(2)}, u32[]{:S(2)}) collective-permute-start(bf16[2,16,1024]{2,1,0:T(8,128)(2,1)S(1)} %both_cores.1), channel_id=1, source_target_pairs={{0,24},{1,25},{4,29},{5,28},{8,16},{9,17},{12,21},{13,20},{16,8},{... | collective-permute-start | bytes 196616 | tf_op jit(solution)/shard_map/ppermute | solution.py:36
  6.6 8.1 %collective-permute-start.6 = (bf16[2,16,1024]{2,1,0:T(8,128)(2,1)S(1)}, bf16[2,16,1024]{2,1,0:T(8,128)(2,1)S(1)}, u32[]{:S(2)}, u32[]{:S(2)}) collective-permute-start(bf16[2,16,1024]{2,1,0:T(8,128)(2,1)S(1)} %both_cores.1), channel_id=1, source_target_pairs={{0,16},{1,17},{4,21},{5,20},{8,24},{9,25},{12,29},{13,28},{16,0},{... | collective-permute-start | bytes 196616 | tf_op jit(solution)/shard_map/ppermute | solution.py:36
  6.6 8.7 %collective-permute-start.4 = (bf16[2,16,1024]{2,1,0:T(8,128)(2,1)S(1)}, bf16[2,16,1024]{2,1,0:T(8,128)(2,1)S(1)}, u32[]{:S(2)}, u32[]{:S(2)}) collective-permute-start(bf16[2,16,1024]{2,1,0:T(8,128)(2,1)S(1)} %both_cores.1), channel_id=1, source_target_pairs={{0,8},{1,9},{4,13},{5,12},{8,0},{9,1},{12,5},{13,4},{16,24},{17,25... | collective-permute-start | bytes 196616 | tf_op jit(solution)/shard_map/ppermute | solution.py:36
  7.2 10.0 %collective-permute-start.8 = (bf16[16,1024]{1,0:T(8,128)(2,1)S(1)}, bf16[16,1024]{1,0:T(8,128)(2,1)S(1)}, u32[]{:S(2)}, u32[]{:S(2)}) collective-permute-start(bf16[16,1024]{1,0:T(8,128)(2,1)S(1)} %copy-done.2), channel_id=1, source_target_pairs={{0,1},{1,0},{2,3},{3,2},{4,5},{5,4},{6,7},{7,6},{8,9},{9,8},{10,11... | collective-permute-start | bytes 98312 | tf_op jit(solution)/shard_map/ppermute | solution.py:26
  11.0 6.3 %copy-start = (bf16[1,1,4096,256]{3,2,1,0:T(8,128)(2,1)S(1)}, bf16[1,1,4096,256]{3,2,1,0:T(8,128)(2,1)}, u32[]{:S(2)}) copy-start(bf16[1,1,4096,256]{3,2,1,0:T(8,128)(2,1)} %param.7) | copy-start | bytes 6291460
  11.0 10.7 %collective-permute-start.3 = (bf16[272,128]{1,0:T(8,128)(2,1)S(1)}, bf16[272,128]{1,0:T(8,128)(2,1)S(1)}, u32[]{:S(2)}, u32[]{:S(2)}) collective-permute-start(bf16[272,128]{1,0:T(8,128)(2,1)S(1)} %get-tuple-element.23), channel_id=1, source_target_pairs={{0,24},{1,25},{4,29},{5,28},{8,16},{9,17},{12,21},{13,20},{16,8},{... | collective-permute-start | bytes 208904 | tf_op jit(solution)/shard_map/ppermute | solution.py:36
  15.2 6.6 %collective-permute-start.7 = (bf16[272,128]{1,0:T(8,128)(2,1)S(1)}, bf16[272,128]{1,0:T(8,128)(2,1)S(1)}, u32[]{:S(2)}, u32[]{:S(2)}) collective-permute-start(bf16[272,128]{1,0:T(8,128)(2,1)S(1)} %suffix_away.5), channel_id=1, source_target_pairs={{0,16},{1,17},{4,21},{5,20},{8,24},{9,25},{12,29},{13,28},{16,0},{... | collective-permute-start | bytes 208904 | tf_op jit(solution)/shard_map/ppermute | solution.py:36
  15.8 6.5 %collective-permute-start.5 = (bf16[272,128]{1,0:T(8,128)(2,1)S(1)}, bf16[272,128]{1,0:T(8,128)(2,1)S(1)}, u32[]{:S(2)}, u32[]{:S(2)}) collective-permute-start(bf16[272,128]{1,0:T(8,128)(2,1)S(1)} %suffix_away.4), channel_id=1, source_target_pairs={{0,8},{1,9},{4,13},{5,12},{8,0},{9,1},{12,5},{13,4},{16,24},{17,25... | collective-permute-start | bytes 208904 | tf_op jit(solution)/shard_map/ppermute | solution.py:36
  18.8 4.5 %collective-permute-start.9 = (bf16[144,128]{1,0:T(8,128)(2,1)S(1)}, bf16[144,128]{1,0:T(8,128)(2,1)S(1)}, u32[]{:S(2)}, u32[]{:S(2)}) collective-permute-start(bf16[144,128]{1,0:T(8,128)(2,1)S(1)} %home_pair_heads.1), channel_id=1, source_target_pairs={{0,1},{1,0},{2,3},{3,2},{4,5},{5,4},{6,7},{7,6},{8,9},{9,8},{10,11... | collective-permute-start | bytes 110600 | tf_op jit(solution)/shard_map/ppermute | solution.py:26
  22.3 1.3 %collective-permute-start.10 = (bf16[144,128]{1,0:T(8,128)(2,1)S(1)}, bf16[144,128]{1,0:T(8,128)(2,1)S(1)}, u32[]{:S(2)}, u32[]{:S(2)}) collective-permute-start(bf16[144,128]{1,0:T(8,128)(2,1)S(1)} %sibling_share.1), channel_id=1, source_target_pairs={{0,4},{4,0},{1,5},{5,1},{2,6},{6,2},{3,7},{7,3},{8,12},{12,8},{9,1... | collective-permute-start | bytes 110600 | tf_op jit(solution)/shard_map/ppermute | solution.py:26

commit v31 on v27

--- a/solution.py
+++ b/solution.py
@@ -101,23 +101,26 @@
 
 
 def store_units(ref, parts):
-    rows = []
-    for i, (top, total, summed) in enumerate(parts):
+    stats = jnp.concatenate([row for top, total, _ in parts for row in (top, total)], axis=0)
+    pieces = three_pieces(stats)
+    padding = jnp.zeros((STAT_ROWS - 3 * stats.shape[0], VECS), jnp.float32)
+    ref[len(parts) * HD :, :] = jnp.concatenate(pieces + [padding], axis=0).astype(jnp.bfloat16)
+    for i, (_, _, summed) in enumerate(parts):
         ref[i * HD : (i + 1) * HD, :] = summed.astype(jnp.bfloat16)
-        rows += three_pieces(top) + three_pieces(total)
-    rows.append(jnp.zeros((STAT_ROWS - len(rows), VECS), jnp.float32))
-    ref[len(parts) * HD :, :] = jnp.concatenate(rows, axis=0).astype(jnp.bfloat16)
 
 
 def load_unit(ref, i=0):
-    sums = ref.shape[0] - STAT_ROWS
-    stats = ref[sums:, :].astype(jnp.float32)
-    if isinstance(i, int):
-        rows = [stats[6 * i + k : 6 * i + k + 1] for k in range(6)]
+    n_parts = ref.shape[0] // HD
+    pieces = ref[n_parts * HD :, :].astype(jnp.float32)
+    rows = 2 * n_parts
+    stats = pieces[:rows] + pieces[rows : 2 * rows] + pieces[2 * rows : 3 * rows]
+    if n_parts == 1:
+        top, total = stats[0:1], stats[1:2]
     else:
-        rows = [jnp.where(i == 0, stats[k : k + 1], stats[6 + k : 7 + k]) for k in range(6)]
+        top = jnp.where(i == 0, stats[0:1], stats[2:3])
+        total = jnp.where(i == 0, stats[1:2], stats[3:4])
     part = ref[pl.ds(pl.multiple_of(i * HD, HD), HD), :]
-    return rows[0] + rows[1] + rows[2], rows[3] + rows[4] + rows[5], part.astype(jnp.float32)
+    return top, total, part.astype(jnp.float32)
 
 
 def count(left, right):

time: 24.5 us -> 24.4 us (level)
  no operation moved by 1% of the time
where the time goes in v31:
time: 24.4 us; the launch traced here: 24.2 us
  starting transfers between devices  14.5 us (59%)
  Pallas kernels  7.17 us (29%)
  waiting for transfers between devices  1.8 us (7%)
  between operations  0.76 us (3%)
    ppermute x6, starting transfers between devices, exchanged(): return lax.ppermute(value, ('z', 'core', 'pair'), pairs)  11.3 us
    ppermute x5, starting transfers between devices, swapped(): return lax.ppermute(value, axis, [(0, 1), (1, 0)])  3.18 us
    pallas_call x1, Pallas kernels, on_device(): pl.pallas_call(pair_heads_kernel, out_shape=pltpu.VMEM((HD + STAT_ROWS, V...  1.57 us
    pallas_call x1, Pallas kernels, on_device(): pl.pallas_call(own_heads_kernel, out_shape=(pltpu.VMEM((HD, VECS), jnp.fl...  1.56 us
    pallas_call x3, Pallas kernels, on_device(): pl.pallas_call(functools.partial(away_kernel, 2 * mask - 2), out_shape=ou...  1.5 us
    ppermute x5, waiting for transfers between devices, swapped(): return lax.ppermute(value, axis, [(0, 1), (1, 0)])  1.11 us
    pallas_call x1, Pallas kernels, on_device(): pl.pallas_call(functools.partial(prepare_kernel, capacity), out_shape=(pl...  0.94 us
    pallas_call x1, Pallas kernels, on_device(): pl.pallas_call(stage_kernel, out_shape=tuple((pltpu.VMEM(each.shape, each...  0.79 us
  transfers between devices with their start and end apart: 11, of which 4 were waited for; matrix products, arithmetic and copies ran while one was open for 0% of the time, Pallas kernels for 26%

profile of v31, /device:TPU:0, one launch (start us, length us, event | category | flops | bytes accessed | tf_op | source)
XLA Modules:
  0.0 24.2 jit_solution(9989049438506683358)
XLA Ops:
  0.0 0.5 %collective-permute-start.1 = (bf16[16,1024]{1,0:T(8,128)(2,1)}, bf16[16,1024]{1,0:T(8,128)(2,1)S(1)}, u32[]{:S(2)}, u32[]{:S(2)}) collective-permute-start(bf16[16,1024]{1,0:T(8,128)(2,1)} %refs_0_.3), channel_id=1, source_target_pairs={{0,4},{4,0},{1,5},{5,1},{2,6},{6,2},{3,7},{7,3},{8,12},{12,8},{9,1... | collective-permute-start | bytes 98312 | tf_op jit(solution)/shard_map/ppermute | solution.py:26
  0.5 0.1 collective-permute-start
  0.5 0.8 %stage.1 = (bf16[16,1024]{1,0:T(8,128)(2,1)S(1)}, s32[4,128]{1,0:T(4,128)S(1)}, s32[1,128]{1,0:T(1,128)S(1)}) custom-call(bf16[16,1024]{1,0:T(8,128)(2,1)} %refs_0_.3, s32[4,128]{1,0:T(4,128)} %bitcast.8, s32[1,128]{1,0:T(1,128)} %bitcast.9), custom_call_target="tpu_custom_call" | custom-call | tf_op jit(solution)/shard_map/stage/pallas_call | solution.py:316
  1.3 0.2 collective-permute-done.1.sibling_ref
  1.5 4.0 %collective-permute-start.2 = (bf16[2,16,1024]{2,1,0:T(8,128)(2,1)S(1)}, bf16[2,16,1024]{2,1,0:T(8,128)(2,1)S(1)}, u32[]{:S(2)}, u32[]{:S(2)}) collective-permute-start(bf16[2,16,1024]{2,1,0:T(8,128)(2,1)S(1)} %both_cores.1), channel_id=1, source_target_pairs={{0,16},{1,17},{4,21},{5,20},{8,24},{9,25},{12,29},{13,28},{16,0},{... | collective-permute-start | bytes 196616 | tf_op jit(solution)/shard_map/ppermute | solution.py:36
  5.5 1.3 %collective-permute-start.6 = (bf16[2,16,1024]{2,1,0:T(8,128)(2,1)S(1)}, bf16[2,16,1024]{2,1,0:T(8,128)(2,1)S(1)}, u32[]{:S(2)}, u32[]{:S(2)}) collective-permute-start(bf16[2,16,1024]{2,1,0:T(8,128)(2,1)S(1)} %both_cores.1), channel_id=1, source_target_pairs={{0,24},{1,25},{4,29},{5,28},{8,16},{9,17},{12,21},{13,20},{16,8},{... | collective-permute-start | bytes 196616 | tf_op jit(solution)/shard_map/ppermute | solution.py:36
  6.9 0.2 collective-permute-start.4
  7.1 1.5 %collective-permute-start.8 = (bf16[16,1024]{1,0:T(8,128)(2,1)S(1)}, bf16[16,1024]{1,0:T(8,128)(2,1)S(1)}, u32[]{:S(2)}, u32[]{:S(2)}) collective-permute-start(bf16[16,1024]{1,0:T(8,128)(2,1)S(1)} %copy-done.2), channel_id=1, source_target_pairs={{0,1},{1,0},{2,3},{3,2},{4,5},{5,4},{6,7},{7,6},{8,9},{9,8},{10,11... | collective-permute-start | bytes 98312 | tf_op jit(solution)/shard_map/ppermute | solution.py:26
  9.3 0.9 %prepare.1 = (bf16[1,512,128]{2,1,0:T(8,128)(2,1)S(1)}, bf16[1,128,512]{2,1,0:T(8,128)(2,1)S(1)}, bf16[6,512,128]{2,1,0:T(8,128)(2,1)S(1)}, bf16[6,128,512]{2,1,0:T(8,128)(2,1)S(1)}, f32[7,8,128]{2,1,0:T(8,128)S(1)}) custom-call(bf16[32,64,256]{2,1,0:T(8,128)(2,1)S(1)} %bitcast.7, s32[4,128]{1,0:T(4,128)S(1)} %get-tuple-element.17.table, ...), custom_call_target="tpu_custom_call" | custom-call | flops 200000000 | bytes 2097152 | tf_op jit(solution)/shard_map/prepare/pallas_call | solution.py:338
  10.2 0.5 %suffix_away.3 = (bf16[272,128]{1,0:T(8,128)(2,1)S(1)}, f32[8,128]{1,0:T(8,128)S(1)}) custom-call(bf16[6,512,128]{2,1,0:T(8,128)(2,1)S(1)} %get-tuple-element.19.keys_ref, bf16[6,128,512]{2,1,0:T(8,128)(2,1)S(1)} %get-tuple-element.20.values_ref, f32[7,8,128]{2,1,0:T(8,128)S(1)} %get-tuple-element.21.member_ref.refs_3_, ...), custom_call_target="tpu_custom_call" | custom-call | flops 200000000 | bytes 2097152 | tf_op jit(solution)/shard_map/suffix_away/pallas_call | solution.py:365
  10.7 0.0 copy-start
  10.8 2.9 %collective-permute-start.3 = (bf16[272,128]{1,0:T(8,128)(2,1)S(1)}, bf16[272,128]{1,0:T(8,128)(2,1)S(1)}, u32[]{:S(2)}, u32[]{:S(2)}) collective-permute-start(bf16[272,128]{1,0:T(8,128)(2,1)S(1)} %get-tuple-element.23), channel_id=1, source_target_pairs={{0,16},{1,17},{4,21},{5,20},{8,24},{9,25},{12,29},{13,28},{16,0},{... | collective-permute-start | bytes 208904 | tf_op jit(solution)/shard_map/ppermute | solution.py:36
  13.6 0.5 %suffix_away.5 = bf16[272,128]{1,0:T(8,128)(2,1)S(1)} custom-call(bf16[6,512,128]{2,1,0:T(8,128)(2,1)S(1)} %get-tuple-element.19.keys_ref, bf16[6,128,512]{2,1,0:T(8,128)(2,1)S(1)} %get-tuple-element.20.values_ref, f32[7,8,128]{2,1,0:T(8,128)S(1)} %get-tuple-element.21.member_ref.refs_3_, bf16[2,16,1024]{2,1,0:T(8,128)(2,1)S(1)} %collective-permute-done.6.message_ref), custom_call_target="tpu_custom_call" | custom-call | flops 200000000 | bytes 2097152 | tf_op jit(solution)/shard_map/suffix_away/pallas_call | solution.py:365
  14.1 2.2 %collective-permute-start.7 = (bf16[272,128]{1,0:T(8,128)(2,1)S(1)}, bf16[272,128]{1,0:T(8,128)(2,1)S(1)}, u32[]{:S(2)}, u32[]{:S(2)}) collective-permute-start(bf16[272,128]{1,0:T(8,128)(2,1)S(1)} %suffix_away.5), channel_id=1, source_target_pairs={{0,24},{1,25},{4,29},{5,28},{8,16},{9,17},{12,21},{13,20},{16,8},{... | collective-permute-start | bytes 208904 | tf_op jit(solution)/shard_map/ppermute | solution.py:36
  16.4 0.5 %suffix_away.4 = bf16[272,128]{1,0:T(8,128)(2,1)S(1)} custom-call(bf16[6,512,128]{2,1,0:T(8,128)(2,1)S(1)} %get-tuple-element.19.keys_ref, bf16[6,128,512]{2,1,0:T(8,128)(2,1)S(1)} %get-tuple-element.20.values_ref, f32[7,8,128]{2,1,0:T(8,128)S(1)} %get-tuple-element.21.member_ref.refs_3_, bf16[2,16,1024]{2,1,0:T(8,128)(2,1)S(1)} %collective-permute-done.4.message_ref), custom_call_target="tpu_custom_call" | custom-call | flops 200000000 | bytes 2097152 | tf_op jit(solution)/shard_map/suffix_away/pallas_call | solution.py:365
  16.9 0.6 %collective-permute-start.5 = (bf16[272,128]{1,0:T(8,128)(2,1)S(1)}, bf16[272,128]{1,0:T(8,128)(2,1)S(1)}, u32[]{:S(2)}, u32[]{:S(2)}) collective-permute-start(bf16[272,128]{1,0:T(8,128)(2,1)S(1)} %suffix_away.4), channel_id=1, source_target_pairs={{0,8},{1,9},{4,13},{5,12},{8,0},{9,1},{12,5},{13,4},{16,24},{17,25... | collective-permute-start | bytes 208904 | tf_op jit(solution)/shard_map/ppermute | solution.py:36
  17.5 1.6 %home_pair_heads.1 = bf16[144,128]{1,0:T(8,128)(2,1)S(1)} custom-call(s32[1]{0:T(128)S(6)} %copy.7.refs_0_, bf16[1,512,128]{2,1,0:T(8,128)(2,1)S(1)} %get-tuple-element.24.refs_1_, bf16[1,128,512]{2,1,0:T(8,128)(2,1)S(1)} %get-tuple-element.25.refs_2_, f32[7,8,128]{2,1,0:T(8,128)S(1)} %get-tuple-element.21.member_ref.refs_3_, ...), custom_call_target="tpu_custom_call" | custom-call | flops 536870912 | bytes 2097152 | tf_op jit(solution)/shard_map/home_pair_heads/pallas_call | solution.py:382
  19.1 0.8 %collective-permute-start.9 = (bf16[144,128]{1,0:T(8,128)(2,1)S(1)}, bf16[144,128]{1,0:T(8,128)(2,1)S(1)}, u32[]{:S(2)}, u32[]{:S(2)}) collective-permute-start(bf16[144,128]{1,0:T(8,128)(2,1)S(1)} %home_pair_heads.1), channel_id=1, source_target_pairs={{0,1},{1,0},{2,3},{3,2},{4,5},{5,4},{6,7},{7,6},{8,9},{9,8},{10,11... | collective-permute-start | bytes 110600 | tf_op jit(solution)/shard_map/ppermute | solution.py:26
  19.9 1.6 %home_own_heads.1 = (f32[128,128]{1,0:T(8,128)S(1)}, f32[8,128]{1,0:T(8,128)S(1)}) custom-call(s32[1]{0:T(128)S(6)} %copy.7.refs_0_, bf16[1,512,128]{2,1,0:T(8,128)(2,1)S(1)} %get-tuple-element.24.refs_1_, bf16[1,128,512]{2,1,0:T(8,128)(2,1)S(1)} %get-tuple-element.25.refs_2_, f32[7,8,128]{2,1,0:T(8,128)S(1)} %get-tuple-element.21.member_ref.refs_3_, ...), custom_call_target="tpu_custom_call" | custom-call | flops 536870912 | bytes 2097152 | tf_op jit(solution)/shard_map/home_own_heads/pallas_call | solution.py:392
  21.5 0.7 %collective-permute-done.5.rest_1_ = bf16[272,128]{1,0:T(8,128)(2,1)S(1)} collective-permute-done((bf16[272,128]{1,0:T(8,128)(2,1)S(1)}, bf16[272,128]{1,0:T(8,128)(2,1)S(1)}, u32[]{:S(2)}, u32[]{:S(2)}) %collective-permute-start.5) | collective-permute-done | bytes 69664 | tf_op jit(solution)/shard_map/ppermute | solution.py:36
  22.2 0.4 %collective-permute-start.10 = (bf16[144,128]{1,0:T(8,128)(2,1)S(1)}, bf16[144,128]{1,0:T(8,128)(2,1)S(1)}, u32[]{:S(2)}, u32[]{:S(2)}) collective-permute-start(bf16[144,128]{1,0:T(8,128)(2,1)S(1)} %sibling_share.1), channel_id=1, source_target_pairs={{0,4},{4,0},{1,5},{5,1},{2,6},{6,2},{3,7},{7,3},{8,12},{12,8},{9,1... | collective-permute-start | bytes 110600 | tf_op jit(solution)/shard_map/ppermute | solution.py:26
  22.6 0.5 %collective-permute-done.9.rest_3_ = bf16[144,128]{1,0:T(8,128)(2,1)S(1)} collective-permute-done((bf16[144,128]{1,0:T(8,128)(2,1)S(1)}, bf16[144,128]{1,0:T(8,128)(2,1)S(1)}, u32[]{:S(2)}, u32[]{:S(2)}) %collective-permute-start.9) | collective-permute-done | bytes 36896 | tf_op jit(solution)/shard_map/ppermute | solution.py:26
  23.1 0.4 %collective-permute-done.10.rest_4_ = bf16[144,128]{1,0:T(8,128)(2,1)S(1)} collective-permute-done((bf16[144,128]{1,0:T(8,128)(2,1)S(1)}, bf16[144,128]{1,0:T(8,128)(2,1)S(1)}, u32[]{:S(2)}, u32[]{:S(2)}) %collective-permute-start.10) | collective-permute-done | bytes 36896 | tf_op jit(solution)/shard_map/ppermute | solution.py:26
  23.5 0.8 %combine.1 = f32[16,1024]{1,0:T(8,128)} custom-call(bf16[272,128]{1,0:T(8,128)(2,1)S(1)} %collective-permute-done.3.rest_0_, bf16[272,128]{1,0:T(8,128)(2,1)S(1)} %collective-permute-done.5.rest_1_, bf16[272,128]{1,0:T(8,128)(2,1)S(1)} %collective-permute-done.7.rest_2_, bf16[144,128]{1,0:T(8,128)(2,1)S(1)} %collective-permute-done.9.rest_3_, ...), custom_call_target="tpu_custom_call" | custom-call | tf_op jit(solution)/shard_map/combine/pallas_call | solution.py:411
  (14 shorter events, 0.1 us)
Async XLA Ops:
  0.0 1.5 %collective-permute-start.1 = (bf16[16,1024]{1,0:T(8,128)(2,1)}, bf16[16,1024]{1,0:T(8,128)(2,1)S(1)}, u32[]{:S(2)}, u32[]{:S(2)}) collective-permute-start(bf16[16,1024]{1,0:T(8,128)(2,1)} %refs_0_.3), channel_id=1, source_target_pairs={{0,4},{4,0},{1,5},{5,1},{2,6},{6,2},{3,7},{7,3},{8,12},{12,8},{9,1... | collective-permute-start | bytes 98312 | tf_op jit(solution)/shard_map/ppermute | solution.py:26
  0.5 8.8 %collective-permute-start = (bf16[32,64,256]{2,1,0:T(8,128)(2,1)}, bf16[32,64,256]{2,1,0:T(8,128)(2,1)S(1)}, u32[]{:S(2)}, u32[]{:S(2)}) collective-permute-start(bf16[32,64,256]{2,1,0:T(8,128)(2,1)} %bitcast.6), channel_id=1, source_target_pairs={{0,4},{4,0},{1,5},{5,1},{2,6},{6,2},{3,7},{7,3},{8,12},{12,8},{9,1... | collective-permute-start | bytes 3145736 | tf_op jit(solution)/shard_map/ppermute | solution.py:26
  1.5 5.6 %copy-start.2 = (bf16[16,1024]{1,0:T(8,128)(2,1)S(1)}, bf16[16,1024]{1,0:T(8,128)(2,1)}, u32[]{:S(2)}) copy-start(bf16[16,1024]{1,0:T(8,128)(2,1)} %refs_0_.3) | copy-start | bytes 98308
  1.5 7.8 %copy-start.1 = (bf16[32,1,64,256]{3,2,1,0:T(8,128)(2,1)S(1)}, bf16[32,1,64,256]{3,2,1,0:T(8,128)(2,1)}, u32[]{:S(2)}) copy-start(bf16[32,1,64,256]{3,2,1,0:T(8,128)(2,1)} %param.8) | copy-start | bytes 3145732
  1.5 8.7 %collective-permute-start.2 = (bf16[2,16,1024]{2,1,0:T(8,128)(2,1)S(1)}, bf16[2,16,1024]{2,1,0:T(8,128)(2,1)S(1)}, u32[]{:S(2)}, u32[]{:S(2)}) collective-permute-start(bf16[2,16,1024]{2,1,0:T(8,128)(2,1)S(1)} %both_cores.1), channel_id=1, source_target_pairs={{0,16},{1,17},{4,21},{5,20},{8,24},{9,25},{12,29},{13,28},{16,0},{... | collective-permute-start | bytes 196616 | tf_op jit(solution)/shard_map/ppermute | solution.py:36
  5.5 8.1 %collective-permute-start.6 = (bf16[2,16,1024]{2,1,0:T(8,128)(2,1)S(1)}, bf16[2,16,1024]{2,1,0:T(8,128)(2,1)S(1)}, u32[]{:S(2)}, u32[]{:S(2)}) collective-permute-start(bf16[2,16,1024]{2,1,0:T(8,128)(2,1)S(1)} %both_cores.1), channel_id=1, source_target_pairs={{0,24},{1,25},{4,29},{5,28},{8,16},{9,17},{12,21},{13,20},{16,8},{... | collective-permute-start | bytes 196616 | tf_op jit(solution)/shard_map/ppermute | solution.py:36
  6.9 9.5 %collective-permute-start.4 = (bf16[2,16,1024]{2,1,0:T(8,128)(2,1)S(1)}, bf16[2,16,1024]{2,1,0:T(8,128)(2,1)S(1)}, u32[]{:S(2)}, u32[]{:S(2)}) collective-permute-start(bf16[2,16,1024]{2,1,0:T(8,128)(2,1)S(1)} %both_cores.1), channel_id=1, source_target_pairs={{0,8},{1,9},{4,13},{5,12},{8,0},{9,1},{12,5},{13,4},{16,24},{17,25... | collective-permute-start | bytes 196616 | tf_op jit(solution)/shard_map/ppermute | solution.py:36
  7.1 10.4 %collective-permute-start.8 = (bf16[16,1024]{1,0:T(8,128)(2,1)S(1)}, bf16[16,1024]{1,0:T(8,128)(2,1)S(1)}, u32[]{:S(2)}, u32[]{:S(2)}) collective-permute-start(bf16[16,1024]{1,0:T(8,128)(2,1)S(1)} %copy-done.2), channel_id=1, source_target_pairs={{0,1},{1,0},{2,3},{3,2},{4,5},{5,4},{6,7},{7,6},{8,9},{9,8},{10,11... | collective-permute-start | bytes 98312 | tf_op jit(solution)/shard_map/ppermute | solution.py:26
  10.7 6.8 %copy-start = (bf16[1,1,4096,256]{3,2,1,0:T(8,128)(2,1)S(1)}, bf16[1,1,4096,256]{3,2,1,0:T(8,128)(2,1)}, u32[]{:S(2)}) copy-start(bf16[1,1,4096,256]{3,2,1,0:T(8,128)(2,1)} %param.7) | copy-start | bytes 6291460
  10.8 10.7 %collective-permute-start.3 = (bf16[272,128]{1,0:T(8,128)(2,1)S(1)}, bf16[272,128]{1,0:T(8,128)(2,1)S(1)}, u32[]{:S(2)}, u32[]{:S(2)}) collective-permute-start(bf16[272,128]{1,0:T(8,128)(2,1)S(1)} %get-tuple-element.23), channel_id=1, source_target_pairs={{0,16},{1,17},{4,21},{5,20},{8,24},{9,25},{12,29},{13,28},{16,0},{... | collective-permute-start | bytes 208904 | tf_op jit(solution)/shard_map/ppermute | solution.py:36
  14.1 7.3 %collective-permute-start.7 = (bf16[272,128]{1,0:T(8,128)(2,1)S(1)}, bf16[272,128]{1,0:T(8,128)(2,1)S(1)}, u32[]{:S(2)}, u32[]{:S(2)}) collective-permute-start(bf16[272,128]{1,0:T(8,128)(2,1)S(1)} %suffix_away.5), channel_id=1, source_target_pairs={{0,24},{1,25},{4,29},{5,28},{8,16},{9,17},{12,21},{13,20},{16,8},{... | collective-permute-start | bytes 208904 | tf_op jit(solution)/shard_map/ppermute | solution.py:36
  16.9 5.3 %collective-permute-start.5 = (bf16[272,128]{1,0:T(8,128)(2,1)S(1)}, bf16[272,128]{1,0:T(8,128)(2,1)S(1)}, u32[]{:S(2)}, u32[]{:S(2)}) collective-permute-start(bf16[272,128]{1,0:T(8,128)(2,1)S(1)} %suffix_away.4), channel_id=1, source_target_pairs={{0,8},{1,9},{4,13},{5,12},{8,0},{9,1},{12,5},{13,4},{16,24},{17,25... | collective-permute-start | bytes 208904 | tf_op jit(solution)/shard_map/ppermute | solution.py:36
  19.1 4.0 %collective-permute-start.9 = (bf16[144,128]{1,0:T(8,128)(2,1)S(1)}, bf16[144,128]{1,0:T(8,128)(2,1)S(1)}, u32[]{:S(2)}, u32[]{:S(2)}) collective-permute-start(bf16[144,128]{1,0:T(8,128)(2,1)S(1)} %home_pair_heads.1), channel_id=1, source_target_pairs={{0,1},{1,0},{2,3},{3,2},{4,5},{5,4},{6,7},{7,6},{8,9},{9,8},{10,11... | collective-permute-start | bytes 110600 | tf_op jit(solution)/shard_map/ppermute | solution.py:26
  22.2 1.3 %collective-permute-start.10 = (bf16[144,128]{1,0:T(8,128)(2,1)S(1)}, bf16[144,128]{1,0:T(8,128)(2,1)S(1)}, u32[]{:S(2)}, u32[]{:S(2)}) collective-permute-start(bf16[144,128]{1,0:T(8,128)(2,1)S(1)} %sibling_share.1), channel_id=1, source_target_pairs={{0,4},{4,0},{1,5},{5,1},{2,6},{6,2},{3,7},{7,3},{8,12},{12,8},{9,1... | collective-permute-start | bytes 110600 | tf_op jit(solution)/shard_map/ppermute | solution.py:26

commit v32 on v31

--- a/solution.py
+++ b/solution.py
@@ -279,11 +279,17 @@
     store_units(out_ref, [merged([load_unit(unit, 1 - core) for unit in units])])
 
 
-def final_kernel(*rest):
-    units, (last_ref, shared_ref, summed_ref, stats_ref, out_ref) = rest[:-5], rest[-5:]
+def own_share_kernel(*rest):
+    units, (summed_ref, stats_ref, out_ref, out_stats_ref) = rest[:-4], rest[-4:]
     core = lax.axis_index("core")
     parts = [load_unit(unit, core) for unit in units]
-    parts += [load_unit(last_ref), load_unit(shared_ref)]
+    parts.append((stats_ref[0:1], stats_ref[1:2], summed_ref[...]))
+    top, total, out_ref[...] = merged(parts)
+    out_stats_ref[...] = jnp.concatenate([top, total, jnp.zeros((6, VECS), jnp.float32)], axis=0)
+
+
+def final_kernel(last_ref, shared_ref, summed_ref, stats_ref, out_ref):
+    parts = [load_unit(last_ref), load_unit(shared_ref)]
     parts.append((stats_ref[0:1], stats_ref[1:2], summed_ref[...]))
     _, total, summed = merged(parts)
     attended = (summed / total).T
@@ -408,14 +414,24 @@
         name="sibling_share",
     )(*received, stats)
 
+    partial = (pltpu.VMEM((HD, VECS), jnp.float32), pltpu.VMEM((8, VECS), jnp.float32))
+    summed, stats = pl.pallas_call(
+        own_share_kernel,
+        out_shape=partial,
+        in_specs=[vmem] * (n_req + 1),
+        out_specs=(vmem,) * 2,
+        compiler_params=params,
+        name="own_share",
+    )(*received, summed, stats)
+
     return pl.pallas_call(
         final_kernel,
         out_shape=jax.ShapeDtypeStruct((BEAMS, HEADS * HD), jnp.float32),
-        in_specs=[vmem] * (3 + n_req),
+        in_specs=[vmem] * 4,
         out_specs=vmem,
         compiler_params=params,
         name="combine",
-    )(*received, last, swapped(share, "core"), summed, stats)
+    )(last, swapped(share, "core"), summed, stats)
 
 
 def solution(mesh):

time: 24.4 us -> 24.4 us (level)
  transfers between devices with their start and end apart: 11 -> 11, of which waited for: 4 -> 4; matrix products, arithmetic and copies ran while one was open for 0% -> 0% of each run, Pallas kernels for 26% -> 27%
where the time goes in v32:
time: 24.4 us; the launch traced here: 24.2 us
  starting transfers between devices  14.5 us (59%)
  Pallas kernels  7.2 us (30%)
  waiting for transfers between devices  1.79 us (7%)
  between operations  0.76 us (3%)
    ppermute x6, starting transfers between devices, exchanged(): return lax.ppermute(value, ('z', 'core', 'pair'), pairs)  11.3 us
    ppermute x5, starting transfers between devices, swapped(): return lax.ppermute(value, axis, [(0, 1), (1, 0)])  3.15 us
    pallas_call x1, Pallas kernels, on_device(): pl.pallas_call(pair_heads_kernel, out_shape=pltpu.VMEM((HD + STAT_ROWS, V...  1.57 us
    pallas_call x1, Pallas kernels, on_device(): pl.pallas_call(own_heads_kernel, out_shape=(pltpu.VMEM((HD, VECS), jnp.fl...  1.56 us
    pallas_call x3, Pallas kernels, on_device(): pl.pallas_call(functools.partial(away_kernel, 2 * mask - 2), out_shape=ou...  1.5 us
    ppermute x5, waiting for transfers between devices, swapped(): return lax.ppermute(value, axis, [(0, 1), (1, 0)])  1.1 us
    pallas_call x1, Pallas kernels, on_device(): pl.pallas_call(functools.partial(prepare_kernel, capacity), out_shape=(pl...  0.94 us
    pallas_call x1, Pallas kernels, on_device(): pl.pallas_call(stage_kernel, out_shape=tuple((pltpu.VMEM(each.shape, each...  0.79 us
  transfers between devices with their start and end apart: 11, of which 4 were waited for; matrix products, arithmetic and copies ran while one was open for 0% of the time, Pallas kernels for 27%

profile of v32, /device:TPU:0, one launch (start us, length us, event | category | flops | bytes accessed | tf_op | source)
XLA Modules:
  0.0 24.2 jit_solution(5976494559545464281)
XLA Ops:
  0.0 0.5 %collective-permute-start.2 = (bf16[16,1024]{1,0:T(8,128)(2,1)}, bf16[16,1024]{1,0:T(8,128)(2,1)S(1)}, u32[]{:S(2)}, u32[]{:S(2)}) collective-permute-start(bf16[16,1024]{1,0:T(8,128)(2,1)} %refs_0_.3), channel_id=1, source_target_pairs={{0,4},{4,0},{1,5},{5,1},{2,6},{6,2},{3,7},{7,3},{8,12},{12,8},{9,1... | collective-permute-start | bytes 98312 | tf_op jit(solution)/shard_map/ppermute | solution.py:26
  0.5 0.1 collective-permute-start
  0.5 0.8 %stage.1 = (bf16[16,1024]{1,0:T(8,128)(2,1)S(1)}, s32[4,128]{1,0:T(4,128)S(1)}, s32[1,128]{1,0:T(1,128)S(1)}) custom-call(bf16[16,1024]{1,0:T(8,128)(2,1)} %refs_0_.3, s32[4,128]{1,0:T(4,128)} %bitcast.8, s32[1,128]{1,0:T(1,128)} %bitcast.9), custom_call_target="tpu_custom_call" | custom-call | tf_op jit(solution)/shard_map/stage/pallas_call | solution.py:322
  1.3 0.2 collective-permute-done.2.sibling_ref
  1.5 4.0 %collective-permute-start.3 = (bf16[2,16,1024]{2,1,0:T(8,128)(2,1)S(1)}, bf16[2,16,1024]{2,1,0:T(8,128)(2,1)S(1)}, u32[]{:S(2)}, u32[]{:S(2)}) collective-permute-start(bf16[2,16,1024]{2,1,0:T(8,128)(2,1)S(1)} %both_cores.1), channel_id=1, source_target_pairs={{0,16},{1,17},{4,21},{5,20},{8,24},{9,25},{12,29},{13,28},{16,0},{... | collective-permute-start | bytes 196616 | tf_op jit(solution)/shard_map/ppermute | solution.py:36
  5.5 1.3 %collective-permute-start.8 = (bf16[2,16,1024]{2,1,0:T(8,128)(2,1)S(1)}, bf16[2,16,1024]{2,1,0:T(8,128)(2,1)S(1)}, u32[]{:S(2)}, u32[]{:S(2)}) collective-permute-start(bf16[2,16,1024]{2,1,0:T(8,128)(2,1)S(1)} %both_cores.1), channel_id=1, source_target_pairs={{0,24},{1,25},{4,29},{5,28},{8,16},{9,17},{12,21},{13,20},{16,8},{... | collective-permute-start | bytes 196616 | tf_op jit(solution)/shard_map/ppermute | solution.py:36
  6.9 0.2 collective-permute-start.6
  7.1 1.5 %collective-permute-start.1 = (bf16[16,1024]{1,0:T(8,128)(2,1)S(1)}, bf16[16,1024]{1,0:T(8,128)(2,1)S(1)}, u32[]{:S(2)}, u32[]{:S(2)}) collective-permute-start(bf16[16,1024]{1,0:T(8,128)(2,1)S(1)} %copy-done.2), channel_id=1, source_target_pairs={{0,1},{1,0},{2,3},{3,2},{4,5},{5,4},{6,7},{7,6},{8,9},{9,8},{10,11... | collective-permute-start | bytes 98312 | tf_op jit(solution)/shard_map/ppermute | solution.py:26
  9.3 0.9 %prepare.1 = (bf16[1,512,128]{2,1,0:T(8,128)(2,1)S(1)}, bf16[1,128,512]{2,1,0:T(8,128)(2,1)S(1)}, bf16[6,512,128]{2,1,0:T(8,128)(2,1)S(1)}, bf16[6,128,512]{2,1,0:T(8,128)(2,1)S(1)}, f32[7,8,128]{2,1,0:T(8,128)S(1)}) custom-call(bf16[32,64,256]{2,1,0:T(8,128)(2,1)S(1)} %bitcast.7, s32[4,128]{1,0:T(4,128)S(1)} %get-tuple-element.19.table, ...), custom_call_target="tpu_custom_call" | custom-call | flops 200000000 | bytes 2097152 | tf_op jit(solution)/shard_map/prepare/pallas_call | solution.py:344
  10.2 0.5 %suffix_away.3 = (bf16[272,128]{1,0:T(8,128)(2,1)S(1)}, f32[8,128]{1,0:T(8,128)S(1)}) custom-call(bf16[6,512,128]{2,1,0:T(8,128)(2,1)S(1)} %get-tuple-element.24.keys_ref, bf16[6,128,512]{2,1,0:T(8,128)(2,1)S(1)} %get-tuple-element.25.values_ref, f32[7,8,128]{2,1,0:T(8,128)S(1)} %get-tuple-element.23.member_ref.refs_3_, ...), custom_call_target="tpu_custom_call" | custom-call | flops 200000000 | bytes 2097152 | tf_op jit(solution)/shard_map/suffix_away/pallas_call | solution.py:371
  10.7 0.0 copy-start
  10.8 2.9 %collective-permute-start.5 = (bf16[272,128]{1,0:T(8,128)(2,1)S(1)}, bf16[272,128]{1,0:T(8,128)(2,1)S(1)}, u32[]{:S(2)}, u32[]{:S(2)}) collective-permute-start(bf16[272,128]{1,0:T(8,128)(2,1)S(1)} %get-tuple-element.28), channel_id=1, source_target_pairs={{0,16},{1,17},{4,21},{5,20},{8,24},{9,25},{12,29},{13,28},{16,0},{... | collective-permute-start | bytes 208904 | tf_op jit(solution)/shard_map/ppermute | solution.py:36
  13.6 0.5 %suffix_away.5 = bf16[272,128]{1,0:T(8,128)(2,1)S(1)} custom-call(bf16[6,512,128]{2,1,0:T(8,128)(2,1)S(1)} %get-tuple-element.24.keys_ref, bf16[6,128,512]{2,1,0:T(8,128)(2,1)S(1)} %get-tuple-element.25.values_ref, f32[7,8,128]{2,1,0:T(8,128)S(1)} %get-tuple-element.23.member_ref.refs_3_, bf16[2,16,1024]{2,1,0:T(8,128)(2,1)S(1)} %collective-permute-done.8.message_ref), custom_call_target="tpu_custom_call" | custom-call | flops 200000000 | bytes 2097152 | tf_op jit(solution)/shard_map/suffix_away/pallas_call | solution.py:371
  14.1 2.2 %collective-permute-start.9 = (bf16[272,128]{1,0:T(8,128)(2,1)S(1)}, bf16[272,128]{1,0:T(8,128)(2,1)S(1)}, u32[]{:S(2)}, u32[]{:S(2)}) collective-permute-start(bf16[272,128]{1,0:T(8,128)(2,1)S(1)} %suffix_away.5), channel_id=1, source_target_pairs={{0,24},{1,25},{4,29},{5,28},{8,16},{9,17},{12,21},{13,20},{16,8},{... | collective-permute-start | bytes 208904 | tf_op jit(solution)/shard_map/ppermute | solution.py:36
  16.4 0.5 %suffix_away.4 = bf16[272,128]{1,0:T(8,128)(2,1)S(1)} custom-call(bf16[6,512,128]{2,1,0:T(8,128)(2,1)S(1)} %get-tuple-element.24.keys_ref, bf16[6,128,512]{2,1,0:T(8,128)(2,1)S(1)} %get-tuple-element.25.values_ref, f32[7,8,128]{2,1,0:T(8,128)S(1)} %get-tuple-element.23.member_ref.refs_3_, bf16[2,16,1024]{2,1,0:T(8,128)(2,1)S(1)} %collective-permute-done.6.message_ref), custom_call_target="tpu_custom_call" | custom-call | flops 200000000 | bytes 2097152 | tf_op jit(solution)/shard_map/suffix_away/pallas_call | solution.py:371
  16.9 0.6 %collective-permute-start.7 = (bf16[272,128]{1,0:T(8,128)(2,1)S(1)}, bf16[272,128]{1,0:T(8,128)(2,1)S(1)}, u32[]{:S(2)}, u32[]{:S(2)}) collective-permute-start(bf16[272,128]{1,0:T(8,128)(2,1)S(1)} %suffix_away.4), channel_id=1, source_target_pairs={{0,8},{1,9},{4,13},{5,12},{8,0},{9,1},{12,5},{13,4},{16,24},{17,25... | collective-permute-start | bytes 208904 | tf_op jit(solution)/shard_map/ppermute | solution.py:36
  17.5 1.6 %home_pair_heads.1 = bf16[144,128]{1,0:T(8,128)(2,1)S(1)} custom-call(s32[1]{0:T(128)S(6)} %copy.7.refs_0_, bf16[1,512,128]{2,1,0:T(8,128)(2,1)S(1)} %get-tuple-element.21.refs_1_, bf16[1,128,512]{2,1,0:T(8,128)(2,1)S(1)} %get-tuple-element.22.refs_2_, f32[7,8,128]{2,1,0:T(8,128)S(1)} %get-tuple-element.23.member_ref.refs_3_, ...), custom_call_target="tpu_custom_call" | custom-call | flops 536870912 | bytes 2097152 | tf_op jit(solution)/shard_map/home_pair_heads/pallas_call | solution.py:388
  19.1 0.8 %collective-permute-start.4 = (bf16[144,128]{1,0:T(8,128)(2,1)S(1)}, bf16[144,128]{1,0:T(8,128)(2,1)S(1)}, u32[]{:S(2)}, u32[]{:S(2)}) collective-permute-start(bf16[144,128]{1,0:T(8,128)(2,1)S(1)} %home_pair_heads.1), channel_id=1, source_target_pairs={{0,1},{1,0},{2,3},{3,2},{4,5},{5,4},{6,7},{7,6},{8,9},{9,8},{10,11... | collective-permute-start | bytes 110600 | tf_op jit(solution)/shard_map/ppermute | solution.py:26
  19.9 1.6 %home_own_heads.1 = (f32[128,128]{1,0:T(8,128)S(1)}, f32[8,128]{1,0:T(8,128)S(1)}) custom-call(s32[1]{0:T(128)S(6)} %copy.7.refs_0_, bf16[1,512,128]{2,1,0:T(8,128)(2,1)S(1)} %get-tuple-element.21.refs_1_, bf16[1,128,512]{2,1,0:T(8,128)(2,1)S(1)} %get-tuple-element.22.refs_2_, f32[7,8,128]{2,1,0:T(8,128)S(1)} %get-tuple-element.23.member_ref.refs_3_, ...), custom_call_target="tpu_custom_call" | custom-call | flops 536870912 | bytes 2097152 | tf_op jit(solution)/shard_map/home_own_heads/pallas_call | solution.py:398
  21.5 0.7 %collective-permute-done.7.rest_1_ = bf16[272,128]{1,0:T(8,128)(2,1)S(1)} collective-permute-done((bf16[272,128]{1,0:T(8,128)(2,1)S(1)}, bf16[272,128]{1,0:T(8,128)(2,1)S(1)}, u32[]{:S(2)}, u32[]{:S(2)}) %collective-permute-start.7) | collective-permute-done | bytes 69664 | tf_op jit(solution)/shard_map/ppermute | solution.py:36
  22.2 0.4 %collective-permute-start.10 = (bf16[144,128]{1,0:T(8,128)(2,1)S(1)}, bf16[144,128]{1,0:T(8,128)(2,1)S(1)}, u32[]{:S(2)}, u32[]{:S(2)}) collective-permute-start(bf16[144,128]{1,0:T(8,128)(2,1)S(1)} %sibling_share.1), channel_id=1, source_target_pairs={{0,4},{4,0},{1,5},{5,1},{2,6},{6,2},{3,7},{7,3},{8,12},{12,8},{9,1... | collective-permute-start | bytes 110600 | tf_op jit(solution)/shard_map/ppermute | solution.py:26
  22.6 0.5 %collective-permute-done.4.last_ref = bf16[144,128]{1,0:T(8,128)(2,1)S(1)} collective-permute-done((bf16[144,128]{1,0:T(8,128)(2,1)S(1)}, bf16[144,128]{1,0:T(8,128)(2,1)S(1)}, u32[]{:S(2)}, u32[]{:S(2)}) %collective-permute-start.4) | collective-permute-done | bytes 36896 | tf_op jit(solution)/shard_map/ppermute | solution.py:26
  23.1 0.4 %collective-permute-done.10.shared_ref = bf16[144,128]{1,0:T(8,128)(2,1)S(1)} collective-permute-done((bf16[144,128]{1,0:T(8,128)(2,1)S(1)}, bf16[144,128]{1,0:T(8,128)(2,1)S(1)}, u32[]{:S(2)}, u32[]{:S(2)}) %collective-permute-start.10) | collective-permute-done | bytes 36896 | tf_op jit(solution)/shard_map/ppermute | solution.py:26
  23.5 0.8 %combine.1 = f32[16,1024]{1,0:T(8,128)} custom-call(bf16[144,128]{1,0:T(8,128)(2,1)S(1)} %collective-permute-done.4.last_ref, bf16[144,128]{1,0:T(8,128)(2,1)S(1)} %collective-permute-done.10.shared_ref, f32[128,128]{1,0:T(8,128)S(1)} %get-tuple-element.31.summed_ref, f32[8,128]{1,0:T(8,128)S(1)} %get-tuple-element.32.stats_ref), custom_call_target="tpu_custom_call" | custom-call | tf_op jit(solution)/shard_map/combine/pallas_call | solution.py:427
  (15 shorter events, 0.1 us)
Async XLA Ops:
  0.0 1.5 %collective-permute-start.2 = (bf16[16,1024]{1,0:T(8,128)(2,1)}, bf16[16,1024]{1,0:T(8,128)(2,1)S(1)}, u32[]{:S(2)}, u32[]{:S(2)}) collective-permute-start(bf16[16,1024]{1,0:T(8,128)(2,1)} %refs_0_.3), channel_id=1, source_target_pairs={{0,4},{4,0},{1,5},{5,1},{2,6},{6,2},{3,7},{7,3},{8,12},{12,8},{9,1... | collective-permute-start | bytes 98312 | tf_op jit(solution)/shard_map/ppermute | solution.py:26
  0.5 8.8 %collective-permute-start = (bf16[32,64,256]{2,1,0:T(8,128)(2,1)}, bf16[32,64,256]{2,1,0:T(8,128)(2,1)S(1)}, u32[]{:S(2)}, u32[]{:S(2)}) collective-permute-start(bf16[32,64,256]{2,1,0:T(8,128)(2,1)} %bitcast.6), channel_id=1, source_target_pairs={{0,4},{4,0},{1,5},{5,1},{2,6},{6,2},{3,7},{7,3},{8,12},{12,8},{9,1... | collective-permute-start | bytes 3145736 | tf_op jit(solution)/shard_map/ppermute | solution.py:26
  1.5 5.6 %copy-start.2 = (bf16[16,1024]{1,0:T(8,128)(2,1)S(1)}, bf16[16,1024]{1,0:T(8,128)(2,1)}, u32[]{:S(2)}) copy-start(bf16[16,1024]{1,0:T(8,128)(2,1)} %refs_0_.3) | copy-start | bytes 98308
  1.5 7.8 %copy-start.1 = (bf16[32,1,64,256]{3,2,1,0:T(8,128)(2,1)S(1)}, bf16[32,1,64,256]{3,2,1,0:T(8,128)(2,1)}, u32[]{:S(2)}) copy-start(bf16[32,1,64,256]{3,2,1,0:T(8,128)(2,1)} %param.8) | copy-start | bytes 3145732
  1.5 8.7 %collective-permute-start.3 = (bf16[2,16,1024]{2,1,0:T(8,128)(2,1)S(1)}, bf16[2,16,1024]{2,1,0:T(8,128)(2,1)S(1)}, u32[]{:S(2)}, u32[]{:S(2)}) collective-permute-start(bf16[2,16,1024]{2,1,0:T(8,128)(2,1)S(1)} %both_cores.1), channel_id=1, source_target_pairs={{0,16},{1,17},{4,21},{5,20},{8,24},{9,25},{12,29},{13,28},{16,0},{... | collective-permute-start | bytes 196616 | tf_op jit(solution)/shard_map/ppermute | solution.py:36
  5.5 8.1 %collective-permute-start.8 = (bf16[2,16,1024]{2,1,0:T(8,128)(2,1)S(1)}, bf16[2,16,1024]{2,1,0:T(8,128)(2,1)S(1)}, u32[]{:S(2)}, u32[]{:S(2)}) collective-permute-start(bf16[2,16,1024]{2,1,0:T(8,128)(2,1)S(1)} %both_cores.1), channel_id=1, source_target_pairs={{0,24},{1,25},{4,29},{5,28},{8,16},{9,17},{12,21},{13,20},{16,8},{... | collective-permute-start | bytes 196616 | tf_op jit(solution)/shard_map/ppermute | solution.py:36
  6.9 9.5 %collective-permute-start.6 = (bf16[2,16,1024]{2,1,0:T(8,128)(2,1)S(1)}, bf16[2,16,1024]{2,1,0:T(8,128)(2,1)S(1)}, u32[]{:S(2)}, u32[]{:S(2)}) collective-permute-start(bf16[2,16,1024]{2,1,0:T(8,128)(2,1)S(1)} %both_cores.1), channel_id=1, source_target_pairs={{0,8},{1,9},{4,13},{5,12},{8,0},{9,1},{12,5},{13,4},{16,24},{17,25... | collective-permute-start | bytes 196616 | tf_op jit(solution)/shard_map/ppermute | solution.py:36
  7.1 10.4 %collective-permute-start.1 = (bf16[16,1024]{1,0:T(8,128)(2,1)S(1)}, bf16[16,1024]{1,0:T(8,128)(2,1)S(1)}, u32[]{:S(2)}, u32[]{:S(2)}) collective-permute-start(bf16[16,1024]{1,0:T(8,128)(2,1)S(1)} %copy-done.2), channel_id=1, source_target_pairs={{0,1},{1,0},{2,3},{3,2},{4,5},{5,4},{6,7},{7,6},{8,9},{9,8},{10,11... | collective-permute-start | bytes 98312 | tf_op jit(solution)/shard_map/ppermute | solution.py:26
  10.7 6.8 %copy-start = (bf16[1,1,4096,256]{3,2,1,0:T(8,128)(2,1)S(1)}, bf16[1,1,4096,256]{3,2,1,0:T(8,128)(2,1)}, u32[]{:S(2)}) copy-start(bf16[1,1,4096,256]{3,2,1,0:T(8,128)(2,1)} %param.7) | copy-start | bytes 6291460
  10.8 10.7 %collective-permute-start.5 = (bf16[272,128]{1,0:T(8,128)(2,1)S(1)}, bf16[272,128]{1,0:T(8,128)(2,1)S(1)}, u32[]{:S(2)}, u32[]{:S(2)}) collective-permute-start(bf16[272,128]{1,0:T(8,128)(2,1)S(1)} %get-tuple-element.28), channel_id=1, source_target_pairs={{0,16},{1,17},{4,21},{5,20},{8,24},{9,25},{12,29},{13,28},{16,0},{... | collective-permute-start | bytes 208904 | tf_op jit(solution)/shard_map/ppermute | solution.py:36
  14.1 7.3 %collective-permute-start.9 = (bf16[272,128]{1,0:T(8,128)(2,1)S(1)}, bf16[272,128]{1,0:T(8,128)(2,1)S(1)}, u32[]{:S(2)}, u32[]{:S(2)}) collective-permute-start(bf16[272,128]{1,0:T(8,128)(2,1)S(1)} %suffix_away.5), channel_id=1, source_target_pairs={{0,24},{1,25},{4,29},{5,28},{8,16},{9,17},{12,21},{13,20},{16,8},{... | collective-permute-start | bytes 208904 | tf_op jit(solution)/shard_map/ppermute | solution.py:36
  16.9 5.3 %collective-permute-start.7 = (bf16[272,128]{1,0:T(8,128)(2,1)S(1)}, bf16[272,128]{1,0:T(8,128)(2,1)S(1)}, u32[]{:S(2)}, u32[]{:S(2)}) collective-permute-start(bf16[272,128]{1,0:T(8,128)(2,1)S(1)} %suffix_away.4), channel_id=1, source_target_pairs={{0,8},{1,9},{4,13},{5,12},{8,0},{9,1},{12,5},{13,4},{16,24},{17,25... | collective-permute-start | bytes 208904 | tf_op jit(solution)/shard_map/ppermute | solution.py:36
  19.1 4.0 %collective-permute-start.4 = (bf16[144,128]{1,0:T(8,128)(2,1)S(1)}, bf16[144,128]{1,0:T(8,128)(2,1)S(1)}, u32[]{:S(2)}, u32[]{:S(2)}) collective-permute-start(bf16[144,128]{1,0:T(8,128)(2,1)S(1)} %home_pair_heads.1), channel_id=1, source_target_pairs={{0,1},{1,0},{2,3},{3,2},{4,5},{5,4},{6,7},{7,6},{8,9},{9,8},{10,11... | collective-permute-start | bytes 110600 | tf_op jit(solution)/shard_map/ppermute | solution.py:26
  22.2 1.3 %collective-permute-start.10 = (bf16[144,128]{1,0:T(8,128)(2,1)S(1)}, bf16[144,128]{1,0:T(8,128)(2,1)S(1)}, u32[]{:S(2)}, u32[]{:S(2)}) collective-permute-start(bf16[144,128]{1,0:T(8,128)(2,1)S(1)} %sibling_share.1), channel_id=1, source_target_pairs={{0,4},{4,0},{1,5},{5,1},{2,6},{6,2},{3,7},{7,3},{8,12},{12,8},{9,1... | collective-permute-start | bytes 110600 | tf_op jit(solution)/shard_map/ppermute | solution.py:26

commit v33 on v32

--- a/solution.py
+++ b/solution.py
@@ -197,15 +197,15 @@
     for i, request in enumerate(requests):
         lane = iota((rows, VECS), 1)
         spread = iota((rows, VECS), 0) == request * BEAMS + lane % BEAMS
-        rows_ref[: 2 * slots, :] = count(continued, spread.astype(jnp.float32))
-        rows_ref[2 * slots :, :] = jnp.zeros((8, VECS), jnp.float32)
+        rows_ref[i, : 2 * slots, :] = count(continued, spread.astype(jnp.float32))
+        rows_ref[i, 2 * slots :, :] = jnp.zeros((8, VECS), jnp.float32)
         mask = iota(found.shape, 1) == request
         picked = jnp.sum(jnp.where(mask, found, 0), axis=1, keepdims=True)
         values = []
         for k in range(2 * capacity):
             index = picked[k, 0]
             row = jnp.where(index > 0, index - 1, 2 * slots)
-            member_ref[i, k : k + 1, :] = rows_ref[pl.ds(row, 1), :]
+            member_ref[i, k : k + 1, :] = rows_ref[i, pl.ds(row, 1), :]
             pool_ref = near if k < capacity else far_ref
             base = 0 if k < capacity else slots
             content = pool_ref[jnp.maximum(index - 1 - base, 0)]
@@ -352,7 +352,7 @@
         ),
         in_specs=[vmem] * 4,
         out_specs=(vmem,) * 5,
-        scratch_shapes=[pltpu.VMEM((2 * slots + 8, VECS), jnp.float32)],
+        scratch_shapes=[pltpu.VMEM((2 * n_req - 1, 2 * slots + 8, VECS), jnp.float32)],
         compiler_params=params,
         cost_estimate=some,
         name="prepare",

time: 24.4 us -> 24.4 us (level)
  no operation moved by 1% of the time
where the time goes in v33:
time: 24.4 us; the launch traced here: 24.2 us
  starting transfers between devices  14.5 us (59%)
  Pallas kernels  7.21 us (30%)
  waiting for transfers between devices  1.81 us (7%)
  between operations  0.77 us (3%)
    ppermute x6, starting transfers between devices, exchanged(): return lax.ppermute(value, ('z', 'core', 'pair'), pairs)  11.3 us
    ppermute x5, starting transfers between devices, swapped(): return lax.ppermute(value, axis, [(0, 1), (1, 0)])  3.14 us
    pallas_call x1, Pallas kernels, on_device(): pl.pallas_call(pair_heads_kernel, out_shape=pltpu.VMEM((HD + STAT_ROWS, V...  1.57 us
    pallas_call x1, Pallas kernels, on_device(): pl.pallas_call(own_heads_kernel, out_shape=(pltpu.VMEM((HD, VECS), jnp.fl...  1.56 us
    pallas_call x3, Pallas kernels, on_device(): pl.pallas_call(functools.partial(away_kernel, 2 * mask - 2), out_shape=ou...  1.5 us
    ppermute x5, waiting for transfers between devices, swapped(): return lax.ppermute(value, axis, [(0, 1), (1, 0)])  1.1 us
    pallas_call x1, Pallas kernels, on_device(): pl.pallas_call(functools.partial(prepare_kernel, capacity), out_shape=(pl...  0.94 us
    pallas_call x1, Pallas kernels, on_device(): pl.pallas_call(stage_kernel, out_shape=tuple((pltpu.VMEM(each.shape, each...  0.79 us
  transfers between devices with their start and end apart: 11, of which 4 were waited for; matrix products, arithmetic and copies ran while one was open for 0% of the time, Pallas kernels for 27%

profile of v33, /device:TPU:0, one launch (start us, length us, event | category | flops | bytes accessed | tf_op | source)
XLA Modules:
  0.0 24.2 jit_solution(17771005806879193748)
XLA Ops:
  0.0 0.5 %collective-permute-start.2 = (bf16[16,1024]{1,0:T(8,128)(2,1)}, bf16[16,1024]{1,0:T(8,128)(2,1)S(1)}, u32[]{:S(2)}, u32[]{:S(2)}) collective-permute-start(bf16[16,1024]{1,0:T(8,128)(2,1)} %refs_0_.3), channel_id=1, source_target_pairs={{0,4},{4,0},{1,5},{5,1},{2,6},{6,2},{3,7},{7,3},{8,12},{12,8},{9,1... | collective-permute-start | bytes 98312 | tf_op jit(solution)/shard_map/ppermute | solution.py:26
  0.5 0.1 collective-permute-start
  0.5 0.8 %stage.1 = (bf16[16,1024]{1,0:T(8,128)(2,1)S(1)}, s32[4,128]{1,0:T(4,128)S(1)}, s32[1,128]{1,0:T(1,128)S(1)}) custom-call(bf16[16,1024]{1,0:T(8,128)(2,1)} %refs_0_.3, s32[4,128]{1,0:T(4,128)} %bitcast.8, s32[1,128]{1,0:T(1,128)} %bitcast.9), custom_call_target="tpu_custom_call" | custom-call | tf_op jit(solution)/shard_map/stage/pallas_call | solution.py:322
  1.3 0.2 collective-permute-done.2.sibling_ref
  1.5 4.0 %collective-permute-start.3 = (bf16[2,16,1024]{2,1,0:T(8,128)(2,1)S(1)}, bf16[2,16,1024]{2,1,0:T(8,128)(2,1)S(1)}, u32[]{:S(2)}, u32[]{:S(2)}) collective-permute-start(bf16[2,16,1024]{2,1,0:T(8,128)(2,1)S(1)} %both_cores.1), channel_id=1, source_target_pairs={{0,16},{1,17},{4,21},{5,20},{8,24},{9,25},{12,29},{13,28},{16,0},{... | collective-permute-start | bytes 196616 | tf_op jit(solution)/shard_map/ppermute | solution.py:36
  5.5 1.3 %collective-permute-start.8 = (bf16[2,16,1024]{2,1,0:T(8,128)(2,1)S(1)}, bf16[2,16,1024]{2,1,0:T(8,128)(2,1)S(1)}, u32[]{:S(2)}, u32[]{:S(2)}) collective-permute-start(bf16[2,16,1024]{2,1,0:T(8,128)(2,1)S(1)} %both_cores.1), channel_id=1, source_target_pairs={{0,24},{1,25},{4,29},{5,28},{8,16},{9,17},{12,21},{13,20},{16,8},{... | collective-permute-start | bytes 196616 | tf_op jit(solution)/shard_map/ppermute | solution.py:36
  6.9 0.2 collective-permute-start.6
  7.1 1.5 %collective-permute-start.1 = (bf16[16,1024]{1,0:T(8,128)(2,1)S(1)}, bf16[16,1024]{1,0:T(8,128)(2,1)S(1)}, u32[]{:S(2)}, u32[]{:S(2)}) collective-permute-start(bf16[16,1024]{1,0:T(8,128)(2,1)S(1)} %copy-done.2), channel_id=1, source_target_pairs={{0,1},{1,0},{2,3},{3,2},{4,5},{5,4},{6,7},{7,6},{8,9},{9,8},{10,11... | collective-permute-start | bytes 98312 | tf_op jit(solution)/shard_map/ppermute | solution.py:26
  9.3 0.9 %prepare.1 = (bf16[1,512,128]{2,1,0:T(8,128)(2,1)S(1)}, bf16[1,128,512]{2,1,0:T(8,128)(2,1)S(1)}, bf16[6,512,128]{2,1,0:T(8,128)(2,1)S(1)}, bf16[6,128,512]{2,1,0:T(8,128)(2,1)S(1)}, f32[7,8,128]{2,1,0:T(8,128)S(1)}) custom-call(bf16[32,64,256]{2,1,0:T(8,128)(2,1)S(1)} %bitcast.7, s32[4,128]{1,0:T(4,128)S(1)} %get-tuple-element.19.table, ...), custom_call_target="tpu_custom_call" | custom-call | flops 200000000 | bytes 2097152 | tf_op jit(solution)/shard_map/prepare/pallas_call | solution.py:344
  10.2 0.5 %suffix_away.3 = (bf16[272,128]{1,0:T(8,128)(2,1)S(1)}, f32[8,128]{1,0:T(8,128)S(1)}) custom-call(bf16[6,512,128]{2,1,0:T(8,128)(2,1)S(1)} %get-tuple-element.24.keys_ref, bf16[6,128,512]{2,1,0:T(8,128)(2,1)S(1)} %get-tuple-element.25.values_ref, f32[7,8,128]{2,1,0:T(8,128)S(1)} %get-tuple-element.23.member_ref.refs_3_, ...), custom_call_target="tpu_custom_call" | custom-call | flops 200000000 | bytes 2097152 | tf_op jit(solution)/shard_map/suffix_away/pallas_call | solution.py:371
  10.8 0.0 copy-start
  10.8 2.9 %collective-permute-start.5 = (bf16[272,128]{1,0:T(8,128)(2,1)S(1)}, bf16[272,128]{1,0:T(8,128)(2,1)S(1)}, u32[]{:S(2)}, u32[]{:S(2)}) collective-permute-start(bf16[272,128]{1,0:T(8,128)(2,1)S(1)} %get-tuple-element.28), channel_id=1, source_target_pairs={{0,16},{1,17},{4,21},{5,20},{8,24},{9,25},{12,29},{13,28},{16,0},{... | collective-permute-start | bytes 208904 | tf_op jit(solution)/shard_map/ppermute | solution.py:36
  13.6 0.5 %suffix_away.5 = bf16[272,128]{1,0:T(8,128)(2,1)S(1)} custom-call(bf16[6,512,128]{2,1,0:T(8,128)(2,1)S(1)} %get-tuple-element.24.keys_ref, bf16[6,128,512]{2,1,0:T(8,128)(2,1)S(1)} %get-tuple-element.25.values_ref, f32[7,8,128]{2,1,0:T(8,128)S(1)} %get-tuple-element.23.member_ref.refs_3_, bf16[2,16,1024]{2,1,0:T(8,128)(2,1)S(1)} %collective-permute-done.8.message_ref), custom_call_target="tpu_custom_call" | custom-call | flops 200000000 | bytes 2097152 | tf_op jit(solution)/shard_map/suffix_away/pallas_call | solution.py:371
  14.2 2.2 %collective-permute-start.9 = (bf16[272,128]{1,0:T(8,128)(2,1)S(1)}, bf16[272,128]{1,0:T(8,128)(2,1)S(1)}, u32[]{:S(2)}, u32[]{:S(2)}) collective-permute-start(bf16[272,128]{1,0:T(8,128)(2,1)S(1)} %suffix_away.5), channel_id=1, source_target_pairs={{0,24},{1,25},{4,29},{5,28},{8,16},{9,17},{12,21},{13,20},{16,8},{... | collective-permute-start | bytes 208904 | tf_op jit(solution)/shard_map/ppermute | solution.py:36
  16.4 0.5 %suffix_away.4 = bf16[272,128]{1,0:T(8,128)(2,1)S(1)} custom-call(bf16[6,512,128]{2,1,0:T(8,128)(2,1)S(1)} %get-tuple-element.24.keys_ref, bf16[6,128,512]{2,1,0:T(8,128)(2,1)S(1)} %get-tuple-element.25.values_ref, f32[7,8,128]{2,1,0:T(8,128)S(1)} %get-tuple-element.23.member_ref.refs_3_, bf16[2,16,1024]{2,1,0:T(8,128)(2,1)S(1)} %collective-permute-done.6.message_ref), custom_call_target="tpu_custom_call" | custom-call | flops 200000000 | bytes 2097152 | tf_op jit(solution)/shard_map/suffix_away/pallas_call | solution.py:371
  16.9 0.6 %collective-permute-start.7 = (bf16[272,128]{1,0:T(8,128)(2,1)S(1)}, bf16[272,128]{1,0:T(8,128)(2,1)S(1)}, u32[]{:S(2)}, u32[]{:S(2)}) collective-permute-start(bf16[272,128]{1,0:T(8,128)(2,1)S(1)} %suffix_away.4), channel_id=1, source_target_pairs={{0,8},{1,9},{4,13},{5,12},{8,0},{9,1},{12,5},{13,4},{16,24},{17,25... | collective-permute-start | bytes 208904 | tf_op jit(solution)/shard_map/ppermute | solution.py:36
  17.5 1.6 %home_pair_heads.1 = bf16[144,128]{1,0:T(8,128)(2,1)S(1)} custom-call(s32[1]{0:T(128)S(6)} %copy.7.refs_0_, bf16[1,512,128]{2,1,0:T(8,128)(2,1)S(1)} %get-tuple-element.21.refs_1_, bf16[1,128,512]{2,1,0:T(8,128)(2,1)S(1)} %get-tuple-element.22.refs_2_, f32[7,8,128]{2,1,0:T(8,128)S(1)} %get-tuple-element.23.member_ref.refs_3_, ...), custom_call_target="tpu_custom_call" | custom-call | flops 536870912 | bytes 2097152 | tf_op jit(solution)/shard_map/home_pair_heads/pallas_call | solution.py:388
  19.1 0.8 %collective-permute-start.4 = (bf16[144,128]{1,0:T(8,128)(2,1)S(1)}, bf16[144,128]{1,0:T(8,128)(2,1)S(1)}, u32[]{:S(2)}, u32[]{:S(2)}) collective-permute-start(bf16[144,128]{1,0:T(8,128)(2,1)S(1)} %home_pair_heads.1), channel_id=1, source_target_pairs={{0,1},{1,0},{2,3},{3,2},{4,5},{5,4},{6,7},{7,6},{8,9},{9,8},{10,11... | collective-permute-start | bytes 110600 | tf_op jit(solution)/shard_map/ppermute | solution.py:26
  19.9 1.6 %home_own_heads.1 = (f32[128,128]{1,0:T(8,128)S(1)}, f32[8,128]{1,0:T(8,128)S(1)}) custom-call(s32[1]{0:T(128)S(6)} %copy.7.refs_0_, bf16[1,512,128]{2,1,0:T(8,128)(2,1)S(1)} %get-tuple-element.21.refs_1_, bf16[1,128,512]{2,1,0:T(8,128)(2,1)S(1)} %get-tuple-element.22.refs_2_, f32[7,8,128]{2,1,0:T(8,128)S(1)} %get-tuple-element.23.member_ref.refs_3_, ...), custom_call_target="tpu_custom_call" | custom-call | flops 536870912 | bytes 2097152 | tf_op jit(solution)/shard_map/home_own_heads/pallas_call | solution.py:398
  21.5 0.7 %collective-permute-done.7.rest_1_ = bf16[272,128]{1,0:T(8,128)(2,1)S(1)} collective-permute-done((bf16[272,128]{1,0:T(8,128)(2,1)S(1)}, bf16[272,128]{1,0:T(8,128)(2,1)S(1)}, u32[]{:S(2)}, u32[]{:S(2)}) %collective-permute-start.7) | collective-permute-done | bytes 69664 | tf_op jit(solution)/shard_map/ppermute | solution.py:36
  22.2 0.3 %collective-permute-start.10 = (bf16[144,128]{1,0:T(8,128)(2,1)S(1)}, bf16[144,128]{1,0:T(8,128)(2,1)S(1)}, u32[]{:S(2)}, u32[]{:S(2)}) collective-permute-start(bf16[144,128]{1,0:T(8,128)(2,1)S(1)} %sibling_share.1), channel_id=1, source_target_pairs={{0,4},{4,0},{1,5},{5,1},{2,6},{6,2},{3,7},{7,3},{8,12},{12,8},{9,1... | collective-permute-start | bytes 110600 | tf_op jit(solution)/shard_map/ppermute | solution.py:26
  22.6 0.5 %collective-permute-done.4.last_ref = bf16[144,128]{1,0:T(8,128)(2,1)S(1)} collective-permute-done((bf16[144,128]{1,0:T(8,128)(2,1)S(1)}, bf16[144,128]{1,0:T(8,128)(2,1)S(1)}, u32[]{:S(2)}, u32[]{:S(2)}) %collective-permute-start.4) | collective-permute-done | bytes 36896 | tf_op jit(solution)/shard_map/ppermute | solution.py:26
  23.1 0.4 %collective-permute-done.10.shared_ref = bf16[144,128]{1,0:T(8,128)(2,1)S(1)} collective-permute-done((bf16[144,128]{1,0:T(8,128)(2,1)S(1)}, bf16[144,128]{1,0:T(8,128)(2,1)S(1)}, u32[]{:S(2)}, u32[]{:S(2)}) %collective-permute-start.10) | collective-permute-done | bytes 36896 | tf_op jit(solution)/shard_map/ppermute | solution.py:26
  23.5 0.8 %combine.1 = f32[16,1024]{1,0:T(8,128)} custom-call(bf16[144,128]{1,0:T(8,128)(2,1)S(1)} %collective-permute-done.4.last_ref, bf16[144,128]{1,0:T(8,128)(2,1)S(1)} %collective-permute-done.10.shared_ref, f32[128,128]{1,0:T(8,128)S(1)} %get-tuple-element.31.summed_ref, f32[8,128]{1,0:T(8,128)S(1)} %get-tuple-element.32.stats_ref), custom_call_target="tpu_custom_call" | custom-call | tf_op jit(solution)/shard_map/combine/pallas_call | solution.py:427
  (15 shorter events, 0.1 us)
Async XLA Ops:
  0.0 1.5 %collective-permute-start.2 = (bf16[16,1024]{1,0:T(8,128)(2,1)}, bf16[16,1024]{1,0:T(8,128)(2,1)S(1)}, u32[]{:S(2)}, u32[]{:S(2)}) collective-permute-start(bf16[16,1024]{1,0:T(8,128)(2,1)} %refs_0_.3), channel_id=1, source_target_pairs={{0,4},{4,0},{1,5},{5,1},{2,6},{6,2},{3,7},{7,3},{8,12},{12,8},{9,1... | collective-permute-start | bytes 98312 | tf_op jit(solution)/shard_map/ppermute | solution.py:26
  0.5 8.8 %collective-permute-start = (bf16[32,64,256]{2,1,0:T(8,128)(2,1)}, bf16[32,64,256]{2,1,0:T(8,128)(2,1)S(1)}, u32[]{:S(2)}, u32[]{:S(2)}) collective-permute-start(bf16[32,64,256]{2,1,0:T(8,128)(2,1)} %bitcast.6), channel_id=1, source_target_pairs={{0,4},{4,0},{1,5},{5,1},{2,6},{6,2},{3,7},{7,3},{8,12},{12,8},{9,1... | collective-permute-start | bytes 3145736 | tf_op jit(solution)/shard_map/ppermute | solution.py:26
  1.5 5.6 %copy-start.2 = (bf16[16,1024]{1,0:T(8,128)(2,1)S(1)}, bf16[16,1024]{1,0:T(8,128)(2,1)}, u32[]{:S(2)}) copy-start(bf16[16,1024]{1,0:T(8,128)(2,1)} %refs_0_.3) | copy-start | bytes 98308
  1.5 7.8 %copy-start.1 = (bf16[32,1,64,256]{3,2,1,0:T(8,128)(2,1)S(1)}, bf16[32,1,64,256]{3,2,1,0:T(8,128)(2,1)}, u32[]{:S(2)}) copy-start(bf16[32,1,64,256]{3,2,1,0:T(8,128)(2,1)} %param.8) | copy-start | bytes 3145732
  1.5 8.7 %collective-permute-start.3 = (bf16[2,16,1024]{2,1,0:T(8,128)(2,1)S(1)}, bf16[2,16,1024]{2,1,0:T(8,128)(2,1)S(1)}, u32[]{:S(2)}, u32[]{:S(2)}) collective-permute-start(bf16[2,16,1024]{2,1,0:T(8,128)(2,1)S(1)} %both_cores.1), channel_id=1, source_target_pairs={{0,16},{1,17},{4,21},{5,20},{8,24},{9,25},{12,29},{13,28},{16,0},{... | collective-permute-start | bytes 196616 | tf_op jit(solution)/shard_map/ppermute | solution.py:36
  5.5 8.1 %collective-permute-start.8 = (bf16[2,16,1024]{2,1,0:T(8,128)(2,1)S(1)}, bf16[2,16,1024]{2,1,0:T(8,128)(2,1)S(1)}, u32[]{:S(2)}, u32[]{:S(2)}) collective-permute-start(bf16[2,16,1024]{2,1,0:T(8,128)(2,1)S(1)} %both_cores.1), channel_id=1, source_target_pairs={{0,24},{1,25},{4,29},{5,28},{8,16},{9,17},{12,21},{13,20},{16,8},{... | collective-permute-start | bytes 196616 | tf_op jit(solution)/shard_map/ppermute | solution.py:36
  6.9 9.5 %collective-permute-start.6 = (bf16[2,16,1024]{2,1,0:T(8,128)(2,1)S(1)}, bf16[2,16,1024]{2,1,0:T(8,128)(2,1)S(1)}, u32[]{:S(2)}, u32[]{:S(2)}) collective-permute-start(bf16[2,16,1024]{2,1,0:T(8,128)(2,1)S(1)} %both_cores.1), channel_id=1, source_target_pairs={{0,8},{1,9},{4,13},{5,12},{8,0},{9,1},{12,5},{13,4},{16,24},{17,25... | collective-permute-start | bytes 196616 | tf_op jit(solution)/shard_map/ppermute | solution.py:36
  7.1 10.4 %collective-permute-start.1 = (bf16[16,1024]{1,0:T(8,128)(2,1)S(1)}, bf16[16,1024]{1,0:T(8,128)(2,1)S(1)}, u32[]{:S(2)}, u32[]{:S(2)}) collective-permute-start(bf16[16,1024]{1,0:T(8,128)(2,1)S(1)} %copy-done.2), channel_id=1, source_target_pairs={{0,1},{1,0},{2,3},{3,2},{4,5},{5,4},{6,7},{7,6},{8,9},{9,8},{10,11... | collective-permute-start | bytes 98312 | tf_op jit(solution)/shard_map/ppermute | solution.py:26
  10.8 6.8 %copy-start = (bf16[1,1,4096,256]{3,2,1,0:T(8,128)(2,1)S(1)}, bf16[1,1,4096,256]{3,2,1,0:T(8,128)(2,1)}, u32[]{:S(2)}) copy-start(bf16[1,1,4096,256]{3,2,1,0:T(8,128)(2,1)} %param.7) | copy-start | bytes 6291460
  10.8 10.7 %collective-permute-start.5 = (bf16[272,128]{1,0:T(8,128)(2,1)S(1)}, bf16[272,128]{1,0:T(8,128)(2,1)S(1)}, u32[]{:S(2)}, u32[]{:S(2)}) collective-permute-start(bf16[272,128]{1,0:T(8,128)(2,1)S(1)} %get-tuple-element.28), channel_id=1, source_target_pairs={{0,16},{1,17},{4,21},{5,20},{8,24},{9,25},{12,29},{13,28},{16,0},{... | collective-permute-start | bytes 208904 | tf_op jit(solution)/shard_map/ppermute | solution.py:36
  14.2 7.3 %collective-permute-start.9 = (bf16[272,128]{1,0:T(8,128)(2,1)S(1)}, bf16[272,128]{1,0:T(8,128)(2,1)S(1)}, u32[]{:S(2)}, u32[]{:S(2)}) collective-permute-start(bf16[272,128]{1,0:T(8,128)(2,1)S(1)} %suffix_away.5), channel_id=1, source_target_pairs={{0,24},{1,25},{4,29},{5,28},{8,16},{9,17},{12,21},{13,20},{16,8},{... | collective-permute-start | bytes 208904 | tf_op jit(solution)/shard_map/ppermute | solution.py:36
  16.9 5.3 %collective-permute-start.7 = (bf16[272,128]{1,0:T(8,128)(2,1)S(1)}, bf16[272,128]{1,0:T(8,128)(2,1)S(1)}, u32[]{:S(2)}, u32[]{:S(2)}) collective-permute-start(bf16[272,128]{1,0:T(8,128)(2,1)S(1)} %suffix_away.4), channel_id=1, source_target_pairs={{0,8},{1,9},{4,13},{5,12},{8,0},{9,1},{12,5},{13,4},{16,24},{17,25... | collective-permute-start | bytes 208904 | tf_op jit(solution)/shard_map/ppermute | solution.py:36
  19.1 4.0 %collective-permute-start.4 = (bf16[144,128]{1,0:T(8,128)(2,1)S(1)}, bf16[144,128]{1,0:T(8,128)(2,1)S(1)}, u32[]{:S(2)}, u32[]{:S(2)}) collective-permute-start(bf16[144,128]{1,0:T(8,128)(2,1)S(1)} %home_pair_heads.1), channel_id=1, source_target_pairs={{0,1},{1,0},{2,3},{3,2},{4,5},{5,4},{6,7},{7,6},{8,9},{9,8},{10,11... | collective-permute-start | bytes 110600 | tf_op jit(solution)/shard_map/ppermute | solution.py:26
  22.2 1.3 %collective-permute-start.10 = (bf16[144,128]{1,0:T(8,128)(2,1)S(1)}, bf16[144,128]{1,0:T(8,128)(2,1)S(1)}, u32[]{:S(2)}, u32[]{:S(2)}) collective-permute-start(bf16[144,128]{1,0:T(8,128)(2,1)S(1)} %sibling_share.1), channel_id=1, source_target_pairs={{0,4},{4,0},{1,5},{5,1},{2,6},{6,2},{3,7},{7,3},{8,12},{12,8},{9,1... | collective-permute-start | bytes 110600 | tf_op jit(solution)/shard_map/ppermute | solution.py:26

commit v34 on v32

--- a/solution.py
+++ b/solution.py
@@ -288,13 +288,20 @@
     out_stats_ref[...] = jnp.concatenate([top, total, jnp.zeros((6, VECS), jnp.float32)], axis=0)
 
 
-def final_kernel(last_ref, shared_ref, summed_ref, stats_ref, out_ref):
+def final_kernel(last_ref, shared_ref, summed_ref, stats_ref, out_ref, held, sems):
     parts = [load_unit(last_ref), load_unit(shared_ref)]
     parts.append((stats_ref[0:1], stats_ref[1:2], summed_ref[...]))
     _, total, summed = merged(parts)
     attended = (summed / total).T
+    copies = []
     for h in range(HEADS):
-        out_ref[:, h * HD : (h + 1) * HD] = attended[h * BEAMS : (h + 1) * BEAMS]
+        lanes = slice(h * HD, (h + 1) * HD)
+        held[:, lanes] = attended[h * BEAMS : (h + 1) * BEAMS]
+        copy = pltpu.make_async_copy(held.at[:, lanes], out_ref.at[:, lanes], sems.at[h])
+        copy.start()
+        copies.append(copy)
+    for copy in copies:
+        copy.wait()
 
 
 def in_hbm(value):
@@ -428,7 +435,11 @@
         final_kernel,
         out_shape=jax.ShapeDtypeStruct((BEAMS, HEADS * HD), jnp.float32),
         in_specs=[vmem] * 4,
-        out_specs=vmem,
+        out_specs=pl.BlockSpec(memory_space=pltpu.HBM),
+        scratch_shapes=[
+            pltpu.VMEM((BEAMS, HEADS * HD), jnp.float32),
+            pltpu.SemaphoreType.DMA((HEADS,)),
+        ],
         compiler_params=params,
         name="combine",
     )(last, swapped(share, "core"), summed, stats)

time: 24.4 us -> 24.5 us (level)
  no operation moved by 1% of the time
where the time goes in v34:
time: 24.5 us; the launch traced here: 24.3 us
  starting transfers between devices  14.5 us (59%)
  Pallas kernels  7.24 us (30%)
  waiting for transfers between devices  1.77 us (7%)
  between operations  0.76 us (3%)
    ppermute x6, starting transfers between devices, exchanged(): return lax.ppermute(value, ('z', 'core', 'pair'), pairs)  11.3 us
    ppermute x5, starting transfers between devices, swapped(): return lax.ppermute(value, axis, [(0, 1), (1, 0)])  3.18 us
    pallas_call x1, Pallas kernels, on_device(): pl.pallas_call(pair_heads_kernel, out_shape=pltpu.VMEM((HD + STAT_ROWS, V...  1.57 us
    pallas_call x1, Pallas kernels, on_device(): pl.pallas_call(own_heads_kernel, out_shape=(pltpu.VMEM((HD, VECS), jnp.fl...  1.56 us
    pallas_call x3, Pallas kernels, on_device(): pl.pallas_call(functools.partial(away_kernel, 2 * mask - 2), out_shape=ou...  1.5 us
    ppermute x5, waiting for transfers between devices, swapped(): return lax.ppermute(value, axis, [(0, 1), (1, 0)])  1.06 us
    pallas_call x1, Pallas kernels, on_device(): pl.pallas_call(functools.partial(prepare_kernel, capacity), out_shape=(pl...  0.94 us
    pallas_call x1, Pallas kernels, on_device(): pl.pallas_call(final_kernel, out_shape=jax.ShapeDtypeStruct((BEAMS, HEADS...  0.8 us
  transfers between devices with their start and end apart: 11, of which 4 were waited for; matrix products, arithmetic and copies ran while one was open for 0% of the time, Pallas kernels for 27%

profile of v34, /device:TPU:0, one launch (start us, length us, event | category | flops | bytes accessed | tf_op | source)
XLA Modules:
  0.0 24.3 jit_solution(3283501316544226648)
XLA Ops:
  0.0 0.5 %collective-permute-start.2 = (bf16[16,1024]{1,0:T(8,128)(2,1)}, bf16[16,1024]{1,0:T(8,128)(2,1)S(1)}, u32[]{:S(2)}, u32[]{:S(2)}) collective-permute-start(bf16[16,1024]{1,0:T(8,128)(2,1)} %refs_0_.3), channel_id=1, source_target_pairs={{0,4},{4,0},{1,5},{5,1},{2,6},{6,2},{3,7},{7,3},{8,12},{12,8},{9,1... | collective-permute-start | bytes 98312 | tf_op jit(solution)/shard_map/ppermute | solution.py:26
  0.5 0.1 collective-permute-start
  0.5 0.8 %stage.1 = (bf16[16,1024]{1,0:T(8,128)(2,1)S(1)}, s32[4,128]{1,0:T(4,128)S(1)}, s32[1,128]{1,0:T(1,128)S(1)}) custom-call(bf16[16,1024]{1,0:T(8,128)(2,1)} %refs_0_.3, s32[4,128]{1,0:T(4,128)} %bitcast.8, s32[1,128]{1,0:T(1,128)} %bitcast.9), custom_call_target="tpu_custom_call" | custom-call | tf_op jit(solution)/shard_map/stage/pallas_call | solution.py:329
  1.3 0.2 collective-permute-done.2.sibling_ref
  1.5 4.0 %collective-permute-start.3 = (bf16[2,16,1024]{2,1,0:T(8,128)(2,1)S(1)}, bf16[2,16,1024]{2,1,0:T(8,128)(2,1)S(1)}, u32[]{:S(2)}, u32[]{:S(2)}) collective-permute-start(bf16[2,16,1024]{2,1,0:T(8,128)(2,1)S(1)} %both_cores.1), channel_id=1, source_target_pairs={{0,16},{1,17},{4,21},{5,20},{8,24},{9,25},{12,29},{13,28},{16,0},{... | collective-permute-start | bytes 196616 | tf_op jit(solution)/shard_map/ppermute | solution.py:36
  5.5 1.3 %collective-permute-start.8 = (bf16[2,16,1024]{2,1,0:T(8,128)(2,1)S(1)}, bf16[2,16,1024]{2,1,0:T(8,128)(2,1)S(1)}, u32[]{:S(2)}, u32[]{:S(2)}) collective-permute-start(bf16[2,16,1024]{2,1,0:T(8,128)(2,1)S(1)} %both_cores.1), channel_id=1, source_target_pairs={{0,24},{1,25},{4,29},{5,28},{8,16},{9,17},{12,21},{13,20},{16,8},{... | collective-permute-start | bytes 196616 | tf_op jit(solution)/shard_map/ppermute | solution.py:36
  6.9 0.2 collective-permute-start.6
  7.1 1.5 %collective-permute-start.1 = (bf16[16,1024]{1,0:T(8,128)(2,1)S(1)}, bf16[16,1024]{1,0:T(8,128)(2,1)S(1)}, u32[]{:S(2)}, u32[]{:S(2)}) collective-permute-start(bf16[16,1024]{1,0:T(8,128)(2,1)S(1)} %copy-done.2), channel_id=1, source_target_pairs={{0,1},{1,0},{2,3},{3,2},{4,5},{5,4},{6,7},{7,6},{8,9},{9,8},{10,11... | collective-permute-start | bytes 98312 | tf_op jit(solution)/shard_map/ppermute | solution.py:26
  9.3 0.9 %prepare.1 = (bf16[1,512,128]{2,1,0:T(8,128)(2,1)S(1)}, bf16[1,128,512]{2,1,0:T(8,128)(2,1)S(1)}, bf16[6,512,128]{2,1,0:T(8,128)(2,1)S(1)}, bf16[6,128,512]{2,1,0:T(8,128)(2,1)S(1)}, f32[7,8,128]{2,1,0:T(8,128)S(1)}) custom-call(bf16[32,64,256]{2,1,0:T(8,128)(2,1)S(1)} %bitcast.7, s32[4,128]{1,0:T(4,128)S(1)} %get-tuple-element.19.table, ...), custom_call_target="tpu_custom_call" | custom-call | flops 200000000 | bytes 2097152 | tf_op jit(solution)/shard_map/prepare/pallas_call | solution.py:351
  10.2 0.5 %suffix_away.3 = (bf16[272,128]{1,0:T(8,128)(2,1)S(1)}, f32[8,128]{1,0:T(8,128)S(1)}) custom-call(bf16[6,512,128]{2,1,0:T(8,128)(2,1)S(1)} %get-tuple-element.24.keys_ref, bf16[6,128,512]{2,1,0:T(8,128)(2,1)S(1)} %get-tuple-element.25.values_ref, f32[7,8,128]{2,1,0:T(8,128)S(1)} %get-tuple-element.23.member_ref.refs_3_, ...), custom_call_target="tpu_custom_call" | custom-call | flops 200000000 | bytes 2097152 | tf_op jit(solution)/shard_map/suffix_away/pallas_call | solution.py:378
  10.7 0.0 copy-start
  10.8 2.9 %collective-permute-start.5 = (bf16[272,128]{1,0:T(8,128)(2,1)S(1)}, bf16[272,128]{1,0:T(8,128)(2,1)S(1)}, u32[]{:S(2)}, u32[]{:S(2)}) collective-permute-start(bf16[272,128]{1,0:T(8,128)(2,1)S(1)} %get-tuple-element.28), channel_id=1, source_target_pairs={{0,16},{1,17},{4,21},{5,20},{8,24},{9,25},{12,29},{13,28},{16,0},{... | collective-permute-start | bytes 208904 | tf_op jit(solution)/shard_map/ppermute | solution.py:36
  13.6 0.5 %suffix_away.5 = bf16[272,128]{1,0:T(8,128)(2,1)S(1)} custom-call(bf16[6,512,128]{2,1,0:T(8,128)(2,1)S(1)} %get-tuple-element.24.keys_ref, bf16[6,128,512]{2,1,0:T(8,128)(2,1)S(1)} %get-tuple-element.25.values_ref, f32[7,8,128]{2,1,0:T(8,128)S(1)} %get-tuple-element.23.member_ref.refs_3_, bf16[2,16,1024]{2,1,0:T(8,128)(2,1)S(1)} %collective-permute-done.8.message_ref), custom_call_target="tpu_custom_call" | custom-call | flops 200000000 | bytes 2097152 | tf_op jit(solution)/shard_map/suffix_away/pallas_call | solution.py:378
  14.1 2.2 %collective-permute-start.9 = (bf16[272,128]{1,0:T(8,128)(2,1)S(1)}, bf16[272,128]{1,0:T(8,128)(2,1)S(1)}, u32[]{:S(2)}, u32[]{:S(2)}) collective-permute-start(bf16[272,128]{1,0:T(8,128)(2,1)S(1)} %suffix_away.5), channel_id=1, source_target_pairs={{0,24},{1,25},{4,29},{5,28},{8,16},{9,17},{12,21},{13,20},{16,8},{... | collective-permute-start | bytes 208904 | tf_op jit(solution)/shard_map/ppermute | solution.py:36
  16.4 0.5 %suffix_away.4 = bf16[272,128]{1,0:T(8,128)(2,1)S(1)} custom-call(bf16[6,512,128]{2,1,0:T(8,128)(2,1)S(1)} %get-tuple-element.24.keys_ref, bf16[6,128,512]{2,1,0:T(8,128)(2,1)S(1)} %get-tuple-element.25.values_ref, f32[7,8,128]{2,1,0:T(8,128)S(1)} %get-tuple-element.23.member_ref.refs_3_, bf16[2,16,1024]{2,1,0:T(8,128)(2,1)S(1)} %collective-permute-done.6.message_ref), custom_call_target="tpu_custom_call" | custom-call | flops 200000000 | bytes 2097152 | tf_op jit(solution)/shard_map/suffix_away/pallas_call | solution.py:378
  16.9 0.6 %collective-permute-start.7 = (bf16[272,128]{1,0:T(8,128)(2,1)S(1)}, bf16[272,128]{1,0:T(8,128)(2,1)S(1)}, u32[]{:S(2)}, u32[]{:S(2)}) collective-permute-start(bf16[272,128]{1,0:T(8,128)(2,1)S(1)} %suffix_away.4), channel_id=1, source_target_pairs={{0,8},{1,9},{4,13},{5,12},{8,0},{9,1},{12,5},{13,4},{16,24},{17,25... | collective-permute-start | bytes 208904 | tf_op jit(solution)/shard_map/ppermute | solution.py:36
  17.5 1.6 %home_pair_heads.1 = bf16[144,128]{1,0:T(8,128)(2,1)S(1)} custom-call(s32[1]{0:T(128)S(6)} %copy.7.refs_0_, bf16[1,512,128]{2,1,0:T(8,128)(2,1)S(1)} %get-tuple-element.21.refs_1_, bf16[1,128,512]{2,1,0:T(8,128)(2,1)S(1)} %get-tuple-element.22.refs_2_, f32[7,8,128]{2,1,0:T(8,128)S(1)} %get-tuple-element.23.member_ref.refs_3_, ...), custom_call_target="tpu_custom_call" | custom-call | flops 536870912 | bytes 2097152 | tf_op jit(solution)/shard_map/home_pair_heads/pallas_call | solution.py:395
  19.1 0.8 %collective-permute-start.4 = (bf16[144,128]{1,0:T(8,128)(2,1)S(1)}, bf16[144,128]{1,0:T(8,128)(2,1)S(1)}, u32[]{:S(2)}, u32[]{:S(2)}) collective-permute-start(bf16[144,128]{1,0:T(8,128)(2,1)S(1)} %home_pair_heads.1), channel_id=1, source_target_pairs={{0,1},{1,0},{2,3},{3,2},{4,5},{5,4},{6,7},{7,6},{8,9},{9,8},{10,11... | collective-permute-start | bytes 110600 | tf_op jit(solution)/shard_map/ppermute | solution.py:26
  19.9 1.6 %home_own_heads.1 = (f32[128,128]{1,0:T(8,128)S(1)}, f32[8,128]{1,0:T(8,128)S(1)}) custom-call(s32[1]{0:T(128)S(6)} %copy.7.refs_0_, bf16[1,512,128]{2,1,0:T(8,128)(2,1)S(1)} %get-tuple-element.21.refs_1_, bf16[1,128,512]{2,1,0:T(8,128)(2,1)S(1)} %get-tuple-element.22.refs_2_, f32[7,8,128]{2,1,0:T(8,128)S(1)} %get-tuple-element.23.member_ref.refs_3_, ...), custom_call_target="tpu_custom_call" | custom-call | flops 536870912 | bytes 2097152 | tf_op jit(solution)/shard_map/home_own_heads/pallas_call | solution.py:405
  21.5 0.7 %collective-permute-done.7.rest_1_ = bf16[272,128]{1,0:T(8,128)(2,1)S(1)} collective-permute-done((bf16[272,128]{1,0:T(8,128)(2,1)S(1)}, bf16[272,128]{1,0:T(8,128)(2,1)S(1)}, u32[]{:S(2)}, u32[]{:S(2)}) %collective-permute-start.7) | collective-permute-done | bytes 69664 | tf_op jit(solution)/shard_map/ppermute | solution.py:36
  22.2 0.4 %collective-permute-start.10 = (bf16[144,128]{1,0:T(8,128)(2,1)S(1)}, bf16[144,128]{1,0:T(8,128)(2,1)S(1)}, u32[]{:S(2)}, u32[]{:S(2)}) collective-permute-start(bf16[144,128]{1,0:T(8,128)(2,1)S(1)} %sibling_share.1), channel_id=1, source_target_pairs={{0,4},{4,0},{1,5},{5,1},{2,6},{6,2},{3,7},{7,3},{8,12},{12,8},{9,1... | collective-permute-start | bytes 110600 | tf_op jit(solution)/shard_map/ppermute | solution.py:26
  22.6 0.5 %collective-permute-done.4.last_ref = bf16[144,128]{1,0:T(8,128)(2,1)S(1)} collective-permute-done((bf16[144,128]{1,0:T(8,128)(2,1)S(1)}, bf16[144,128]{1,0:T(8,128)(2,1)S(1)}, u32[]{:S(2)}, u32[]{:S(2)}) %collective-permute-start.4) | collective-permute-done | bytes 36896 | tf_op jit(solution)/shard_map/ppermute | solution.py:26
  23.1 0.4 %collective-permute-done.10.shared_ref = bf16[144,128]{1,0:T(8,128)(2,1)S(1)} collective-permute-done((bf16[144,128]{1,0:T(8,128)(2,1)S(1)}, bf16[144,128]{1,0:T(8,128)(2,1)S(1)}, u32[]{:S(2)}, u32[]{:S(2)}) %collective-permute-start.10) | collective-permute-done | bytes 36896 | tf_op jit(solution)/shard_map/ppermute | solution.py:26
  23.5 0.8 %combine.1 = f32[16,1024]{1,0:T(8,128)} custom-call(bf16[144,128]{1,0:T(8,128)(2,1)S(1)} %collective-permute-done.4.last_ref, bf16[144,128]{1,0:T(8,128)(2,1)S(1)} %collective-permute-done.10.shared_ref, f32[128,128]{1,0:T(8,128)S(1)} %get-tuple-element.31.summed_ref, f32[8,128]{1,0:T(8,128)S(1)} %get-tuple-element.32.stats_ref), custom_call_target="tpu_custom_call" | custom-call | tf_op jit(solution)/shard_map/combine/pallas_call | solution.py:434
  (15 shorter events, 0.1 us)
Async XLA Ops:
  0.0 1.5 %collective-permute-start.2 = (bf16[16,1024]{1,0:T(8,128)(2,1)}, bf16[16,1024]{1,0:T(8,128)(2,1)S(1)}, u32[]{:S(2)}, u32[]{:S(2)}) collective-permute-start(bf16[16,1024]{1,0:T(8,128)(2,1)} %refs_0_.3), channel_id=1, source_target_pairs={{0,4},{4,0},{1,5},{5,1},{2,6},{6,2},{3,7},{7,3},{8,12},{12,8},{9,1... | collective-permute-start | bytes 98312 | tf_op jit(solution)/shard_map/ppermute | solution.py:26
  0.5 8.8 %collective-permute-start = (bf16[32,64,256]{2,1,0:T(8,128)(2,1)}, bf16[32,64,256]{2,1,0:T(8,128)(2,1)S(1)}, u32[]{:S(2)}, u32[]{:S(2)}) collective-permute-start(bf16[32,64,256]{2,1,0:T(8,128)(2,1)} %bitcast.6), channel_id=1, source_target_pairs={{0,4},{4,0},{1,5},{5,1},{2,6},{6,2},{3,7},{7,3},{8,12},{12,8},{9,1... | collective-permute-start | bytes 3145736 | tf_op jit(solution)/shard_map/ppermute | solution.py:26
  1.5 5.6 %copy-start.2 = (bf16[16,1024]{1,0:T(8,128)(2,1)S(1)}, bf16[16,1024]{1,0:T(8,128)(2,1)}, u32[]{:S(2)}) copy-start(bf16[16,1024]{1,0:T(8,128)(2,1)} %refs_0_.3) | copy-start | bytes 98308
  1.5 7.8 %copy-start.1 = (bf16[32,1,64,256]{3,2,1,0:T(8,128)(2,1)S(1)}, bf16[32,1,64,256]{3,2,1,0:T(8,128)(2,1)}, u32[]{:S(2)}) copy-start(bf16[32,1,64,256]{3,2,1,0:T(8,128)(2,1)} %param.8) | copy-start | bytes 3145732
  1.5 8.7 %collective-permute-start.3 = (bf16[2,16,1024]{2,1,0:T(8,128)(2,1)S(1)}, bf16[2,16,1024]{2,1,0:T(8,128)(2,1)S(1)}, u32[]{:S(2)}, u32[]{:S(2)}) collective-permute-start(bf16[2,16,1024]{2,1,0:T(8,128)(2,1)S(1)} %both_cores.1), channel_id=1, source_target_pairs={{0,16},{1,17},{4,21},{5,20},{8,24},{9,25},{12,29},{13,28},{16,0},{... | collective-permute-start | bytes 196616 | tf_op jit(solution)/shard_map/ppermute | solution.py:36
  5.5 8.1 %collective-permute-start.8 = (bf16[2,16,1024]{2,1,0:T(8,128)(2,1)S(1)}, bf16[2,16,1024]{2,1,0:T(8,128)(2,1)S(1)}, u32[]{:S(2)}, u32[]{:S(2)}) collective-permute-start(bf16[2,16,1024]{2,1,0:T(8,128)(2,1)S(1)} %both_cores.1), channel_id=1, source_target_pairs={{0,24},{1,25},{4,29},{5,28},{8,16},{9,17},{12,21},{13,20},{16,8},{... | collective-permute-start | bytes 196616 | tf_op jit(solution)/shard_map/ppermute | solution.py:36
  6.9 9.5 %collective-permute-start.6 = (bf16[2,16,1024]{2,1,0:T(8,128)(2,1)S(1)}, bf16[2,16,1024]{2,1,0:T(8,128)(2,1)S(1)}, u32[]{:S(2)}, u32[]{:S(2)}) collective-permute-start(bf16[2,16,1024]{2,1,0:T(8,128)(2,1)S(1)} %both_cores.1), channel_id=1, source_target_pairs={{0,8},{1,9},{4,13},{5,12},{8,0},{9,1},{12,5},{13,4},{16,24},{17,25... | collective-permute-start | bytes 196616 | tf_op jit(solution)/shard_map/ppermute | solution.py:36
  7.1 10.4 %collective-permute-start.1 = (bf16[16,1024]{1,0:T(8,128)(2,1)S(1)}, bf16[16,1024]{1,0:T(8,128)(2,1)S(1)}, u32[]{:S(2)}, u32[]{:S(2)}) collective-permute-start(bf16[16,1024]{1,0:T(8,128)(2,1)S(1)} %copy-done.2), channel_id=1, source_target_pairs={{0,1},{1,0},{2,3},{3,2},{4,5},{5,4},{6,7},{7,6},{8,9},{9,8},{10,11... | collective-permute-start | bytes 98312 | tf_op jit(solution)/shard_map/ppermute | solution.py:26
  10.7 6.8 %copy-start = (bf16[1,1,4096,256]{3,2,1,0:T(8,128)(2,1)S(1)}, bf16[1,1,4096,256]{3,2,1,0:T(8,128)(2,1)}, u32[]{:S(2)}) copy-start(bf16[1,1,4096,256]{3,2,1,0:T(8,128)(2,1)} %param.7) | copy-start | bytes 6291460
  10.8 10.7 %collective-permute-start.5 = (bf16[272,128]{1,0:T(8,128)(2,1)S(1)}, bf16[272,128]{1,0:T(8,128)(2,1)S(1)}, u32[]{:S(2)}, u32[]{:S(2)}) collective-permute-start(bf16[272,128]{1,0:T(8,128)(2,1)S(1)} %get-tuple-element.28), channel_id=1, source_target_pairs={{0,16},{1,17},{4,21},{5,20},{8,24},{9,25},{12,29},{13,28},{16,0},{... | collective-permute-start | bytes 208904 | tf_op jit(solution)/shard_map/ppermute | solution.py:36
  14.1 7.3 %collective-permute-start.9 = (bf16[272,128]{1,0:T(8,128)(2,1)S(1)}, bf16[272,128]{1,0:T(8,128)(2,1)S(1)}, u32[]{:S(2)}, u32[]{:S(2)}) collective-permute-start(bf16[272,128]{1,0:T(8,128)(2,1)S(1)} %suffix_away.5), channel_id=1, source_target_pairs={{0,24},{1,25},{4,29},{5,28},{8,16},{9,17},{12,21},{13,20},{16,8},{... | collective-permute-start | bytes 208904 | tf_op jit(solution)/shard_map/ppermute | solution.py:36
  16.9 5.3 %collective-permute-start.7 = (bf16[272,128]{1,0:T(8,128)(2,1)S(1)}, bf16[272,128]{1,0:T(8,128)(2,1)S(1)}, u32[]{:S(2)}, u32[]{:S(2)}) collective-permute-start(bf16[272,128]{1,0:T(8,128)(2,1)S(1)} %suffix_away.4), channel_id=1, source_target_pairs={{0,8},{1,9},{4,13},{5,12},{8,0},{9,1},{12,5},{13,4},{16,24},{17,25... | collective-permute-start | bytes 208904 | tf_op jit(solution)/shard_map/ppermute | solution.py:36
  19.1 4.0 %collective-permute-start.4 = (bf16[144,128]{1,0:T(8,128)(2,1)S(1)}, bf16[144,128]{1,0:T(8,128)(2,1)S(1)}, u32[]{:S(2)}, u32[]{:S(2)}) collective-permute-start(bf16[144,128]{1,0:T(8,128)(2,1)S(1)} %home_pair_heads.1), channel_id=1, source_target_pairs={{0,1},{1,0},{2,3},{3,2},{4,5},{5,4},{6,7},{7,6},{8,9},{9,8},{10,11... | collective-permute-start | bytes 110600 | tf_op jit(solution)/shard_map/ppermute | solution.py:26
  22.2 1.3 %collective-permute-start.10 = (bf16[144,128]{1,0:T(8,128)(2,1)S(1)}, bf16[144,128]{1,0:T(8,128)(2,1)S(1)}, u32[]{:S(2)}, u32[]{:S(2)}) collective-permute-start(bf16[144,128]{1,0:T(8,128)(2,1)S(1)} %sibling_share.1), channel_id=1, source_target_pairs={{0,4},{4,0},{1,5},{5,1},{2,6},{6,2},{3,7},{7,3},{8,12},{12,8},{9,1... | collective-permute-start | bytes 110600 | tf_op jit(solution)/shard_map/ppermute | solution.py:26
